TPU v7x, 32 devices: a whole 2x2x4 slice. The times are simulated.
32 devices in a mesh: dp: 8 (over z, y), tensor: 4 (over x, core).
Axes of the slice: x: 2, y: 2, z: 4, core: 2. Of those that a mesh axis runs over, the one named last changes fastest.
Arguments:
- inputs: bfloat16 [5632, 1280], P('dp'), may hold values from -24 to 24
- targets: bfloat16 [5632, 1280], P('dp'), may hold values from -6 to 6
- w_in: bfloat16 [1280, 5120], P(None, 'tensor'), may hold values from -0.15625 to 0.15625
- w_out: bfloat16 [5120, 1280], P('tensor'), may hold values from -0.078125 to 0.078125
Outputs:
- merged_in: float32 [1280, 5120], P('dp', 'tensor')
- merged_out: float32 [1280, 5120], P('dp', 'tensor')
All inputs are finite; a program needn't handle non-finite values.
Results may differ from a plain program's by a relative error of at most 0.0033.
Values may be sent and summed in bfloat16 or wider, within the bound.
No kernel may reach another device: no remote copies, remote signals or barrier semaphores. Data moves between devices by JAX's collectives and lax.ppermute only.
A program may use at most 128 MiB of HBM per device.

v0:
```python
import jax
import jax.numpy as jnp
from jax import lax
from jax.sharding import PartitionSpec as P

epsilon = 1e-06


def from_partner(value, axis, distance):
    mask = 2**distance
    pairs = [(source, source ^ mask) for source in range(lax.axis_size(axis))]
    return lax.ppermute(value, axis, pairs)


def activate(values):
    return jax.nn.gelu(values, approximate=True)


def split_piece(piece, upper_flag):
    half = piece.shape[0] // 2
    keep = lax.dynamic_slice_in_dim(piece, upper_flag * half, half, 0)
    send = lax.dynamic_slice_in_dim(piece, (1 - upper_flag) * half, half, 0)
    return (keep, send)


def group_total(values, section, levels):
    summed = lax.psum(values, "tensor")
    for offset in range(section + 1):
        summed = summed + from_partner(summed, "dp", levels - 1 - offset)
    return summed


def combine(own, incoming, upper_flag, section, levels):
    product = jnp.sum(own[0] * incoming[0]) + jnp.sum(own[1] * incoming[1])
    norm_own = jnp.sum(own[0] * own[0]) + jnp.sum(own[1] * own[1])
    norm_incoming = jnp.sum(incoming[0] * incoming[0]) + jnp.sum(incoming[1] * incoming[1])
    is_upper = upper_flag == 1
    norm_low = jnp.where(is_upper, norm_incoming, norm_own)
    norm_high = jnp.where(is_upper, norm_own, norm_incoming)
    totals = group_total(jnp.stack([product, norm_low, norm_high]), section, levels)
    coef_low = 1.0 - totals[0] / (2.0 * (totals[1] + epsilon))
    coef_high = 1.0 - totals[0] / (2.0 * (totals[2] + epsilon))
    coef_own = jnp.where(is_upper, coef_high, coef_low)
    coef_incoming = jnp.where(is_upper, coef_low, coef_high)
    return (
        coef_own * own[0] + coef_incoming * incoming[0],
        coef_own * own[1] + coef_incoming * incoming[1],
    )


def on_device(inputs, targets, w_in, w_out):
    row_count = inputs.shape[0]
    preact = jnp.dot(inputs, w_in, preferred_element_type=jnp.float32)
    hidden = activate(preact).astype(jnp.bfloat16)
    partial_out = jnp.dot(hidden, w_out, preferred_element_type=jnp.float32)
    whole = lax.psum(partial_out, "tensor")
    error = ((whole - targets.astype(jnp.float32)) / row_count).astype(jnp.bfloat16)
    back = jnp.dot(error, w_out.T, preferred_element_type=jnp.float32)
    _, pullback = jax.vjp(activate, preact)
    dpre = pullback(back)[0].astype(jnp.bfloat16)
    contract_rows = (((0,), (0,)), ((), ()))
    second = lax.dot_general(error, hidden, contract_rows, preferred_element_type=jnp.float32)
    levels = lax.axis_size("dp").bit_length() - 1
    position = lax.axis_index("dp")

    def flag_of(section):
        return position >> levels - 1 - section & 1

    upper_flag = flag_of(0)
    keep_second, send_second = split_piece(second, upper_flag)
    got_second = from_partner(send_second.astype(jnp.bfloat16), "dp", levels - 1).astype(
        send_second.dtype
    )
    first = lax.dot_general(inputs, dpre, contract_rows, preferred_element_type=jnp.float32)
    keep_first, send_first = split_piece(first, upper_flag)
    got_first = from_partner(send_first, "dp", levels - 1)
    pieces = combine((keep_first, keep_second), (got_first, got_second), upper_flag, 0, levels)
    begin = 1
    for section in range(begin, levels):
        upper_flag = flag_of(section)
        keep_first, send_first = split_piece(pieces[0], upper_flag)
        keep_second, send_second = split_piece(pieces[1], upper_flag)
        got_first, got_second = from_partner((send_first, send_second), "dp", levels - 1 - section)
        pieces = combine(
            (keep_first, keep_second), (got_first, got_second), upper_flag, section, levels
        )
    return (pieces[0], pieces[1])


def solution(mesh):
    placed = (P("dp", None), P("dp", None), P(None, "tensor"), P("tensor", None))
    return jax.shard_map(
        on_device,
        mesh=mesh,
        in_specs=placed,
        out_specs=(P("dp", "tensor"), P("dp", "tensor")),
        check_vma=False,
    )
```

profile of v0, /device:TPU:0, one launch (start us, length us, event | category | flops | bytes accessed | tf_op | source)
XLA Modules:
  0.0 531.3 jit_solution(4205678895485817457)
XLA Ops:
  7.2 5.1 fusion.27
  14.2 5.1 fusion.23
  19.3 78.7 %all-reduce.2.cloned.1.call-done = f32[704,1280]{1,0:T(8,128)} async-done(((f32[704,1280]{1,0:T(8,128)}), f32[704,1280]{1,0:T(8,128)}) %all-reduce.2.cloned.1.call-update) | async-done | bytes 3604496 | tf_op jit(solution)/shard_map/psum | solution.py:56
  98.0 13.3 %fusion.13 = f32[1280,1280]{0,1:T(8,128)} fusion(bf16[704,1280]{1,0:T(8,128)(2,1)} %param.4, f32[704,1280]{1,0:T(8,128)} %copy-done.10, bf16[1280,1280]{1,0:T(8,128)(2,1)S(1)} %copy-done, f32[704,1280]{1,0:T(8,128)} %all-reduce.2.cloned.1.call-done, bf16[704,1280]{1,0:T(8,128)(2,1)} %param.5), kind=kOutput, calls=%fused_computation.27 | convolution fusion | flops 4635361280 | bytes 20643840 | tf_op jit(solution)/shard_map/dot_general | solution.py:74
  111.3 4.0 dynamic-slice_bitcast_fusion
  115.4 2.4 collective-permute-start
  117.8 5.3 fusion.21
  123.1 2.8 copy-done.5
  127.7 201.8 %collective-permute-done.1 = bf16[640,1280]{1,0:T(8,128)(2,1)} collective-permute-done((bf16[640,1280]{1,0:T(8,128)(2,1)}, bf16[640,1280]{1,0:T(8,128)(2,1)}, u32[]{:S(2)}, u32[]{:S(2)}) %collective-permute-start.1) | collective-permute-done | bytes 1638432 | tf_op jit(solution)/shard_map/ppermute | solution.py:12
  329.5 3.9 fusion.7
  333.5 4.4 fusion.10
  341.6 5.6 %psum.29 = f32[3]{0:T(128)S(1)} all-reduce(f32[3]{0:T(128)S(1)} %pad_maximum_fusion), channel_id=1, replica_groups=mesh['dp'=8,'tensor'=4] {'tensor'}, use_global_device_ids=true, to_apply=%region_7.8 | all-reduce | flops 3 | bytes 24 | tf_op jit(solution)/shard_map/psum | solution.py:27
  347.3 4.4 collective-permute-done.2
  354.8 3.3 fusion.12
  362.0 2.8 fusion.9
  368.2 31.2 %collective-permute-done.3 = f32[320,1280]{1,0:T(8,128)} collective-permute-done((f32[320,1280]{1,0:T(8,128)}, f32[320,1280]{1,0:T(8,128)}, u32[]{:S(2)}, u32[]{:S(2)}) %collective-permute-start.3) | collective-permute-done | bytes 1638432 | tf_op jit(solution)/shard_map/ppermute | solution.py:12
  399.4 3.0 multiply_reduce_fusion.7
  402.4 29.8 %collective-permute-done.4 = f32[320,1280]{1,0:T(8,128)} collective-permute-done((f32[320,1280]{1,0:T(8,128)}, f32[320,1280]{1,0:T(8,128)}, u32[]{:S(2)}, u32[]{:S(2)}) %collective-permute-start.4) | collective-permute-done | bytes 1638432 | tf_op jit(solution)/shard_map/ppermute | solution.py:12
  432.2 2.7 multiply_reduce_fusion.6
  438.9 5.6 %psum.30 = f32[3]{0:T(128)S(1)} all-reduce(f32[3]{0:T(128)S(1)} %pad_maximum_fusion.1), channel_id=1, replica_groups=mesh['dp'=8,'tensor'=4] {'tensor'}, use_global_device_ids=true, to_apply=%region_14.15 | all-reduce | flops 3 | bytes 24 | tf_op jit(solution)/shard_map/psum | solution.py:27
  446.7 2.3 collective-permute-done.5
  450.2 2.3 collective-permute-done.6
  455.6 2.3 multiply_add_fusion
  464.1 16.4 %collective-permute-done.8 = f32[160,1280]{1,0:T(8,128)} collective-permute-done((f32[160,1280]{1,0:T(8,128)}, f32[160,1280]{1,0:T(8,128)}, u32[]{:S(2)}, u32[]{:S(2)}) %collective-permute-start.8) | collective-permute-done | bytes 819232 | tf_op jit(solution)/shard_map/ppermute | solution.py:12
  480.4 2.3 multiply_reduce_fusion.12
  482.7 11.8 %collective-permute-done.7 = f32[160,1280]{1,0:T(8,128)} collective-permute-done((f32[160,1280]{1,0:T(8,128)}, f32[160,1280]{1,0:T(8,128)}, u32[]{:S(2)}, u32[]{:S(2)}) %collective-permute-start.7) | collective-permute-done | bytes 819232 | tf_op jit(solution)/shard_map/ppermute | solution.py:12
  494.5 2.3 multiply_reduce_fusion.13
  500.8 5.6 %psum.31 = f32[3]{0:T(128)S(1)} all-reduce(f32[3]{0:T(128)S(1)} %pad_maximum_fusion.2), channel_id=1, replica_groups=mesh['dp'=8,'tensor'=4] {'tensor'}, use_global_device_ids=true, to_apply=%region_21.22 | all-reduce | flops 3 | bytes 24 | tf_op jit(solution)/shard_map/psum | solution.py:27
  506.4 2.2 collective-permute-start.9
  508.6 2.3 collective-permute-done.9
  512.1 2.3 collective-permute-done.10
  521.2 3.2 multiply_add_fusion.2
  (53 shorter events, 27.4 us)
Async XLA Ops:
  7.2 7.0 %copy-start = (bf16[1280,1280]{1,0:T(8,128)(2,1)S(1)}, bf16[1280,1280]{1,0:T(8,128)(2,1)}, u32[]{:S(2)}) copy-start(bf16[1280,1280]{1,0:T(8,128)(2,1)} %param.7) | copy-start | bytes 9830404
  7.2 90.8 %all-reduce.2.cloned.1.call-start = ((), (), s32[]{:S(2)}) async-start(), calls=%async_computation | async-start | bytes 7208960 | tf_op jit(solution)/shard_map/psum | solution.py:56
  12.3 1.8 copy-start.10
  111.3 6.4 %copy-start.8 = (f32[704,1280]{1,0:T(8,128)S(1)}, f32[704,1280]{1,0:T(8,128)}, u32[]{:S(2)}) copy-start(f32[704,1280]{1,0:T(8,128)} %all-reduce.2.cloned.1.call-done) | copy-start | bytes 10813444
  111.3 6.4 %copy-start.9 = (bf16[704,1280]{1,0:T(8,128)(2,1)S(1)}, bf16[704,1280]{1,0:T(8,128)(2,1)}, u32[]{:S(2)}) copy-start(bf16[704,1280]{1,0:T(8,128)(2,1)} %param.5) | copy-start | bytes 5406724
  115.4 218.1 %collective-permute-start = (f32[640,1280]{1,0:T(8,128)}, f32[640,1280]{1,0:T(8,128)}, u32[]{:S(2)}, u32[]{:S(2)}) collective-permute-start(f32[640,1280]{1,0:T(8,128)} %dynamic-slice_bitcast_fusion), channel_id=1, source_target_pairs={{0,16},{4,20},{8,24},{12,28},{16,0},{20,4},{24,8},{28,12},{1,17},{... | collective-permute-start | bytes 9830408 | tf_op jit(solution)/shard_map/ppermute | solution.py:12
  123.1 2.8 copy-start.5
  127.2 202.4 %collective-permute-start.1 = (bf16[640,1280]{1,0:T(8,128)(2,1)}, bf16[640,1280]{1,0:T(8,128)(2,1)}, u32[]{:S(2)}, u32[]{:S(2)}) collective-permute-start(bf16[640,1280]{1,0:T(8,128)(2,1)} %dynamic-slice_convert_fusion), channel_id=1, source_target_pairs={{0,16},{4,20},{8,24},{12,28},{16,0},{20,4},{24,8},{28,12},{1,17},{... | collective-permute-start | bytes 4915208 | tf_op jit(solution)/shard_map/ppermute | solution.py:12
  347.2 4.5 collective-permute-start.2
  358.1 2.3 copy-start.3
  360.4 39.1 %collective-permute-start.3 = (f32[320,1280]{1,0:T(8,128)}, f32[320,1280]{1,0:T(8,128)}, u32[]{:S(2)}, u32[]{:S(2)}) collective-permute-start(f32[320,1280]{1,0:T(8,128)} %constant_dynamic-slice_fusion.3), channel_id=1, source_target_pairs={{0,8},{4,12},{8,0},{12,4},{16,24},{20,28},{24,16},{28,20},{1,9},{5... | collective-permute-start | bytes 4915208 | tf_op jit(solution)/shard_map/ppermute | solution.py:12
  364.8 1.7 copy-start.1
  367.8 64.5 %collective-permute-start.4 = (f32[320,1280]{1,0:T(8,128)}, f32[320,1280]{1,0:T(8,128)}, u32[]{:S(2)}, u32[]{:S(2)}) collective-permute-start(f32[320,1280]{1,0:T(8,128)} %constant_dynamic-slice_fusion.2), channel_id=1, source_target_pairs={{0,8},{4,12},{8,0},{12,4},{16,24},{20,28},{24,16},{28,20},{1,9},{5... | collective-permute-start | bytes 4915208 | tf_op jit(solution)/shard_map/ppermute | solution.py:12
  368.2 64.0 %copy-start.2 = (f32[640,1280]{1,0:T(8,128)S(1)}, f32[640,1280]{1,0:T(8,128)}, u32[]{:S(2)}) copy-start(f32[640,1280]{1,0:T(8,128)} %copy-done.1) | copy-start | bytes 9830404
  444.5 4.5 collective-permute-start.5
  449.0 3.5 collective-permute-start.6
  455.6 4.8 copy-start.4
  457.9 4.1 copy-start.6
  459.0 21.5 %collective-permute-start.8 = (f32[160,1280]{1,0:T(8,128)}, f32[160,1280]{1,0:T(8,128)}, u32[]{:S(2)}, u32[]{:S(2)}) collective-permute-start(f32[160,1280]{1,0:T(8,128)} %constant_dynamic-slice_fusion), channel_id=1, source_target_pairs={{0,4},{4,0},{8,12},{12,8},{16,20},{20,16},{24,28},{28,24},{1,5},{5... | collective-permute-start | bytes 2457608 | tf_op jit(solution)/shard_map/ppermute | solution.py:12
  462.1 1.5 copy-start.7
  463.5 31.0 %collective-permute-start.7 = (f32[160,1280]{1,0:T(8,128)}, f32[160,1280]{1,0:T(8,128)}, u32[]{:S(2)}, u32[]{:S(2)}) collective-permute-start(f32[160,1280]{1,0:T(8,128)} %constant_dynamic-slice_fusion.1), channel_id=1, source_target_pairs={{0,4},{4,0},{8,12},{12,8},{16,20},{20,16},{24,28},{28,24},{1,5},{5... | collective-permute-start | bytes 2457608 | tf_op jit(solution)/shard_map/ppermute | solution.py:12
  506.4 4.5 collective-permute-start.9
  510.9 3.5 collective-permute-start.10
  514.4 3.5 collective-permute-start.11
Sparse Core Ops, SparseCore 0:
  19.4 78.5 all-reduce.1
where the time goes:
time: 532 us; the launch traced here: 531 us
  waiting for transfers between devices  386 us (73%)
  between operations  33.1 us (6%)
  other arithmetic  32.1 us (6%)
  matrix products  28.8 us (5%)
  local copies, waits for them, and re-layouts  19.5 us (4%)
  blocking collectives  16.9 us (3%)
  starting transfers between devices  15.3 us (3%)
    ppermute x12, waiting for transfers between devices, from_partner(): return lax.ppermute(value, axis, pairs)  307 us
    psum x1, waiting for transfers between devices, on_device(): whole = lax.psum(partial_out, 'tensor')  78.7 us
    reduce_sum x6, other arithmetic, combine(): product = jnp.sum(own[0] * incoming[0]) + jnp.sum(own[1] * incoming[1])  18.6 us
    psum x3, blocking collectives, group_total(): summed = lax.psum(values, 'tensor')  16.9 us
    ppermute x12, starting transfers between devices, from_partner(): return lax.ppermute(value, axis, pairs)  15.3 us
    dot_general x1, matrix products, on_device(): lax.dot_general(inputs, dpre, contract_rows, preferred_element_type=jnp.f...  13.3 us
  transfers between devices with their start and end apart: 13, of which 12 were waited for; matrix products, arithmetic and copies ran while one was open for 4% of the time, Pallas kernels for 0%

commit v1 on v0

--- a/solution.py
+++ b/solution.py
@@ -1,9 +1,14 @@
+import functools
+
 import jax
 import jax.numpy as jnp
 from jax import lax
+from jax.experimental import pallas as pl
+from jax.experimental.pallas import tpu as pltpu
 from jax.sharding import PartitionSpec as P
 
 epsilon = 1e-06
+gather_levels_limit = 3
 
 
 def from_partner(value, axis, distance):
@@ -24,6 +29,8 @@
 
 
 def group_total(values, section, levels):
+    if section + 1 == levels:
+        return lax.psum(values, ("dp", "tensor"))
     summed = lax.psum(values, "tensor")
     for offset in range(section + 1):
         summed = summed + from_partner(summed, "dp", levels - 1 - offset)
@@ -48,36 +55,175 @@
     )
 
 
+def pair_list(count):
+    return [(i, j) for i in range(count) for j in range(i, count)]
+
+
+def gram_kernel(count, first_ref, second_ref, out_ref, totals):
+    pairs = pair_list(count)
+    step = pl.program_id(0)
+
+    @pl.when(step == 0)
+    def _():
+        totals[...] = jnp.zeros_like(totals)
+
+    columns = first_ref.shape[2] // 128
+    groups = first_ref.shape[1] // 8
+
+    for ref in (first_ref, second_ref):
+
+        def body(index, sums, ref=ref):
+            row = pl.multiple_of((index // columns) * 8, 8)
+            column = pl.multiple_of((index % columns) * 128, 128)
+            members = [ref[i, pl.ds(row, 8), pl.ds(column, 128)] for i in range(count)]
+            return tuple(s + members[i] * members[j] for s, (i, j) in zip(sums, pairs))
+
+        zero = jnp.zeros((8, 128), jnp.float32)
+        sums = lax.fori_loop(0, groups * columns, body, (zero,) * len(pairs))
+        for n, s in enumerate(sums):
+            totals[n] += s
+
+    @pl.when(step == pl.num_programs(0) - 1)
+    def _():
+        out_ref[...] = jnp.sum(totals[...], axis=1)
+
+
+def gram(first, second):
+    count, rows, width = first.shape
+    block = max(b for b in range(8, min(rows, 40) + 1, 8) if rows % b == 0)
+    pairs = len(pair_list(count))
+    spec = pl.BlockSpec((count, block, width), lambda i: (0, i, 0))
+    return pl.pallas_call(
+        functools.partial(gram_kernel, count),
+        grid=(rows // block,),
+        in_specs=[spec, spec],
+        out_specs=pl.BlockSpec((pairs, 128), lambda i: (0, 0)),
+        out_shape=jax.ShapeDtypeStruct((pairs, 128), jnp.float32),
+        scratch_shapes=[pltpu.VMEM((pairs, 8, 128), jnp.float32)],
+        compiler_params=pltpu.CompilerParams(vmem_limit_bytes=40 * 2**20),
+        name="gram",
+    )(first, second)
+
+
+def tree_weights(count, entry):
+    def inner(a, b):
+        total = 0.0
+        for i, u in a.items():
+            for j, v in b.items():
+                total = total + u * v * entry(i, j)
+        return total
+
+    items = [{i: 1.0} for i in range(count)]
+    while len(items) > 1:
+        half = len(items) // 2
+        merged = []
+        for low, high in zip(items[:half], items[half:]):
+            product = inner(low, high)
+            scale_low = 1.0 - product / (2.0 * (jnp.maximum(inner(low, low), 0.0) + epsilon))
+            scale_high = 1.0 - product / (2.0 * (jnp.maximum(inner(high, high), 0.0) + epsilon))
+            joined = {i: u * scale_low for i, u in low.items()}
+            joined.update({i: u * scale_high for i, u in high.items()})
+            merged.append(joined)
+        items = merged
+    return [items[0][i] for i in range(count)]
+
+
+def merge_kernel(count, totals_ref, first_ref, second_ref, first_out, second_out):
+    place = {pair: n for n, pair in enumerate(pair_list(count))}
+
+    def entry(i, j):
+        return totals_ref[place[(min(i, j), max(i, j))]]
+
+    weights = tree_weights(count, entry)
+    for source, target in ((first_ref, first_out), (second_ref, second_out)):
+        total = weights[0] * source[0]
+        for i in range(1, count):
+            total = total + weights[i] * source[i]
+        target[...] = total
+
+
+def merge(totals, first, second):
+    count, rows, width = first.shape
+    block = max(b for b in range(8, min(rows, 32) + 1, 8) if rows % b == 0)
+    spec = pl.BlockSpec((count, block, width), lambda i: (0, i, 0))
+    out_spec = pl.BlockSpec((block, width), lambda i: (i, 0))
+    shape = jax.ShapeDtypeStruct((rows, width), jnp.float32)
+    return pl.pallas_call(
+        functools.partial(merge_kernel, count),
+        grid=(rows // block,),
+        in_specs=[pl.BlockSpec(memory_space=pltpu.SMEM), spec, spec],
+        out_specs=[out_spec, out_spec],
+        out_shape=[shape, shape],
+        compiler_params=pltpu.CompilerParams(vmem_limit_bytes=40 * 2**20),
+        name="merge",
+    )(totals, first, second)
+
+
 def on_device(inputs, targets, w_in, w_out):
     row_count = inputs.shape[0]
-    preact = jnp.dot(inputs, w_in, preferred_element_type=jnp.float32)
-    hidden = activate(preact).astype(jnp.bfloat16)
-    partial_out = jnp.dot(hidden, w_out, preferred_element_type=jnp.float32)
-    whole = lax.psum(partial_out, "tensor")
-    error = ((whole - targets.astype(jnp.float32)) / row_count).astype(jnp.bfloat16)
-    back = jnp.dot(error, w_out.T, preferred_element_type=jnp.float32)
-    _, pullback = jax.vjp(activate, preact)
-    dpre = pullback(back)[0].astype(jnp.bfloat16)
-    contract_rows = (((0,), (0,)), ((), ()))
-    second = lax.dot_general(error, hidden, contract_rows, preferred_element_type=jnp.float32)
-    levels = lax.axis_size("dp").bit_length() - 1
+    workers = lax.axis_size("dp")
+    shards = lax.axis_size("tensor")
+    levels = workers.bit_length() - 1
+    shard_levels = shards.bit_length() - 1
+    gathered = min(levels, gather_levels_limit)
+    members = 2**gathered
+    others = workers // members
     position = lax.axis_index("dp")
-
-    def flag_of(section):
-        return position >> levels - 1 - section & 1
-
-    upper_flag = flag_of(0)
-    keep_second, send_second = split_piece(second, upper_flag)
-    got_second = from_partner(send_second.astype(jnp.bfloat16), "dp", levels - 1).astype(
-        send_second.dtype
-    )
-    first = lax.dot_general(inputs, dpre, contract_rows, preferred_element_type=jnp.float32)
-    keep_first, send_first = split_piece(first, upper_flag)
-    got_first = from_partner(send_first, "dp", levels - 1)
-    pieces = combine((keep_first, keep_second), (got_first, got_second), upper_flag, 0, levels)
-    begin = 1
-    for section in range(begin, levels):
-        upper_flag = flag_of(section)
+    shard = lax.axis_index("tensor")
+
+    if others == 1:
+        groups = None
+    else:
+        groups = [
+            [(m * others + r) * shards + t for m in range(members) for t in range(shards)]
+            for r in range(others)
+        ]
+
+    def gather_rows(part):
+        return lax.all_gather(part, ("dp", "tensor"), axis_index_groups=groups, tiled=True)
+
+    part_rows = row_count // shards
+    part = 0
+    for bit in range(shard_levels):
+        part = part * 2 + (shard >> bit & 1)
+    inputs_part = lax.dynamic_slice_in_dim(inputs, part * part_rows, part_rows, 0)
+    targets_part = lax.dynamic_slice_in_dim(targets, part * part_rows, part_rows, 0)
+    all_inputs = gather_rows(inputs_part)
+
+    hidden = activate(jnp.dot(inputs, w_in, preferred_element_type=jnp.float32)).astype(jnp.bfloat16)
+    summed = jnp.dot(hidden, w_out, preferred_element_type=jnp.float32)
+    for bit in range(shard_levels):
+        keep, send = split_piece(summed, shard >> bit & 1)
+        summed = keep + from_partner(send, "tensor", bit)
+    error = ((summed - targets_part.astype(jnp.float32)) / row_count).astype(jnp.bfloat16)
+    all_errors = gather_rows(error)
+
+    all_preact = jnp.dot(all_inputs, w_in, preferred_element_type=jnp.float32)
+    all_hidden, pullback = jax.vjp(activate, all_preact)
+    all_hidden = all_hidden.astype(jnp.bfloat16)
+    back = jnp.dot(all_errors, w_out.T, preferred_element_type=jnp.float32)
+    all_dpre = pullback(back)[0].astype(jnp.bfloat16)
+
+    member = position // others
+    width = inputs.shape[1] // members
+    by_member = (members, row_count, -1)
+
+    def gradient_rows(left, right):
+        own = lax.dynamic_slice_in_dim(left, member * width, width, 1)
+        return lax.dot_general(
+            own.reshape(by_member),
+            right.reshape(by_member),
+            (((1,), (1,)), ((0,), (0,))),
+            preferred_element_type=jnp.float32,
+        )
+
+    first = gradient_rows(all_inputs, all_dpre)
+    second = gradient_rows(all_errors, all_hidden)
+    totals = group_total(jnp.sum(gram(first, second), axis=1), gathered - 1, levels)
+    pieces = merge(totals, first, second)
+
+    for section in range(gathered, levels):
+        upper_flag = position >> levels - 1 - section & 1
         keep_first, send_first = split_piece(pieces[0], upper_flag)
         keep_second, send_second = split_piece(pieces[1], upper_flag)
         got_first, got_second = from_partner((send_first, send_second), "dp", levels - 1 - section)

time: 532 us -> 371 us (0.70)
  waiting for transfers between devices: 386 us -> 172 us
  matrix products: 28.8 us -> 92.8 us
  other arithmetic: 32.1 us -> 4.82 us
  blocking collectives: 16.9 us -> 38.4 us
  between operations: 33.1 us -> 14.1 us
  Pallas kernels: 0 us -> 18.1 us
  starting transfers between devices: 15.3 us -> 3.4 us
  local copies, waits for them, and re-layouts: 19.5 us -> 27 us
    ppermute x12 -> x2, waiting for transfers between devices: 307 us -> 34.4 us  [from_partner(): return lax.ppermute(value, axis, pairs)]
    all_gather x0 -> x2, waiting for transfers between devices: none -> 138 us  [gather_rows(): lax.all_gather(part, ('dp', 'tensor'), axis_index_groups=groups, tiled=True)]
    psum x1 -> x0, waiting for transfers between devices: 78.7 us -> none  [on_device(): whole = lax.psum(partial_out, 'tensor')]
    dot_general x4 -> x5, matrix products: 28.8 us -> 92.8 us  [the longest x1 42.6 us: on_device(): back = jnp.dot(all_errors, w_out.T, preferred_element_type=jnp.float32)]
    psum x3 -> x1, blocking collectives: 16.9 us -> 38.4 us  [group_total(): return lax.psum(values, ('dp', 'tensor'))]
    reduce_sum x6 -> x1, other arithmetic: 18.6 us -> 0.11 us  [on_device(): jnp.sum(gram(first, second), axis=1)]
    pallas_call x0 -> x2, Pallas kernels: none -> 18.1 us  [the longest x1 13.9 us: gram(): pl.pallas_call(functools.partial(gram_kernel, count), grid=(rows // block...]
    dynamic_slice x0 -> x3, local copies, waits for them, and re-layouts: none -> 13.5 us  [the longest x2 11.5 us: gradient_rows(): own = lax.dynamic_slice_in_dim(left, member * width, width, 1)]
  transfers between devices with their start and end apart: 13 -> 4, of which waited for: 12 -> 4; matrix products, arithmetic and copies ran while one was open for 4% -> 13% of each run, Pallas kernels for 0% -> 0%
where the time goes in v1:
time: 371 us
  waiting for transfers between devices  172 us (46%)
  matrix products  92.8 us (25%)
  blocking collectives  38.4 us (10%)
  local copies, waits for them, and re-layouts  27 us (7%)
  Pallas kernels  18.1 us (5%)
  between operations  14.1 us (4%)
  other arithmetic  4.82 us (1%)
    all_gather x2, waiting for transfers between devices, gather_rows(): lax.all_gather(part, ('dp', 'tensor'), axis_index_groups=groups, tiled=True)  138 us
    dot_general x1, matrix products, on_device(): back = jnp.dot(all_errors, w_out.T, preferred_element_type=jnp.float32)  42.6 us
    psum x1, blocking collectives, group_total(): return lax.psum(values, ('dp', 'tensor'))  38.4 us
    ppermute x2, waiting for transfers between devices, from_partner(): return lax.ppermute(value, axis, pairs)  34.4 us
    dot_general x1, matrix products, on_device(): all_preact = jnp.dot(all_inputs, w_in, preferred_element_type=jnp.float32)  25.5 us
    dot_general x2, matrix products, gradient_rows(): lax.dot_general(own.reshape(by_member), right.reshape(by_member), (((1,),...  15.5 us
    pallas_call x1, Pallas kernels, gram(): pl.pallas_call(functools.partial(gram_kernel, count), grid=(rows // block...  13.9 us
    dynamic_slice x2, local copies, waits for them, and re-layouts, gradient_rows(): own = lax.dynamic_slice_in_dim(left, member * width, width, 1)  11.5 us
  transfers between devices with their start and end apart: 4, of which 4 were waited for; matrix products, arithmetic and copies ran while one was open for 13% of the time, Pallas kernels for 0%

profile of v1, /device:TPU:0, one launch (start us, length us, event | category | flops | bytes accessed | tf_op | source)
XLA Modules:
  0.0 371.1 jit_solution(6272013295519258736)
XLA Ops:
  7.2 0.0 copy-start
  7.2 0.0 all-gather.3.cloned.1.call-start
  7.2 2.0 constant_dynamic-slice_fusion.4
  9.2 0.0 all-gather.3.cloned.1.call-update
  9.2 0.0 all-gather.5.cloned.1.call-start
  9.3 9.2 %fusion.15 = f32[704,1280]{1,0:T(8,128)} fusion(bf16[1280,1280]{1,0:T(8,128)(2,1)S(1)} %copy-done, bf16[704,1280]{1,0:T(8,128)(2,1)} %param.4, bf16[1280,1280]{1,0:T(8,128)(2,1)} %param.6), kind=kOutput, calls=%fused_computation.19 | convolution fusion | flops 4621844480 | bytes 11960320 | tf_op jit(solution)/shard_map/dot_general | solution.py:194
  18.5 2.9 constant_dynamic-slice_fusion.2
  21.4 0.5 collective-permute-start
  21.8 3.7 collective-permute-done
  25.6 2.2 dynamic-slice_add_fusion
  27.8 1.2 copy-done.6
  29.0 1.0 constant_dynamic-slice_fusion.1
  30.0 2.9 collective-permute-start.1
  32.9 30.7 %collective-permute-done.1 = f32[176,1280]{1,0:T(8,128)} collective-permute-done((f32[176,1280]{1,0:T(8,128)}, f32[176,1280]{1,0:T(8,128)}, u32[]{:S(2)}, u32[]{:S(2)}) %collective-permute-start.1) | collective-permute-done | bytes 901152 | tf_op jit(solution)/shard_map/ppermute | solution.py:17
  63.6 2.5 multiply_convert_fusion.1
  66.1 0.0 all-gather.5.cloned.1.call-update
  66.1 62.9 %all-gather.3.cloned.1.call-done = bf16[5632,1280]{1,0:T(8,128)(2,1)} async-done(((bf16[176,1280]{1,0:T(8,128)(2,1)}), bf16[5632,1280]{1,0:T(8,128)(2,1)}) %all-gather.3.cloned.1.call-update) | async-done | bytes 14417936 | tf_op jit(solution)/shard_map/all_gather | solution.py:183
  129.0 5.4 %constant_dynamic-slice_fusion.3 = bf16[5632,160]{1,0:T(8,128)(2,1)} fusion(bf16[5632,1280]{1,0:T(8,128)(2,1)} %all-gather.3.cloned.1.call-done, s32[]{:T(128)S(6)} %select_n.24), kind=kLoop, calls=%fused_computation.29 | loop fusion | bytes 3604484 | tf_op jit(solution)/shard_map/dynamic_slice | solution.py:212
  134.4 0.0 copy-done.7
  134.4 25.5 %fusion.27 = f32[5632,1280]{1,0:T(8,128)} fusion(bf16[5632,1280]{1,0:T(8,128)(2,1)} %all-gather.3.cloned.1.call-done, bf16[1280,1280]{1,0:T(8,128)(2,1)S(1)} %copy-done.7), kind=kOutput, calls=%fused_computation.36 | convolution fusion | flops 18454937600 | bytes 46530560 | tf_op jit(solution)/shard_map/dot_general | solution.py:201
  159.9 75.1 %all-gather.5.cloned.1.call-done = bf16[5632,1280]{1,0:T(8,128)(2,1)} async-done(((bf16[176,1280]{1,0:T(8,128)(2,1)}), bf16[5632,1280]{1,0:T(8,128)(2,1)}) %all-gather.5.cloned.1.call-update) | async-done | bytes 14417936 | tf_op jit(solution)/shard_map/all_gather | solution.py:183
  235.0 42.6 %multiply_convert_fusion = (bf16[5632,1280]{1,0:T(8,128)(2,1)}, bf16[5632,1280]{1,0:T(8,128)(2,1)}) fusion(f32[5632,1280]{1,0:T(8,128)} %fusion.27, bf16[5632,1280]{1,0:T(8,128)(2,1)} %all-gather.5.cloned.1.call-done, bf16[1280,1280]{1,0:T(8,128)(2,1)S(1)} %copy-done), kind=kOutput, calls=%fused_computation.9 | convolution fusion | flops 18613534720 | bytes 75366400 | tf_op jit(solution)/shard_map/dot_general | solution.py:204
  277.6 8.8 %fusion.28.first_ref = f32[8,160,1280]{2,1,0:T(8,128)S(1)} fusion(bf16[8,704,160]{2,1,0:T(8,128)(2,1)} %bitcast.17, bf16[8,704,1280]{2,1,0:T(8,128)(2,1)} %bitcast.16), kind=kOutput, calls=%fused_computation.37 | convolution fusion | flops 2306867200 | bytes 22773760 | tf_op jit(solution)/shard_map/dot_general | solution.py:213
  286.4 6.1 %constant_dynamic-slice_fusion = bf16[5632,160]{1,0:T(8,128)(2,1)S(1)} fusion(bf16[5632,1280]{1,0:T(8,128)(2,1)} %all-gather.5.cloned.1.call-done, s32[]{:T(128)S(6)} %select_n.24), kind=kLoop, calls=%fused_computation.26 | loop fusion | bytes 3604484 | tf_op jit(solution)/shard_map/dynamic_slice | solution.py:212
  292.5 6.6 %fusion.29.second_ref = f32[8,160,1280]{2,1,0:T(8,128)S(1)} fusion(bf16[8,704,160]{2,1,0:T(8,128)(2,1)S(1)} %bitcast.18, bf16[8,704,1280]{2,1,0:T(8,128)(2,1)} %bitcast.15), kind=kOutput, calls=%fused_computation.38 | convolution fusion | flops 2306867200 | bytes 22773760 | tf_op jit(solution)/shard_map/dot_general | solution.py:213
  299.1 13.9 %gram.1 = f32[36,128]{1,0:T(8,128)S(1)} custom-call(f32[8,160,1280]{2,1,0:T(8,128)S(1)} %fusion.28.first_ref, f32[8,160,1280]{2,1,0:T(8,128)S(1)} %fusion.29.second_ref), custom_call_target="tpu_custom_call" | custom-call | tf_op jit(solution)/shard_map/gram/pallas_call | solution.py:96
  313.1 2.7 copy-done.4
  315.8 0.1 reduce_sum.9
  315.9 38.4 %psum.7.totals_ref = f32[36]{0:T(128)S(1)} all-reduce(f32[36]{0:T(128)S(1)} %reduce_sum.9), channel_id=1, replica_groups=mesh['dp'=8,'tensor'=4] {'dp','tensor'}, use_global_device_ids=true, to_apply=%region_1.2 | all-reduce | flops 36 | bytes 288 | tf_op jit(solution)/shard_map/psum | solution.py:33
  354.4 2.9 copy-done.3
  357.2 2.9 copy-done.5
  360.1 4.2 %merge.1 = (f32[160,1280]{1,0:T(8,128)}, f32[160,1280]{1,0:T(8,128)}) custom-call(f32[36]{0:T(128)S(1)} %psum.7.totals_ref, f32[8,160,1280]{2,1,0:T(8,128)S(1)} %copy-done.3, f32[8,160,1280]{2,1,0:T(8,128)S(1)} %copy-done.5), custom_call_target="tpu_custom_call" | custom-call | tf_op jit(solution)/shard_map/merge/pallas_call | solution.py:151
  (10 shorter events, 0.0 us)
Async XLA Ops:
  7.2 2.1 copy-start
  7.2 121.8 %all-gather.3.cloned.1.call-start = ((), (), s32[]{:S(2)}) async-start(), calls=%async_computation | async-start | bytes 14868480 | tf_op jit(solution)/shard_map/all_gather | solution.py:183
  9.2 225.8 %all-gather.5.cloned.1.call-start = ((), (), s32[]{:S(2)}) async-start(), calls=%async_computation.1 | async-start | bytes 14868480 | tf_op jit(solution)/shard_map/all_gather | solution.py:183
  21.4 4.2 %collective-permute-start = (f32[352,1280]{1,0:T(8,128)}, f32[352,1280]{1,0:T(8,128)}, u32[]{:S(2)}, u32[]{:S(2)}) collective-permute-start(f32[352,1280]{1,0:T(8,128)} %constant_dynamic-slice_fusion.2), channel_id=1, source_target_pairs={{0,1},{1,0},{2,3},{3,2},{4,5},{5,4},{6,7},{7,6},{8,9},{9,8},{10,11... | collective-permute-start | bytes 5406728 | tf_op jit(solution)/shard_map/ppermute | solution.py:17
  27.8 1.2 copy-start.6
  30.0 33.6 %collective-permute-start.1 = (f32[176,1280]{1,0:T(8,128)}, f32[176,1280]{1,0:T(8,128)}, u32[]{:S(2)}, u32[]{:S(2)}) collective-permute-start(f32[176,1280]{1,0:T(8,128)} %constant_dynamic-slice_fusion.1), channel_id=1, source_target_pairs={{0,2},{1,3},{2,0},{3,1},{4,6},{5,7},{6,4},{7,5},{8,10},{9,11},{10,... | collective-permute-start | bytes 2703368 | tf_op jit(solution)/shard_map/ppermute | solution.py:17
  129.0 5.4 %copy-start.7 = (bf16[1280,1280]{1,0:T(8,128)(2,1)S(1)}, bf16[1280,1280]{1,0:T(8,128)(2,1)}, u32[]{:S(2)}) copy-start(bf16[1280,1280]{1,0:T(8,128)(2,1)} %param.6) | copy-start | bytes 9830404
  286.4 12.7 %copy-start.2 = (f32[8,160,1280]{2,1,0:T(8,128)}, f32[8,160,1280]{2,1,0:T(8,128)S(1)}, u32[]{:S(2)}) copy-start(f32[8,160,1280]{2,1,0:T(8,128)S(1)} %fusion.28.first_ref) | copy-start | bytes 19660804
  313.1 2.7 copy-start.4
  315.9 48.4 %copy-start.1 = (bf16[1280,1280]{1,0:T(8,128)(2,1)S(1)}, bf16[1280,1280]{1,0:T(8,128)(2,1)}, u32[]{:S(2)}) copy-start(bf16[1280,1280]{1,0:T(8,128)(2,1)} %param.7) | copy-start | bytes 9830404
  354.4 2.9 copy-start.3
  357.2 2.9 copy-start.5
Sparse Core Ops, SparseCore 0:
  11.4 117.5 all-gather.2
  132.4 102.5 all-gather.4

commit v2 on v0

v2 whole, which is shorter than its diff:
```python
import functools
import math

import jax
import jax.numpy as jnp
from jax import lax
from jax.experimental import pallas as pl
from jax.experimental.pallas import tpu as pltpu
from jax.sharding import PartitionSpec as P

epsilon = 1e-06
gather_levels_limit = 3
vmem_bytes = 40 * 2**20


def from_partner(value, axis, distance):
    mask = 2**distance
    pairs = [(source, source ^ mask) for source in range(lax.axis_size(axis))]
    return lax.ppermute(value, axis, pairs)


def from_mask(value, dp_mask, tensor_mask):
    shards = lax.axis_size("tensor")
    mask = dp_mask * shards + tensor_mask
    pairs = [(source, source ^ mask) for source in range(lax.axis_size("dp") * shards)]
    return lax.ppermute(value, ("dp", "tensor"), pairs)


def split_piece(piece, upper_flag):
    half = piece.shape[0] // 2
    keep = lax.dynamic_slice_in_dim(piece, upper_flag * half, half, 0)
    send = lax.dynamic_slice_in_dim(piece, (1 - upper_flag) * half, half, 0)
    return (keep, send)


def group_total(values, section, levels):
    summed = lax.psum(values, "tensor")
    for offset in range(section + 1):
        summed = summed + from_partner(summed, "dp", levels - 1 - offset)
    return summed


def combine(own, incoming, upper_flag, section, levels):
    product = jnp.sum(own[0] * incoming[0]) + jnp.sum(own[1] * incoming[1])
    norm_own = jnp.sum(own[0] * own[0]) + jnp.sum(own[1] * own[1])
    norm_incoming = jnp.sum(incoming[0] * incoming[0]) + jnp.sum(incoming[1] * incoming[1])
    is_upper = upper_flag == 1
    norm_low = jnp.where(is_upper, norm_incoming, norm_own)
    norm_high = jnp.where(is_upper, norm_own, norm_incoming)
    totals = group_total(jnp.stack([product, norm_low, norm_high]), section, levels)
    coef_low = 1.0 - totals[0] / (2.0 * (totals[1] + epsilon))
    coef_high = 1.0 - totals[0] / (2.0 * (totals[2] + epsilon))
    coef_own = jnp.where(is_upper, coef_high, coef_low)
    coef_incoming = jnp.where(is_upper, coef_low, coef_high)
    return (
        coef_own * own[0] + coef_incoming * incoming[0],
        coef_own * own[1] + coef_incoming * incoming[1],
    )


def tile_of(size, limit):
    return max(b for b in range(128, limit + 1, 128) if size % b == 0)


def contract(left, right, left_dim, right_dim):
    dims = (((left_dim,), (right_dim,)), ((), ()))
    return lax.dot_general(left, right, dims, preferred_element_type=jnp.float32)


def call(kernel, name, flops, operands, shapes, **spec):
    moved = sum(math.prod(a.shape) * a.dtype.itemsize for a in (*operands, *shapes))
    return pl.pallas_call(
        kernel,
        grid_spec=pltpu.PrefetchScalarGridSpec(num_scalar_prefetch=1, **spec),
        out_shape=shapes,
        compiler_params=pltpu.CompilerParams(vmem_limit_bytes=vmem_bytes),
        cost_estimate=pl.CostEstimate(flops=flops, bytes_accessed=moved, transcendentals=0),
        name=name,
    )(*operands)


def forward_kernel(place_ref, *refs):
    halves, (w_ref, hidden_ref, slope_ref) = refs[:-3], refs[-3:]
    for n, half in enumerate(halves):
        rows = half.shape[0]
        start = pl.multiple_of(jnp.bitwise_xor(place_ref[0], n) * rows, 16)
        if len(halves) == 1:
            start = 0
        v = jnp.dot(half[...], w_ref[...], preferred_element_type=jnp.float32)
        scale = math.sqrt(2.0 / math.pi)
        square = v * v
        t = jnp.tanh(v * (scale + (scale * 0.044715) * square))
        upper = 0.5 + 0.5 * t
        slope = upper + (0.5 * v) * (1.0 - t * t) * (scale + (3.0 * scale * 0.044715) * square)
        hidden_ref[pl.ds(start, rows), :] = (v * upper).astype(jnp.bfloat16)
        slope_ref[pl.ds(start, rows), :] = slope


def forward(place, halves, w_in):
    rows = sum(h.shape[0] for h in halves)
    depth, width = w_in.shape
    tile = tile_of(width, 256)
    out_spec = pl.BlockSpec((rows, tile), lambda n, s: (0, n))
    return call(
        forward_kernel,
        "forward",
        2 * rows * depth * width,
        (place, *halves, w_in),
        [
            jax.ShapeDtypeStruct((rows, width), jnp.bfloat16),
            jax.ShapeDtypeStruct((rows, width), jnp.float32),
        ],
        grid=(width // tile,),
        in_specs=[pl.BlockSpec(h.shape, lambda n, s: (0, 0)) for h in halves]
        + [pl.BlockSpec((depth, tile), lambda n, s: (0, n))],
        out_specs=[out_spec, out_spec],
    )


def output_kernel(place_ref, hidden_ref, w_ref, out_ref):
    out_ref[...] = jnp.dot(hidden_ref[...], w_ref[...], preferred_element_type=jnp.float32)


def output_half(index, hidden, w_out):
    rows = hidden.shape[0] // 2
    depth, width = w_out.shape
    tile = tile_of(width, 256)
    return call(
        output_kernel,
        "output_half",
        2 * rows * depth * width,
        (index, hidden, w_out),
        [jax.ShapeDtypeStruct((rows, width), jnp.float32)],
        grid=(width // tile,),
        in_specs=[
            pl.BlockSpec((rows, depth), lambda n, s: (s[0], 0)),
            pl.BlockSpec((depth, tile), lambda n, s: (0, n)),
        ],
        out_specs=[pl.BlockSpec((rows, tile), lambda n, s: (0, n))],
    )[0]


def gradient_kernel(shape, place_ref, *refs):
    blocks, halves, window, earlier, width, step_rows = shape
    refs = list(refs)

    def take(n):
        taken = refs[:n]
        del refs[:n]
        return taken

    error_refs = take(blocks)
    input_refs = [take(window) for _ in range(halves)]
    hidden_ref, slope_ref, w_ref = take(3)
    old_first, old_second = take(earlier), take(earlier)
    first_ref, second_ref, products_ref = take(3)
    errors, own_inputs, own_errors, spread, totals = refs
    step = pl.program_id(0)

    @pl.when(step == 0)
    def _():
        totals[...] = jnp.zeros_like(totals)
        part = place_ref[1]
        for n, block in enumerate(error_refs):
            rows = block.shape[0]
            start = pl.multiple_of(place_ref[4 + n] * rows, 16)
            errors[pl.ds(start, rows), :] = block[...]
        for n, pieces in enumerate(input_refs):
            rows = pieces[0].shape[0]
            start = pl.multiple_of(jnp.bitwise_xor(place_ref[0], n) * rows, 16)
            if halves == 1:
                start = 0
            for m, piece in enumerate(pieces):
                own_inputs[pl.ds(start, rows), m * 128 : (m + 1) * 128] = piece[...]
        lane = pl.multiple_of(place_ref[2] * 128, 128)
        own_errors[...] = errors[:, pl.ds(lane, window * 128)]

    shift = pl.multiple_of(place_ref[3], step_rows)
    back = contract(errors[...], w_ref[...], 1, 1)
    dpre = (back * slope_ref[...]).astype(jnp.bfloat16)
    spread[...] = contract(own_inputs[...], dpre, 0, 0)
    first_ref[...] = spread[pl.ds(shift, width), :]
    spread[...] = contract(own_errors[...], hidden_ref[...], 0, 0)
    second_ref[...] = spread[pl.ds(shift, width), :]

    first, second = first_ref[...], second_ref[...]
    for n in range(earlier + 1):
        f = first if n == earlier else old_first[n][...]
        s = second if n == earlier else old_second[n][...]
        both = first * f + second * s
        totals[n] += jnp.sum(both.reshape(width // 8, 8, -1), axis=0)

    @pl.when(step == pl.num_programs(0) - 1)
    def _():
        products_ref[...] = jnp.zeros_like(products_ref)
        for n in range(earlier + 1):
            lanes = jnp.sum(totals[n], axis=0, keepdims=True)
            products_ref[n : n + 1, :] = sum(
                lanes[:, i : i + 128] for i in range(0, lanes.shape[1], 128)
            )


def gradient(place, members, blocks, inputs, hidden, slope, w_out, first, second):
    rows, width = hidden.shape
    depth = w_out.shape[1]
    own = depth // members
    step_rows = math.gcd(own, 128)
    reach = max(m * own % 128 + own for m in range(members))
    window = -(-reach // 128)
    tile = tile_of(width, 256)
    earlier = len(first)
    shape = (len(blocks), len(inputs), window, earlier, own, step_rows)

    def lanes(offset):
        return lambda n, s: (0, s[2] + offset)

    whole = lambda n, s: (0, 0)
    column = lambda n, s: (0, n)
    old_spec = [pl.BlockSpec((own, tile), column)] * earlier
    return call(
        functools.partial(gradient_kernel, shape),
        "gradient",
        2 * rows * depth * width + 4 * rows * own * width,
        (
            place,
            *blocks,
            *[half for half in inputs for _ in range(window)],
            hidden,
            slope,
            w_out,
            *first,
            *second,
        ),
        [
            jax.ShapeDtypeStruct((own, width), jnp.float32),
            jax.ShapeDtypeStruct((own, width), jnp.float32),
            jax.ShapeDtypeStruct((members, 128), jnp.float32),
        ],
        grid=(width // tile,),
        in_specs=[pl.BlockSpec(b.shape, whole) for b in blocks]
        + [pl.BlockSpec((h.shape[0], 128), lanes(m)) for h in inputs for m in range(window)]
        + [
            pl.BlockSpec((rows, tile), column),
            pl.BlockSpec((rows, tile), column),
            pl.BlockSpec((tile, depth), lambda n, s: (n, 0)),
        ]
        + old_spec
        + old_spec,
        out_specs=[
            pl.BlockSpec((own, tile), column),
            pl.BlockSpec((own, tile), column),
            pl.BlockSpec((members, 128), whole),
        ],
        scratch_shapes=[
            pltpu.VMEM((rows, depth), jnp.bfloat16),
            pltpu.VMEM((rows, window * 128), jnp.bfloat16),
            pltpu.VMEM((rows, window * 128), jnp.bfloat16),
            pltpu.VMEM((window * 128, tile), jnp.float32),
            pltpu.VMEM((earlier + 1, 8, tile), jnp.float32),
        ],
    )


def tree_weights(count, entry):
    def inner(a, b):
        total = 0.0
        for i, u in a.items():
            for j, v in b.items():
                total = total + u * v * entry(i, j)
        return total

    items = [{i: 1.0} for i in range(count)]
    while len(items) > 1:
        half = len(items) // 2
        merged = []
        for low, high in zip(items[:half], items[half:]):
            product = inner(low, high)
            scale_low = 1.0 - product / (2.0 * (jnp.maximum(inner(low, low), 0.0) + epsilon))
            scale_high = 1.0 - product / (2.0 * (jnp.maximum(inner(high, high), 0.0) + epsilon))
            joined = {i: u * scale_low for i, u in low.items()}
            joined.update({i: u * scale_high for i, u in high.items()})
            merged.append(joined)
        items = merged
    return [items[0][i] for i in range(count)]


def merge_kernel(count, totals_ref, *refs):
    weights = tree_weights(count, lambda i, j: totals_ref[max(i, j), min(i, j)])
    for n in range(2):
        sources = refs[n * count : (n + 1) * count]
        total = weights[0] * sources[0][...]
        for i in range(1, count):
            total = total + weights[i] * sources[i][...]
        refs[2 * count + n][...] = total


def merge(totals, first, second):
    count = len(first)
    rows, width = first[0].shape
    block = max(b for b in range(8, min(rows, 32) + 1, 8) if rows % b == 0)
    spec = pl.BlockSpec((block, width), lambda i: (i, 0))
    shape = jax.ShapeDtypeStruct((rows, width), jnp.float32)
    return pl.pallas_call(
        functools.partial(merge_kernel, count),
        grid=(rows // block,),
        in_specs=[pl.BlockSpec(memory_space=pltpu.SMEM)] + [spec] * (2 * count),
        out_specs=[spec, spec],
        out_shape=[shape, shape],
        compiler_params=pltpu.CompilerParams(vmem_limit_bytes=vmem_bytes),
        name="merge",
    )(totals, *first, *second)


def relabel(matrix, mask):
    bits = matrix.shape[0].bit_length() - 1
    axes = [bits - 1 - b for b in range(bits) if mask >> b & 1]
    cube = matrix.reshape((2,) * (2 * bits))
    return lax.rev(cube, axes + [bits + a for a in axes]).reshape(matrix.shape)


def on_device(inputs, targets, w_in, w_out):
    row_count = inputs.shape[0]
    workers = lax.axis_size("dp")
    shards = lax.axis_size("tensor")
    levels = workers.bit_length() - 1
    shard_levels = shards.bit_length() - 1
    gathered = min(levels, gather_levels_limit)
    members = 2**gathered
    others = workers // members
    position = lax.axis_index("dp")
    shard = lax.axis_index("tensor")
    member = position // others

    def part_of(index):
        part = 0
        for bit in range(shard_levels):
            part = part * 2 + (index >> bit & 1)
        return part

    near = shard & 1
    part_rows = row_count // shards
    half_rows = row_count // 2
    own = inputs.shape[1] // members
    place = jnp.stack(
        [near, part_of(shard), member * own // 128, member * own % 128]
        + [part_of(shard ^ mask) for mask in range(shards)]
    ).astype(jnp.int32)

    own_half = lax.dynamic_slice_in_dim(inputs, near * half_rows, half_rows, 0)
    near_half = {0: own_half}
    for mask in range(1, members):
        if mask == 1 or mask % 2 == 0:
            near_half[mask] = from_mask(own_half, mask * others, 0)
        else:
            near_half[mask] = from_mask(near_half[mask - 1], others, 0)
    far_half = {m: from_mask(near_half[m], 0, 1) for m in range(1, members)}

    hidden, slope = {}, {}
    hidden[0], slope[0] = forward(place, [inputs], w_in)

    got = from_mask(output_half((1 - near).reshape(1), hidden[0], w_out), 0, 1)
    summed = output_half(near.reshape(1), hidden[0], w_out) + got
    for bit in range(1, shard_levels):
        keep, send = split_piece(summed, shard >> bit & 1)
        summed = keep + from_mask(send, 0, 2**bit)
    targets_part = lax.dynamic_slice_in_dim(targets, part_of(shard) * part_rows, part_rows, 0)
    error = ((summed - targets_part.astype(jnp.float32)) / row_count).astype(jnp.bfloat16)

    for m in range(1, members):
        hidden[m], slope[m] = forward(place, [near_half[m], far_half[m]], w_in)

    errors = {(0, 0): error}
    for m in range(1, members):
        if m == 1 or m % 2 == 0:
            errors[m, 0] = from_mask(error, m * others, 0)
        else:
            errors[m, 0] = from_mask(errors[m - 1, 0], others, 0)
    for m in range(members):
        for bit in reversed(range(shard_levels)):
            for mask in [k for s, k in errors if s == m]:
                errors[m, mask | 2**bit] = from_mask(errors[m, mask], 0, 2**bit)

    first, second, products = [], [], []
    for m in range(members):
        results = gradient(
            place,
            members,
            [errors[m, k] for k in range(shards)],
            [inputs] if m == 0 else [near_half[m], far_half[m]],
            hidden[m],
            slope[m],
            w_out,
            first,
            second,
        )
        first.append(results[0])
        second.append(results[1])
        products.append(results[2])

    lower = jnp.sum(jnp.stack(products), axis=2)
    totals = lax.psum(lower + jnp.tril(lower, -1).T, "tensor")
    gathered_totals = [from_mask(totals, m * others, 0) for m in range(1, members)]
    for m, got in enumerate(gathered_totals, 1):
        totals = totals + relabel(got, m)
    pieces = merge(totals, first, second)

    for section in range(gathered, levels):
        upper_flag = position >> levels - 1 - section & 1
        keep_first, send_first = split_piece(pieces[0], upper_flag)
        keep_second, send_second = split_piece(pieces[1], upper_flag)
        got_first, got_second = from_partner((send_first, send_second), "dp", levels - 1 - section)
        pieces = combine(
            (keep_first, keep_second), (got_first, got_second), upper_flag, section, levels
        )
    return (pieces[0], pieces[1])


def solution(mesh):
    placed = (P("dp", None), P("dp", None), P(None, "tensor"), P("tensor", None))
    return jax.shard_map(
        on_device,
        mesh=mesh,
        in_specs=placed,
        out_specs=(P("dp", "tensor"), P("dp", "tensor")),
        check_vma=False,
    )
```

time: 532 us -> 366 us (0.69)
  waiting for transfers between devices: 386 us -> 88.4 us
  Pallas kernels: 0 us -> 147 us
  starting transfers between devices: 15.3 us -> 59.6 us
  local copies, waits for them, and re-layouts: 19.5 us -> 57.6 us
  between operations: 33.1 us -> 1.39 us
  matrix products: 28.8 us -> 0 us
  other arithmetic: 32.1 us -> 3.99 us
  blocking collectives: 16.9 us -> 6.35 us
    ppermute x12 -> x54, waiting for transfers between devices: 307 us -> 88.4 us  [from_mask(): return lax.ppermute(value, ('dp', 'tensor'), pairs)]
    pallas_call x0 -> x19, Pallas kernels: none -> 147 us  [the longest x18 144 us: call(): pl.pallas_call(kernel, grid_spec=pltpu.PrefetchScalarGridSpec(num_scalar_...]
    psum x1 -> x0, waiting for transfers between devices: 78.7 us -> none  [on_device(): whole = lax.psum(partial_out, 'tensor')]
    unnamed x22 -> x135, local copies, waits for them, and re-layouts: 7.54 us -> 52.6 us
    ppermute x12 -> x54, starting transfers between devices: 15.3 us -> 59.6 us  [from_mask(): return lax.ppermute(value, ('dp', 'tensor'), pairs)]
    dot_general x4 -> x0, matrix products: 28.8 us -> none  [the longest x1 13.3 us: on_device(): lax.dot_general(inputs, dpre, contract_rows, preferred_element_type=jnp.f...]
    reduce_sum x6 -> x1, other arithmetic: 18.6 us -> 0.08 us  [on_device(): lower = jnp.sum(jnp.stack(products), axis=2)]
    add x11 -> x4, other arithmetic: 13.3 us -> 1.71 us  [the longest x1 1.69 us: on_device(): summed = output_half(near.reshape(1), hidden[0], w_out) + got]
  transfers between devices with their start and end apart: 13 -> 54, of which waited for: 12 -> 9; matrix products, arithmetic and copies ran while one was open for 4% -> 2% of each run, Pallas kernels for 0% -> 34%
where the time goes in v2:
time: 366 us; the launch traced here: 365 us
  Pallas kernels  147 us (40%)
  waiting for transfers between devices  88.4 us (24%)
  starting transfers between devices  59.6 us (16%)
  local copies, waits for them, and re-layouts  57.6 us (16%)
  blocking collectives  6.35 us (2%)
  other arithmetic  3.99 us (1%)
    pallas_call x18, Pallas kernels, call(): pl.pallas_call(kernel, grid_spec=pltpu.PrefetchScalarGridSpec(num_scalar_...  144 us
    ppermute x54, waiting for transfers between devices, from_mask(): return lax.ppermute(value, ('dp', 'tensor'), pairs)  88.4 us
    ppermute x54, starting transfers between devices, from_mask(): return lax.ppermute(value, ('dp', 'tensor'), pairs)  59.6 us
    unnamed x135, local copies, waits for them, and re-layouts  52.6 us
  transfers between devices with their start and end apart: 54, of which 9 were waited for; matrix products, arithmetic and copies ran while one was open for 2% of the time, Pallas kernels for 34%

profile of v2, /device:TPU:0, one launch (start us, length us, event | category | flops | bytes accessed | tf_op | source)
XLA Modules:
  0.0 364.7 jit_solution(6414088917997428896)
XLA Ops:
  4.2 5.5 %forward.8 = (bf16[704,1280]{1,0:T(8,128)(2,1)S(1)}, f32[704,1280]{1,0:T(8,128)S(1)}) custom-call(s32[8]{0:T(128)S(1)} %stack.59.place_ref, bf16[704,1280]{1,0:T(8,128)(2,1)S(1)} %copy-done.16, bf16[1280,1280]{1,0:T(8,128)(2,1)S(1)} %copy-done.59), custom_call_target="tpu_custom_call" | custom-call | flops 2306867200 | bytes 10485792 | tf_op jit(solution)/shard_map/forward/pallas_call | solution.py:72
  11.5 3.8 %output_half.3 = f32[352,1280]{1,0:T(8,128)} custom-call(s32[1]{0:T(128)} %bitcast.7.place_ref, bf16[704,1280]{1,0:T(8,128)(2,1)S(1)} %get-tuple-element.42.hidden_ref.refs_6_, bf16[1280,1280]{1,0:T(8,128)(2,1)S(1)} %copy-done), custom_call_target="tpu_custom_call" | custom-call | flops 1153433600 | bytes 6881284 | tf_op jit(solution)/shard_map/output_half/pallas_call | solution.py:72
  17.9 2.5 collective-permute-start.9
  22.0 2.6 collective-permute-start.27
  24.8 16.6 %collective-permute-done.9.refs_0_.refs_4_.refs_5_ = bf16[352,1280]{1,0:T(8,128)(2,1)} collective-permute-done((bf16[352,1280]{1,0:T(8,128)(2,1)}, bf16[352,1280]{1,0:T(8,128)(2,1)}, u32[]{:S(2)}, u32[]{:S(2)}) %collective-permute-start.9) | collective-permute-done | bytes 901152 | tf_op jit(solution)/shard_map/ppermute | solution.py:26
  41.4 20.2 %collective-permute-done.15.refs_0_.refs_4_.refs_5_ = bf16[352,1280]{1,0:T(8,128)(2,1)} collective-permute-done((bf16[352,1280]{1,0:T(8,128)(2,1)}, bf16[352,1280]{1,0:T(8,128)(2,1)}, u32[]{:S(2)}, u32[]{:S(2)}) %collective-permute-start.15) | collective-permute-done | bytes 901152 | tf_op jit(solution)/shard_map/ppermute | solution.py:26
  61.6 23.1 %collective-permute-done.27.refs_0_.refs_4_.refs_5_ = bf16[352,1280]{1,0:T(8,128)(2,1)} collective-permute-done((bf16[352,1280]{1,0:T(8,128)(2,1)}, bf16[352,1280]{1,0:T(8,128)(2,1)}, u32[]{:S(2)}, u32[]{:S(2)}) %collective-permute-start.27) | collective-permute-done | bytes 901152 | tf_op jit(solution)/shard_map/ppermute | solution.py:26
  86.7 2.4 output_half.2
  96.6 9.8 %collective-permute-done.21.refs_0_.refs_4_.refs_5_ = bf16[352,1280]{1,0:T(8,128)(2,1)} collective-permute-done((bf16[352,1280]{1,0:T(8,128)(2,1)}, bf16[352,1280]{1,0:T(8,128)(2,1)}, u32[]{:S(2)}, u32[]{:S(2)}) %collective-permute-start.21) | collective-permute-done | bytes 901152 | tf_op jit(solution)/shard_map/ppermute | solution.py:26
  108.3 7.4 %forward.9 = (bf16[704,1280]{1,0:T(8,128)(2,1)S(1)}, f32[704,1280]{1,0:T(8,128)S(1)}) custom-call(s32[8]{0:T(128)S(1)} %stack.59.place_ref, bf16[352,1280]{1,0:T(8,128)(2,1)} %collective-permute-done.9.refs_0_.refs_4_.refs_5_, bf16[352,1280]{1,0:T(8,128)(2,1)} %collective-permute-done.10.refs_1_.refs_6_.refs_7_, bf16[1280,1280]{1,0:T(8,128)(2,1)S(1)} %copy-done.60), custom_call_target="tpu_custom_call" | custom-call | flops 2306867200 | bytes 10485792 | tf_op jit(solution)/shard_map/forward/pallas_call | solution.py:72
  120.4 5.3 %collective-permute-done.45.refs_0_.refs_4_.refs_5_ = bf16[352,1280]{1,0:T(8,128)(2,1)} collective-permute-done((bf16[352,1280]{1,0:T(8,128)(2,1)}, bf16[352,1280]{1,0:T(8,128)(2,1)}, u32[]{:S(2)}, u32[]{:S(2)}) %collective-permute-start.45) | collective-permute-done | bytes 901152 | tf_op jit(solution)/shard_map/ppermute | solution.py:26
  126.8 7.4 %forward.10 = (bf16[704,1280]{1,0:T(8,128)(2,1)S(1)}, f32[704,1280]{1,0:T(8,128)S(1)}) custom-call(s32[8]{0:T(128)S(1)} %stack.59.place_ref, bf16[352,1280]{1,0:T(8,128)(2,1)} %collective-permute-done.15.refs_0_.refs_4_.refs_5_, bf16[352,1280]{1,0:T(8,128)(2,1)} %collective-permute-done.16.refs_1_.refs_6_.refs_7_, bf16[1280,1280]{1,0:T(8,128)(2,1)S(1)} %copy-done.60), custom_call_target="tpu_custom_call" | custom-call | flops 2306867200 | bytes 10485792 | tf_op jit(solution)/shard_map/forward/pallas_call | solution.py:72
  137.3 7.4 %forward.12 = (bf16[704,1280]{1,0:T(8,128)(2,1)S(1)}, f32[704,1280]{1,0:T(8,128)S(1)}) custom-call(s32[8]{0:T(128)S(1)} %stack.59.place_ref, bf16[352,1280]{1,0:T(8,128)(2,1)} %collective-permute-done.27.refs_0_.refs_4_.refs_5_, bf16[352,1280]{1,0:T(8,128)(2,1)} %collective-permute-done.28.refs_1_.refs_6_.refs_7_, bf16[1280,1280]{1,0:T(8,128)(2,1)S(1)} %copy-done.60), custom_call_target="tpu_custom_call" | custom-call | flops 2306867200 | bytes 10485792 | tf_op jit(solution)/shard_map/forward/pallas_call | solution.py:72
  147.8 3.0 collective-permute-start.11
  150.8 7.4 %forward.14 = (bf16[704,1280]{1,0:T(8,128)(2,1)S(1)}, f32[704,1280]{1,0:T(8,128)S(1)}) custom-call(s32[8]{0:T(128)S(1)} %stack.59.place_ref, bf16[352,1280]{1,0:T(8,128)(2,1)} %collective-permute-done.39.refs_0_.refs_4_.refs_5_, bf16[352,1280]{1,0:T(8,128)(2,1)} %collective-permute-done.40.refs_1_.refs_6_.refs_7_, bf16[1280,1280]{1,0:T(8,128)(2,1)S(1)} %copy-done.60), custom_call_target="tpu_custom_call" | custom-call | flops 2306867200 | bytes 10485792 | tf_op jit(solution)/shard_map/forward/pallas_call | solution.py:72
  162.0 7.2 %forward.11 = (bf16[704,1280]{1,0:T(8,128)(2,1)S(1)}, f32[704,1280]{1,0:T(8,128)S(1)}) custom-call(s32[8]{0:T(128)S(1)} %stack.59.place_ref, bf16[352,1280]{1,0:T(8,128)(2,1)} %collective-permute-done.21.refs_0_.refs_4_.refs_5_, bf16[352,1280]{1,0:T(8,128)(2,1)S(1)} %collective-permute-done.22.refs_1_.refs_6_.refs_7_, bf16[1280,1280]{1,0:T(8,128)(2,1)S(1)} %copy-done.60), custom_call_target="tpu_custom_call" | custom-call | flops 2306867200 | bytes 10485792 | tf_op jit(solution)/shard_map/forward/pallas_call | solution.py:72
  172.3 7.2 %forward.13 = (bf16[704,1280]{1,0:T(8,128)(2,1)S(1)}, f32[704,1280]{1,0:T(8,128)S(1)}) custom-call(s32[8]{0:T(128)S(1)} %stack.59.place_ref, bf16[352,1280]{1,0:T(8,128)(2,1)} %collective-permute-done.33.refs_0_.refs_4_.refs_5_, bf16[352,1280]{1,0:T(8,128)(2,1)S(1)} %collective-permute-done.34.refs_1_.refs_6_.refs_7_, bf16[1280,1280]{1,0:T(8,128)(2,1)S(1)} %copy-done.60), custom_call_target="tpu_custom_call" | custom-call | flops 2306867200 | bytes 10485792 | tf_op jit(solution)/shard_map/forward/pallas_call | solution.py:72
  182.5 19.1 %collective-permute-start.23 = (bf16[176,1280]{1,0:T(8,128)(2,1)}, bf16[176,1280]{1,0:T(8,128)(2,1)}, u32[]{:S(2)}, u32[]{:S(2)}) collective-permute-start(bf16[176,1280]{1,0:T(8,128)(2,1)} %multiply_convert_fusion.refs_0_), channel_id=1, source_target_pairs={{0,16},{1,17},{2,18},{3,19},{4,20},{5,21},{6,22},{7,23},{8,24},{9,... | collective-permute-start | bytes 1351688 | tf_op jit(solution)/shard_map/ppermute | solution.py:26
  206.5 7.5 %forward.15 = (bf16[704,1280]{1,0:T(8,128)(2,1)S(1)}, f32[704,1280]{1,0:T(8,128)S(1)}) custom-call(s32[8]{0:T(128)S(1)} %stack.59.place_ref, bf16[352,1280]{1,0:T(8,128)(2,1)} %collective-permute-done.45.refs_0_.refs_4_.refs_5_, bf16[352,1280]{1,0:T(8,128)(2,1)S(1)} %collective-permute-done.46.refs_1_.refs_6_.refs_7_, bf16[1280,1280]{1,0:T(8,128)(2,1)S(1)} %copy-done.61), custom_call_target="tpu_custom_call" | custom-call | flops 2306867200 | bytes 10485792 | tf_op jit(solution)/shard_map/forward/pallas_call | solution.py:72
  218.2 9.2 %gradient.8 = (f32[160,1280]{1,0:T(8,128)S(1)}, f32[160,1280]{1,0:T(8,128)S(1)}, f32[8,128]{1,0:T(8,128)S(1)}) custom-call(s32[8]{0:T(128)S(1)} %stack.59.place_ref, bf16[176,1280]{1,0:T(8,128)(2,1)} %multiply_convert_fusion.refs_0_, bf16[176,1280]{1,0:T(8,128)(2,1)S(1)} %copy-done.54, bf16[176,1280]{1,0:T(8,128)(2,1)S(1)} %copy-done.52, ...), custom_call_target="tpu_custom_call" | custom-call | flops 2883584000 | bytes 15732768 | tf_op jit(solution)/shard_map/gradient/pallas_call | solution.py:72
  233.6 9.5 %gradient.9 = (f32[160,1280]{1,0:T(8,128)S(1)}, f32[160,1280]{1,0:T(8,128)S(1)}, f32[8,128]{1,0:T(8,128)S(1)}) custom-call(s32[8]{0:T(128)S(1)} %stack.59.place_ref, bf16[176,1280]{1,0:T(8,128)(2,1)} %collective-permute-done.5.refs_0_, bf16[176,1280]{1,0:T(8,128)(2,1)S(1)} %copy-done.56, bf16[176,1280]{1,0:T(8,128)(2,1)} %collective-permute-done.7.refs_2_, ...), custom_call_target="tpu_custom_call" | custom-call | flops 2883584000 | bytes 17371168 | tf_op jit(solution)/shard_map/gradient/pallas_call | solution.py:72
  244.2 9.7 %gradient.10 = (f32[160,1280]{1,0:T(8,128)S(1)}, f32[160,1280]{1,0:T(8,128)S(1)}, f32[8,128]{1,0:T(8,128)S(1)}) custom-call(s32[8]{0:T(128)S(1)} %stack.59.place_ref, bf16[176,1280]{1,0:T(8,128)(2,1)} %collective-permute-done.11.refs_0_, bf16[176,1280]{1,0:T(8,128)(2,1)S(1)} %collective-permute-done.12.refs_1_, ...), custom_call_target="tpu_custom_call" | custom-call | flops 2883584000 | bytes 19009568 | tf_op jit(solution)/shard_map/gradient/pallas_call | solution.py:72
  257.7 9.9 %gradient.11 = (f32[160,1280]{1,0:T(8,128)S(1)}, f32[160,1280]{1,0:T(8,128)S(1)}, f32[8,128]{1,0:T(8,128)S(1)}) custom-call(s32[8]{0:T(128)S(1)} %stack.59.place_ref, bf16[176,1280]{1,0:T(8,128)(2,1)} %collective-permute-done.17.refs_0_, bf16[176,1280]{1,0:T(8,128)(2,1)S(1)} %collective-permute-done.18.refs_1_, ...), custom_call_target="tpu_custom_call" | custom-call | flops 2883584000 | bytes 20647968 | tf_op jit(solution)/shard_map/gradient/pallas_call | solution.py:72
  269.0 8.0 %collective-permute-done.31.refs_2_ = bf16[176,1280]{1,0:T(8,128)(2,1)S(1)} collective-permute-done((bf16[176,1280]{1,0:T(8,128)(2,1)S(1)}, bf16[176,1280]{1,0:T(8,128)(2,1)S(1)}, u32[]{:S(2)}, u32[]{:S(2)}) %collective-permute-start.31) | collective-permute-done | bytes 450592 | tf_op jit(solution)/shard_map/ppermute | solution.py:26
  276.9 10.2 %gradient.12 = (f32[160,1280]{1,0:T(8,128)S(1)}, f32[160,1280]{1,0:T(8,128)S(1)}, f32[8,128]{1,0:T(8,128)S(1)}) custom-call(s32[8]{0:T(128)S(1)} %stack.59.place_ref, bf16[176,1280]{1,0:T(8,128)(2,1)} %collective-permute-done.23.refs_0_, bf16[176,1280]{1,0:T(8,128)(2,1)S(1)} %collective-permute-done.24.refs_1_, ...), custom_call_target="tpu_custom_call" | custom-call | flops 2883584000 | bytes 22286368 | tf_op jit(solution)/shard_map/gradient/pallas_call | solution.py:72
  287.8 10.3 %gradient.13 = (f32[160,1280]{1,0:T(8,128)S(1)}, f32[160,1280]{1,0:T(8,128)S(1)}, f32[8,128]{1,0:T(8,128)S(1)}) custom-call(s32[8]{0:T(128)S(1)} %stack.59.place_ref, bf16[176,1280]{1,0:T(8,128)(2,1)S(1)} %collective-permute-done.29.refs_0_, bf16[176,1280]{1,0:T(8,128)(2,1)S(1)} %collective-permute-done.30.refs_1_, ...), custom_call_target="tpu_custom_call" | custom-call | flops 2883584000 | bytes 23924768 | tf_op jit(solution)/shard_map/gradient/pallas_call | solution.py:72
  298.2 10.7 %gradient.14 = (f32[160,1280]{1,0:T(8,128)S(1)}, f32[160,1280]{1,0:T(8,128)S(1)}, f32[8,128]{1,0:T(8,128)S(1)}) custom-call(s32[8]{0:T(128)S(1)} %stack.59.place_ref, bf16[176,1280]{1,0:T(8,128)(2,1)S(1)} %collective-permute-done.35.refs_0_, bf16[176,1280]{1,0:T(8,128)(2,1)S(1)} %collective-permute-done.36.refs_1_, ...), custom_call_target="tpu_custom_call" | custom-call | flops 2883584000 | bytes 25563168 | tf_op jit(solution)/shard_map/gradient/pallas_call | solution.py:72
  309.9 10.9 %gradient.15 = (f32[160,1280]{1,0:T(8,128)S(1)}, f32[160,1280]{1,0:T(8,128)S(1)}, f32[8,128]{1,0:T(8,128)S(1)}) custom-call(s32[8]{0:T(128)S(1)} %stack.59.place_ref, bf16[176,1280]{1,0:T(8,128)(2,1)S(1)} %collective-permute-done.41.refs_0_, bf16[176,1280]{1,0:T(8,128)(2,1)S(1)} %collective-permute-done.42.refs_1_, ...), custom_call_target="tpu_custom_call" | custom-call | flops 2883584000 | bytes 27201568 | tf_op jit(solution)/shard_map/gradient/pallas_call | solution.py:72
  322.7 6.4 %psum.7 = f32[8,8]{1,0:T(8,128)S(1)} all-reduce(f32[8,8]{1,0:T(8,128)S(1)} %fusion), channel_id=1, replica_groups=mesh['dp'=8,'tensor'=4] {'tensor'}, use_global_device_ids=true, to_apply=%region_1.2 | all-reduce | flops 64 | bytes 512 | tf_op jit(solution)/shard_map/psum | solution.py:401
  336.4 3.8 %collective-permute-start.52 = (f32[8,8]{1,0:T(8,128)S(1)}, f32[8,8]{1,0:T(8,128)S(1)}, u32[]{:S(2)}, u32[]{:S(2)}) collective-permute-start(f32[8,8]{1,0:T(8,128)S(1)} %psum.7), channel_id=1, source_target_pairs={{0,24},{1,25},{2,26},{3,27},{4,28},{5,29},{6,30},{7,31},{8,16},{9,... | collective-permute-start | bytes 776 | tf_op jit(solution)/shard_map/ppermute | solution.py:26
  342.0 4.8 %collective-permute-done.53 = f32[8,8]{1,0:T(8,128)S(1)} collective-permute-done((f32[8,8]{1,0:T(8,128)S(1)}, f32[8,8]{1,0:T(8,128)S(1)}, u32[]{:S(2)}, u32[]{:S(2)}) %collective-permute-start.53) | collective-permute-done | bytes 288 | tf_op jit(solution)/shard_map/ppermute | solution.py:26
  360.9 3.9 %merge.1 = (f32[160,1280]{1,0:T(8,128)}, f32[160,1280]{1,0:T(8,128)}) custom-call(f32[8,8]{1,0:T(8,128)S(1)} %add_add_fusion.totals_ref, f32[160,1280]{1,0:T(8,128)S(1)} %copy-done.2, f32[160,1280]{1,0:T(8,128)S(1)} %copy-done.6, f32[160,1280]{1,0:T(8,128)S(1)} %copy-done.10, f32[160,1280]{1,0:T(8,128)S(1)} %get-tuple-element.62.refs_14_.refs_3_, ...), custom_call_target="tpu_custom_call" | custom-call | tf_op jit(solution)/shard_map/merge/pallas_call | solution.py:303
  (263 shorter events, 90.9 us)
Async XLA Ops:
  15.3 73.8 %collective-permute-start = (f32[352,1280]{1,0:T(8,128)}, f32[352,1280]{1,0:T(8,128)}, u32[]{:S(2)}, u32[]{:S(2)}) collective-permute-start(f32[352,1280]{1,0:T(8,128)} %output_half.3), channel_id=1, source_target_pairs={{0,1},{1,0},{2,3},{3,2},{4,5},{5,4},{6,7},{7,6},{8,9},{9,8},{10,11... | collective-permute-start | bytes 5406728 | tf_op jit(solution)/shard_map/ppermute | solution.py:26
  17.9 23.5 %collective-permute-start.9 = (bf16[352,1280]{1,0:T(8,128)(2,1)}, bf16[352,1280]{1,0:T(8,128)(2,1)}, u32[]{:S(2)}, u32[]{:S(2)}) collective-permute-start(bf16[352,1280]{1,0:T(8,128)(2,1)} %constant_dynamic-slice_fusion), channel_id=1, source_target_pairs={{0,4},{1,5},{2,6},{3,7},{4,0},{5,1},{6,2},{7,3},{8,12},{9,13},{10,... | collective-permute-start | bytes 2703368 | tf_op jit(solution)/shard_map/ppermute | solution.py:26
  20.4 41.2 %collective-permute-start.15 = (bf16[352,1280]{1,0:T(8,128)(2,1)}, bf16[352,1280]{1,0:T(8,128)(2,1)}, u32[]{:S(2)}, u32[]{:S(2)}) collective-permute-start(bf16[352,1280]{1,0:T(8,128)(2,1)} %constant_dynamic-slice_fusion), channel_id=1, source_target_pairs={{0,8},{1,9},{2,10},{3,11},{4,12},{5,13},{6,14},{7,15},{8,0},{9,1},... | collective-permute-start | bytes 2703368 | tf_op jit(solution)/shard_map/ppermute | solution.py:26
  22.0 62.7 %collective-permute-start.27 = (bf16[352,1280]{1,0:T(8,128)(2,1)}, bf16[352,1280]{1,0:T(8,128)(2,1)}, u32[]{:S(2)}, u32[]{:S(2)}) collective-permute-start(bf16[352,1280]{1,0:T(8,128)(2,1)} %constant_dynamic-slice_fusion), channel_id=1, source_target_pairs={{0,16},{1,17},{2,18},{3,19},{4,20},{5,21},{6,22},{7,23},{8,24},{9,... | collective-permute-start | bytes 2703368 | tf_op jit(solution)/shard_map/ppermute | solution.py:26
  24.6 70.0 %collective-permute-start.39 = (bf16[352,1280]{1,0:T(8,128)(2,1)}, bf16[352,1280]{1,0:T(8,128)(2,1)}, u32[]{:S(2)}, u32[]{:S(2)}) collective-permute-start(bf16[352,1280]{1,0:T(8,128)(2,1)} %constant_dynamic-slice_fusion), channel_id=1, source_target_pairs={{0,24},{1,25},{2,26},{3,27},{4,28},{5,29},{6,30},{7,31},{8,16},{9,... | collective-permute-start | bytes 2703368 | tf_op jit(solution)/shard_map/ppermute | solution.py:26
  41.4 54.7 %collective-permute-start.10 = (bf16[352,1280]{1,0:T(8,128)(2,1)}, bf16[352,1280]{1,0:T(8,128)(2,1)}, u32[]{:S(2)}, u32[]{:S(2)}) collective-permute-start(bf16[352,1280]{1,0:T(8,128)(2,1)} %collective-permute-done.9.refs_0_.refs_4_.refs_5_), channel_id=1, source_target_pairs={{0,1},{1,0},{2,3},{3,2},{4,5},{5,4},{6,7},{7,6},{8,9},{9,8},{10,11... | collective-permute-start | bytes 2703368 | tf_op jit(solution)/shard_map/ppermute | solution.py:26
  61.6 35.0 %collective-permute-start.16 = (bf16[352,1280]{1,0:T(8,128)(2,1)}, bf16[352,1280]{1,0:T(8,128)(2,1)}, u32[]{:S(2)}, u32[]{:S(2)}) collective-permute-start(bf16[352,1280]{1,0:T(8,128)(2,1)} %collective-permute-done.15.refs_0_.refs_4_.refs_5_), channel_id=1, source_target_pairs={{0,1},{1,0},{2,3},{3,2},{4,5},{5,4},{6,7},{7,6},{8,9},{9,8},{10,11... | collective-permute-start | bytes 2703368 | tf_op jit(solution)/shard_map/ppermute | solution.py:26
  84.7 21.7 %collective-permute-start.21 = (bf16[352,1280]{1,0:T(8,128)(2,1)}, bf16[352,1280]{1,0:T(8,128)(2,1)}, u32[]{:S(2)}, u32[]{:S(2)}) collective-permute-start(bf16[352,1280]{1,0:T(8,128)(2,1)} %collective-permute-done.15.refs_0_.refs_4_.refs_5_), channel_id=1, source_target_pairs={{0,4},{1,5},{2,6},{3,7},{4,0},{5,1},{6,2},{7,3},{8,12},{9,13},{10,... | collective-permute-start | bytes 2703368 | tf_op jit(solution)/shard_map/ppermute | solution.py:26
  89.1 28.5 %collective-permute-start.33 = (bf16[352,1280]{1,0:T(8,128)(2,1)}, bf16[352,1280]{1,0:T(8,128)(2,1)}, u32[]{:S(2)}, u32[]{:S(2)}) collective-permute-start(bf16[352,1280]{1,0:T(8,128)(2,1)} %collective-permute-done.27.refs_0_.refs_4_.refs_5_), channel_id=1, source_target_pairs={{0,4},{1,5},{2,6},{3,7},{4,0},{5,1},{6,2},{7,3},{8,12},{9,13},{10,... | collective-permute-start | bytes 2703368 | tf_op jit(solution)/shard_map/ppermute | solution.py:26
  94.6 23.5 %collective-permute-start.1 = (f32[176,1280]{1,0:T(8,128)}, f32[176,1280]{1,0:T(8,128)}, u32[]{:S(2)}, u32[]{:S(2)}) collective-permute-start(f32[176,1280]{1,0:T(8,128)} %constant_dynamic-slice_fusion.1), channel_id=1, source_target_pairs={{0,2},{1,3},{2,0},{3,1},{4,6},{5,7},{6,4},{7,5},{8,10},{9,11},{10,... | collective-permute-start | bytes 2703368 | tf_op jit(solution)/shard_map/ppermute | solution.py:26
  96.1 29.6 %collective-permute-start.45 = (bf16[352,1280]{1,0:T(8,128)(2,1)}, bf16[352,1280]{1,0:T(8,128)(2,1)}, u32[]{:S(2)}, u32[]{:S(2)}) collective-permute-start(bf16[352,1280]{1,0:T(8,128)(2,1)} %collective-permute-done.39.refs_0_.refs_4_.refs_5_), channel_id=1, source_target_pairs={{0,4},{1,5},{2,6},{3,7},{4,0},{5,1},{6,2},{7,3},{8,12},{9,13},{10,... | collective-permute-start | bytes 2703368 | tf_op jit(solution)/shard_map/ppermute | solution.py:26
  96.6 29.1 %collective-permute-start.28 = (bf16[352,1280]{1,0:T(8,128)(2,1)}, bf16[352,1280]{1,0:T(8,128)(2,1)}, u32[]{:S(2)}, u32[]{:S(2)}) collective-permute-start(bf16[352,1280]{1,0:T(8,128)(2,1)} %collective-permute-done.27.refs_0_.refs_4_.refs_5_), channel_id=1, source_target_pairs={{0,1},{1,0},{2,3},{3,2},{4,5},{5,4},{6,7},{7,6},{8,9},{9,8},{10,11... | collective-permute-start | bytes 2703368 | tf_op jit(solution)/shard_map/ppermute | solution.py:26
  106.4 19.9 %collective-permute-start.40 = (bf16[352,1280]{1,0:T(8,128)(2,1)}, bf16[352,1280]{1,0:T(8,128)(2,1)}, u32[]{:S(2)}, u32[]{:S(2)}) collective-permute-start(bf16[352,1280]{1,0:T(8,128)(2,1)} %collective-permute-done.39.refs_0_.refs_4_.refs_5_), channel_id=1, source_target_pairs={{0,1},{1,0},{2,3},{3,2},{4,5},{5,4},{6,7},{7,6},{8,9},{9,8},{10,11... | collective-permute-start | bytes 2703368 | tf_op jit(solution)/shard_map/ppermute | solution.py:26
  117.6 30.1 %collective-permute-start.22 = (bf16[352,1280]{1,0:T(8,128)(2,1)}, bf16[352,1280]{1,0:T(8,128)(2,1)S(1)}, u32[]{:S(2)}, u32[]{:S(2)}) collective-permute-start(bf16[352,1280]{1,0:T(8,128)(2,1)} %collective-permute-done.21.refs_0_.refs_4_.refs_5_), channel_id=1, source_target_pairs={{0,1},{1,0},{2,3},{3,2},{4,5},{5,4},{6,7},{7,6},{8,9},{9,8},{10,11... | collective-permute-start | bytes 2703368 | tf_op jit(solution)/shard_map/ppermute | solution.py:26
  118.1 29.6 %collective-permute-start.34 = (bf16[352,1280]{1,0:T(8,128)(2,1)}, bf16[352,1280]{1,0:T(8,128)(2,1)S(1)}, u32[]{:S(2)}, u32[]{:S(2)}) collective-permute-start(bf16[352,1280]{1,0:T(8,128)(2,1)} %collective-permute-done.33.refs_0_.refs_4_.refs_5_), channel_id=1, source_target_pairs={{0,1},{1,0},{2,3},{3,2},{4,5},{5,4},{6,7},{7,6},{8,9},{9,8},{10,11... | collective-permute-start | bytes 2703368 | tf_op jit(solution)/shard_map/ppermute | solution.py:26
  125.7 56.8 %collective-permute-start.46 = (bf16[352,1280]{1,0:T(8,128)(2,1)}, bf16[352,1280]{1,0:T(8,128)(2,1)S(1)}, u32[]{:S(2)}, u32[]{:S(2)}) collective-permute-start(bf16[352,1280]{1,0:T(8,128)(2,1)} %collective-permute-done.45.refs_0_.refs_4_.refs_5_), channel_id=1, source_target_pairs={{0,1},{1,0},{2,3},{3,2},{4,5},{5,4},{6,7},{7,6},{8,9},{9,8},{10,11... | collective-permute-start | bytes 2703368 | tf_op jit(solution)/shard_map/ppermute | solution.py:26
  125.7 35.6 %collective-permute-start.3 = (bf16[176,1280]{1,0:T(8,128)(2,1)}, bf16[176,1280]{1,0:T(8,128)(2,1)S(1)}, u32[]{:S(2)}, u32[]{:S(2)}) collective-permute-start(bf16[176,1280]{1,0:T(8,128)(2,1)} %multiply_convert_fusion.refs_0_), channel_id=1, source_target_pairs={{0,2},{1,3},{2,0},{3,1},{4,6},{5,7},{6,4},{7,5},{8,10},{9,11},{10,... | collective-permute-start | bytes 1351688 | tf_op jit(solution)/shard_map/ppermute | solution.py:26
  126.3 35.2 %collective-permute-start.5 = (bf16[176,1280]{1,0:T(8,128)(2,1)}, bf16[176,1280]{1,0:T(8,128)(2,1)}, u32[]{:S(2)}, u32[]{:S(2)}) collective-permute-start(bf16[176,1280]{1,0:T(8,128)(2,1)} %multiply_convert_fusion.refs_0_), channel_id=1, source_target_pairs={{0,4},{1,5},{2,6},{3,7},{4,0},{5,1},{6,2},{7,3},{8,12},{9,13},{10,... | collective-permute-start | bytes 1351688 | tf_op jit(solution)/shard_map/ppermute | solution.py:26
  147.8 55.3 %collective-permute-start.2 = (bf16[176,1280]{1,0:T(8,128)(2,1)}, bf16[176,1280]{1,0:T(8,128)(2,1)S(1)}, u32[]{:S(2)}, u32[]{:S(2)}) collective-permute-start(bf16[176,1280]{1,0:T(8,128)(2,1)} %multiply_convert_fusion.refs_0_), channel_id=1, source_target_pairs={{0,1},{1,0},{2,3},{3,2},{4,5},{5,4},{6,7},{7,6},{8,9},{9,8},{10,11... | collective-permute-start | bytes 1351688 | tf_op jit(solution)/shard_map/ppermute | solution.py:26
  147.8 53.8 %collective-permute-start.11 = (bf16[176,1280]{1,0:T(8,128)(2,1)}, bf16[176,1280]{1,0:T(8,128)(2,1)}, u32[]{:S(2)}, u32[]{:S(2)}) collective-permute-start(bf16[176,1280]{1,0:T(8,128)(2,1)} %multiply_convert_fusion.refs_0_), channel_id=1, source_target_pairs={{0,8},{1,9},{2,10},{3,11},{4,12},{5,13},{6,14},{7,15},{8,0},{9,1},... | collective-permute-start | bytes 1351688 | tf_op jit(solution)/shard_map/ppermute | solution.py:26
  161.3 54.0 %collective-permute-start.4 = (bf16[176,1280]{1,0:T(8,128)(2,1)S(1)}, bf16[176,1280]{1,0:T(8,128)(2,1)}, u32[]{:S(2)}, u32[]{:S(2)}) collective-permute-start(bf16[176,1280]{1,0:T(8,128)(2,1)S(1)} %collective-permute-done.3.refs_2_), channel_id=1, source_target_pairs={{0,1},{1,0},{2,3},{3,2},{4,5},{5,4},{6,7},{7,6},{8,9},{9,8},{10,11... | collective-permute-start | bytes 1351688 | tf_op jit(solution)/shard_map/ppermute | solution.py:26
  161.5 53.8 %collective-permute-start.7 = (bf16[176,1280]{1,0:T(8,128)(2,1)}, bf16[176,1280]{1,0:T(8,128)(2,1)}, u32[]{:S(2)}, u32[]{:S(2)}) collective-permute-start(bf16[176,1280]{1,0:T(8,128)(2,1)} %collective-permute-done.5.refs_0_), channel_id=1, source_target_pairs={{0,2},{1,3},{2,0},{3,1},{4,6},{5,7},{6,4},{7,5},{8,10},{9,11},{10,... | collective-permute-start | bytes 1351688 | tf_op jit(solution)/shard_map/ppermute | solution.py:26
  182.5 44.9 %collective-permute-start.23 = (bf16[176,1280]{1,0:T(8,128)(2,1)}, bf16[176,1280]{1,0:T(8,128)(2,1)}, u32[]{:S(2)}, u32[]{:S(2)}) collective-permute-start(bf16[176,1280]{1,0:T(8,128)(2,1)} %multiply_convert_fusion.refs_0_), channel_id=1, source_target_pairs={{0,16},{1,17},{2,18},{3,19},{4,20},{5,21},{6,22},{7,23},{8,24},{9,... | collective-permute-start | bytes 1351688 | tf_op jit(solution)/shard_map/ppermute | solution.py:26
  201.6 25.9 %collective-permute-start.13 = (bf16[176,1280]{1,0:T(8,128)(2,1)}, bf16[176,1280]{1,0:T(8,128)(2,1)}, u32[]{:S(2)}, u32[]{:S(2)}) collective-permute-start(bf16[176,1280]{1,0:T(8,128)(2,1)} %collective-permute-done.11.refs_0_), channel_id=1, source_target_pairs={{0,2},{1,3},{2,0},{3,1},{4,6},{5,7},{6,4},{7,5},{8,10},{9,11},{10,... | collective-permute-start | bytes 1351688 | tf_op jit(solution)/shard_map/ppermute | solution.py:26
  203.1 24.9 %collective-permute-start.17 = (bf16[176,1280]{1,0:T(8,128)(2,1)}, bf16[176,1280]{1,0:T(8,128)(2,1)}, u32[]{:S(2)}, u32[]{:S(2)}) collective-permute-start(bf16[176,1280]{1,0:T(8,128)(2,1)} %collective-permute-done.11.refs_0_), channel_id=1, source_target_pairs={{0,4},{1,5},{2,6},{3,7},{4,0},{5,1},{6,2},{7,3},{8,12},{9,13},{10,... | collective-permute-start | bytes 1351688 | tf_op jit(solution)/shard_map/ppermute | solution.py:26
  229.3 24.6 %collective-permute-start.35 = (bf16[176,1280]{1,0:T(8,128)(2,1)}, bf16[176,1280]{1,0:T(8,128)(2,1)S(1)}, u32[]{:S(2)}, u32[]{:S(2)}) collective-permute-start(bf16[176,1280]{1,0:T(8,128)(2,1)} %multiply_convert_fusion.refs_0_), channel_id=1, source_target_pairs={{0,24},{1,25},{2,26},{3,27},{4,28},{5,29},{6,30},{7,31},{8,16},{9,... | collective-permute-start | bytes 1351688 | tf_op jit(solution)/shard_map/ppermute | solution.py:26
  230.1 24.0 %collective-permute-start.25 = (bf16[176,1280]{1,0:T(8,128)(2,1)}, bf16[176,1280]{1,0:T(8,128)(2,1)S(1)}, u32[]{:S(2)}, u32[]{:S(2)}) collective-permute-start(bf16[176,1280]{1,0:T(8,128)(2,1)} %collective-permute-done.23.refs_0_), channel_id=1, source_target_pairs={{0,2},{1,3},{2,0},{3,1},{4,6},{5,7},{6,4},{7,5},{8,10},{9,11},{10,... | collective-permute-start | bytes 1351688 | tf_op jit(solution)/shard_map/ppermute | solution.py:26
  256.2 20.7 %collective-permute-start.31 = (bf16[176,1280]{1,0:T(8,128)(2,1)S(1)}, bf16[176,1280]{1,0:T(8,128)(2,1)S(1)}, u32[]{:S(2)}, u32[]{:S(2)}) collective-permute-start(bf16[176,1280]{1,0:T(8,128)(2,1)S(1)} %collective-permute-done.29.refs_0_), channel_id=1, source_target_pairs={{0,2},{1,3},{2,0},{3,1},{4,6},{5,7},{6,4},{7,5},{8,10},{9,11},{10,... | collective-permute-start | bytes 1351688 | tf_op jit(solution)/shard_map/ppermute | solution.py:26
  267.7 30.5 %collective-permute-start.36 = (bf16[176,1280]{1,0:T(8,128)(2,1)S(1)}, bf16[176,1280]{1,0:T(8,128)(2,1)S(1)}, u32[]{:S(2)}, u32[]{:S(2)}) collective-permute-start(bf16[176,1280]{1,0:T(8,128)(2,1)S(1)} %collective-permute-done.35.refs_0_), channel_id=1, source_target_pairs={{0,1},{1,0},{2,3},{3,2},{4,5},{5,4},{6,7},{7,6},{8,9},{9,8},{10,11... | collective-permute-start | bytes 1351688 | tf_op jit(solution)/shard_map/ppermute | solution.py:26
  268.3 29.9 %collective-permute-start.38 = (bf16[176,1280]{1,0:T(8,128)(2,1)S(1)}, bf16[176,1280]{1,0:T(8,128)(2,1)S(1)}, u32[]{:S(2)}, u32[]{:S(2)}) collective-permute-start(bf16[176,1280]{1,0:T(8,128)(2,1)S(1)} %collective-permute-done.37.refs_2_), channel_id=1, source_target_pairs={{0,1},{1,0},{2,3},{3,2},{4,5},{5,4},{6,7},{7,6},{8,9},{9,8},{10,11... | collective-permute-start | bytes 1351688 | tf_op jit(solution)/shard_map/ppermute | solution.py:26
  287.2 22.6 %collective-permute-start.42 = (bf16[176,1280]{1,0:T(8,128)(2,1)S(1)}, bf16[176,1280]{1,0:T(8,128)(2,1)S(1)}, u32[]{:S(2)}, u32[]{:S(2)}) collective-permute-start(bf16[176,1280]{1,0:T(8,128)(2,1)S(1)} %collective-permute-done.41.refs_0_), channel_id=1, source_target_pairs={{0,1},{1,0},{2,3},{3,2},{4,5},{5,4},{6,7},{7,6},{8,9},{9,8},{10,11... | collective-permute-start | bytes 1351688 | tf_op jit(solution)/shard_map/ppermute | solution.py:26
  287.8 22.0 %collective-permute-start.44 = (bf16[176,1280]{1,0:T(8,128)(2,1)S(1)}, bf16[176,1280]{1,0:T(8,128)(2,1)S(1)}, u32[]{:S(2)}, u32[]{:S(2)}) collective-permute-start(bf16[176,1280]{1,0:T(8,128)(2,1)S(1)} %collective-permute-done.43.refs_2_), channel_id=1, source_target_pairs={{0,1},{1,0},{2,3},{3,2},{4,5},{5,4},{6,7},{7,6},{8,9},{9,8},{10,11... | collective-permute-start | bytes 1351688 | tf_op jit(solution)/shard_map/ppermute | solution.py:26
  (86 other events, 989.5 us)

commit v3 on v2

v3 whole, which is shorter than its diff:
```python
import functools
import math

import jax
import jax.numpy as jnp
from jax import lax
from jax.experimental import pallas as pl
from jax.experimental.pallas import tpu as pltpu
from jax.sharding import PartitionSpec as P

epsilon = 1e-06
gather_levels_limit = 3
vmem_bytes = 60 * 2**20


def from_partner(value, axis, distance):
    mask = 2**distance
    pairs = [(source, source ^ mask) for source in range(lax.axis_size(axis))]
    return lax.ppermute(value, axis, pairs)


def from_mask(value, dp_mask, tensor_mask):
    shards = lax.axis_size("tensor")
    mask = dp_mask * shards + tensor_mask
    pairs = [(source, source ^ mask) for source in range(lax.axis_size("dp") * shards)]
    return lax.ppermute(value, ("dp", "tensor"), pairs)


def split_piece(piece, upper_flag):
    half = piece.shape[0] // 2
    keep = lax.dynamic_slice_in_dim(piece, upper_flag * half, half, 0)
    send = lax.dynamic_slice_in_dim(piece, (1 - upper_flag) * half, half, 0)
    return (keep, send)


def group_total(values, section, levels):
    summed = lax.psum(values, "tensor")
    for offset in range(section + 1):
        summed = summed + from_partner(summed, "dp", levels - 1 - offset)
    return summed


def combine(own, incoming, upper_flag, section, levels):
    product = jnp.sum(own[0] * incoming[0]) + jnp.sum(own[1] * incoming[1])
    norm_own = jnp.sum(own[0] * own[0]) + jnp.sum(own[1] * own[1])
    norm_incoming = jnp.sum(incoming[0] * incoming[0]) + jnp.sum(incoming[1] * incoming[1])
    is_upper = upper_flag == 1
    norm_low = jnp.where(is_upper, norm_incoming, norm_own)
    norm_high = jnp.where(is_upper, norm_own, norm_incoming)
    totals = group_total(jnp.stack([product, norm_low, norm_high]), section, levels)
    coef_low = 1.0 - totals[0] / (2.0 * (totals[1] + epsilon))
    coef_high = 1.0 - totals[0] / (2.0 * (totals[2] + epsilon))
    coef_own = jnp.where(is_upper, coef_high, coef_low)
    coef_incoming = jnp.where(is_upper, coef_low, coef_high)
    return (
        coef_own * own[0] + coef_incoming * incoming[0],
        coef_own * own[1] + coef_incoming * incoming[1],
    )


def tile_of(size, limit):
    return max(b for b in range(128, limit + 1, 128) if size % b == 0)


def contract(left, right, left_dim, right_dim):
    dims = (((left_dim,), (right_dim,)), ((), ()))
    return lax.dot_general(left, right, dims, preferred_element_type=jnp.float32)


def call(kernel, name, flops, operands, shapes, after=(), **spec):
    moved = sum(math.prod(a.shape) * a.dtype.itemsize for a in (*operands, *shapes))
    spec["in_specs"] = [pl.BlockSpec(memory_space=pl.ANY)] * len(after) + spec["in_specs"]

    def body(place_ref, *refs):
        kernel(place_ref, *refs[len(after) :])

    return pl.pallas_call(
        body,
        grid_spec=pltpu.PrefetchScalarGridSpec(num_scalar_prefetch=1, **spec),
        out_shape=shapes,
        compiler_params=pltpu.CompilerParams(vmem_limit_bytes=vmem_bytes),
        cost_estimate=pl.CostEstimate(flops=flops, bytes_accessed=moved, transcendentals=0),
        name=name,
    )(operands[0], *after, *operands[1:])


WINDOW, SHIFT, OTHER_SHIFT, MEMBER, NEAR, FAR, PARTS = range(7)


def row_start(place_ref, block, where):
    return 0 if where is None else pl.multiple_of(place_ref[where] * block.shape[0], 16)


def forward_kernel(wheres, place_ref, *refs):
    blocks, (w_ref, hidden_ref, slope_ref) = refs[:-3], refs[-3:]
    chunks = []
    for block, where in zip(blocks, wheres):
        rows = block.shape[0]
        pieces = 2 if where is None else 1
        for n in range(pieces):
            begin = n * rows // pieces
            chunks.append((block, begin, rows // pieces, row_start(place_ref, block, where) + begin))
    for block, begin, rows, start in chunks:
        left = block[begin : begin + rows, :]
        v = jnp.dot(left, w_ref[...], preferred_element_type=jnp.float32)
        scale = math.sqrt(2.0 / math.pi)
        square = v * v
        t = jnp.tanh(v * (scale + (scale * 0.044715) * square))
        upper = 0.5 + 0.5 * t
        slope = upper + (0.5 * v) * (1.0 - t * t) * (scale + (3.0 * scale * 0.044715) * square)
        hidden_ref[pl.ds(start, rows), :] = (v * upper).astype(jnp.bfloat16)
        slope_ref[pl.ds(start, rows), :] = slope


def forward(place, blocks, w_in, after=()):
    arrays, wheres = zip(*blocks)
    rows = sum(a.shape[0] for a in arrays)
    depth, width = w_in.shape
    tile = tile_of(width, 256)
    out_spec = pl.BlockSpec((rows, tile), lambda n, s: (0, n))
    return call(
        functools.partial(forward_kernel, wheres),
        "forward",
        2 * rows * depth * width,
        (place, *arrays, w_in),
        [
            jax.ShapeDtypeStruct((rows, width), jnp.bfloat16),
            jax.ShapeDtypeStruct((rows, width), jnp.float32),
        ],
        after,
        grid=(width // tile,),
        in_specs=[pl.BlockSpec(a.shape, lambda n, s: (0, 0)) for a in arrays]
        + [pl.BlockSpec((depth, tile), lambda n, s: (0, n))],
        out_specs=[out_spec, out_spec],
    )


def output_kernel(place_ref, hidden_ref, w_ref, out_ref):
    out_ref[...] = jnp.dot(hidden_ref[...], w_ref[...], preferred_element_type=jnp.float32)


def output_half(index, hidden, w_out, after=()):
    rows = hidden.shape[0] // 2
    depth, width = w_out.shape
    tile = tile_of(width, 256)
    return call(
        output_kernel,
        "output_half",
        2 * rows * depth * width,
        (index, hidden, w_out),
        [jax.ShapeDtypeStruct((rows, width), jnp.float32)],
        after,
        grid=(width // tile,),
        in_specs=[
            pl.BlockSpec((rows, depth), lambda n, s: (s[0], 0)),
            pl.BlockSpec((depth, tile), lambda n, s: (0, n)),
        ],
        out_specs=[pl.BlockSpec((rows, tile), lambda n, s: (0, n))],
    )[0]


def gradient_kernel(wheres, window, own, step_rows, place_ref, *refs):
    error_wheres, input_wheres = wheres
    refs = list(refs)

    def take(n):
        taken = refs[:n]
        del refs[:n]
        return taken

    error_refs = take(len(error_wheres))
    input_refs = [take(window) for _ in input_wheres]
    hidden_ref, slope_ref, w_ref, first_ref, second_ref, send_ref = take(6)
    errors, inputs, inputs_turned, errors_turned, spread_first, spread_second = refs

    @pl.when(pl.program_id(0) == 0)
    def _():
        for block, where in zip(error_refs, error_wheres):
            errors[pl.ds(row_start(place_ref, block, where), block.shape[0]), :] = block[...]
        for pieces, where in zip(input_refs, input_wheres):
            start = row_start(place_ref, pieces[0], where)
            for m, piece in enumerate(pieces):
                inputs[pl.ds(start, piece.shape[0]), m * 128 : (m + 1) * 128] = piece[...]
        lane = pl.multiple_of(place_ref[WINDOW] * 128, 128)
        inputs_turned[...] = inputs[...].T
        errors_turned[...] = errors[:, pl.ds(lane, window * 128)].T

    shift = pl.multiple_of(place_ref[SHIFT], step_rows)
    other_shift = pl.multiple_of(place_ref[OTHER_SHIFT], step_rows)
    back = jnp.dot(errors[...], w_ref[...], preferred_element_type=jnp.float32)
    dpre = (back * slope_ref[...]).astype(jnp.bfloat16)
    spread_second[...] = jnp.dot(
        errors_turned[...], hidden_ref[...], preferred_element_type=jnp.float32
    )
    spread_first[...] = jnp.dot(inputs_turned[...], dpre, preferred_element_type=jnp.float32)
    second_ref[...] = spread_second[pl.ds(shift, own), :]
    send_ref[own:, :] = spread_second[pl.ds(other_shift, own), :].astype(jnp.bfloat16)
    first_ref[...] = spread_first[pl.ds(shift, own), :]
    send_ref[:own, :] = spread_first[pl.ds(other_shift, own), :].astype(jnp.bfloat16)


def gradient(place, members, errors, inputs, hidden, slope, turned_w_out, after=()):
    error_arrays, error_wheres = zip(*errors)
    input_arrays, input_wheres = zip(*inputs)
    rows, width = hidden.shape
    depth = turned_w_out.shape[0]
    own = depth // members
    reach = max(m * own % 128 + 2 * own for m in range(0, members, 2))
    window = -(-reach // 128)
    tile = tile_of(width, 256)

    def lanes(offset):
        return lambda n, s: (0, s[WINDOW] + offset)

    whole = lambda n, s: (0, 0)
    column = lambda n, s: (0, n)
    return call(
        functools.partial(
            gradient_kernel, (error_wheres, input_wheres), window, own, math.gcd(own, 128)
        ),
        "gradient",
        2 * rows * depth * width + 4 * rows * window * 128 * width,
        (
            place,
            *error_arrays,
            *[a for a in input_arrays for _ in range(window)],
            hidden,
            slope,
            turned_w_out,
        ),
        [
            jax.ShapeDtypeStruct((own, width), jnp.float32),
            jax.ShapeDtypeStruct((own, width), jnp.float32),
            jax.ShapeDtypeStruct((2 * own, width), jnp.bfloat16),
        ],
        after,
        grid=(width // tile,),
        in_specs=[pl.BlockSpec(a.shape, whole) for a in error_arrays]
        + [pl.BlockSpec((a.shape[0], 128), lanes(m)) for a in input_arrays for m in range(window)]
        + [
            pl.BlockSpec((rows, tile), column),
            pl.BlockSpec((rows, tile), column),
            pl.BlockSpec((depth, tile), column),
        ],
        out_specs=[
            pl.BlockSpec((own, tile), column),
            pl.BlockSpec((own, tile), column),
            pl.BlockSpec((2 * own, tile), column),
        ],
        scratch_shapes=[
            pltpu.VMEM((rows, depth), jnp.bfloat16),
            pltpu.VMEM((rows, window * 128), jnp.bfloat16),
            pltpu.VMEM((window * 128, rows), jnp.bfloat16),
            pltpu.VMEM((window * 128, rows), jnp.bfloat16),
            pltpu.VMEM((window * 128, tile), jnp.float32),
            pltpu.VMEM((window * 128, tile), jnp.float32),
        ],
    )


def products_kernel(counts, fresh, place_ref, *refs):
    own = refs[0].shape[0]
    slots, at = [], 0
    for count in counts:
        slots.append(refs[at : at + count])
        at += count
    known_ref, out_ref, totals = refs[at:]
    pairs = [(i, j) for i in range(len(slots) - fresh, len(slots)) for j in range(i + 1)]

    @pl.when(pl.program_id(0) == 0)
    def _():
        totals[...] = jnp.zeros_like(totals)

    def values(slot):
        if len(slot) == 2:
            return slot[0][...], slot[1][...]
        return slot[0][:own, :].astype(jnp.float32), slot[0][own:, :].astype(jnp.float32)

    for n, (i, j) in enumerate(pairs):
        a, b = values(slots[i]), values(slots[j])
        both = a[0] * b[0] + a[1] * b[1]
        totals[n] += jnp.sum(both.reshape(own // 8, 8, -1), axis=0)

    @pl.when(pl.program_id(0) == pl.num_programs(0) - 1)
    def _():
        result = known_ref[...]
        row = lax.broadcasted_iota(jnp.int32, result.shape, 0)
        column = lax.broadcasted_iota(jnp.int32, result.shape, 1)
        for n, (i, j) in enumerate(pairs):
            i, j = (jnp.bitwise_xor(place_ref[MEMBER], k) for k in (i, j))
            here = ((row == i) & (column == j)) | ((row == j) & (column == i))
            result = result + jnp.where(here, jnp.sum(totals[n]), 0.0)
        out_ref[...] = result


def products(place, slots, fresh, known, after=()):
    arrays = [a for slot in slots for a in slot]
    own, width = slots[0][0].shape
    tile = tile_of(width, 256)
    pairs = sum(len(slots) - n for n in range(fresh))
    whole = lambda n, s: (0, 0)
    return call(
        functools.partial(products_kernel, [len(slot) for slot in slots], fresh),
        "products",
        4 * pairs * own * width,
        (place, *arrays, known),
        [jax.ShapeDtypeStruct(known.shape, jnp.float32)],
        after,
        grid=(width // tile,),
        in_specs=[pl.BlockSpec((a.shape[0], tile), lambda n, s: (0, n)) for a in arrays]
        + [pl.BlockSpec(known.shape, whole)],
        out_specs=[pl.BlockSpec(known.shape, whole)],
        scratch_shapes=[pltpu.VMEM((pairs, 8, tile), jnp.float32)],
    )[0]


def tree_weights(count, entry):
    def inner(a, b):
        total = 0.0
        for i, u in a.items():
            for j, v in b.items():
                total = total + u * v * entry(i, j)
        return total

    items = [{i: 1.0} for i in range(count)]
    while len(items) > 1:
        half = len(items) // 2
        merged = []
        for low, high in zip(items[:half], items[half:]):
            product = inner(low, high)
            scale_low = 1.0 - product / (2.0 * (jnp.maximum(inner(low, low), 0.0) + epsilon))
            scale_high = 1.0 - product / (2.0 * (jnp.maximum(inner(high, high), 0.0) + epsilon))
            joined = {i: u * scale_low for i, u in low.items()}
            joined.update({i: u * scale_high for i, u in high.items()})
            merged.append(joined)
        items = merged
    return [items[0][i] for i in range(count)]


def merge_kernel(counts, place_ref, totals_ref, *refs):
    refs, (first_ref, second_ref, weights_ref) = refs[:-3], refs[-3:]

    @pl.when(pl.program_id(0) == 0)
    def _():
        def entry(i, j):
            i, j = (jnp.bitwise_xor(place_ref[MEMBER], k) for k in (i, j))
            return totals_ref[i, j]

        for n, weight in enumerate(tree_weights(len(counts), entry)):
            weights_ref[n] = weight

    first = second = 0.0
    for n in range(len(counts)):
        weight = weights_ref[n]
        first = first + weight * refs[2 * n][...].astype(jnp.float32)
        second = second + weight * refs[2 * n + 1][...].astype(jnp.float32)
    first_ref[...] = first
    second_ref[...] = second


def merge(place, totals, slots):
    own, width = slots[0][0].shape
    block = max(b for b in range(16, min(own, 32) + 1, 16) if own % b == 0)
    steps = own // block
    upper = pl.BlockSpec((block, width), lambda n, s: (n, 0))
    lower = pl.BlockSpec((block, width), lambda n, s: (n + steps, 0))
    arrays, specs = [], []
    for slot in slots:
        arrays += [slot[0], slot[-1]]
        specs += [upper, upper if len(slot) == 2 else lower]
    shape = jax.ShapeDtypeStruct((own, width), jnp.float32)
    return call(
        functools.partial(merge_kernel, [len(slot) for slot in slots]),
        "merge",
        4 * len(slots) * own * width,
        (place, totals, *arrays),
        [shape, shape],
        grid=(steps,),
        in_specs=[pl.BlockSpec(memory_space=pltpu.SMEM)] + specs,
        out_specs=[upper, upper],
        scratch_shapes=[pltpu.SMEM((len(slots),), jnp.float32)],
    )


def on_device(inputs, targets, w_in, w_out):
    row_count = inputs.shape[0]
    workers = lax.axis_size("dp")
    shards = lax.axis_size("tensor")
    levels = workers.bit_length() - 1
    shard_levels = shards.bit_length() - 1
    gathered = min(levels, gather_levels_limit)
    members = 2**gathered
    others = workers // members
    position = lax.axis_index("dp")
    shard = lax.axis_index("tensor")
    member = position // others

    def part_of(index):
        part = 0
        for bit in range(shard_levels):
            part = part * 2 + (index >> bit & 1)
        return part

    near = shard & 1
    part_rows = row_count // shards
    half_rows = row_count // 2
    own = inputs.shape[1] // members
    pair_start = member // 2 * 2 * own
    place = jnp.stack(
        [
            pair_start // 128,
            pair_start % 128 + member % 2 * own,
            pair_start % 128 + (1 - member % 2) * own,
            member,
            near,
            1 - near,
        ]
        + [part_of(shard ^ mask) for mask in range(shards)]
    ).astype(jnp.int32)
    turned_w_out = w_out.T

    own_half = lax.dynamic_slice_in_dim(inputs, near * half_rows, half_rows, 0)
    own_part = lax.dynamic_slice_in_dim(inputs, part_of(shard) * part_rows, part_rows, 0)
    blocks = {0: [(inputs, None)]}
    for m in range(1, members // 2):
        if m == 1:
            got = from_mask(own_half, 2 * m * others, 0)
            blocks[m] = [(got, NEAR), (from_mask(got, 0, 1), FAR)]
        else:
            found = {0: from_mask(own_part, 2 * m * others, 0)}
            for bit in reversed(range(shard_levels)):
                for mask in list(found):
                    found[mask | 2**bit] = from_mask(found[mask], 0, 2**bit)
            blocks[m] = [(found[k], PARTS + k) for k in range(shards)]

    hidden, slope = {}, {}
    hidden[0], slope[0] = forward(place, blocks[0], w_in)

    got = from_mask(output_half((1 - near).reshape(1), hidden[0], w_out), 0, 1)
    summed = output_half(near.reshape(1), hidden[0], w_out) + got
    for bit in range(1, shard_levels):
        keep, send = split_piece(summed, shard >> bit & 1)
        summed = keep + from_mask(send, 0, 2**bit)
    targets_part = lax.dynamic_slice_in_dim(targets, part_of(shard) * part_rows, part_rows, 0)
    error = ((summed - targets_part.astype(jnp.float32)) / row_count).astype(jnp.bfloat16)

    errors = {}
    for m in range(members // 2):
        found = {0: from_mask(error, 2 * m * others, 0) if m else error}
        for bit in reversed(range(shard_levels)):
            for mask in list(found):
                found[mask | 2**bit] = from_mask(found[mask], 0, 2**bit)
        errors[m] = [(found[k], PARTS + k) for k in range(shards)]

    for m in range(1, members // 2):
        hidden[m], slope[m] = forward(place, blocks[m], w_in)

    slots = []
    totals = jnp.zeros((8, 128), jnp.float32)
    for m in range(members // 2):
        first, second, send = gradient(
            place, members, errors[m], blocks[m], hidden[m], slope[m], turned_w_out
        )
        slots.append((first, second))
        if m == members // 2 - 1:
            totals = products(place, slots, 1, totals)
        slots.append((from_mask(send, others, 0),))
        totals = products(place, slots, 1 if m == members // 2 - 1 else 2, totals)

    totals = group_total(totals, gathered - 1, levels)
    pieces = merge(place, totals, slots)

    for section in range(gathered, levels):
        upper_flag = position >> levels - 1 - section & 1
        keep_first, send_first = split_piece(pieces[0], upper_flag)
        keep_second, send_second = split_piece(pieces[1], upper_flag)
        got_first, got_second = from_partner((send_first, send_second), "dp", levels - 1 - section)
        pieces = combine(
            (keep_first, keep_second), (got_first, got_second), upper_flag, section, levels
        )
    return (pieces[0], pieces[1])


def solution(mesh):
    placed = (P("dp", None), P("dp", None), P(None, "tensor"), P("tensor", None))
    return jax.shard_map(
        on_device,
        mesh=mesh,
        in_specs=placed,
        out_specs=(P("dp", "tensor"), P("dp", "tensor")),
        check_vma=False,
    )
```

time: 366 us -> 267 us (0.73)
  local copies, waits for them, and re-layouts: 57.6 us -> 13.1 us
  starting transfers between devices: 59.6 us -> 26.7 us
  Pallas kernels: 147 us -> 135 us
  waiting for transfers between devices: 88.4 us -> 78.7 us
    unnamed x135 -> x27, local copies, waits for them, and re-layouts: 52.6 us -> 8.99 us
    ppermute x54 -> x31, starting transfers between devices: 59.6 us -> 25.1 us  [from_mask(): return lax.ppermute(value, ('dp', 'tensor'), pairs)]
    ppermute x54 -> x31, waiting for transfers between devices: 88.4 us -> 68.6 us  [from_mask(): return lax.ppermute(value, ('dp', 'tensor'), pairs)]
    pallas_call x19 -> x16, Pallas kernels: 147 us -> 135 us  [call(): pl.pallas_call(body, grid_spec=pltpu.PrefetchScalarGridSpec(num_scalar_pr...]
    ppermute x0 -> x3, waiting for transfers between devices: none -> 10.1 us  [from_partner(): return lax.ppermute(value, axis, pairs)]
  transfers between devices with their start and end apart: 54 -> 34, of which waited for: 9 -> 11; matrix products, arithmetic and copies ran while one was open for 2% -> 4% of each run, Pallas kernels for 34% -> 40%
where the time goes in v3:
time: 267 us; the launch traced here: 265 us
  Pallas kernels  135 us (51%)
  waiting for transfers between devices  78.7 us (29%)
  starting transfers between devices  26.7 us (10%)
  local copies, waits for them, and re-layouts  13.1 us (5%)
  blocking collectives  6.06 us (2%)
  other arithmetic  5.29 us (2%)
    pallas_call x16, Pallas kernels, call(): pl.pallas_call(body, grid_spec=pltpu.PrefetchScalarGridSpec(num_scalar_pr...  135 us
    ppermute x31, waiting for transfers between devices, from_mask(): return lax.ppermute(value, ('dp', 'tensor'), pairs)  68.6 us
    ppermute x31, starting transfers between devices, from_mask(): return lax.ppermute(value, ('dp', 'tensor'), pairs)  25.1 us
    ppermute x3, waiting for transfers between devices, from_partner(): return lax.ppermute(value, axis, pairs)  10.1 us
    unnamed x27, local copies, waits for them, and re-layouts  8.99 us
    psum x1, blocking collectives, group_total(): summed = lax.psum(values, 'tensor')  6.06 us
  transfers between devices with their start and end apart: 34, of which 11 were waited for; matrix products, arithmetic and copies ran while one was open for 4% of the time, Pallas kernels for 40%

profile of v3, /device:TPU:0, one launch (start us, length us, event | category | flops | bytes accessed | tf_op | source)
XLA Modules:
  0.0 265.5 jit_solution(18218359004237446277)
XLA Ops:
  1.3 9.2 %forward.4 = (bf16[704,1280]{1,0:T(8,128)(2,1)}, f32[704,1280]{1,0:T(8,128)}) custom-call(s32[10]{0:T(128)} %stack.43.place_ref, bf16[704,1280]{1,0:T(8,128)(2,1)} %refs_6_.1, bf16[1280,1280]{1,0:T(8,128)(2,1)} %refs_4_.5), custom_call_target="tpu_custom_call" | custom-call | flops 2306867200 | bytes 10485800 | tf_op jit(solution)/shard_map/forward/pallas_call | solution.py:77
  10.6 6.0 %output_half.3 = f32[352,1280]{1,0:T(8,128)} custom-call(s32[1]{0:T(128)} %bitcast.5.place_ref, bf16[704,1280]{1,0:T(8,128)(2,1)} %get-tuple-element.22.refs_0_.refs_7_, bf16[1280,1280]{1,0:T(8,128)(2,1)} %refs_1_.5), custom_call_target="tpu_custom_call" | custom-call | flops 1153433600 | bytes 6881284 | tf_op jit(solution)/shard_map/output_half/pallas_call | solution.py:77
  17.9 3.6 %collective-permute-start.17 = (bf16[176,1280]{1,0:T(8,128)(2,1)}, bf16[176,1280]{1,0:T(8,128)(2,1)}, u32[]{:S(2)}, u32[]{:S(2)}) collective-permute-start(bf16[176,1280]{1,0:T(8,128)(2,1)} %constant_dynamic-slice_fusion.1), channel_id=1, source_target_pairs={{0,16},{1,17},{2,18},{3,19},{4,20},{5,21},{6,22},{7,23},{8,24},{9,... | collective-permute-start | bytes 1351688 | tf_op jit(solution)/shard_map/ppermute | solution.py:26
  24.0 5.9 %output_half.2 = f32[352,1280]{1,0:T(8,128)} custom-call(s32[1]{0:T(128)} %bitcast.4.place_ref, bf16[704,1280]{1,0:T(8,128)(2,1)} %get-tuple-element.22.refs_0_.refs_7_, bf16[1280,1280]{1,0:T(8,128)(2,1)} %refs_1_.5), custom_call_target="tpu_custom_call" | custom-call | flops 1153433600 | bytes 6881284 | tf_op jit(solution)/shard_map/output_half/pallas_call | solution.py:77
  29.9 2.2 add.70
  35.9 16.4 %collective-permute-done.17.refs_0_.refs_4_.refs_5_.refs_6_ = bf16[176,1280]{1,0:T(8,128)(2,1)} collective-permute-done((bf16[176,1280]{1,0:T(8,128)(2,1)}, bf16[176,1280]{1,0:T(8,128)(2,1)}, u32[]{:S(2)}, u32[]{:S(2)}) %collective-permute-start.17) | collective-permute-done | bytes 450592 | tf_op jit(solution)/shard_map/ppermute | solution.py:26
  54.3 9.8 %collective-permute-done.10.refs_0_.refs_4_.refs_5_.refs_6_ = bf16[352,1280]{1,0:T(8,128)(2,1)} collective-permute-done((bf16[352,1280]{1,0:T(8,128)(2,1)}, bf16[352,1280]{1,0:T(8,128)(2,1)}, u32[]{:S(2)}, u32[]{:S(2)}) %collective-permute-start.10) | collective-permute-done | bytes 901152 | tf_op jit(solution)/shard_map/ppermute | solution.py:26
  64.1 3.2 %collective-permute-done.19.refs_2_.refs_10_.refs_11_.refs_12_ = bf16[176,1280]{1,0:T(8,128)(2,1)} collective-permute-done((bf16[176,1280]{1,0:T(8,128)(2,1)}, bf16[176,1280]{1,0:T(8,128)(2,1)}, u32[]{:S(2)}, u32[]{:S(2)}) %collective-permute-start.19) | collective-permute-done | bytes 450592 | tf_op jit(solution)/shard_map/ppermute | solution.py:26
  67.3 8.6 %collective-permute-done.28.refs_2_.refs_10_.refs_11_.refs_12_ = bf16[176,1280]{1,0:T(8,128)(2,1)} collective-permute-done((bf16[176,1280]{1,0:T(8,128)(2,1)}, bf16[176,1280]{1,0:T(8,128)(2,1)}, u32[]{:S(2)}, u32[]{:S(2)}) %collective-permute-start.28) | collective-permute-done | bytes 450592 | tf_op jit(solution)/shard_map/ppermute | solution.py:26
  76.4 2.5 multiply_convert_fusion.refs_0_
  84.9 14.8 %collective-permute-done.6.refs_0_ = bf16[176,1280]{1,0:T(8,128)(2,1)} collective-permute-done((bf16[176,1280]{1,0:T(8,128)(2,1)}, bf16[176,1280]{1,0:T(8,128)(2,1)}, u32[]{:S(2)}, u32[]{:S(2)}) %collective-permute-start.6) | collective-permute-done | bytes 450592 | tf_op jit(solution)/shard_map/ppermute | solution.py:26
  101.6 3.5 %copy.6 = bf16[1280,1280]{0,1:T(8,128)(2,1)} copy(bf16[1280,1280]{1,0:T(8,128)(2,1)S(1)} %copy-done.2) | data formatting | bytes 6553600 | tf_op args[3]
  105.1 10.6 %collective-permute-done.13.refs_0_ = bf16[176,1280]{1,0:T(8,128)(2,1)} collective-permute-done((bf16[176,1280]{1,0:T(8,128)(2,1)}, bf16[176,1280]{1,0:T(8,128)(2,1)}, u32[]{:S(2)}, u32[]{:S(2)}) %collective-permute-start.13) | collective-permute-done | bytes 450592 | tf_op jit(solution)/shard_map/ppermute | solution.py:26
  116.3 9.2 %forward.6 = (bf16[704,1280]{1,0:T(8,128)(2,1)}, f32[704,1280]{1,0:T(8,128)}) custom-call(s32[10]{0:T(128)} %stack.43.place_ref, bf16[176,1280]{1,0:T(8,128)(2,1)} %collective-permute-done.17.refs_0_.refs_4_.refs_5_.refs_6_, bf16[176,1280]{1,0:T(8,128)(2,1)} %collective-permute-done.18.refs_1_.refs_7_.refs_8_.refs_9_, ...), custom_call_target="tpu_custom_call" | custom-call | flops 2306867200 | bytes 10485800 | tf_op jit(solution)/shard_map/forward/pallas_call | solution.py:77
  125.4 9.2 %forward.7 = (bf16[704,1280]{1,0:T(8,128)(2,1)}, f32[704,1280]{1,0:T(8,128)}) custom-call(s32[10]{0:T(128)} %stack.43.place_ref, bf16[176,1280]{1,0:T(8,128)(2,1)} %collective-permute-done.26.refs_0_.refs_4_.refs_5_.refs_6_, bf16[176,1280]{1,0:T(8,128)(2,1)} %collective-permute-done.27.refs_1_.refs_7_.refs_8_.refs_9_, ...), custom_call_target="tpu_custom_call" | custom-call | flops 2306867200 | bytes 10485800 | tf_op jit(solution)/shard_map/forward/pallas_call | solution.py:77
  136.3 9.3 %forward.5 = (bf16[704,1280]{1,0:T(8,128)(2,1)}, f32[704,1280]{1,0:T(8,128)}) custom-call(s32[10]{0:T(128)} %stack.43.place_ref, bf16[352,1280]{1,0:T(8,128)(2,1)} %collective-permute-done.10.refs_0_.refs_4_.refs_5_.refs_6_, bf16[352,1280]{1,0:T(8,128)(2,1)} %collective-permute-done.11.refs_1_.refs_7_.refs_8_.refs_9_, bf16[1280,1280]{1,0:T(8,128)(2,1)} %refs_4_.5), custom_call_target="tpu_custom_call" | custom-call | flops 2306867200 | bytes 10485800 | tf_op jit(solution)/shard_map/forward/pallas_call | solution.py:77
  146.4 11.5 %gradient.4 = (f32[160,1280]{1,0:T(8,128)}, f32[160,1280]{1,0:T(8,128)}, bf16[320,1280]{1,0:T(8,128)(2,1)}) custom-call(s32[10]{0:T(128)} %stack.43.place_ref, bf16[176,1280]{1,0:T(8,128)(2,1)} %multiply_convert_fusion.refs_0_, bf16[176,1280]{1,0:T(8,128)(2,1)} %collective-permute-done.2.refs_1_, bf16[176,1280]{1,0:T(8,128)(2,1)} %collective-permute-done.3.refs_2_, ...), custom_call_target="tpu_custom_call" | custom-call | flops 3690987520 | bytes 18350120 | tf_op jit(solution)/shard_map/gradient/pallas_call | solution.py:77
  159.9 11.6 %gradient.5 = (f32[160,1280]{1,0:T(8,128)}, f32[160,1280]{1,0:T(8,128)}, bf16[320,1280]{1,0:T(8,128)(2,1)}) custom-call(s32[10]{0:T(128)} %stack.43.place_ref, bf16[176,1280]{1,0:T(8,128)(2,1)} %collective-permute-done.6.refs_0_, bf16[176,1280]{1,0:T(8,128)(2,1)} %copy-done.11, bf16[176,1280]{1,0:T(8,128)(2,1)} %collective-permute-done.8.refs_2_, ...), custom_call_target="tpu_custom_call" | custom-call | flops 3690987520 | bytes 18350120 | tf_op jit(solution)/shard_map/gradient/pallas_call | solution.py:77
  172.2 11.7 %gradient.6 = (f32[160,1280]{1,0:T(8,128)}, f32[160,1280]{1,0:T(8,128)}, bf16[320,1280]{1,0:T(8,128)(2,1)}) custom-call(s32[10]{0:T(128)} %stack.43.place_ref, bf16[176,1280]{1,0:T(8,128)(2,1)} %collective-permute-done.13.refs_0_, bf16[176,1280]{1,0:T(8,128)(2,1)} %copy-done.10, bf16[176,1280]{1,0:T(8,128)(2,1)} %copy-done.8, ...), custom_call_target="tpu_custom_call" | custom-call | flops 3690987520 | bytes 18350120 | tf_op jit(solution)/shard_map/gradient/pallas_call | solution.py:77
  186.1 11.9 %gradient.7 = (f32[160,1280]{1,0:T(8,128)}, f32[160,1280]{1,0:T(8,128)}, bf16[320,1280]{1,0:T(8,128)(2,1)}) custom-call(s32[10]{0:T(128)} %stack.43.place_ref, bf16[176,1280]{1,0:T(8,128)(2,1)} %collective-permute-done.22.refs_0_, bf16[176,1280]{1,0:T(8,128)(2,1)} %copy-done.9, bf16[176,1280]{1,0:T(8,128)(2,1)} %copy-done.7, ...), custom_call_target="tpu_custom_call" | custom-call | flops 3690987520 | bytes 18350120 | tf_op jit(solution)/shard_map/gradient/pallas_call | solution.py:77
  199.8 5.0 %products.5.refs_6_ = f32[8,128]{1,0:T(8,128)} custom-call(s32[10]{0:T(128)} %stack.43.place_ref, f32[160,1280]{1,0:T(8,128)} %get-tuple-element.24.refs_0_.refs_1_, f32[160,1280]{1,0:T(8,128)} %get-tuple-element.25.refs_1_.refs_2_, bf16[320,1280]{1,0:T(8,128)(2,1)} %copy-done, f32[8,128]{1,0:T(8,128)} %broadcast_in_dim.3.refs_3_), custom_call_target="tpu_custom_call" | custom-call | flops 2457600 | bytes 2465832 | tf_op jit(solution)/shard_map/products/pallas_call | solution.py:77
  205.7 6.0 %products.6.refs_9_ = f32[8,128]{1,0:T(8,128)} custom-call(s32[10]{0:T(128)} %stack.43.place_ref, f32[160,1280]{1,0:T(8,128)} %get-tuple-element.24.refs_0_.refs_1_, f32[160,1280]{1,0:T(8,128)} %get-tuple-element.25.refs_1_.refs_2_, bf16[320,1280]{1,0:T(8,128)(2,1)} %copy-done, f32[160,1280]{1,0:T(8,128)} %get-tuple-element.29.refs_3_.refs_5_, ...), custom_call_target="tpu_custom_call" | custom-call | flops 5734400 | bytes 4923432 | tf_op jit(solution)/shard_map/products/pallas_call | solution.py:77
  211.7 3.1 %collective-permute-done.21.refs_8_.refs_11_.refs_12_ = bf16[320,1280]{1,0:T(8,128)(2,1)S(1)} collective-permute-done((bf16[320,1280]{1,0:T(8,128)(2,1)}, bf16[320,1280]{1,0:T(8,128)(2,1)S(1)}, u32[]{:S(2)}, u32[]{:S(2)}) %collective-permute-start.21) | collective-permute-done | bytes 819232 | tf_op jit(solution)/shard_map/ppermute | solution.py:26
  215.6 7.0 %products.7.refs_11_ = f32[8,128]{1,0:T(8,128)} custom-call(s32[10]{0:T(128)} %stack.43.place_ref, f32[160,1280]{1,0:T(8,128)} %get-tuple-element.24.refs_0_.refs_1_, f32[160,1280]{1,0:T(8,128)} %get-tuple-element.25.refs_1_.refs_2_, bf16[320,1280]{1,0:T(8,128)(2,1)} %copy-done, f32[160,1280]{1,0:T(8,128)} %get-tuple-element.29.refs_3_.refs_5_, ...), custom_call_target="tpu_custom_call" | custom-call | flops 9011200 | bytes 7381032 | tf_op jit(solution)/shard_map/products/pallas_call | solution.py:77
  222.6 6.8 %products.8.refs_12_ = f32[8,128]{1,0:T(8,128)} custom-call(s32[10]{0:T(128)} %stack.43.place_ref, f32[160,1280]{1,0:T(8,128)} %get-tuple-element.24.refs_0_.refs_1_, f32[160,1280]{1,0:T(8,128)} %get-tuple-element.25.refs_1_.refs_2_, bf16[320,1280]{1,0:T(8,128)(2,1)} %copy-done, f32[160,1280]{1,0:T(8,128)} %get-tuple-element.29.refs_3_.refs_5_, ...), custom_call_target="tpu_custom_call" | custom-call | flops 5734400 | bytes 9019432 | tf_op jit(solution)/shard_map/products/pallas_call | solution.py:77
  229.4 2.1 collective-permute-done.30.refs_11_.refs_15_.refs_16_
  232.4 7.2 %products.9 = f32[8,128]{1,0:T(8,128)} custom-call(s32[10]{0:T(128)} %stack.43.place_ref, f32[160,1280]{1,0:T(8,128)} %get-tuple-element.24.refs_0_.refs_1_, f32[160,1280]{1,0:T(8,128)} %get-tuple-element.25.refs_1_.refs_2_, bf16[320,1280]{1,0:T(8,128)(2,1)} %copy-done, f32[160,1280]{1,0:T(8,128)} %get-tuple-element.29.refs_3_.refs_5_, ...), custom_call_target="tpu_custom_call" | custom-call | flops 6553600 | bytes 9838632 | tf_op jit(solution)/shard_map/products/pallas_call | solution.py:77
  239.6 6.1 %psum.7 = f32[8,128]{1,0:T(8,128)S(1)} all-reduce(f32[8,128]{1,0:T(8,128)} %products.9), channel_id=1, replica_groups=mesh['dp'=8,'tensor'=4] {'tensor'}, use_global_device_ids=true, to_apply=%region_0.1 | all-reduce | flops 1024 | bytes 8192 | tf_op jit(solution)/shard_map/psum | solution.py:37
  245.7 4.5 %collective-permute-done.31 = f32[8,128]{1,0:T(8,128)S(1)} collective-permute-done((f32[8,128]{1,0:T(8,128)S(1)}, f32[8,128]{1,0:T(8,128)S(1)}, u32[]{:S(2)}, u32[]{:S(2)}) %collective-permute-start.31) | collective-permute-done | bytes 4128 | tf_op jit(solution)/shard_map/ppermute | solution.py:19
  250.3 3.5 %collective-permute-done.32 = f32[8,128]{1,0:T(8,128)S(1)} collective-permute-done((f32[8,128]{1,0:T(8,128)S(1)}, f32[8,128]{1,0:T(8,128)S(1)}, u32[]{:S(2)}, u32[]{:S(2)}) %collective-permute-start.32) | collective-permute-done | bytes 4128 | tf_op jit(solution)/shard_map/ppermute | solution.py:19
  255.3 2.1 collective-permute-done.33
  258.0 7.3 %merge.1 = (f32[160,1280]{1,0:T(8,128)}, f32[160,1280]{1,0:T(8,128)}) custom-call(s32[10]{0:T(128)} %stack.43.place_ref, f32[8,128]{1,0:T(8,128)} %add.78.refs_0_, f32[160,1280]{1,0:T(8,128)} %get-tuple-element.24.refs_0_.refs_1_, f32[160,1280]{1,0:T(8,128)} %get-tuple-element.25.refs_1_.refs_2_, bf16[320,1280]{1,0:T(8,128)(2,1)} %copy-done, ...), custom_call_target="tpu_custom_call" | custom-call | flops 6553600 | bytes 14749736 | tf_op jit(solution)/shard_map/merge/pallas_call | solution.py:77
  (90 shorter events, 33.4 us)
Async XLA Ops:
  16.6 13.3 %collective-permute-start = (f32[352,1280]{1,0:T(8,128)}, f32[352,1280]{1,0:T(8,128)}, u32[]{:S(2)}, u32[]{:S(2)}) collective-permute-start(f32[352,1280]{1,0:T(8,128)} %output_half.3), channel_id=1, source_target_pairs={{0,1},{1,0},{2,3},{3,2},{4,5},{5,4},{6,7},{7,6},{8,9},{9,8},{10,11... | collective-permute-start | bytes 5406728 | tf_op jit(solution)/shard_map/ppermute | solution.py:26
  17.9 34.4 %collective-permute-start.17 = (bf16[176,1280]{1,0:T(8,128)(2,1)}, bf16[176,1280]{1,0:T(8,128)(2,1)}, u32[]{:S(2)}, u32[]{:S(2)}) collective-permute-start(bf16[176,1280]{1,0:T(8,128)(2,1)} %constant_dynamic-slice_fusion.1), channel_id=1, source_target_pairs={{0,16},{1,17},{2,18},{3,19},{4,20},{5,21},{6,22},{7,23},{8,24},{9,... | collective-permute-start | bytes 1351688 | tf_op jit(solution)/shard_map/ppermute | solution.py:26
  21.4 32.6 %collective-permute-start.26 = (bf16[176,1280]{1,0:T(8,128)(2,1)}, bf16[176,1280]{1,0:T(8,128)(2,1)}, u32[]{:S(2)}, u32[]{:S(2)}) collective-permute-start(bf16[176,1280]{1,0:T(8,128)(2,1)} %constant_dynamic-slice_fusion.1), channel_id=1, source_target_pairs={{0,24},{1,25},{2,26},{3,27},{4,28},{5,29},{6,30},{7,31},{8,16},{9,... | collective-permute-start | bytes 1351688 | tf_op jit(solution)/shard_map/ppermute | solution.py:26
  23.8 40.3 %collective-permute-start.10 = (bf16[352,1280]{1,0:T(8,128)(2,1)}, bf16[352,1280]{1,0:T(8,128)(2,1)}, u32[]{:S(2)}, u32[]{:S(2)}) collective-permute-start(bf16[352,1280]{1,0:T(8,128)(2,1)} %constant_dynamic-slice_fusion), channel_id=1, source_target_pairs={{0,8},{1,9},{2,10},{3,11},{4,12},{5,13},{6,14},{7,15},{8,0},{9,1},... | collective-permute-start | bytes 2703368 | tf_op jit(solution)/shard_map/ppermute | solution.py:26
  34.4 41.5 %collective-permute-start.1 = (f32[176,1280]{1,0:T(8,128)}, f32[176,1280]{1,0:T(8,128)}, u32[]{:S(2)}, u32[]{:S(2)}) collective-permute-start(f32[176,1280]{1,0:T(8,128)} %constant_dynamic-slice_fusion.2), channel_id=1, source_target_pairs={{0,2},{1,3},{2,0},{3,1},{4,6},{5,7},{6,4},{7,5},{8,10},{9,11},{10,... | collective-permute-start | bytes 2703368 | tf_op jit(solution)/shard_map/ppermute | solution.py:26
  52.3 15.0 %collective-permute-start.19 = (bf16[176,1280]{1,0:T(8,128)(2,1)}, bf16[176,1280]{1,0:T(8,128)(2,1)}, u32[]{:S(2)}, u32[]{:S(2)}) collective-permute-start(bf16[176,1280]{1,0:T(8,128)(2,1)} %collective-permute-done.17.refs_0_.refs_4_.refs_5_.refs_6_), channel_id=1, source_target_pairs={{0,2},{1,3},{2,0},{3,1},{4,6},{5,7},{6,4},{7,5},{8,10},{9,11},{10,... | collective-permute-start | bytes 1351688 | tf_op jit(solution)/shard_map/ppermute | solution.py:26
  54.1 21.9 %collective-permute-start.28 = (bf16[176,1280]{1,0:T(8,128)(2,1)}, bf16[176,1280]{1,0:T(8,128)(2,1)}, u32[]{:S(2)}, u32[]{:S(2)}) collective-permute-start(bf16[176,1280]{1,0:T(8,128)(2,1)} %collective-permute-done.26.refs_0_.refs_4_.refs_5_.refs_6_), channel_id=1, source_target_pairs={{0,2},{1,3},{2,0},{3,1},{4,6},{5,7},{6,4},{7,5},{8,10},{9,11},{10,... | collective-permute-start | bytes 1351688 | tf_op jit(solution)/shard_map/ppermute | solution.py:26
  54.3 24.6 %collective-permute-start.18 = (bf16[176,1280]{1,0:T(8,128)(2,1)}, bf16[176,1280]{1,0:T(8,128)(2,1)}, u32[]{:S(2)}, u32[]{:S(2)}) collective-permute-start(bf16[176,1280]{1,0:T(8,128)(2,1)} %collective-permute-done.17.refs_0_.refs_4_.refs_5_.refs_6_), channel_id=1, source_target_pairs={{0,1},{1,0},{2,3},{3,2},{4,5},{5,4},{6,7},{7,6},{8,9},{9,8},{10,11... | collective-permute-start | bytes 1351688 | tf_op jit(solution)/shard_map/ppermute | solution.py:26
  64.1 16.3 %collective-permute-start.27 = (bf16[176,1280]{1,0:T(8,128)(2,1)}, bf16[176,1280]{1,0:T(8,128)(2,1)}, u32[]{:S(2)}, u32[]{:S(2)}) collective-permute-start(bf16[176,1280]{1,0:T(8,128)(2,1)} %collective-permute-done.26.refs_0_.refs_4_.refs_5_.refs_6_), channel_id=1, source_target_pairs={{0,1},{1,0},{2,3},{3,2},{4,5},{5,4},{6,7},{7,6},{8,9},{9,8},{10,11... | collective-permute-start | bytes 1351688 | tf_op jit(solution)/shard_map/ppermute | solution.py:26
  67.3 16.3 %collective-permute-start.11 = (bf16[352,1280]{1,0:T(8,128)(2,1)}, bf16[352,1280]{1,0:T(8,128)(2,1)}, u32[]{:S(2)}, u32[]{:S(2)}) collective-permute-start(bf16[352,1280]{1,0:T(8,128)(2,1)} %collective-permute-done.10.refs_0_.refs_4_.refs_5_.refs_6_), channel_id=1, source_target_pairs={{0,1},{1,0},{2,3},{3,2},{4,5},{5,4},{6,7},{7,6},{8,9},{9,8},{10,11... | collective-permute-start | bytes 2703368 | tf_op jit(solution)/shard_map/ppermute | solution.py:26
  75.9 6.0 %collective-permute-start.20 = (bf16[176,1280]{1,0:T(8,128)(2,1)}, bf16[176,1280]{1,0:T(8,128)(2,1)}, u32[]{:S(2)}, u32[]{:S(2)}) collective-permute-start(bf16[176,1280]{1,0:T(8,128)(2,1)} %collective-permute-done.19.refs_2_.refs_10_.refs_11_.refs_12_), channel_id=1, source_target_pairs={{0,1},{1,0},{2,3},{3,2},{4,5},{5,4},{6,7},{7,6},{8,9},{9,8},{10,11... | collective-permute-start | bytes 1351688 | tf_op jit(solution)/shard_map/ppermute | solution.py:26
  75.9 7.7 %collective-permute-start.29 = (bf16[176,1280]{1,0:T(8,128)(2,1)}, bf16[176,1280]{1,0:T(8,128)(2,1)}, u32[]{:S(2)}, u32[]{:S(2)}) collective-permute-start(bf16[176,1280]{1,0:T(8,128)(2,1)} %collective-permute-done.28.refs_2_.refs_10_.refs_11_.refs_12_), channel_id=1, source_target_pairs={{0,1},{1,0},{2,3},{3,2},{4,5},{5,4},{6,7},{7,6},{8,9},{9,8},{10,11... | collective-permute-start | bytes 1351688 | tf_op jit(solution)/shard_map/ppermute | solution.py:26
  78.9 20.8 %collective-permute-start.6 = (bf16[176,1280]{1,0:T(8,128)(2,1)}, bf16[176,1280]{1,0:T(8,128)(2,1)}, u32[]{:S(2)}, u32[]{:S(2)}) collective-permute-start(bf16[176,1280]{1,0:T(8,128)(2,1)} %multiply_convert_fusion.refs_0_), channel_id=1, source_target_pairs={{0,8},{1,9},{2,10},{3,11},{4,12},{5,13},{6,14},{7,15},{8,0},{9,1},... | collective-permute-start | bytes 1351688 | tf_op jit(solution)/shard_map/ppermute | solution.py:26
  80.4 24.7 %collective-permute-start.3 = (bf16[176,1280]{1,0:T(8,128)(2,1)}, bf16[176,1280]{1,0:T(8,128)(2,1)}, u32[]{:S(2)}, u32[]{:S(2)}) collective-permute-start(bf16[176,1280]{1,0:T(8,128)(2,1)} %multiply_convert_fusion.refs_0_), channel_id=1, source_target_pairs={{0,2},{1,3},{2,0},{3,1},{4,6},{5,7},{6,4},{7,5},{8,10},{9,11},{10,... | collective-permute-start | bytes 1351688 | tf_op jit(solution)/shard_map/ppermute | solution.py:26
  81.9 33.8 %collective-permute-start.13 = (bf16[176,1280]{1,0:T(8,128)(2,1)}, bf16[176,1280]{1,0:T(8,128)(2,1)}, u32[]{:S(2)}, u32[]{:S(2)}) collective-permute-start(bf16[176,1280]{1,0:T(8,128)(2,1)} %multiply_convert_fusion.refs_0_), channel_id=1, source_target_pairs={{0,16},{1,17},{2,18},{3,19},{4,20},{5,21},{6,22},{7,23},{8,24},{9,... | collective-permute-start | bytes 1351688 | tf_op jit(solution)/shard_map/ppermute | solution.py:26
  83.6 51.0 %collective-permute-start.2 = (bf16[176,1280]{1,0:T(8,128)(2,1)}, bf16[176,1280]{1,0:T(8,128)(2,1)}, u32[]{:S(2)}, u32[]{:S(2)}) collective-permute-start(bf16[176,1280]{1,0:T(8,128)(2,1)} %multiply_convert_fusion.refs_0_), channel_id=1, source_target_pairs={{0,1},{1,0},{2,3},{3,2},{4,5},{5,4},{6,7},{7,6},{8,9},{9,8},{10,11... | collective-permute-start | bytes 1351688 | tf_op jit(solution)/shard_map/ppermute | solution.py:26
  83.6 51.0 %collective-permute-start.22 = (bf16[176,1280]{1,0:T(8,128)(2,1)}, bf16[176,1280]{1,0:T(8,128)(2,1)}, u32[]{:S(2)}, u32[]{:S(2)}) collective-permute-start(bf16[176,1280]{1,0:T(8,128)(2,1)} %multiply_convert_fusion.refs_0_), channel_id=1, source_target_pairs={{0,24},{1,25},{2,26},{3,27},{4,28},{5,29},{6,30},{7,31},{8,16},{9,... | collective-permute-start | bytes 1351688 | tf_op jit(solution)/shard_map/ppermute | solution.py:26
  99.7 36.5 %collective-permute-start.8 = (bf16[176,1280]{1,0:T(8,128)(2,1)}, bf16[176,1280]{1,0:T(8,128)(2,1)}, u32[]{:S(2)}, u32[]{:S(2)}) collective-permute-start(bf16[176,1280]{1,0:T(8,128)(2,1)} %collective-permute-done.6.refs_0_), channel_id=1, source_target_pairs={{0,2},{1,3},{2,0},{3,1},{4,6},{5,7},{6,4},{7,5},{8,10},{9,11},{10,... | collective-permute-start | bytes 1351688 | tf_op jit(solution)/shard_map/ppermute | solution.py:26
  105.1 40.5 %collective-permute-start.4 = (bf16[176,1280]{1,0:T(8,128)(2,1)}, bf16[176,1280]{1,0:T(8,128)(2,1)S(1)}, u32[]{:S(2)}, u32[]{:S(2)}) collective-permute-start(bf16[176,1280]{1,0:T(8,128)(2,1)} %collective-permute-done.3.refs_2_), channel_id=1, source_target_pairs={{0,1},{1,0},{2,3},{3,2},{4,5},{5,4},{6,7},{7,6},{8,9},{9,8},{10,11... | collective-permute-start | bytes 1351688 | tf_op jit(solution)/shard_map/ppermute | solution.py:26
  115.7 30.3 %collective-permute-start.15 = (bf16[176,1280]{1,0:T(8,128)(2,1)}, bf16[176,1280]{1,0:T(8,128)(2,1)S(1)}, u32[]{:S(2)}, u32[]{:S(2)}) collective-permute-start(bf16[176,1280]{1,0:T(8,128)(2,1)} %collective-permute-done.13.refs_0_), channel_id=1, source_target_pairs={{0,2},{1,3},{2,0},{3,1},{4,6},{5,7},{6,4},{7,5},{8,10},{9,11},{10,... | collective-permute-start | bytes 1351688 | tf_op jit(solution)/shard_map/ppermute | solution.py:26
  134.6 23.3 %collective-permute-start.7 = (bf16[176,1280]{1,0:T(8,128)(2,1)}, bf16[176,1280]{1,0:T(8,128)(2,1)S(1)}, u32[]{:S(2)}, u32[]{:S(2)}) collective-permute-start(bf16[176,1280]{1,0:T(8,128)(2,1)} %collective-permute-done.6.refs_0_), channel_id=1, source_target_pairs={{0,1},{1,0},{2,3},{3,2},{4,5},{5,4},{6,7},{7,6},{8,9},{9,8},{10,11... | collective-permute-start | bytes 1351688 | tf_op jit(solution)/shard_map/ppermute | solution.py:26
  134.6 23.7 %collective-permute-start.24 = (bf16[176,1280]{1,0:T(8,128)(2,1)}, bf16[176,1280]{1,0:T(8,128)(2,1)S(1)}, u32[]{:S(2)}, u32[]{:S(2)}) collective-permute-start(bf16[176,1280]{1,0:T(8,128)(2,1)} %collective-permute-done.22.refs_0_), channel_id=1, source_target_pairs={{0,2},{1,3},{2,0},{3,1},{4,6},{5,7},{6,4},{7,5},{8,10},{9,11},{10,... | collective-permute-start | bytes 1351688 | tf_op jit(solution)/shard_map/ppermute | solution.py:26
  136.2 23.7 %collective-permute-start.9 = (bf16[176,1280]{1,0:T(8,128)(2,1)}, bf16[176,1280]{1,0:T(8,128)(2,1)}, u32[]{:S(2)}, u32[]{:S(2)}) collective-permute-start(bf16[176,1280]{1,0:T(8,128)(2,1)} %collective-permute-done.8.refs_2_), channel_id=1, source_target_pairs={{0,1},{1,0},{2,3},{3,2},{4,5},{5,4},{6,7},{7,6},{8,9},{9,8},{10,11... | collective-permute-start | bytes 1351688 | tf_op jit(solution)/shard_map/ppermute | solution.py:26
  145.6 25.8 %collective-permute-start.14 = (bf16[176,1280]{1,0:T(8,128)(2,1)}, bf16[176,1280]{1,0:T(8,128)(2,1)S(1)}, u32[]{:S(2)}, u32[]{:S(2)}) collective-permute-start(bf16[176,1280]{1,0:T(8,128)(2,1)} %collective-permute-done.13.refs_0_), channel_id=1, source_target_pairs={{0,1},{1,0},{2,3},{3,2},{4,5},{5,4},{6,7},{7,6},{8,9},{9,8},{10,11... | collective-permute-start | bytes 1351688 | tf_op jit(solution)/shard_map/ppermute | solution.py:26
  146.0 26.0 %collective-permute-start.16 = (bf16[176,1280]{1,0:T(8,128)(2,1)S(1)}, bf16[176,1280]{1,0:T(8,128)(2,1)}, u32[]{:S(2)}, u32[]{:S(2)}) collective-permute-start(bf16[176,1280]{1,0:T(8,128)(2,1)S(1)} %collective-permute-done.15.refs_2_), channel_id=1, source_target_pairs={{0,1},{1,0},{2,3},{3,2},{4,5},{5,4},{6,7},{7,6},{8,9},{9,8},{10,11... | collective-permute-start | bytes 1351688 | tf_op jit(solution)/shard_map/ppermute | solution.py:26
  157.9 27.4 %collective-permute-start.23 = (bf16[176,1280]{1,0:T(8,128)(2,1)}, bf16[176,1280]{1,0:T(8,128)(2,1)S(1)}, u32[]{:S(2)}, u32[]{:S(2)}) collective-permute-start(bf16[176,1280]{1,0:T(8,128)(2,1)} %collective-permute-done.22.refs_0_), channel_id=1, source_target_pairs={{0,1},{1,0},{2,3},{3,2},{4,5},{5,4},{6,7},{7,6},{8,9},{9,8},{10,11... | collective-permute-start | bytes 1351688 | tf_op jit(solution)/shard_map/ppermute | solution.py:26
  158.3 40.5 %collective-permute-start.5 = (bf16[320,1280]{1,0:T(8,128)(2,1)}, bf16[320,1280]{1,0:T(8,128)(2,1)S(1)}, u32[]{:S(2)}, u32[]{:S(2)}) collective-permute-start(bf16[320,1280]{1,0:T(8,128)(2,1)} %get-tuple-element.26), channel_id=1, source_target_pairs={{0,4},{1,5},{2,6},{3,7},{4,0},{5,1},{6,2},{7,3},{8,12},{9,13},{10,... | collective-permute-start | bytes 2457608 | tf_op jit(solution)/shard_map/ppermute | solution.py:26
  159.9 25.5 %collective-permute-start.25 = (bf16[176,1280]{1,0:T(8,128)(2,1)S(1)}, bf16[176,1280]{1,0:T(8,128)(2,1)}, u32[]{:S(2)}, u32[]{:S(2)}) collective-permute-start(bf16[176,1280]{1,0:T(8,128)(2,1)S(1)} %collective-permute-done.24.refs_2_), channel_id=1, source_target_pairs={{0,1},{1,0},{2,3},{3,2},{4,5},{5,4},{6,7},{7,6},{8,9},{9,8},{10,11... | collective-permute-start | bytes 1351688 | tf_op jit(solution)/shard_map/ppermute | solution.py:26
  171.4 33.3 %collective-permute-start.12 = (bf16[320,1280]{1,0:T(8,128)(2,1)}, bf16[320,1280]{1,0:T(8,128)(2,1)S(1)}, u32[]{:S(2)}, u32[]{:S(2)}) collective-permute-start(bf16[320,1280]{1,0:T(8,128)(2,1)} %get-tuple-element.31), channel_id=1, source_target_pairs={{0,4},{1,5},{2,6},{3,7},{4,0},{5,1},{6,2},{7,3},{8,12},{9,13},{10,... | collective-permute-start | bytes 2457608 | tf_op jit(solution)/shard_map/ppermute | solution.py:26
  183.9 30.8 %collective-permute-start.21 = (bf16[320,1280]{1,0:T(8,128)(2,1)}, bf16[320,1280]{1,0:T(8,128)(2,1)S(1)}, u32[]{:S(2)}, u32[]{:S(2)}) collective-permute-start(bf16[320,1280]{1,0:T(8,128)(2,1)} %get-tuple-element.36), channel_id=1, source_target_pairs={{0,4},{1,5},{2,6},{3,7},{4,0},{5,1},{6,2},{7,3},{8,12},{9,13},{10,... | collective-permute-start | bytes 2457608 | tf_op jit(solution)/shard_map/ppermute | solution.py:26
  198.1 33.4 %collective-permute-start.30 = (bf16[320,1280]{1,0:T(8,128)(2,1)}, bf16[320,1280]{1,0:T(8,128)(2,1)S(1)}, u32[]{:S(2)}, u32[]{:S(2)}) collective-permute-start(bf16[320,1280]{1,0:T(8,128)(2,1)} %get-tuple-element.41), channel_id=1, source_target_pairs={{0,4},{1,5},{2,6},{3,7},{4,0},{5,1},{6,2},{7,3},{8,12},{9,13},{10,... | collective-permute-start | bytes 2457608 | tf_op jit(solution)/shard_map/ppermute | solution.py:26
  245.6 4.6 %collective-permute-start.31 = (f32[8,128]{1,0:T(8,128)S(1)}, f32[8,128]{1,0:T(8,128)S(1)}, u32[]{:S(2)}, u32[]{:S(2)}) collective-permute-start(f32[8,128]{1,0:T(8,128)S(1)} %psum.7), channel_id=1, source_target_pairs={{0,16},{4,20},{8,24},{12,28},{16,0},{20,4},{24,8},{28,12},{1,17},{... | collective-permute-start | bytes 12296 | tf_op jit(solution)/shard_map/ppermute | solution.py:19
  (15 other events, 116.2 us)

commit v4 on v3

--- a/solution.py
+++ b/solution.py
@@ -10,7 +10,7 @@
 
 epsilon = 1e-06
 gather_levels_limit = 3
-vmem_bytes = 60 * 2**20
+vmem_bytes = 24 * 2**20
 
 
 def from_partner(value, axis, distance):
@@ -24,6 +24,10 @@
     mask = dp_mask * shards + tensor_mask
     pairs = [(source, source ^ mask) for source in range(lax.axis_size("dp") * shards)]
     return lax.ppermute(value, ("dp", "tensor"), pairs)
+
+
+def ordered(value, *before):
+    return lax.optimization_barrier((value, *before))[0]
 
 
 def split_piece(piece, upper_flag):
@@ -91,71 +95,103 @@
     return 0 if where is None else pl.multiple_of(place_ref[where] * block.shape[0], 16)
 
 
-def forward_kernel(wheres, place_ref, *refs):
-    blocks, (w_ref, hidden_ref, slope_ref) = refs[:-3], refs[-3:]
-    chunks = []
-    for block, where in zip(blocks, wheres):
-        rows = block.shape[0]
-        pieces = 2 if where is None else 1
-        for n in range(pieces):
-            begin = n * rows // pieces
-            chunks.append((block, begin, rows // pieces, row_start(place_ref, block, where) + begin))
-    for block, begin, rows, start in chunks:
-        left = block[begin : begin + rows, :]
-        v = jnp.dot(left, w_ref[...], preferred_element_type=jnp.float32)
-        scale = math.sqrt(2.0 / math.pi)
-        square = v * v
-        t = jnp.tanh(v * (scale + (scale * 0.044715) * square))
-        upper = 0.5 + 0.5 * t
-        slope = upper + (0.5 * v) * (1.0 - t * t) * (scale + (3.0 * scale * 0.044715) * square)
-        hidden_ref[pl.ds(start, rows), :] = (v * upper).astype(jnp.bfloat16)
-        slope_ref[pl.ds(start, rows), :] = slope
-
-
-def forward(place, blocks, w_in, after=()):
-    arrays, wheres = zip(*blocks)
-    rows = sum(a.shape[0] for a in arrays)
+def whole(n, s):
+    return (0, 0)
+
+
+def column(n, s):
+    return (0, n)
+
+
+SCALE = math.sqrt(2.0 / math.pi)
+CUBE = 0.044715
+
+
+def output_kernel(place_ref, rows_ref, w_in_ref, w_out_ref, out_ref, total):
+    step = pl.program_id(0)
+    v = jnp.dot(rows_ref[...], w_in_ref[...], preferred_element_type=jnp.float32)
+    t = jnp.tanh(v * (SCALE + (SCALE * CUBE) * (v * v)))
+    hidden = (v * (0.5 + 0.5 * t)).astype(jnp.bfloat16)
+    part = jnp.dot(hidden, w_out_ref[...], preferred_element_type=jnp.float32)
+
+    @pl.when(step == 0)
+    def _():
+        total[...] = part
+
+    @pl.when(step > 0)
+    def _():
+        total[...] += part
+
+    @pl.when(step == pl.num_programs(0) - 1)
+    def _():
+        out_ref[...] = total[...]
+
+
+def output_half(place, which, inputs, w_in, w_out, after=()):
+    rows = inputs.shape[0] // 2
     depth, width = w_in.shape
-    tile = tile_of(width, 256)
-    out_spec = pl.BlockSpec((rows, tile), lambda n, s: (0, n))
-    return call(
-        functools.partial(forward_kernel, wheres),
-        "forward",
-        2 * rows * depth * width,
-        (place, *arrays, w_in),
-        [
-            jax.ShapeDtypeStruct((rows, width), jnp.bfloat16),
-            jax.ShapeDtypeStruct((rows, width), jnp.float32),
-        ],
-        after,
-        grid=(width // tile,),
-        in_specs=[pl.BlockSpec(a.shape, lambda n, s: (0, 0)) for a in arrays]
-        + [pl.BlockSpec((depth, tile), lambda n, s: (0, n))],
-        out_specs=[out_spec, out_spec],
-    )
-
-
-def output_kernel(place_ref, hidden_ref, w_ref, out_ref):
-    out_ref[...] = jnp.dot(hidden_ref[...], w_ref[...], preferred_element_type=jnp.float32)
-
-
-def output_half(index, hidden, w_out, after=()):
-    rows = hidden.shape[0] // 2
-    depth, width = w_out.shape
     tile = tile_of(width, 256)
     return call(
         output_kernel,
         "output_half",
-        2 * rows * depth * width,
-        (index, hidden, w_out),
-        [jax.ShapeDtypeStruct((rows, width), jnp.float32)],
+        4 * rows * depth * width,
+        (place, inputs, w_in, w_out),
+        [jax.ShapeDtypeStruct((rows, depth), jnp.float32)],
         after,
         grid=(width // tile,),
         in_specs=[
-            pl.BlockSpec((rows, depth), lambda n, s: (s[0], 0)),
-            pl.BlockSpec((depth, tile), lambda n, s: (0, n)),
+            pl.BlockSpec((rows, depth), lambda n, s: (s[which], 0)),
+            pl.BlockSpec((depth, tile), column),
+            pl.BlockSpec((tile, depth), lambda n, s: (n, 0)),
         ],
-        out_specs=[pl.BlockSpec((rows, tile), lambda n, s: (0, n))],
+        out_specs=[pl.BlockSpec((rows, depth), whole)],
+        scratch_shapes=[pltpu.VMEM((rows, depth), jnp.float32)],
+    )[0]
+
+
+def add_kernel(place_ref, own_send, got_send, own_keep, got_keep, send_ref, keep_ref):
+    send_ref[...] = own_send[...] + got_send[...]
+    keep_ref[...] = own_keep[...] + got_keep[...]
+
+
+def add_and_split(flag, own, got):
+    rows, depth = own.shape[0] // 2, own.shape[1]
+    sent = pl.BlockSpec((rows, depth), lambda n, s: (1 - s[0], 0))
+    kept = pl.BlockSpec((rows, depth), lambda n, s: (s[0], 0))
+    shape = jax.ShapeDtypeStruct((rows, depth), jnp.float32)
+    return call(
+        add_kernel,
+        "add_and_split",
+        2 * rows * depth,
+        (flag.reshape(1), own, got, own, got),
+        [shape, shape],
+        grid=(1,),
+        in_specs=[sent, sent, kept, kept],
+        out_specs=[pl.BlockSpec((rows, depth), whole)] * 2,
+    )
+
+
+def error_kernel(row_count, place_ref, own_ref, got_ref, targets_ref, error_ref):
+    out = own_ref[...] + got_ref[...]
+    error = (out - targets_ref[...].astype(jnp.float32)) / row_count
+    error_ref[...] = error.astype(jnp.bfloat16)
+
+
+def error_part(place, own, got, targets):
+    rows, depth = own.shape
+    return call(
+        functools.partial(error_kernel, targets.shape[0]),
+        "error_part",
+        3 * rows * depth,
+        (place, own, got, targets),
+        [jax.ShapeDtypeStruct((rows, depth), jnp.bfloat16)],
+        grid=(1,),
+        in_specs=[
+            pl.BlockSpec((rows, depth), whole),
+            pl.BlockSpec((rows, depth), whole),
+            pl.BlockSpec((rows, depth), lambda n, s: (s[PARTS], 0)),
+        ],
+        out_specs=[pl.BlockSpec((rows, depth), whole)],
     )[0]
 
 
@@ -168,30 +204,31 @@
         del refs[:n]
         return taken
 
-    error_refs = take(len(error_wheres))
-    input_refs = [take(window) for _ in input_wheres]
-    hidden_ref, slope_ref, w_ref, first_ref, second_ref, send_ref = take(6)
+    error_refs, input_refs = take(len(error_wheres)), take(len(input_wheres))
+    w_in_ref, w_out_ref, first_ref, second_ref, send_ref = take(5)
     errors, inputs, inputs_turned, errors_turned, spread_first, spread_second = refs
 
     @pl.when(pl.program_id(0) == 0)
     def _():
         for block, where in zip(error_refs, error_wheres):
             errors[pl.ds(row_start(place_ref, block, where), block.shape[0]), :] = block[...]
-        for pieces, where in zip(input_refs, input_wheres):
-            start = row_start(place_ref, pieces[0], where)
-            for m, piece in enumerate(pieces):
-                inputs[pl.ds(start, piece.shape[0]), m * 128 : (m + 1) * 128] = piece[...]
+        for block, where in zip(input_refs, input_wheres):
+            inputs[pl.ds(row_start(place_ref, block, where), block.shape[0]), :] = block[...]
         lane = pl.multiple_of(place_ref[WINDOW] * 128, 128)
-        inputs_turned[...] = inputs[...].T
+        inputs_turned[...] = inputs[:, pl.ds(lane, window * 128)].T
         errors_turned[...] = errors[:, pl.ds(lane, window * 128)].T
 
     shift = pl.multiple_of(place_ref[SHIFT], step_rows)
     other_shift = pl.multiple_of(place_ref[OTHER_SHIFT], step_rows)
-    back = jnp.dot(errors[...], w_ref[...], preferred_element_type=jnp.float32)
-    dpre = (back * slope_ref[...]).astype(jnp.bfloat16)
-    spread_second[...] = jnp.dot(
-        errors_turned[...], hidden_ref[...], preferred_element_type=jnp.float32
-    )
+    v = jnp.dot(inputs[...], w_in_ref[...], preferred_element_type=jnp.float32)
+    back = jnp.dot(errors[...], w_out_ref[...], preferred_element_type=jnp.float32)
+    square = v * v
+    t = jnp.tanh(v * (SCALE + (SCALE * CUBE) * square))
+    upper = 0.5 + 0.5 * t
+    hidden = (v * upper).astype(jnp.bfloat16)
+    spread_second[...] = jnp.dot(errors_turned[...], hidden, preferred_element_type=jnp.float32)
+    slope = upper + (0.5 * v) * (1.0 - t * t) * (SCALE + (3.0 * SCALE * CUBE) * square)
+    dpre = (back * slope).astype(jnp.bfloat16)
     spread_first[...] = jnp.dot(inputs_turned[...], dpre, preferred_element_type=jnp.float32)
     second_ref[...] = spread_second[pl.ds(shift, own), :]
     send_ref[own:, :] = spread_second[pl.ds(other_shift, own), :].astype(jnp.bfloat16)
@@ -199,35 +236,22 @@
     send_ref[:own, :] = spread_first[pl.ds(other_shift, own), :].astype(jnp.bfloat16)
 
 
-def gradient(place, members, errors, inputs, hidden, slope, turned_w_out, after=()):
+def gradient(place, members, errors, inputs, w_in, turned_w_out, after=()):
     error_arrays, error_wheres = zip(*errors)
     input_arrays, input_wheres = zip(*inputs)
-    rows, width = hidden.shape
-    depth = turned_w_out.shape[0]
+    depth, width = w_in.shape
+    rows = sum(a.shape[0] for a in input_arrays)
     own = depth // members
     reach = max(m * own % 128 + 2 * own for m in range(0, members, 2))
     window = -(-reach // 128)
     tile = tile_of(width, 256)
-
-    def lanes(offset):
-        return lambda n, s: (0, s[WINDOW] + offset)
-
-    whole = lambda n, s: (0, 0)
-    column = lambda n, s: (0, n)
     return call(
         functools.partial(
             gradient_kernel, (error_wheres, input_wheres), window, own, math.gcd(own, 128)
         ),
         "gradient",
-        2 * rows * depth * width + 4 * rows * window * 128 * width,
-        (
-            place,
-            *error_arrays,
-            *[a for a in input_arrays for _ in range(window)],
-            hidden,
-            slope,
-            turned_w_out,
-        ),
+        4 * rows * depth * width + 4 * rows * window * 128 * width,
+        (place, *error_arrays, *input_arrays, w_in, turned_w_out),
         [
             jax.ShapeDtypeStruct((own, width), jnp.float32),
             jax.ShapeDtypeStruct((own, width), jnp.float32),
@@ -235,13 +259,8 @@
         ],
         after,
         grid=(width // tile,),
-        in_specs=[pl.BlockSpec(a.shape, whole) for a in error_arrays]
-        + [pl.BlockSpec((a.shape[0], 128), lanes(m)) for a in input_arrays for m in range(window)]
-        + [
-            pl.BlockSpec((rows, tile), column),
-            pl.BlockSpec((rows, tile), column),
-            pl.BlockSpec((depth, tile), column),
-        ],
+        in_specs=[pl.BlockSpec(a.shape, whole) for a in (*error_arrays, *input_arrays)]
+        + [pl.BlockSpec((depth, tile), column)] * 2,
         out_specs=[
             pl.BlockSpec((own, tile), column),
             pl.BlockSpec((own, tile), column),
@@ -249,7 +268,7 @@
         ],
         scratch_shapes=[
             pltpu.VMEM((rows, depth), jnp.bfloat16),
-            pltpu.VMEM((rows, window * 128), jnp.bfloat16),
+            pltpu.VMEM((rows, depth), jnp.bfloat16),
             pltpu.VMEM((window * 128, rows), jnp.bfloat16),
             pltpu.VMEM((window * 128, rows), jnp.bfloat16),
             pltpu.VMEM((window * 128, tile), jnp.float32),
@@ -298,7 +317,6 @@
     own, width = slots[0][0].shape
     tile = tile_of(width, 256)
     pairs = sum(len(slots) - n for n in range(fresh))
-    whole = lambda n, s: (0, 0)
     return call(
         functools.partial(products_kernel, [len(slot) for slot in slots], fresh),
         "products",
@@ -417,49 +435,43 @@
         ]
         + [part_of(shard ^ mask) for mask in range(shards)]
     ).astype(jnp.int32)
-    turned_w_out = w_out.T
 
     own_half = lax.dynamic_slice_in_dim(inputs, near * half_rows, half_rows, 0)
     own_part = lax.dynamic_slice_in_dim(inputs, part_of(shard) * part_rows, part_rows, 0)
-    blocks = {0: [(inputs, None)]}
-    for m in range(1, members // 2):
-        if m == 1:
-            got = from_mask(own_half, 2 * m * others, 0)
-            blocks[m] = [(got, NEAR), (from_mask(got, 0, 1), FAR)]
-        else:
-            found = {0: from_mask(own_part, 2 * m * others, 0)}
-            for bit in reversed(range(shard_levels)):
-                for mask in list(found):
-                    found[mask | 2**bit] = from_mask(found[mask], 0, 2**bit)
-            blocks[m] = [(found[k], PARTS + k) for k in range(shards)]
-
-    hidden, slope = {}, {}
-    hidden[0], slope[0] = forward(place, blocks[0], w_in)
-
-    got = from_mask(output_half((1 - near).reshape(1), hidden[0], w_out), 0, 1)
-    summed = output_half(near.reshape(1), hidden[0], w_out) + got
+    arrived = {
+        m: from_mask(own_half if m == 1 else own_part, 2 * m * others, 0)
+        for m in range(1, members // 2)
+    }
+
+    got = from_mask(output_half(place, FAR, inputs, w_in, w_out), 0, 1)
+    summed = output_half(place, NEAR, inputs, w_in, w_out)
     for bit in range(1, shard_levels):
-        keep, send = split_piece(summed, shard >> bit & 1)
-        summed = keep + from_mask(send, 0, 2**bit)
-    targets_part = lax.dynamic_slice_in_dim(targets, part_of(shard) * part_rows, part_rows, 0)
-    error = ((summed - targets_part.astype(jnp.float32)) / row_count).astype(jnp.bfloat16)
-
-    errors = {}
-    for m in range(members // 2):
-        found = {0: from_mask(error, 2 * m * others, 0) if m else error}
+        send, summed = add_and_split(shard >> bit & 1, summed, got)
+        got = from_mask(send, 0, 2**bit)
+    turned_w_out = ordered(w_out, send).T
+    error = error_part(place, summed, got, targets)
+
+    def spread_over_tensor(found):
         for bit in reversed(range(shard_levels)):
             for mask in list(found):
                 found[mask | 2**bit] = from_mask(found[mask], 0, 2**bit)
-        errors[m] = [(found[k], PARTS + k) for k in range(shards)]
-
+        return [(found[k], PARTS + k) for k in range(shards)]
+
+    errors, blocks = {}, {0: [(inputs, None)]}
+    for m in range(members // 2):
+        errors[m] = spread_over_tensor({0: from_mask(error, 2 * m * others, 0) if m else error})
     for m in range(1, members // 2):
-        hidden[m], slope[m] = forward(place, blocks[m], w_in)
+        block = ordered(arrived[m], error)
+        if m == 1:
+            blocks[m] = [(block, NEAR), (from_mask(block, 0, 1), FAR)]
+        else:
+            blocks[m] = spread_over_tensor({0: block})
 
     slots = []
     totals = jnp.zeros((8, 128), jnp.float32)
     for m in range(members // 2):
         first, second, send = gradient(
-            place, members, errors[m], blocks[m], hidden[m], slope[m], turned_w_out
+            place, members, errors[m], blocks[m], w_in, turned_w_out
         )
         slots.append((first, second))
         if m == members // 2 - 1:

time: 267 us -> 255 us (0.955)
  Pallas kernels: 135 us -> 82.9 us
  local copies, waits for them, and re-layouts: 13.1 us -> 36 us
  waiting for transfers between devices: 78.7 us -> 101 us
  other arithmetic: 5.29 us -> 0.01 us
    pallas_call x16 -> x14, Pallas kernels: 135 us -> 82.9 us  [call(): pl.pallas_call(body, grid_spec=pltpu.PrefetchScalarGridSpec(num_scalar_pr...]
    ppermute x31, waiting for transfers between devices: 68.6 us -> 90.6 us  [from_mask(): return lax.ppermute(value, ('dp', 'tensor'), pairs)]
    unnamed x27 -> x76, local copies, waits for them, and re-layouts: 8.99 us -> 30.4 us
    optimization_barrier x0 -> x1, local copies, waits for them, and re-layouts: none -> 3.42 us  [ordered(): return lax.optimization_barrier((value, *before))[0]]
  transfers between devices with their start and end apart: 34 -> 34, of which waited for: 11 -> 13; matrix products, arithmetic and copies ran while one was open for 4% -> 2% of each run, Pallas kernels for 40% -> 25%
where the time goes in v4:
time: 255 us; the launch traced here: 254 us
  waiting for transfers between devices  101 us (40%)
  Pallas kernels  82.9 us (33%)
  local copies, waits for them, and re-layouts  36 us (14%)
  starting transfers between devices  27.7 us (11%)
  blocking collectives  5.63 us (2%)
    ppermute x31, waiting for transfers between devices, from_mask(): return lax.ppermute(value, ('dp', 'tensor'), pairs)  90.6 us
    pallas_call x14, Pallas kernels, call(): pl.pallas_call(body, grid_spec=pltpu.PrefetchScalarGridSpec(num_scalar_pr...  82.9 us
    unnamed x76, local copies, waits for them, and re-layouts  30.4 us
    ppermute x31, starting transfers between devices, from_mask(): return lax.ppermute(value, ('dp', 'tensor'), pairs)  26.1 us
    ppermute x3, waiting for transfers between devices, from_partner(): return lax.ppermute(value, axis, pairs)  10.2 us
    psum x1, blocking collectives, group_total(): summed = lax.psum(values, 'tensor')  5.63 us
  transfers between devices with their start and end apart: 34, of which 13 were waited for; matrix products, arithmetic and copies ran while one was open for 2% of the time, Pallas kernels for 25%

profile of v4, /device:TPU:0, one launch (start us, length us, event | category | flops | bytes accessed | tf_op | source)
XLA Modules:
  0.0 254.0 jit_solution(4605769909991566965)
XLA Ops:
  0.8 1.9 copy-done
  4.2 1.9 copy-done.12
  6.1 8.6 %output_half.3 = f32[352,1280]{1,0:T(8,128)} custom-call(s32[10]{0:T(128)S(1)} %stack.43.place_ref, bf16[704,1280]{1,0:T(8,128)(2,1)S(1)} %copy-done.8, bf16[1280,1280]{1,0:T(8,128)(2,1)S(1)} %copy-done.12, bf16[1280,1280]{1,0:T(8,128)(2,1)S(1)} %copy-done), custom_call_target="tpu_custom_call" | custom-call | flops 2306867200 | bytes 10158120 | tf_op jit(solution)/shard_map/output_half/pallas_call | solution.py:81
  16.7 1.9 copy-done.13
  18.6 7.3 %output_half.2.refs_0_.refs_2_ = f32[352,1280]{1,0:T(8,128)S(1)} custom-call(s32[10]{0:T(128)S(1)} %stack.43.place_ref, bf16[704,1280]{1,0:T(8,128)(2,1)S(1)} %copy-done.9, bf16[1280,1280]{1,0:T(8,128)(2,1)S(1)} %copy-done.13, bf16[1280,1280]{1,0:T(8,128)(2,1)S(1)} %copy-done.1), custom_call_target="tpu_custom_call" | custom-call | flops 2306867200 | bytes 10158120 | tf_op jit(solution)/shard_map/output_half/pallas_call | solution.py:81
  26.0 2.7 %add_and_split.1 = (f32[176,1280]{1,0:T(8,128)}, f32[176,1280]{1,0:T(8,128)S(1)}) custom-call(s32[1]{0:T(128)} %bitcast.10.place_ref, f32[352,1280]{1,0:T(8,128)S(1)} %output_half.2.refs_0_.refs_2_, f32[352,1280]{1,0:T(8,128)} %collective-permute-done.refs_1_.refs_3_, f32[352,1280]{1,0:T(8,128)S(1)} %output_half.2.refs_0_.refs_2_, ...), custom_call_target="tpu_custom_call" | custom-call | flops 450560 | bytes 9011204 | tf_op jit(solution)/shard_map/add_and_split/pallas_call | solution.py:81
  28.7 2.5 collective-permute-start.1
  34.9 2.7 %collective-permute-start.17 = (bf16[176,1280]{1,0:T(8,128)(2,1)S(1)}, bf16[176,1280]{1,0:T(8,128)(2,1)}, u32[]{:S(2)}, u32[]{:S(2)}) collective-permute-start(bf16[176,1280]{1,0:T(8,128)(2,1)S(1)} %constant_dynamic-slice_fusion), channel_id=1, source_target_pairs={{0,16},{1,17},{2,18},{3,19},{4,20},{5,21},{6,22},{7,23},{8,24},{9,... | collective-permute-start | bytes 1351688 | tf_op jit(solution)/shard_map/ppermute | solution.py:26
  37.7 14.4 %collective-permute-done.1.refs_1_ = f32[176,1280]{1,0:T(8,128)} collective-permute-done((f32[176,1280]{1,0:T(8,128)}, f32[176,1280]{1,0:T(8,128)}, u32[]{:S(2)}, u32[]{:S(2)}) %collective-permute-start.1) | collective-permute-done | bytes 901152 | tf_op jit(solution)/shard_map/ppermute | solution.py:26
  58.7 5.4 %collective-permute-done.17.refs_4_ = bf16[176,1280]{1,0:T(8,128)(2,1)} collective-permute-done((bf16[176,1280]{1,0:T(8,128)(2,1)S(1)}, bf16[176,1280]{1,0:T(8,128)(2,1)}, u32[]{:S(2)}, u32[]{:S(2)}) %collective-permute-start.17) | collective-permute-done | bytes 450592 | tf_op jit(solution)/shard_map/ppermute | solution.py:26
  64.1 3.7 %collective-permute-start.6 = (bf16[176,1280]{1,0:T(8,128)(2,1)S(1)}, bf16[176,1280]{1,0:T(8,128)(2,1)}, u32[]{:S(2)}, u32[]{:S(2)}) collective-permute-start(bf16[176,1280]{1,0:T(8,128)(2,1)S(1)} %error_part.1.refs_0_), channel_id=1, source_target_pairs={{0,8},{1,9},{2,10},{3,11},{4,12},{5,13},{6,14},{7,15},{8,0},{9,1},... | collective-permute-start | bytes 1351688 | tf_op jit(solution)/shard_map/ppermute | solution.py:26
  67.7 9.0 %collective-permute-done.26.refs_4_ = bf16[176,1280]{1,0:T(8,128)(2,1)S(1)} collective-permute-done((bf16[176,1280]{1,0:T(8,128)(2,1)S(1)}, bf16[176,1280]{1,0:T(8,128)(2,1)S(1)}, u32[]{:S(2)}, u32[]{:S(2)}) %collective-permute-start.26) | collective-permute-done | bytes 450592 | tf_op jit(solution)/shard_map/ppermute | solution.py:26
  80.2 12.4 %collective-permute-done.6.refs_0_ = bf16[176,1280]{1,0:T(8,128)(2,1)} collective-permute-done((bf16[176,1280]{1,0:T(8,128)(2,1)S(1)}, bf16[176,1280]{1,0:T(8,128)(2,1)}, u32[]{:S(2)}, u32[]{:S(2)}) %collective-permute-start.6) | collective-permute-done | bytes 450592 | tf_op jit(solution)/shard_map/ppermute | solution.py:26
  93.1 5.2 %collective-permute-done.13.refs_0_ = bf16[176,1280]{1,0:T(8,128)(2,1)S(1)} collective-permute-done((bf16[176,1280]{1,0:T(8,128)(2,1)S(1)}, bf16[176,1280]{1,0:T(8,128)(2,1)S(1)}, u32[]{:S(2)}, u32[]{:S(2)}) %collective-permute-start.13) | collective-permute-done | bytes 450592 | tf_op jit(solution)/shard_map/ppermute | solution.py:26
  99.0 3.4 %copy.6 = bf16[1280,1280]{0,1:T(8,128)(2,1)} copy(bf16[1280,1280]{1,0:T(8,128)(2,1)S(1)} %copy-done.1) | data formatting | bytes 6553600 | tf_op jit(solution)/shard_map/optimization_barrier | solution.py:30
  112.6 11.5 %gradient.4 = (f32[160,1280]{1,0:T(8,128)S(1)}, f32[160,1280]{1,0:T(8,128)S(1)}, bf16[320,1280]{1,0:T(8,128)(2,1)S(1)}) custom-call(s32[10]{0:T(128)S(1)} %stack.43.place_ref, bf16[176,1280]{1,0:T(8,128)(2,1)S(1)} %copy-done.31, bf16[176,1280]{1,0:T(8,128)(2,1)S(1)} %copy-done.37, bf16[176,1280]{1,0:T(8,128)(2,1)} %collective-permute-done.3.refs_2_, ...), custom_call_target="tpu_custom_call" | custom-call | flops 5997854720 | bytes 12615720 | tf_op jit(solution)/shard_map/gradient/pallas_call | solution.py:81
  126.7 11.8 %gradient.5 = (f32[160,1280]{1,0:T(8,128)S(1)}, f32[160,1280]{1,0:T(8,128)S(1)}, bf16[320,1280]{1,0:T(8,128)(2,1)S(1)}) custom-call(s32[10]{0:T(128)S(1)} %stack.43.place_ref, bf16[176,1280]{1,0:T(8,128)(2,1)} %collective-permute-done.6.refs_0_, bf16[176,1280]{1,0:T(8,128)(2,1)S(1)} %collective-permute-done.7.refs_1_, ...), custom_call_target="tpu_custom_call" | custom-call | flops 5997854720 | bytes 12615720 | tf_op jit(solution)/shard_map/gradient/pallas_call | solution.py:81
  139.7 6.9 %collective-permute-done.24.refs_2_ = bf16[176,1280]{1,0:T(8,128)(2,1)S(1)} collective-permute-done((bf16[176,1280]{1,0:T(8,128)(2,1)S(1)}, bf16[176,1280]{1,0:T(8,128)(2,1)S(1)}, u32[]{:S(2)}, u32[]{:S(2)}) %collective-permute-start.24) | collective-permute-done | bytes 450592 | tf_op jit(solution)/shard_map/ppermute | solution.py:26
  148.1 11.4 %gradient.6 = (f32[160,1280]{1,0:T(8,128)S(1)}, f32[160,1280]{1,0:T(8,128)S(1)}, bf16[320,1280]{1,0:T(8,128)(2,1)S(1)}) custom-call(s32[10]{0:T(128)S(1)} %stack.43.place_ref, bf16[176,1280]{1,0:T(8,128)(2,1)S(1)} %copy-done.35, bf16[176,1280]{1,0:T(8,128)(2,1)S(1)} %collective-permute-done.14.refs_1_, ...), custom_call_target="tpu_custom_call" | custom-call | flops 5997854720 | bytes 12615720 | tf_op jit(solution)/shard_map/gradient/pallas_call | solution.py:81
  161.6 10.4 %gradient.7 = (f32[160,1280]{1,0:T(8,128)S(1)}, f32[160,1280]{1,0:T(8,128)S(1)}, bf16[320,1280]{1,0:T(8,128)(2,1)S(1)}) custom-call(s32[10]{0:T(128)S(1)} %stack.43.place_ref, bf16[176,1280]{1,0:T(8,128)(2,1)S(1)} %collective-permute-done.22.refs_0_, bf16[176,1280]{1,0:T(8,128)(2,1)S(1)} %collective-permute-done.23.refs_1_, ...), custom_call_target="tpu_custom_call" | custom-call | flops 5997854720 | bytes 12615720 | tf_op jit(solution)/shard_map/gradient/pallas_call | solution.py:81
  174.0 11.3 %collective-permute-done.12.refs_5_.refs_7_.refs_8_ = bf16[320,1280]{1,0:T(8,128)(2,1)S(1)} collective-permute-done((bf16[320,1280]{1,0:T(8,128)(2,1)S(1)}, bf16[320,1280]{1,0:T(8,128)(2,1)S(1)}, u32[]{:S(2)}, u32[]{:S(2)}) %collective-permute-start.12) | collective-permute-done | bytes 819232 | tf_op jit(solution)/shard_map/ppermute | solution.py:26
  185.3 2.4 products.6.refs_9_
  187.7 15.2 %collective-permute-done.21.refs_8_.refs_11_.refs_12_ = bf16[320,1280]{1,0:T(8,128)(2,1)S(1)} collective-permute-done((bf16[320,1280]{1,0:T(8,128)(2,1)S(1)}, bf16[320,1280]{1,0:T(8,128)(2,1)S(1)}, u32[]{:S(2)}, u32[]{:S(2)}) %collective-permute-start.21) | collective-permute-done | bytes 819232 | tf_op jit(solution)/shard_map/ppermute | solution.py:26
  202.8 3.4 %products.7.refs_11_ = f32[8,128]{1,0:T(8,128)S(1)} custom-call(s32[10]{0:T(128)S(1)} %stack.43.place_ref, f32[160,1280]{1,0:T(8,128)S(1)} %get-tuple-element.23.refs_0_.refs_1_, f32[160,1280]{1,0:T(8,128)S(1)} %get-tuple-element.24.refs_1_.refs_2_, bf16[320,1280]{1,0:T(8,128)(2,1)S(1)} %collective-permute-done.5.refs_2_.refs_3_.refs_4_, ...), custom_call_target="tpu_custom_call" | custom-call | flops 9011200 | bytes 7381032 | tf_op jit(solution)/shard_map/products/pallas_call | solution.py:81
  206.2 2.7 %products.8.refs_12_ = f32[8,128]{1,0:T(8,128)S(1)} custom-call(s32[10]{0:T(128)S(1)} %stack.43.place_ref, f32[160,1280]{1,0:T(8,128)S(1)} %get-tuple-element.23.refs_0_.refs_1_, f32[160,1280]{1,0:T(8,128)S(1)} %get-tuple-element.24.refs_1_.refs_2_, bf16[320,1280]{1,0:T(8,128)(2,1)S(1)} %collective-permute-done.5.refs_2_.refs_3_.refs_4_, ...), custom_call_target="tpu_custom_call" | custom-call | flops 5734400 | bytes 9019432 | tf_op jit(solution)/shard_map/products/pallas_call | solution.py:81
  208.9 10.2 %collective-permute-done.30.refs_11_.refs_15_.refs_16_ = bf16[320,1280]{1,0:T(8,128)(2,1)S(1)} collective-permute-done((bf16[320,1280]{1,0:T(8,128)(2,1)S(1)}, bf16[320,1280]{1,0:T(8,128)(2,1)S(1)}, u32[]{:S(2)}, u32[]{:S(2)}) %collective-permute-start.30) | collective-permute-done | bytes 819232 | tf_op jit(solution)/shard_map/ppermute | solution.py:26
  219.2 3.2 %products.9 = f32[8,128]{1,0:T(8,128)S(1)} custom-call(s32[10]{0:T(128)S(1)} %stack.43.place_ref, f32[160,1280]{1,0:T(8,128)S(1)} %get-tuple-element.23.refs_0_.refs_1_, f32[160,1280]{1,0:T(8,128)S(1)} %get-tuple-element.24.refs_1_.refs_2_, bf16[320,1280]{1,0:T(8,128)(2,1)S(1)} %collective-permute-done.5.refs_2_.refs_3_.refs_4_, ...), custom_call_target="tpu_custom_call" | custom-call | flops 6553600 | bytes 9838632 | tf_op jit(solution)/shard_map/products/pallas_call | solution.py:81
  223.2 5.6 %psum.7 = f32[8,128]{1,0:T(8,128)S(1)} all-reduce(f32[8,128]{1,0:T(8,128)S(1)} %products.9), channel_id=1, replica_groups=mesh['dp'=8,'tensor'=4] {'tensor'}, use_global_device_ids=true, to_apply=%region_0.1 | all-reduce | flops 1024 | bytes 8192 | tf_op jit(solution)/shard_map/psum | solution.py:41
  228.9 4.5 %collective-permute-done.31 = f32[8,128]{1,0:T(8,128)S(1)} collective-permute-done((f32[8,128]{1,0:T(8,128)S(1)}, f32[8,128]{1,0:T(8,128)S(1)}, u32[]{:S(2)}, u32[]{:S(2)}) %collective-permute-start.31) | collective-permute-done | bytes 4128 | tf_op jit(solution)/shard_map/ppermute | solution.py:19
  233.4 3.6 %collective-permute-done.32 = f32[8,128]{1,0:T(8,128)S(1)} collective-permute-done((f32[8,128]{1,0:T(8,128)S(1)}, f32[8,128]{1,0:T(8,128)S(1)}, u32[]{:S(2)}, u32[]{:S(2)}) %collective-permute-start.32) | collective-permute-done | bytes 4128 | tf_op jit(solution)/shard_map/ppermute | solution.py:19
  238.6 2.1 collective-permute-done.33
  249.8 4.2 %merge.1 = (f32[160,1280]{1,0:T(8,128)}, f32[160,1280]{1,0:T(8,128)}) custom-call(s32[10]{0:T(128)S(1)} %stack.43.place_ref, f32[8,128]{1,0:T(8,128)S(1)} %add.60.refs_0_, f32[160,1280]{1,0:T(8,128)S(1)} %get-tuple-element.23.refs_0_.refs_1_, f32[160,1280]{1,0:T(8,128)S(1)} %get-tuple-element.24.refs_1_.refs_2_, ...), custom_call_target="tpu_custom_call" | custom-call | flops 6553600 | bytes 14749736 | tf_op jit(solution)/shard_map/merge/pallas_call | solution.py:81
  (135 shorter events, 49.7 us)
Async XLA Ops:
  14.7 11.2 %collective-permute-start = (f32[352,1280]{1,0:T(8,128)}, f32[352,1280]{1,0:T(8,128)}, u32[]{:S(2)}, u32[]{:S(2)}) collective-permute-start(f32[352,1280]{1,0:T(8,128)} %output_half.3), channel_id=1, source_target_pairs={{0,1},{1,0},{2,3},{3,2},{4,5},{5,4},{6,7},{7,6},{8,9},{9,8},{10,11... | collective-permute-start | bytes 5406728 | tf_op jit(solution)/shard_map/ppermute | solution.py:26
  28.7 23.5 %collective-permute-start.1 = (f32[176,1280]{1,0:T(8,128)}, f32[176,1280]{1,0:T(8,128)}, u32[]{:S(2)}, u32[]{:S(2)}) collective-permute-start(f32[176,1280]{1,0:T(8,128)} %get-tuple-element.21), channel_id=1, source_target_pairs={{0,2},{1,3},{2,0},{3,1},{4,6},{5,7},{6,4},{7,5},{8,10},{9,11},{10,... | collective-permute-start | bytes 2703368 | tf_op jit(solution)/shard_map/ppermute | solution.py:26
  32.2 46.4 %collective-permute-start.10 = (bf16[352,1280]{1,0:T(8,128)(2,1)}, bf16[352,1280]{1,0:T(8,128)(2,1)}, u32[]{:S(2)}, u32[]{:S(2)}) collective-permute-start(bf16[352,1280]{1,0:T(8,128)(2,1)} %constant_dynamic-slice_fusion.1), channel_id=1, source_target_pairs={{0,8},{1,9},{2,10},{3,11},{4,12},{5,13},{6,14},{7,15},{8,0},{9,1},... | collective-permute-start | bytes 2703368 | tf_op jit(solution)/shard_map/ppermute | solution.py:26
  34.9 29.2 %collective-permute-start.17 = (bf16[176,1280]{1,0:T(8,128)(2,1)S(1)}, bf16[176,1280]{1,0:T(8,128)(2,1)}, u32[]{:S(2)}, u32[]{:S(2)}) collective-permute-start(bf16[176,1280]{1,0:T(8,128)(2,1)S(1)} %constant_dynamic-slice_fusion), channel_id=1, source_target_pairs={{0,16},{1,17},{2,18},{3,19},{4,20},{5,21},{6,22},{7,23},{8,24},{9,... | collective-permute-start | bytes 1351688 | tf_op jit(solution)/shard_map/ppermute | solution.py:26
  37.5 39.2 %collective-permute-start.26 = (bf16[176,1280]{1,0:T(8,128)(2,1)S(1)}, bf16[176,1280]{1,0:T(8,128)(2,1)S(1)}, u32[]{:S(2)}, u32[]{:S(2)}) collective-permute-start(bf16[176,1280]{1,0:T(8,128)(2,1)S(1)} %constant_dynamic-slice_fusion), channel_id=1, source_target_pairs={{0,24},{1,25},{2,26},{3,27},{4,28},{5,29},{6,30},{7,31},{8,16},{9,... | collective-permute-start | bytes 1351688 | tf_op jit(solution)/shard_map/ppermute | solution.py:26
  56.8 21.9 %collective-permute-start.2 = (bf16[176,1280]{1,0:T(8,128)(2,1)S(1)}, bf16[176,1280]{1,0:T(8,128)(2,1)S(1)}, u32[]{:S(2)}, u32[]{:S(2)}) collective-permute-start(bf16[176,1280]{1,0:T(8,128)(2,1)S(1)} %error_part.1.refs_0_), channel_id=1, source_target_pairs={{0,1},{1,0},{2,3},{3,2},{4,5},{5,4},{6,7},{7,6},{8,9},{9,8},{10,11... | collective-permute-start | bytes 1351688 | tf_op jit(solution)/shard_map/ppermute | solution.py:26
  56.9 23.1 %collective-permute-start.3 = (bf16[176,1280]{1,0:T(8,128)(2,1)S(1)}, bf16[176,1280]{1,0:T(8,128)(2,1)}, u32[]{:S(2)}, u32[]{:S(2)}) collective-permute-start(bf16[176,1280]{1,0:T(8,128)(2,1)S(1)} %error_part.1.refs_0_), channel_id=1, source_target_pairs={{0,2},{1,3},{2,0},{3,1},{4,6},{5,7},{6,4},{7,5},{8,10},{9,11},{10,... | collective-permute-start | bytes 1351688 | tf_op jit(solution)/shard_map/ppermute | solution.py:26
  64.1 28.5 %collective-permute-start.6 = (bf16[176,1280]{1,0:T(8,128)(2,1)S(1)}, bf16[176,1280]{1,0:T(8,128)(2,1)}, u32[]{:S(2)}, u32[]{:S(2)}) collective-permute-start(bf16[176,1280]{1,0:T(8,128)(2,1)S(1)} %error_part.1.refs_0_), channel_id=1, source_target_pairs={{0,8},{1,9},{2,10},{3,11},{4,12},{5,13},{6,14},{7,15},{8,0},{9,1},... | collective-permute-start | bytes 1351688 | tf_op jit(solution)/shard_map/ppermute | solution.py:26
  76.7 21.6 %collective-permute-start.13 = (bf16[176,1280]{1,0:T(8,128)(2,1)S(1)}, bf16[176,1280]{1,0:T(8,128)(2,1)S(1)}, u32[]{:S(2)}, u32[]{:S(2)}) collective-permute-start(bf16[176,1280]{1,0:T(8,128)(2,1)S(1)} %error_part.1.refs_0_), channel_id=1, source_target_pairs={{0,16},{1,17},{2,18},{3,19},{4,20},{5,21},{6,22},{7,23},{8,24},{9,... | collective-permute-start | bytes 1351688 | tf_op jit(solution)/shard_map/ppermute | solution.py:26
  78.6 23.8 %collective-permute-start.18 = (bf16[176,1280]{1,0:T(8,128)(2,1)}, bf16[176,1280]{1,0:T(8,128)(2,1)}, u32[]{:S(2)}, u32[]{:S(2)}) collective-permute-start(bf16[176,1280]{1,0:T(8,128)(2,1)} %collective-permute-done.17.refs_4_), channel_id=1, source_target_pairs={{0,1},{1,0},{2,3},{3,2},{4,5},{5,4},{6,7},{7,6},{8,9},{9,8},{10,11... | collective-permute-start | bytes 1351688 | tf_op jit(solution)/shard_map/ppermute | solution.py:26
  79.4 24.4 %collective-permute-start.19 = (bf16[176,1280]{1,0:T(8,128)(2,1)}, bf16[176,1280]{1,0:T(8,128)(2,1)}, u32[]{:S(2)}, u32[]{:S(2)}) collective-permute-start(bf16[176,1280]{1,0:T(8,128)(2,1)} %collective-permute-done.17.refs_4_), channel_id=1, source_target_pairs={{0,2},{1,3},{2,0},{3,1},{4,6},{5,7},{6,4},{7,5},{8,10},{9,11},{10,... | collective-permute-start | bytes 1351688 | tf_op jit(solution)/shard_map/ppermute | solution.py:26
  79.9 24.1 %collective-permute-start.4 = (bf16[176,1280]{1,0:T(8,128)(2,1)}, bf16[176,1280]{1,0:T(8,128)(2,1)}, u32[]{:S(2)}, u32[]{:S(2)}) collective-permute-start(bf16[176,1280]{1,0:T(8,128)(2,1)} %collective-permute-done.3.refs_2_), channel_id=1, source_target_pairs={{0,1},{1,0},{2,3},{3,2},{4,5},{5,4},{6,7},{7,6},{8,9},{9,8},{10,11... | collective-permute-start | bytes 1351688 | tf_op jit(solution)/shard_map/ppermute | solution.py:26
  92.6 12.6 %collective-permute-start.8 = (bf16[176,1280]{1,0:T(8,128)(2,1)}, bf16[176,1280]{1,0:T(8,128)(2,1)}, u32[]{:S(2)}, u32[]{:S(2)}) collective-permute-start(bf16[176,1280]{1,0:T(8,128)(2,1)} %collective-permute-done.6.refs_0_), channel_id=1, source_target_pairs={{0,2},{1,3},{2,0},{3,1},{4,6},{5,7},{6,4},{7,5},{8,10},{9,11},{10,... | collective-permute-start | bytes 1351688 | tf_op jit(solution)/shard_map/ppermute | solution.py:26
  99.0 26.3 %collective-permute-start.11 = (bf16[352,1280]{1,0:T(8,128)(2,1)}, bf16[352,1280]{1,0:T(8,128)(2,1)}, u32[]{:S(2)}, u32[]{:S(2)}) collective-permute-start(bf16[352,1280]{1,0:T(8,128)(2,1)} %collective-permute-done.10.refs_4_), channel_id=1, source_target_pairs={{0,1},{1,0},{2,3},{3,2},{4,5},{5,4},{6,7},{7,6},{8,9},{9,8},{10,11... | collective-permute-start | bytes 2703368 | tf_op jit(solution)/shard_map/ppermute | solution.py:26
  102.5 21.6 %collective-permute-start.22 = (bf16[176,1280]{1,0:T(8,128)(2,1)}, bf16[176,1280]{1,0:T(8,128)(2,1)S(1)}, u32[]{:S(2)}, u32[]{:S(2)}) collective-permute-start(bf16[176,1280]{1,0:T(8,128)(2,1)} %copy-done.30), channel_id=1, source_target_pairs={{0,24},{1,25},{2,26},{3,27},{4,28},{5,29},{6,30},{7,31},{8,16},{9,... | collective-permute-start | bytes 1351688 | tf_op jit(solution)/shard_map/ppermute | solution.py:26
  103.8 21.3 %collective-permute-start.7 = (bf16[176,1280]{1,0:T(8,128)(2,1)}, bf16[176,1280]{1,0:T(8,128)(2,1)S(1)}, u32[]{:S(2)}, u32[]{:S(2)}) collective-permute-start(bf16[176,1280]{1,0:T(8,128)(2,1)} %collective-permute-done.6.refs_0_), channel_id=1, source_target_pairs={{0,1},{1,0},{2,3},{3,2},{4,5},{5,4},{6,7},{7,6},{8,9},{9,8},{10,11... | collective-permute-start | bytes 1351688 | tf_op jit(solution)/shard_map/ppermute | solution.py:26
  104.0 21.5 %collective-permute-start.15 = (bf16[176,1280]{1,0:T(8,128)(2,1)}, bf16[176,1280]{1,0:T(8,128)(2,1)S(1)}, u32[]{:S(2)}, u32[]{:S(2)}) collective-permute-start(bf16[176,1280]{1,0:T(8,128)(2,1)} %copy-done.34), channel_id=1, source_target_pairs={{0,2},{1,3},{2,0},{3,1},{4,6},{5,7},{6,4},{7,5},{8,10},{9,11},{10,... | collective-permute-start | bytes 1351688 | tf_op jit(solution)/shard_map/ppermute | solution.py:26
  105.2 21.5 %collective-permute-start.9 = (bf16[176,1280]{1,0:T(8,128)(2,1)}, bf16[176,1280]{1,0:T(8,128)(2,1)S(1)}, u32[]{:S(2)}, u32[]{:S(2)}) collective-permute-start(bf16[176,1280]{1,0:T(8,128)(2,1)} %collective-permute-done.8.refs_2_), channel_id=1, source_target_pairs={{0,1},{1,0},{2,3},{3,2},{4,5},{5,4},{6,7},{7,6},{8,9},{9,8},{10,11... | collective-permute-start | bytes 1351688 | tf_op jit(solution)/shard_map/ppermute | solution.py:26
  124.1 14.5 %collective-permute-start.28 = (bf16[176,1280]{1,0:T(8,128)(2,1)S(1)}, bf16[176,1280]{1,0:T(8,128)(2,1)S(1)}, u32[]{:S(2)}, u32[]{:S(2)}) collective-permute-start(bf16[176,1280]{1,0:T(8,128)(2,1)S(1)} %copy-done.33), channel_id=1, source_target_pairs={{0,2},{1,3},{2,0},{3,1},{4,6},{5,7},{6,4},{7,5},{8,10},{9,11},{10,... | collective-permute-start | bytes 1351688 | tf_op jit(solution)/shard_map/ppermute | solution.py:26
  125.1 14.1 %collective-permute-start.14 = (bf16[176,1280]{1,0:T(8,128)(2,1)S(1)}, bf16[176,1280]{1,0:T(8,128)(2,1)S(1)}, u32[]{:S(2)}, u32[]{:S(2)}) collective-permute-start(bf16[176,1280]{1,0:T(8,128)(2,1)S(1)} %copy-done.35), channel_id=1, source_target_pairs={{0,1},{1,0},{2,3},{3,2},{4,5},{5,4},{6,7},{7,6},{8,9},{9,8},{10,11... | collective-permute-start | bytes 1351688 | tf_op jit(solution)/shard_map/ppermute | solution.py:26
  125.3 13.9 %collective-permute-start.20 = (bf16[176,1280]{1,0:T(8,128)(2,1)}, bf16[176,1280]{1,0:T(8,128)(2,1)S(1)}, u32[]{:S(2)}, u32[]{:S(2)}) collective-permute-start(bf16[176,1280]{1,0:T(8,128)(2,1)} %collective-permute-done.19.refs_6_), channel_id=1, source_target_pairs={{0,1},{1,0},{2,3},{3,2},{4,5},{5,4},{6,7},{7,6},{8,9},{9,8},{10,11... | collective-permute-start | bytes 1351688 | tf_op jit(solution)/shard_map/ppermute | solution.py:26
  125.6 21.0 %collective-permute-start.24 = (bf16[176,1280]{1,0:T(8,128)(2,1)S(1)}, bf16[176,1280]{1,0:T(8,128)(2,1)S(1)}, u32[]{:S(2)}, u32[]{:S(2)}) collective-permute-start(bf16[176,1280]{1,0:T(8,128)(2,1)S(1)} %collective-permute-done.22.refs_0_), channel_id=1, source_target_pairs={{0,2},{1,3},{2,0},{3,1},{4,6},{5,7},{6,4},{7,5},{8,10},{9,11},{10,... | collective-permute-start | bytes 1351688 | tf_op jit(solution)/shard_map/ppermute | solution.py:26
  126.7 21.4 %collective-permute-start.16 = (bf16[176,1280]{1,0:T(8,128)(2,1)S(1)}, bf16[176,1280]{1,0:T(8,128)(2,1)S(1)}, u32[]{:S(2)}, u32[]{:S(2)}) collective-permute-start(bf16[176,1280]{1,0:T(8,128)(2,1)S(1)} %collective-permute-done.15.refs_2_), channel_id=1, source_target_pairs={{0,1},{1,0},{2,3},{3,2},{4,5},{5,4},{6,7},{7,6},{8,9},{9,8},{10,11... | collective-permute-start | bytes 1351688 | tf_op jit(solution)/shard_map/ppermute | solution.py:26
  138.6 20.9 %collective-permute-start.27 = (bf16[176,1280]{1,0:T(8,128)(2,1)S(1)}, bf16[176,1280]{1,0:T(8,128)(2,1)S(1)}, u32[]{:S(2)}, u32[]{:S(2)}) collective-permute-start(bf16[176,1280]{1,0:T(8,128)(2,1)S(1)} %copy-done.33), channel_id=1, source_target_pairs={{0,1},{1,0},{2,3},{3,2},{4,5},{5,4},{6,7},{7,6},{8,9},{9,8},{10,11... | collective-permute-start | bytes 1351688 | tf_op jit(solution)/shard_map/ppermute | solution.py:26
  139.2 20.9 %collective-permute-start.23 = (bf16[176,1280]{1,0:T(8,128)(2,1)S(1)}, bf16[176,1280]{1,0:T(8,128)(2,1)S(1)}, u32[]{:S(2)}, u32[]{:S(2)}) collective-permute-start(bf16[176,1280]{1,0:T(8,128)(2,1)S(1)} %collective-permute-done.22.refs_0_), channel_id=1, source_target_pairs={{0,1},{1,0},{2,3},{3,2},{4,5},{5,4},{6,7},{7,6},{8,9},{9,8},{10,11... | collective-permute-start | bytes 1351688 | tf_op jit(solution)/shard_map/ppermute | solution.py:26
  139.3 22.4 %collective-permute-start.29 = (bf16[176,1280]{1,0:T(8,128)(2,1)S(1)}, bf16[176,1280]{1,0:T(8,128)(2,1)S(1)}, u32[]{:S(2)}, u32[]{:S(2)}) collective-permute-start(bf16[176,1280]{1,0:T(8,128)(2,1)S(1)} %collective-permute-done.28.refs_6_), channel_id=1, source_target_pairs={{0,1},{1,0},{2,3},{3,2},{4,5},{5,4},{6,7},{7,6},{8,9},{9,8},{10,11... | collective-permute-start | bytes 1351688 | tf_op jit(solution)/shard_map/ppermute | solution.py:26
  146.6 26.0 %collective-permute-start.5 = (bf16[320,1280]{1,0:T(8,128)(2,1)S(1)}, bf16[320,1280]{1,0:T(8,128)(2,1)S(1)}, u32[]{:S(2)}, u32[]{:S(2)}) collective-permute-start(bf16[320,1280]{1,0:T(8,128)(2,1)S(1)} %get-tuple-element.25), channel_id=1, source_target_pairs={{0,4},{1,5},{2,6},{3,7},{4,0},{5,1},{6,2},{7,3},{8,12},{9,13},{10,... | collective-permute-start | bytes 2457608 | tf_op jit(solution)/shard_map/ppermute | solution.py:26
  148.1 13.5 %collective-permute-start.25 = (bf16[176,1280]{1,0:T(8,128)(2,1)S(1)}, bf16[176,1280]{1,0:T(8,128)(2,1)S(1)}, u32[]{:S(2)}, u32[]{:S(2)}) collective-permute-start(bf16[176,1280]{1,0:T(8,128)(2,1)S(1)} %collective-permute-done.24.refs_2_), channel_id=1, source_target_pairs={{0,1},{1,0},{2,3},{3,2},{4,5},{5,4},{6,7},{7,6},{8,9},{9,8},{10,11... | collective-permute-start | bytes 1351688 | tf_op jit(solution)/shard_map/ppermute | solution.py:26
  159.5 25.8 %collective-permute-start.12 = (bf16[320,1280]{1,0:T(8,128)(2,1)S(1)}, bf16[320,1280]{1,0:T(8,128)(2,1)S(1)}, u32[]{:S(2)}, u32[]{:S(2)}) collective-permute-start(bf16[320,1280]{1,0:T(8,128)(2,1)S(1)} %get-tuple-element.29), channel_id=1, source_target_pairs={{0,4},{1,5},{2,6},{3,7},{4,0},{5,1},{6,2},{7,3},{8,12},{9,13},{10,... | collective-permute-start | bytes 2457608 | tf_op jit(solution)/shard_map/ppermute | solution.py:26
  160.1 42.7 %collective-permute-start.21 = (bf16[320,1280]{1,0:T(8,128)(2,1)S(1)}, bf16[320,1280]{1,0:T(8,128)(2,1)S(1)}, u32[]{:S(2)}, u32[]{:S(2)}) collective-permute-start(bf16[320,1280]{1,0:T(8,128)(2,1)S(1)} %get-tuple-element.33), channel_id=1, source_target_pairs={{0,4},{1,5},{2,6},{3,7},{4,0},{5,1},{6,2},{7,3},{8,12},{9,13},{10,... | collective-permute-start | bytes 2457608 | tf_op jit(solution)/shard_map/ppermute | solution.py:26
  172.0 47.1 %collective-permute-start.30 = (bf16[320,1280]{1,0:T(8,128)(2,1)S(1)}, bf16[320,1280]{1,0:T(8,128)(2,1)S(1)}, u32[]{:S(2)}, u32[]{:S(2)}) collective-permute-start(bf16[320,1280]{1,0:T(8,128)(2,1)S(1)} %get-tuple-element.37), channel_id=1, source_target_pairs={{0,4},{1,5},{2,6},{3,7},{4,0},{5,1},{6,2},{7,3},{8,12},{9,13},{10,... | collective-permute-start | bytes 2457608 | tf_op jit(solution)/shard_map/ppermute | solution.py:26
  228.9 4.6 %collective-permute-start.31 = (f32[8,128]{1,0:T(8,128)S(1)}, f32[8,128]{1,0:T(8,128)S(1)}, u32[]{:S(2)}, u32[]{:S(2)}) collective-permute-start(f32[8,128]{1,0:T(8,128)S(1)} %psum.7), channel_id=1, source_target_pairs={{0,16},{4,20},{8,24},{12,28},{16,0},{20,4},{24,8},{28,12},{1,17},{... | collective-permute-start | bytes 12296 | tf_op jit(solution)/shard_map/ppermute | solution.py:19
  (40 other events, 526.1 us)

commit v5 on v4

--- a/solution.py
+++ b/solution.py
@@ -10,7 +10,8 @@
 
 epsilon = 1e-06
 gather_levels_limit = 3
-vmem_bytes = 24 * 2**20
+vmem_bytes = 36 * 2**20
+vmem_most = 60 * 2**20
 
 
 def from_partner(value, axis, distance):
@@ -71,8 +72,7 @@
     return lax.dot_general(left, right, dims, preferred_element_type=jnp.float32)
 
 
-def call(kernel, name, flops, operands, shapes, after=(), **spec):
-    moved = sum(math.prod(a.shape) * a.dtype.itemsize for a in (*operands, *shapes))
+def call(kernel, name, operands, shapes, after=(), vmem=vmem_bytes, **spec):
     spec["in_specs"] = [pl.BlockSpec(memory_space=pl.ANY)] * len(after) + spec["in_specs"]
 
     def body(place_ref, *refs):
@@ -82,8 +82,8 @@
         body,
         grid_spec=pltpu.PrefetchScalarGridSpec(num_scalar_prefetch=1, **spec),
         out_shape=shapes,
-        compiler_params=pltpu.CompilerParams(vmem_limit_bytes=vmem_bytes),
-        cost_estimate=pl.CostEstimate(flops=flops, bytes_accessed=moved, transcendentals=0),
+        compiler_params=pltpu.CompilerParams(vmem_limit_bytes=vmem),
+        cost_estimate=pl.CostEstimate(flops=1, bytes_accessed=1, transcendentals=0),
         name=name,
     )(operands[0], *after, *operands[1:])
 
@@ -107,7 +107,7 @@
 CUBE = 0.044715
 
 
-def output_kernel(place_ref, rows_ref, w_in_ref, w_out_ref, out_ref, total):
+def output_kernel(place_ref, rows_ref, w_in_ref, w_out_ref, far_ref, near_ref, total):
     step = pl.program_id(0)
     v = jnp.dot(rows_ref[...], w_in_ref[...], preferred_element_type=jnp.float32)
     t = jnp.tanh(v * (SCALE + (SCALE * CUBE) * (v * v)))
@@ -124,29 +124,30 @@
 
     @pl.when(step == pl.num_programs(0) - 1)
     def _():
-        out_ref[...] = total[...]
-
-
-def output_half(place, which, inputs, w_in, w_out, after=()):
-    rows = inputs.shape[0] // 2
+        far_ref[...] = total[pl.ds(row_start(place_ref, far_ref, FAR), far_ref.shape[0]), :]
+        near_ref[...] = total[pl.ds(row_start(place_ref, near_ref, NEAR), near_ref.shape[0]), :]
+
+
+def output_halves(place, inputs, w_in, w_out):
+    rows = inputs.shape[0]
     depth, width = w_in.shape
     tile = tile_of(width, 256)
+    shape = jax.ShapeDtypeStruct((rows // 2, depth), jnp.float32)
     return call(
         output_kernel,
-        "output_half",
-        4 * rows * depth * width,
+        "output_halves",
         (place, inputs, w_in, w_out),
-        [jax.ShapeDtypeStruct((rows, depth), jnp.float32)],
-        after,
+        [shape, shape],
+        vmem=vmem_most,
         grid=(width // tile,),
         in_specs=[
-            pl.BlockSpec((rows, depth), lambda n, s: (s[which], 0)),
+            pl.BlockSpec((rows, depth), whole),
             pl.BlockSpec((depth, tile), column),
             pl.BlockSpec((tile, depth), lambda n, s: (n, 0)),
         ],
-        out_specs=[pl.BlockSpec((rows, depth), whole)],
+        out_specs=[pl.BlockSpec((rows // 2, depth), whole)] * 2,
         scratch_shapes=[pltpu.VMEM((rows, depth), jnp.float32)],
-    )[0]
+    )
 
 
 def add_kernel(place_ref, own_send, got_send, own_keep, got_keep, send_ref, keep_ref):
@@ -162,7 +163,6 @@
     return call(
         add_kernel,
         "add_and_split",
-        2 * rows * depth,
         (flag.reshape(1), own, got, own, got),
         [shape, shape],
         grid=(1,),
@@ -182,7 +182,6 @@
     return call(
         functools.partial(error_kernel, targets.shape[0]),
         "error_part",
-        3 * rows * depth,
         (place, own, got, targets),
         [jax.ShapeDtypeStruct((rows, depth), jnp.bfloat16)],
         grid=(1,),
@@ -221,7 +220,9 @@
     shift = pl.multiple_of(place_ref[SHIFT], step_rows)
     other_shift = pl.multiple_of(place_ref[OTHER_SHIFT], step_rows)
     v = jnp.dot(inputs[...], w_in_ref[...], preferred_element_type=jnp.float32)
-    back = jnp.dot(errors[...], w_out_ref[...], preferred_element_type=jnp.float32)
+    back = lax.dot_general(
+        errors[...], w_out_ref[...], (((1,), (1,)), ((), ())), preferred_element_type=jnp.float32
+    )
     square = v * v
     t = jnp.tanh(v * (SCALE + (SCALE * CUBE) * square))
     upper = 0.5 + 0.5 * t
@@ -236,7 +237,7 @@
     send_ref[:own, :] = spread_first[pl.ds(other_shift, own), :].astype(jnp.bfloat16)
 
 
-def gradient(place, members, errors, inputs, w_in, turned_w_out, after=()):
+def gradient(place, members, errors, inputs, w_in, w_out, after=()):
     error_arrays, error_wheres = zip(*errors)
     input_arrays, input_wheres = zip(*inputs)
     depth, width = w_in.shape
@@ -244,14 +245,14 @@
     own = depth // members
     reach = max(m * own % 128 + 2 * own for m in range(0, members, 2))
     window = -(-reach // 128)
-    tile = tile_of(width, 256)
+    tile = tile_of(width, 640)
+    once = pl.Buffered(1)
     return call(
         functools.partial(
             gradient_kernel, (error_wheres, input_wheres), window, own, math.gcd(own, 128)
         ),
         "gradient",
-        4 * rows * depth * width + 4 * rows * window * 128 * width,
-        (place, *error_arrays, *input_arrays, w_in, turned_w_out),
+        (place, *error_arrays, *input_arrays, w_in, w_out),
         [
             jax.ShapeDtypeStruct((own, width), jnp.float32),
             jax.ShapeDtypeStruct((own, width), jnp.float32),
@@ -259,8 +260,11 @@
         ],
         after,
         grid=(width // tile,),
-        in_specs=[pl.BlockSpec(a.shape, whole) for a in (*error_arrays, *input_arrays)]
-        + [pl.BlockSpec((depth, tile), column)] * 2,
+        in_specs=[
+            pl.BlockSpec(a.shape, whole, pipeline_mode=once)
+            for a in (*error_arrays, *input_arrays)
+        ]
+        + [pl.BlockSpec((depth, tile), column), pl.BlockSpec((tile, depth), lambda n, s: (n, 0))],
         out_specs=[
             pl.BlockSpec((own, tile), column),
             pl.BlockSpec((own, tile), column),
@@ -320,7 +324,6 @@
     return call(
         functools.partial(products_kernel, [len(slot) for slot in slots], fresh),
         "products",
-        4 * pairs * own * width,
         (place, *arrays, known),
         [jax.ShapeDtypeStruct(known.shape, jnp.float32)],
         after,
@@ -390,9 +393,9 @@
     return call(
         functools.partial(merge_kernel, [len(slot) for slot in slots]),
         "merge",
-        4 * len(slots) * own * width,
         (place, totals, *arrays),
         [shape, shape],
+        vmem=vmem_most,
         grid=(steps,),
         in_specs=[pl.BlockSpec(memory_space=pltpu.SMEM)] + specs,
         out_specs=[upper, upper],
@@ -443,12 +446,11 @@
         for m in range(1, members // 2)
     }
 
-    got = from_mask(output_half(place, FAR, inputs, w_in, w_out), 0, 1)
-    summed = output_half(place, NEAR, inputs, w_in, w_out)
+    send, summed = output_halves(place, inputs, w_in, w_out)
+    got = from_mask(send, 0, 1)
     for bit in range(1, shard_levels):
         send, summed = add_and_split(shard >> bit & 1, summed, got)
         got = from_mask(send, 0, 2**bit)
-    turned_w_out = ordered(w_out, send).T
     error = error_part(place, summed, got, targets)
 
     def spread_over_tensor(found):
@@ -467,17 +469,18 @@
         else:
             blocks[m] = spread_over_tensor({0: block})
 
-    slots = []
+    slots, known = [], []
     totals = jnp.zeros((8, 128), jnp.float32)
     for m in range(members // 2):
         first, second, send = gradient(
-            place, members, errors[m], blocks[m], w_in, turned_w_out
+            place, members, errors[m], blocks[m], w_in, w_out, known[-2:-1]
         )
         slots.append((first, second))
         if m == members // 2 - 1:
             totals = products(place, slots, 1, totals)
         slots.append((from_mask(send, others, 0),))
         totals = products(place, slots, 1 if m == members // 2 - 1 else 2, totals)
+        known.append(totals)
 
     totals = group_total(totals, gathered - 1, levels)
     pieces = merge(place, totals, slots)

time: 255 us -> 243 us (0.953)
  local copies, waits for them, and re-layouts: 36 us -> 10.7 us
  waiting for transfers between devices: 101 us -> 116 us
  Pallas kernels: 82.9 us -> 79.9 us
    unnamed x76 -> x40, local copies, waits for them, and re-layouts: 30.4 us -> 6.64 us
    ppermute x31, waiting for transfers between devices: 90.6 us -> 106 us  [from_mask(): return lax.ppermute(value, ('dp', 'tensor'), pairs)]
    optimization_barrier x1 -> x0, local copies, waits for them, and re-layouts: 3.42 us -> none  [ordered(): return lax.optimization_barrier((value, *before))[0]]
    pallas_call x14 -> x13, Pallas kernels: 82.9 us -> 79.9 us  [call(): pl.pallas_call(body, grid_spec=pltpu.PrefetchScalarGridSpec(num_scalar_pr...]
  transfers between devices with their start and end apart: 34 -> 34, of which waited for: 13 -> 16; matrix products, arithmetic and copies ran while one was open for 2% -> 1% of each run, Pallas kernels for 25% -> 21%
where the time goes in v5:
time: 243 us; the launch traced here: 242 us
  waiting for transfers between devices  116 us (48%)
  Pallas kernels  79.9 us (33%)
  starting transfers between devices  27.3 us (11%)
  local copies, waits for them, and re-layouts  10.7 us (4%)
  blocking collectives  5.92 us (2%)
    ppermute x31, waiting for transfers between devices, from_mask(): return lax.ppermute(value, ('dp', 'tensor'), pairs)  106 us
    pallas_call x13, Pallas kernels, call(): pl.pallas_call(body, grid_spec=pltpu.PrefetchScalarGridSpec(num_scalar_pr...  79.9 us
    ppermute x31, starting transfers between devices, from_mask(): return lax.ppermute(value, ('dp', 'tensor'), pairs)  25.7 us
    ppermute x3, waiting for transfers between devices, from_partner(): return lax.ppermute(value, axis, pairs)  10.2 us
    unnamed x40, local copies, waits for them, and re-layouts  6.64 us
    psum x1, blocking collectives, group_total(): summed = lax.psum(values, 'tensor')  5.92 us
  transfers between devices with their start and end apart: 34, of which 16 were waited for; matrix products, arithmetic and copies ran while one was open for 1% of the time, Pallas kernels for 21%

profile of v5, /device:TPU:0, one launch (start us, length us, event | category | flops | bytes accessed | tf_op | source)
XLA Modules:
  0.0 242.1 jit_solution(2820114136181837663)
XLA Ops:
  1.4 16.4 %output_halves.1 = (f32[352,1280]{1,0:T(8,128)}, f32[352,1280]{1,0:T(8,128)}) custom-call(s32[10]{0:T(128)} %stack.43.place_ref, bf16[704,1280]{1,0:T(8,128)(2,1)} %refs_4_.1, bf16[1280,1280]{1,0:T(8,128)(2,1)} %refs_9_.3, bf16[1280,1280]{1,0:T(8,128)(2,1)} %refs_10_.3), custom_call_target="tpu_custom_call" | custom-call | flops 1 | bytes 1 | tf_op jit(solution)/shard_map/output_halves/pallas_call | solution.py:81
  18.2 3.6 %collective-permute-done.refs_1_.refs_3_ = f32[352,1280]{1,0:T(8,128)S(1)} collective-permute-done((f32[352,1280]{1,0:T(8,128)}, f32[352,1280]{1,0:T(8,128)S(1)}, u32[]{:S(2)}, u32[]{:S(2)}) %collective-permute-start) | collective-permute-done | bytes 1802272 | tf_op jit(solution)/shard_map/ppermute | solution.py:27
  25.4 2.9 %collective-permute-start.1 = (f32[176,1280]{1,0:T(8,128)}, f32[176,1280]{1,0:T(8,128)}, u32[]{:S(2)}, u32[]{:S(2)}) collective-permute-start(f32[176,1280]{1,0:T(8,128)} %get-tuple-element.24), channel_id=1, source_target_pairs={{0,2},{1,3},{2,0},{3,1},{4,6},{5,7},{6,4},{7,5},{8,10},{9,11},{10,... | collective-permute-start | bytes 2703368 | tf_op jit(solution)/shard_map/ppermute | solution.py:27
  28.3 2.3 constant_dynamic-slice_fusion.1
  33.2 2.7 %collective-permute-start.17 = (bf16[176,1280]{1,0:T(8,128)(2,1)S(1)}, bf16[176,1280]{1,0:T(8,128)(2,1)S(1)}, u32[]{:S(2)}, u32[]{:S(2)}) collective-permute-start(bf16[176,1280]{1,0:T(8,128)(2,1)S(1)} %constant_dynamic-slice_fusion), channel_id=1, source_target_pairs={{0,16},{1,17},{2,18},{3,19},{4,20},{5,21},{6,22},{7,23},{8,24},{9,... | collective-permute-start | bytes 1351688 | tf_op jit(solution)/shard_map/ppermute | solution.py:27
  36.1 12.8 %collective-permute-done.1.refs_1_ = f32[176,1280]{1,0:T(8,128)} collective-permute-done((f32[176,1280]{1,0:T(8,128)}, f32[176,1280]{1,0:T(8,128)}, u32[]{:S(2)}, u32[]{:S(2)}) %collective-permute-start.1) | collective-permute-done | bytes 901152 | tf_op jit(solution)/shard_map/ppermute | solution.py:27
  51.6 2.1 error_part.1.refs_0_
  53.8 1.8 collective-permute-start.3
  55.6 6.9 %collective-permute-done.17.refs_5_ = bf16[176,1280]{1,0:T(8,128)(2,1)S(1)} collective-permute-done((bf16[176,1280]{1,0:T(8,128)(2,1)S(1)}, bf16[176,1280]{1,0:T(8,128)(2,1)S(1)}, u32[]{:S(2)}, u32[]{:S(2)}) %collective-permute-start.17) | collective-permute-done | bytes 450592 | tf_op jit(solution)/shard_map/ppermute | solution.py:27
  62.5 3.5 %collective-permute-start.6 = (bf16[176,1280]{1,0:T(8,128)(2,1)S(1)}, bf16[176,1280]{1,0:T(8,128)(2,1)S(1)}, u32[]{:S(2)}, u32[]{:S(2)}) collective-permute-start(bf16[176,1280]{1,0:T(8,128)(2,1)S(1)} %error_part.1.refs_0_), channel_id=1, source_target_pairs={{0,8},{1,9},{2,10},{3,11},{4,12},{5,13},{6,14},{7,15},{8,0},{9,1},... | collective-permute-start | bytes 1351688 | tf_op jit(solution)/shard_map/ppermute | solution.py:27
  66.1 9.1 %collective-permute-done.26.refs_5_ = bf16[176,1280]{1,0:T(8,128)(2,1)S(1)} collective-permute-done((bf16[176,1280]{1,0:T(8,128)(2,1)S(1)}, bf16[176,1280]{1,0:T(8,128)(2,1)S(1)}, u32[]{:S(2)}, u32[]{:S(2)}) %collective-permute-start.26) | collective-permute-done | bytes 450592 | tf_op jit(solution)/shard_map/ppermute | solution.py:27
  78.5 11.7 %collective-permute-done.6.refs_0_ = bf16[176,1280]{1,0:T(8,128)(2,1)S(1)} collective-permute-done((bf16[176,1280]{1,0:T(8,128)(2,1)S(1)}, bf16[176,1280]{1,0:T(8,128)(2,1)S(1)}, u32[]{:S(2)}, u32[]{:S(2)}) %collective-permute-start.6) | collective-permute-done | bytes 450592 | tf_op jit(solution)/shard_map/ppermute | solution.py:27
  90.2 18.5 %collective-permute-done.13.refs_1_ = bf16[176,1280]{1,0:T(8,128)(2,1)S(1)} collective-permute-done((bf16[176,1280]{1,0:T(8,128)(2,1)S(1)}, bf16[176,1280]{1,0:T(8,128)(2,1)S(1)}, u32[]{:S(2)}, u32[]{:S(2)}) %collective-permute-start.13) | collective-permute-done | bytes 450592 | tf_op jit(solution)/shard_map/ppermute | solution.py:27
  111.2 8.9 %collective-permute-done.28.refs_7_ = bf16[176,1280]{1,0:T(8,128)(2,1)S(1)} collective-permute-done((bf16[176,1280]{1,0:T(8,128)(2,1)S(1)}, bf16[176,1280]{1,0:T(8,128)(2,1)S(1)}, u32[]{:S(2)}, u32[]{:S(2)}) %collective-permute-start.28) | collective-permute-done | bytes 450592 | tf_op jit(solution)/shard_map/ppermute | solution.py:27
  120.7 6.0 %collective-permute-done.8.refs_2_ = bf16[176,1280]{1,0:T(8,128)(2,1)S(1)} collective-permute-done((bf16[176,1280]{1,0:T(8,128)(2,1)S(1)}, bf16[176,1280]{1,0:T(8,128)(2,1)S(1)}, u32[]{:S(2)}, u32[]{:S(2)}) %collective-permute-start.8) | collective-permute-done | bytes 450592 | tf_op jit(solution)/shard_map/ppermute | solution.py:27
  128.7 9.7 %gradient.4 = (f32[160,1280]{1,0:T(8,128)S(1)}, f32[160,1280]{1,0:T(8,128)S(1)}, bf16[320,1280]{1,0:T(8,128)(2,1)S(1)}) custom-call(s32[10]{0:T(128)S(1)} %copy-done.19, bf16[176,1280]{1,0:T(8,128)(2,1)S(1)} %error_part.1.refs_0_, bf16[176,1280]{1,0:T(8,128)(2,1)S(1)} %collective-permute-done.2.refs_1_, ...), custom_call_target="tpu_custom_call" | custom-call | flops 1 | bytes 1 | tf_op jit(solution)/shard_map/gradient/pallas_call | solution.py:81
  140.7 10.9 %gradient.5 = (f32[160,1280]{1,0:T(8,128)S(1)}, f32[160,1280]{1,0:T(8,128)S(1)}, bf16[320,1280]{1,0:T(8,128)(2,1)S(1)}) custom-call(s32[10]{0:T(128)S(1)} %copy-done.19, bf16[176,1280]{1,0:T(8,128)(2,1)S(1)} %collective-permute-done.6.refs_0_, bf16[176,1280]{1,0:T(8,128)(2,1)S(1)} %collective-permute-done.7.refs_1_, ...), custom_call_target="tpu_custom_call" | custom-call | flops 1 | bytes 1 | tf_op jit(solution)/shard_map/gradient/pallas_call | solution.py:81
  153.2 6.3 %collective-permute-done.5.refs_2_.refs_3_.refs_4_ = bf16[320,1280]{1,0:T(8,128)(2,1)S(1)} collective-permute-done((bf16[320,1280]{1,0:T(8,128)(2,1)S(1)}, bf16[320,1280]{1,0:T(8,128)(2,1)S(1)}, u32[]{:S(2)}, u32[]{:S(2)}) %collective-permute-start.5) | collective-permute-done | bytes 819232 | tf_op jit(solution)/shard_map/ppermute | solution.py:27
  161.0 9.7 %gradient.6 = (f32[160,1280]{1,0:T(8,128)S(1)}, f32[160,1280]{1,0:T(8,128)S(1)}, bf16[320,1280]{1,0:T(8,128)(2,1)S(1)}) custom-call(s32[10]{0:T(128)S(1)} %copy-done.19, f32[8,128]{1,0:T(8,128)S(1)} %products.5.refs_0_.refs_6_, bf16[176,1280]{1,0:T(8,128)(2,1)S(1)} %collective-permute-done.13.refs_1_, bf16[176,1280]{1,0:T(8,128)(2,1)S(1)} %collective-permute-done.14.refs_2_, ...), custom_call_target="tpu_custom_call" | custom-call | flops 1 | bytes 1 | tf_op jit(solution)/shard_map/gradient/pallas_call | solution.py:81
  170.7 5.5 %collective-permute-done.12.refs_5_.refs_7_.refs_8_ = bf16[320,1280]{1,0:T(8,128)(2,1)S(1)} collective-permute-done((bf16[320,1280]{1,0:T(8,128)(2,1)S(1)}, bf16[320,1280]{1,0:T(8,128)(2,1)S(1)}, u32[]{:S(2)}, u32[]{:S(2)}) %collective-permute-start.12) | collective-permute-done | bytes 819232 | tf_op jit(solution)/shard_map/ppermute | solution.py:27
  177.7 2.4 products.6.refs_0_.refs_9_
  180.1 9.7 %gradient.7 = (f32[160,1280]{1,0:T(8,128)S(1)}, f32[160,1280]{1,0:T(8,128)S(1)}, bf16[320,1280]{1,0:T(8,128)(2,1)S(1)}) custom-call(s32[10]{0:T(128)S(1)} %copy-done.19, f32[8,128]{1,0:T(8,128)S(1)} %products.6.refs_0_.refs_9_, bf16[176,1280]{1,0:T(8,128)(2,1)S(1)} %collective-permute-done.22.refs_1_, bf16[176,1280]{1,0:T(8,128)(2,1)S(1)} %collective-permute-done.23.refs_2_, ...), custom_call_target="tpu_custom_call" | custom-call | flops 1 | bytes 1 | tf_op jit(solution)/shard_map/gradient/pallas_call | solution.py:81
  190.4 7.0 %collective-permute-done.21.refs_8_.refs_11_.refs_12_ = bf16[320,1280]{1,0:T(8,128)(2,1)S(1)} collective-permute-done((bf16[320,1280]{1,0:T(8,128)(2,1)S(1)}, bf16[320,1280]{1,0:T(8,128)(2,1)S(1)}, u32[]{:S(2)}, u32[]{:S(2)}) %collective-permute-start.21) | collective-permute-done | bytes 819232 | tf_op jit(solution)/shard_map/ppermute | solution.py:27
  197.3 3.4 %products.7.refs_11_ = f32[8,128]{1,0:T(8,128)S(1)} custom-call(s32[10]{0:T(128)S(1)} %copy-done.19, f32[160,1280]{1,0:T(8,128)S(1)} %get-tuple-element.25.refs_0_.refs_1_, f32[160,1280]{1,0:T(8,128)S(1)} %get-tuple-element.26.refs_1_.refs_2_, bf16[320,1280]{1,0:T(8,128)(2,1)S(1)} %collective-permute-done.5.refs_2_.refs_3_.refs_4_, ...), custom_call_target="tpu_custom_call" | custom-call | flops 1 | bytes 1 | tf_op jit(solution)/shard_map/products/pallas_call | solution.py:81
  200.7 2.7 %products.8.refs_12_ = f32[8,128]{1,0:T(8,128)S(1)} custom-call(s32[10]{0:T(128)S(1)} %copy-done.19, f32[160,1280]{1,0:T(8,128)S(1)} %get-tuple-element.25.refs_0_.refs_1_, f32[160,1280]{1,0:T(8,128)S(1)} %get-tuple-element.26.refs_1_.refs_2_, bf16[320,1280]{1,0:T(8,128)(2,1)S(1)} %collective-permute-done.5.refs_2_.refs_3_.refs_4_, ...), custom_call_target="tpu_custom_call" | custom-call | flops 1 | bytes 1 | tf_op jit(solution)/shard_map/products/pallas_call | solution.py:81
  203.4 9.6 %collective-permute-done.30.refs_11_.refs_15_.refs_16_ = bf16[320,1280]{1,0:T(8,128)(2,1)S(1)} collective-permute-done((bf16[320,1280]{1,0:T(8,128)(2,1)S(1)}, bf16[320,1280]{1,0:T(8,128)(2,1)S(1)}, u32[]{:S(2)}, u32[]{:S(2)}) %collective-permute-start.30) | collective-permute-done | bytes 819232 | tf_op jit(solution)/shard_map/ppermute | solution.py:27
  213.1 3.2 %products.9 = f32[8,128]{1,0:T(8,128)S(1)} custom-call(s32[10]{0:T(128)S(1)} %copy-done.19, f32[160,1280]{1,0:T(8,128)S(1)} %get-tuple-element.25.refs_0_.refs_1_, f32[160,1280]{1,0:T(8,128)S(1)} %get-tuple-element.26.refs_1_.refs_2_, bf16[320,1280]{1,0:T(8,128)(2,1)S(1)} %collective-permute-done.5.refs_2_.refs_3_.refs_4_, ...), custom_call_target="tpu_custom_call" | custom-call | flops 1 | bytes 1 | tf_op jit(solution)/shard_map/products/pallas_call | solution.py:81
  216.3 5.9 %psum.7 = f32[8,128]{1,0:T(8,128)S(1)} all-reduce(f32[8,128]{1,0:T(8,128)S(1)} %products.9), channel_id=1, replica_groups=mesh['dp'=8,'tensor'=4] {'tensor'}, use_global_device_ids=true, to_apply=%region_0.1 | all-reduce | flops 1024 | bytes 8192 | tf_op jit(solution)/shard_map/psum | solution.py:42
  222.3 4.5 %collective-permute-done.31 = f32[8,128]{1,0:T(8,128)S(1)} collective-permute-done((f32[8,128]{1,0:T(8,128)S(1)}, f32[8,128]{1,0:T(8,128)S(1)}, u32[]{:S(2)}, u32[]{:S(2)}) %collective-permute-start.31) | collective-permute-done | bytes 4128 | tf_op jit(solution)/shard_map/ppermute | solution.py:20
  226.8 3.6 %collective-permute-done.32 = f32[8,128]{1,0:T(8,128)S(1)} collective-permute-done((f32[8,128]{1,0:T(8,128)S(1)}, f32[8,128]{1,0:T(8,128)S(1)}, u32[]{:S(2)}, u32[]{:S(2)}) %collective-permute-start.32) | collective-permute-done | bytes 4128 | tf_op jit(solution)/shard_map/ppermute | solution.py:20
  231.9 2.1 collective-permute-done.33
  234.6 7.3 %merge.1 = (f32[160,1280]{1,0:T(8,128)}, f32[160,1280]{1,0:T(8,128)}) custom-call(s32[10]{0:T(128)} %stack.43.place_ref, f32[8,128]{1,0:T(8,128)} %add.60.refs_0_, f32[160,1280]{1,0:T(8,128)} %copy-done.4, f32[160,1280]{1,0:T(8,128)} %copy-done.5, bf16[320,1280]{1,0:T(8,128)(2,1)} %copy-done.2, bf16[320,1280]{1,0:T(8,128)(2,1)} %copy-done.2, ...), custom_call_target="tpu_custom_call" | custom-call | flops 1 | bytes 1 | tf_op jit(solution)/shard_map/merge/pallas_call | solution.py:81
  (97 shorter events, 28.5 us)
Async XLA Ops:
  17.8 4.0 %collective-permute-start = (f32[352,1280]{1,0:T(8,128)}, f32[352,1280]{1,0:T(8,128)S(1)}, u32[]{:S(2)}, u32[]{:S(2)}) collective-permute-start(f32[352,1280]{1,0:T(8,128)} %get-tuple-element.22), channel_id=1, source_target_pairs={{0,1},{1,0},{2,3},{3,2},{4,5},{5,4},{6,7},{7,6},{8,9},{9,8},{10,11... | collective-permute-start | bytes 5406728 | tf_op jit(solution)/shard_map/ppermute | solution.py:27
  25.4 23.5 %collective-permute-start.1 = (f32[176,1280]{1,0:T(8,128)}, f32[176,1280]{1,0:T(8,128)}, u32[]{:S(2)}, u32[]{:S(2)}) collective-permute-start(f32[176,1280]{1,0:T(8,128)} %get-tuple-element.24), channel_id=1, source_target_pairs={{0,2},{1,3},{2,0},{3,1},{4,6},{5,7},{6,4},{7,5},{8,10},{9,11},{10,... | collective-permute-start | bytes 2703368 | tf_op jit(solution)/shard_map/ppermute | solution.py:27
  30.6 46.0 %collective-permute-start.10 = (bf16[352,1280]{1,0:T(8,128)(2,1)}, bf16[352,1280]{1,0:T(8,128)(2,1)}, u32[]{:S(2)}, u32[]{:S(2)}) collective-permute-start(bf16[352,1280]{1,0:T(8,128)(2,1)} %constant_dynamic-slice_fusion.1), channel_id=1, source_target_pairs={{0,8},{1,9},{2,10},{3,11},{4,12},{5,13},{6,14},{7,15},{8,0},{9,1},... | collective-permute-start | bytes 2703368 | tf_op jit(solution)/shard_map/ppermute | solution.py:27
  33.2 29.3 %collective-permute-start.17 = (bf16[176,1280]{1,0:T(8,128)(2,1)S(1)}, bf16[176,1280]{1,0:T(8,128)(2,1)S(1)}, u32[]{:S(2)}, u32[]{:S(2)}) collective-permute-start(bf16[176,1280]{1,0:T(8,128)(2,1)S(1)} %constant_dynamic-slice_fusion), channel_id=1, source_target_pairs={{0,16},{1,17},{2,18},{3,19},{4,20},{5,21},{6,22},{7,23},{8,24},{9,... | collective-permute-start | bytes 1351688 | tf_op jit(solution)/shard_map/ppermute | solution.py:27
  35.9 39.2 %collective-permute-start.26 = (bf16[176,1280]{1,0:T(8,128)(2,1)S(1)}, bf16[176,1280]{1,0:T(8,128)(2,1)S(1)}, u32[]{:S(2)}, u32[]{:S(2)}) collective-permute-start(bf16[176,1280]{1,0:T(8,128)(2,1)S(1)} %constant_dynamic-slice_fusion), channel_id=1, source_target_pairs={{0,24},{1,25},{2,26},{3,27},{4,28},{5,29},{6,30},{7,31},{8,16},{9,... | collective-permute-start | bytes 1351688 | tf_op jit(solution)/shard_map/ppermute | solution.py:27
  53.7 22.9 %collective-permute-start.2 = (bf16[176,1280]{1,0:T(8,128)(2,1)S(1)}, bf16[176,1280]{1,0:T(8,128)(2,1)S(1)}, u32[]{:S(2)}, u32[]{:S(2)}) collective-permute-start(bf16[176,1280]{1,0:T(8,128)(2,1)S(1)} %error_part.1.refs_0_), channel_id=1, source_target_pairs={{0,1},{1,0},{2,3},{3,2},{4,5},{5,4},{6,7},{7,6},{8,9},{9,8},{10,11... | collective-permute-start | bytes 1351688 | tf_op jit(solution)/shard_map/ppermute | solution.py:27
  53.8 23.5 %collective-permute-start.3 = (bf16[176,1280]{1,0:T(8,128)(2,1)S(1)}, bf16[176,1280]{1,0:T(8,128)(2,1)S(1)}, u32[]{:S(2)}, u32[]{:S(2)}) collective-permute-start(bf16[176,1280]{1,0:T(8,128)(2,1)S(1)} %error_part.1.refs_0_), channel_id=1, source_target_pairs={{0,2},{1,3},{2,0},{3,1},{4,6},{5,7},{6,4},{7,5},{8,10},{9,11},{10,... | collective-permute-start | bytes 1351688 | tf_op jit(solution)/shard_map/ppermute | solution.py:27
  62.5 27.7 %collective-permute-start.6 = (bf16[176,1280]{1,0:T(8,128)(2,1)S(1)}, bf16[176,1280]{1,0:T(8,128)(2,1)S(1)}, u32[]{:S(2)}, u32[]{:S(2)}) collective-permute-start(bf16[176,1280]{1,0:T(8,128)(2,1)S(1)} %error_part.1.refs_0_), channel_id=1, source_target_pairs={{0,8},{1,9},{2,10},{3,11},{4,12},{5,13},{6,14},{7,15},{8,0},{9,1},... | collective-permute-start | bytes 1351688 | tf_op jit(solution)/shard_map/ppermute | solution.py:27
  75.1 33.5 %collective-permute-start.13 = (bf16[176,1280]{1,0:T(8,128)(2,1)S(1)}, bf16[176,1280]{1,0:T(8,128)(2,1)S(1)}, u32[]{:S(2)}, u32[]{:S(2)}) collective-permute-start(bf16[176,1280]{1,0:T(8,128)(2,1)S(1)} %error_part.1.refs_0_), channel_id=1, source_target_pairs={{0,16},{1,17},{2,18},{3,19},{4,20},{5,21},{6,22},{7,23},{8,24},{9,... | collective-permute-start | bytes 1351688 | tf_op jit(solution)/shard_map/ppermute | solution.py:27
  76.6 32.6 %collective-permute-start.18 = (bf16[176,1280]{1,0:T(8,128)(2,1)S(1)}, bf16[176,1280]{1,0:T(8,128)(2,1)S(1)}, u32[]{:S(2)}, u32[]{:S(2)}) collective-permute-start(bf16[176,1280]{1,0:T(8,128)(2,1)S(1)} %collective-permute-done.17.refs_5_), channel_id=1, source_target_pairs={{0,1},{1,0},{2,3},{3,2},{4,5},{5,4},{6,7},{7,6},{8,9},{9,8},{10,11... | collective-permute-start | bytes 1351688 | tf_op jit(solution)/shard_map/ppermute | solution.py:27
  76.6 34.0 %collective-permute-start.19 = (bf16[176,1280]{1,0:T(8,128)(2,1)S(1)}, bf16[176,1280]{1,0:T(8,128)(2,1)S(1)}, u32[]{:S(2)}, u32[]{:S(2)}) collective-permute-start(bf16[176,1280]{1,0:T(8,128)(2,1)S(1)} %collective-permute-done.17.refs_5_), channel_id=1, source_target_pairs={{0,2},{1,3},{2,0},{3,1},{4,6},{5,7},{6,4},{7,5},{8,10},{9,11},{10,... | collective-permute-start | bytes 1351688 | tf_op jit(solution)/shard_map/ppermute | solution.py:27
  77.2 33.4 %collective-permute-start.22 = (bf16[176,1280]{1,0:T(8,128)(2,1)S(1)}, bf16[176,1280]{1,0:T(8,128)(2,1)S(1)}, u32[]{:S(2)}, u32[]{:S(2)}) collective-permute-start(bf16[176,1280]{1,0:T(8,128)(2,1)S(1)} %error_part.1.refs_0_), channel_id=1, source_target_pairs={{0,24},{1,25},{2,26},{3,27},{4,28},{5,29},{6,30},{7,31},{8,16},{9,... | collective-permute-start | bytes 1351688 | tf_op jit(solution)/shard_map/ppermute | solution.py:27
  90.2 49.8 %collective-permute-start.11 = (bf16[352,1280]{1,0:T(8,128)(2,1)}, bf16[352,1280]{1,0:T(8,128)(2,1)S(1)}, u32[]{:S(2)}, u32[]{:S(2)}) collective-permute-start(bf16[352,1280]{1,0:T(8,128)(2,1)} %collective-permute-done.10.refs_4_), channel_id=1, source_target_pairs={{0,1},{1,0},{2,3},{3,2},{4,5},{5,4},{6,7},{7,6},{8,9},{9,8},{10,11... | collective-permute-start | bytes 2703368 | tf_op jit(solution)/shard_map/ppermute | solution.py:27
  108.6 11.5 %collective-permute-start.28 = (bf16[176,1280]{1,0:T(8,128)(2,1)S(1)}, bf16[176,1280]{1,0:T(8,128)(2,1)S(1)}, u32[]{:S(2)}, u32[]{:S(2)}) collective-permute-start(bf16[176,1280]{1,0:T(8,128)(2,1)S(1)} %collective-permute-done.26.refs_5_), channel_id=1, source_target_pairs={{0,2},{1,3},{2,0},{3,1},{4,6},{5,7},{6,4},{7,5},{8,10},{9,11},{10,... | collective-permute-start | bytes 1351688 | tf_op jit(solution)/shard_map/ppermute | solution.py:27
  109.2 17.5 %collective-permute-start.8 = (bf16[176,1280]{1,0:T(8,128)(2,1)S(1)}, bf16[176,1280]{1,0:T(8,128)(2,1)S(1)}, u32[]{:S(2)}, u32[]{:S(2)}) collective-permute-start(bf16[176,1280]{1,0:T(8,128)(2,1)S(1)} %collective-permute-done.6.refs_0_), channel_id=1, source_target_pairs={{0,2},{1,3},{2,0},{3,1},{4,6},{5,7},{6,4},{7,5},{8,10},{9,11},{10,... | collective-permute-start | bytes 1351688 | tf_op jit(solution)/shard_map/ppermute | solution.py:27
  110.7 16.0 %collective-permute-start.4 = (bf16[176,1280]{1,0:T(8,128)(2,1)S(1)}, bf16[176,1280]{1,0:T(8,128)(2,1)S(1)}, u32[]{:S(2)}, u32[]{:S(2)}) collective-permute-start(bf16[176,1280]{1,0:T(8,128)(2,1)S(1)} %collective-permute-done.3.refs_2_), channel_id=1, source_target_pairs={{0,1},{1,0},{2,3},{3,2},{4,5},{5,4},{6,7},{7,6},{8,9},{9,8},{10,11... | collective-permute-start | bytes 1351688 | tf_op jit(solution)/shard_map/ppermute | solution.py:27
  110.7 27.7 %collective-permute-start.7 = (bf16[176,1280]{1,0:T(8,128)(2,1)S(1)}, bf16[176,1280]{1,0:T(8,128)(2,1)S(1)}, u32[]{:S(2)}, u32[]{:S(2)}) collective-permute-start(bf16[176,1280]{1,0:T(8,128)(2,1)S(1)} %collective-permute-done.6.refs_0_), channel_id=1, source_target_pairs={{0,1},{1,0},{2,3},{3,2},{4,5},{5,4},{6,7},{7,6},{8,9},{9,8},{10,11... | collective-permute-start | bytes 1351688 | tf_op jit(solution)/shard_map/ppermute | solution.py:27
  120.1 19.8 %collective-permute-start.15 = (bf16[176,1280]{1,0:T(8,128)(2,1)S(1)}, bf16[176,1280]{1,0:T(8,128)(2,1)S(1)}, u32[]{:S(2)}, u32[]{:S(2)}) collective-permute-start(bf16[176,1280]{1,0:T(8,128)(2,1)S(1)} %collective-permute-done.13.refs_1_), channel_id=1, source_target_pairs={{0,2},{1,3},{2,0},{3,1},{4,6},{5,7},{6,4},{7,5},{8,10},{9,11},{10,... | collective-permute-start | bytes 1351688 | tf_op jit(solution)/shard_map/ppermute | solution.py:27
  126.7 13.9 %collective-permute-start.9 = (bf16[176,1280]{1,0:T(8,128)(2,1)S(1)}, bf16[176,1280]{1,0:T(8,128)(2,1)S(1)}, u32[]{:S(2)}, u32[]{:S(2)}) collective-permute-start(bf16[176,1280]{1,0:T(8,128)(2,1)S(1)} %collective-permute-done.8.refs_2_), channel_id=1, source_target_pairs={{0,1},{1,0},{2,3},{3,2},{4,5},{5,4},{6,7},{7,6},{8,9},{9,8},{10,11... | collective-permute-start | bytes 1351688 | tf_op jit(solution)/shard_map/ppermute | solution.py:27
  126.7 25.0 %collective-permute-start.14 = (bf16[176,1280]{1,0:T(8,128)(2,1)S(1)}, bf16[176,1280]{1,0:T(8,128)(2,1)S(1)}, u32[]{:S(2)}, u32[]{:S(2)}) collective-permute-start(bf16[176,1280]{1,0:T(8,128)(2,1)S(1)} %collective-permute-done.13.refs_1_), channel_id=1, source_target_pairs={{0,1},{1,0},{2,3},{3,2},{4,5},{5,4},{6,7},{7,6},{8,9},{9,8},{10,11... | collective-permute-start | bytes 1351688 | tf_op jit(solution)/shard_map/ppermute | solution.py:27
  138.4 21.2 %collective-permute-start.5 = (bf16[320,1280]{1,0:T(8,128)(2,1)S(1)}, bf16[320,1280]{1,0:T(8,128)(2,1)S(1)}, u32[]{:S(2)}, u32[]{:S(2)}) collective-permute-start(bf16[320,1280]{1,0:T(8,128)(2,1)S(1)} %get-tuple-element.27), channel_id=1, source_target_pairs={{0,4},{1,5},{2,6},{3,7},{4,0},{5,1},{6,2},{7,3},{8,12},{9,13},{10,... | collective-permute-start | bytes 2457608 | tf_op jit(solution)/shard_map/ppermute | solution.py:27
  140.0 12.3 %collective-permute-start.20 = (bf16[176,1280]{1,0:T(8,128)(2,1)S(1)}, bf16[176,1280]{1,0:T(8,128)(2,1)S(1)}, u32[]{:S(2)}, u32[]{:S(2)}) collective-permute-start(bf16[176,1280]{1,0:T(8,128)(2,1)S(1)} %collective-permute-done.19.refs_7_), channel_id=1, source_target_pairs={{0,1},{1,0},{2,3},{3,2},{4,5},{5,4},{6,7},{7,6},{8,9},{9,8},{10,11... | collective-permute-start | bytes 1351688 | tf_op jit(solution)/shard_map/ppermute | solution.py:27
  140.0 12.8 %collective-permute-start.24 = (bf16[176,1280]{1,0:T(8,128)(2,1)S(1)}, bf16[176,1280]{1,0:T(8,128)(2,1)S(1)}, u32[]{:S(2)}, u32[]{:S(2)}) collective-permute-start(bf16[176,1280]{1,0:T(8,128)(2,1)S(1)} %collective-permute-done.22.refs_1_), channel_id=1, source_target_pairs={{0,2},{1,3},{2,0},{3,1},{4,6},{5,7},{6,4},{7,5},{8,10},{9,11},{10,... | collective-permute-start | bytes 1351688 | tf_op jit(solution)/shard_map/ppermute | solution.py:27
  140.6 12.2 %collective-permute-start.16 = (bf16[176,1280]{1,0:T(8,128)(2,1)S(1)}, bf16[176,1280]{1,0:T(8,128)(2,1)S(1)}, u32[]{:S(2)}, u32[]{:S(2)}) collective-permute-start(bf16[176,1280]{1,0:T(8,128)(2,1)S(1)} %collective-permute-done.15.refs_3_), channel_id=1, source_target_pairs={{0,1},{1,0},{2,3},{3,2},{4,5},{5,4},{6,7},{7,6},{8,9},{9,8},{10,11... | collective-permute-start | bytes 1351688 | tf_op jit(solution)/shard_map/ppermute | solution.py:27
  151.6 24.5 %collective-permute-start.12 = (bf16[320,1280]{1,0:T(8,128)(2,1)S(1)}, bf16[320,1280]{1,0:T(8,128)(2,1)S(1)}, u32[]{:S(2)}, u32[]{:S(2)}) collective-permute-start(bf16[320,1280]{1,0:T(8,128)(2,1)S(1)} %get-tuple-element.31), channel_id=1, source_target_pairs={{0,4},{1,5},{2,6},{3,7},{4,0},{5,1},{6,2},{7,3},{8,12},{9,13},{10,... | collective-permute-start | bytes 2457608 | tf_op jit(solution)/shard_map/ppermute | solution.py:27
  152.2 27.9 %collective-permute-start.27 = (bf16[176,1280]{1,0:T(8,128)(2,1)S(1)}, bf16[176,1280]{1,0:T(8,128)(2,1)S(1)}, u32[]{:S(2)}, u32[]{:S(2)}) collective-permute-start(bf16[176,1280]{1,0:T(8,128)(2,1)S(1)} %collective-permute-done.26.refs_5_), channel_id=1, source_target_pairs={{0,1},{1,0},{2,3},{3,2},{4,5},{5,4},{6,7},{7,6},{8,9},{9,8},{10,11... | collective-permute-start | bytes 1351688 | tf_op jit(solution)/shard_map/ppermute | solution.py:27
  152.7 27.4 %collective-permute-start.23 = (bf16[176,1280]{1,0:T(8,128)(2,1)S(1)}, bf16[176,1280]{1,0:T(8,128)(2,1)S(1)}, u32[]{:S(2)}, u32[]{:S(2)}) collective-permute-start(bf16[176,1280]{1,0:T(8,128)(2,1)S(1)} %collective-permute-done.22.refs_1_), channel_id=1, source_target_pairs={{0,1},{1,0},{2,3},{3,2},{4,5},{5,4},{6,7},{7,6},{8,9},{9,8},{10,11... | collective-permute-start | bytes 1351688 | tf_op jit(solution)/shard_map/ppermute | solution.py:27
  152.7 27.4 %collective-permute-start.29 = (bf16[176,1280]{1,0:T(8,128)(2,1)S(1)}, bf16[176,1280]{1,0:T(8,128)(2,1)S(1)}, u32[]{:S(2)}, u32[]{:S(2)}) collective-permute-start(bf16[176,1280]{1,0:T(8,128)(2,1)S(1)} %collective-permute-done.28.refs_7_), channel_id=1, source_target_pairs={{0,1},{1,0},{2,3},{3,2},{4,5},{5,4},{6,7},{7,6},{8,9},{9,8},{10,11... | collective-permute-start | bytes 1351688 | tf_op jit(solution)/shard_map/ppermute | solution.py:27
  159.6 20.6 %collective-permute-start.25 = (bf16[176,1280]{1,0:T(8,128)(2,1)S(1)}, bf16[176,1280]{1,0:T(8,128)(2,1)S(1)}, u32[]{:S(2)}, u32[]{:S(2)}) collective-permute-start(bf16[176,1280]{1,0:T(8,128)(2,1)S(1)} %collective-permute-done.24.refs_3_), channel_id=1, source_target_pairs={{0,1},{1,0},{2,3},{3,2},{4,5},{5,4},{6,7},{7,6},{8,9},{9,8},{10,11... | collective-permute-start | bytes 1351688 | tf_op jit(solution)/shard_map/ppermute | solution.py:27
  176.2 21.2 %collective-permute-start.21 = (bf16[320,1280]{1,0:T(8,128)(2,1)S(1)}, bf16[320,1280]{1,0:T(8,128)(2,1)S(1)}, u32[]{:S(2)}, u32[]{:S(2)}) collective-permute-start(bf16[320,1280]{1,0:T(8,128)(2,1)S(1)} %get-tuple-element.35), channel_id=1, source_target_pairs={{0,4},{1,5},{2,6},{3,7},{4,0},{5,1},{6,2},{7,3},{8,12},{9,13},{10,... | collective-permute-start | bytes 2457608 | tf_op jit(solution)/shard_map/ppermute | solution.py:27
  189.8 23.2 %collective-permute-start.30 = (bf16[320,1280]{1,0:T(8,128)(2,1)S(1)}, bf16[320,1280]{1,0:T(8,128)(2,1)S(1)}, u32[]{:S(2)}, u32[]{:S(2)}) collective-permute-start(bf16[320,1280]{1,0:T(8,128)(2,1)S(1)} %get-tuple-element.39), channel_id=1, source_target_pairs={{0,4},{1,5},{2,6},{3,7},{4,0},{5,1},{6,2},{7,3},{8,12},{9,13},{10,... | collective-permute-start | bytes 2457608 | tf_op jit(solution)/shard_map/ppermute | solution.py:27
  222.2 4.6 %collective-permute-start.31 = (f32[8,128]{1,0:T(8,128)S(1)}, f32[8,128]{1,0:T(8,128)S(1)}, u32[]{:S(2)}, u32[]{:S(2)}) collective-permute-start(f32[8,128]{1,0:T(8,128)S(1)} %psum.7), channel_id=1, source_target_pairs={{0,16},{4,20},{8,24},{12,28},{16,0},{20,4},{24,8},{28,12},{1,17},{... | collective-permute-start | bytes 12296 | tf_op jit(solution)/shard_map/ppermute | solution.py:20
  (22 other events, 724.8 us)

commit v6 on v5

--- a/solution.py
+++ b/solution.py
@@ -11,6 +11,7 @@
 epsilon = 1e-06
 gather_levels_limit = 3
 vmem_bytes = 36 * 2**20
+vmem_large = 46 * 2**20
 vmem_most = 60 * 2**20
 
 
@@ -88,7 +89,7 @@
     )(operands[0], *after, *operands[1:])
 
 
-WINDOW, SHIFT, OTHER_SHIFT, MEMBER, NEAR, FAR, PARTS = range(7)
+WINDOW, SHIFT, OTHER_SHIFT, MEMBER, NEAR, FAR, ZERO, PARTS = range(8)
 
 
 def row_start(place_ref, block, where):
@@ -107,47 +108,75 @@
 CUBE = 0.044715
 
 
-def output_kernel(place_ref, rows_ref, w_in_ref, w_out_ref, far_ref, near_ref, total):
+def forward_kernel(steps, place_ref, rows_ref, w_in_ref, w_out_ref, out_ref, near_ref, hidden):
     step = pl.program_id(0)
-    v = jnp.dot(rows_ref[...], w_in_ref[...], preferred_element_type=jnp.float32)
-    t = jnp.tanh(v * (SCALE + (SCALE * CUBE) * (v * v)))
-    hidden = (v * (0.5 + 0.5 * t)).astype(jnp.bfloat16)
-    part = jnp.dot(hidden, w_out_ref[...], preferred_element_type=jnp.float32)
-
-    @pl.when(step == 0)
+    half = out_ref.shape[0]
+    far = pl.ds(row_start(place_ref, out_ref, FAR), half)
+    tile = w_in_ref.shape[1]
+
+    for n in range(steps):
+
+        @pl.when(step == n)
+        def _():
+            v = jnp.dot(rows_ref[...], w_in_ref[...], preferred_element_type=jnp.float32)
+            t = jnp.tanh(v * (SCALE + (SCALE * CUBE) * (v * v)))
+            hidden[:, n * tile : (n + 1) * tile] = (v * (0.5 + 0.5 * t)).astype(jnp.bfloat16)
+
+    @pl.when(step == steps)
     def _():
-        total[...] = part
-
-    @pl.when(step > 0)
+        near_ref[...] = hidden[pl.ds(row_start(place_ref, out_ref, NEAR), half), :]
+
+    @pl.when(step >= steps)
     def _():
-        total[...] += part
-
-    @pl.when(step == pl.num_programs(0) - 1)
-    def _():
-        far_ref[...] = total[pl.ds(row_start(place_ref, far_ref, FAR), far_ref.shape[0]), :]
-        near_ref[...] = total[pl.ds(row_start(place_ref, near_ref, NEAR), near_ref.shape[0]), :]
-
-
-def output_halves(place, inputs, w_in, w_out):
+        out_ref[...] = jnp.dot(hidden[far, :], w_out_ref[...], preferred_element_type=jnp.float32)
+
+
+def forward(place, inputs, w_in, w_out):
     rows = inputs.shape[0]
     depth, width = w_in.shape
-    tile = tile_of(width, 256)
-    shape = jax.ShapeDtypeStruct((rows // 2, depth), jnp.float32)
-    return call(
-        output_kernel,
-        "output_halves",
+    tile, out_tile = tile_of(width, 640), tile_of(depth, 640)
+    steps = width // tile
+    last = lambda n: jnp.maximum(n - steps, 0)
+    return call(
+        functools.partial(forward_kernel, steps),
+        "forward",
         (place, inputs, w_in, w_out),
-        [shape, shape],
+        [
+            jax.ShapeDtypeStruct((rows // 2, depth), jnp.float32),
+            jax.ShapeDtypeStruct((rows // 2, width), jnp.bfloat16),
+        ],
         vmem=vmem_most,
-        grid=(width // tile,),
+        grid=(steps + depth // out_tile,),
         in_specs=[
             pl.BlockSpec((rows, depth), whole),
-            pl.BlockSpec((depth, tile), column),
-            pl.BlockSpec((tile, depth), lambda n, s: (n, 0)),
-        ],
-        out_specs=[pl.BlockSpec((rows // 2, depth), whole)] * 2,
-        scratch_shapes=[pltpu.VMEM((rows, depth), jnp.float32)],
-    )
+            pl.BlockSpec((depth, tile), lambda n, s: (0, jnp.minimum(n, steps - 1))),
+            pl.BlockSpec((width, out_tile), lambda n, s: (0, last(n))),
+        ],
+        out_specs=[
+            pl.BlockSpec((rows // 2, out_tile), lambda n, s: (0, last(n))),
+            pl.BlockSpec((rows // 2, width), whole),
+        ],
+        scratch_shapes=[pltpu.VMEM((rows, width), jnp.bfloat16)],
+    )
+
+
+def product_kernel(place_ref, left_ref, right_ref, out_ref):
+    out_ref[...] = jnp.dot(left_ref[...], right_ref[...], preferred_element_type=jnp.float32)
+
+
+def product(place, left, right):
+    rows, depth = left.shape
+    width = right.shape[1]
+    tile = tile_of(width, 640)
+    return call(
+        product_kernel,
+        "product",
+        (place, left, right),
+        [jax.ShapeDtypeStruct((rows, width), jnp.float32)],
+        grid=(width // tile,),
+        in_specs=[pl.BlockSpec((rows, depth), whole), pl.BlockSpec((depth, tile), column)],
+        out_specs=[pl.BlockSpec((rows, tile), column)],
+    )[0]
 
 
 def add_kernel(place_ref, own_send, got_send, own_keep, got_keep, send_ref, keep_ref):
@@ -194,28 +223,23 @@
     )[0]
 
 
-def gradient_kernel(wheres, window, own, step_rows, place_ref, *refs):
-    error_wheres, input_wheres = wheres
-    refs = list(refs)
-
-    def take(n):
-        taken = refs[:n]
-        del refs[:n]
-        return taken
-
-    error_refs, input_refs = take(len(error_wheres)), take(len(input_wheres))
-    w_in_ref, w_out_ref, first_ref, second_ref, send_ref = take(5)
-    errors, inputs, inputs_turned, errors_turned, spread_first, spread_second = refs
+def gradient_kernel(wheres, worker, window, own, step_rows, place_ref, *refs):
+    error_refs, refs = refs[: len(wheres)], refs[len(wheres) :]
+    all_inputs, w_in_ref, w_out_ref, first_ref, second_ref, send_ref = refs[:6]
+    errors, inputs, inputs_turned, errors_turned, spread_first, spread_second, done = refs[6:]
 
     @pl.when(pl.program_id(0) == 0)
     def _():
-        for block, where in zip(error_refs, error_wheres):
+        rows = inputs.shape[0]
+        start = pl.multiple_of(place_ref[worker] * rows, 16)
+        fetch = pltpu.make_async_copy(all_inputs.at[pl.ds(start, rows), :], inputs, done)
+        fetch.start()
+        for block, where in zip(error_refs, wheres):
             errors[pl.ds(row_start(place_ref, block, where), block.shape[0]), :] = block[...]
-        for block, where in zip(input_refs, input_wheres):
-            inputs[pl.ds(row_start(place_ref, block, where), block.shape[0]), :] = block[...]
         lane = pl.multiple_of(place_ref[WINDOW] * 128, 128)
+        errors_turned[...] = errors[:, pl.ds(lane, window * 128)].T
+        fetch.wait()
         inputs_turned[...] = inputs[:, pl.ds(lane, window * 128)].T
-        errors_turned[...] = errors[:, pl.ds(lane, window * 128)].T
 
     shift = pl.multiple_of(place_ref[SHIFT], step_rows)
     other_shift = pl.multiple_of(place_ref[OTHER_SHIFT], step_rows)
@@ -237,34 +261,32 @@
     send_ref[:own, :] = spread_first[pl.ds(other_shift, own), :].astype(jnp.bfloat16)
 
 
-def gradient(place, members, errors, inputs, w_in, w_out, after=()):
-    error_arrays, error_wheres = zip(*errors)
-    input_arrays, input_wheres = zip(*inputs)
+def gradient(place, members, rows, errors, inputs, worker, w_in, w_out, after=()):
+    arrays, wheres = zip(*errors)
     depth, width = w_in.shape
-    rows = sum(a.shape[0] for a in input_arrays)
     own = depth // members
     reach = max(m * own % 128 + 2 * own for m in range(0, members, 2))
     window = -(-reach // 128)
     tile = tile_of(width, 640)
     once = pl.Buffered(1)
     return call(
-        functools.partial(
-            gradient_kernel, (error_wheres, input_wheres), window, own, math.gcd(own, 128)
-        ),
+        functools.partial(gradient_kernel, wheres, worker, window, own, math.gcd(own, 128)),
         "gradient",
-        (place, *error_arrays, *input_arrays, w_in, w_out),
+        (place, *arrays, inputs, w_in, w_out),
         [
             jax.ShapeDtypeStruct((own, width), jnp.float32),
             jax.ShapeDtypeStruct((own, width), jnp.float32),
             jax.ShapeDtypeStruct((2 * own, width), jnp.bfloat16),
         ],
         after,
+        vmem=vmem_large,
         grid=(width // tile,),
-        in_specs=[
-            pl.BlockSpec(a.shape, whole, pipeline_mode=once)
-            for a in (*error_arrays, *input_arrays)
-        ]
-        + [pl.BlockSpec((depth, tile), column), pl.BlockSpec((tile, depth), lambda n, s: (n, 0))],
+        in_specs=[pl.BlockSpec(a.shape, whole, pipeline_mode=once) for a in arrays]
+        + [
+            pl.BlockSpec(memory_space=pltpu.HBM),
+            pl.BlockSpec((depth, tile), column),
+            pl.BlockSpec((tile, depth), lambda n, s: (n, 0)),
+        ],
         out_specs=[
             pl.BlockSpec((own, tile), column),
             pl.BlockSpec((own, tile), column),
@@ -277,6 +299,7 @@
             pltpu.VMEM((window * 128, rows), jnp.bfloat16),
             pltpu.VMEM((window * 128, tile), jnp.float32),
             pltpu.VMEM((window * 128, tile), jnp.float32),
+            pltpu.SemaphoreType.DMA,
         ],
     )
 
@@ -424,7 +447,6 @@
 
     near = shard & 1
     part_rows = row_count // shards
-    half_rows = row_count // 2
     own = inputs.shape[1] // members
     pair_start = member // 2 * 2 * own
     place = jnp.stack(
@@ -435,19 +457,29 @@
             member,
             near,
             1 - near,
+            jnp.zeros_like(near),
         ]
         + [part_of(shard ^ mask) for mask in range(shards)]
+        + [member // 2 ^ mask for mask in range(1, members // 2)]
     ).astype(jnp.int32)
 
-    own_half = lax.dynamic_slice_in_dim(inputs, near * half_rows, half_rows, 0)
-    own_part = lax.dynamic_slice_in_dim(inputs, part_of(shard) * part_rows, part_rows, 0)
-    arrived = {
-        m: from_mask(own_half if m == 1 else own_part, 2 * m * others, 0)
-        for m in range(1, members // 2)
-    }
-
-    send, summed = output_halves(place, inputs, w_in, w_out)
+    groups = [
+        [
+            ((2 * m + lowest) * others + r) * shards + t
+            for m in range(members // 2)
+            for t in range(shards)
+        ]
+        for lowest in range(2)
+        for r in range(others)
+    ]
+    inputs_part = lax.dynamic_slice_in_dim(inputs, shard * part_rows, part_rows, 0)
+    all_inputs = lax.all_gather(
+        inputs_part, ("dp", "tensor"), axis_index_groups=groups, tiled=True
+    )
+
+    send, hidden_near = forward(place, inputs, w_in, w_out)
     got = from_mask(send, 0, 1)
+    summed = product(place, hidden_near, w_out)
     for bit in range(1, shard_levels):
         send, summed = add_and_split(shard >> bit & 1, summed, got)
         got = from_mask(send, 0, 2**bit)
@@ -459,22 +491,25 @@
                 found[mask | 2**bit] = from_mask(found[mask], 0, 2**bit)
         return [(found[k], PARTS + k) for k in range(shards)]
 
-    errors, blocks = {}, {0: [(inputs, None)]}
-    for m in range(members // 2):
-        errors[m] = spread_over_tensor({0: from_mask(error, 2 * m * others, 0) if m else error})
-    for m in range(1, members // 2):
-        block = ordered(arrived[m], error)
-        if m == 1:
-            blocks[m] = [(block, NEAR), (from_mask(block, 0, 1), FAR)]
-        else:
-            blocks[m] = spread_over_tensor({0: block})
-
+    arrived = {m: from_mask(error, 2 * m * others, 0) for m in range(1, members // 2)}
+    arrived[0] = error
     slots, known = [], []
     totals = jnp.zeros((8, 128), jnp.float32)
     for m in range(members // 2):
+        found = ordered(arrived[m], sent, arrived[min(2, members // 2 - 1)]) if m else error
         first, second, send = gradient(
-            place, members, errors[m], blocks[m], w_in, w_out, known[-2:-1]
+            place,
+            members,
+            row_count,
+            spread_over_tensor({0: found}),
+            all_inputs if m else inputs,
+            PARTS + shards + m - 1 if m else ZERO,
+            w_in,
+            w_out,
+            known[-2:-1],
         )
+        if m == 0:
+            sent = send
         slots.append((first, second))
         if m == members // 2 - 1:
             totals = products(place, slots, 1, totals)

time: 243 us -> 244 us (level)
  waiting for transfers between devices: 116 us -> 79.9 us
  Pallas kernels: 79.9 us -> 93.6 us
  between operations: 1.19 us -> 14.4 us
  starting transfers between devices: 27.3 us -> 35.5 us
    ppermute x31 -> x21, waiting for transfers between devices: 106 us -> 74.3 us  [from_mask(): return lax.ppermute(value, ('dp', 'tensor'), pairs)]
    pallas_call x13 -> x14, Pallas kernels: 79.9 us -> 93.6 us  [call(): pl.pallas_call(body, grid_spec=pltpu.PrefetchScalarGridSpec(num_scalar_pr...]
    ppermute x3, starting transfers between devices: 1.58 us -> 13.1 us  [from_partner(): return lax.ppermute(value, axis, pairs)]
    ppermute x3, waiting for transfers between devices: 10.2 us -> 5.57 us  [from_partner(): return lax.ppermute(value, axis, pairs)]
    unnamed x40 -> x54, local copies, waits for them, and re-layouts: 6.64 us -> 10.4 us
    ppermute x31 -> x21, starting transfers between devices: 25.7 us -> 22.3 us  [from_mask(): return lax.ppermute(value, ('dp', 'tensor'), pairs)]
  transfers between devices with their start and end apart: 34 -> 25, of which waited for: 16 -> 11; matrix products, arithmetic and copies ran while one was open for 1% -> 0% of each run, Pallas kernels for 21% -> 34%
where the time goes in v6:
time: 244 us; the launch traced here: 243 us
  Pallas kernels  93.6 us (38%)
  waiting for transfers between devices  79.9 us (33%)
  starting transfers between devices  35.5 us (15%)
  between operations  14.4 us (6%)
  local copies, waits for them, and re-layouts  12.8 us (5%)
  blocking collectives  6.15 us (3%)
    pallas_call x14, Pallas kernels, call(): pl.pallas_call(body, grid_spec=pltpu.PrefetchScalarGridSpec(num_scalar_pr...  93.6 us
    ppermute x21, waiting for transfers between devices, from_mask(): return lax.ppermute(value, ('dp', 'tensor'), pairs)  74.3 us
    ppermute x21, starting transfers between devices, from_mask(): return lax.ppermute(value, ('dp', 'tensor'), pairs)  22.3 us
    ppermute x3, starting transfers between devices, from_partner(): return lax.ppermute(value, axis, pairs)  13.1 us
    unnamed x54, local copies, waits for them, and re-layouts  10.4 us
    psum x1, blocking collectives, group_total(): summed = lax.psum(values, 'tensor')  6.15 us
    ppermute x3, waiting for transfers between devices, from_partner(): return lax.ppermute(value, axis, pairs)  5.57 us
  transfers between devices with their start and end apart: 25, of which 11 were waited for; matrix products, arithmetic and copies ran while one was open for 0% of the time, Pallas kernels for 34%

profile of v6, /device:TPU:0, one launch (start us, length us, event | category | flops | bytes accessed | tf_op | source)
XLA Modules:
  0.0 243.0 jit_solution(12309820734037883685)
XLA Ops:
  7.2 1.8 constant_dynamic-slice_fusion
  9.8 10.5 %forward.1 = (f32[352,1280]{1,0:T(8,128)}, bf16[352,1280]{1,0:T(8,128)(2,1)}) custom-call(s32[14]{0:T(128)} %stack.55.place_ref, bf16[704,1280]{1,0:T(8,128)(2,1)} %refs_4_.1, bf16[1280,1280]{1,0:T(8,128)(2,1)} %refs_6_.7, bf16[1280,1280]{1,0:T(8,128)(2,1)} %refs_7_.3), custom_call_target="tpu_custom_call" | custom-call | flops 1 | bytes 1 | tf_op jit(solution)/shard_map/forward/pallas_call | solution.py:82
  21.9 2.7 %product.1.refs_0_.refs_2_ = f32[352,1280]{1,0:T(8,128)S(1)} custom-call(s32[14]{0:T(128)S(1)} %copy-done.26, bf16[352,1280]{1,0:T(8,128)(2,1)S(1)} %copy-done.17, bf16[1280,1280]{1,0:T(8,128)(2,1)S(1)} %copy-done), custom_call_target="tpu_custom_call" | custom-call | flops 1 | bytes 1 | tf_op jit(solution)/shard_map/product/pallas_call | solution.py:82
  24.9 2.7 %collective-permute-start.1 = (f32[176,1280]{1,0:T(8,128)S(1)}, f32[176,1280]{1,0:T(8,128)S(1)}, u32[]{:S(2)}, u32[]{:S(2)}) collective-permute-start(f32[176,1280]{1,0:T(8,128)S(1)} %get-tuple-element.24), channel_id=1, source_target_pairs={{0,2},{1,3},{2,0},{3,1},{4,6},{5,7},{6,4},{7,5},{8,10},{9,11},{10,... | collective-permute-start | bytes 2703368 | tf_op jit(solution)/shard_map/ppermute | solution.py:28
  27.6 23.4 %collective-permute-done.1.refs_1_ = f32[176,1280]{1,0:T(8,128)S(1)} collective-permute-done((f32[176,1280]{1,0:T(8,128)S(1)}, f32[176,1280]{1,0:T(8,128)S(1)}, u32[]{:S(2)}, u32[]{:S(2)}) %collective-permute-start.1) | collective-permute-done | bytes 901152 | tf_op jit(solution)/shard_map/ppermute | solution.py:28
  51.6 2.6 %collective-permute-start.3 = (bf16[176,1280]{1,0:T(8,128)(2,1)S(1)}, bf16[176,1280]{1,0:T(8,128)(2,1)S(1)}, u32[]{:S(2)}, u32[]{:S(2)}) collective-permute-start(bf16[176,1280]{1,0:T(8,128)(2,1)S(1)} %error_part.1.refs_0_), channel_id=1, source_target_pairs={{0,2},{1,3},{2,0},{3,1},{4,6},{5,7},{6,4},{7,5},{8,10},{9,11},{10,... | collective-permute-start | bytes 1351688 | tf_op jit(solution)/shard_map/ppermute | solution.py:28
  54.2 20.1 %collective-permute-done.3.refs_2_ = bf16[176,1280]{1,0:T(8,128)(2,1)S(1)} collective-permute-done((bf16[176,1280]{1,0:T(8,128)(2,1)S(1)}, bf16[176,1280]{1,0:T(8,128)(2,1)S(1)}, u32[]{:S(2)}, u32[]{:S(2)}) %collective-permute-start.3) | collective-permute-done | bytes 450592 | tf_op jit(solution)/shard_map/ppermute | solution.py:28
  75.7 2.7 %collective-permute-start.7 = (bf16[176,1280]{1,0:T(8,128)(2,1)S(1)}, bf16[176,1280]{1,0:T(8,128)(2,1)}, u32[]{:S(2)}, u32[]{:S(2)}) collective-permute-start(bf16[176,1280]{1,0:T(8,128)(2,1)S(1)} %error_part.1.refs_0_), channel_id=1, source_target_pairs={{0,16},{1,17},{2,18},{3,19},{4,20},{5,21},{6,22},{7,23},{8,24},{9,... | collective-permute-start | bytes 1351688 | tf_op jit(solution)/shard_map/ppermute | solution.py:28
  78.5 12.7 %gradient.4 = (f32[160,1280]{1,0:T(8,128)S(1)}, f32[160,1280]{1,0:T(8,128)S(1)}, bf16[320,1280]{1,0:T(8,128)(2,1)}) custom-call(s32[14]{0:T(128)S(1)} %copy-done.26, bf16[176,1280]{1,0:T(8,128)(2,1)S(1)} %error_part.1.refs_0_, bf16[176,1280]{1,0:T(8,128)(2,1)S(1)} %collective-permute-done.2.refs_1_, bf16[176,1280]{1,0:T(8,128)(2,1)S(1)} %collective-permute-done.3.refs_2_, ...), custom_call_target="tpu_custom_call" | custom-call | flops 1 | bytes 1 | tf_op jit(solution)/shard_map/gradient/pallas_call | solution.py:82
  93.1 13.2 %collective-permute-done.6.refs_0_ = bf16[176,1280]{1,0:T(8,128)(2,1)S(1)} collective-permute-done((bf16[176,1280]{1,0:T(8,128)(2,1)S(1)}, bf16[176,1280]{1,0:T(8,128)(2,1)S(1)}, u32[]{:S(2)}, u32[]{:S(2)}) %collective-permute-start.6) | collective-permute-done | bytes 450592 | tf_op jit(solution)/shard_map/ppermute | solution.py:28
  106.3 2.3 collective-permute-done.7.refs_1_
  108.6 1.9 collective-permute-start.9
  110.6 2.4 collective-permute-start.16
  113.7 4.8 %collective-permute-done.9.refs_2_ = bf16[176,1280]{1,0:T(8,128)(2,1)S(1)} collective-permute-done((bf16[176,1280]{1,0:T(8,128)(2,1)S(1)}, bf16[176,1280]{1,0:T(8,128)(2,1)S(1)}, u32[]{:S(2)}, u32[]{:S(2)}) %collective-permute-start.9) | collective-permute-done | bytes 450592 | tf_op jit(solution)/shard_map/ppermute | solution.py:28
  120.6 1.6 collective-permute-start.13
  129.2 12.5 %gradient.5 = (f32[160,1280]{1,0:T(8,128)S(1)}, f32[160,1280]{1,0:T(8,128)S(1)}, bf16[320,1280]{1,0:T(8,128)(2,1)S(1)}) custom-call(s32[14]{0:T(128)S(1)} %copy-done.26, bf16[176,1280]{1,0:T(8,128)(2,1)S(1)} %copy-done.19, bf16[176,1280]{1,0:T(8,128)(2,1)S(1)} %copy-done.23, bf16[176,1280]{1,0:T(8,128)(2,1)S(1)} %copy-done.21, ...), custom_call_target="tpu_custom_call" | custom-call | flops 1 | bytes 1 | tf_op jit(solution)/shard_map/gradient/pallas_call | solution.py:82
  141.7 1.7 collective-permute-start.11
  144.5 3.8 %products.5.refs_0_.refs_6_ = f32[8,128]{1,0:T(8,128)S(1)} custom-call(s32[14]{0:T(128)S(1)} %copy-done.26, f32[160,1280]{1,0:T(8,128)S(1)} %copy-done.4, f32[160,1280]{1,0:T(8,128)S(1)} %copy-done.6, bf16[320,1280]{1,0:T(8,128)(2,1)} %collective-permute-done.5.refs_2_.refs_3_.refs_4_, f32[8,128]{1,0:T(8,128)S(1)} %broadcast_in_dim.3.refs_3_), custom_call_target="tpu_custom_call" | custom-call | flops 1 | bytes 1 | tf_op jit(solution)/shard_map/products/pallas_call | solution.py:82
  148.3 12.6 %gradient.6 = (f32[160,1280]{1,0:T(8,128)S(1)}, f32[160,1280]{1,0:T(8,128)S(1)}, bf16[320,1280]{1,0:T(8,128)(2,1)S(1)}) custom-call(s32[14]{0:T(128)S(1)} %copy-done.26, f32[8,128]{1,0:T(8,128)S(1)} %products.5.refs_0_.refs_6_, bf16[176,1280]{1,0:T(8,128)(2,1)} %collective-permute-done.7.refs_1_, bf16[176,1280]{1,0:T(8,128)(2,1)S(1)} %collective-permute-done.12.refs_2_, ...), custom_call_target="tpu_custom_call" | custom-call | flops 1 | bytes 1 | tf_op jit(solution)/shard_map/gradient/pallas_call | solution.py:82
  161.4 4.3 %products.6.refs_0_.refs_9_ = f32[8,128]{1,0:T(8,128)S(1)} custom-call(s32[14]{0:T(128)S(1)} %copy-done.26, f32[160,1280]{1,0:T(8,128)S(1)} %copy-done.4, f32[160,1280]{1,0:T(8,128)S(1)} %copy-done.6, bf16[320,1280]{1,0:T(8,128)(2,1)} %collective-permute-done.5.refs_2_.refs_3_.refs_4_, f32[160,1280]{1,0:T(8,128)S(1)} %get-tuple-element.29.refs_3_.refs_5_, ...), custom_call_target="tpu_custom_call" | custom-call | flops 1 | bytes 1 | tf_op jit(solution)/shard_map/products/pallas_call | solution.py:82
  165.7 12.8 %gradient.7 = (f32[160,1280]{1,0:T(8,128)S(1)}, f32[160,1280]{1,0:T(8,128)S(1)}, bf16[320,1280]{1,0:T(8,128)(2,1)S(1)}) custom-call(s32[14]{0:T(128)S(1)} %copy-done.26, f32[8,128]{1,0:T(8,128)S(1)} %products.6.refs_0_.refs_9_, bf16[176,1280]{1,0:T(8,128)(2,1)} %collective-permute-done.16.refs_1_, bf16[176,1280]{1,0:T(8,128)(2,1)S(1)} %collective-permute-done.17.refs_2_, ...), custom_call_target="tpu_custom_call" | custom-call | flops 1 | bytes 1 | tf_op jit(solution)/shard_map/gradient/pallas_call | solution.py:82
  178.5 1.7 collective-permute-start.20
  181.3 4.8 %products.7.refs_11_ = f32[8,128]{1,0:T(8,128)S(1)} custom-call(s32[14]{0:T(128)S(1)} %copy-done.26, f32[160,1280]{1,0:T(8,128)S(1)} %copy-done.4, f32[160,1280]{1,0:T(8,128)S(1)} %copy-done.6, bf16[320,1280]{1,0:T(8,128)(2,1)} %collective-permute-done.5.refs_2_.refs_3_.refs_4_, f32[160,1280]{1,0:T(8,128)S(1)} %get-tuple-element.29.refs_3_.refs_5_, ...), custom_call_target="tpu_custom_call" | custom-call | flops 1 | bytes 1 | tf_op jit(solution)/shard_map/products/pallas_call | solution.py:82
  186.1 4.3 %products.8.refs_12_ = f32[8,128]{1,0:T(8,128)S(1)} custom-call(s32[14]{0:T(128)S(1)} %copy-done.26, f32[160,1280]{1,0:T(8,128)S(1)} %copy-done.4, f32[160,1280]{1,0:T(8,128)S(1)} %copy-done.6, bf16[320,1280]{1,0:T(8,128)(2,1)} %collective-permute-done.5.refs_2_.refs_3_.refs_4_, f32[160,1280]{1,0:T(8,128)S(1)} %get-tuple-element.29.refs_3_.refs_5_, ...), custom_call_target="tpu_custom_call" | custom-call | flops 1 | bytes 1 | tf_op jit(solution)/shard_map/products/pallas_call | solution.py:82
  190.4 8.3 %collective-permute-done.20.refs_11_.refs_15_.refs_16_ = bf16[320,1280]{1,0:T(8,128)(2,1)S(1)} collective-permute-done((bf16[320,1280]{1,0:T(8,128)(2,1)S(1)}, bf16[320,1280]{1,0:T(8,128)(2,1)S(1)}, u32[]{:S(2)}, u32[]{:S(2)}) %collective-permute-start.20) | collective-permute-done | bytes 819232 | tf_op jit(solution)/shard_map/ppermute | solution.py:28
  198.8 4.5 %products.9 = f32[8,128]{1,0:T(8,128)S(1)} custom-call(s32[14]{0:T(128)S(1)} %copy-done.26, f32[160,1280]{1,0:T(8,128)S(1)} %copy-done.4, f32[160,1280]{1,0:T(8,128)S(1)} %copy-done.6, bf16[320,1280]{1,0:T(8,128)(2,1)} %collective-permute-done.5.refs_2_.refs_3_.refs_4_, f32[160,1280]{1,0:T(8,128)S(1)} %get-tuple-element.29.refs_3_.refs_5_, ...), custom_call_target="tpu_custom_call" | custom-call | flops 1 | bytes 1 | tf_op jit(solution)/shard_map/products/pallas_call | solution.py:82
  203.4 6.1 %psum.7 = f32[8,128]{1,0:T(8,128)S(1)} all-reduce(f32[8,128]{1,0:T(8,128)S(1)} %products.9), channel_id=1, replica_groups=mesh['dp'=8,'tensor'=4] {'tensor'}, use_global_device_ids=true, to_apply=%region_0.1 | all-reduce | flops 1024 | bytes 8192 | tf_op jit(solution)/shard_map/psum | solution.py:43
  209.5 8.8 %collective-permute-start.21 = (f32[8,128]{1,0:T(8,128)S(1)}, f32[8,128]{1,0:T(8,128)S(1)}, u32[]{:S(2)}, u32[]{:S(2)}) collective-permute-start(f32[8,128]{1,0:T(8,128)S(1)} %psum.7), channel_id=1, source_target_pairs={{0,16},{4,20},{8,24},{12,28},{16,0},{20,4},{24,8},{28,12},{1,17},{... | collective-permute-start | bytes 12296 | tf_op jit(solution)/shard_map/ppermute | solution.py:21
  218.3 1.6 collective-permute-done.21
  219.9 3.1 %collective-permute-start.22 = (f32[8,128]{1,0:T(8,128)S(1)}, f32[8,128]{1,0:T(8,128)S(1)}, u32[]{:S(2)}, u32[]{:S(2)}) collective-permute-start(f32[8,128]{1,0:T(8,128)S(1)} %add.53), channel_id=1, source_target_pairs={{0,8},{4,12},{8,0},{12,4},{16,24},{20,28},{24,16},{28,20},{1,9},{5... | collective-permute-start | bytes 12296 | tf_op jit(solution)/shard_map/ppermute | solution.py:21
  225.8 2.4 collective-permute-done.23
  228.8 7.3 %merge.1 = (f32[160,1280]{1,0:T(8,128)}, f32[160,1280]{1,0:T(8,128)}) custom-call(s32[14]{0:T(128)} %stack.55.place_ref, f32[8,128]{1,0:T(8,128)} %add.55.refs_0_, f32[160,1280]{1,0:T(8,128)} %copy-done.3, f32[160,1280]{1,0:T(8,128)} %copy-done.5, bf16[320,1280]{1,0:T(8,128)(2,1)} %collective-permute-done.5.refs_2_.refs_3_.refs_4_, ...), custom_call_target="tpu_custom_call" | custom-call | flops 1 | bytes 1 | tf_op jit(solution)/shard_map/merge/pallas_call | solution.py:82
  (94 shorter events, 22.5 us)
Async XLA Ops:
  7.2 118.0 %all-gather.2.cloned.1.call-start = ((), (), s32[]{:S(2)}) async-start(), calls=%async_computation | async-start | bytes 7659520 | tf_op jit(solution)/shard_map/all_gather | solution.py:476
  20.3 4.4 %collective-permute-start = (f32[352,1280]{1,0:T(8,128)}, f32[352,1280]{1,0:T(8,128)S(1)}, u32[]{:S(2)}, u32[]{:S(2)}) collective-permute-start(f32[352,1280]{1,0:T(8,128)} %get-tuple-element.22), channel_id=1, source_target_pairs={{0,1},{1,0},{2,3},{3,2},{4,5},{5,4},{6,7},{7,6},{8,9},{9,8},{10,11... | collective-permute-start | bytes 5406728 | tf_op jit(solution)/shard_map/ppermute | solution.py:28
  24.9 26.0 %collective-permute-start.1 = (f32[176,1280]{1,0:T(8,128)S(1)}, f32[176,1280]{1,0:T(8,128)S(1)}, u32[]{:S(2)}, u32[]{:S(2)}) collective-permute-start(f32[176,1280]{1,0:T(8,128)S(1)} %get-tuple-element.24), channel_id=1, source_target_pairs={{0,2},{1,3},{2,0},{3,1},{4,6},{5,7},{6,4},{7,5},{8,10},{9,11},{10,... | collective-permute-start | bytes 2703368 | tf_op jit(solution)/shard_map/ppermute | solution.py:28
  50.9 27.5 %copy-start.12 = (bf16[704,1280]{1,0:T(8,128)(2,1)S(1)}, bf16[704,1280]{1,0:T(8,128)(2,1)}, u32[]{:S(2)}) copy-start(bf16[704,1280]{1,0:T(8,128)(2,1)} %refs_4_.1) | copy-start | bytes 5406724
  51.6 22.7 %collective-permute-start.3 = (bf16[176,1280]{1,0:T(8,128)(2,1)S(1)}, bf16[176,1280]{1,0:T(8,128)(2,1)S(1)}, u32[]{:S(2)}, u32[]{:S(2)}) collective-permute-start(bf16[176,1280]{1,0:T(8,128)(2,1)S(1)} %error_part.1.refs_0_), channel_id=1, source_target_pairs={{0,2},{1,3},{2,0},{3,1},{4,6},{5,7},{6,4},{7,5},{8,10},{9,11},{10,... | collective-permute-start | bytes 1351688 | tf_op jit(solution)/shard_map/ppermute | solution.py:28
  54.1 24.3 %collective-permute-start.2 = (bf16[176,1280]{1,0:T(8,128)(2,1)S(1)}, bf16[176,1280]{1,0:T(8,128)(2,1)S(1)}, u32[]{:S(2)}, u32[]{:S(2)}) collective-permute-start(bf16[176,1280]{1,0:T(8,128)(2,1)S(1)} %error_part.1.refs_0_), channel_id=1, source_target_pairs={{0,1},{1,0},{2,3},{3,2},{4,5},{5,4},{6,7},{7,6},{8,9},{9,8},{10,11... | collective-permute-start | bytes 1351688 | tf_op jit(solution)/shard_map/ppermute | solution.py:28
  74.3 4.2 %collective-permute-start.4 = (bf16[176,1280]{1,0:T(8,128)(2,1)S(1)}, bf16[176,1280]{1,0:T(8,128)(2,1)S(1)}, u32[]{:S(2)}, u32[]{:S(2)}) collective-permute-start(bf16[176,1280]{1,0:T(8,128)(2,1)S(1)} %collective-permute-done.3.refs_2_), channel_id=1, source_target_pairs={{0,1},{1,0},{2,3},{3,2},{4,5},{5,4},{6,7},{7,6},{8,9},{9,8},{10,11... | collective-permute-start | bytes 1351688 | tf_op jit(solution)/shard_map/ppermute | solution.py:28
  74.3 32.0 %collective-permute-start.6 = (bf16[176,1280]{1,0:T(8,128)(2,1)S(1)}, bf16[176,1280]{1,0:T(8,128)(2,1)S(1)}, u32[]{:S(2)}, u32[]{:S(2)}) collective-permute-start(bf16[176,1280]{1,0:T(8,128)(2,1)S(1)} %error_part.1.refs_0_), channel_id=1, source_target_pairs={{0,8},{1,9},{2,10},{3,11},{4,12},{5,13},{6,14},{7,15},{8,0},{9,1},... | collective-permute-start | bytes 1351688 | tf_op jit(solution)/shard_map/ppermute | solution.py:28
  75.7 32.9 %collective-permute-start.7 = (bf16[176,1280]{1,0:T(8,128)(2,1)S(1)}, bf16[176,1280]{1,0:T(8,128)(2,1)}, u32[]{:S(2)}, u32[]{:S(2)}) collective-permute-start(bf16[176,1280]{1,0:T(8,128)(2,1)S(1)} %error_part.1.refs_0_), channel_id=1, source_target_pairs={{0,16},{1,17},{2,18},{3,19},{4,20},{5,21},{6,22},{7,23},{8,24},{9,... | collective-permute-start | bytes 1351688 | tf_op jit(solution)/shard_map/ppermute | solution.py:28
  78.4 46.7 %copy-start.1 = (bf16[1280,1280]{1,0:T(8,128)(2,1)S(1)}, bf16[1280,1280]{1,0:T(8,128)(2,1)}, u32[]{:S(2)}) copy-start(bf16[1280,1280]{1,0:T(8,128)(2,1)} %refs_6_.7) | copy-start | bytes 9830404
  108.6 9.9 %collective-permute-start.9 = (bf16[176,1280]{1,0:T(8,128)(2,1)S(1)}, bf16[176,1280]{1,0:T(8,128)(2,1)S(1)}, u32[]{:S(2)}, u32[]{:S(2)}) collective-permute-start(bf16[176,1280]{1,0:T(8,128)(2,1)S(1)} %collective-permute-done.6.refs_0_), channel_id=1, source_target_pairs={{0,2},{1,3},{2,0},{3,1},{4,6},{5,7},{6,4},{7,5},{8,10},{9,11},{10,... | collective-permute-start | bytes 1351688 | tf_op jit(solution)/shard_map/ppermute | solution.py:28
  110.6 12.7 %collective-permute-start.16 = (bf16[176,1280]{1,0:T(8,128)(2,1)S(1)}, bf16[176,1280]{1,0:T(8,128)(2,1)}, u32[]{:S(2)}, u32[]{:S(2)}) collective-permute-start(bf16[176,1280]{1,0:T(8,128)(2,1)S(1)} %error_part.1.refs_0_), channel_id=1, source_target_pairs={{0,24},{1,25},{2,26},{3,27},{4,28},{5,29},{6,30},{7,31},{8,16},{9,... | collective-permute-start | bytes 1351688 | tf_op jit(solution)/shard_map/ppermute | solution.py:28
  112.9 10.6 %collective-permute-start.8 = (bf16[176,1280]{1,0:T(8,128)(2,1)S(1)}, bf16[176,1280]{1,0:T(8,128)(2,1)S(1)}, u32[]{:S(2)}, u32[]{:S(2)}) collective-permute-start(bf16[176,1280]{1,0:T(8,128)(2,1)S(1)} %collective-permute-done.6.refs_0_), channel_id=1, source_target_pairs={{0,1},{1,0},{2,3},{3,2},{4,5},{5,4},{6,7},{7,6},{8,9},{9,8},{10,11... | collective-permute-start | bytes 1351688 | tf_op jit(solution)/shard_map/ppermute | solution.py:28
  118.5 5.8 %collective-permute-start.10 = (bf16[176,1280]{1,0:T(8,128)(2,1)S(1)}, bf16[176,1280]{1,0:T(8,128)(2,1)S(1)}, u32[]{:S(2)}, u32[]{:S(2)}) collective-permute-start(bf16[176,1280]{1,0:T(8,128)(2,1)S(1)} %collective-permute-done.9.refs_2_), channel_id=1, source_target_pairs={{0,1},{1,0},{2,3},{3,2},{4,5},{5,4},{6,7},{7,6},{8,9},{9,8},{10,11... | collective-permute-start | bytes 1351688 | tf_op jit(solution)/shard_map/ppermute | solution.py:28
  119.3 24.7 %collective-permute-start.5 = (bf16[320,1280]{1,0:T(8,128)(2,1)}, bf16[320,1280]{1,0:T(8,128)(2,1)}, u32[]{:S(2)}, u32[]{:S(2)}) collective-permute-start(bf16[320,1280]{1,0:T(8,128)(2,1)} %get-tuple-element.27), channel_id=1, source_target_pairs={{0,4},{1,5},{2,6},{3,7},{4,0},{5,1},{6,2},{7,3},{8,12},{9,13},{10,... | collective-permute-start | bytes 2457608 | tf_op jit(solution)/shard_map/ppermute | solution.py:28
  120.6 22.8 %collective-permute-start.13 = (bf16[176,1280]{1,0:T(8,128)(2,1)}, bf16[176,1280]{1,0:T(8,128)(2,1)}, u32[]{:S(2)}, u32[]{:S(2)}) collective-permute-start(bf16[176,1280]{1,0:T(8,128)(2,1)} %collective-permute-done.7.refs_1_), channel_id=1, source_target_pairs={{0,2},{1,3},{2,0},{3,1},{4,6},{5,7},{6,4},{7,5},{8,10},{9,11},{10,... | collective-permute-start | bytes 1351688 | tf_op jit(solution)/shard_map/ppermute | solution.py:28
  123.3 20.7 %collective-permute-start.18 = (bf16[176,1280]{1,0:T(8,128)(2,1)}, bf16[176,1280]{1,0:T(8,128)(2,1)}, u32[]{:S(2)}, u32[]{:S(2)}) collective-permute-start(bf16[176,1280]{1,0:T(8,128)(2,1)} %collective-permute-done.16.refs_1_), channel_id=1, source_target_pairs={{0,2},{1,3},{2,0},{3,1},{4,6},{5,7},{6,4},{7,5},{8,10},{9,11},{10,... | collective-permute-start | bytes 1351688 | tf_op jit(solution)/shard_map/ppermute | solution.py:28
  141.7 57.0 %copy-start.7 = (f32[160,1280]{1,0:T(8,128)}, f32[160,1280]{1,0:T(8,128)S(1)}, u32[]{:S(2)}) copy-start(f32[160,1280]{1,0:T(8,128)S(1)} %get-tuple-element.29.refs_3_.refs_5_) | copy-start | bytes 2457604
  141.7 57.0 %copy-start.8 = (f32[160,1280]{1,0:T(8,128)}, f32[160,1280]{1,0:T(8,128)S(1)}, u32[]{:S(2)}) copy-start(f32[160,1280]{1,0:T(8,128)S(1)} %get-tuple-element.30.refs_4_.refs_6_) | copy-start | bytes 2457604
  141.7 19.6 %collective-permute-start.11 = (bf16[320,1280]{1,0:T(8,128)(2,1)S(1)}, bf16[320,1280]{1,0:T(8,128)(2,1)S(1)}, u32[]{:S(2)}, u32[]{:S(2)}) collective-permute-start(bf16[320,1280]{1,0:T(8,128)(2,1)S(1)} %get-tuple-element.31), channel_id=1, source_target_pairs={{0,4},{1,5},{2,6},{3,7},{4,0},{5,1},{6,2},{7,3},{8,12},{9,13},{10,... | collective-permute-start | bytes 2457608 | tf_op jit(solution)/shard_map/ppermute | solution.py:28
  143.4 4.9 %collective-permute-start.12 = (bf16[176,1280]{1,0:T(8,128)(2,1)}, bf16[176,1280]{1,0:T(8,128)(2,1)S(1)}, u32[]{:S(2)}, u32[]{:S(2)}) collective-permute-start(bf16[176,1280]{1,0:T(8,128)(2,1)} %collective-permute-done.7.refs_1_), channel_id=1, source_target_pairs={{0,1},{1,0},{2,3},{3,2},{4,5},{5,4},{6,7},{7,6},{8,9},{9,8},{10,11... | collective-permute-start | bytes 1351688 | tf_op jit(solution)/shard_map/ppermute | solution.py:28
  143.4 4.9 %collective-permute-start.14 = (bf16[176,1280]{1,0:T(8,128)(2,1)}, bf16[176,1280]{1,0:T(8,128)(2,1)S(1)}, u32[]{:S(2)}, u32[]{:S(2)}) collective-permute-start(bf16[176,1280]{1,0:T(8,128)(2,1)} %collective-permute-done.13.refs_3_), channel_id=1, source_target_pairs={{0,1},{1,0},{2,3},{3,2},{4,5},{5,4},{6,7},{7,6},{8,9},{9,8},{10,11... | collective-permute-start | bytes 1351688 | tf_op jit(solution)/shard_map/ppermute | solution.py:28
  143.9 21.7 %collective-permute-start.17 = (bf16[176,1280]{1,0:T(8,128)(2,1)}, bf16[176,1280]{1,0:T(8,128)(2,1)S(1)}, u32[]{:S(2)}, u32[]{:S(2)}) collective-permute-start(bf16[176,1280]{1,0:T(8,128)(2,1)} %collective-permute-done.16.refs_1_), channel_id=1, source_target_pairs={{0,1},{1,0},{2,3},{3,2},{4,5},{5,4},{6,7},{7,6},{8,9},{9,8},{10,11... | collective-permute-start | bytes 1351688 | tf_op jit(solution)/shard_map/ppermute | solution.py:28
  144.0 21.7 %collective-permute-start.19 = (bf16[176,1280]{1,0:T(8,128)(2,1)}, bf16[176,1280]{1,0:T(8,128)(2,1)S(1)}, u32[]{:S(2)}, u32[]{:S(2)}) collective-permute-start(bf16[176,1280]{1,0:T(8,128)(2,1)} %collective-permute-done.18.refs_3_), channel_id=1, source_target_pairs={{0,1},{1,0},{2,3},{3,2},{4,5},{5,4},{6,7},{7,6},{8,9},{9,8},{10,11... | collective-permute-start | bytes 1351688 | tf_op jit(solution)/shard_map/ppermute | solution.py:28
  160.9 37.9 %copy-start.10 = (f32[160,1280]{1,0:T(8,128)}, f32[160,1280]{1,0:T(8,128)S(1)}, u32[]{:S(2)}) copy-start(f32[160,1280]{1,0:T(8,128)S(1)} %get-tuple-element.33.refs_6_.refs_9_) | copy-start | bytes 2457604
  160.9 37.9 %copy-start.11 = (f32[160,1280]{1,0:T(8,128)}, f32[160,1280]{1,0:T(8,128)S(1)}, u32[]{:S(2)}) copy-start(f32[160,1280]{1,0:T(8,128)S(1)} %get-tuple-element.34.refs_7_.refs_10_) | copy-start | bytes 2457604
  160.9 20.4 %collective-permute-start.15 = (bf16[320,1280]{1,0:T(8,128)(2,1)S(1)}, bf16[320,1280]{1,0:T(8,128)(2,1)S(1)}, u32[]{:S(2)}, u32[]{:S(2)}) collective-permute-start(bf16[320,1280]{1,0:T(8,128)(2,1)S(1)} %get-tuple-element.35), channel_id=1, source_target_pairs={{0,4},{1,5},{2,6},{3,7},{4,0},{5,1},{6,2},{7,3},{8,12},{9,13},{10,... | collective-permute-start | bytes 2457608 | tf_op jit(solution)/shard_map/ppermute | solution.py:28
  161.4 37.4 %copy-start.2 = (bf16[320,1280]{1,0:T(8,128)(2,1)}, bf16[320,1280]{1,0:T(8,128)(2,1)S(1)}, u32[]{:S(2)}) copy-start(bf16[320,1280]{1,0:T(8,128)(2,1)S(1)} %collective-permute-done.11.refs_5_.refs_7_.refs_8_) | copy-start | bytes 2457604
  178.5 20.2 %collective-permute-start.20 = (bf16[320,1280]{1,0:T(8,128)(2,1)S(1)}, bf16[320,1280]{1,0:T(8,128)(2,1)S(1)}, u32[]{:S(2)}, u32[]{:S(2)}) collective-permute-start(bf16[320,1280]{1,0:T(8,128)(2,1)S(1)} %get-tuple-element.39), channel_id=1, source_target_pairs={{0,4},{1,5},{2,6},{3,7},{4,0},{5,1},{6,2},{7,3},{8,12},{9,13},{10,... | collective-permute-start | bytes 2457608 | tf_op jit(solution)/shard_map/ppermute | solution.py:28
  209.5 10.4 %collective-permute-start.21 = (f32[8,128]{1,0:T(8,128)S(1)}, f32[8,128]{1,0:T(8,128)S(1)}, u32[]{:S(2)}, u32[]{:S(2)}) collective-permute-start(f32[8,128]{1,0:T(8,128)S(1)} %psum.7), channel_id=1, source_target_pairs={{0,16},{4,20},{8,24},{12,28},{16,0},{20,4},{24,8},{28,12},{1,17},{... | collective-permute-start | bytes 12296 | tf_op jit(solution)/shard_map/ppermute | solution.py:21
  219.9 4.7 %collective-permute-start.22 = (f32[8,128]{1,0:T(8,128)S(1)}, f32[8,128]{1,0:T(8,128)S(1)}, u32[]{:S(2)}, u32[]{:S(2)}) collective-permute-start(f32[8,128]{1,0:T(8,128)S(1)} %add.53), channel_id=1, source_target_pairs={{0,8},{4,12},{8,0},{12,4},{16,24},{20,28},{24,16},{28,20},{1,9},{5... | collective-permute-start | bytes 12296 | tf_op jit(solution)/shard_map/ppermute | solution.py:21
  224.6 3.6 %collective-permute-start.23 = (f32[8,128]{1,0:T(8,128)S(1)}, f32[8,128]{1,0:T(8,128)S(1)}, u32[]{:S(2)}, u32[]{:S(2)}) collective-permute-start(f32[8,128]{1,0:T(8,128)S(1)} %add.54), channel_id=1, source_target_pairs={{0,4},{4,0},{8,12},{12,8},{16,20},{20,16},{24,28},{28,24},{1,5},{5... | collective-permute-start | bytes 12296 | tf_op jit(solution)/shard_map/ppermute | solution.py:21
  (20 other events, 151.6 us)
Sparse Core Ops, SparseCore 0:
  10.3 95.2 all-gather.1

commit v7 on v6

--- a/solution.py
+++ b/solution.py
@@ -11,7 +11,6 @@
 epsilon = 1e-06
 gather_levels_limit = 3
 vmem_bytes = 36 * 2**20
-vmem_large = 46 * 2**20
 vmem_most = 60 * 2**20
 
 
@@ -89,7 +88,7 @@
     )(operands[0], *after, *operands[1:])
 
 
-WINDOW, SHIFT, OTHER_SHIFT, MEMBER, NEAR, FAR, ZERO, PARTS = range(8)
+WINDOW, SHIFT, OTHER_SHIFT, MEMBER, NEAR, FAR, PART = range(7)
 
 
 def row_start(place_ref, block, where):
@@ -200,46 +199,74 @@
     )
 
 
+def join_kernel(place_ref, own_ref, got_ref, out_ref):
+    rows = own_ref.shape[0]
+    out_ref[pl.ds(pl.multiple_of(place_ref[0] * rows, 16), rows), :] = own_ref[...]
+    out_ref[pl.ds(pl.multiple_of((1 - place_ref[0]) * rows, 16), rows), :] = got_ref[...]
+
+
+def join(flag, own, got):
+    rows, depth = own.shape
+    return call(
+        join_kernel,
+        "join",
+        (flag.reshape(1), own, got),
+        [jax.ShapeDtypeStruct((2 * rows, depth), own.dtype)],
+        grid=(1,),
+        in_specs=[pl.BlockSpec((rows, depth), whole)] * 2,
+        out_specs=[pl.BlockSpec((2 * rows, depth), whole)],
+    )[0]
+
+
 def error_kernel(row_count, place_ref, own_ref, got_ref, targets_ref, error_ref):
     out = own_ref[...] + got_ref[...]
     error = (out - targets_ref[...].astype(jnp.float32)) / row_count
     error_ref[...] = error.astype(jnp.bfloat16)
 
 
-def error_part(place, own, got, targets):
+def error_part(place, own, got, targets, after):
     rows, depth = own.shape
     return call(
         functools.partial(error_kernel, targets.shape[0]),
         "error_part",
         (place, own, got, targets),
         [jax.ShapeDtypeStruct((rows, depth), jnp.bfloat16)],
+        after,
         grid=(1,),
         in_specs=[
             pl.BlockSpec((rows, depth), whole),
             pl.BlockSpec((rows, depth), whole),
-            pl.BlockSpec((rows, depth), lambda n, s: (s[PARTS], 0)),
+            pl.BlockSpec((rows, depth), lambda n, s: (s[PART], 0)),
         ],
         out_specs=[pl.BlockSpec((rows, depth), whole)],
     )[0]
 
 
-def gradient_kernel(wheres, worker, window, own, step_rows, place_ref, *refs):
-    error_refs, refs = refs[: len(wheres)], refs[len(wheres) :]
-    all_inputs, w_in_ref, w_out_ref, first_ref, second_ref, send_ref = refs[:6]
-    errors, inputs, inputs_turned, errors_turned, spread_first, spread_second, done = refs[6:]
+def gradient_kernel(wheres, window, own, step_rows, place_ref, *refs):
+    error_wheres, input_wheres = wheres
+    refs = list(refs)
+
+    def take(n):
+        taken = refs[:n]
+        del refs[:n]
+        return taken
+
+    error_refs, input_refs = take(len(error_wheres)), take(len(input_wheres))
+    w_in_ref, w_out_ref, first_ref, second_ref, send_ref = take(5)
+    errors, inputs, inputs_turned, errors_turned, spread_first, spread_second = refs
+    if len(input_refs) == 1:
+        inputs = input_refs[0]
 
     @pl.when(pl.program_id(0) == 0)
     def _():
-        rows = inputs.shape[0]
-        start = pl.multiple_of(place_ref[worker] * rows, 16)
-        fetch = pltpu.make_async_copy(all_inputs.at[pl.ds(start, rows), :], inputs, done)
-        fetch.start()
-        for block, where in zip(error_refs, wheres):
+        for block, where in zip(error_refs, error_wheres):
             errors[pl.ds(row_start(place_ref, block, where), block.shape[0]), :] = block[...]
+        if len(input_refs) > 1:
+            for block, where in zip(input_refs, input_wheres):
+                inputs[pl.ds(row_start(place_ref, block, where), block.shape[0]), :] = block[...]
         lane = pl.multiple_of(place_ref[WINDOW] * 128, 128)
+        inputs_turned[...] = inputs[:, pl.ds(lane, window * 128)].T
         errors_turned[...] = errors[:, pl.ds(lane, window * 128)].T
-        fetch.wait()
-        inputs_turned[...] = inputs[:, pl.ds(lane, window * 128)].T
 
     shift = pl.multiple_of(place_ref[SHIFT], step_rows)
     other_shift = pl.multiple_of(place_ref[OTHER_SHIFT], step_rows)
@@ -261,32 +288,34 @@
     send_ref[:own, :] = spread_first[pl.ds(other_shift, own), :].astype(jnp.bfloat16)
 
 
-def gradient(place, members, rows, errors, inputs, worker, w_in, w_out, after=()):
-    arrays, wheres = zip(*errors)
+def gradient(place, members, swap, errors, inputs, w_in, w_out, after=()):
+    error_arrays, error_wheres = zip(*errors)
+    input_arrays, input_wheres = zip(*inputs)
     depth, width = w_in.shape
+    rows = sum(a.shape[0] for a in input_arrays)
     own = depth // members
-    reach = max(m * own % 128 + 2 * own for m in range(0, members, 2))
+    reach = max(m * own % 128 for m in range(members) if not m & swap) + (swap + 1) * own
     window = -(-reach // 128)
     tile = tile_of(width, 640)
     once = pl.Buffered(1)
     return call(
-        functools.partial(gradient_kernel, wheres, worker, window, own, math.gcd(own, 128)),
+        functools.partial(
+            gradient_kernel, (error_wheres, input_wheres), window, own, math.gcd(own, 128)
+        ),
         "gradient",
-        (place, *arrays, inputs, w_in, w_out),
+        (place, *error_arrays, *input_arrays, w_in, w_out),
         [
             jax.ShapeDtypeStruct((own, width), jnp.float32),
             jax.ShapeDtypeStruct((own, width), jnp.float32),
             jax.ShapeDtypeStruct((2 * own, width), jnp.bfloat16),
         ],
         after,
-        vmem=vmem_large,
         grid=(width // tile,),
-        in_specs=[pl.BlockSpec(a.shape, whole, pipeline_mode=once) for a in arrays]
-        + [
-            pl.BlockSpec(memory_space=pltpu.HBM),
-            pl.BlockSpec((depth, tile), column),
-            pl.BlockSpec((tile, depth), lambda n, s: (n, 0)),
-        ],
+        in_specs=[
+            pl.BlockSpec(a.shape, whole, pipeline_mode=once)
+            for a in (*error_arrays, *input_arrays)
+        ]
+        + [pl.BlockSpec((depth, tile), column), pl.BlockSpec((tile, depth), lambda n, s: (n, 0))],
         out_specs=[
             pl.BlockSpec((own, tile), column),
             pl.BlockSpec((own, tile), column),
@@ -299,12 +328,11 @@
             pltpu.VMEM((window * 128, rows), jnp.bfloat16),
             pltpu.VMEM((window * 128, tile), jnp.float32),
             pltpu.VMEM((window * 128, tile), jnp.float32),
-            pltpu.SemaphoreType.DMA,
-        ],
-    )
-
-
-def products_kernel(counts, fresh, place_ref, *refs):
+        ],
+    )
+
+
+def products_kernel(counts, labels, fresh, place_ref, *refs):
     own = refs[0].shape[0]
     slots, at = [], 0
     for count in counts:
@@ -333,19 +361,19 @@
         row = lax.broadcasted_iota(jnp.int32, result.shape, 0)
         column = lax.broadcasted_iota(jnp.int32, result.shape, 1)
         for n, (i, j) in enumerate(pairs):
-            i, j = (jnp.bitwise_xor(place_ref[MEMBER], k) for k in (i, j))
+            i, j = (jnp.bitwise_xor(place_ref[MEMBER], labels[k]) for k in (i, j))
             here = ((row == i) & (column == j)) | ((row == j) & (column == i))
             result = result + jnp.where(here, jnp.sum(totals[n]), 0.0)
         out_ref[...] = result
 
 
-def products(place, slots, fresh, known, after=()):
+def products(place, slots, labels, fresh, known, after=()):
     arrays = [a for slot in slots for a in slot]
     own, width = slots[0][0].shape
     tile = tile_of(width, 256)
     pairs = sum(len(slots) - n for n in range(fresh))
     return call(
-        functools.partial(products_kernel, [len(slot) for slot in slots], fresh),
+        functools.partial(products_kernel, [len(slot) for slot in slots], tuple(labels), fresh),
         "products",
         (place, *arrays, known),
         [jax.ShapeDtypeStruct(known.shape, jnp.float32)],
@@ -381,7 +409,7 @@
     return [items[0][i] for i in range(count)]
 
 
-def merge_kernel(counts, place_ref, totals_ref, *refs):
+def merge_kernel(labels, place_ref, totals_ref, *refs):
     refs, (first_ref, second_ref, weights_ref) = refs[:-3], refs[-3:]
 
     @pl.when(pl.program_id(0) == 0)
@@ -390,19 +418,19 @@
             i, j = (jnp.bitwise_xor(place_ref[MEMBER], k) for k in (i, j))
             return totals_ref[i, j]
 
-        for n, weight in enumerate(tree_weights(len(counts), entry)):
+        for n, weight in enumerate(tree_weights(len(labels), entry)):
             weights_ref[n] = weight
 
     first = second = 0.0
-    for n in range(len(counts)):
-        weight = weights_ref[n]
+    for n, label in enumerate(labels):
+        weight = weights_ref[label]
         first = first + weight * refs[2 * n][...].astype(jnp.float32)
         second = second + weight * refs[2 * n + 1][...].astype(jnp.float32)
     first_ref[...] = first
     second_ref[...] = second
 
 
-def merge(place, totals, slots):
+def merge(place, totals, slots, labels):
     own, width = slots[0][0].shape
     block = max(b for b in range(16, min(own, 32) + 1, 16) if own % b == 0)
     steps = own // block
@@ -414,7 +442,7 @@
         specs += [upper, upper if len(slot) == 2 else lower]
     shape = jax.ShapeDtypeStruct((own, width), jnp.float32)
     return call(
-        functools.partial(merge_kernel, [len(slot) for slot in slots]),
+        functools.partial(merge_kernel, tuple(labels)),
         "merge",
         (place, totals, *arrays),
         [shape, shape],
@@ -447,35 +475,35 @@
 
     near = shard & 1
     part_rows = row_count // shards
+    half_rows = row_count // 2
     own = inputs.shape[1] // members
-    pair_start = member // 2 * 2 * own
+    swap = min(2, members // 2)
+    bits = [2**b for b in reversed(range(gathered)) if 2**b != swap]
+    upper = member // swap % 2
+    first_row = (member - upper * swap) * own
     place = jnp.stack(
         [
-            pair_start // 128,
-            pair_start % 128 + member % 2 * own,
-            pair_start % 128 + (1 - member % 2) * own,
+            first_row // 128,
+            first_row % 128 + upper * swap * own,
+            first_row % 128 + (1 - upper) * swap * own,
             member,
             near,
             1 - near,
-            jnp.zeros_like(near),
+            part_of(shard),
         ]
-        + [part_of(shard ^ mask) for mask in range(shards)]
-        + [member // 2 ^ mask for mask in range(1, members // 2)]
     ).astype(jnp.int32)
 
-    groups = [
-        [
-            ((2 * m + lowest) * others + r) * shards + t
-            for m in range(members // 2)
-            for t in range(shards)
-        ]
-        for lowest in range(2)
-        for r in range(others)
-    ]
-    inputs_part = lax.dynamic_slice_in_dim(inputs, shard * part_rows, part_rows, 0)
-    all_inputs = lax.all_gather(
-        inputs_part, ("dp", "tensor"), axis_index_groups=groups, tiled=True
-    )
+    def to_half(piece, *before):
+        for bit in reversed(range(1, shard_levels)):
+            got = ordered(from_mask(piece, 0, 2**bit), *before)
+            piece = join(shard >> bit & 1, piece, got)
+        return piece
+
+    own_half = lax.dynamic_slice_in_dim(inputs, near * half_rows, half_rows, 0)
+    own_part = lax.dynamic_slice_in_dim(inputs, part_of(shard) * part_rows, part_rows, 0)
+    inputs_near = {
+        bit: from_mask(own_part if bit == bits[0] else own_half, bit * others, 0) for bit in bits
+    }
 
     send, hidden_near = forward(place, inputs, w_in, w_out)
     got = from_mask(send, 0, 1)
@@ -483,42 +511,59 @@
     for bit in range(1, shard_levels):
         send, summed = add_and_split(shard >> bit & 1, summed, got)
         got = from_mask(send, 0, 2**bit)
-    error = error_part(place, summed, got, targets)
-
-    def spread_over_tensor(found):
-        for bit in reversed(range(shard_levels)):
-            for mask in list(found):
-                found[mask | 2**bit] = from_mask(found[mask], 0, 2**bit)
-        return [(found[k], PARTS + k) for k in range(shards)]
-
-    arrived = {m: from_mask(error, 2 * m * others, 0) for m in range(1, members // 2)}
-    arrived[0] = error
-    slots, known = [], []
+    error = error_part(place, summed, got, targets, tuple(inputs_near.values()))
+
+    errors_near = {bit: from_mask(error, bit * others, 0) for bit in bits[:1]}
+    error = to_half(error)
+    errors_near.update({bit: from_mask(error, bit * others, 0) for bit in bits[1:]})
+    masks = [m for m in range(members) if not m & swap]
+    lowest = {m: m & -m for m in masks}
+
+    def both_halves(half):
+        return [(half, NEAR), (from_mask(half, 0, 1), FAR)]
+
+    slots, labels, known, sent = [], [], [], []
     totals = jnp.zeros((8, 128), jnp.float32)
-    for m in range(members // 2):
-        found = ordered(arrived[m], sent, arrived[min(2, members // 2 - 1)]) if m else error
+    for n, m in enumerate(masks):
+        if n == 0:
+            half = error
+        elif m not in errors_near:
+            half = from_mask(errors_near[m - lowest[m]], lowest[m] * others, 0)
+            ready = ordered(inputs_near[m - lowest[m]], errors_near[lowest[m]])
+            inputs_near[m] = from_mask(ready, lowest[m] * others, 0)
+            half, inputs_near[m] = (ordered(a, sent[-1]) for a in (half, inputs_near[m]))
+        elif m == bits[0]:
+            half = ordered(errors_near[m], sent[0])
+            half = errors_near[m] = to_half(half, *sent[1:2], *(s for slot in slots[1:2] for s in slot))
+        else:
+            half = errors_near[m] = ordered(errors_near[m], sent[0], inputs_near[bits[0]])
+        if n > 1:
+            half = ordered(half, slots[2 * n - 3][0])
         first, second, send = gradient(
             place,
             members,
-            row_count,
-            spread_over_tensor({0: found}),
-            all_inputs if m else inputs,
-            PARTS + shards + m - 1 if m else ZERO,
+            swap,
+            both_halves(half),
+            both_halves(inputs_near[m]) if n else [(inputs, None)],
             w_in,
             w_out,
             known[-2:-1],
         )
-        if m == 0:
-            sent = send
+        if n == 0 and len(masks) > 1:
+            inputs_near[bits[0]] = to_half(inputs_near[bits[0]], send)
+        sent.append(send)
         slots.append((first, second))
-        if m == members // 2 - 1:
-            totals = products(place, slots, 1, totals)
-        slots.append((from_mask(send, others, 0),))
-        totals = products(place, slots, 1 if m == members // 2 - 1 else 2, totals)
+        labels.append(m)
+        last = n == len(masks) - 1
+        if last:
+            totals = products(place, slots, labels, 1, totals)
+        slots.append((from_mask(send, swap * others, 0),))
+        labels.append(m ^ swap)
+        totals = products(place, slots, labels, 1 if last else 2, totals)
         known.append(totals)
 
     totals = group_total(totals, gathered - 1, levels)
-    pieces = merge(place, totals, slots)
+    pieces = merge(place, totals, slots, labels)
 
     for section in range(gathered, levels):
         upper_flag = position >> levels - 1 - section & 1

time: 244 us -> 218 us (0.89)
  waiting for transfers between devices: 79.9 us -> 96.4 us
  between operations: 14.4 us -> 1.23 us
  Pallas kernels: 93.6 us -> 81.5 us
  starting transfers between devices: 35.5 us -> 24.4 us
  local copies, waits for them, and re-layouts: 12.8 us -> 7.55 us
    ppermute x21 -> x22, waiting for transfers between devices: 74.3 us -> 90 us  [from_mask(): return lax.ppermute(value, ('dp', 'tensor'), pairs)]
    pallas_call x14 -> x17, Pallas kernels: 93.6 us -> 81.5 us  [call(): pl.pallas_call(body, grid_spec=pltpu.PrefetchScalarGridSpec(num_scalar_pr...]
    ppermute x3, starting transfers between devices: 13.1 us -> 5.69 us  [from_partner(): return lax.ppermute(value, axis, pairs)]
    unnamed x54 -> x40, local copies, waits for them, and re-layouts: 10.4 us -> 3.67 us
    ppermute x21 -> x22, starting transfers between devices: 22.3 us -> 18.7 us  [from_mask(): return lax.ppermute(value, ('dp', 'tensor'), pairs)]
  transfers between devices with their start and end apart: 25 -> 25, of which waited for: 11 -> 14; matrix products, arithmetic and copies ran while one was open for 0% -> 2% of each run, Pallas kernels for 34% -> 27%
where the time goes in v7:
time: 218 us
  waiting for transfers between devices  96.4 us (44%)
  Pallas kernels  81.5 us (37%)
  starting transfers between devices  24.4 us (11%)
  local copies, waits for them, and re-layouts  7.55 us (3%)
  blocking collectives  5.94 us (3%)
    ppermute x22, waiting for transfers between devices, from_mask(): return lax.ppermute(value, ('dp', 'tensor'), pairs)  90 us
    pallas_call x17, Pallas kernels, call(): pl.pallas_call(body, grid_spec=pltpu.PrefetchScalarGridSpec(num_scalar_pr...  81.5 us
    ppermute x22, starting transfers between devices, from_mask(): return lax.ppermute(value, ('dp', 'tensor'), pairs)  18.7 us
    ppermute x3, waiting for transfers between devices, from_partner(): return lax.ppermute(value, axis, pairs)  6.42 us
    psum x1, blocking collectives, group_total(): summed = lax.psum(values, 'tensor')  5.94 us
    ppermute x3, starting transfers between devices, from_partner(): return lax.ppermute(value, axis, pairs)  5.69 us
  transfers between devices with their start and end apart: 25, of which 14 were waited for; matrix products, arithmetic and copies ran while one was open for 2% of the time, Pallas kernels for 27%

profile of v7, /device:TPU:0, one launch (start us, length us, event | category | flops | bytes accessed | tf_op | source)
XLA Modules:
  0.0 217.6 jit_solution(331754165186711398)
XLA Ops:
  1.3 10.5 %forward.1 = (f32[352,1280]{1,0:T(8,128)}, bf16[352,1280]{1,0:T(8,128)(2,1)}) custom-call(s32[7]{0:T(128)} %stack.31.place_ref, bf16[704,1280]{1,0:T(8,128)(2,1)} %refs_2_.3, bf16[1280,1280]{1,0:T(8,128)(2,1)} %refs_5_.5, bf16[1280,1280]{1,0:T(8,128)(2,1)} %refs_6_.3), custom_call_target="tpu_custom_call" | custom-call | flops 1 | bytes 1 | tf_op jit(solution)/shard_map/forward/pallas_call | solution.py:81
  12.3 2.3 %constant_dynamic-slice_fusion = bf16[352,1280]{1,0:T(8,128)(2,1)} fusion(bf16[704,1280]{1,0:T(8,128)(2,1)} %refs_2_.3, s32[]{:T(128)S(6)} %select_n.32), kind=kLoop, calls=%fused_computation | loop fusion | bytes 1802244 | tf_op jit(solution)/shard_map/dynamic_slice | solution.py:502
  14.6 2.5 %collective-permute-start.1 = (bf16[352,1280]{1,0:T(8,128)(2,1)}, bf16[352,1280]{1,0:T(8,128)(2,1)}, u32[]{:S(2)}, u32[]{:S(2)}) collective-permute-start(bf16[352,1280]{1,0:T(8,128)(2,1)} %constant_dynamic-slice_fusion), channel_id=1, source_target_pairs={{0,4},{1,5},{2,6},{3,7},{4,0},{5,1},{6,2},{7,3},{8,12},{9,13},{10,... | collective-permute-start | bytes 2703368 | tf_op jit(solution)/shard_map/ppermute | solution.py:27
  17.1 2.7 %product.1.refs_0_.refs_2_ = f32[352,1280]{1,0:T(8,128)S(1)} custom-call(s32[7]{0:T(128)S(1)} %copy-done.19, bf16[352,1280]{1,0:T(8,128)(2,1)S(1)} %copy-done.16, bf16[1280,1280]{1,0:T(8,128)(2,1)S(1)} %copy-done), custom_call_target="tpu_custom_call" | custom-call | flops 1 | bytes 1 | tf_op jit(solution)/shard_map/product/pallas_call | solution.py:81
  19.8 2.6 %add_and_split.1 = (f32[176,1280]{1,0:T(8,128)}, f32[176,1280]{1,0:T(8,128)S(1)}) custom-call(s32[1]{0:T(128)} %bitcast.7.place_ref, f32[352,1280]{1,0:T(8,128)S(1)} %product.1.refs_0_.refs_2_, f32[352,1280]{1,0:T(8,128)} %collective-permute-done.2.refs_1_.refs_3_, f32[352,1280]{1,0:T(8,128)S(1)} %product.1.refs_0_.refs_2_, ...), custom_call_target="tpu_custom_call" | custom-call | flops 1 | bytes 1 | tf_op jit(solution)/shard_map/add_and_split/pallas_call | solution.py:81
  25.9 2.7 %collective-permute-start = (bf16[176,1280]{1,0:T(8,128)(2,1)S(1)}, bf16[176,1280]{1,0:T(8,128)(2,1)S(1)}, u32[]{:S(2)}, u32[]{:S(2)}) collective-permute-start(bf16[176,1280]{1,0:T(8,128)(2,1)S(1)} %constant_dynamic-slice_fusion.1), channel_id=1, source_target_pairs={{0,16},{1,17},{2,18},{3,19},{4,20},{5,21},{6,22},{7,23},{8,24},{9,... | collective-permute-start | bytes 1351688 | tf_op jit(solution)/shard_map/ppermute | solution.py:27
  28.5 20.1 %collective-permute-done.refs_0_ = bf16[176,1280]{1,0:T(8,128)(2,1)S(1)} collective-permute-done((bf16[176,1280]{1,0:T(8,128)(2,1)S(1)}, bf16[176,1280]{1,0:T(8,128)(2,1)S(1)}, u32[]{:S(2)}, u32[]{:S(2)}) %collective-permute-start) | collective-permute-done | bytes 450592 | tf_op jit(solution)/shard_map/ppermute | solution.py:27
  51.3 2.1 error_part.1.refs_0_
  54.1 10.8 %collective-permute-done.4.refs_1_ = bf16[176,1280]{1,0:T(8,128)(2,1)S(1)} collective-permute-done((bf16[176,1280]{1,0:T(8,128)(2,1)S(1)}, bf16[176,1280]{1,0:T(8,128)(2,1)S(1)}, u32[]{:S(2)}, u32[]{:S(2)}) %collective-permute-start.4) | collective-permute-done | bytes 450592 | tf_op jit(solution)/shard_map/ppermute | solution.py:27
  67.5 10.3 %gradient.4 = (f32[160,1280]{1,0:T(8,128)S(1)}, f32[160,1280]{1,0:T(8,128)S(1)}, bf16[320,1280]{1,0:T(8,128)(2,1)S(1)}) custom-call(s32[7]{0:T(128)S(1)} %copy-done.19, bf16[352,1280]{1,0:T(8,128)(2,1)S(1)} %join.3.refs_0_, bf16[352,1280]{1,0:T(8,128)(2,1)S(1)} %collective-permute-done.5.refs_1_, bf16[704,1280]{1,0:T(8,128)(2,1)S(1)} %copy-done.9, ...), custom_call_target="tpu_custom_call" | custom-call | flops 1 | bytes 1 | tf_op jit(solution)/shard_map/gradient/pallas_call | solution.py:81
  78.1 9.4 %collective-permute-done.7.refs_0_ = bf16[352,1280]{1,0:T(8,128)(2,1)S(1)} collective-permute-done((bf16[352,1280]{1,0:T(8,128)(2,1)S(1)}, bf16[352,1280]{1,0:T(8,128)(2,1)S(1)}, u32[]{:S(2)}, u32[]{:S(2)}) %collective-permute-start.7) | collective-permute-done | bytes 901152 | tf_op jit(solution)/shard_map/ppermute | solution.py:27
  87.4 1.6 collective-permute-start.6
  91.0 11.6 %gradient.5 = (f32[160,1280]{1,0:T(8,128)S(1)}, f32[160,1280]{1,0:T(8,128)S(1)}, bf16[320,1280]{1,0:T(8,128)(2,1)S(1)}) custom-call(s32[7]{0:T(128)S(1)} %copy-done.19, bf16[352,1280]{1,0:T(8,128)(2,1)S(1)} %collective-permute-done.7.refs_0_, bf16[352,1280]{1,0:T(8,128)(2,1)S(1)} %collective-permute-done.9.refs_1_, ...), custom_call_target="tpu_custom_call" | custom-call | flops 1 | bytes 1 | tf_op jit(solution)/shard_map/gradient/pallas_call | solution.py:81
  102.6 5.5 %collective-permute-done.6.refs_2_.refs_3_.refs_4_ = bf16[320,1280]{1,0:T(8,128)(2,1)S(1)} collective-permute-done((bf16[320,1280]{1,0:T(8,128)(2,1)S(1)}, bf16[320,1280]{1,0:T(8,128)(2,1)S(1)}, u32[]{:S(2)}, u32[]{:S(2)}) %collective-permute-start.6) | collective-permute-done | bytes 819232 | tf_op jit(solution)/shard_map/ppermute | solution.py:27
  110.3 1.6 collective-permute-start.11
  113.4 10.4 %gradient.6 = (f32[160,1280]{1,0:T(8,128)S(1)}, f32[160,1280]{1,0:T(8,128)S(1)}, bf16[320,1280]{1,0:T(8,128)(2,1)S(1)}) custom-call(s32[7]{0:T(128)S(1)} %copy-done.19, f32[8,128]{1,0:T(8,128)S(1)} %products.5.refs_0_.refs_6_, bf16[352,1280]{1,0:T(8,128)(2,1)S(1)} %join.5.refs_1_, bf16[352,1280]{1,0:T(8,128)(2,1)S(1)} %collective-permute-done.14.refs_2_, ...), custom_call_target="tpu_custom_call" | custom-call | flops 1 | bytes 1 | tf_op jit(solution)/shard_map/gradient/pallas_call | solution.py:81
  123.9 7.2 %collective-permute-done.17.refs_1_ = bf16[352,1280]{1,0:T(8,128)(2,1)S(1)} collective-permute-done((bf16[352,1280]{1,0:T(8,128)(2,1)S(1)}, bf16[352,1280]{1,0:T(8,128)(2,1)S(1)}, u32[]{:S(2)}, u32[]{:S(2)}) %collective-permute-start.17) | collective-permute-done | bytes 901152 | tf_op jit(solution)/shard_map/ppermute | solution.py:27
  131.1 18.8 %collective-permute-done.19.refs_3_ = bf16[352,1280]{1,0:T(8,128)(2,1)S(1)} collective-permute-done((bf16[352,1280]{1,0:T(8,128)(2,1)S(1)}, bf16[352,1280]{1,0:T(8,128)(2,1)S(1)}, u32[]{:S(2)}, u32[]{:S(2)}) %collective-permute-start.19) | collective-permute-done | bytes 901152 | tf_op jit(solution)/shard_map/ppermute | solution.py:27
  150.0 1.6 collective-permute-start.16
  151.6 2.4 %products.6.refs_0_.refs_9_ = f32[8,128]{1,0:T(8,128)S(1)} custom-call(s32[7]{0:T(128)S(1)} %copy-done.19, f32[160,1280]{1,0:T(8,128)S(1)} %get-tuple-element.31.refs_0_.refs_1_, f32[160,1280]{1,0:T(8,128)S(1)} %get-tuple-element.32.refs_1_.refs_2_, bf16[320,1280]{1,0:T(8,128)(2,1)S(1)} %collective-permute-done.6.refs_2_.refs_3_.refs_4_, ...), custom_call_target="tpu_custom_call" | custom-call | flops 1 | bytes 1 | tf_op jit(solution)/shard_map/products/pallas_call | solution.py:81
  154.0 10.7 %gradient.7 = (f32[160,1280]{1,0:T(8,128)S(1)}, f32[160,1280]{1,0:T(8,128)S(1)}, bf16[320,1280]{1,0:T(8,128)(2,1)S(1)}) custom-call(s32[7]{0:T(128)S(1)} %copy-done.19, f32[8,128]{1,0:T(8,128)S(1)} %products.6.refs_0_.refs_9_, bf16[352,1280]{1,0:T(8,128)(2,1)S(1)} %collective-permute-done.17.refs_1_, bf16[352,1280]{1,0:T(8,128)(2,1)S(1)} %collective-permute-done.18.refs_2_, ...), custom_call_target="tpu_custom_call" | custom-call | flops 1 | bytes 1 | tf_op jit(solution)/shard_map/gradient/pallas_call | solution.py:81
  165.2 5.9 %collective-permute-done.16.refs_8_.refs_11_.refs_12_ = bf16[320,1280]{1,0:T(8,128)(2,1)S(1)} collective-permute-done((bf16[320,1280]{1,0:T(8,128)(2,1)S(1)}, bf16[320,1280]{1,0:T(8,128)(2,1)S(1)}, u32[]{:S(2)}, u32[]{:S(2)}) %collective-permute-start.16) | collective-permute-done | bytes 819232 | tf_op jit(solution)/shard_map/ppermute | solution.py:27
  171.0 3.4 %products.7.refs_11_ = f32[8,128]{1,0:T(8,128)S(1)} custom-call(s32[7]{0:T(128)S(1)} %copy-done.19, f32[160,1280]{1,0:T(8,128)S(1)} %get-tuple-element.31.refs_0_.refs_1_, f32[160,1280]{1,0:T(8,128)S(1)} %get-tuple-element.32.refs_1_.refs_2_, bf16[320,1280]{1,0:T(8,128)(2,1)S(1)} %collective-permute-done.6.refs_2_.refs_3_.refs_4_, ...), custom_call_target="tpu_custom_call" | custom-call | flops 1 | bytes 1 | tf_op jit(solution)/shard_map/products/pallas_call | solution.py:81
  174.4 2.7 %products.8.refs_12_ = f32[8,128]{1,0:T(8,128)S(1)} custom-call(s32[7]{0:T(128)S(1)} %copy-done.19, f32[160,1280]{1,0:T(8,128)S(1)} %get-tuple-element.31.refs_0_.refs_1_, f32[160,1280]{1,0:T(8,128)S(1)} %get-tuple-element.32.refs_1_.refs_2_, bf16[320,1280]{1,0:T(8,128)(2,1)S(1)} %collective-permute-done.6.refs_2_.refs_3_.refs_4_, ...), custom_call_target="tpu_custom_call" | custom-call | flops 1 | bytes 1 | tf_op jit(solution)/shard_map/products/pallas_call | solution.py:81
  177.1 11.1 %collective-permute-done.21.refs_11_.refs_15_.refs_16_ = bf16[320,1280]{1,0:T(8,128)(2,1)S(1)} collective-permute-done((bf16[320,1280]{1,0:T(8,128)(2,1)S(1)}, bf16[320,1280]{1,0:T(8,128)(2,1)S(1)}, u32[]{:S(2)}, u32[]{:S(2)}) %collective-permute-start.21) | collective-permute-done | bytes 819232 | tf_op jit(solution)/shard_map/ppermute | solution.py:27
  188.3 3.2 %products.9 = f32[8,128]{1,0:T(8,128)S(1)} custom-call(s32[7]{0:T(128)S(1)} %copy-done.19, f32[160,1280]{1,0:T(8,128)S(1)} %get-tuple-element.31.refs_0_.refs_1_, f32[160,1280]{1,0:T(8,128)S(1)} %get-tuple-element.32.refs_1_.refs_2_, bf16[320,1280]{1,0:T(8,128)(2,1)S(1)} %collective-permute-done.6.refs_2_.refs_3_.refs_4_, ...), custom_call_target="tpu_custom_call" | custom-call | flops 1 | bytes 1 | tf_op jit(solution)/shard_map/products/pallas_call | solution.py:81
  191.5 5.9 %psum.7 = f32[8,128]{1,0:T(8,128)S(1)} all-reduce(f32[8,128]{1,0:T(8,128)S(1)} %products.9), channel_id=1, replica_groups=mesh['dp'=8,'tensor'=4] {'tensor'}, use_global_device_ids=true, to_apply=%region_0.1 | all-reduce | flops 1024 | bytes 8192 | tf_op jit(solution)/shard_map/psum | solution.py:42
  197.4 3.3 %collective-permute-start.22 = (f32[8,128]{1,0:T(8,128)S(1)}, f32[8,128]{1,0:T(8,128)S(1)}, u32[]{:S(2)}, u32[]{:S(2)}) collective-permute-start(f32[8,128]{1,0:T(8,128)S(1)} %psum.7), channel_id=1, source_target_pairs={{0,16},{4,20},{8,24},{12,28},{16,0},{20,4},{24,8},{28,12},{1,17},{... | collective-permute-start | bytes 12296 | tf_op jit(solution)/shard_map/ppermute | solution.py:20
  202.3 1.7 collective-permute-start.23
  204.1 1.9 collective-permute-done.23
  206.6 3.0 %collective-permute-done.24 = f32[8,128]{1,0:T(8,128)S(1)} collective-permute-done((f32[8,128]{1,0:T(8,128)S(1)}, f32[8,128]{1,0:T(8,128)S(1)}, u32[]{:S(2)}, u32[]{:S(2)}) %collective-permute-start.24) | collective-permute-done | bytes 4128 | tf_op jit(solution)/shard_map/ppermute | solution.py:20
  210.1 7.3 %merge.1 = (f32[160,1280]{1,0:T(8,128)}, f32[160,1280]{1,0:T(8,128)}) custom-call(s32[7]{0:T(128)} %stack.31.place_ref, f32[8,128]{1,0:T(8,128)} %add.47.refs_0_, f32[160,1280]{1,0:T(8,128)} %copy-done.4, f32[160,1280]{1,0:T(8,128)} %copy-done.5, bf16[320,1280]{1,0:T(8,128)(2,1)} %copy-done.2, bf16[320,1280]{1,0:T(8,128)(2,1)} %copy-done.2, ...), custom_call_target="tpu_custom_call" | custom-call | flops 1 | bytes 1 | tf_op jit(solution)/shard_map/merge/pallas_call | solution.py:81
  (83 shorter events, 19.6 us)
Async XLA Ops:
  11.8 8.0 %collective-permute-start.2 = (f32[352,1280]{1,0:T(8,128)}, f32[352,1280]{1,0:T(8,128)}, u32[]{:S(2)}, u32[]{:S(2)}) collective-permute-start(f32[352,1280]{1,0:T(8,128)} %get-tuple-element.28), channel_id=1, source_target_pairs={{0,1},{1,0},{2,3},{3,2},{4,5},{5,4},{6,7},{7,6},{8,9},{9,8},{10,11... | collective-permute-start | bytes 5406728 | tf_op jit(solution)/shard_map/ppermute | solution.py:27
  14.6 34.1 %collective-permute-start.1 = (bf16[352,1280]{1,0:T(8,128)(2,1)}, bf16[352,1280]{1,0:T(8,128)(2,1)}, u32[]{:S(2)}, u32[]{:S(2)}) collective-permute-start(bf16[352,1280]{1,0:T(8,128)(2,1)} %constant_dynamic-slice_fusion), channel_id=1, source_target_pairs={{0,4},{1,5},{2,6},{3,7},{4,0},{5,1},{6,2},{7,3},{8,12},{9,13},{10,... | collective-permute-start | bytes 2703368 | tf_op jit(solution)/shard_map/ppermute | solution.py:27
  23.3 25.3 %collective-permute-start.3 = (f32[176,1280]{1,0:T(8,128)}, f32[176,1280]{1,0:T(8,128)}, u32[]{:S(2)}, u32[]{:S(2)}) collective-permute-start(f32[176,1280]{1,0:T(8,128)} %get-tuple-element.30), channel_id=1, source_target_pairs={{0,2},{1,3},{2,0},{3,1},{4,6},{5,7},{6,4},{7,5},{8,10},{9,11},{10,... | collective-permute-start | bytes 2703368 | tf_op jit(solution)/shard_map/ppermute | solution.py:27
  25.9 22.8 %collective-permute-start = (bf16[176,1280]{1,0:T(8,128)(2,1)S(1)}, bf16[176,1280]{1,0:T(8,128)(2,1)S(1)}, u32[]{:S(2)}, u32[]{:S(2)}) collective-permute-start(bf16[176,1280]{1,0:T(8,128)(2,1)S(1)} %constant_dynamic-slice_fusion.1), channel_id=1, source_target_pairs={{0,16},{1,17},{2,18},{3,19},{4,20},{5,21},{6,22},{7,23},{8,24},{9,... | collective-permute-start | bytes 1351688 | tf_op jit(solution)/shard_map/ppermute | solution.py:27
  53.5 11.4 %collective-permute-start.4 = (bf16[176,1280]{1,0:T(8,128)(2,1)S(1)}, bf16[176,1280]{1,0:T(8,128)(2,1)S(1)}, u32[]{:S(2)}, u32[]{:S(2)}) collective-permute-start(bf16[176,1280]{1,0:T(8,128)(2,1)S(1)} %error_part.1.refs_0_), channel_id=1, source_target_pairs={{0,2},{1,3},{2,0},{3,1},{4,6},{5,7},{6,4},{7,5},{8,10},{9,11},{10,... | collective-permute-start | bytes 1351688 | tf_op jit(solution)/shard_map/ppermute | solution.py:27
  64.9 2.5 %collective-permute-start.5 = (bf16[352,1280]{1,0:T(8,128)(2,1)S(1)}, bf16[352,1280]{1,0:T(8,128)(2,1)S(1)}, u32[]{:S(2)}, u32[]{:S(2)}) collective-permute-start(bf16[352,1280]{1,0:T(8,128)(2,1)S(1)} %join.3.refs_0_), channel_id=1, source_target_pairs={{0,1},{1,0},{2,3},{3,2},{4,5},{5,4},{6,7},{7,6},{8,9},{9,8},{10,11... | collective-permute-start | bytes 2703368 | tf_op jit(solution)/shard_map/ppermute | solution.py:27
  65.0 22.4 %collective-permute-start.7 = (bf16[352,1280]{1,0:T(8,128)(2,1)S(1)}, bf16[352,1280]{1,0:T(8,128)(2,1)S(1)}, u32[]{:S(2)}, u32[]{:S(2)}) collective-permute-start(bf16[352,1280]{1,0:T(8,128)(2,1)S(1)} %join.3.refs_0_), channel_id=1, source_target_pairs={{0,4},{1,5},{2,6},{3,7},{4,0},{5,1},{6,2},{7,3},{8,12},{9,13},{10,... | collective-permute-start | bytes 2703368 | tf_op jit(solution)/shard_map/ppermute | solution.py:27
  65.6 12.4 %collective-permute-start.8 = (bf16[176,1280]{1,0:T(8,128)(2,1)S(1)}, bf16[176,1280]{1,0:T(8,128)(2,1)S(1)}, u32[]{:S(2)}, u32[]{:S(2)}) collective-permute-start(bf16[176,1280]{1,0:T(8,128)(2,1)S(1)} %collective-permute-done.refs_0_), channel_id=1, source_target_pairs={{0,2},{1,3},{2,0},{3,1},{4,6},{5,7},{6,4},{7,5},{8,10},{9,11},{10,... | collective-permute-start | bytes 1351688 | tf_op jit(solution)/shard_map/ppermute | solution.py:27
  66.4 24.5 %collective-permute-start.10 = (bf16[352,1280]{1,0:T(8,128)(2,1)}, bf16[352,1280]{1,0:T(8,128)(2,1)S(1)}, u32[]{:S(2)}, u32[]{:S(2)}) collective-permute-start(bf16[352,1280]{1,0:T(8,128)(2,1)} %collective-permute-done.1.refs_1_.refs_2_), channel_id=1, source_target_pairs={{0,1},{1,0},{2,3},{3,2},{4,5},{5,4},{6,7},{7,6},{8,9},{9,8},{10,11... | collective-permute-start | bytes 2703368 | tf_op jit(solution)/shard_map/ppermute | solution.py:27
  66.4 23.3 %collective-permute-start.12 = (bf16[176,1280]{1,0:T(8,128)(2,1)S(1)}, bf16[176,1280]{1,0:T(8,128)(2,1)S(1)}, u32[]{:S(2)}, u32[]{:S(2)}) collective-permute-start(bf16[176,1280]{1,0:T(8,128)(2,1)S(1)} %error_part.1.refs_0_), channel_id=1, source_target_pairs={{0,16},{1,17},{2,18},{3,19},{4,20},{5,21},{6,22},{7,23},{8,24},{9,... | collective-permute-start | bytes 1351688 | tf_op jit(solution)/shard_map/ppermute | solution.py:27
  77.8 110.4 %copy-start.4 = (f32[160,1280]{1,0:T(8,128)}, f32[160,1280]{1,0:T(8,128)S(1)}, u32[]{:S(2)}) copy-start(f32[160,1280]{1,0:T(8,128)S(1)} %get-tuple-element.31.refs_0_.refs_1_) | copy-start | bytes 2457604
  77.8 110.4 %copy-start.5 = (f32[160,1280]{1,0:T(8,128)}, f32[160,1280]{1,0:T(8,128)S(1)}, u32[]{:S(2)}) copy-start(f32[160,1280]{1,0:T(8,128)S(1)} %get-tuple-element.32.refs_1_.refs_2_) | copy-start | bytes 2457604
  87.4 3.5 %collective-permute-start.9 = (bf16[352,1280]{1,0:T(8,128)(2,1)S(1)}, bf16[352,1280]{1,0:T(8,128)(2,1)S(1)}, u32[]{:S(2)}, u32[]{:S(2)}) collective-permute-start(bf16[352,1280]{1,0:T(8,128)(2,1)S(1)} %collective-permute-done.7.refs_0_), channel_id=1, source_target_pairs={{0,1},{1,0},{2,3},{3,2},{4,5},{5,4},{6,7},{7,6},{8,9},{9,8},{10,11... | collective-permute-start | bytes 2703368 | tf_op jit(solution)/shard_map/ppermute | solution.py:27
  87.4 20.7 %collective-permute-start.6 = (bf16[320,1280]{1,0:T(8,128)(2,1)S(1)}, bf16[320,1280]{1,0:T(8,128)(2,1)S(1)}, u32[]{:S(2)}, u32[]{:S(2)}) collective-permute-start(bf16[320,1280]{1,0:T(8,128)(2,1)S(1)} %get-tuple-element.33), channel_id=1, source_target_pairs={{0,8},{1,9},{2,10},{3,11},{4,12},{5,13},{6,14},{7,15},{8,0},{9,1},... | collective-permute-start | bytes 2457608 | tf_op jit(solution)/shard_map/ppermute | solution.py:27
  89.7 12.9 %collective-permute-start.13 = (bf16[176,1280]{1,0:T(8,128)(2,1)S(1)}, bf16[176,1280]{1,0:T(8,128)(2,1)S(1)}, u32[]{:S(2)}, u32[]{:S(2)}) collective-permute-start(bf16[176,1280]{1,0:T(8,128)(2,1)S(1)} %collective-permute-done.12.refs_0_), channel_id=1, source_target_pairs={{0,2},{1,3},{2,0},{3,1},{4,6},{5,7},{6,4},{7,5},{8,10},{9,11},{10,... | collective-permute-start | bytes 1351688 | tf_op jit(solution)/shard_map/ppermute | solution.py:27
  90.9 22.4 %collective-permute-start.15 = (bf16[352,1280]{1,0:T(8,128)(2,1)S(1)}, bf16[352,1280]{1,0:T(8,128)(2,1)S(1)}, u32[]{:S(2)}, u32[]{:S(2)}) collective-permute-start(bf16[352,1280]{1,0:T(8,128)(2,1)S(1)} %join.4.refs_3_), channel_id=1, source_target_pairs={{0,1},{1,0},{2,3},{3,2},{4,5},{5,4},{6,7},{7,6},{8,9},{9,8},{10,11... | collective-permute-start | bytes 2703368 | tf_op jit(solution)/shard_map/ppermute | solution.py:27
  102.6 85.6 %copy-start.6 = (f32[160,1280]{1,0:T(8,128)}, f32[160,1280]{1,0:T(8,128)S(1)}, u32[]{:S(2)}) copy-start(f32[160,1280]{1,0:T(8,128)S(1)} %get-tuple-element.36.refs_3_.refs_5_) | copy-start | bytes 2457604
  102.6 85.6 %copy-start.7 = (f32[160,1280]{1,0:T(8,128)}, f32[160,1280]{1,0:T(8,128)S(1)}, u32[]{:S(2)}) copy-start(f32[160,1280]{1,0:T(8,128)S(1)} %get-tuple-element.37.refs_4_.refs_6_) | copy-start | bytes 2457604
  108.1 80.1 %copy-start.2 = (bf16[320,1280]{1,0:T(8,128)(2,1)}, bf16[320,1280]{1,0:T(8,128)(2,1)S(1)}, u32[]{:S(2)}) copy-start(bf16[320,1280]{1,0:T(8,128)(2,1)S(1)} %collective-permute-done.6.refs_2_.refs_3_.refs_4_) | copy-start | bytes 2457604
  108.2 5.2 %collective-permute-start.14 = (bf16[352,1280]{1,0:T(8,128)(2,1)S(1)}, bf16[352,1280]{1,0:T(8,128)(2,1)S(1)}, u32[]{:S(2)}, u32[]{:S(2)}) collective-permute-start(bf16[352,1280]{1,0:T(8,128)(2,1)S(1)} %join.5.refs_1_), channel_id=1, source_target_pairs={{0,1},{1,0},{2,3},{3,2},{4,5},{5,4},{6,7},{7,6},{8,9},{9,8},{10,11... | collective-permute-start | bytes 2703368 | tf_op jit(solution)/shard_map/ppermute | solution.py:27
  108.2 22.9 %collective-permute-start.17 = (bf16[352,1280]{1,0:T(8,128)(2,1)S(1)}, bf16[352,1280]{1,0:T(8,128)(2,1)S(1)}, u32[]{:S(2)}, u32[]{:S(2)}) collective-permute-start(bf16[352,1280]{1,0:T(8,128)(2,1)S(1)} %join.5.refs_1_), channel_id=1, source_target_pairs={{0,4},{1,5},{2,6},{3,7},{4,0},{5,1},{6,2},{7,3},{8,12},{9,13},{10,... | collective-permute-start | bytes 2703368 | tf_op jit(solution)/shard_map/ppermute | solution.py:27
  108.8 41.1 %collective-permute-start.19 = (bf16[352,1280]{1,0:T(8,128)(2,1)S(1)}, bf16[352,1280]{1,0:T(8,128)(2,1)S(1)}, u32[]{:S(2)}, u32[]{:S(2)}) collective-permute-start(bf16[352,1280]{1,0:T(8,128)(2,1)S(1)} %join.4.refs_3_), channel_id=1, source_target_pairs={{0,4},{1,5},{2,6},{3,7},{4,0},{5,1},{6,2},{7,3},{8,12},{9,13},{10,... | collective-permute-start | bytes 2703368 | tf_op jit(solution)/shard_map/ppermute | solution.py:27
  110.3 20.8 %collective-permute-start.11 = (bf16[320,1280]{1,0:T(8,128)(2,1)S(1)}, bf16[320,1280]{1,0:T(8,128)(2,1)S(1)}, u32[]{:S(2)}, u32[]{:S(2)}) collective-permute-start(bf16[320,1280]{1,0:T(8,128)(2,1)S(1)} %get-tuple-element.38), channel_id=1, source_target_pairs={{0,8},{1,9},{2,10},{3,11},{4,12},{5,13},{6,14},{7,15},{8,0},{9,1},... | collective-permute-start | bytes 2457608 | tf_op jit(solution)/shard_map/ppermute | solution.py:27
  123.9 64.4 %copy-start.10 = (f32[160,1280]{1,0:T(8,128)}, f32[160,1280]{1,0:T(8,128)S(1)}, u32[]{:S(2)}) copy-start(f32[160,1280]{1,0:T(8,128)S(1)} %get-tuple-element.42.refs_6_.refs_9_) | copy-start | bytes 2457604
  123.9 64.4 %copy-start.11 = (f32[160,1280]{1,0:T(8,128)}, f32[160,1280]{1,0:T(8,128)S(1)}, u32[]{:S(2)}) copy-start(f32[160,1280]{1,0:T(8,128)S(1)} %get-tuple-element.43.refs_7_.refs_10_) | copy-start | bytes 2457604
  131.1 22.9 %collective-permute-start.18 = (bf16[352,1280]{1,0:T(8,128)(2,1)S(1)}, bf16[352,1280]{1,0:T(8,128)(2,1)S(1)}, u32[]{:S(2)}, u32[]{:S(2)}) collective-permute-start(bf16[352,1280]{1,0:T(8,128)(2,1)S(1)} %collective-permute-done.17.refs_1_), channel_id=1, source_target_pairs={{0,1},{1,0},{2,3},{3,2},{4,5},{5,4},{6,7},{7,6},{8,9},{9,8},{10,11... | collective-permute-start | bytes 2703368 | tf_op jit(solution)/shard_map/ppermute | solution.py:27
  150.0 4.0 %collective-permute-start.20 = (bf16[352,1280]{1,0:T(8,128)(2,1)S(1)}, bf16[352,1280]{1,0:T(8,128)(2,1)S(1)}, u32[]{:S(2)}, u32[]{:S(2)}) collective-permute-start(bf16[352,1280]{1,0:T(8,128)(2,1)S(1)} %collective-permute-done.19.refs_3_), channel_id=1, source_target_pairs={{0,1},{1,0},{2,3},{3,2},{4,5},{5,4},{6,7},{7,6},{8,9},{9,8},{10,11... | collective-permute-start | bytes 2703368 | tf_op jit(solution)/shard_map/ppermute | solution.py:27
  150.0 21.0 %collective-permute-start.16 = (bf16[320,1280]{1,0:T(8,128)(2,1)S(1)}, bf16[320,1280]{1,0:T(8,128)(2,1)S(1)}, u32[]{:S(2)}, u32[]{:S(2)}) collective-permute-start(bf16[320,1280]{1,0:T(8,128)(2,1)S(1)} %get-tuple-element.44), channel_id=1, source_target_pairs={{0,8},{1,9},{2,10},{3,11},{4,12},{5,13},{6,14},{7,15},{8,0},{9,1},... | collective-permute-start | bytes 2457608 | tf_op jit(solution)/shard_map/ppermute | solution.py:27
  164.7 23.5 %collective-permute-start.21 = (bf16[320,1280]{1,0:T(8,128)(2,1)S(1)}, bf16[320,1280]{1,0:T(8,128)(2,1)S(1)}, u32[]{:S(2)}, u32[]{:S(2)}) collective-permute-start(bf16[320,1280]{1,0:T(8,128)(2,1)S(1)} %get-tuple-element.51), channel_id=1, source_target_pairs={{0,8},{1,9},{2,10},{3,11},{4,12},{5,13},{6,14},{7,15},{8,0},{9,1},... | collective-permute-start | bytes 2457608 | tf_op jit(solution)/shard_map/ppermute | solution.py:27
  197.4 4.9 %collective-permute-start.22 = (f32[8,128]{1,0:T(8,128)S(1)}, f32[8,128]{1,0:T(8,128)S(1)}, u32[]{:S(2)}, u32[]{:S(2)}) collective-permute-start(f32[8,128]{1,0:T(8,128)S(1)} %psum.7), channel_id=1, source_target_pairs={{0,16},{4,20},{8,24},{12,28},{16,0},{20,4},{24,8},{28,12},{1,17},{... | collective-permute-start | bytes 12296 | tf_op jit(solution)/shard_map/ppermute | solution.py:20
  202.3 3.6 %collective-permute-start.23 = (f32[8,128]{1,0:T(8,128)S(1)}, f32[8,128]{1,0:T(8,128)S(1)}, u32[]{:S(2)}, u32[]{:S(2)}) collective-permute-start(f32[8,128]{1,0:T(8,128)S(1)} %add.45), channel_id=1, source_target_pairs={{0,8},{4,12},{8,0},{12,4},{16,24},{20,28},{24,16},{28,20},{1,9},{5... | collective-permute-start | bytes 12296 | tf_op jit(solution)/shard_map/ppermute | solution.py:20
  205.9 3.6 %collective-permute-start.24 = (f32[8,128]{1,0:T(8,128)S(1)}, f32[8,128]{1,0:T(8,128)S(1)}, u32[]{:S(2)}, u32[]{:S(2)}) collective-permute-start(f32[8,128]{1,0:T(8,128)S(1)} %add.46), channel_id=1, source_target_pairs={{0,4},{4,0},{8,12},{12,8},{16,20},{20,16},{24,28},{28,24},{1,5},{5... | collective-permute-start | bytes 12296 | tf_op jit(solution)/shard_map/ppermute | solution.py:20
  (13 other events, 184.4 us)

commit v8 on v7

--- a/solution.py
+++ b/solution.py
@@ -107,7 +107,9 @@
 CUBE = 0.044715
 
 
-def forward_kernel(steps, place_ref, rows_ref, w_in_ref, w_out_ref, out_ref, near_ref, hidden):
+def forward_kernel(
+    steps, place_ref, rows_ref, w_in_ref, w_out_ref, out_ref, near_ref, half_ref, part_ref, hidden
+):
     step = pl.program_id(0)
     half = out_ref.shape[0]
     far = pl.ds(row_start(place_ref, out_ref, FAR), half)
@@ -121,6 +123,11 @@
             t = jnp.tanh(v * (SCALE + (SCALE * CUBE) * (v * v)))
             hidden[:, n * tile : (n + 1) * tile] = (v * (0.5 + 0.5 * t)).astype(jnp.bfloat16)
 
+    @pl.when(step == 0)
+    def _():
+        half_ref[...] = rows_ref[pl.ds(row_start(place_ref, half_ref, NEAR), half), :]
+        part_ref[...] = rows_ref[pl.ds(row_start(place_ref, part_ref, PART), part_ref.shape[0]), :]
+
     @pl.when(step == steps)
     def _():
         near_ref[...] = hidden[pl.ds(row_start(place_ref, out_ref, NEAR), half), :]
@@ -130,7 +137,7 @@
         out_ref[...] = jnp.dot(hidden[far, :], w_out_ref[...], preferred_element_type=jnp.float32)
 
 
-def forward(place, inputs, w_in, w_out):
+def forward(place, part_rows, inputs, w_in, w_out):
     rows = inputs.shape[0]
     depth, width = w_in.shape
     tile, out_tile = tile_of(width, 640), tile_of(depth, 640)
@@ -143,6 +150,8 @@
         [
             jax.ShapeDtypeStruct((rows // 2, depth), jnp.float32),
             jax.ShapeDtypeStruct((rows // 2, width), jnp.bfloat16),
+            jax.ShapeDtypeStruct((rows // 2, depth), jnp.bfloat16),
+            jax.ShapeDtypeStruct((part_rows, depth), jnp.bfloat16),
         ],
         vmem=vmem_most,
         grid=(steps + depth // out_tile,),
@@ -154,6 +163,8 @@
         out_specs=[
             pl.BlockSpec((rows // 2, out_tile), lambda n, s: (0, last(n))),
             pl.BlockSpec((rows // 2, width), whole),
+            pl.BlockSpec((rows // 2, depth), whole),
+            pl.BlockSpec((part_rows, depth), whole),
         ],
         scratch_shapes=[pltpu.VMEM((rows, width), jnp.bfloat16)],
     )
@@ -252,7 +263,7 @@
         return taken
 
     error_refs, input_refs = take(len(error_wheres)), take(len(input_wheres))
-    w_in_ref, w_out_ref, first_ref, second_ref, send_ref = take(5)
+    w_in_ref, w_out_ref, first_ref, second_ref, send_first_ref, send_second_ref = take(6)
     errors, inputs, inputs_turned, errors_turned, spread_first, spread_second = refs
     if len(input_refs) == 1:
         inputs = input_refs[0]
@@ -283,9 +294,9 @@
     dpre = (back * slope).astype(jnp.bfloat16)
     spread_first[...] = jnp.dot(inputs_turned[...], dpre, preferred_element_type=jnp.float32)
     second_ref[...] = spread_second[pl.ds(shift, own), :]
-    send_ref[own:, :] = spread_second[pl.ds(other_shift, own), :].astype(jnp.bfloat16)
+    send_second_ref[...] = spread_second[pl.ds(other_shift, own), :].astype(jnp.bfloat16)
     first_ref[...] = spread_first[pl.ds(shift, own), :]
-    send_ref[:own, :] = spread_first[pl.ds(other_shift, own), :].astype(jnp.bfloat16)
+    send_first_ref[...] = spread_first[pl.ds(other_shift, own), :].astype(jnp.bfloat16)
 
 
 def gradient(place, members, swap, errors, inputs, w_in, w_out, after=()):
@@ -307,7 +318,8 @@
         [
             jax.ShapeDtypeStruct((own, width), jnp.float32),
             jax.ShapeDtypeStruct((own, width), jnp.float32),
-            jax.ShapeDtypeStruct((2 * own, width), jnp.bfloat16),
+            jax.ShapeDtypeStruct((own, width), jnp.bfloat16),
+            jax.ShapeDtypeStruct((own, width), jnp.bfloat16),
         ],
         after,
         grid=(width // tile,),
@@ -316,11 +328,7 @@
             for a in (*error_arrays, *input_arrays)
         ]
         + [pl.BlockSpec((depth, tile), column), pl.BlockSpec((tile, depth), lambda n, s: (n, 0))],
-        out_specs=[
-            pl.BlockSpec((own, tile), column),
-            pl.BlockSpec((own, tile), column),
-            pl.BlockSpec((2 * own, tile), column),
-        ],
+        out_specs=[pl.BlockSpec((own, tile), column)] * 4,
         scratch_shapes=[
             pltpu.VMEM((rows, depth), jnp.bfloat16),
             pltpu.VMEM((rows, depth), jnp.bfloat16),
@@ -332,13 +340,10 @@
     )
 
 
-def products_kernel(counts, labels, fresh, place_ref, *refs):
+def products_kernel(labels, fresh, place_ref, *refs):
     own = refs[0].shape[0]
-    slots, at = [], 0
-    for count in counts:
-        slots.append(refs[at : at + count])
-        at += count
-    known_ref, out_ref, totals = refs[at:]
+    slots = [refs[2 * n : 2 * n + 2] for n in range(len(labels))]
+    known_ref, out_ref, totals = refs[2 * len(labels) :]
     pairs = [(i, j) for i in range(len(slots) - fresh, len(slots)) for j in range(i + 1)]
 
     @pl.when(pl.program_id(0) == 0)
@@ -346,9 +351,7 @@
         totals[...] = jnp.zeros_like(totals)
 
     def values(slot):
-        if len(slot) == 2:
-            return slot[0][...], slot[1][...]
-        return slot[0][:own, :].astype(jnp.float32), slot[0][own:, :].astype(jnp.float32)
+        return [ref[...].astype(jnp.float32) for ref in slot]
 
     for n, (i, j) in enumerate(pairs):
         a, b = values(slots[i]), values(slots[j])
@@ -373,7 +376,7 @@
     tile = tile_of(width, 256)
     pairs = sum(len(slots) - n for n in range(fresh))
     return call(
-        functools.partial(products_kernel, [len(slot) for slot in slots], tuple(labels), fresh),
+        functools.partial(products_kernel, tuple(labels), fresh),
         "products",
         (place, *arrays, known),
         [jax.ShapeDtypeStruct(known.shape, jnp.float32)],
@@ -433,13 +436,8 @@
 def merge(place, totals, slots, labels):
     own, width = slots[0][0].shape
     block = max(b for b in range(16, min(own, 32) + 1, 16) if own % b == 0)
-    steps = own // block
-    upper = pl.BlockSpec((block, width), lambda n, s: (n, 0))
-    lower = pl.BlockSpec((block, width), lambda n, s: (n + steps, 0))
-    arrays, specs = [], []
-    for slot in slots:
-        arrays += [slot[0], slot[-1]]
-        specs += [upper, upper if len(slot) == 2 else lower]
+    spec = pl.BlockSpec((block, width), lambda n, s: (n, 0))
+    arrays = [a for slot in slots for a in slot]
     shape = jax.ShapeDtypeStruct((own, width), jnp.float32)
     return call(
         functools.partial(merge_kernel, tuple(labels)),
@@ -447,9 +445,9 @@
         (place, totals, *arrays),
         [shape, shape],
         vmem=vmem_most,
-        grid=(steps,),
-        in_specs=[pl.BlockSpec(memory_space=pltpu.SMEM)] + specs,
-        out_specs=[upper, upper],
+        grid=(own // block,),
+        in_specs=[pl.BlockSpec(memory_space=pltpu.SMEM)] + [spec] * len(arrays),
+        out_specs=[spec, spec],
         scratch_shapes=[pltpu.SMEM((len(slots),), jnp.float32)],
     )
 
@@ -475,7 +473,6 @@
 
     near = shard & 1
     part_rows = row_count // shards
-    half_rows = row_count // 2
     own = inputs.shape[1] // members
     swap = min(2, members // 2)
     bits = [2**b for b in reversed(range(gathered)) if 2**b != swap]
@@ -499,14 +496,11 @@
             piece = join(shard >> bit & 1, piece, got)
         return piece
 
-    own_half = lax.dynamic_slice_in_dim(inputs, near * half_rows, half_rows, 0)
-    own_part = lax.dynamic_slice_in_dim(inputs, part_of(shard) * part_rows, part_rows, 0)
+    send, hidden_near, own_half, own_part = forward(place, part_rows, inputs, w_in, w_out)
+    got = from_mask(send, 0, 1)
     inputs_near = {
         bit: from_mask(own_part if bit == bits[0] else own_half, bit * others, 0) for bit in bits
     }
-
-    send, hidden_near = forward(place, inputs, w_in, w_out)
-    got = from_mask(send, 0, 1)
     summed = product(place, hidden_near, w_out)
     for bit in range(1, shard_levels):
         send, summed = add_and_split(shard >> bit & 1, summed, got)
@@ -529,17 +523,22 @@
             half = error
         elif m not in errors_near:
             half = from_mask(errors_near[m - lowest[m]], lowest[m] * others, 0)
-            ready = ordered(inputs_near[m - lowest[m]], errors_near[lowest[m]])
-            inputs_near[m] = from_mask(ready, lowest[m] * others, 0)
             half, inputs_near[m] = (ordered(a, sent[-1]) for a in (half, inputs_near[m]))
+            half = ordered(half, *slots[2 * n - 3])
         elif m == bits[0]:
-            half = ordered(errors_near[m], sent[0])
-            half = errors_near[m] = to_half(half, *sent[1:2], *(s for slot in slots[1:2] for s in slot))
+            before = [sent[-1], *slots[1]]
+            for bit in bits[1:]:
+                ready = ordered(inputs_near[m], errors_near[bit])
+                inputs_near[m | bit] = from_mask(ready, bit * others, 0)
+                before.append(inputs_near[m | bit])
+            half = to_half(ordered(errors_near[m], sent[0]), *before)
+            errors_near[m] = half
         else:
-            half = errors_near[m] = ordered(errors_near[m], sent[0], inputs_near[bits[0]])
-        if n > 1:
-            half = ordered(half, slots[2 * n - 3][0])
-        first, second, send = gradient(
+            first_bit = bits[0]
+            half = ordered(errors_near[m], sent[0], inputs_near[first_bit], errors_near[first_bit])
+            errors_near[m] = half
+            half = ordered(half, slots[2 * n - 1][0])
+        first, second, *send = gradient(
             place,
             members,
             swap,
@@ -550,14 +549,14 @@
             known[-2:-1],
         )
         if n == 0 and len(masks) > 1:
-            inputs_near[bits[0]] = to_half(inputs_near[bits[0]], send)
-        sent.append(send)
+            inputs_near[bits[0]] = to_half(inputs_near[bits[0]], send[0])
+        sent.append(send[0])
         slots.append((first, second))
         labels.append(m)
         last = n == len(masks) - 1
         if last:
             totals = products(place, slots, labels, 1, totals)
-        slots.append((from_mask(send, swap * others, 0),))
+        slots.append(tuple(from_mask(a, swap * others, 0) for a in send))
         labels.append(m ^ swap)
         totals = products(place, slots, labels, 1 if last else 2, totals)
         known.append(totals)

time: 218 us -> 202 us (0.927)
  waiting for transfers between devices: 96.4 us -> 86.1 us
  local copies, waits for them, and re-layouts: 7.55 us -> 1.94 us
  starting transfers between devices: 24.4 us -> 28.4 us
  Pallas kernels: 81.5 us -> 77.7 us
    ppermute x22 -> x26, waiting for transfers between devices: 90 us -> 77.1 us  [from_mask(): return lax.ppermute(value, ('dp', 'tensor'), pairs)]
    ppermute x22 -> x26, starting transfers between devices: 18.7 us -> 25.7 us  [from_mask(): return lax.ppermute(value, ('dp', 'tensor'), pairs)]
    pallas_call x17, Pallas kernels: 81.5 us -> 77.7 us  [call(): pl.pallas_call(body, grid_spec=pltpu.PrefetchScalarGridSpec(num_scalar_pr...]
    dynamic_slice x2 -> x0, local copies, waits for them, and re-layouts: 3.3 us -> none  [the longest x1 2.26 us: on_device(): own_half = lax.dynamic_slice_in_dim(inputs, near * half_rows, half_rows, 0)]
    ppermute x3, starting transfers between devices: 5.69 us -> 2.75 us  [from_partner(): return lax.ppermute(value, axis, pairs)]
    ppermute x3, waiting for transfers between devices: 6.42 us -> 9.03 us  [from_partner(): return lax.ppermute(value, axis, pairs)]
    unnamed x40 -> x46, local copies, waits for them, and re-layouts: 3.67 us -> 1.27 us
  transfers between devices with their start and end apart: 25 -> 29, of which waited for: 14 -> 15; matrix products, arithmetic and copies ran while one was open for 2% -> 0% of each run, Pallas kernels for 27% -> 27%
where the time goes in v8:
time: 202 us
  waiting for transfers between devices  86.1 us (43%)
  Pallas kernels  77.7 us (38%)
  starting transfers between devices  28.4 us (14%)
  blocking collectives  5.67 us (3%)
    pallas_call x17, Pallas kernels, call(): pl.pallas_call(body, grid_spec=pltpu.PrefetchScalarGridSpec(num_scalar_pr...  77.7 us
    ppermute x26, waiting for transfers between devices, from_mask(): return lax.ppermute(value, ('dp', 'tensor'), pairs)  77.1 us
    ppermute x26, starting transfers between devices, from_mask(): return lax.ppermute(value, ('dp', 'tensor'), pairs)  25.7 us
    ppermute x3, waiting for transfers between devices, from_partner(): return lax.ppermute(value, axis, pairs)  9.03 us
    psum x1, blocking collectives, group_total(): summed = lax.psum(values, 'tensor')  5.67 us
  transfers between devices with their start and end apart: 29, of which 15 were waited for; matrix products, arithmetic and copies ran while one was open for 0% of the time, Pallas kernels for 27%

profile of v8, /device:TPU:0, one launch (start us, length us, event | category | flops | bytes accessed | tf_op | source)
XLA Modules:
  0.0 201.8 jit_solution(9516653113153307394)
XLA Ops:
  1.4 11.0 %forward.1 = (f32[352,1280]{1,0:T(8,128)}, bf16[352,1280]{1,0:T(8,128)(2,1)}, bf16[352,1280]{1,0:T(8,128)(2,1)}, bf16[176,1280]{1,0:T(8,128)(2,1)}) custom-call(s32[7]{0:T(128)} %stack.31.place_ref, bf16[704,1280]{1,0:T(8,128)(2,1)} %refs_2_.3, bf16[1280,1280]{1,0:T(8,128)(2,1)} %refs_5_.5, bf16[1280,1280]{1,0:T(8,128)(2,1)} %refs_6_.3), custom_call_target="tpu_custom_call" | custom-call | flops 1 | bytes 1 | tf_op jit(solution)/shard_map/forward/pallas_call | solution.py:81
  12.8 2.6 %collective-permute-start.1 = (bf16[352,1280]{1,0:T(8,128)(2,1)}, bf16[352,1280]{1,0:T(8,128)(2,1)S(1)}, u32[]{:S(2)}, u32[]{:S(2)}) collective-permute-start(bf16[352,1280]{1,0:T(8,128)(2,1)} %get-tuple-element.34), channel_id=1, source_target_pairs={{0,4},{1,5},{2,6},{3,7},{4,0},{5,1},{6,2},{7,3},{8,12},{9,13},{10,... | collective-permute-start | bytes 2703368 | tf_op jit(solution)/shard_map/ppermute | solution.py:27
  16.6 2.7 %product.1.refs_0_.refs_2_ = f32[352,1280]{1,0:T(8,128)S(1)} custom-call(s32[7]{0:T(128)S(1)} %copy-done.21, bf16[352,1280]{1,0:T(8,128)(2,1)S(1)} %copy-done.20, bf16[1280,1280]{1,0:T(8,128)(2,1)S(1)} %copy-done), custom_call_target="tpu_custom_call" | custom-call | flops 1 | bytes 1 | tf_op jit(solution)/shard_map/product/pallas_call | solution.py:81
  19.6 1.6 collective-permute-start.3
  21.1 2.6 %collective-permute-start = (bf16[176,1280]{1,0:T(8,128)(2,1)S(1)}, bf16[176,1280]{1,0:T(8,128)(2,1)S(1)}, u32[]{:S(2)}, u32[]{:S(2)}) collective-permute-start(bf16[176,1280]{1,0:T(8,128)(2,1)S(1)} %copy-done.22), channel_id=1, source_target_pairs={{0,16},{1,17},{2,18},{3,19},{4,20},{5,21},{6,22},{7,23},{8,24},{9,... | collective-permute-start | bytes 1351688 | tf_op jit(solution)/shard_map/ppermute | solution.py:27
  23.7 20.1 %collective-permute-done.refs_0_ = bf16[176,1280]{1,0:T(8,128)(2,1)S(1)} collective-permute-done((bf16[176,1280]{1,0:T(8,128)(2,1)S(1)}, bf16[176,1280]{1,0:T(8,128)(2,1)S(1)}, u32[]{:S(2)}, u32[]{:S(2)}) %collective-permute-start) | collective-permute-done | bytes 450592 | tf_op jit(solution)/shard_map/ppermute | solution.py:27
  45.6 10.2 %collective-permute-done.4.refs_1_ = bf16[176,1280]{1,0:T(8,128)(2,1)S(1)} collective-permute-done((bf16[176,1280]{1,0:T(8,128)(2,1)S(1)}, bf16[176,1280]{1,0:T(8,128)(2,1)S(1)}, u32[]{:S(2)}, u32[]{:S(2)}) %collective-permute-start.4) | collective-permute-done | bytes 450592 | tf_op jit(solution)/shard_map/ppermute | solution.py:27
  58.8 10.4 %gradient.4 = (f32[160,1280]{1,0:T(8,128)S(1)}, f32[160,1280]{1,0:T(8,128)S(1)}, bf16[160,1280]{1,0:T(8,128)(2,1)S(1)}, bf16[160,1280]{1,0:T(8,128)(2,1)S(1)}) custom-call(s32[7]{0:T(128)S(1)} %copy-done.21, bf16[352,1280]{1,0:T(8,128)(2,1)S(1)} %join.3.refs_0_, bf16[352,1280]{1,0:T(8,128)(2,1)S(1)} %collective-permute-done.5.refs_1_, ...), custom_call_target="tpu_custom_call" | custom-call | flops 1 | bytes 1 | tf_op jit(solution)/shard_map/gradient/pallas_call | solution.py:81
  69.3 3.9 %collective-permute-start.6 = (bf16[160,1280]{1,0:T(8,128)(2,1)S(1)}, bf16[160,1280]{1,0:T(8,128)(2,1)S(1)}, u32[]{:S(2)}, u32[]{:S(2)}) collective-permute-start(bf16[160,1280]{1,0:T(8,128)(2,1)S(1)} %get-tuple-element.41), channel_id=1, source_target_pairs={{0,8},{1,9},{2,10},{3,11},{4,12},{5,13},{6,14},{7,15},{8,0},{9,1},... | collective-permute-start | bytes 1228808 | tf_op jit(solution)/shard_map/ppermute | solution.py:27
  73.2 7.4 %collective-permute-done.10.refs_0_ = bf16[176,1280]{1,0:T(8,128)(2,1)S(1)} collective-permute-done((bf16[176,1280]{1,0:T(8,128)(2,1)S(1)}, bf16[176,1280]{1,0:T(8,128)(2,1)S(1)}, u32[]{:S(2)}, u32[]{:S(2)}) %collective-permute-start.10) | collective-permute-done | bytes 450592 | tf_op jit(solution)/shard_map/ppermute | solution.py:27
  80.7 8.7 %collective-permute-done.6.refs_2_.refs_3_ = bf16[160,1280]{1,0:T(8,128)(2,1)S(1)} collective-permute-done((bf16[160,1280]{1,0:T(8,128)(2,1)S(1)}, bf16[160,1280]{1,0:T(8,128)(2,1)S(1)}, u32[]{:S(2)}, u32[]{:S(2)}) %collective-permute-start.6) | collective-permute-done | bytes 409632 | tf_op jit(solution)/shard_map/ppermute | solution.py:27
  91.8 10.6 %gradient.5 = (f32[160,1280]{1,0:T(8,128)S(1)}, f32[160,1280]{1,0:T(8,128)S(1)}, bf16[160,1280]{1,0:T(8,128)(2,1)S(1)}, bf16[160,1280]{1,0:T(8,128)(2,1)S(1)}) custom-call(s32[7]{0:T(128)S(1)} %copy-done.21, bf16[352,1280]{1,0:T(8,128)(2,1)S(1)} %collective-permute-done.8.refs_0_, bf16[352,1280]{1,0:T(8,128)(2,1)S(1)} %collective-permute-done.11.refs_1_, ...), custom_call_target="tpu_custom_call" | custom-call | flops 1 | bytes 1 | tf_op jit(solution)/shard_map/gradient/pallas_call | solution.py:81
  103.4 8.4 %collective-permute-done.16.refs_3_ = bf16[352,1280]{1,0:T(8,128)(2,1)S(1)} collective-permute-done((bf16[352,1280]{1,0:T(8,128)(2,1)S(1)}, bf16[352,1280]{1,0:T(8,128)(2,1)S(1)}, u32[]{:S(2)}, u32[]{:S(2)}) %collective-permute-start.16) | collective-permute-done | bytes 901152 | tf_op jit(solution)/shard_map/ppermute | solution.py:27
  111.9 1.6 collective-permute-start.21
  113.5 2.0 %collective-permute-start.14 = (bf16[160,1280]{1,0:T(8,128)(2,1)S(1)}, bf16[160,1280]{1,0:T(8,128)(2,1)S(1)}, u32[]{:S(2)}, u32[]{:S(2)}) collective-permute-start(bf16[160,1280]{1,0:T(8,128)(2,1)S(1)} %get-tuple-element.49), channel_id=1, source_target_pairs={{0,8},{1,9},{2,10},{3,11},{4,12},{5,13},{6,14},{7,15},{8,0},{9,1},... | collective-permute-start | bytes 1228808 | tf_op jit(solution)/shard_map/ppermute | solution.py:27
  117.0 10.4 %gradient.6 = (f32[160,1280]{1,0:T(8,128)S(1)}, f32[160,1280]{1,0:T(8,128)S(1)}, bf16[160,1280]{1,0:T(8,128)(2,1)S(1)}, bf16[160,1280]{1,0:T(8,128)(2,1)S(1)}) custom-call(s32[7]{0:T(128)S(1)} %copy-done.21, f32[8,128]{1,0:T(8,128)S(1)} %products.5.refs_0_.refs_8_, bf16[352,1280]{1,0:T(8,128)(2,1)S(1)} %join.5.refs_1_, ...), custom_call_target="tpu_custom_call" | custom-call | flops 1 | bytes 1 | tf_op jit(solution)/shard_map/gradient/pallas_call | solution.py:81
  127.5 6.9 %collective-permute-done.21.refs_1_ = bf16[352,1280]{1,0:T(8,128)(2,1)S(1)} collective-permute-done((bf16[352,1280]{1,0:T(8,128)(2,1)S(1)}, bf16[352,1280]{1,0:T(8,128)(2,1)S(1)}, u32[]{:S(2)}, u32[]{:S(2)}) %collective-permute-start.21) | collective-permute-done | bytes 901152 | tf_op jit(solution)/shard_map/ppermute | solution.py:27
  134.9 2.0 %collective-permute-start.20 = (bf16[160,1280]{1,0:T(8,128)(2,1)S(1)}, bf16[160,1280]{1,0:T(8,128)(2,1)S(1)}, u32[]{:S(2)}, u32[]{:S(2)}) collective-permute-start(bf16[160,1280]{1,0:T(8,128)(2,1)S(1)} %get-tuple-element.56), channel_id=1, source_target_pairs={{0,8},{1,9},{2,10},{3,11},{4,12},{5,13},{6,14},{7,15},{8,0},{9,1},... | collective-permute-start | bytes 1228808 | tf_op jit(solution)/shard_map/ppermute | solution.py:27
  137.0 2.4 %products.6.refs_0_.refs_12_ = f32[8,128]{1,0:T(8,128)S(1)} custom-call(s32[7]{0:T(128)S(1)} %copy-done.21, f32[160,1280]{1,0:T(8,128)S(1)} %get-tuple-element.39.refs_0_.refs_1_, f32[160,1280]{1,0:T(8,128)S(1)} %get-tuple-element.40.refs_1_.refs_2_, bf16[160,1280]{1,0:T(8,128)(2,1)S(1)} %collective-permute-done.6.refs_2_.refs_3_, ...), custom_call_target="tpu_custom_call" | custom-call | flops 1 | bytes 1 | tf_op jit(solution)/shard_map/products/pallas_call | solution.py:81
  139.4 10.7 %gradient.7 = (f32[160,1280]{1,0:T(8,128)S(1)}, f32[160,1280]{1,0:T(8,128)S(1)}, bf16[160,1280]{1,0:T(8,128)(2,1)S(1)}, bf16[160,1280]{1,0:T(8,128)(2,1)S(1)}) custom-call(s32[7]{0:T(128)S(1)} %copy-done.21, f32[8,128]{1,0:T(8,128)S(1)} %products.6.refs_0_.refs_12_, bf16[352,1280]{1,0:T(8,128)(2,1)S(1)} %collective-permute-done.21.refs_1_, ...), custom_call_target="tpu_custom_call" | custom-call | flops 1 | bytes 1 | tf_op jit(solution)/shard_map/gradient/pallas_call | solution.py:81
  150.2 2.0 collective-permute-start.25
  152.2 3.8 %collective-permute-done.20.refs_11_.refs_12_ = bf16[160,1280]{1,0:T(8,128)(2,1)S(1)} collective-permute-done((bf16[160,1280]{1,0:T(8,128)(2,1)S(1)}, bf16[160,1280]{1,0:T(8,128)(2,1)S(1)}, u32[]{:S(2)}, u32[]{:S(2)}) %collective-permute-start.20) | collective-permute-done | bytes 409632 | tf_op jit(solution)/shard_map/ppermute | solution.py:27
  156.0 3.4 %products.7.refs_14_ = f32[8,128]{1,0:T(8,128)S(1)} custom-call(s32[7]{0:T(128)S(1)} %copy-done.21, f32[160,1280]{1,0:T(8,128)S(1)} %get-tuple-element.39.refs_0_.refs_1_, f32[160,1280]{1,0:T(8,128)S(1)} %get-tuple-element.40.refs_1_.refs_2_, bf16[160,1280]{1,0:T(8,128)(2,1)S(1)} %collective-permute-done.6.refs_2_.refs_3_, ...), custom_call_target="tpu_custom_call" | custom-call | flops 1 | bytes 1 | tf_op jit(solution)/shard_map/products/pallas_call | solution.py:81
  159.5 2.8 %products.8.refs_16_ = f32[8,128]{1,0:T(8,128)S(1)} custom-call(s32[7]{0:T(128)S(1)} %copy-done.21, f32[160,1280]{1,0:T(8,128)S(1)} %get-tuple-element.39.refs_0_.refs_1_, f32[160,1280]{1,0:T(8,128)S(1)} %get-tuple-element.40.refs_1_.refs_2_, bf16[160,1280]{1,0:T(8,128)(2,1)S(1)} %collective-permute-done.6.refs_2_.refs_3_, ...), custom_call_target="tpu_custom_call" | custom-call | flops 1 | bytes 1 | tf_op jit(solution)/shard_map/products/pallas_call | solution.py:81
  162.3 2.5 %collective-permute-done.24.refs_14_.refs_15_ = bf16[160,1280]{1,0:T(8,128)(2,1)S(1)} collective-permute-done((bf16[160,1280]{1,0:T(8,128)(2,1)S(1)}, bf16[160,1280]{1,0:T(8,128)(2,1)S(1)}, u32[]{:S(2)}, u32[]{:S(2)}) %collective-permute-start.24) | collective-permute-done | bytes 409632 | tf_op jit(solution)/shard_map/ppermute | solution.py:27
  164.8 7.9 %collective-permute-done.25.refs_15_.refs_16_ = bf16[160,1280]{1,0:T(8,128)(2,1)S(1)} collective-permute-done((bf16[160,1280]{1,0:T(8,128)(2,1)S(1)}, bf16[160,1280]{1,0:T(8,128)(2,1)S(1)}, u32[]{:S(2)}, u32[]{:S(2)}) %collective-permute-start.25) | collective-permute-done | bytes 409632 | tf_op jit(solution)/shard_map/ppermute | solution.py:27
  172.8 3.4 %products.9 = f32[8,128]{1,0:T(8,128)S(1)} custom-call(s32[7]{0:T(128)S(1)} %copy-done.21, f32[160,1280]{1,0:T(8,128)S(1)} %get-tuple-element.39.refs_0_.refs_1_, f32[160,1280]{1,0:T(8,128)S(1)} %get-tuple-element.40.refs_1_.refs_2_, bf16[160,1280]{1,0:T(8,128)(2,1)S(1)} %collective-permute-done.6.refs_2_.refs_3_, ...), custom_call_target="tpu_custom_call" | custom-call | flops 1 | bytes 1 | tf_op jit(solution)/shard_map/products/pallas_call | solution.py:81
  176.2 5.7 %psum.7 = f32[8,128]{1,0:T(8,128)S(1)} all-reduce(f32[8,128]{1,0:T(8,128)S(1)} %products.9), channel_id=1, replica_groups=mesh['dp'=8,'tensor'=4] {'tensor'}, use_global_device_ids=true, to_apply=%region_0.1 | all-reduce | flops 1024 | bytes 8192 | tf_op jit(solution)/shard_map/psum | solution.py:42
  182.9 3.6 %collective-permute-done.26 = f32[8,128]{1,0:T(8,128)S(1)} collective-permute-done((f32[8,128]{1,0:T(8,128)S(1)}, f32[8,128]{1,0:T(8,128)S(1)}, u32[]{:S(2)}, u32[]{:S(2)}) %collective-permute-start.26) | collective-permute-done | bytes 4128 | tf_op jit(solution)/shard_map/ppermute | solution.py:20
  186.8 3.3 %collective-permute-done.27 = f32[8,128]{1,0:T(8,128)S(1)} collective-permute-done((f32[8,128]{1,0:T(8,128)S(1)}, f32[8,128]{1,0:T(8,128)S(1)}, u32[]{:S(2)}, u32[]{:S(2)}) %collective-permute-start.27) | collective-permute-done | bytes 4128 | tf_op jit(solution)/shard_map/ppermute | solution.py:20
  191.6 2.1 %collective-permute-done.28 = f32[8,128]{1,0:T(8,128)S(1)} collective-permute-done((f32[8,128]{1,0:T(8,128)S(1)}, f32[8,128]{1,0:T(8,128)S(1)}, u32[]{:S(2)}, u32[]{:S(2)}) %collective-permute-start.28) | collective-permute-done | bytes 4128 | tf_op jit(solution)/shard_map/ppermute | solution.py:20
  194.3 7.3 %merge.1 = (f32[160,1280]{1,0:T(8,128)}, f32[160,1280]{1,0:T(8,128)}) custom-call(s32[7]{0:T(128)} %stack.31.place_ref, f32[8,128]{1,0:T(8,128)} %add.38.refs_0_, f32[160,1280]{1,0:T(8,128)} %copy-done.2, f32[160,1280]{1,0:T(8,128)} %copy-done.3, bf16[160,1280]{1,0:T(8,128)(2,1)} %copy-done.6, bf16[160,1280]{1,0:T(8,128)(2,1)} %copy-done.7, ...), custom_call_target="tpu_custom_call" | custom-call | flops 1 | bytes 1 | tf_op jit(solution)/shard_map/merge/pallas_call | solution.py:81
  (95 shorter events, 16.3 us)
Async XLA Ops:
  12.4 6.9 %collective-permute-start.2 = (f32[352,1280]{1,0:T(8,128)}, f32[352,1280]{1,0:T(8,128)S(1)}, u32[]{:S(2)}, u32[]{:S(2)}) collective-permute-start(f32[352,1280]{1,0:T(8,128)} %get-tuple-element.36), channel_id=1, source_target_pairs={{0,1},{1,0},{2,3},{3,2},{4,5},{5,4},{6,7},{7,6},{8,9},{9,8},{10,11... | collective-permute-start | bytes 5406728 | tf_op jit(solution)/shard_map/ppermute | solution.py:27
  12.8 31.0 %collective-permute-start.1 = (bf16[352,1280]{1,0:T(8,128)(2,1)}, bf16[352,1280]{1,0:T(8,128)(2,1)S(1)}, u32[]{:S(2)}, u32[]{:S(2)}) collective-permute-start(bf16[352,1280]{1,0:T(8,128)(2,1)} %get-tuple-element.34), channel_id=1, source_target_pairs={{0,4},{1,5},{2,6},{3,7},{4,0},{5,1},{6,2},{7,3},{8,12},{9,13},{10,... | collective-permute-start | bytes 2703368 | tf_op jit(solution)/shard_map/ppermute | solution.py:27
  19.6 24.3 %collective-permute-start.3 = (f32[176,1280]{1,0:T(8,128)S(1)}, f32[176,1280]{1,0:T(8,128)S(1)}, u32[]{:S(2)}, u32[]{:S(2)}) collective-permute-start(f32[176,1280]{1,0:T(8,128)S(1)} %get-tuple-element.38), channel_id=1, source_target_pairs={{0,2},{1,3},{2,0},{3,1},{4,6},{5,7},{6,4},{7,5},{8,10},{9,11},{10,... | collective-permute-start | bytes 2703368 | tf_op jit(solution)/shard_map/ppermute | solution.py:27
  21.1 22.7 %collective-permute-start = (bf16[176,1280]{1,0:T(8,128)(2,1)S(1)}, bf16[176,1280]{1,0:T(8,128)(2,1)S(1)}, u32[]{:S(2)}, u32[]{:S(2)}) collective-permute-start(bf16[176,1280]{1,0:T(8,128)(2,1)S(1)} %copy-done.22), channel_id=1, source_target_pairs={{0,16},{1,17},{2,18},{3,19},{4,20},{5,21},{6,22},{7,23},{8,24},{9,... | collective-permute-start | bytes 1351688 | tf_op jit(solution)/shard_map/ppermute | solution.py:27
  44.5 11.3 %collective-permute-start.4 = (bf16[176,1280]{1,0:T(8,128)(2,1)S(1)}, bf16[176,1280]{1,0:T(8,128)(2,1)S(1)}, u32[]{:S(2)}, u32[]{:S(2)}) collective-permute-start(bf16[176,1280]{1,0:T(8,128)(2,1)S(1)} %error_part.1.refs_0_), channel_id=1, source_target_pairs={{0,2},{1,3},{2,0},{3,1},{4,6},{5,7},{6,4},{7,5},{8,10},{9,11},{10,... | collective-permute-start | bytes 1351688 | tf_op jit(solution)/shard_map/ppermute | solution.py:27
  55.9 2.9 %collective-permute-start.5 = (bf16[352,1280]{1,0:T(8,128)(2,1)S(1)}, bf16[352,1280]{1,0:T(8,128)(2,1)S(1)}, u32[]{:S(2)}, u32[]{:S(2)}) collective-permute-start(bf16[352,1280]{1,0:T(8,128)(2,1)S(1)} %join.3.refs_0_), channel_id=1, source_target_pairs={{0,1},{1,0},{2,3},{3,2},{4,5},{5,4},{6,7},{7,6},{8,9},{9,8},{10,11... | collective-permute-start | bytes 2703368 | tf_op jit(solution)/shard_map/ppermute | solution.py:27
  56.0 24.7 %collective-permute-start.8 = (bf16[352,1280]{1,0:T(8,128)(2,1)S(1)}, bf16[352,1280]{1,0:T(8,128)(2,1)S(1)}, u32[]{:S(2)}, u32[]{:S(2)}) collective-permute-start(bf16[352,1280]{1,0:T(8,128)(2,1)S(1)} %join.3.refs_0_), channel_id=1, source_target_pairs={{0,4},{1,5},{2,6},{3,7},{4,0},{5,1},{6,2},{7,3},{8,12},{9,13},{10,... | collective-permute-start | bytes 2703368 | tf_op jit(solution)/shard_map/ppermute | solution.py:27
  56.6 16.6 %collective-permute-start.9 = (bf16[176,1280]{1,0:T(8,128)(2,1)S(1)}, bf16[176,1280]{1,0:T(8,128)(2,1)S(1)}, u32[]{:S(2)}, u32[]{:S(2)}) collective-permute-start(bf16[176,1280]{1,0:T(8,128)(2,1)S(1)} %collective-permute-done.refs_0_), channel_id=1, source_target_pairs={{0,2},{1,3},{2,0},{3,1},{4,6},{5,7},{6,4},{7,5},{8,10},{9,11},{10,... | collective-permute-start | bytes 1351688 | tf_op jit(solution)/shard_map/ppermute | solution.py:27
  57.9 22.8 %collective-permute-start.10 = (bf16[176,1280]{1,0:T(8,128)(2,1)S(1)}, bf16[176,1280]{1,0:T(8,128)(2,1)S(1)}, u32[]{:S(2)}, u32[]{:S(2)}) collective-permute-start(bf16[176,1280]{1,0:T(8,128)(2,1)S(1)} %error_part.1.refs_0_), channel_id=1, source_target_pairs={{0,16},{1,17},{2,18},{3,19},{4,20},{5,21},{6,22},{7,23},{8,24},{9,... | collective-permute-start | bytes 1351688 | tf_op jit(solution)/shard_map/ppermute | solution.py:27
  69.3 103.5 %copy-start.2 = (f32[160,1280]{1,0:T(8,128)}, f32[160,1280]{1,0:T(8,128)S(1)}, u32[]{:S(2)}) copy-start(f32[160,1280]{1,0:T(8,128)S(1)} %get-tuple-element.39.refs_0_.refs_1_) | copy-start | bytes 2457604
  69.3 103.5 %copy-start.3 = (f32[160,1280]{1,0:T(8,128)}, f32[160,1280]{1,0:T(8,128)S(1)}, u32[]{:S(2)}) copy-start(f32[160,1280]{1,0:T(8,128)S(1)} %get-tuple-element.40.refs_1_.refs_2_) | copy-start | bytes 2457604
  69.3 20.1 %collective-permute-start.6 = (bf16[160,1280]{1,0:T(8,128)(2,1)S(1)}, bf16[160,1280]{1,0:T(8,128)(2,1)S(1)}, u32[]{:S(2)}, u32[]{:S(2)}) collective-permute-start(bf16[160,1280]{1,0:T(8,128)(2,1)S(1)} %get-tuple-element.41), channel_id=1, source_target_pairs={{0,8},{1,9},{2,10},{3,11},{4,12},{5,13},{6,14},{7,15},{8,0},{9,1},... | collective-permute-start | bytes 1228808 | tf_op jit(solution)/shard_map/ppermute | solution.py:27
  73.2 18.4 %collective-permute-start.12 = (bf16[352,1280]{1,0:T(8,128)(2,1)S(1)}, bf16[352,1280]{1,0:T(8,128)(2,1)S(1)}, u32[]{:S(2)}, u32[]{:S(2)}) collective-permute-start(bf16[352,1280]{1,0:T(8,128)(2,1)S(1)} %collective-permute-done.1.refs_1_.refs_2_), channel_id=1, source_target_pairs={{0,1},{1,0},{2,3},{3,2},{4,5},{5,4},{6,7},{7,6},{8,9},{9,8},{10,11... | collective-permute-start | bytes 2703368 | tf_op jit(solution)/shard_map/ppermute | solution.py:27
  89.4 83.4 %copy-start.6 = (bf16[160,1280]{1,0:T(8,128)(2,1)}, bf16[160,1280]{1,0:T(8,128)(2,1)S(1)}, u32[]{:S(2)}) copy-start(bf16[160,1280]{1,0:T(8,128)(2,1)S(1)} %collective-permute-done.6.refs_2_.refs_3_) | copy-start | bytes 1228804
  89.4 2.4 %collective-permute-start.11 = (bf16[352,1280]{1,0:T(8,128)(2,1)S(1)}, bf16[352,1280]{1,0:T(8,128)(2,1)S(1)}, u32[]{:S(2)}, u32[]{:S(2)}) collective-permute-start(bf16[352,1280]{1,0:T(8,128)(2,1)S(1)} %collective-permute-done.8.refs_0_), channel_id=1, source_target_pairs={{0,1},{1,0},{2,3},{3,2},{4,5},{5,4},{6,7},{7,6},{8,9},{9,8},{10,11... | collective-permute-start | bytes 2703368 | tf_op jit(solution)/shard_map/ppermute | solution.py:27
  89.4 22.4 %collective-permute-start.16 = (bf16[352,1280]{1,0:T(8,128)(2,1)S(1)}, bf16[352,1280]{1,0:T(8,128)(2,1)S(1)}, u32[]{:S(2)}, u32[]{:S(2)}) collective-permute-start(bf16[352,1280]{1,0:T(8,128)(2,1)S(1)} %join.4.refs_3_), channel_id=1, source_target_pairs={{0,4},{1,5},{2,6},{3,7},{4,0},{5,1},{6,2},{7,3},{8,12},{9,13},{10,... | collective-permute-start | bytes 2703368 | tf_op jit(solution)/shard_map/ppermute | solution.py:27
  90.9 12.5 %collective-permute-start.15 = (bf16[176,1280]{1,0:T(8,128)(2,1)S(1)}, bf16[176,1280]{1,0:T(8,128)(2,1)S(1)}, u32[]{:S(2)}, u32[]{:S(2)}) collective-permute-start(bf16[176,1280]{1,0:T(8,128)(2,1)S(1)} %collective-permute-done.10.refs_0_), channel_id=1, source_target_pairs={{0,2},{1,3},{2,0},{3,1},{4,6},{5,7},{6,4},{7,5},{8,10},{9,11},{10,... | collective-permute-start | bytes 1351688 | tf_op jit(solution)/shard_map/ppermute | solution.py:27
  91.6 11.3 %collective-permute-start.7 = (bf16[160,1280]{1,0:T(8,128)(2,1)S(1)}, bf16[160,1280]{1,0:T(8,128)(2,1)S(1)}, u32[]{:S(2)}, u32[]{:S(2)}) collective-permute-start(bf16[160,1280]{1,0:T(8,128)(2,1)S(1)} %get-tuple-element.42), channel_id=1, source_target_pairs={{0,8},{1,9},{2,10},{3,11},{4,12},{5,13},{6,14},{7,15},{8,0},{9,1},... | collective-permute-start | bytes 1228808 | tf_op jit(solution)/shard_map/ppermute | solution.py:27
  91.6 25.4 %collective-permute-start.18 = (bf16[352,1280]{1,0:T(8,128)(2,1)S(1)}, bf16[352,1280]{1,0:T(8,128)(2,1)S(1)}, u32[]{:S(2)}, u32[]{:S(2)}) collective-permute-start(bf16[352,1280]{1,0:T(8,128)(2,1)S(1)} %join.4.refs_3_), channel_id=1, source_target_pairs={{0,1},{1,0},{2,3},{3,2},{4,5},{5,4},{6,7},{7,6},{8,9},{9,8},{10,11... | collective-permute-start | bytes 2703368 | tf_op jit(solution)/shard_map/ppermute | solution.py:27
  111.8 5.2 %collective-permute-start.17 = (bf16[352,1280]{1,0:T(8,128)(2,1)S(1)}, bf16[352,1280]{1,0:T(8,128)(2,1)S(1)}, u32[]{:S(2)}, u32[]{:S(2)}) collective-permute-start(bf16[352,1280]{1,0:T(8,128)(2,1)S(1)} %join.5.refs_1_), channel_id=1, source_target_pairs={{0,1},{1,0},{2,3},{3,2},{4,5},{5,4},{6,7},{7,6},{8,9},{9,8},{10,11... | collective-permute-start | bytes 2703368 | tf_op jit(solution)/shard_map/ppermute | solution.py:27
  111.9 22.4 %collective-permute-start.21 = (bf16[352,1280]{1,0:T(8,128)(2,1)S(1)}, bf16[352,1280]{1,0:T(8,128)(2,1)S(1)}, u32[]{:S(2)}, u32[]{:S(2)}) collective-permute-start(bf16[352,1280]{1,0:T(8,128)(2,1)S(1)} %join.5.refs_1_), channel_id=1, source_target_pairs={{0,4},{1,5},{2,6},{3,7},{4,0},{5,1},{6,2},{7,3},{8,12},{9,13},{10,... | collective-permute-start | bytes 2703368 | tf_op jit(solution)/shard_map/ppermute | solution.py:27
  113.5 20.8 %collective-permute-start.13 = (bf16[160,1280]{1,0:T(8,128)(2,1)S(1)}, bf16[160,1280]{1,0:T(8,128)(2,1)S(1)}, u32[]{:S(2)}, u32[]{:S(2)}) collective-permute-start(bf16[160,1280]{1,0:T(8,128)(2,1)S(1)} %get-tuple-element.48), channel_id=1, source_target_pairs={{0,8},{1,9},{2,10},{3,11},{4,12},{5,13},{6,14},{7,15},{8,0},{9,1},... | collective-permute-start | bytes 1228808 | tf_op jit(solution)/shard_map/ppermute | solution.py:27
  113.5 20.8 %collective-permute-start.14 = (bf16[160,1280]{1,0:T(8,128)(2,1)S(1)}, bf16[160,1280]{1,0:T(8,128)(2,1)S(1)}, u32[]{:S(2)}, u32[]{:S(2)}) collective-permute-start(bf16[160,1280]{1,0:T(8,128)(2,1)S(1)} %get-tuple-element.49), channel_id=1, source_target_pairs={{0,8},{1,9},{2,10},{3,11},{4,12},{5,13},{6,14},{7,15},{8,0},{9,1},... | collective-permute-start | bytes 1228808 | tf_op jit(solution)/shard_map/ppermute | solution.py:27
  134.4 5.0 %collective-permute-start.22 = (bf16[352,1280]{1,0:T(8,128)(2,1)S(1)}, bf16[352,1280]{1,0:T(8,128)(2,1)S(1)}, u32[]{:S(2)}, u32[]{:S(2)}) collective-permute-start(bf16[352,1280]{1,0:T(8,128)(2,1)S(1)} %collective-permute-done.21.refs_1_), channel_id=1, source_target_pairs={{0,1},{1,0},{2,3},{3,2},{4,5},{5,4},{6,7},{7,6},{8,9},{9,8},{10,11... | collective-permute-start | bytes 2703368 | tf_op jit(solution)/shard_map/ppermute | solution.py:27
  134.4 5.0 %collective-permute-start.23 = (bf16[352,1280]{1,0:T(8,128)(2,1)S(1)}, bf16[352,1280]{1,0:T(8,128)(2,1)S(1)}, u32[]{:S(2)}, u32[]{:S(2)}) collective-permute-start(bf16[352,1280]{1,0:T(8,128)(2,1)S(1)} %collective-permute-done.16.refs_3_), channel_id=1, source_target_pairs={{0,1},{1,0},{2,3},{3,2},{4,5},{5,4},{6,7},{7,6},{8,9},{9,8},{10,11... | collective-permute-start | bytes 2703368 | tf_op jit(solution)/shard_map/ppermute | solution.py:27
  134.9 17.3 %collective-permute-start.19 = (bf16[160,1280]{1,0:T(8,128)(2,1)S(1)}, bf16[160,1280]{1,0:T(8,128)(2,1)S(1)}, u32[]{:S(2)}, u32[]{:S(2)}) collective-permute-start(bf16[160,1280]{1,0:T(8,128)(2,1)S(1)} %get-tuple-element.55), channel_id=1, source_target_pairs={{0,8},{1,9},{2,10},{3,11},{4,12},{5,13},{6,14},{7,15},{8,0},{9,1},... | collective-permute-start | bytes 1228808 | tf_op jit(solution)/shard_map/ppermute | solution.py:27
  134.9 21.1 %collective-permute-start.20 = (bf16[160,1280]{1,0:T(8,128)(2,1)S(1)}, bf16[160,1280]{1,0:T(8,128)(2,1)S(1)}, u32[]{:S(2)}, u32[]{:S(2)}) collective-permute-start(bf16[160,1280]{1,0:T(8,128)(2,1)S(1)} %get-tuple-element.56), channel_id=1, source_target_pairs={{0,8},{1,9},{2,10},{3,11},{4,12},{5,13},{6,14},{7,15},{8,0},{9,1},... | collective-permute-start | bytes 1228808 | tf_op jit(solution)/shard_map/ppermute | solution.py:27
  150.1 14.7 %collective-permute-start.24 = (bf16[160,1280]{1,0:T(8,128)(2,1)S(1)}, bf16[160,1280]{1,0:T(8,128)(2,1)S(1)}, u32[]{:S(2)}, u32[]{:S(2)}) collective-permute-start(bf16[160,1280]{1,0:T(8,128)(2,1)S(1)} %get-tuple-element.62), channel_id=1, source_target_pairs={{0,8},{1,9},{2,10},{3,11},{4,12},{5,13},{6,14},{7,15},{8,0},{9,1},... | collective-permute-start | bytes 1228808 | tf_op jit(solution)/shard_map/ppermute | solution.py:27
  150.2 22.5 %collective-permute-start.25 = (bf16[160,1280]{1,0:T(8,128)(2,1)S(1)}, bf16[160,1280]{1,0:T(8,128)(2,1)S(1)}, u32[]{:S(2)}, u32[]{:S(2)}) collective-permute-start(bf16[160,1280]{1,0:T(8,128)(2,1)S(1)} %get-tuple-element.63), channel_id=1, source_target_pairs={{0,8},{1,9},{2,10},{3,11},{4,12},{5,13},{6,14},{7,15},{8,0},{9,1},... | collective-permute-start | bytes 1228808 | tf_op jit(solution)/shard_map/ppermute | solution.py:27
  181.9 4.6 %collective-permute-start.26 = (f32[8,128]{1,0:T(8,128)S(1)}, f32[8,128]{1,0:T(8,128)S(1)}, u32[]{:S(2)}, u32[]{:S(2)}) collective-permute-start(f32[8,128]{1,0:T(8,128)S(1)} %psum.7), channel_id=1, source_target_pairs={{0,16},{4,20},{8,24},{12,28},{16,0},{20,4},{24,8},{28,12},{1,17},{... | collective-permute-start | bytes 12296 | tf_op jit(solution)/shard_map/ppermute | solution.py:20
  186.5 3.6 %collective-permute-start.27 = (f32[8,128]{1,0:T(8,128)S(1)}, f32[8,128]{1,0:T(8,128)S(1)}, u32[]{:S(2)}, u32[]{:S(2)}) collective-permute-start(f32[8,128]{1,0:T(8,128)S(1)} %add.36), channel_id=1, source_target_pairs={{0,8},{4,12},{8,0},{12,4},{16,24},{20,28},{24,16},{28,20},{1,9},{5... | collective-permute-start | bytes 12296 | tf_op jit(solution)/shard_map/ppermute | solution.py:20
  190.1 3.6 %collective-permute-start.28 = (f32[8,128]{1,0:T(8,128)S(1)}, f32[8,128]{1,0:T(8,128)S(1)}, u32[]{:S(2)}, u32[]{:S(2)}) collective-permute-start(f32[8,128]{1,0:T(8,128)S(1)} %add.37), channel_id=1, source_target_pairs={{0,4},{4,0},{8,12},{12,8},{16,20},{20,16},{24,28},{28,24},{1,5},{5... | collective-permute-start | bytes 12296 | tf_op jit(solution)/shard_map/ppermute | solution.py:20
  (20 other events, 560.5 us)

commit v9 on v8

--- a/solution.py
+++ b/solution.py
@@ -88,7 +88,7 @@
     )(operands[0], *after, *operands[1:])
 
 
-WINDOW, SHIFT, OTHER_SHIFT, MEMBER, NEAR, FAR, PART = range(7)
+WINDOW, SHIFT, OTHER_SHIFT, MEMBER, NEAR, FAR, PART, PIECE = range(8)
 
 
 def row_start(place_ref, block, where):
@@ -189,24 +189,23 @@
     )[0]
 
 
-def add_kernel(place_ref, own_send, got_send, own_keep, got_keep, send_ref, keep_ref):
-    send_ref[...] = own_send[...] + got_send[...]
-    keep_ref[...] = own_keep[...] + got_keep[...]
-
-
-def add_and_split(flag, own, got):
-    rows, depth = own.shape[0] // 2, own.shape[1]
-    sent = pl.BlockSpec((rows, depth), lambda n, s: (1 - s[0], 0))
-    kept = pl.BlockSpec((rows, depth), lambda n, s: (s[0], 0))
-    shape = jax.ShapeDtypeStruct((rows, depth), jnp.float32)
+def add_kernel(place_ref, own_ref, got_ref, sum_ref, rounded_ref):
+    total = own_ref[...] + got_ref[...].astype(jnp.float32)
+    sum_ref[...] = total
+    rounded_ref[...] = total.astype(jnp.bfloat16)
+
+
+def add_and_round(place, own, got):
+    shape = own.shape
+    spec = pl.BlockSpec((shape[0] // 2, shape[1]), lambda n, s: (n, 0))
     return call(
         add_kernel,
-        "add_and_split",
-        (flag.reshape(1), own, got, own, got),
-        [shape, shape],
-        grid=(1,),
-        in_specs=[sent, sent, kept, kept],
-        out_specs=[pl.BlockSpec((rows, depth), whole)] * 2,
+        "add_and_round",
+        (place, own, got),
+        [jax.ShapeDtypeStruct(shape, jnp.float32), jax.ShapeDtypeStruct(shape, jnp.bfloat16)],
+        grid=(2,),
+        in_specs=[spec, spec],
+        out_specs=[spec, spec],
     )
 
 
@@ -229,28 +228,33 @@
     )[0]
 
 
-def error_kernel(row_count, place_ref, own_ref, got_ref, targets_ref, error_ref):
-    out = own_ref[...] + got_ref[...]
+def error_kernel(row_count, place_ref, own_ref, got_ref, targets_ref, half_ref, part_ref):
+    out = own_ref[...] + got_ref[...].astype(jnp.float32)
     error = (out - targets_ref[...].astype(jnp.float32)) / row_count
-    error_ref[...] = error.astype(jnp.bfloat16)
-
-
-def error_part(place, own, got, targets, after):
+    half_ref[...] = error.astype(jnp.bfloat16)
+    rows = part_ref.shape[0]
+    part_ref[...] = half_ref[pl.ds(pl.multiple_of(place_ref[PIECE] * rows, 16), rows), :]
+
+
+def error_half(place, part_rows, own, got, targets, after):
     rows, depth = own.shape
     return call(
         functools.partial(error_kernel, targets.shape[0]),
-        "error_part",
+        "error_half",
         (place, own, got, targets),
-        [jax.ShapeDtypeStruct((rows, depth), jnp.bfloat16)],
+        [
+            jax.ShapeDtypeStruct((rows, depth), jnp.bfloat16),
+            jax.ShapeDtypeStruct((part_rows, depth), jnp.bfloat16),
+        ],
         after,
         grid=(1,),
         in_specs=[
             pl.BlockSpec((rows, depth), whole),
             pl.BlockSpec((rows, depth), whole),
-            pl.BlockSpec((rows, depth), lambda n, s: (s[PART], 0)),
-        ],
-        out_specs=[pl.BlockSpec((rows, depth), whole)],
-    )[0]
+            pl.BlockSpec((rows, depth), lambda n, s: (s[NEAR], 0)),
+        ],
+        out_specs=[pl.BlockSpec((rows, depth), whole), pl.BlockSpec((part_rows, depth), whole)],
+    )
 
 
 def gradient_kernel(wheres, window, own, step_rows, place_ref, *refs):
@@ -487,8 +491,27 @@
             near,
             1 - near,
             part_of(shard),
+            part_of(shard) - near * (shards // 2),
         ]
     ).astype(jnp.int32)
+
+    first_bit = bits[0]
+    send, hidden_near, own_half, own_part = forward(place, part_rows, inputs, w_in, w_out)
+    got = from_mask(send, 0, 1)
+    inputs_of = {
+        bit: from_mask(own_part if bit == first_bit else own_half, bit * others, 0) for bit in bits
+    }
+
+    summed = product(place, hidden_near, w_out)
+    for bit in range(1, shard_levels):
+        summed, rounded = add_and_round(place, summed, got)
+        got = from_mask(rounded, 0, 2**bit)
+    error, error_piece = error_half(
+        place, part_rows, summed, got, targets, tuple(inputs_of.values())
+    )
+    errors_of = {
+        bit: from_mask(error_piece if bit == first_bit else error, bit * others, 0) for bit in bits
+    }
 
     def to_half(piece, *before):
         for bit in reversed(range(1, shard_levels)):
@@ -496,60 +519,43 @@
             piece = join(shard >> bit & 1, piece, got)
         return piece
 
-    send, hidden_near, own_half, own_part = forward(place, part_rows, inputs, w_in, w_out)
-    got = from_mask(send, 0, 1)
-    inputs_near = {
-        bit: from_mask(own_part if bit == bits[0] else own_half, bit * others, 0) for bit in bits
-    }
-    summed = product(place, hidden_near, w_out)
-    for bit in range(1, shard_levels):
-        send, summed = add_and_split(shard >> bit & 1, summed, got)
-        got = from_mask(send, 0, 2**bit)
-    error = error_part(place, summed, got, targets, tuple(inputs_near.values()))
-
-    errors_near = {bit: from_mask(error, bit * others, 0) for bit in bits[:1]}
-    error = to_half(error)
-    errors_near.update({bit: from_mask(error, bit * others, 0) for bit in bits[1:]})
-    masks = [m for m in range(members) if not m & swap]
-    lowest = {m: m & -m for m in masks}
-
     def both_halves(half):
         return [(half, NEAR), (from_mask(half, 0, 1), FAR)]
 
     slots, labels, known, sent = [], [], [], []
     totals = jnp.zeros((8, 128), jnp.float32)
+    masks = [m for m in range(members) if not m & swap]
     for n, m in enumerate(masks):
         if n == 0:
             half = error
-        elif m not in errors_near:
-            half = from_mask(errors_near[m - lowest[m]], lowest[m] * others, 0)
-            half, inputs_near[m] = (ordered(a, sent[-1]) for a in (half, inputs_near[m]))
-            half = ordered(half, *slots[2 * n - 3])
-        elif m == bits[0]:
-            before = [sent[-1], *slots[1]]
+        elif not m & first_bit:
+            half = errors_of[m] = ordered(errors_of[m], sent[0], inputs_half, errors_of[first_bit])
+            half = ordered(half, slots[2 * n - 1][0])
+            other_inputs = inputs_of[m]
+        elif m == first_bit:
             for bit in bits[1:]:
-                ready = ordered(inputs_near[m], errors_near[bit])
-                inputs_near[m | bit] = from_mask(ready, bit * others, 0)
-                before.append(inputs_near[m | bit])
-            half = to_half(ordered(errors_near[m], sent[0]), *before)
-            errors_near[m] = half
+                ready = ordered(inputs_of[first_bit], errors_of[bit])
+                inputs_of[first_bit | bit] = from_mask(ready, bit * others, 0)
+                ready = ordered(errors_of[first_bit], errors_of[bit])
+                errors_of[first_bit | bit] = from_mask(ready, bit * others, 0)
+            before = [errors_of[first_bit | bit] for bit in bits[1:]]
+            half = to_half(ordered(errors_of[m], sent[0]), sent[-1], *slots[1], *before)
+            other_inputs = inputs_half
         else:
-            first_bit = bits[0]
-            half = ordered(errors_near[m], sent[0], inputs_near[first_bit], errors_near[first_bit])
-            errors_near[m] = half
-            half = ordered(half, slots[2 * n - 1][0])
+            other_inputs = to_half(ordered(inputs_of[m], sent[-1]))
+            half = to_half(ordered(errors_of[m], sent[-2]), sent[-1], *slots[2 * n - 3])
         first, second, *send = gradient(
             place,
             members,
             swap,
             both_halves(half),
-            both_halves(inputs_near[m]) if n else [(inputs, None)],
+            both_halves(other_inputs) if n else [(inputs, None)],
             w_in,
             w_out,
             known[-2:-1],
         )
-        if n == 0 and len(masks) > 1:
-            inputs_near[bits[0]] = to_half(inputs_near[bits[0]], send[0])
+        if n == 0:
+            inputs_half = to_half(inputs_of[first_bit], send[0])
         sent.append(send[0])
         slots.append((first, second))
         labels.append(m)

time: 202 us -> 196 us (0.970)
  waiting for transfers between devices: 86.1 us -> 78.1 us
    ppermute x26 -> x27, waiting for transfers between devices: 77.1 us -> 69.5 us  [from_mask(): return lax.ppermute(value, ('dp', 'tensor'), pairs)]
    pallas_call x17 -> x18, Pallas kernels: 77.7 us -> 78.9 us  [call(): pl.pallas_call(body, grid_spec=pltpu.PrefetchScalarGridSpec(num_scalar_pr...]
    ppermute x26 -> x27, starting transfers between devices: 25.7 us -> 25.8 us  [from_mask(): return lax.ppermute(value, ('dp', 'tensor'), pairs)]
  transfers between devices with their start and end apart: 29 -> 30, of which waited for: 15 -> 12; matrix products, arithmetic and copies ran while one was open for 0% -> 0% of each run, Pallas kernels for 27% -> 29%
where the time goes in v9:
time: 196 us; the launch traced here: 195 us
  Pallas kernels  78.9 us (40%)
  waiting for transfers between devices  78.1 us (40%)
  starting transfers between devices  28.9 us (15%)
  blocking collectives  5.67 us (3%)
    pallas_call x18, Pallas kernels, call(): pl.pallas_call(body, grid_spec=pltpu.PrefetchScalarGridSpec(num_scalar_pr...  78.9 us
    ppermute x27, waiting for transfers between devices, from_mask(): return lax.ppermute(value, ('dp', 'tensor'), pairs)  69.5 us
    ppermute x27, starting transfers between devices, from_mask(): return lax.ppermute(value, ('dp', 'tensor'), pairs)  25.8 us
    ppermute x3, waiting for transfers between devices, from_partner(): return lax.ppermute(value, axis, pairs)  8.62 us
    psum x1, blocking collectives, group_total(): summed = lax.psum(values, 'tensor')  5.67 us
  transfers between devices with their start and end apart: 30, of which 12 were waited for; matrix products, arithmetic and copies ran while one was open for 0% of the time, Pallas kernels for 29%

profile of v9, /device:TPU:0, one launch (start us, length us, event | category | flops | bytes accessed | tf_op | source)
XLA Modules:
  0.0 195.4 jit_solution(6497159774276549078)
XLA Ops:
  1.4 11.0 %forward.1 = (f32[352,1280]{1,0:T(8,128)}, bf16[352,1280]{1,0:T(8,128)(2,1)}, bf16[352,1280]{1,0:T(8,128)(2,1)}, bf16[176,1280]{1,0:T(8,128)(2,1)}) custom-call(s32[8]{0:T(128)} %stack.35.place_ref, bf16[704,1280]{1,0:T(8,128)(2,1)} %refs_2_.3, bf16[1280,1280]{1,0:T(8,128)(2,1)} %refs_5_.5, bf16[1280,1280]{1,0:T(8,128)(2,1)} %refs_6_.3), custom_call_target="tpu_custom_call" | custom-call | flops 1 | bytes 1 | tf_op jit(solution)/shard_map/forward/pallas_call | solution.py:81
  12.8 2.6 %collective-permute-start.1 = (bf16[352,1280]{1,0:T(8,128)(2,1)}, bf16[352,1280]{1,0:T(8,128)(2,1)S(1)}, u32[]{:S(2)}, u32[]{:S(2)}) collective-permute-start(bf16[352,1280]{1,0:T(8,128)(2,1)} %get-tuple-element.37), channel_id=1, source_target_pairs={{0,4},{1,5},{2,6},{3,7},{4,0},{5,1},{6,2},{7,3},{8,12},{9,13},{10,... | collective-permute-start | bytes 2703368 | tf_op jit(solution)/shard_map/ppermute | solution.py:27
  16.6 2.7 %product.1.refs_0_ = f32[352,1280]{1,0:T(8,128)S(1)} custom-call(s32[8]{0:T(128)S(1)} %copy-done.21, bf16[352,1280]{1,0:T(8,128)(2,1)S(1)} %copy-done.20, bf16[1280,1280]{1,0:T(8,128)(2,1)S(1)} %copy-done), custom_call_target="tpu_custom_call" | custom-call | flops 1 | bytes 1 | tf_op jit(solution)/shard_map/product/pallas_call | solution.py:81
  20.1 1.6 collective-permute-start.3
  21.7 2.6 %collective-permute-start = (bf16[176,1280]{1,0:T(8,128)(2,1)S(1)}, bf16[176,1280]{1,0:T(8,128)(2,1)S(1)}, u32[]{:S(2)}, u32[]{:S(2)}) collective-permute-start(bf16[176,1280]{1,0:T(8,128)(2,1)S(1)} %copy-done.22), channel_id=1, source_target_pairs={{0,16},{1,17},{2,18},{3,19},{4,20},{5,21},{6,22},{7,23},{8,24},{9,... | collective-permute-start | bytes 1351688 | tf_op jit(solution)/shard_map/ppermute | solution.py:27
  24.3 20.1 %collective-permute-done.refs_0_ = bf16[176,1280]{1,0:T(8,128)(2,1)S(1)} collective-permute-done((bf16[176,1280]{1,0:T(8,128)(2,1)S(1)}, bf16[176,1280]{1,0:T(8,128)(2,1)S(1)}, u32[]{:S(2)}, u32[]{:S(2)}) %collective-permute-start) | collective-permute-done | bytes 450592 | tf_op jit(solution)/shard_map/ppermute | solution.py:27
  46.8 1.4 collective-permute-start.9
  48.2 10.4 %gradient.4 = (f32[160,1280]{1,0:T(8,128)S(1)}, f32[160,1280]{1,0:T(8,128)S(1)}, bf16[160,1280]{1,0:T(8,128)(2,1)S(1)}, bf16[160,1280]{1,0:T(8,128)(2,1)S(1)}) custom-call(s32[8]{0:T(128)S(1)} %copy-done.21, bf16[352,1280]{1,0:T(8,128)(2,1)S(1)} %get-tuple-element.42.refs_0_, bf16[352,1280]{1,0:T(8,128)(2,1)S(1)} %collective-permute-done.4.refs_1_, ...), custom_call_target="tpu_custom_call" | custom-call | flops 1 | bytes 1 | tf_op jit(solution)/shard_map/gradient/pallas_call | solution.py:81
  58.6 2.7 %collective-permute-start.5 = (bf16[160,1280]{1,0:T(8,128)(2,1)S(1)}, bf16[160,1280]{1,0:T(8,128)(2,1)S(1)}, u32[]{:S(2)}, u32[]{:S(2)}) collective-permute-start(bf16[160,1280]{1,0:T(8,128)(2,1)S(1)} %get-tuple-element.45), channel_id=1, source_target_pairs={{0,8},{1,9},{2,10},{3,11},{4,12},{5,13},{6,14},{7,15},{8,0},{9,1},... | collective-permute-start | bytes 1228808 | tf_op jit(solution)/shard_map/ppermute | solution.py:27
  61.4 8.1 %collective-permute-done.9.refs_0_ = bf16[176,1280]{1,0:T(8,128)(2,1)S(1)} collective-permute-done((bf16[176,1280]{1,0:T(8,128)(2,1)S(1)}, bf16[176,1280]{1,0:T(8,128)(2,1)S(1)}, u32[]{:S(2)}, u32[]{:S(2)}) %collective-permute-start.9) | collective-permute-done | bytes 450592 | tf_op jit(solution)/shard_map/ppermute | solution.py:27
  69.6 8.7 %collective-permute-done.5.refs_2_.refs_3_ = bf16[160,1280]{1,0:T(8,128)(2,1)S(1)} collective-permute-done((bf16[160,1280]{1,0:T(8,128)(2,1)S(1)}, bf16[160,1280]{1,0:T(8,128)(2,1)S(1)}, u32[]{:S(2)}, u32[]{:S(2)}) %collective-permute-start.5) | collective-permute-done | bytes 409632 | tf_op jit(solution)/shard_map/ppermute | solution.py:27
  78.3 1.5 collective-permute-start.14
  79.8 1.5 collective-permute-start.15
  81.3 10.6 %gradient.5 = (f32[160,1280]{1,0:T(8,128)S(1)}, f32[160,1280]{1,0:T(8,128)S(1)}, bf16[160,1280]{1,0:T(8,128)(2,1)S(1)}, bf16[160,1280]{1,0:T(8,128)(2,1)S(1)}) custom-call(s32[8]{0:T(128)S(1)} %copy-done.21, bf16[352,1280]{1,0:T(8,128)(2,1)S(1)} %collective-permute-done.7.refs_0_, bf16[352,1280]{1,0:T(8,128)(2,1)S(1)} %collective-permute-done.10.refs_1_, ...), custom_call_target="tpu_custom_call" | custom-call | flops 1 | bytes 1 | tf_op jit(solution)/shard_map/gradient/pallas_call | solution.py:81
  94.0 1.4 products.5.refs_0_.refs_8_
  96.2 10.4 %gradient.6 = (f32[160,1280]{1,0:T(8,128)S(1)}, f32[160,1280]{1,0:T(8,128)S(1)}, bf16[160,1280]{1,0:T(8,128)(2,1)S(1)}, bf16[160,1280]{1,0:T(8,128)(2,1)S(1)}) custom-call(s32[8]{0:T(128)S(1)} %copy-done.21, f32[8,128]{1,0:T(8,128)S(1)} %products.5.refs_0_.refs_8_, bf16[352,1280]{1,0:T(8,128)(2,1)S(1)} %join.5.refs_1_, ...), custom_call_target="tpu_custom_call" | custom-call | flops 1 | bytes 1 | tf_op jit(solution)/shard_map/gradient/pallas_call | solution.py:81
  106.7 1.3 collective-permute-start.23
  110.1 10.4 %collective-permute-done.12.refs_6_.refs_7_ = bf16[160,1280]{1,0:T(8,128)(2,1)S(1)} collective-permute-done((bf16[160,1280]{1,0:T(8,128)(2,1)S(1)}, bf16[160,1280]{1,0:T(8,128)(2,1)S(1)}, u32[]{:S(2)}, u32[]{:S(2)}) %collective-permute-start.12) | collective-permute-done | bytes 409632 | tf_op jit(solution)/shard_map/ppermute | solution.py:27
  120.5 7.4 %collective-permute-done.13.refs_7_.refs_8_ = bf16[160,1280]{1,0:T(8,128)(2,1)S(1)} collective-permute-done((bf16[160,1280]{1,0:T(8,128)(2,1)S(1)}, bf16[160,1280]{1,0:T(8,128)(2,1)S(1)}, u32[]{:S(2)}, u32[]{:S(2)}) %collective-permute-start.13) | collective-permute-done | bytes 409632 | tf_op jit(solution)/shard_map/ppermute | solution.py:27
  130.6 2.4 %products.6.refs_0_.refs_12_ = f32[8,128]{1,0:T(8,128)S(1)} custom-call(s32[8]{0:T(128)S(1)} %copy-done.21, f32[160,1280]{1,0:T(8,128)S(1)} %get-tuple-element.43.refs_0_.refs_1_, f32[160,1280]{1,0:T(8,128)S(1)} %get-tuple-element.44.refs_1_.refs_2_, bf16[160,1280]{1,0:T(8,128)(2,1)S(1)} %collective-permute-done.5.refs_2_.refs_3_, ...), custom_call_target="tpu_custom_call" | custom-call | flops 1 | bytes 1 | tf_op jit(solution)/shard_map/products/pallas_call | solution.py:81
  133.1 10.7 %gradient.7 = (f32[160,1280]{1,0:T(8,128)S(1)}, f32[160,1280]{1,0:T(8,128)S(1)}, bf16[160,1280]{1,0:T(8,128)(2,1)S(1)}, bf16[160,1280]{1,0:T(8,128)(2,1)S(1)}) custom-call(s32[8]{0:T(128)S(1)} %copy-done.21, f32[8,128]{1,0:T(8,128)S(1)} %products.6.refs_0_.refs_12_, bf16[352,1280]{1,0:T(8,128)(2,1)S(1)} %join.6.refs_1_, ...), custom_call_target="tpu_custom_call" | custom-call | flops 1 | bytes 1 | tf_op jit(solution)/shard_map/gradient/pallas_call | solution.py:81
  145.9 3.8 %collective-permute-done.19.refs_11_.refs_12_ = bf16[160,1280]{1,0:T(8,128)(2,1)S(1)} collective-permute-done((bf16[160,1280]{1,0:T(8,128)(2,1)S(1)}, bf16[160,1280]{1,0:T(8,128)(2,1)S(1)}, u32[]{:S(2)}, u32[]{:S(2)}) %collective-permute-start.19) | collective-permute-done | bytes 409632 | tf_op jit(solution)/shard_map/ppermute | solution.py:27
  149.7 3.4 %products.7.refs_14_ = f32[8,128]{1,0:T(8,128)S(1)} custom-call(s32[8]{0:T(128)S(1)} %copy-done.21, f32[160,1280]{1,0:T(8,128)S(1)} %get-tuple-element.43.refs_0_.refs_1_, f32[160,1280]{1,0:T(8,128)S(1)} %get-tuple-element.44.refs_1_.refs_2_, bf16[160,1280]{1,0:T(8,128)(2,1)S(1)} %collective-permute-done.5.refs_2_.refs_3_, ...), custom_call_target="tpu_custom_call" | custom-call | flops 1 | bytes 1 | tf_op jit(solution)/shard_map/products/pallas_call | solution.py:81
  153.2 2.8 %products.8.refs_16_ = f32[8,128]{1,0:T(8,128)S(1)} custom-call(s32[8]{0:T(128)S(1)} %copy-done.21, f32[160,1280]{1,0:T(8,128)S(1)} %get-tuple-element.43.refs_0_.refs_1_, f32[160,1280]{1,0:T(8,128)S(1)} %get-tuple-element.44.refs_1_.refs_2_, bf16[160,1280]{1,0:T(8,128)(2,1)S(1)} %collective-permute-done.5.refs_2_.refs_3_, ...), custom_call_target="tpu_custom_call" | custom-call | flops 1 | bytes 1 | tf_op jit(solution)/shard_map/products/pallas_call | solution.py:81
  156.0 2.5 %collective-permute-done.25.refs_14_.refs_15_ = bf16[160,1280]{1,0:T(8,128)(2,1)S(1)} collective-permute-done((bf16[160,1280]{1,0:T(8,128)(2,1)S(1)}, bf16[160,1280]{1,0:T(8,128)(2,1)S(1)}, u32[]{:S(2)}, u32[]{:S(2)}) %collective-permute-start.25) | collective-permute-done | bytes 409632 | tf_op jit(solution)/shard_map/ppermute | solution.py:27
  158.5 7.9 %collective-permute-done.26.refs_15_.refs_16_ = bf16[160,1280]{1,0:T(8,128)(2,1)S(1)} collective-permute-done((bf16[160,1280]{1,0:T(8,128)(2,1)S(1)}, bf16[160,1280]{1,0:T(8,128)(2,1)S(1)}, u32[]{:S(2)}, u32[]{:S(2)}) %collective-permute-start.26) | collective-permute-done | bytes 409632 | tf_op jit(solution)/shard_map/ppermute | solution.py:27
  166.5 3.4 %products.9 = f32[8,128]{1,0:T(8,128)S(1)} custom-call(s32[8]{0:T(128)S(1)} %copy-done.21, f32[160,1280]{1,0:T(8,128)S(1)} %get-tuple-element.43.refs_0_.refs_1_, f32[160,1280]{1,0:T(8,128)S(1)} %get-tuple-element.44.refs_1_.refs_2_, bf16[160,1280]{1,0:T(8,128)(2,1)S(1)} %collective-permute-done.5.refs_2_.refs_3_, ...), custom_call_target="tpu_custom_call" | custom-call | flops 1 | bytes 1 | tf_op jit(solution)/shard_map/products/pallas_call | solution.py:81
  169.9 5.7 %psum.7 = f32[8,128]{1,0:T(8,128)S(1)} all-reduce(f32[8,128]{1,0:T(8,128)S(1)} %products.9), channel_id=1, replica_groups=mesh['dp'=8,'tensor'=4] {'tensor'}, use_global_device_ids=true, to_apply=%region_0.1 | all-reduce | flops 1024 | bytes 8192 | tf_op jit(solution)/shard_map/psum | solution.py:42
  176.8 3.4 %collective-permute-done.27 = f32[8,128]{1,0:T(8,128)S(1)} collective-permute-done((f32[8,128]{1,0:T(8,128)S(1)}, f32[8,128]{1,0:T(8,128)S(1)}, u32[]{:S(2)}, u32[]{:S(2)}) %collective-permute-start.27) | collective-permute-done | bytes 4128 | tf_op jit(solution)/shard_map/ppermute | solution.py:20
  181.0 2.8 %collective-permute-done.28 = f32[8,128]{1,0:T(8,128)S(1)} collective-permute-done((f32[8,128]{1,0:T(8,128)S(1)}, f32[8,128]{1,0:T(8,128)S(1)}, u32[]{:S(2)}, u32[]{:S(2)}) %collective-permute-start.28) | collective-permute-done | bytes 4128 | tf_op jit(solution)/shard_map/ppermute | solution.py:20
  184.9 2.5 %collective-permute-done.29 = f32[8,128]{1,0:T(8,128)S(1)} collective-permute-done((f32[8,128]{1,0:T(8,128)S(1)}, f32[8,128]{1,0:T(8,128)S(1)}, u32[]{:S(2)}, u32[]{:S(2)}) %collective-permute-start.29) | collective-permute-done | bytes 4128 | tf_op jit(solution)/shard_map/ppermute | solution.py:20
  188.0 7.3 %merge.1 = (f32[160,1280]{1,0:T(8,128)}, f32[160,1280]{1,0:T(8,128)}) custom-call(s32[8]{0:T(128)} %stack.35.place_ref, f32[8,128]{1,0:T(8,128)} %add.39.refs_0_, f32[160,1280]{1,0:T(8,128)} %copy-done.2, f32[160,1280]{1,0:T(8,128)} %copy-done.3, bf16[160,1280]{1,0:T(8,128)(2,1)} %copy-done.6, bf16[160,1280]{1,0:T(8,128)(2,1)} %copy-done.7, ...), custom_call_target="tpu_custom_call" | custom-call | flops 1 | bytes 1 | tf_op jit(solution)/shard_map/merge/pallas_call | solution.py:81
  (98 shorter events, 19.1 us)
Async XLA Ops:
  12.4 7.0 %collective-permute-start.2 = (f32[352,1280]{1,0:T(8,128)}, f32[352,1280]{1,0:T(8,128)S(1)}, u32[]{:S(2)}, u32[]{:S(2)}) collective-permute-start(f32[352,1280]{1,0:T(8,128)} %get-tuple-element.39), channel_id=1, source_target_pairs={{0,1},{1,0},{2,3},{3,2},{4,5},{5,4},{6,7},{7,6},{8,9},{9,8},{10,11... | collective-permute-start | bytes 5406728 | tf_op jit(solution)/shard_map/ppermute | solution.py:27
  12.8 31.6 %collective-permute-start.1 = (bf16[352,1280]{1,0:T(8,128)(2,1)}, bf16[352,1280]{1,0:T(8,128)(2,1)S(1)}, u32[]{:S(2)}, u32[]{:S(2)}) collective-permute-start(bf16[352,1280]{1,0:T(8,128)(2,1)} %get-tuple-element.37), channel_id=1, source_target_pairs={{0,4},{1,5},{2,6},{3,7},{4,0},{5,1},{6,2},{7,3},{8,12},{9,13},{10,... | collective-permute-start | bytes 2703368 | tf_op jit(solution)/shard_map/ppermute | solution.py:27
  20.1 24.2 %collective-permute-start.3 = (bf16[352,1280]{1,0:T(8,128)(2,1)S(1)}, bf16[352,1280]{1,0:T(8,128)(2,1)S(1)}, u32[]{:S(2)}, u32[]{:S(2)}) collective-permute-start(bf16[352,1280]{1,0:T(8,128)(2,1)S(1)} %get-tuple-element.41), channel_id=1, source_target_pairs={{0,2},{1,3},{2,0},{3,1},{4,6},{5,7},{6,4},{7,5},{8,10},{9,11},{10,... | collective-permute-start | bytes 2703368 | tf_op jit(solution)/shard_map/ppermute | solution.py:27
  21.7 22.7 %collective-permute-start = (bf16[176,1280]{1,0:T(8,128)(2,1)S(1)}, bf16[176,1280]{1,0:T(8,128)(2,1)S(1)}, u32[]{:S(2)}, u32[]{:S(2)}) collective-permute-start(bf16[176,1280]{1,0:T(8,128)(2,1)S(1)} %copy-done.22), channel_id=1, source_target_pairs={{0,16},{1,17},{2,18},{3,19},{4,20},{5,21},{6,22},{7,23},{8,24},{9,... | collective-permute-start | bytes 1351688 | tf_op jit(solution)/shard_map/ppermute | solution.py:27
  45.6 2.6 %collective-permute-start.4 = (bf16[352,1280]{1,0:T(8,128)(2,1)S(1)}, bf16[352,1280]{1,0:T(8,128)(2,1)S(1)}, u32[]{:S(2)}, u32[]{:S(2)}) collective-permute-start(bf16[352,1280]{1,0:T(8,128)(2,1)S(1)} %get-tuple-element.42.refs_0_), channel_id=1, source_target_pairs={{0,1},{1,0},{2,3},{3,2},{4,5},{5,4},{6,7},{7,6},{8,9},{9,8},{10,11... | collective-permute-start | bytes 2703368 | tf_op jit(solution)/shard_map/ppermute | solution.py:27
  45.7 23.9 %collective-permute-start.7 = (bf16[352,1280]{1,0:T(8,128)(2,1)S(1)}, bf16[352,1280]{1,0:T(8,128)(2,1)S(1)}, u32[]{:S(2)}, u32[]{:S(2)}) collective-permute-start(bf16[352,1280]{1,0:T(8,128)(2,1)S(1)} %get-tuple-element.42.refs_0_), channel_id=1, source_target_pairs={{0,4},{1,5},{2,6},{3,7},{4,0},{5,1},{6,2},{7,3},{8,12},{9,13},{10,... | collective-permute-start | bytes 2703368 | tf_op jit(solution)/shard_map/ppermute | solution.py:27
  46.3 15.1 %collective-permute-start.8 = (bf16[176,1280]{1,0:T(8,128)(2,1)S(1)}, bf16[176,1280]{1,0:T(8,128)(2,1)S(1)}, u32[]{:S(2)}, u32[]{:S(2)}) collective-permute-start(bf16[176,1280]{1,0:T(8,128)(2,1)S(1)} %collective-permute-done.refs_0_), channel_id=1, source_target_pairs={{0,2},{1,3},{2,0},{3,1},{4,6},{5,7},{6,4},{7,5},{8,10},{9,11},{10,... | collective-permute-start | bytes 1351688 | tf_op jit(solution)/shard_map/ppermute | solution.py:27
  46.8 22.8 %collective-permute-start.9 = (bf16[176,1280]{1,0:T(8,128)(2,1)S(1)}, bf16[176,1280]{1,0:T(8,128)(2,1)S(1)}, u32[]{:S(2)}, u32[]{:S(2)}) collective-permute-start(bf16[176,1280]{1,0:T(8,128)(2,1)S(1)} %get-tuple-element.48), channel_id=1, source_target_pairs={{0,16},{1,17},{2,18},{3,19},{4,20},{5,21},{6,22},{7,23},{8,24},{9,... | collective-permute-start | bytes 1351688 | tf_op jit(solution)/shard_map/ppermute | solution.py:27
  58.6 107.8 %copy-start.2 = (f32[160,1280]{1,0:T(8,128)}, f32[160,1280]{1,0:T(8,128)S(1)}, u32[]{:S(2)}) copy-start(f32[160,1280]{1,0:T(8,128)S(1)} %get-tuple-element.43.refs_0_.refs_1_) | copy-start | bytes 2457604
  58.6 107.8 %copy-start.3 = (f32[160,1280]{1,0:T(8,128)}, f32[160,1280]{1,0:T(8,128)S(1)}, u32[]{:S(2)}) copy-start(f32[160,1280]{1,0:T(8,128)S(1)} %get-tuple-element.44.refs_1_.refs_2_) | copy-start | bytes 2457604
  58.6 19.6 %collective-permute-start.5 = (bf16[160,1280]{1,0:T(8,128)(2,1)S(1)}, bf16[160,1280]{1,0:T(8,128)(2,1)S(1)}, u32[]{:S(2)}, u32[]{:S(2)}) collective-permute-start(bf16[160,1280]{1,0:T(8,128)(2,1)S(1)} %get-tuple-element.45), channel_id=1, source_target_pairs={{0,8},{1,9},{2,10},{3,11},{4,12},{5,13},{6,14},{7,15},{8,0},{9,1},... | collective-permute-start | bytes 1228808 | tf_op jit(solution)/shard_map/ppermute | solution.py:27
  61.3 20.0 %collective-permute-start.11 = (bf16[352,1280]{1,0:T(8,128)(2,1)S(1)}, bf16[352,1280]{1,0:T(8,128)(2,1)S(1)}, u32[]{:S(2)}, u32[]{:S(2)}) collective-permute-start(bf16[352,1280]{1,0:T(8,128)(2,1)S(1)} %collective-permute-done.1.refs_1_.refs_2_), channel_id=1, source_target_pairs={{0,1},{1,0},{2,3},{3,2},{4,5},{5,4},{6,7},{7,6},{8,9},{9,8},{10,11... | collective-permute-start | bytes 2703368 | tf_op jit(solution)/shard_map/ppermute | solution.py:27
  78.2 3.1 %collective-permute-start.10 = (bf16[352,1280]{1,0:T(8,128)(2,1)S(1)}, bf16[352,1280]{1,0:T(8,128)(2,1)S(1)}, u32[]{:S(2)}, u32[]{:S(2)}) collective-permute-start(bf16[352,1280]{1,0:T(8,128)(2,1)S(1)} %collective-permute-done.7.refs_0_), channel_id=1, source_target_pairs={{0,1},{1,0},{2,3},{3,2},{4,5},{5,4},{6,7},{7,6},{8,9},{9,8},{10,11... | collective-permute-start | bytes 2703368 | tf_op jit(solution)/shard_map/ppermute | solution.py:27
  78.3 14.4 %collective-permute-start.14 = (bf16[176,1280]{1,0:T(8,128)(2,1)S(1)}, bf16[176,1280]{1,0:T(8,128)(2,1)S(1)}, u32[]{:S(2)}, u32[]{:S(2)}) collective-permute-start(bf16[176,1280]{1,0:T(8,128)(2,1)S(1)} %collective-permute-done.9.refs_0_), channel_id=1, source_target_pairs={{0,2},{1,3},{2,0},{3,1},{4,6},{5,7},{6,4},{7,5},{8,10},{9,11},{10,... | collective-permute-start | bytes 1351688 | tf_op jit(solution)/shard_map/ppermute | solution.py:27
  79.8 12.8 %collective-permute-start.15 = (bf16[176,1280]{1,0:T(8,128)(2,1)S(1)}, bf16[176,1280]{1,0:T(8,128)(2,1)S(1)}, u32[]{:S(2)}, u32[]{:S(2)}) collective-permute-start(bf16[176,1280]{1,0:T(8,128)(2,1)S(1)} %collective-permute-done.9.refs_0_), channel_id=1, source_target_pairs={{0,4},{1,5},{2,6},{3,7},{4,0},{5,1},{6,2},{7,3},{8,12},{9,13},{10,... | collective-permute-start | bytes 1351688 | tf_op jit(solution)/shard_map/ppermute | solution.py:27
  81.3 11.3 %collective-permute-start.6 = (bf16[160,1280]{1,0:T(8,128)(2,1)S(1)}, bf16[160,1280]{1,0:T(8,128)(2,1)S(1)}, u32[]{:S(2)}, u32[]{:S(2)}) collective-permute-start(bf16[160,1280]{1,0:T(8,128)(2,1)S(1)} %get-tuple-element.46), channel_id=1, source_target_pairs={{0,8},{1,9},{2,10},{3,11},{4,12},{5,13},{6,14},{7,15},{8,0},{9,1},... | collective-permute-start | bytes 1228808 | tf_op jit(solution)/shard_map/ppermute | solution.py:27
  81.3 14.9 %collective-permute-start.17 = (bf16[352,1280]{1,0:T(8,128)(2,1)S(1)}, bf16[352,1280]{1,0:T(8,128)(2,1)S(1)}, u32[]{:S(2)}, u32[]{:S(2)}) collective-permute-start(bf16[352,1280]{1,0:T(8,128)(2,1)S(1)} %join.4.refs_3_), channel_id=1, source_target_pairs={{0,1},{1,0},{2,3},{3,2},{4,5},{5,4},{6,7},{7,6},{8,9},{9,8},{10,11... | collective-permute-start | bytes 2703368 | tf_op jit(solution)/shard_map/ppermute | solution.py:27
  92.7 3.5 %collective-permute-start.16 = (bf16[352,1280]{1,0:T(8,128)(2,1)S(1)}, bf16[352,1280]{1,0:T(8,128)(2,1)S(1)}, u32[]{:S(2)}, u32[]{:S(2)}) collective-permute-start(bf16[352,1280]{1,0:T(8,128)(2,1)S(1)} %join.5.refs_1_), channel_id=1, source_target_pairs={{0,1},{1,0},{2,3},{3,2},{4,5},{5,4},{6,7},{7,6},{8,9},{9,8},{10,11... | collective-permute-start | bytes 2703368 | tf_op jit(solution)/shard_map/ppermute | solution.py:27
  92.8 13.9 %collective-permute-start.22 = (bf16[176,1280]{1,0:T(8,128)(2,1)S(1)}, bf16[176,1280]{1,0:T(8,128)(2,1)S(1)}, u32[]{:S(2)}, u32[]{:S(2)}) collective-permute-start(bf16[176,1280]{1,0:T(8,128)(2,1)S(1)} %collective-permute-done.refs_0_), channel_id=1, source_target_pairs={{0,4},{1,5},{2,6},{3,7},{4,0},{5,1},{6,2},{7,3},{8,12},{9,13},{10,... | collective-permute-start | bytes 1351688 | tf_op jit(solution)/shard_map/ppermute | solution.py:27
  95.4 32.4 %collective-permute-start.20 = (bf16[176,1280]{1,0:T(8,128)(2,1)S(1)}, bf16[176,1280]{1,0:T(8,128)(2,1)S(1)}, u32[]{:S(2)}, u32[]{:S(2)}) collective-permute-start(bf16[176,1280]{1,0:T(8,128)(2,1)S(1)} %collective-permute-done.15.refs_0_), channel_id=1, source_target_pairs={{0,2},{1,3},{2,0},{3,1},{4,6},{5,7},{6,4},{7,5},{8,10},{9,11},{10,... | collective-permute-start | bytes 1351688 | tf_op jit(solution)/shard_map/ppermute | solution.py:27
  106.7 21.2 %collective-permute-start.23 = (bf16[176,1280]{1,0:T(8,128)(2,1)S(1)}, bf16[176,1280]{1,0:T(8,128)(2,1)S(1)}, u32[]{:S(2)}, u32[]{:S(2)}) collective-permute-start(bf16[176,1280]{1,0:T(8,128)(2,1)S(1)} %collective-permute-done.22.refs_0_), channel_id=1, source_target_pairs={{0,2},{1,3},{2,0},{3,1},{4,6},{5,7},{6,4},{7,5},{8,10},{9,11},{10,... | collective-permute-start | bytes 1351688 | tf_op jit(solution)/shard_map/ppermute | solution.py:27
  108.1 12.4 %collective-permute-start.12 = (bf16[160,1280]{1,0:T(8,128)(2,1)S(1)}, bf16[160,1280]{1,0:T(8,128)(2,1)S(1)}, u32[]{:S(2)}, u32[]{:S(2)}) collective-permute-start(bf16[160,1280]{1,0:T(8,128)(2,1)S(1)} %get-tuple-element.53), channel_id=1, source_target_pairs={{0,8},{1,9},{2,10},{3,11},{4,12},{5,13},{6,14},{7,15},{8,0},{9,1},... | collective-permute-start | bytes 1228808 | tf_op jit(solution)/shard_map/ppermute | solution.py:27
  109.3 18.5 %collective-permute-start.13 = (bf16[160,1280]{1,0:T(8,128)(2,1)S(1)}, bf16[160,1280]{1,0:T(8,128)(2,1)S(1)}, u32[]{:S(2)}, u32[]{:S(2)}) collective-permute-start(bf16[160,1280]{1,0:T(8,128)(2,1)S(1)} %get-tuple-element.54), channel_id=1, source_target_pairs={{0,8},{1,9},{2,10},{3,11},{4,12},{5,13},{6,14},{7,15},{8,0},{9,1},... | collective-permute-start | bytes 1228808 | tf_op jit(solution)/shard_map/ppermute | solution.py:27
  127.9 5.2 %collective-permute-start.21 = (bf16[352,1280]{1,0:T(8,128)(2,1)S(1)}, bf16[352,1280]{1,0:T(8,128)(2,1)S(1)}, u32[]{:S(2)}, u32[]{:S(2)}) collective-permute-start(bf16[352,1280]{1,0:T(8,128)(2,1)S(1)} %join.6.refs_1_), channel_id=1, source_target_pairs={{0,1},{1,0},{2,3},{3,2},{4,5},{5,4},{6,7},{7,6},{8,9},{9,8},{10,11... | collective-permute-start | bytes 2703368 | tf_op jit(solution)/shard_map/ppermute | solution.py:27
  128.1 5.0 %collective-permute-start.24 = (bf16[352,1280]{1,0:T(8,128)(2,1)S(1)}, bf16[352,1280]{1,0:T(8,128)(2,1)S(1)}, u32[]{:S(2)}, u32[]{:S(2)}) collective-permute-start(bf16[352,1280]{1,0:T(8,128)(2,1)S(1)} %join.7.refs_3_), channel_id=1, source_target_pairs={{0,1},{1,0},{2,3},{3,2},{4,5},{5,4},{6,7},{7,6},{8,9},{9,8},{10,11... | collective-permute-start | bytes 2703368 | tf_op jit(solution)/shard_map/ppermute | solution.py:27
  128.6 17.3 %collective-permute-start.18 = (bf16[160,1280]{1,0:T(8,128)(2,1)S(1)}, bf16[160,1280]{1,0:T(8,128)(2,1)S(1)}, u32[]{:S(2)}, u32[]{:S(2)}) collective-permute-start(bf16[160,1280]{1,0:T(8,128)(2,1)S(1)} %get-tuple-element.60), channel_id=1, source_target_pairs={{0,8},{1,9},{2,10},{3,11},{4,12},{5,13},{6,14},{7,15},{8,0},{9,1},... | collective-permute-start | bytes 1228808 | tf_op jit(solution)/shard_map/ppermute | solution.py:27
  129.5 20.3 %collective-permute-start.19 = (bf16[160,1280]{1,0:T(8,128)(2,1)S(1)}, bf16[160,1280]{1,0:T(8,128)(2,1)S(1)}, u32[]{:S(2)}, u32[]{:S(2)}) collective-permute-start(bf16[160,1280]{1,0:T(8,128)(2,1)S(1)} %get-tuple-element.61), channel_id=1, source_target_pairs={{0,8},{1,9},{2,10},{3,11},{4,12},{5,13},{6,14},{7,15},{8,0},{9,1},... | collective-permute-start | bytes 1228808 | tf_op jit(solution)/shard_map/ppermute | solution.py:27
  143.8 14.7 %collective-permute-start.25 = (bf16[160,1280]{1,0:T(8,128)(2,1)S(1)}, bf16[160,1280]{1,0:T(8,128)(2,1)S(1)}, u32[]{:S(2)}, u32[]{:S(2)}) collective-permute-start(bf16[160,1280]{1,0:T(8,128)(2,1)S(1)} %get-tuple-element.68), channel_id=1, source_target_pairs={{0,8},{1,9},{2,10},{3,11},{4,12},{5,13},{6,14},{7,15},{8,0},{9,1},... | collective-permute-start | bytes 1228808 | tf_op jit(solution)/shard_map/ppermute | solution.py:27
  144.7 21.7 %collective-permute-start.26 = (bf16[160,1280]{1,0:T(8,128)(2,1)S(1)}, bf16[160,1280]{1,0:T(8,128)(2,1)S(1)}, u32[]{:S(2)}, u32[]{:S(2)}) collective-permute-start(bf16[160,1280]{1,0:T(8,128)(2,1)S(1)} %get-tuple-element.69), channel_id=1, source_target_pairs={{0,8},{1,9},{2,10},{3,11},{4,12},{5,13},{6,14},{7,15},{8,0},{9,1},... | collective-permute-start | bytes 1228808 | tf_op jit(solution)/shard_map/ppermute | solution.py:27
  175.6 4.6 %collective-permute-start.27 = (f32[8,128]{1,0:T(8,128)S(1)}, f32[8,128]{1,0:T(8,128)S(1)}, u32[]{:S(2)}, u32[]{:S(2)}) collective-permute-start(f32[8,128]{1,0:T(8,128)S(1)} %psum.7), channel_id=1, source_target_pairs={{0,16},{4,20},{8,24},{12,28},{16,0},{20,4},{24,8},{28,12},{1,17},{... | collective-permute-start | bytes 12296 | tf_op jit(solution)/shard_map/ppermute | solution.py:20
  180.2 3.6 %collective-permute-start.28 = (f32[8,128]{1,0:T(8,128)S(1)}, f32[8,128]{1,0:T(8,128)S(1)}, u32[]{:S(2)}, u32[]{:S(2)}) collective-permute-start(f32[8,128]{1,0:T(8,128)S(1)} %add.37), channel_id=1, source_target_pairs={{0,8},{4,12},{8,0},{12,4},{16,24},{20,28},{24,16},{28,20},{1,9},{5... | collective-permute-start | bytes 12296 | tf_op jit(solution)/shard_map/ppermute | solution.py:20
  183.8 3.6 %collective-permute-start.29 = (f32[8,128]{1,0:T(8,128)S(1)}, f32[8,128]{1,0:T(8,128)S(1)}, u32[]{:S(2)}, u32[]{:S(2)}) collective-permute-start(f32[8,128]{1,0:T(8,128)S(1)} %add.38), channel_id=1, source_target_pairs={{0,4},{4,0},{8,12},{12,8},{16,20},{20,16},{24,28},{28,24},{1,5},{5... | collective-permute-start | bytes 12296 | tf_op jit(solution)/shard_map/ppermute | solution.py:20
  (21 other events, 677.1 us)

commit v10 on v9

--- a/solution.py
+++ b/solution.py
@@ -189,26 +189,6 @@
     )[0]
 
 
-def add_kernel(place_ref, own_ref, got_ref, sum_ref, rounded_ref):
-    total = own_ref[...] + got_ref[...].astype(jnp.float32)
-    sum_ref[...] = total
-    rounded_ref[...] = total.astype(jnp.bfloat16)
-
-
-def add_and_round(place, own, got):
-    shape = own.shape
-    spec = pl.BlockSpec((shape[0] // 2, shape[1]), lambda n, s: (n, 0))
-    return call(
-        add_kernel,
-        "add_and_round",
-        (place, own, got),
-        [jax.ShapeDtypeStruct(shape, jnp.float32), jax.ShapeDtypeStruct(shape, jnp.bfloat16)],
-        grid=(2,),
-        in_specs=[spec, spec],
-        out_specs=[spec, spec],
-    )
-
-
 def join_kernel(place_ref, own_ref, got_ref, out_ref):
     rows = own_ref.shape[0]
     out_ref[pl.ds(pl.multiple_of(place_ref[0] * rows, 16), rows), :] = own_ref[...]
@@ -229,7 +209,7 @@
 
 
 def error_kernel(row_count, place_ref, own_ref, got_ref, targets_ref, half_ref, part_ref):
-    out = own_ref[...] + got_ref[...].astype(jnp.float32)
+    out = own_ref[...] + got_ref[...]
     error = (out - targets_ref[...].astype(jnp.float32)) / row_count
     half_ref[...] = error.astype(jnp.bfloat16)
     rows = part_ref.shape[0]
@@ -416,6 +396,24 @@
     return [items[0][i] for i in range(count)]
 
 
+def sum_kernel(place_ref, *refs):
+    refs[-1][...] = sum(ref[...] for ref in refs[:-1])
+
+
+def sum_of(place, parts):
+    shape = parts[0].shape
+    return call(
+        sum_kernel,
+        "sum_of",
+        (place, *parts),
+        [jax.ShapeDtypeStruct(shape, jnp.float32)],
+        vmem=4 * 2**20,
+        grid=(1,),
+        in_specs=[pl.BlockSpec(shape, whole)] * len(parts),
+        out_specs=[pl.BlockSpec(shape, whole)],
+    )[0]
+
+
 def merge_kernel(labels, place_ref, totals_ref, *refs):
     refs, (first_ref, second_ref, weights_ref) = refs[:-3], refs[-3:]
 
@@ -448,7 +446,7 @@
         "merge",
         (place, totals, *arrays),
         [shape, shape],
-        vmem=vmem_most,
+        vmem=16 * 2**20,
         grid=(own // block,),
         in_specs=[pl.BlockSpec(memory_space=pltpu.SMEM)] + [spec] * len(arrays),
         out_specs=[spec, spec],
@@ -498,16 +496,25 @@
     first_bit = bits[0]
     send, hidden_near, own_half, own_part = forward(place, part_rows, inputs, w_in, w_out)
     got = from_mask(send, 0, 1)
+
     inputs_of = {
         bit: from_mask(own_part if bit == first_bit else own_half, bit * others, 0) for bit in bits
     }
 
-    summed = product(place, hidden_near, w_out)
+    summed = product(place, hidden_near, w_out) + got
+    most = 24.0 * 0.15625 * 0.078125 * inputs.shape[1] * w_in.shape[1] * shards
+    scale = 2.0 ** math.ceil(math.log2(most / 65504.0))
+    sums = [summed]
     for bit in range(1, shard_levels):
-        summed, rounded = add_and_round(place, summed, got)
-        got = from_mask(rounded, 0, 2**bit)
+        rounded = (sum(sums) * (1.0 / scale)).astype(jnp.float16)
+        sums.append(from_mask(rounded, 0, 2**bit).astype(jnp.float32) * scale)
     error, error_piece = error_half(
-        place, part_rows, summed, got, targets, tuple(inputs_of.values())
+        place,
+        part_rows,
+        sum(sums[:-1]),
+        sums[-1],
+        targets,
+        tuple(inputs_of.values()),
     )
     errors_of = {
         bit: from_mask(error_piece if bit == first_bit else error, bit * others, 0) for bit in bits
@@ -530,7 +537,6 @@
             half = error
         elif not m & first_bit:
             half = errors_of[m] = ordered(errors_of[m], sent[0], inputs_half, errors_of[first_bit])
-            half = ordered(half, slots[2 * n - 1][0])
             other_inputs = inputs_of[m]
         elif m == first_bit:
             for bit in bits[1:]:
@@ -542,7 +548,7 @@
             half = to_half(ordered(errors_of[m], sent[0]), sent[-1], *slots[1], *before)
             other_inputs = inputs_half
         else:
-            other_inputs = to_half(ordered(inputs_of[m], sent[-1]))
+            other_inputs = to_half(ordered(inputs_of[m], sent[-1], slots[2 * n - 3][0]))
             half = to_half(ordered(errors_of[m], sent[-2]), sent[-1], *slots[2 * n - 3])
         first, second, *send = gradient(
             place,
@@ -567,7 +573,11 @@
         totals = products(place, slots, labels, 1 if last else 2, totals)
         known.append(totals)
 
-    totals = group_total(totals, gathered - 1, levels)
+    rounds = [[(0, mask) for mask in range(1, shards)]]
+    rounds.append([(m * others, 0) for m in range(2, members, 2)])
+    rounds.append([(others, 0)])
+    for partners in rounds:
+        totals = sum_of(place, [totals] + [from_mask(totals, *mask) for mask in partners])
     pieces = merge(place, totals, slots, labels)
 
     for section in range(gathered, levels):

time: 196 us -> 182 us (0.929)
  waiting for transfers between devices: 78.1 us -> 70.8 us
  blocking collectives: 5.67 us -> 0 us
  Pallas kernels: 78.9 us -> 76.5 us
  starting transfers between devices: 28.9 us -> 31.3 us
    ppermute x3 -> x0, waiting for transfers between devices: 8.62 us -> none  [from_partner(): return lax.ppermute(value, axis, pairs)]
    psum x1 -> x0, blocking collectives: 5.67 us -> none  [group_total(): summed = lax.psum(values, 'tensor')]
    ppermute x27 -> x34, starting transfers between devices: 25.8 us -> 31.3 us  [from_mask(): return lax.ppermute(value, ('dp', 'tensor'), pairs)]
    ppermute x3 -> x0, starting transfers between devices: 3.16 us -> none  [from_partner(): return lax.ppermute(value, axis, pairs)]
    pallas_call x18 -> x20, Pallas kernels: 78.9 us -> 76.5 us  [call(): pl.pallas_call(body, grid_spec=pltpu.PrefetchScalarGridSpec(num_scalar_pr...]
    ppermute x27 -> x34, waiting for transfers between devices: 69.5 us -> 70.8 us  [from_mask(): return lax.ppermute(value, ('dp', 'tensor'), pairs)]
  transfers between devices with their start and end apart: 30 -> 34, of which waited for: 12 -> 14; matrix products, arithmetic and copies ran while one was open for 0% -> 0% of each run, Pallas kernels for 29% -> 30%
where the time goes in v10:
time: 182 us
  Pallas kernels  76.5 us (42%)
  waiting for transfers between devices  70.8 us (39%)
  starting transfers between devices  31.3 us (17%)
  local copies, waits for them, and re-layouts  1.88 us (1%)
    pallas_call x20, Pallas kernels, call(): pl.pallas_call(body, grid_spec=pltpu.PrefetchScalarGridSpec(num_scalar_pr...  76.5 us
    ppermute x34, waiting for transfers between devices, from_mask(): return lax.ppermute(value, ('dp', 'tensor'), pairs)  70.8 us
    ppermute x34, starting transfers between devices, from_mask(): return lax.ppermute(value, ('dp', 'tensor'), pairs)  31.3 us
  transfers between devices with their start and end apart: 34, of which 14 were waited for; matrix products, arithmetic and copies ran while one was open for 0% of the time, Pallas kernels for 30%

profile of v10, /device:TPU:0, one launch (start us, length us, event | category | flops | bytes accessed | tf_op | source)
XLA Modules:
  0.0 181.8 jit_solution(5529554620493498016)
XLA Ops:
  1.4 11.0 %forward.1 = (f32[352,1280]{1,0:T(8,128)}, bf16[352,1280]{1,0:T(8,128)(2,1)}, bf16[352,1280]{1,0:T(8,128)(2,1)}, bf16[176,1280]{1,0:T(8,128)(2,1)}) custom-call(s32[8]{0:T(128)} %stack.35.place_ref, bf16[704,1280]{1,0:T(8,128)(2,1)} %refs_2_.3, bf16[1280,1280]{1,0:T(8,128)(2,1)} %refs_5_.5, bf16[1280,1280]{1,0:T(8,128)(2,1)} %refs_6_.3), custom_call_target="tpu_custom_call" | custom-call | flops 1 | bytes 1 | tf_op jit(solution)/shard_map/forward/pallas_call | solution.py:81
  14.0 2.7 %product.1 = f32[352,1280]{1,0:T(8,128)S(1)} custom-call(s32[8]{0:T(128)S(1)} %copy-done.5, bf16[352,1280]{1,0:T(8,128)(2,1)S(1)} %copy-done.4, bf16[1280,1280]{1,0:T(8,128)(2,1)S(1)} %copy-done), custom_call_target="tpu_custom_call" | custom-call | flops 1 | bytes 1 | tf_op jit(solution)/shard_map/product/pallas_call | solution.py:81
  17.0 2.6 %collective-permute-start.3 = (f16[352,1280]{1,0:T(8,128)(2,1)S(1)}, f16[352,1280]{1,0:T(8,128)(2,1)S(1)}, u32[]{:S(2)}, u32[]{:S(2)}) collective-permute-start(f16[352,1280]{1,0:T(8,128)(2,1)S(1)} %get-tuple-element.64), channel_id=1, source_target_pairs={{0,2},{1,3},{2,0},{3,1},{4,6},{5,7},{6,4},{7,5},{8,10},{9,11},{10,... | collective-permute-start | bytes 2703368 | tf_op jit(solution)/shard_map/ppermute | solution.py:27
  19.6 1.5 collective-permute-start.1
  21.2 2.6 %collective-permute-start = (bf16[176,1280]{1,0:T(8,128)(2,1)S(1)}, bf16[176,1280]{1,0:T(8,128)(2,1)S(1)}, u32[]{:S(2)}, u32[]{:S(2)}) collective-permute-start(bf16[176,1280]{1,0:T(8,128)(2,1)S(1)} %copy-done.7), channel_id=1, source_target_pairs={{0,16},{1,17},{2,18},{3,19},{4,20},{5,21},{6,22},{7,23},{8,24},{9,... | collective-permute-start | bytes 1351688 | tf_op jit(solution)/shard_map/ppermute | solution.py:27
  23.7 16.5 %collective-permute-done.3 = f16[352,1280]{1,0:T(8,128)(2,1)S(1)} collective-permute-done((f16[352,1280]{1,0:T(8,128)(2,1)S(1)}, f16[352,1280]{1,0:T(8,128)(2,1)S(1)}, u32[]{:S(2)}, u32[]{:S(2)}) %collective-permute-start.3) | collective-permute-done | bytes 901152 | tf_op jit(solution)/shard_map/ppermute | solution.py:27
  40.4 3.5 %collective-permute-done.refs_0_ = bf16[176,1280]{1,0:T(8,128)(2,1)S(1)} collective-permute-done((bf16[176,1280]{1,0:T(8,128)(2,1)S(1)}, bf16[176,1280]{1,0:T(8,128)(2,1)S(1)}, u32[]{:S(2)}, u32[]{:S(2)}) %collective-permute-start) | collective-permute-done | bytes 450592 | tf_op jit(solution)/shard_map/ppermute | solution.py:27
  48.2 10.4 %gradient.4 = (f32[160,1280]{1,0:T(8,128)S(1)}, f32[160,1280]{1,0:T(8,128)S(1)}, bf16[160,1280]{1,0:T(8,128)(2,1)S(1)}, bf16[160,1280]{1,0:T(8,128)(2,1)S(1)}) custom-call(s32[8]{0:T(128)S(1)} %copy-done.5, bf16[352,1280]{1,0:T(8,128)(2,1)S(1)} %get-tuple-element.37.refs_0_, bf16[352,1280]{1,0:T(8,128)(2,1)S(1)} %collective-permute-done.4.refs_1_, ...), custom_call_target="tpu_custom_call" | custom-call | flops 1 | bytes 1 | tf_op jit(solution)/shard_map/gradient/pallas_call | solution.py:81
  58.7 10.8 %collective-permute-done.9.refs_0_ = bf16[176,1280]{1,0:T(8,128)(2,1)S(1)} collective-permute-done((bf16[176,1280]{1,0:T(8,128)(2,1)S(1)}, bf16[176,1280]{1,0:T(8,128)(2,1)S(1)}, u32[]{:S(2)}, u32[]{:S(2)}) %collective-permute-start.9) | collective-permute-done | bytes 450592 | tf_op jit(solution)/shard_map/ppermute | solution.py:27
  70.4 1.5 collective-permute-start.15
  71.9 2.0 %collective-permute-start.6 = (bf16[160,1280]{1,0:T(8,128)(2,1)S(1)}, bf16[160,1280]{1,0:T(8,128)(2,1)S(1)}, u32[]{:S(2)}, u32[]{:S(2)}) collective-permute-start(bf16[160,1280]{1,0:T(8,128)(2,1)S(1)} %get-tuple-element.41), channel_id=1, source_target_pairs={{0,8},{1,9},{2,10},{3,11},{4,12},{5,13},{6,14},{7,15},{8,0},{9,1},... | collective-permute-start | bytes 1228808 | tf_op jit(solution)/shard_map/ppermute | solution.py:27
  73.9 10.6 %gradient.5 = (f32[160,1280]{1,0:T(8,128)S(1)}, f32[160,1280]{1,0:T(8,128)S(1)}, bf16[160,1280]{1,0:T(8,128)(2,1)S(1)}, bf16[160,1280]{1,0:T(8,128)(2,1)S(1)}) custom-call(s32[8]{0:T(128)S(1)} %copy-done.5, bf16[352,1280]{1,0:T(8,128)(2,1)S(1)} %collective-permute-done.7.refs_0_, bf16[352,1280]{1,0:T(8,128)(2,1)S(1)} %collective-permute-done.10.refs_1_, ...), custom_call_target="tpu_custom_call" | custom-call | flops 1 | bytes 1 | tf_op jit(solution)/shard_map/gradient/pallas_call | solution.py:81
  84.6 7.4 %collective-permute-done.6.refs_3_.refs_4_ = bf16[160,1280]{1,0:T(8,128)(2,1)S(1)} collective-permute-done((bf16[160,1280]{1,0:T(8,128)(2,1)S(1)}, bf16[160,1280]{1,0:T(8,128)(2,1)S(1)}, u32[]{:S(2)}, u32[]{:S(2)}) %collective-permute-start.6) | collective-permute-done | bytes 409632 | tf_op jit(solution)/shard_map/ppermute | solution.py:27
  95.6 10.5 %gradient.6 = (f32[160,1280]{1,0:T(8,128)S(1)}, f32[160,1280]{1,0:T(8,128)S(1)}, bf16[160,1280]{1,0:T(8,128)(2,1)S(1)}, bf16[160,1280]{1,0:T(8,128)(2,1)S(1)}) custom-call(s32[8]{0:T(128)S(1)} %copy-done.5, f32[8,128]{1,0:T(8,128)S(1)} %products.5.refs_0_.refs_8_, bf16[352,1280]{1,0:T(8,128)(2,1)S(1)} %join.5.refs_1_, ...), custom_call_target="tpu_custom_call" | custom-call | flops 1 | bytes 1 | tf_op jit(solution)/shard_map/gradient/pallas_call | solution.py:81
  107.1 1.7 collective-permute-start.13
  108.8 9.0 %collective-permute-done.13.refs_7_.refs_8_ = bf16[160,1280]{1,0:T(8,128)(2,1)S(1)} collective-permute-done((bf16[160,1280]{1,0:T(8,128)(2,1)S(1)}, bf16[160,1280]{1,0:T(8,128)(2,1)S(1)}, u32[]{:S(2)}, u32[]{:S(2)}) %collective-permute-start.13) | collective-permute-done | bytes 409632 | tf_op jit(solution)/shard_map/ppermute | solution.py:27
  118.7 1.7 collective-permute-start.18
  120.7 2.4 %products.6.refs_0_.refs_12_ = f32[8,128]{1,0:T(8,128)S(1)} custom-call(s32[8]{0:T(128)S(1)} %copy-done.5, f32[160,1280]{1,0:T(8,128)S(1)} %get-tuple-element.38.refs_0_.refs_1_, f32[160,1280]{1,0:T(8,128)S(1)} %get-tuple-element.39.refs_1_.refs_2_, bf16[160,1280]{1,0:T(8,128)(2,1)S(1)} %collective-permute-done.5.refs_2_.refs_3_, ...), custom_call_target="tpu_custom_call" | custom-call | flops 1 | bytes 1 | tf_op jit(solution)/shard_map/products/pallas_call | solution.py:81
  123.1 10.7 %gradient.7 = (f32[160,1280]{1,0:T(8,128)S(1)}, f32[160,1280]{1,0:T(8,128)S(1)}, bf16[160,1280]{1,0:T(8,128)(2,1)S(1)}, bf16[160,1280]{1,0:T(8,128)(2,1)S(1)}) custom-call(s32[8]{0:T(128)S(1)} %copy-done.5, f32[8,128]{1,0:T(8,128)S(1)} %products.6.refs_0_.refs_12_, bf16[352,1280]{1,0:T(8,128)(2,1)S(1)} %join.6.refs_1_, ...), custom_call_target="tpu_custom_call" | custom-call | flops 1 | bytes 1 | tf_op jit(solution)/shard_map/gradient/pallas_call | solution.py:81
  133.8 1.8 collective-permute-start.25
  135.9 3.8 %collective-permute-done.19.refs_11_.refs_12_ = bf16[160,1280]{1,0:T(8,128)(2,1)S(1)} collective-permute-done((bf16[160,1280]{1,0:T(8,128)(2,1)S(1)}, bf16[160,1280]{1,0:T(8,128)(2,1)S(1)}, u32[]{:S(2)}, u32[]{:S(2)}) %collective-permute-start.19) | collective-permute-done | bytes 409632 | tf_op jit(solution)/shard_map/ppermute | solution.py:27
  139.7 3.4 %products.7.refs_14_ = f32[8,128]{1,0:T(8,128)S(1)} custom-call(s32[8]{0:T(128)S(1)} %copy-done.5, f32[160,1280]{1,0:T(8,128)S(1)} %get-tuple-element.38.refs_0_.refs_1_, f32[160,1280]{1,0:T(8,128)S(1)} %get-tuple-element.39.refs_1_.refs_2_, bf16[160,1280]{1,0:T(8,128)(2,1)S(1)} %collective-permute-done.5.refs_2_.refs_3_, ...), custom_call_target="tpu_custom_call" | custom-call | flops 1 | bytes 1 | tf_op jit(solution)/shard_map/products/pallas_call | solution.py:81
  143.2 2.8 %products.8.refs_16_ = f32[8,128]{1,0:T(8,128)S(1)} custom-call(s32[8]{0:T(128)S(1)} %copy-done.5, f32[160,1280]{1,0:T(8,128)S(1)} %get-tuple-element.38.refs_0_.refs_1_, f32[160,1280]{1,0:T(8,128)S(1)} %get-tuple-element.39.refs_1_.refs_2_, bf16[160,1280]{1,0:T(8,128)(2,1)S(1)} %collective-permute-done.5.refs_2_.refs_3_, ...), custom_call_target="tpu_custom_call" | custom-call | flops 1 | bytes 1 | tf_op jit(solution)/shard_map/products/pallas_call | solution.py:81
  146.0 2.5 %collective-permute-done.25.refs_14_.refs_15_ = bf16[160,1280]{1,0:T(8,128)(2,1)S(1)} collective-permute-done((bf16[160,1280]{1,0:T(8,128)(2,1)S(1)}, bf16[160,1280]{1,0:T(8,128)(2,1)S(1)}, u32[]{:S(2)}, u32[]{:S(2)}) %collective-permute-start.25) | collective-permute-done | bytes 409632 | tf_op jit(solution)/shard_map/ppermute | solution.py:27
  148.5 7.9 %collective-permute-done.26.refs_15_.refs_16_ = bf16[160,1280]{1,0:T(8,128)(2,1)S(1)} collective-permute-done((bf16[160,1280]{1,0:T(8,128)(2,1)S(1)}, bf16[160,1280]{1,0:T(8,128)(2,1)S(1)}, u32[]{:S(2)}, u32[]{:S(2)}) %collective-permute-start.26) | collective-permute-done | bytes 409632 | tf_op jit(solution)/shard_map/ppermute | solution.py:27
  156.4 3.4 %products.9.refs_0_ = f32[8,128]{1,0:T(8,128)S(1)} custom-call(s32[8]{0:T(128)S(1)} %copy-done.5, f32[160,1280]{1,0:T(8,128)S(1)} %get-tuple-element.38.refs_0_.refs_1_, f32[160,1280]{1,0:T(8,128)S(1)} %get-tuple-element.39.refs_1_.refs_2_, bf16[160,1280]{1,0:T(8,128)(2,1)S(1)} %collective-permute-done.5.refs_2_.refs_3_, ...), custom_call_target="tpu_custom_call" | custom-call | flops 1 | bytes 1 | tf_op jit(solution)/shard_map/products/pallas_call | solution.py:81
  161.7 1.8 collective-permute-done.28.refs_2_
  164.5 1.8 collective-permute-start.30
  169.0 1.9 %collective-permute-done.31.refs_2_ = f32[8,128]{1,0:T(8,128)S(1)} collective-permute-done((f32[8,128]{1,0:T(8,128)S(1)}, f32[8,128]{1,0:T(8,128)S(1)}, u32[]{:S(2)}, u32[]{:S(2)}) %collective-permute-start.31) | collective-permute-done | bytes 4128 | tf_op jit(solution)/shard_map/ppermute | solution.py:27
  170.9 2.1 %collective-permute-done.32.refs_3_ = f32[8,128]{1,0:T(8,128)S(1)} collective-permute-done((f32[8,128]{1,0:T(8,128)S(1)}, f32[8,128]{1,0:T(8,128)S(1)}, u32[]{:S(2)}, u32[]{:S(2)}) %collective-permute-start.32) | collective-permute-done | bytes 4128 | tf_op jit(solution)/shard_map/ppermute | solution.py:27
  174.1 3.1 %collective-permute-done.33.refs_1_ = f32[8,128]{1,0:T(8,128)S(1)} collective-permute-done((f32[8,128]{1,0:T(8,128)S(1)}, f32[8,128]{1,0:T(8,128)S(1)}, u32[]{:S(2)}, u32[]{:S(2)}) %collective-permute-start.33) | collective-permute-done | bytes 4128 | tf_op jit(solution)/shard_map/ppermute | solution.py:27
  177.7 4.1 %merge.1 = (f32[160,1280]{1,0:T(8,128)}, f32[160,1280]{1,0:T(8,128)}) custom-call(s32[8]{0:T(128)S(1)} %copy-done.5, f32[8,128]{1,0:T(8,128)S(1)} %sum_of.5.refs_0_, f32[160,1280]{1,0:T(8,128)S(1)} %get-tuple-element.38.refs_0_.refs_1_, f32[160,1280]{1,0:T(8,128)S(1)} %get-tuple-element.39.refs_1_.refs_2_, ...), custom_call_target="tpu_custom_call" | custom-call | flops 1 | bytes 1 | tf_op jit(solution)/shard_map/merge/pallas_call | solution.py:81
  (76 shorter events, 21.2 us)
Async XLA Ops:
  12.4 4.4 %collective-permute-start.2 = (f32[352,1280]{1,0:T(8,128)}, f32[352,1280]{1,0:T(8,128)S(1)}, u32[]{:S(2)}, u32[]{:S(2)}) collective-permute-start(f32[352,1280]{1,0:T(8,128)} %get-tuple-element.36), channel_id=1, source_target_pairs={{0,1},{1,0},{2,3},{3,2},{4,5},{5,4},{6,7},{7,6},{8,9},{9,8},{10,11... | collective-permute-start | bytes 5406728 | tf_op jit(solution)/shard_map/ppermute | solution.py:27
  17.0 23.2 %collective-permute-start.3 = (f16[352,1280]{1,0:T(8,128)(2,1)S(1)}, f16[352,1280]{1,0:T(8,128)(2,1)S(1)}, u32[]{:S(2)}, u32[]{:S(2)}) collective-permute-start(f16[352,1280]{1,0:T(8,128)(2,1)S(1)} %get-tuple-element.64), channel_id=1, source_target_pairs={{0,2},{1,3},{2,0},{3,1},{4,6},{5,7},{6,4},{7,5},{8,10},{9,11},{10,... | collective-permute-start | bytes 2703368 | tf_op jit(solution)/shard_map/ppermute | solution.py:27
  19.6 24.3 %collective-permute-start.1 = (bf16[352,1280]{1,0:T(8,128)(2,1)S(1)}, bf16[352,1280]{1,0:T(8,128)(2,1)S(1)}, u32[]{:S(2)}, u32[]{:S(2)}) collective-permute-start(bf16[352,1280]{1,0:T(8,128)(2,1)S(1)} %copy-done.6), channel_id=1, source_target_pairs={{0,4},{1,5},{2,6},{3,7},{4,0},{5,1},{6,2},{7,3},{8,12},{9,13},{10,... | collective-permute-start | bytes 2703368 | tf_op jit(solution)/shard_map/ppermute | solution.py:27
  21.2 22.7 %collective-permute-start = (bf16[176,1280]{1,0:T(8,128)(2,1)S(1)}, bf16[176,1280]{1,0:T(8,128)(2,1)S(1)}, u32[]{:S(2)}, u32[]{:S(2)}) collective-permute-start(bf16[176,1280]{1,0:T(8,128)(2,1)S(1)} %copy-done.7), channel_id=1, source_target_pairs={{0,16},{1,17},{2,18},{3,19},{4,20},{5,21},{6,22},{7,23},{8,24},{9,... | collective-permute-start | bytes 1351688 | tf_op jit(solution)/shard_map/ppermute | solution.py:27
  45.0 3.2 %collective-permute-start.4 = (bf16[352,1280]{1,0:T(8,128)(2,1)S(1)}, bf16[352,1280]{1,0:T(8,128)(2,1)S(1)}, u32[]{:S(2)}, u32[]{:S(2)}) collective-permute-start(bf16[352,1280]{1,0:T(8,128)(2,1)S(1)} %get-tuple-element.37.refs_0_), channel_id=1, source_target_pairs={{0,1},{1,0},{2,3},{3,2},{4,5},{5,4},{6,7},{7,6},{8,9},{9,8},{10,11... | collective-permute-start | bytes 2703368 | tf_op jit(solution)/shard_map/ppermute | solution.py:27
  45.1 24.3 %collective-permute-start.7 = (bf16[352,1280]{1,0:T(8,128)(2,1)S(1)}, bf16[352,1280]{1,0:T(8,128)(2,1)S(1)}, u32[]{:S(2)}, u32[]{:S(2)}) collective-permute-start(bf16[352,1280]{1,0:T(8,128)(2,1)S(1)} %get-tuple-element.37.refs_0_), channel_id=1, source_target_pairs={{0,4},{1,5},{2,6},{3,7},{4,0},{5,1},{6,2},{7,3},{8,12},{9,13},{10,... | collective-permute-start | bytes 2703368 | tf_op jit(solution)/shard_map/ppermute | solution.py:27
  45.6 13.0 %collective-permute-start.8 = (bf16[176,1280]{1,0:T(8,128)(2,1)S(1)}, bf16[176,1280]{1,0:T(8,128)(2,1)S(1)}, u32[]{:S(2)}, u32[]{:S(2)}) collective-permute-start(bf16[176,1280]{1,0:T(8,128)(2,1)S(1)} %collective-permute-done.refs_0_), channel_id=1, source_target_pairs={{0,2},{1,3},{2,0},{3,1},{4,6},{5,7},{6,4},{7,5},{8,10},{9,11},{10,... | collective-permute-start | bytes 1351688 | tf_op jit(solution)/shard_map/ppermute | solution.py:27
  46.7 22.7 %collective-permute-start.9 = (bf16[176,1280]{1,0:T(8,128)(2,1)S(1)}, bf16[176,1280]{1,0:T(8,128)(2,1)S(1)}, u32[]{:S(2)}, u32[]{:S(2)}) collective-permute-start(bf16[176,1280]{1,0:T(8,128)(2,1)S(1)} %get-tuple-element.43), channel_id=1, source_target_pairs={{0,16},{1,17},{2,18},{3,19},{4,20},{5,21},{6,22},{7,23},{8,24},{9,... | collective-permute-start | bytes 1351688 | tf_op jit(solution)/shard_map/ppermute | solution.py:27
  48.2 23.7 %collective-permute-start.11 = (bf16[352,1280]{1,0:T(8,128)(2,1)S(1)}, bf16[352,1280]{1,0:T(8,128)(2,1)S(1)}, u32[]{:S(2)}, u32[]{:S(2)}) collective-permute-start(bf16[352,1280]{1,0:T(8,128)(2,1)S(1)} %collective-permute-done.1.refs_1_.refs_2_), channel_id=1, source_target_pairs={{0,1},{1,0},{2,3},{3,2},{4,5},{5,4},{6,7},{7,6},{8,9},{9,8},{10,11... | collective-permute-start | bytes 2703368 | tf_op jit(solution)/shard_map/ppermute | solution.py:27
  69.4 4.5 %collective-permute-start.10 = (bf16[352,1280]{1,0:T(8,128)(2,1)S(1)}, bf16[352,1280]{1,0:T(8,128)(2,1)S(1)}, u32[]{:S(2)}, u32[]{:S(2)}) collective-permute-start(bf16[352,1280]{1,0:T(8,128)(2,1)S(1)} %collective-permute-done.7.refs_0_), channel_id=1, source_target_pairs={{0,1},{1,0},{2,3},{3,2},{4,5},{5,4},{6,7},{7,6},{8,9},{9,8},{10,11... | collective-permute-start | bytes 2703368 | tf_op jit(solution)/shard_map/ppermute | solution.py:27
  69.4 22.6 %collective-permute-start.14 = (bf16[176,1280]{1,0:T(8,128)(2,1)S(1)}, bf16[176,1280]{1,0:T(8,128)(2,1)S(1)}, u32[]{:S(2)}, u32[]{:S(2)}) collective-permute-start(bf16[176,1280]{1,0:T(8,128)(2,1)S(1)} %collective-permute-done.9.refs_0_), channel_id=1, source_target_pairs={{0,2},{1,3},{2,0},{3,1},{4,6},{5,7},{6,4},{7,5},{8,10},{9,11},{10,... | collective-permute-start | bytes 1351688 | tf_op jit(solution)/shard_map/ppermute | solution.py:27
  70.4 21.6 %collective-permute-start.15 = (bf16[176,1280]{1,0:T(8,128)(2,1)S(1)}, bf16[176,1280]{1,0:T(8,128)(2,1)S(1)}, u32[]{:S(2)}, u32[]{:S(2)}) collective-permute-start(bf16[176,1280]{1,0:T(8,128)(2,1)S(1)} %collective-permute-done.9.refs_0_), channel_id=1, source_target_pairs={{0,4},{1,5},{2,6},{3,7},{4,0},{5,1},{6,2},{7,3},{8,12},{9,13},{10,... | collective-permute-start | bytes 1351688 | tf_op jit(solution)/shard_map/ppermute | solution.py:27
  71.9 12.7 %collective-permute-start.5 = (bf16[160,1280]{1,0:T(8,128)(2,1)S(1)}, bf16[160,1280]{1,0:T(8,128)(2,1)S(1)}, u32[]{:S(2)}, u32[]{:S(2)}) collective-permute-start(bf16[160,1280]{1,0:T(8,128)(2,1)S(1)} %get-tuple-element.40), channel_id=1, source_target_pairs={{0,8},{1,9},{2,10},{3,11},{4,12},{5,13},{6,14},{7,15},{8,0},{9,1},... | collective-permute-start | bytes 1228808 | tf_op jit(solution)/shard_map/ppermute | solution.py:27
  71.9 20.1 %collective-permute-start.6 = (bf16[160,1280]{1,0:T(8,128)(2,1)S(1)}, bf16[160,1280]{1,0:T(8,128)(2,1)S(1)}, u32[]{:S(2)}, u32[]{:S(2)}) collective-permute-start(bf16[160,1280]{1,0:T(8,128)(2,1)S(1)} %get-tuple-element.41), channel_id=1, source_target_pairs={{0,8},{1,9},{2,10},{3,11},{4,12},{5,13},{6,14},{7,15},{8,0},{9,1},... | collective-permute-start | bytes 1228808 | tf_op jit(solution)/shard_map/ppermute | solution.py:27
  73.9 21.7 %collective-permute-start.17 = (bf16[352,1280]{1,0:T(8,128)(2,1)S(1)}, bf16[352,1280]{1,0:T(8,128)(2,1)S(1)}, u32[]{:S(2)}, u32[]{:S(2)}) collective-permute-start(bf16[352,1280]{1,0:T(8,128)(2,1)S(1)} %join.4.refs_3_), channel_id=1, source_target_pairs={{0,1},{1,0},{2,3},{3,2},{4,5},{5,4},{6,7},{7,6},{8,9},{9,8},{10,11... | collective-permute-start | bytes 2703368 | tf_op jit(solution)/shard_map/ppermute | solution.py:27
  92.1 3.5 %collective-permute-start.16 = (bf16[352,1280]{1,0:T(8,128)(2,1)S(1)}, bf16[352,1280]{1,0:T(8,128)(2,1)S(1)}, u32[]{:S(2)}, u32[]{:S(2)}) collective-permute-start(bf16[352,1280]{1,0:T(8,128)(2,1)S(1)} %join.5.refs_1_), channel_id=1, source_target_pairs={{0,1},{1,0},{2,3},{3,2},{4,5},{5,4},{6,7},{7,6},{8,9},{9,8},{10,11... | collective-permute-start | bytes 2703368 | tf_op jit(solution)/shard_map/ppermute | solution.py:27
  92.1 13.9 %collective-permute-start.22 = (bf16[176,1280]{1,0:T(8,128)(2,1)S(1)}, bf16[176,1280]{1,0:T(8,128)(2,1)S(1)}, u32[]{:S(2)}, u32[]{:S(2)}) collective-permute-start(bf16[176,1280]{1,0:T(8,128)(2,1)S(1)} %collective-permute-done.refs_0_), channel_id=1, source_target_pairs={{0,4},{1,5},{2,6},{3,7},{4,0},{5,1},{6,2},{7,3},{8,12},{9,13},{10,... | collective-permute-start | bytes 1351688 | tf_op jit(solution)/shard_map/ppermute | solution.py:27
  92.7 13.4 %collective-permute-start.12 = (bf16[160,1280]{1,0:T(8,128)(2,1)S(1)}, bf16[160,1280]{1,0:T(8,128)(2,1)S(1)}, u32[]{:S(2)}, u32[]{:S(2)}) collective-permute-start(bf16[160,1280]{1,0:T(8,128)(2,1)S(1)} %get-tuple-element.47), channel_id=1, source_target_pairs={{0,8},{1,9},{2,10},{3,11},{4,12},{5,13},{6,14},{7,15},{8,0},{9,1},... | collective-permute-start | bytes 1228808 | tf_op jit(solution)/shard_map/ppermute | solution.py:27
  94.4 23.4 %collective-permute-start.20 = (bf16[176,1280]{1,0:T(8,128)(2,1)S(1)}, bf16[176,1280]{1,0:T(8,128)(2,1)S(1)}, u32[]{:S(2)}, u32[]{:S(2)}) collective-permute-start(bf16[176,1280]{1,0:T(8,128)(2,1)S(1)} %collective-permute-done.15.refs_0_), channel_id=1, source_target_pairs={{0,2},{1,3},{2,0},{3,1},{4,6},{5,7},{6,4},{7,5},{8,10},{9,11},{10,... | collective-permute-start | bytes 1351688 | tf_op jit(solution)/shard_map/ppermute | solution.py:27
  106.1 11.9 %collective-permute-start.23 = (bf16[176,1280]{1,0:T(8,128)(2,1)S(1)}, bf16[176,1280]{1,0:T(8,128)(2,1)S(1)}, u32[]{:S(2)}, u32[]{:S(2)}) collective-permute-start(bf16[176,1280]{1,0:T(8,128)(2,1)S(1)} %collective-permute-done.22.refs_0_), channel_id=1, source_target_pairs={{0,2},{1,3},{2,0},{3,1},{4,6},{5,7},{6,4},{7,5},{8,10},{9,11},{10,... | collective-permute-start | bytes 1351688 | tf_op jit(solution)/shard_map/ppermute | solution.py:27
  107.1 10.7 %collective-permute-start.13 = (bf16[160,1280]{1,0:T(8,128)(2,1)S(1)}, bf16[160,1280]{1,0:T(8,128)(2,1)S(1)}, u32[]{:S(2)}, u32[]{:S(2)}) collective-permute-start(bf16[160,1280]{1,0:T(8,128)(2,1)S(1)} %get-tuple-element.48), channel_id=1, source_target_pairs={{0,8},{1,9},{2,10},{3,11},{4,12},{5,13},{6,14},{7,15},{8,0},{9,1},... | collective-permute-start | bytes 1228808 | tf_op jit(solution)/shard_map/ppermute | solution.py:27
  118.0 5.1 %collective-permute-start.21 = (bf16[352,1280]{1,0:T(8,128)(2,1)S(1)}, bf16[352,1280]{1,0:T(8,128)(2,1)S(1)}, u32[]{:S(2)}, u32[]{:S(2)}) collective-permute-start(bf16[352,1280]{1,0:T(8,128)(2,1)S(1)} %join.6.refs_1_), channel_id=1, source_target_pairs={{0,1},{1,0},{2,3},{3,2},{4,5},{5,4},{6,7},{7,6},{8,9},{9,8},{10,11... | collective-permute-start | bytes 2703368 | tf_op jit(solution)/shard_map/ppermute | solution.py:27
  118.1 5.0 %collective-permute-start.24 = (bf16[352,1280]{1,0:T(8,128)(2,1)S(1)}, bf16[352,1280]{1,0:T(8,128)(2,1)S(1)}, u32[]{:S(2)}, u32[]{:S(2)}) collective-permute-start(bf16[352,1280]{1,0:T(8,128)(2,1)S(1)} %join.7.refs_3_), channel_id=1, source_target_pairs={{0,1},{1,0},{2,3},{3,2},{4,5},{5,4},{6,7},{7,6},{8,9},{9,8},{10,11... | collective-permute-start | bytes 2703368 | tf_op jit(solution)/shard_map/ppermute | solution.py:27
  118.7 17.3 %collective-permute-start.18 = (bf16[160,1280]{1,0:T(8,128)(2,1)S(1)}, bf16[160,1280]{1,0:T(8,128)(2,1)S(1)}, u32[]{:S(2)}, u32[]{:S(2)}) collective-permute-start(bf16[160,1280]{1,0:T(8,128)(2,1)S(1)} %get-tuple-element.54), channel_id=1, source_target_pairs={{0,8},{1,9},{2,10},{3,11},{4,12},{5,13},{6,14},{7,15},{8,0},{9,1},... | collective-permute-start | bytes 1228808 | tf_op jit(solution)/shard_map/ppermute | solution.py:27
  120.4 19.4 %collective-permute-start.19 = (bf16[160,1280]{1,0:T(8,128)(2,1)S(1)}, bf16[160,1280]{1,0:T(8,128)(2,1)S(1)}, u32[]{:S(2)}, u32[]{:S(2)}) collective-permute-start(bf16[160,1280]{1,0:T(8,128)(2,1)S(1)} %get-tuple-element.55), channel_id=1, source_target_pairs={{0,8},{1,9},{2,10},{3,11},{4,12},{5,13},{6,14},{7,15},{8,0},{9,1},... | collective-permute-start | bytes 1228808 | tf_op jit(solution)/shard_map/ppermute | solution.py:27
  133.8 14.7 %collective-permute-start.25 = (bf16[160,1280]{1,0:T(8,128)(2,1)S(1)}, bf16[160,1280]{1,0:T(8,128)(2,1)S(1)}, u32[]{:S(2)}, u32[]{:S(2)}) collective-permute-start(bf16[160,1280]{1,0:T(8,128)(2,1)S(1)} %get-tuple-element.62), channel_id=1, source_target_pairs={{0,8},{1,9},{2,10},{3,11},{4,12},{5,13},{6,14},{7,15},{8,0},{9,1},... | collective-permute-start | bytes 1228808 | tf_op jit(solution)/shard_map/ppermute | solution.py:27
  135.6 20.8 %collective-permute-start.26 = (bf16[160,1280]{1,0:T(8,128)(2,1)S(1)}, bf16[160,1280]{1,0:T(8,128)(2,1)S(1)}, u32[]{:S(2)}, u32[]{:S(2)}) collective-permute-start(bf16[160,1280]{1,0:T(8,128)(2,1)S(1)} %get-tuple-element.63), channel_id=1, source_target_pairs={{0,8},{1,9},{2,10},{3,11},{4,12},{5,13},{6,14},{7,15},{8,0},{9,1},... | collective-permute-start | bytes 1228808 | tf_op jit(solution)/shard_map/ppermute | solution.py:27
  159.9 3.7 %collective-permute-start.28 = (f32[8,128]{1,0:T(8,128)S(1)}, f32[8,128]{1,0:T(8,128)S(1)}, u32[]{:S(2)}, u32[]{:S(2)}) collective-permute-start(f32[8,128]{1,0:T(8,128)S(1)} %products.9.refs_0_), channel_id=1, source_target_pairs={{0,2},{1,3},{2,0},{3,1},{4,6},{5,7},{6,4},{7,5},{8,10},{9,11},{10,... | collective-permute-start | bytes 12296 | tf_op jit(solution)/shard_map/ppermute | solution.py:27
  164.5 4.5 %collective-permute-start.30 = (f32[8,128]{1,0:T(8,128)S(1)}, f32[8,128]{1,0:T(8,128)S(1)}, u32[]{:S(2)}, u32[]{:S(2)}) collective-permute-start(f32[8,128]{1,0:T(8,128)S(1)} %sum_of.3.refs_0_), channel_id=1, source_target_pairs={{0,8},{1,9},{2,10},{3,11},{4,12},{5,13},{6,14},{7,15},{8,0},{9,1},... | collective-permute-start | bytes 12296 | tf_op jit(solution)/shard_map/ppermute | solution.py:27
  166.4 4.5 %collective-permute-start.31 = (f32[8,128]{1,0:T(8,128)S(1)}, f32[8,128]{1,0:T(8,128)S(1)}, u32[]{:S(2)}, u32[]{:S(2)}) collective-permute-start(f32[8,128]{1,0:T(8,128)S(1)} %sum_of.3.refs_0_), channel_id=1, source_target_pairs={{0,16},{1,17},{2,18},{3,19},{4,20},{5,21},{6,22},{7,23},{8,24},{9,... | collective-permute-start | bytes 12296 | tf_op jit(solution)/shard_map/ppermute | solution.py:27
  167.5 5.4 %collective-permute-start.32 = (f32[8,128]{1,0:T(8,128)S(1)}, f32[8,128]{1,0:T(8,128)S(1)}, u32[]{:S(2)}, u32[]{:S(2)}) collective-permute-start(f32[8,128]{1,0:T(8,128)S(1)} %sum_of.3.refs_0_), channel_id=1, source_target_pairs={{0,24},{1,25},{2,26},{3,27},{4,28},{5,29},{6,30},{7,31},{8,16},{9,... | collective-permute-start | bytes 12296 | tf_op jit(solution)/shard_map/ppermute | solution.py:27
  173.5 3.7 %collective-permute-start.33 = (f32[8,128]{1,0:T(8,128)S(1)}, f32[8,128]{1,0:T(8,128)S(1)}, u32[]{:S(2)}, u32[]{:S(2)}) collective-permute-start(f32[8,128]{1,0:T(8,128)S(1)} %sum_of.4.refs_0_), channel_id=1, source_target_pairs={{0,4},{1,5},{2,6},{3,7},{4,0},{5,1},{6,2},{7,3},{8,12},{9,13},{10,... | collective-permute-start | bytes 12296 | tf_op jit(solution)/shard_map/ppermute | solution.py:27
  (10 other events, 71.8 us)

commit v11 on v10

--- a/solution.py
+++ b/solution.py
@@ -326,8 +326,9 @@
 
 def products_kernel(labels, fresh, place_ref, *refs):
     own = refs[0].shape[0]
-    slots = [refs[2 * n : 2 * n + 2] for n in range(len(labels))]
-    known_ref, out_ref, totals = refs[2 * len(labels) :]
+    refs, (known_ref, out_ref, totals) = refs[:-3], refs[-3:]
+    each = len(refs) // len(labels)
+    slots = [refs[each * n : each * (n + 1)] for n in range(len(labels))]
     pairs = [(i, j) for i in range(len(slots) - fresh, len(slots)) for j in range(i + 1)]
 
     @pl.when(pl.program_id(0) == 0)
@@ -339,7 +340,7 @@
 
     for n, (i, j) in enumerate(pairs):
         a, b = values(slots[i]), values(slots[j])
-        both = a[0] * b[0] + a[1] * b[1]
+        both = sum(u * v for u, v in zip(a, b))
         totals[n] += jnp.sum(both.reshape(own // 8, 8, -1), axis=0)
 
     @pl.when(pl.program_id(0) == pl.num_programs(0) - 1)
@@ -476,7 +477,7 @@
     near = shard & 1
     part_rows = row_count // shards
     own = inputs.shape[1] // members
-    swap = min(2, members // 2)
+    swap = 1
     bits = [2**b for b in reversed(range(gathered)) if 2**b != swap]
     upper = member // swap % 2
     first_row = (member - upper * swap) * own
@@ -514,11 +515,11 @@
         sum(sums[:-1]),
         sums[-1],
         targets,
-        tuple(inputs_of.values()),
-    )
-    errors_of = {
-        bit: from_mask(error_piece if bit == first_bit else error, bit * others, 0) for bit in bits
-    }
+        (inputs_of[first_bit],),
+    )
+    errors_of = {first_bit: from_mask(error_piece, first_bit * others, 0)}
+    for bit in bits[1:]:
+        errors_of[bit] = from_mask(ordered(error, inputs_of[bit]), bit * others, 0)
 
     def to_half(piece, *before):
         for bit in reversed(range(1, shard_levels)):
@@ -536,7 +537,9 @@
         if n == 0:
             half = error
         elif not m & first_bit:
-            half = errors_of[m] = ordered(errors_of[m], sent[0], inputs_half, errors_of[first_bit])
+            half = errors_of[m] = ordered(
+                errors_of[m], sent[0], inputs_half, errors_of[first_bit], slots[1][0]
+            )
             other_inputs = inputs_of[m]
         elif m == first_bit:
             for bit in bits[1:]:
@@ -544,12 +547,14 @@
                 inputs_of[first_bit | bit] = from_mask(ready, bit * others, 0)
                 ready = ordered(errors_of[first_bit], errors_of[bit])
                 errors_of[first_bit | bit] = from_mask(ready, bit * others, 0)
-            before = [errors_of[first_bit | bit] for bit in bits[1:]]
+            before = [of[first_bit | bit] for bit in bits[1:] for of in (errors_of, inputs_of)]
             half = to_half(ordered(errors_of[m], sent[0]), sent[-1], *slots[1], *before)
             other_inputs = inputs_half
         else:
-            other_inputs = to_half(ordered(inputs_of[m], sent[-1], slots[2 * n - 3][0]))
-            half = to_half(ordered(errors_of[m], sent[-2]), sent[-1], *slots[2 * n - 3])
+            other_inputs, half = (
+                to_half(ordered(of[m], sent[-2]), sent[-1], *slots[2 * n - 3])
+                for of in (inputs_of, errors_of)
+            )
         first, second, *send = gradient(
             place,
             members,
@@ -570,7 +575,11 @@
             totals = products(place, slots, labels, 1, totals)
         slots.append(tuple(from_mask(a, swap * others, 0) for a in send))
         labels.append(m ^ swap)
-        totals = products(place, slots, labels, 1 if last else 2, totals)
+        if last:
+            for k in range(2):
+                totals = products(place, [slot[k : k + 1] for slot in slots], labels, 1, totals)
+        else:
+            totals = products(place, slots, labels, 2, totals)
         known.append(totals)
 
     rounds = [[(0, mask) for mask in range(1, shards)]]

time: 182 us -> 192 us (1.055)
  waiting for transfers between devices: 70.8 us -> 79.9 us
  starting transfers between devices: 31.3 us -> 34.7 us
  Pallas kernels: 76.5 us -> 73.5 us
    ppermute x34, waiting for transfers between devices: 70.8 us -> 79.9 us  [from_mask(): return lax.ppermute(value, ('dp', 'tensor'), pairs)]
    ppermute x34, starting transfers between devices: 31.3 us -> 34.7 us  [from_mask(): return lax.ppermute(value, ('dp', 'tensor'), pairs)]
    pallas_call x20 -> x21, Pallas kernels: 76.5 us -> 73.5 us  [call(): pl.pallas_call(body, grid_spec=pltpu.PrefetchScalarGridSpec(num_scalar_pr...]
  transfers between devices with their start and end apart: 34 -> 34, of which waited for: 14 -> 16; matrix products, arithmetic and copies ran while one was open for 0% -> 0% of each run, Pallas kernels for 30% -> 29%
where the time goes in v11:
time: 192 us; the launch traced here: 191 us
  waiting for transfers between devices  79.9 us (42%)
  Pallas kernels  73.5 us (38%)
  starting transfers between devices  34.7 us (18%)
    ppermute x34, waiting for transfers between devices, from_mask(): return lax.ppermute(value, ('dp', 'tensor'), pairs)  79.9 us
    pallas_call x21, Pallas kernels, call(): pl.pallas_call(body, grid_spec=pltpu.PrefetchScalarGridSpec(num_scalar_pr...  73.5 us
    ppermute x34, starting transfers between devices, from_mask(): return lax.ppermute(value, ('dp', 'tensor'), pairs)  34.7 us
  transfers between devices with their start and end apart: 34, of which 16 were waited for; matrix products, arithmetic and copies ran while one was open for 0% of the time, Pallas kernels for 29%

profile of v11, /device:TPU:0, one launch (start us, length us, event | category | flops | bytes accessed | tf_op | source)
XLA Modules:
  0.0 191.4 jit_solution(8162245521017114111)
XLA Ops:
  1.4 11.0 %forward.1 = (f32[352,1280]{1,0:T(8,128)}, bf16[352,1280]{1,0:T(8,128)(2,1)}, bf16[352,1280]{1,0:T(8,128)(2,1)}, bf16[176,1280]{1,0:T(8,128)(2,1)}) custom-call(s32[8]{0:T(128)} %stack.35.place_ref, bf16[704,1280]{1,0:T(8,128)(2,1)} %refs_2_.3, bf16[1280,1280]{1,0:T(8,128)(2,1)} %refs_5_.5, bf16[1280,1280]{1,0:T(8,128)(2,1)} %refs_6_.3), custom_call_target="tpu_custom_call" | custom-call | flops 1 | bytes 1 | tf_op jit(solution)/shard_map/forward/pallas_call | solution.py:81
  14.0 2.7 %product.1 = f32[352,1280]{1,0:T(8,128)S(1)} custom-call(s32[8]{0:T(128)S(1)} %copy-done.5, bf16[352,1280]{1,0:T(8,128)(2,1)S(1)} %copy-done.4, bf16[1280,1280]{1,0:T(8,128)(2,1)S(1)} %copy-done), custom_call_target="tpu_custom_call" | custom-call | flops 1 | bytes 1 | tf_op jit(solution)/shard_map/product/pallas_call | solution.py:81
  17.0 2.6 %collective-permute-start.2 = (f16[352,1280]{1,0:T(8,128)(2,1)S(1)}, f16[352,1280]{1,0:T(8,128)(2,1)S(1)}, u32[]{:S(2)}, u32[]{:S(2)}) collective-permute-start(f16[352,1280]{1,0:T(8,128)(2,1)S(1)} %get-tuple-element.68), channel_id=1, source_target_pairs={{0,2},{1,3},{2,0},{3,1},{4,6},{5,7},{6,4},{7,5},{8,10},{9,11},{10,... | collective-permute-start | bytes 2703368 | tf_op jit(solution)/shard_map/ppermute | solution.py:27
  19.6 2.6 %collective-permute-start = (bf16[176,1280]{1,0:T(8,128)(2,1)S(1)}, bf16[176,1280]{1,0:T(8,128)(2,1)S(1)}, u32[]{:S(2)}, u32[]{:S(2)}) collective-permute-start(bf16[176,1280]{1,0:T(8,128)(2,1)S(1)} %copy-done.7), channel_id=1, source_target_pairs={{0,16},{1,17},{2,18},{3,19},{4,20},{5,21},{6,22},{7,23},{8,24},{9,... | collective-permute-start | bytes 1351688 | tf_op jit(solution)/shard_map/ppermute | solution.py:27
  23.8 16.5 %collective-permute-done.2 = f16[352,1280]{1,0:T(8,128)(2,1)S(1)} collective-permute-done((f16[352,1280]{1,0:T(8,128)(2,1)S(1)}, f16[352,1280]{1,0:T(8,128)(2,1)S(1)}, u32[]{:S(2)}, u32[]{:S(2)}) %collective-permute-start.2) | collective-permute-done | bytes 901152 | tf_op jit(solution)/shard_map/ppermute | solution.py:27
  40.4 2.3 %collective-permute-done.refs_0_ = bf16[176,1280]{1,0:T(8,128)(2,1)S(1)} collective-permute-done((bf16[176,1280]{1,0:T(8,128)(2,1)S(1)}, bf16[176,1280]{1,0:T(8,128)(2,1)S(1)}, u32[]{:S(2)}, u32[]{:S(2)}) %collective-permute-start) | collective-permute-done | bytes 450592 | tf_op jit(solution)/shard_map/ppermute | solution.py:27
  43.9 8.6 %collective-permute-done.5.refs_2_ = bf16[352,1280]{1,0:T(8,128)(2,1)S(1)} collective-permute-done((bf16[352,1280]{1,0:T(8,128)(2,1)S(1)}, bf16[352,1280]{1,0:T(8,128)(2,1)S(1)}, u32[]{:S(2)}, u32[]{:S(2)}) %collective-permute-start.5) | collective-permute-done | bytes 901152 | tf_op jit(solution)/shard_map/ppermute | solution.py:27
  55.0 1.8 collective-permute-start.8
  56.8 9.7 %gradient.4 = (f32[160,1280]{1,0:T(8,128)S(1)}, f32[160,1280]{1,0:T(8,128)S(1)}, bf16[160,1280]{1,0:T(8,128)(2,1)S(1)}, bf16[160,1280]{1,0:T(8,128)(2,1)S(1)}) custom-call(s32[8]{0:T(128)S(1)} %copy-done.5, bf16[352,1280]{1,0:T(8,128)(2,1)S(1)} %get-tuple-element.42.refs_0_, bf16[352,1280]{1,0:T(8,128)(2,1)S(1)} %collective-permute-done.3.refs_1_, ...), custom_call_target="tpu_custom_call" | custom-call | flops 1 | bytes 1 | tf_op jit(solution)/shard_map/gradient/pallas_call | solution.py:81
  68.1 14.4 %collective-permute-done.8.refs_0_ = bf16[176,1280]{1,0:T(8,128)(2,1)S(1)} collective-permute-done((bf16[176,1280]{1,0:T(8,128)(2,1)S(1)}, bf16[176,1280]{1,0:T(8,128)(2,1)S(1)}, u32[]{:S(2)}, u32[]{:S(2)}) %collective-permute-start.8) | collective-permute-done | bytes 450592 | tf_op jit(solution)/shard_map/ppermute | solution.py:27
  84.5 1.8 collective-permute-start.14
  88.0 9.9 %gradient.5 = (f32[160,1280]{1,0:T(8,128)S(1)}, f32[160,1280]{1,0:T(8,128)S(1)}, bf16[160,1280]{1,0:T(8,128)(2,1)S(1)}, bf16[160,1280]{1,0:T(8,128)(2,1)S(1)}) custom-call(s32[8]{0:T(128)S(1)} %copy-done.5, bf16[352,1280]{1,0:T(8,128)(2,1)S(1)} %collective-permute-done.6.refs_0_, bf16[352,1280]{1,0:T(8,128)(2,1)S(1)} %collective-permute-done.10.refs_1_, ...), custom_call_target="tpu_custom_call" | custom-call | flops 1 | bytes 1 | tf_op jit(solution)/shard_map/gradient/pallas_call | solution.py:81
  98.0 8.7 %collective-permute-done.15.refs_0_ = bf16[176,1280]{1,0:T(8,128)(2,1)S(1)} collective-permute-done((bf16[176,1280]{1,0:T(8,128)(2,1)S(1)}, bf16[176,1280]{1,0:T(8,128)(2,1)S(1)}, u32[]{:S(2)}, u32[]{:S(2)}) %collective-permute-start.15) | collective-permute-done | bytes 450592 | tf_op jit(solution)/shard_map/ppermute | solution.py:27
  112.4 9.7 %gradient.6 = (f32[160,1280]{1,0:T(8,128)S(1)}, f32[160,1280]{1,0:T(8,128)S(1)}, bf16[160,1280]{1,0:T(8,128)(2,1)S(1)}, bf16[160,1280]{1,0:T(8,128)(2,1)S(1)}) custom-call(s32[8]{0:T(128)S(1)} %copy-done.5, f32[8,128]{1,0:T(8,128)S(1)} %products.6.refs_0_.refs_8_, bf16[352,1280]{1,0:T(8,128)(2,1)S(1)} %join.5.refs_1_, ...), custom_call_target="tpu_custom_call" | custom-call | flops 1 | bytes 1 | tf_op jit(solution)/shard_map/gradient/pallas_call | solution.py:81
  122.1 6.8 %collective-permute-done.19.refs_6_.refs_3_.refs_7_ = bf16[160,1280]{1,0:T(8,128)(2,1)S(1)} collective-permute-done((bf16[160,1280]{1,0:T(8,128)(2,1)S(1)}, bf16[160,1280]{1,0:T(8,128)(2,1)S(1)}, u32[]{:S(2)}, u32[]{:S(2)}) %collective-permute-start.19) | collective-permute-done | bytes 409632 | tf_op jit(solution)/shard_map/ppermute | solution.py:27
  131.7 2.4 %products.7.refs_0_.refs_12_ = f32[8,128]{1,0:T(8,128)S(1)} custom-call(s32[8]{0:T(128)S(1)} %copy-done.5, f32[160,1280]{1,0:T(8,128)S(1)} %get-tuple-element.49.refs_0_.refs_1_, f32[160,1280]{1,0:T(8,128)S(1)} %get-tuple-element.39.refs_1_.refs_0_.refs_2_, bf16[160,1280]{1,0:T(8,128)(2,1)S(1)} %collective-permute-done.9.refs_2_.refs_1_.refs_3_, ...), custom_call_target="tpu_custom_call" | custom-call | flops 1 | bytes 1 | tf_op jit(solution)/shard_map/products/pallas_call | solution.py:81
  134.2 9.9 %gradient.7 = (f32[160,1280]{1,0:T(8,128)S(1)}, f32[160,1280]{1,0:T(8,128)S(1)}, bf16[160,1280]{1,0:T(8,128)(2,1)S(1)}, bf16[160,1280]{1,0:T(8,128)(2,1)S(1)}) custom-call(s32[8]{0:T(128)S(1)} %copy-done.5, f32[8,128]{1,0:T(8,128)S(1)} %products.7.refs_0_.refs_12_, bf16[352,1280]{1,0:T(8,128)(2,1)S(1)} %join.6.refs_1_, ...), custom_call_target="tpu_custom_call" | custom-call | flops 1 | bytes 1 | tf_op jit(solution)/shard_map/gradient/pallas_call | solution.py:81
  144.1 1.6 collective-permute-start.26
  146.2 4.6 %collective-permute-done.18.refs_11_.refs_5_.refs_12_ = bf16[160,1280]{1,0:T(8,128)(2,1)S(1)} collective-permute-done((bf16[160,1280]{1,0:T(8,128)(2,1)S(1)}, bf16[160,1280]{1,0:T(8,128)(2,1)S(1)}, u32[]{:S(2)}, u32[]{:S(2)}) %collective-permute-start.18) | collective-permute-done | bytes 409632 | tf_op jit(solution)/shard_map/ppermute | solution.py:27
  150.8 3.4 %products.8.refs_14_ = f32[8,128]{1,0:T(8,128)S(1)} custom-call(s32[8]{0:T(128)S(1)} %copy-done.5, f32[160,1280]{1,0:T(8,128)S(1)} %get-tuple-element.49.refs_0_.refs_1_, f32[160,1280]{1,0:T(8,128)S(1)} %get-tuple-element.39.refs_1_.refs_0_.refs_2_, bf16[160,1280]{1,0:T(8,128)(2,1)S(1)} %collective-permute-done.9.refs_2_.refs_1_.refs_3_, ...), custom_call_target="tpu_custom_call" | custom-call | flops 1 | bytes 1 | tf_op jit(solution)/shard_map/products/pallas_call | solution.py:81
  154.2 2.8 %products.9.refs_8_ = f32[8,128]{1,0:T(8,128)S(1)} custom-call(s32[8]{0:T(128)S(1)} %copy-done.5, f32[160,1280]{1,0:T(8,128)S(1)} %get-tuple-element.49.refs_0_.refs_1_, f32[160,1280]{1,0:T(8,128)S(1)} %get-tuple-element.39.refs_1_.refs_0_.refs_2_, bf16[160,1280]{1,0:T(8,128)(2,1)S(1)} %collective-permute-done.9.refs_2_.refs_1_.refs_3_, ...), custom_call_target="tpu_custom_call" | custom-call | flops 1 | bytes 1 | tf_op jit(solution)/shard_map/products/pallas_call | solution.py:81
  157.1 2.5 %collective-permute-done.26.refs_7_.refs_15_ = bf16[160,1280]{1,0:T(8,128)(2,1)S(1)} collective-permute-done((bf16[160,1280]{1,0:T(8,128)(2,1)S(1)}, bf16[160,1280]{1,0:T(8,128)(2,1)S(1)}, u32[]{:S(2)}, u32[]{:S(2)}) %collective-permute-start.26) | collective-permute-done | bytes 409632 | tf_op jit(solution)/shard_map/ppermute | solution.py:27
  159.6 1.6 products.10.refs_8_
  161.2 6.3 %collective-permute-done.24.refs_7_.refs_16_ = bf16[160,1280]{1,0:T(8,128)(2,1)S(1)} collective-permute-done((bf16[160,1280]{1,0:T(8,128)(2,1)S(1)}, bf16[160,1280]{1,0:T(8,128)(2,1)S(1)}, u32[]{:S(2)}, u32[]{:S(2)}) %collective-permute-start.24) | collective-permute-done | bytes 409632 | tf_op jit(solution)/shard_map/ppermute | solution.py:27
  167.6 1.6 products.11.refs_0_
  171.2 1.8 collective-permute-done.28.refs_2_
  173.7 1.7 collective-permute-start.30
  175.4 1.7 collective-permute-start.31
  178.1 1.7 collective-permute-done.31.refs_2_
  179.9 2.6 %collective-permute-done.32.refs_3_ = f32[8,128]{1,0:T(8,128)S(1)} collective-permute-done((f32[8,128]{1,0:T(8,128)S(1)}, f32[8,128]{1,0:T(8,128)S(1)}, u32[]{:S(2)}, u32[]{:S(2)}) %collective-permute-start.32) | collective-permute-done | bytes 4128 | tf_op jit(solution)/shard_map/ppermute | solution.py:27
  184.6 2.1 %collective-permute-done.33.refs_1_ = f32[8,128]{1,0:T(8,128)S(1)} collective-permute-done((f32[8,128]{1,0:T(8,128)S(1)}, f32[8,128]{1,0:T(8,128)S(1)}, u32[]{:S(2)}, u32[]{:S(2)}) %collective-permute-start.33) | collective-permute-done | bytes 4128 | tf_op jit(solution)/shard_map/ppermute | solution.py:27
  187.2 4.1 %merge.1 = (f32[160,1280]{1,0:T(8,128)}, f32[160,1280]{1,0:T(8,128)}) custom-call(s32[8]{0:T(128)S(1)} %copy-done.5, f32[8,128]{1,0:T(8,128)S(1)} %sum_of.5.refs_0_, f32[160,1280]{1,0:T(8,128)S(1)} %get-tuple-element.49.refs_0_.refs_1_, f32[160,1280]{1,0:T(8,128)S(1)} %get-tuple-element.39.refs_1_.refs_0_.refs_2_, ...), custom_call_target="tpu_custom_call" | custom-call | flops 1 | bytes 1 | tf_op jit(solution)/shard_map/merge/pallas_call | solution.py:81
  (77 shorter events, 28.7 us)
Async XLA Ops:
  12.4 4.4 %collective-permute-start.1 = (f32[352,1280]{1,0:T(8,128)}, f32[352,1280]{1,0:T(8,128)S(1)}, u32[]{:S(2)}, u32[]{:S(2)}) collective-permute-start(f32[352,1280]{1,0:T(8,128)} %get-tuple-element.37), channel_id=1, source_target_pairs={{0,1},{1,0},{2,3},{3,2},{4,5},{5,4},{6,7},{7,6},{8,9},{9,8},{10,11... | collective-permute-start | bytes 5406728 | tf_op jit(solution)/shard_map/ppermute | solution.py:27
  17.0 23.2 %collective-permute-start.2 = (f16[352,1280]{1,0:T(8,128)(2,1)S(1)}, f16[352,1280]{1,0:T(8,128)(2,1)S(1)}, u32[]{:S(2)}, u32[]{:S(2)}) collective-permute-start(f16[352,1280]{1,0:T(8,128)(2,1)S(1)} %get-tuple-element.68), channel_id=1, source_target_pairs={{0,2},{1,3},{2,0},{3,1},{4,6},{5,7},{6,4},{7,5},{8,10},{9,11},{10,... | collective-permute-start | bytes 2703368 | tf_op jit(solution)/shard_map/ppermute | solution.py:27
  19.6 23.1 %collective-permute-start = (bf16[176,1280]{1,0:T(8,128)(2,1)S(1)}, bf16[176,1280]{1,0:T(8,128)(2,1)S(1)}, u32[]{:S(2)}, u32[]{:S(2)}) collective-permute-start(bf16[176,1280]{1,0:T(8,128)(2,1)S(1)} %copy-done.7), channel_id=1, source_target_pairs={{0,16},{1,17},{2,18},{3,19},{4,20},{5,21},{6,22},{7,23},{8,24},{9,... | collective-permute-start | bytes 1351688 | tf_op jit(solution)/shard_map/ppermute | solution.py:27
  22.2 30.4 %collective-permute-start.5 = (bf16[352,1280]{1,0:T(8,128)(2,1)S(1)}, bf16[352,1280]{1,0:T(8,128)(2,1)S(1)}, u32[]{:S(2)}, u32[]{:S(2)}) collective-permute-start(bf16[352,1280]{1,0:T(8,128)(2,1)S(1)} %copy-done.6), channel_id=1, source_target_pairs={{0,8},{1,9},{2,10},{3,11},{4,12},{5,13},{6,14},{7,15},{8,0},{9,1},... | collective-permute-start | bytes 2703368 | tf_op jit(solution)/shard_map/ppermute | solution.py:27
  43.9 12.9 %collective-permute-start.3 = (bf16[352,1280]{1,0:T(8,128)(2,1)S(1)}, bf16[352,1280]{1,0:T(8,128)(2,1)S(1)}, u32[]{:S(2)}, u32[]{:S(2)}) collective-permute-start(bf16[352,1280]{1,0:T(8,128)(2,1)S(1)} %get-tuple-element.42.refs_0_), channel_id=1, source_target_pairs={{0,1},{1,0},{2,3},{3,2},{4,5},{5,4},{6,7},{7,6},{8,9},{9,8},{10,11... | collective-permute-start | bytes 2703368 | tf_op jit(solution)/shard_map/ppermute | solution.py:27
  52.6 30.7 %collective-permute-start.6 = (bf16[352,1280]{1,0:T(8,128)(2,1)S(1)}, bf16[352,1280]{1,0:T(8,128)(2,1)S(1)}, u32[]{:S(2)}, u32[]{:S(2)}) collective-permute-start(bf16[352,1280]{1,0:T(8,128)(2,1)S(1)} %get-tuple-element.42.refs_0_), channel_id=1, source_target_pairs={{0,8},{1,9},{2,10},{3,11},{4,12},{5,13},{6,14},{7,15},{8,0},{9,1},... | collective-permute-start | bytes 2703368 | tf_op jit(solution)/shard_map/ppermute | solution.py:27
  54.0 14.0 %collective-permute-start.7 = (bf16[176,1280]{1,0:T(8,128)(2,1)S(1)}, bf16[176,1280]{1,0:T(8,128)(2,1)S(1)}, u32[]{:S(2)}, u32[]{:S(2)}) collective-permute-start(bf16[176,1280]{1,0:T(8,128)(2,1)S(1)} %collective-permute-done.refs_0_), channel_id=1, source_target_pairs={{0,2},{1,3},{2,0},{3,1},{4,6},{5,7},{6,4},{7,5},{8,10},{9,11},{10,... | collective-permute-start | bytes 1351688 | tf_op jit(solution)/shard_map/ppermute | solution.py:27
  55.0 27.5 %collective-permute-start.8 = (bf16[176,1280]{1,0:T(8,128)(2,1)S(1)}, bf16[176,1280]{1,0:T(8,128)(2,1)S(1)}, u32[]{:S(2)}, u32[]{:S(2)}) collective-permute-start(bf16[176,1280]{1,0:T(8,128)(2,1)S(1)} %get-tuple-element.45), channel_id=1, source_target_pairs={{0,16},{1,17},{2,18},{3,19},{4,20},{5,21},{6,22},{7,23},{8,24},{9,... | collective-permute-start | bytes 1351688 | tf_op jit(solution)/shard_map/ppermute | solution.py:27
  66.5 16.8 %collective-permute-start.9 = (bf16[160,1280]{1,0:T(8,128)(2,1)S(1)}, bf16[160,1280]{1,0:T(8,128)(2,1)S(1)}, u32[]{:S(2)}, u32[]{:S(2)}) collective-permute-start(bf16[160,1280]{1,0:T(8,128)(2,1)S(1)} %get-tuple-element.43), channel_id=1, source_target_pairs={{0,4},{1,5},{2,6},{3,7},{4,0},{5,1},{6,2},{7,3},{8,12},{9,13},{10,... | collective-permute-start | bytes 1228808 | tf_op jit(solution)/shard_map/ppermute | solution.py:27
  68.1 18.5 %collective-permute-start.11 = (bf16[352,1280]{1,0:T(8,128)(2,1)S(1)}, bf16[352,1280]{1,0:T(8,128)(2,1)S(1)}, u32[]{:S(2)}, u32[]{:S(2)}) collective-permute-start(bf16[352,1280]{1,0:T(8,128)(2,1)S(1)} %collective-permute-done.5.refs_2_), channel_id=1, source_target_pairs={{0,1},{1,0},{2,3},{3,2},{4,5},{5,4},{6,7},{7,6},{8,9},{9,8},{10,11... | collective-permute-start | bytes 2703368 | tf_op jit(solution)/shard_map/ppermute | solution.py:27
  83.2 4.8 %collective-permute-start.10 = (bf16[352,1280]{1,0:T(8,128)(2,1)S(1)}, bf16[352,1280]{1,0:T(8,128)(2,1)S(1)}, u32[]{:S(2)}, u32[]{:S(2)}) collective-permute-start(bf16[352,1280]{1,0:T(8,128)(2,1)S(1)} %collective-permute-done.6.refs_0_), channel_id=1, source_target_pairs={{0,1},{1,0},{2,3},{3,2},{4,5},{5,4},{6,7},{7,6},{8,9},{9,8},{10,11... | collective-permute-start | bytes 2703368 | tf_op jit(solution)/shard_map/ppermute | solution.py:27
  83.2 14.7 %collective-permute-start.13 = (bf16[176,1280]{1,0:T(8,128)(2,1)S(1)}, bf16[176,1280]{1,0:T(8,128)(2,1)S(1)}, u32[]{:S(2)}, u32[]{:S(2)}) collective-permute-start(bf16[176,1280]{1,0:T(8,128)(2,1)S(1)} %collective-permute-done.8.refs_0_), channel_id=1, source_target_pairs={{0,2},{1,3},{2,0},{3,1},{4,6},{5,7},{6,4},{7,5},{8,10},{9,11},{10,... | collective-permute-start | bytes 1351688 | tf_op jit(solution)/shard_map/ppermute | solution.py:27
  84.5 13.5 %collective-permute-start.14 = (bf16[176,1280]{1,0:T(8,128)(2,1)S(1)}, bf16[176,1280]{1,0:T(8,128)(2,1)S(1)}, u32[]{:S(2)}, u32[]{:S(2)}) collective-permute-start(bf16[176,1280]{1,0:T(8,128)(2,1)S(1)} %collective-permute-done.8.refs_0_), channel_id=1, source_target_pairs={{0,8},{1,9},{2,10},{3,11},{4,12},{5,13},{6,14},{7,15},{8,0},{9,1},... | collective-permute-start | bytes 1351688 | tf_op jit(solution)/shard_map/ppermute | solution.py:27
  86.3 20.3 %collective-permute-start.15 = (bf16[176,1280]{1,0:T(8,128)(2,1)S(1)}, bf16[176,1280]{1,0:T(8,128)(2,1)S(1)}, u32[]{:S(2)}, u32[]{:S(2)}) collective-permute-start(bf16[176,1280]{1,0:T(8,128)(2,1)S(1)} %collective-permute-done.refs_0_), channel_id=1, source_target_pairs={{0,8},{1,9},{2,10},{3,11},{4,12},{5,13},{6,14},{7,15},{8,0},{9,1},... | collective-permute-start | bytes 1351688 | tf_op jit(solution)/shard_map/ppermute | solution.py:27
  86.5 11.4 %collective-permute-start.4 = (bf16[160,1280]{1,0:T(8,128)(2,1)S(1)}, bf16[160,1280]{1,0:T(8,128)(2,1)S(1)}, u32[]{:S(2)}, u32[]{:S(2)}) collective-permute-start(bf16[160,1280]{1,0:T(8,128)(2,1)S(1)} %get-tuple-element.40), channel_id=1, source_target_pairs={{0,4},{1,5},{2,6},{3,7},{4,0},{5,1},{6,2},{7,3},{8,12},{9,13},{10,... | collective-permute-start | bytes 1228808 | tf_op jit(solution)/shard_map/ppermute | solution.py:27
  88.0 22.4 %collective-permute-start.17 = (bf16[352,1280]{1,0:T(8,128)(2,1)S(1)}, bf16[352,1280]{1,0:T(8,128)(2,1)S(1)}, u32[]{:S(2)}, u32[]{:S(2)}) collective-permute-start(bf16[352,1280]{1,0:T(8,128)(2,1)S(1)} %join.4.refs_3_), channel_id=1, source_target_pairs={{0,1},{1,0},{2,3},{3,2},{4,5},{5,4},{6,7},{7,6},{8,9},{9,8},{10,11... | collective-permute-start | bytes 2703368 | tf_op jit(solution)/shard_map/ppermute | solution.py:27
  106.7 5.6 %collective-permute-start.16 = (bf16[352,1280]{1,0:T(8,128)(2,1)S(1)}, bf16[352,1280]{1,0:T(8,128)(2,1)S(1)}, u32[]{:S(2)}, u32[]{:S(2)}) collective-permute-start(bf16[352,1280]{1,0:T(8,128)(2,1)S(1)} %join.5.refs_1_), channel_id=1, source_target_pairs={{0,1},{1,0},{2,3},{3,2},{4,5},{5,4},{6,7},{7,6},{8,9},{9,8},{10,11... | collective-permute-start | bytes 2703368 | tf_op jit(solution)/shard_map/ppermute | solution.py:27
  106.8 22.1 %collective-permute-start.20 = (bf16[176,1280]{1,0:T(8,128)(2,1)S(1)}, bf16[176,1280]{1,0:T(8,128)(2,1)S(1)}, u32[]{:S(2)}, u32[]{:S(2)}) collective-permute-start(bf16[176,1280]{1,0:T(8,128)(2,1)S(1)} %collective-permute-done.14.refs_0_), channel_id=1, source_target_pairs={{0,2},{1,3},{2,0},{3,1},{4,6},{5,7},{6,4},{7,5},{8,10},{9,11},{10,... | collective-permute-start | bytes 1351688 | tf_op jit(solution)/shard_map/ppermute | solution.py:27
  107.6 21.6 %collective-permute-start.22 = (bf16[176,1280]{1,0:T(8,128)(2,1)S(1)}, bf16[176,1280]{1,0:T(8,128)(2,1)S(1)}, u32[]{:S(2)}, u32[]{:S(2)}) collective-permute-start(bf16[176,1280]{1,0:T(8,128)(2,1)S(1)} %collective-permute-done.15.refs_0_), channel_id=1, source_target_pairs={{0,2},{1,3},{2,0},{3,1},{4,6},{5,7},{6,4},{7,5},{8,10},{9,11},{10,... | collective-permute-start | bytes 1351688 | tf_op jit(solution)/shard_map/ppermute | solution.py:27
  108.9 13.2 %collective-permute-start.12 = (bf16[160,1280]{1,0:T(8,128)(2,1)S(1)}, bf16[160,1280]{1,0:T(8,128)(2,1)S(1)}, u32[]{:S(2)}, u32[]{:S(2)}) collective-permute-start(bf16[160,1280]{1,0:T(8,128)(2,1)S(1)} %get-tuple-element.48), channel_id=1, source_target_pairs={{0,4},{1,5},{2,6},{3,7},{4,0},{5,1},{6,2},{7,3},{8,12},{9,13},{10,... | collective-permute-start | bytes 1228808 | tf_op jit(solution)/shard_map/ppermute | solution.py:27
  110.5 18.5 %collective-permute-start.19 = (bf16[160,1280]{1,0:T(8,128)(2,1)S(1)}, bf16[160,1280]{1,0:T(8,128)(2,1)S(1)}, u32[]{:S(2)}, u32[]{:S(2)}) collective-permute-start(bf16[160,1280]{1,0:T(8,128)(2,1)S(1)} %get-tuple-element.51), channel_id=1, source_target_pairs={{0,4},{1,5},{2,6},{3,7},{4,0},{5,1},{6,2},{7,3},{8,12},{9,13},{10,... | collective-permute-start | bytes 1228808 | tf_op jit(solution)/shard_map/ppermute | solution.py:27
  129.0 5.2 %collective-permute-start.21 = (bf16[352,1280]{1,0:T(8,128)(2,1)S(1)}, bf16[352,1280]{1,0:T(8,128)(2,1)S(1)}, u32[]{:S(2)}, u32[]{:S(2)}) collective-permute-start(bf16[352,1280]{1,0:T(8,128)(2,1)S(1)} %join.6.refs_1_), channel_id=1, source_target_pairs={{0,1},{1,0},{2,3},{3,2},{4,5},{5,4},{6,7},{7,6},{8,9},{9,8},{10,11... | collective-permute-start | bytes 2703368 | tf_op jit(solution)/shard_map/ppermute | solution.py:27
  129.3 4.9 %collective-permute-start.23 = (bf16[352,1280]{1,0:T(8,128)(2,1)S(1)}, bf16[352,1280]{1,0:T(8,128)(2,1)S(1)}, u32[]{:S(2)}, u32[]{:S(2)}) collective-permute-start(bf16[352,1280]{1,0:T(8,128)(2,1)S(1)} %join.7.refs_3_), channel_id=1, source_target_pairs={{0,1},{1,0},{2,3},{3,2},{4,5},{5,4},{6,7},{7,6},{8,9},{9,8},{10,11... | collective-permute-start | bytes 2703368 | tf_op jit(solution)/shard_map/ppermute | solution.py:27
  129.7 21.1 %collective-permute-start.25 = (bf16[160,1280]{1,0:T(8,128)(2,1)S(1)}, bf16[160,1280]{1,0:T(8,128)(2,1)S(1)}, u32[]{:S(2)}, u32[]{:S(2)}) collective-permute-start(bf16[160,1280]{1,0:T(8,128)(2,1)S(1)} %get-tuple-element.59), channel_id=1, source_target_pairs={{0,4},{1,5},{2,6},{3,7},{4,0},{5,1},{6,2},{7,3},{8,12},{9,13},{10,... | collective-permute-start | bytes 1228808 | tf_op jit(solution)/shard_map/ppermute | solution.py:27
  131.3 19.5 %collective-permute-start.18 = (bf16[160,1280]{1,0:T(8,128)(2,1)S(1)}, bf16[160,1280]{1,0:T(8,128)(2,1)S(1)}, u32[]{:S(2)}, u32[]{:S(2)}) collective-permute-start(bf16[160,1280]{1,0:T(8,128)(2,1)S(1)} %get-tuple-element.56), channel_id=1, source_target_pairs={{0,4},{1,5},{2,6},{3,7},{4,0},{5,1},{6,2},{7,3},{8,12},{9,13},{10,... | collective-permute-start | bytes 1228808 | tf_op jit(solution)/shard_map/ppermute | solution.py:27
  144.1 15.4 %collective-permute-start.26 = (bf16[160,1280]{1,0:T(8,128)(2,1)S(1)}, bf16[160,1280]{1,0:T(8,128)(2,1)S(1)}, u32[]{:S(2)}, u32[]{:S(2)}) collective-permute-start(bf16[160,1280]{1,0:T(8,128)(2,1)S(1)} %get-tuple-element.67), channel_id=1, source_target_pairs={{0,4},{1,5},{2,6},{3,7},{4,0},{5,1},{6,2},{7,3},{8,12},{9,13},{10,... | collective-permute-start | bytes 1228808 | tf_op jit(solution)/shard_map/ppermute | solution.py:27
  145.7 21.8 %collective-permute-start.24 = (bf16[160,1280]{1,0:T(8,128)(2,1)S(1)}, bf16[160,1280]{1,0:T(8,128)(2,1)S(1)}, u32[]{:S(2)}, u32[]{:S(2)}) collective-permute-start(bf16[160,1280]{1,0:T(8,128)(2,1)S(1)} %get-tuple-element.64), channel_id=1, source_target_pairs={{0,4},{1,5},{2,6},{3,7},{4,0},{5,1},{6,2},{7,3},{8,12},{9,13},{10,... | collective-permute-start | bytes 1228808 | tf_op jit(solution)/shard_map/ppermute | solution.py:27
  169.3 3.7 %collective-permute-start.28 = (f32[8,128]{1,0:T(8,128)S(1)}, f32[8,128]{1,0:T(8,128)S(1)}, u32[]{:S(2)}, u32[]{:S(2)}) collective-permute-start(f32[8,128]{1,0:T(8,128)S(1)} %products.11.refs_0_), channel_id=1, source_target_pairs={{0,2},{1,3},{2,0},{3,1},{4,6},{5,7},{6,4},{7,5},{8,10},{9,11},{10,... | collective-permute-start | bytes 12296 | tf_op jit(solution)/shard_map/ppermute | solution.py:27
  173.7 4.5 %collective-permute-start.30 = (f32[8,128]{1,0:T(8,128)S(1)}, f32[8,128]{1,0:T(8,128)S(1)}, u32[]{:S(2)}, u32[]{:S(2)}) collective-permute-start(f32[8,128]{1,0:T(8,128)S(1)} %sum_of.3.refs_0_), channel_id=1, source_target_pairs={{0,8},{1,9},{2,10},{3,11},{4,12},{5,13},{6,14},{7,15},{8,0},{9,1},... | collective-permute-start | bytes 12296 | tf_op jit(solution)/shard_map/ppermute | solution.py:27
  175.4 4.5 %collective-permute-start.31 = (f32[8,128]{1,0:T(8,128)S(1)}, f32[8,128]{1,0:T(8,128)S(1)}, u32[]{:S(2)}, u32[]{:S(2)}) collective-permute-start(f32[8,128]{1,0:T(8,128)S(1)} %sum_of.3.refs_0_), channel_id=1, source_target_pairs={{0,16},{1,17},{2,18},{3,19},{4,20},{5,21},{6,22},{7,23},{8,24},{9,... | collective-permute-start | bytes 12296 | tf_op jit(solution)/shard_map/ppermute | solution.py:27
  177.1 5.4 %collective-permute-start.32 = (f32[8,128]{1,0:T(8,128)S(1)}, f32[8,128]{1,0:T(8,128)S(1)}, u32[]{:S(2)}, u32[]{:S(2)}) collective-permute-start(f32[8,128]{1,0:T(8,128)S(1)} %sum_of.3.refs_0_), channel_id=1, source_target_pairs={{0,24},{1,25},{2,26},{3,27},{4,28},{5,29},{6,30},{7,31},{8,16},{9,... | collective-permute-start | bytes 12296 | tf_op jit(solution)/shard_map/ppermute | solution.py:27
  183.0 3.7 %collective-permute-start.33 = (f32[8,128]{1,0:T(8,128)S(1)}, f32[8,128]{1,0:T(8,128)S(1)}, u32[]{:S(2)}, u32[]{:S(2)}) collective-permute-start(f32[8,128]{1,0:T(8,128)S(1)} %sum_of.4.refs_0_), channel_id=1, source_target_pairs={{0,4},{1,5},{2,6},{3,7},{4,0},{5,1},{6,2},{7,3},{8,12},{9,13},{10,... | collective-permute-start | bytes 12296 | tf_op jit(solution)/shard_map/ppermute | solution.py:27
  (10 other events, 91.3 us)

commit v12 on v11

--- a/solution.py
+++ b/solution.py
@@ -108,7 +108,7 @@
 
 
 def forward_kernel(
-    steps, place_ref, rows_ref, w_in_ref, w_out_ref, out_ref, near_ref, half_ref, part_ref, hidden
+    steps, place_ref, rows_ref, w_in_ref, w_out_ref, out_ref, near_ref, part_ref, hidden
 ):
     step = pl.program_id(0)
     half = out_ref.shape[0]
@@ -125,7 +125,6 @@
 
     @pl.when(step == 0)
     def _():
-        half_ref[...] = rows_ref[pl.ds(row_start(place_ref, half_ref, NEAR), half), :]
         part_ref[...] = rows_ref[pl.ds(row_start(place_ref, part_ref, PART), part_ref.shape[0]), :]
 
     @pl.when(step == steps)
@@ -150,7 +149,6 @@
         [
             jax.ShapeDtypeStruct((rows // 2, depth), jnp.float32),
             jax.ShapeDtypeStruct((rows // 2, width), jnp.bfloat16),
-            jax.ShapeDtypeStruct((rows // 2, depth), jnp.bfloat16),
             jax.ShapeDtypeStruct((part_rows, depth), jnp.bfloat16),
         ],
         vmem=vmem_most,
@@ -163,7 +161,6 @@
         out_specs=[
             pl.BlockSpec((rows // 2, out_tile), lambda n, s: (0, last(n))),
             pl.BlockSpec((rows // 2, width), whole),
-            pl.BlockSpec((rows // 2, depth), whole),
             pl.BlockSpec((part_rows, depth), whole),
         ],
         scratch_shapes=[pltpu.VMEM((rows, width), jnp.bfloat16)],
@@ -494,13 +491,9 @@
         ]
     ).astype(jnp.int32)
 
-    first_bit = bits[0]
-    send, hidden_near, own_half, own_part = forward(place, part_rows, inputs, w_in, w_out)
+    send, hidden_near, own_part = forward(place, part_rows, inputs, w_in, w_out)
     got = from_mask(send, 0, 1)
-
-    inputs_of = {
-        bit: from_mask(own_part if bit == first_bit else own_half, bit * others, 0) for bit in bits
-    }
+    inputs_of = {bit: from_mask(own_part, bit * others, 0) for bit in bits}
 
     summed = product(place, hidden_near, w_out) + got
     most = 24.0 * 0.15625 * 0.078125 * inputs.shape[1] * w_in.shape[1] * shards
@@ -515,11 +508,9 @@
         sum(sums[:-1]),
         sums[-1],
         targets,
-        (inputs_of[first_bit],),
-    )
-    errors_of = {first_bit: from_mask(error_piece, first_bit * others, 0)}
-    for bit in bits[1:]:
-        errors_of[bit] = from_mask(ordered(error, inputs_of[bit]), bit * others, 0)
+        tuple(inputs_of.values()),
+    )
+    errors_of = {bit: from_mask(error_piece, bit * others, 0) for bit in bits}
 
     def to_half(piece, *before):
         for bit in reversed(range(1, shard_levels)):
@@ -530,26 +521,21 @@
     def both_halves(half):
         return [(half, NEAR), (from_mask(half, 0, 1), FAR)]
 
-    slots, labels, known, sent = [], [], [], []
+    slots, labels, known, sent, halves = [], [], [], [], {}
     totals = jnp.zeros((8, 128), jnp.float32)
     masks = [m for m in range(members) if not m & swap]
     for n, m in enumerate(masks):
         if n == 0:
             half = error
-        elif not m & first_bit:
-            half = errors_of[m] = ordered(
-                errors_of[m], sent[0], inputs_half, errors_of[first_bit], slots[1][0]
-            )
-            other_inputs = inputs_of[m]
-        elif m == first_bit:
-            for bit in bits[1:]:
-                ready = ordered(inputs_of[first_bit], errors_of[bit])
-                inputs_of[first_bit | bit] = from_mask(ready, bit * others, 0)
-                ready = ordered(errors_of[first_bit], errors_of[bit])
-                errors_of[first_bit | bit] = from_mask(ready, bit * others, 0)
-            before = [of[first_bit | bit] for bit in bits[1:] for of in (errors_of, inputs_of)]
-            half = to_half(ordered(errors_of[m], sent[0]), sent[-1], *slots[1], *before)
-            other_inputs = inputs_half
+        elif m in bits:
+            errors_of[m] = ordered(errors_of[m], sent[0])
+            top, of = (bits[0], inputs_of) if n == 1 else (m, errors_of)
+            both = [top | bit for bit in bits[1:]]
+            for to in both:
+                of[to] = from_mask(ordered(of[top], errors_of[m]), (to ^ top) * others, 0)
+            before = [of[to] for to in both] + list(slots[1][: 2 * n - 1]) + sent[1:]
+            half = to_half(errors_of[m], *before)
+            other_inputs = halves[m]
         else:
             other_inputs, half = (
                 to_half(ordered(of[m], sent[-2]), sent[-1], *slots[2 * n - 3])
@@ -566,7 +552,8 @@
             known[-2:-1],
         )
         if n == 0:
-            inputs_half = to_half(inputs_of[first_bit], send[0])
+            for bit in bits:
+                halves[bit] = to_half(inputs_of[bit], send[0], errors_of[bits[0]], *halves.values())
         sent.append(send[0])
         slots.append((first, second))
         labels.append(m)

time: 192 us -> 177 us (0.922)
  waiting for transfers between devices: 79.9 us -> 64.9 us
    ppermute x34 -> x36, waiting for transfers between devices: 79.9 us -> 64.9 us  [from_mask(): return lax.ppermute(value, ('dp', 'tensor'), pairs)]
    ppermute x34 -> x36, starting transfers between devices: 34.7 us -> 35.1 us  [from_mask(): return lax.ppermute(value, ('dp', 'tensor'), pairs)]
    pallas_call x21 -> x23, Pallas kernels: 73.5 us -> 73.2 us  [call(): pl.pallas_call(body, grid_spec=pltpu.PrefetchScalarGridSpec(num_scalar_pr...]
  transfers between devices with their start and end apart: 34 -> 36, of which waited for: 16 -> 21; matrix products, arithmetic and copies ran while one was open for 0% -> 0% of each run, Pallas kernels for 29% -> 31%
where the time goes in v12:
time: 177 us; the launch traced here: 176 us
  Pallas kernels  73.2 us (41%)
  waiting for transfers between devices  64.9 us (37%)
  starting transfers between devices  35.1 us (20%)
  local copies, waits for them, and re-layouts  1.8 us (1%)
    pallas_call x23, Pallas kernels, call(): pl.pallas_call(body, grid_spec=pltpu.PrefetchScalarGridSpec(num_scalar_pr...  73.2 us
    ppermute x36, waiting for transfers between devices, from_mask(): return lax.ppermute(value, ('dp', 'tensor'), pairs)  64.9 us
    ppermute x36, starting transfers between devices, from_mask(): return lax.ppermute(value, ('dp', 'tensor'), pairs)  35.1 us
  transfers between devices with their start and end apart: 36, of which 21 were waited for; matrix products, arithmetic and copies ran while one was open for 0% of the time, Pallas kernels for 31%

profile of v12, /device:TPU:0, one launch (start us, length us, event | category | flops | bytes accessed | tf_op | source)
XLA Modules:
  0.0 176.4 jit_solution(16049701495691770286)
XLA Ops:
  1.3 10.7 %forward.1 = (f32[352,1280]{1,0:T(8,128)}, bf16[352,1280]{1,0:T(8,128)(2,1)}, bf16[176,1280]{1,0:T(8,128)(2,1)}) custom-call(s32[8]{0:T(128)} %stack.35.place_ref, bf16[704,1280]{1,0:T(8,128)(2,1)} %refs_2_.3, bf16[1280,1280]{1,0:T(8,128)(2,1)} %refs_5_.5, bf16[1280,1280]{1,0:T(8,128)(2,1)} %refs_6_.3), custom_call_target="tpu_custom_call" | custom-call | flops 1 | bytes 1 | tf_op jit(solution)/shard_map/forward/pallas_call | solution.py:81
  13.6 2.7 %product.1 = f32[352,1280]{1,0:T(8,128)S(1)} custom-call(s32[8]{0:T(128)S(1)} %copy-done.5, bf16[352,1280]{1,0:T(8,128)(2,1)S(1)} %copy-done.4, bf16[1280,1280]{1,0:T(8,128)(2,1)S(1)} %copy-done), custom_call_target="tpu_custom_call" | custom-call | flops 1 | bytes 1 | tf_op jit(solution)/shard_map/product/pallas_call | solution.py:81
  16.6 2.6 %collective-permute-start.3 = (f16[352,1280]{1,0:T(8,128)(2,1)S(1)}, f16[352,1280]{1,0:T(8,128)(2,1)S(1)}, u32[]{:S(2)}, u32[]{:S(2)}) collective-permute-start(f16[352,1280]{1,0:T(8,128)(2,1)S(1)} %get-tuple-element.68), channel_id=1, source_target_pairs={{0,2},{1,3},{2,0},{3,1},{4,6},{5,7},{6,4},{7,5},{8,10},{9,11},{10,... | collective-permute-start | bytes 2703368 | tf_op jit(solution)/shard_map/ppermute | solution.py:27
  19.2 2.6 %collective-permute-start = (bf16[176,1280]{1,0:T(8,128)(2,1)S(1)}, bf16[176,1280]{1,0:T(8,128)(2,1)S(1)}, u32[]{:S(2)}, u32[]{:S(2)}) collective-permute-start(bf16[176,1280]{1,0:T(8,128)(2,1)S(1)} %copy-done.6), channel_id=1, source_target_pairs={{0,16},{1,17},{2,18},{3,19},{4,20},{5,21},{6,22},{7,23},{8,24},{9,... | collective-permute-start | bytes 1351688 | tf_op jit(solution)/shard_map/ppermute | solution.py:27
  21.7 1.6 collective-permute-start.1
  23.3 16.5 %collective-permute-done.3 = f16[352,1280]{1,0:T(8,128)(2,1)S(1)} collective-permute-done((f16[352,1280]{1,0:T(8,128)(2,1)S(1)}, f16[352,1280]{1,0:T(8,128)(2,1)S(1)}, u32[]{:S(2)}, u32[]{:S(2)}) %collective-permute-start.3) | collective-permute-done | bytes 901152 | tf_op jit(solution)/shard_map/ppermute | solution.py:27
  40.0 2.3 %collective-permute-done.refs_0_ = bf16[176,1280]{1,0:T(8,128)(2,1)S(1)} collective-permute-done((bf16[176,1280]{1,0:T(8,128)(2,1)S(1)}, bf16[176,1280]{1,0:T(8,128)(2,1)S(1)}, u32[]{:S(2)}, u32[]{:S(2)}) %collective-permute-start) | collective-permute-done | bytes 450592 | tf_op jit(solution)/shard_map/ppermute | solution.py:27
  46.1 2.3 %collective-permute-start.12 = (bf16[176,1280]{1,0:T(8,128)(2,1)S(1)}, bf16[176,1280]{1,0:T(8,128)(2,1)S(1)}, u32[]{:S(2)}, u32[]{:S(2)}) collective-permute-start(bf16[176,1280]{1,0:T(8,128)(2,1)S(1)} %get-tuple-element.41), channel_id=1, source_target_pairs={{0,16},{1,17},{2,18},{3,19},{4,20},{5,21},{6,22},{7,23},{8,24},{9,... | collective-permute-start | bytes 1351688 | tf_op jit(solution)/shard_map/ppermute | solution.py:27
  49.5 9.6 %gradient.4 = (f32[160,1280]{1,0:T(8,128)S(1)}, f32[160,1280]{1,0:T(8,128)S(1)}, bf16[160,1280]{1,0:T(8,128)(2,1)S(1)}, bf16[160,1280]{1,0:T(8,128)(2,1)S(1)}) custom-call(s32[8]{0:T(128)S(1)} %copy-done.5, bf16[352,1280]{1,0:T(8,128)(2,1)S(1)} %get-tuple-element.38.refs_0_, bf16[352,1280]{1,0:T(8,128)(2,1)S(1)} %collective-permute-done.4.refs_1_, ...), custom_call_target="tpu_custom_call" | custom-call | flops 1 | bytes 1 | tf_op jit(solution)/shard_map/gradient/pallas_call | solution.py:81
  59.2 5.7 %collective-permute-done.6.refs_0_ = bf16[176,1280]{1,0:T(8,128)(2,1)S(1)} collective-permute-done((bf16[176,1280]{1,0:T(8,128)(2,1)S(1)}, bf16[176,1280]{1,0:T(8,128)(2,1)S(1)}, u32[]{:S(2)}, u32[]{:S(2)}) %collective-permute-start.6) | collective-permute-done | bytes 450592 | tf_op jit(solution)/shard_map/ppermute | solution.py:27
  67.2 1.7 collective-permute-done.12.refs_0_
  69.2 7.2 %collective-permute-done.9.refs_2_.refs_1_.refs_3_ = bf16[160,1280]{1,0:T(8,128)(2,1)S(1)} collective-permute-done((bf16[160,1280]{1,0:T(8,128)(2,1)S(1)}, bf16[160,1280]{1,0:T(8,128)(2,1)S(1)}, u32[]{:S(2)}, u32[]{:S(2)}) %collective-permute-start.9) | collective-permute-done | bytes 409632 | tf_op jit(solution)/shard_map/ppermute | solution.py:27
  76.9 1.6 collective-permute-done.8.refs_0_
  81.3 9.9 %gradient.5 = (f32[160,1280]{1,0:T(8,128)S(1)}, f32[160,1280]{1,0:T(8,128)S(1)}, bf16[160,1280]{1,0:T(8,128)(2,1)S(1)}, bf16[160,1280]{1,0:T(8,128)(2,1)S(1)}) custom-call(s32[8]{0:T(128)S(1)} %copy-done.5, bf16[352,1280]{1,0:T(8,128)(2,1)S(1)} %join.6.refs_0_, bf16[352,1280]{1,0:T(8,128)(2,1)S(1)} %collective-permute-done.10.refs_1_, ...), custom_call_target="tpu_custom_call" | custom-call | flops 1 | bytes 1 | tf_op jit(solution)/shard_map/gradient/pallas_call | solution.py:81
  97.9 9.7 %gradient.6 = (f32[160,1280]{1,0:T(8,128)S(1)}, f32[160,1280]{1,0:T(8,128)S(1)}, bf16[160,1280]{1,0:T(8,128)(2,1)S(1)}, bf16[160,1280]{1,0:T(8,128)(2,1)S(1)}) custom-call(s32[8]{0:T(128)S(1)} %copy-done.5, f32[8,128]{1,0:T(8,128)S(1)} %products.6.refs_0_.refs_8_, bf16[352,1280]{1,0:T(8,128)(2,1)S(1)} %join.9.refs_1_, ...), custom_call_target="tpu_custom_call" | custom-call | flops 1 | bytes 1 | tf_op jit(solution)/shard_map/gradient/pallas_call | solution.py:81
  107.7 6.8 %collective-permute-done.21.refs_6_.refs_3_.refs_7_ = bf16[160,1280]{1,0:T(8,128)(2,1)S(1)} collective-permute-done((bf16[160,1280]{1,0:T(8,128)(2,1)S(1)}, bf16[160,1280]{1,0:T(8,128)(2,1)S(1)}, u32[]{:S(2)}, u32[]{:S(2)}) %collective-permute-start.21) | collective-permute-done | bytes 409632 | tf_op jit(solution)/shard_map/ppermute | solution.py:27
  117.3 2.4 %products.7.refs_0_.refs_12_ = f32[8,128]{1,0:T(8,128)S(1)} custom-call(s32[8]{0:T(128)S(1)} %copy-done.5, f32[160,1280]{1,0:T(8,128)S(1)} %get-tuple-element.50.refs_0_.refs_1_, f32[160,1280]{1,0:T(8,128)S(1)} %get-tuple-element.39.refs_1_.refs_0_.refs_2_, bf16[160,1280]{1,0:T(8,128)(2,1)S(1)} %collective-permute-done.9.refs_2_.refs_1_.refs_3_, ...), custom_call_target="tpu_custom_call" | custom-call | flops 1 | bytes 1 | tf_op jit(solution)/shard_map/products/pallas_call | solution.py:81
  119.7 9.9 %gradient.7 = (f32[160,1280]{1,0:T(8,128)S(1)}, f32[160,1280]{1,0:T(8,128)S(1)}, bf16[160,1280]{1,0:T(8,128)(2,1)S(1)}, bf16[160,1280]{1,0:T(8,128)(2,1)S(1)}) custom-call(s32[8]{0:T(128)S(1)} %copy-done.5, f32[8,128]{1,0:T(8,128)S(1)} %products.7.refs_0_.refs_12_, bf16[352,1280]{1,0:T(8,128)(2,1)S(1)} %join.10.refs_1_, ...), custom_call_target="tpu_custom_call" | custom-call | flops 1 | bytes 1 | tf_op jit(solution)/shard_map/gradient/pallas_call | solution.py:81
  129.7 1.6 collective-permute-start.28
  131.8 4.6 %collective-permute-done.20.refs_11_.refs_5_.refs_12_ = bf16[160,1280]{1,0:T(8,128)(2,1)S(1)} collective-permute-done((bf16[160,1280]{1,0:T(8,128)(2,1)S(1)}, bf16[160,1280]{1,0:T(8,128)(2,1)S(1)}, u32[]{:S(2)}, u32[]{:S(2)}) %collective-permute-start.20) | collective-permute-done | bytes 409632 | tf_op jit(solution)/shard_map/ppermute | solution.py:27
  136.3 3.4 %products.8.refs_14_ = f32[8,128]{1,0:T(8,128)S(1)} custom-call(s32[8]{0:T(128)S(1)} %copy-done.5, f32[160,1280]{1,0:T(8,128)S(1)} %get-tuple-element.50.refs_0_.refs_1_, f32[160,1280]{1,0:T(8,128)S(1)} %get-tuple-element.39.refs_1_.refs_0_.refs_2_, bf16[160,1280]{1,0:T(8,128)(2,1)S(1)} %collective-permute-done.9.refs_2_.refs_1_.refs_3_, ...), custom_call_target="tpu_custom_call" | custom-call | flops 1 | bytes 1 | tf_op jit(solution)/shard_map/products/pallas_call | solution.py:81
  139.8 2.8 %products.9.refs_8_ = f32[8,128]{1,0:T(8,128)S(1)} custom-call(s32[8]{0:T(128)S(1)} %copy-done.5, f32[160,1280]{1,0:T(8,128)S(1)} %get-tuple-element.50.refs_0_.refs_1_, f32[160,1280]{1,0:T(8,128)S(1)} %get-tuple-element.39.refs_1_.refs_0_.refs_2_, bf16[160,1280]{1,0:T(8,128)(2,1)S(1)} %collective-permute-done.9.refs_2_.refs_1_.refs_3_, ...), custom_call_target="tpu_custom_call" | custom-call | flops 1 | bytes 1 | tf_op jit(solution)/shard_map/products/pallas_call | solution.py:81
  142.6 2.5 %collective-permute-done.28.refs_7_.refs_15_ = bf16[160,1280]{1,0:T(8,128)(2,1)S(1)} collective-permute-done((bf16[160,1280]{1,0:T(8,128)(2,1)S(1)}, bf16[160,1280]{1,0:T(8,128)(2,1)S(1)}, u32[]{:S(2)}, u32[]{:S(2)}) %collective-permute-start.28) | collective-permute-done | bytes 409632 | tf_op jit(solution)/shard_map/ppermute | solution.py:27
  145.1 1.6 products.10.refs_8_
  146.8 6.3 %collective-permute-done.26.refs_7_.refs_16_ = bf16[160,1280]{1,0:T(8,128)(2,1)S(1)} collective-permute-done((bf16[160,1280]{1,0:T(8,128)(2,1)S(1)}, bf16[160,1280]{1,0:T(8,128)(2,1)S(1)}, u32[]{:S(2)}, u32[]{:S(2)}) %collective-permute-start.26) | collective-permute-done | bytes 409632 | tf_op jit(solution)/shard_map/ppermute | solution.py:27
  153.1 1.6 products.11.refs_0_
  156.7 1.8 %collective-permute-done.30.refs_2_ = f32[8,128]{1,0:T(8,128)S(1)} collective-permute-done((f32[8,128]{1,0:T(8,128)S(1)}, f32[8,128]{1,0:T(8,128)S(1)}, u32[]{:S(2)}, u32[]{:S(2)}) %collective-permute-start.30) | collective-permute-done | bytes 4128 | tf_op jit(solution)/shard_map/ppermute | solution.py:27
  162.1 1.8 %collective-permute-start.34 = (f32[8,128]{1,0:T(8,128)S(1)}, f32[8,128]{1,0:T(8,128)S(1)}, u32[]{:S(2)}, u32[]{:S(2)}) collective-permute-start(f32[8,128]{1,0:T(8,128)S(1)} %sum_of.3.refs_0_), channel_id=1, source_target_pairs={{0,24},{1,25},{2,26},{3,27},{4,28},{5,29},{6,30},{7,31},{8,16},{9,... | collective-permute-start | bytes 12296 | tf_op jit(solution)/shard_map/ppermute | solution.py:27
  165.2 2.3 %collective-permute-done.34.refs_3_ = f32[8,128]{1,0:T(8,128)S(1)} collective-permute-done((f32[8,128]{1,0:T(8,128)S(1)}, f32[8,128]{1,0:T(8,128)S(1)}, u32[]{:S(2)}, u32[]{:S(2)}) %collective-permute-start.34) | collective-permute-done | bytes 4128 | tf_op jit(solution)/shard_map/ppermute | solution.py:27
  168.0 1.6 collective-permute-start.35
  169.6 2.1 %collective-permute-done.35.refs_1_ = f32[8,128]{1,0:T(8,128)S(1)} collective-permute-done((f32[8,128]{1,0:T(8,128)S(1)}, f32[8,128]{1,0:T(8,128)S(1)}, u32[]{:S(2)}, u32[]{:S(2)}) %collective-permute-start.35) | collective-permute-done | bytes 4128 | tf_op jit(solution)/shard_map/ppermute | solution.py:27
  172.3 4.1 %merge.1 = (f32[160,1280]{1,0:T(8,128)}, f32[160,1280]{1,0:T(8,128)}) custom-call(s32[8]{0:T(128)S(1)} %copy-done.5, f32[8,128]{1,0:T(8,128)S(1)} %sum_of.5.refs_0_, f32[160,1280]{1,0:T(8,128)S(1)} %get-tuple-element.50.refs_0_.refs_1_, f32[160,1280]{1,0:T(8,128)S(1)} %get-tuple-element.39.refs_1_.refs_0_.refs_2_, ...), custom_call_target="tpu_custom_call" | custom-call | flops 1 | bytes 1 | tf_op jit(solution)/shard_map/merge/pallas_call | solution.py:81
  (81 shorter events, 31.2 us)
Async XLA Ops:
  11.9 4.4 %collective-permute-start.2 = (f32[352,1280]{1,0:T(8,128)}, f32[352,1280]{1,0:T(8,128)S(1)}, u32[]{:S(2)}, u32[]{:S(2)}) collective-permute-start(f32[352,1280]{1,0:T(8,128)} %get-tuple-element.37), channel_id=1, source_target_pairs={{0,1},{1,0},{2,3},{3,2},{4,5},{5,4},{6,7},{7,6},{8,9},{9,8},{10,11... | collective-permute-start | bytes 5406728 | tf_op jit(solution)/shard_map/ppermute | solution.py:27
  16.6 23.2 %collective-permute-start.3 = (f16[352,1280]{1,0:T(8,128)(2,1)S(1)}, f16[352,1280]{1,0:T(8,128)(2,1)S(1)}, u32[]{:S(2)}, u32[]{:S(2)}) collective-permute-start(f16[352,1280]{1,0:T(8,128)(2,1)S(1)} %get-tuple-element.68), channel_id=1, source_target_pairs={{0,2},{1,3},{2,0},{3,1},{4,6},{5,7},{6,4},{7,5},{8,10},{9,11},{10,... | collective-permute-start | bytes 2703368 | tf_op jit(solution)/shard_map/ppermute | solution.py:27
  19.2 23.1 %collective-permute-start = (bf16[176,1280]{1,0:T(8,128)(2,1)S(1)}, bf16[176,1280]{1,0:T(8,128)(2,1)S(1)}, u32[]{:S(2)}, u32[]{:S(2)}) collective-permute-start(bf16[176,1280]{1,0:T(8,128)(2,1)S(1)} %copy-done.6), channel_id=1, source_target_pairs={{0,16},{1,17},{2,18},{3,19},{4,20},{5,21},{6,22},{7,23},{8,24},{9,... | collective-permute-start | bytes 1351688 | tf_op jit(solution)/shard_map/ppermute | solution.py:27
  21.7 20.7 %collective-permute-start.1 = (bf16[176,1280]{1,0:T(8,128)(2,1)S(1)}, bf16[176,1280]{1,0:T(8,128)(2,1)S(1)}, u32[]{:S(2)}, u32[]{:S(2)}) collective-permute-start(bf16[176,1280]{1,0:T(8,128)(2,1)S(1)} %copy-done.6), channel_id=1, source_target_pairs={{0,8},{1,9},{2,10},{3,11},{4,12},{5,13},{6,14},{7,15},{8,0},{9,1},... | collective-permute-start | bytes 1351688 | tf_op jit(solution)/shard_map/ppermute | solution.py:27
  43.6 6.0 %collective-permute-start.4 = (bf16[352,1280]{1,0:T(8,128)(2,1)S(1)}, bf16[352,1280]{1,0:T(8,128)(2,1)S(1)}, u32[]{:S(2)}, u32[]{:S(2)}) collective-permute-start(bf16[352,1280]{1,0:T(8,128)(2,1)S(1)} %get-tuple-element.38.refs_0_), channel_id=1, source_target_pairs={{0,1},{1,0},{2,3},{3,2},{4,5},{5,4},{6,7},{7,6},{8,9},{9,8},{10,11... | collective-permute-start | bytes 2703368 | tf_op jit(solution)/shard_map/ppermute | solution.py:27
  43.6 21.2 %collective-permute-start.6 = (bf16[176,1280]{1,0:T(8,128)(2,1)S(1)}, bf16[176,1280]{1,0:T(8,128)(2,1)S(1)}, u32[]{:S(2)}, u32[]{:S(2)}) collective-permute-start(bf16[176,1280]{1,0:T(8,128)(2,1)S(1)} %get-tuple-element.41), channel_id=1, source_target_pairs={{0,8},{1,9},{2,10},{3,11},{4,12},{5,13},{6,14},{7,15},{8,0},{9,1},... | collective-permute-start | bytes 1351688 | tf_op jit(solution)/shard_map/ppermute | solution.py:27
  45.2 20.5 %collective-permute-start.13 = (bf16[176,1280]{1,0:T(8,128)(2,1)S(1)}, bf16[176,1280]{1,0:T(8,128)(2,1)S(1)}, u32[]{:S(2)}, u32[]{:S(2)}) collective-permute-start(bf16[176,1280]{1,0:T(8,128)(2,1)S(1)} %collective-permute-done.refs_0_), channel_id=1, source_target_pairs={{0,2},{1,3},{2,0},{3,1},{4,6},{5,7},{6,4},{7,5},{8,10},{9,11},{10,... | collective-permute-start | bytes 1351688 | tf_op jit(solution)/shard_map/ppermute | solution.py:27
  46.1 22.8 %collective-permute-start.12 = (bf16[176,1280]{1,0:T(8,128)(2,1)S(1)}, bf16[176,1280]{1,0:T(8,128)(2,1)S(1)}, u32[]{:S(2)}, u32[]{:S(2)}) collective-permute-start(bf16[176,1280]{1,0:T(8,128)(2,1)S(1)} %get-tuple-element.41), channel_id=1, source_target_pairs={{0,16},{1,17},{2,18},{3,19},{4,20},{5,21},{6,22},{7,23},{8,24},{9,... | collective-permute-start | bytes 1351688 | tf_op jit(solution)/shard_map/ppermute | solution.py:27
  48.4 20.6 %collective-permute-start.11 = (bf16[176,1280]{1,0:T(8,128)(2,1)S(1)}, bf16[176,1280]{1,0:T(8,128)(2,1)S(1)}, u32[]{:S(2)}, u32[]{:S(2)}) collective-permute-start(bf16[176,1280]{1,0:T(8,128)(2,1)S(1)} %collective-permute-done.1.refs_1_.refs_0_), channel_id=1, source_target_pairs={{0,2},{1,3},{2,0},{3,1},{4,6},{5,7},{6,4},{7,5},{8,10},{9,11},{10,... | collective-permute-start | bytes 1351688 | tf_op jit(solution)/shard_map/ppermute | solution.py:27
  64.8 12.0 %collective-permute-start.7 = (bf16[176,1280]{1,0:T(8,128)(2,1)S(1)}, bf16[176,1280]{1,0:T(8,128)(2,1)S(1)}, u32[]{:S(2)}, u32[]{:S(2)}) collective-permute-start(bf16[176,1280]{1,0:T(8,128)(2,1)S(1)} %collective-permute-done.6.refs_0_), channel_id=1, source_target_pairs={{0,2},{1,3},{2,0},{3,1},{4,6},{5,7},{6,4},{7,5},{8,10},{9,11},{10,... | collective-permute-start | bytes 1351688 | tf_op jit(solution)/shard_map/ppermute | solution.py:27
  65.7 12.8 %collective-permute-start.8 = (bf16[176,1280]{1,0:T(8,128)(2,1)S(1)}, bf16[176,1280]{1,0:T(8,128)(2,1)S(1)}, u32[]{:S(2)}, u32[]{:S(2)}) collective-permute-start(bf16[176,1280]{1,0:T(8,128)(2,1)S(1)} %collective-permute-done.refs_0_), channel_id=1, source_target_pairs={{0,8},{1,9},{2,10},{3,11},{4,12},{5,13},{6,14},{7,15},{8,0},{9,1},... | collective-permute-start | bytes 1351688 | tf_op jit(solution)/shard_map/ppermute | solution.py:27
  65.7 10.8 %collective-permute-start.9 = (bf16[160,1280]{1,0:T(8,128)(2,1)S(1)}, bf16[160,1280]{1,0:T(8,128)(2,1)S(1)}, u32[]{:S(2)}, u32[]{:S(2)}) collective-permute-start(bf16[160,1280]{1,0:T(8,128)(2,1)S(1)} %get-tuple-element.42), channel_id=1, source_target_pairs={{0,4},{1,5},{2,6},{3,7},{4,0},{5,1},{6,2},{7,3},{8,12},{9,13},{10,... | collective-permute-start | bytes 1228808 | tf_op jit(solution)/shard_map/ppermute | solution.py:27
  69.1 12.2 %collective-permute-start.14 = (bf16[352,1280]{1,0:T(8,128)(2,1)S(1)}, bf16[352,1280]{1,0:T(8,128)(2,1)S(1)}, u32[]{:S(2)}, u32[]{:S(2)}) collective-permute-start(bf16[352,1280]{1,0:T(8,128)(2,1)S(1)} %join.8.refs_2_), channel_id=1, source_target_pairs={{0,1},{1,0},{2,3},{3,2},{4,5},{5,4},{6,7},{7,6},{8,9},{9,8},{10,11... | collective-permute-start | bytes 2703368 | tf_op jit(solution)/shard_map/ppermute | solution.py:27
  78.6 12.8 %collective-permute-start.16 = (bf16[176,1280]{1,0:T(8,128)(2,1)S(1)}, bf16[176,1280]{1,0:T(8,128)(2,1)S(1)}, u32[]{:S(2)}, u32[]{:S(2)}) collective-permute-start(bf16[176,1280]{1,0:T(8,128)(2,1)S(1)} %collective-permute-done.12.refs_0_), channel_id=1, source_target_pairs={{0,2},{1,3},{2,0},{3,1},{4,6},{5,7},{6,4},{7,5},{8,10},{9,11},{10,... | collective-permute-start | bytes 1351688 | tf_op jit(solution)/shard_map/ppermute | solution.py:27
  79.8 12.4 %collective-permute-start.17 = (bf16[176,1280]{1,0:T(8,128)(2,1)S(1)}, bf16[176,1280]{1,0:T(8,128)(2,1)S(1)}, u32[]{:S(2)}, u32[]{:S(2)}) collective-permute-start(bf16[176,1280]{1,0:T(8,128)(2,1)S(1)} %collective-permute-done.12.refs_0_), channel_id=1, source_target_pairs={{0,8},{1,9},{2,10},{3,11},{4,12},{5,13},{6,14},{7,15},{8,0},{9,1},... | collective-permute-start | bytes 1351688 | tf_op jit(solution)/shard_map/ppermute | solution.py:27
  79.8 11.5 %collective-permute-start.5 = (bf16[160,1280]{1,0:T(8,128)(2,1)S(1)}, bf16[160,1280]{1,0:T(8,128)(2,1)S(1)}, u32[]{:S(2)}, u32[]{:S(2)}) collective-permute-start(bf16[160,1280]{1,0:T(8,128)(2,1)S(1)} %get-tuple-element.40), channel_id=1, source_target_pairs={{0,4},{1,5},{2,6},{3,7},{4,0},{5,1},{6,2},{7,3},{8,12},{9,13},{10,... | collective-permute-start | bytes 1228808 | tf_op jit(solution)/shard_map/ppermute | solution.py:27
  81.3 14.6 %collective-permute-start.19 = (bf16[352,1280]{1,0:T(8,128)(2,1)S(1)}, bf16[352,1280]{1,0:T(8,128)(2,1)S(1)}, u32[]{:S(2)}, u32[]{:S(2)}) collective-permute-start(bf16[352,1280]{1,0:T(8,128)(2,1)S(1)} %join.7.refs_3_), channel_id=1, source_target_pairs={{0,1},{1,0},{2,3},{3,2},{4,5},{5,4},{6,7},{7,6},{8,9},{9,8},{10,11... | collective-permute-start | bytes 2703368 | tf_op jit(solution)/shard_map/ppermute | solution.py:27
  92.3 5.6 %collective-permute-start.18 = (bf16[352,1280]{1,0:T(8,128)(2,1)S(1)}, bf16[352,1280]{1,0:T(8,128)(2,1)S(1)}, u32[]{:S(2)}, u32[]{:S(2)}) collective-permute-start(bf16[352,1280]{1,0:T(8,128)(2,1)S(1)} %join.9.refs_1_), channel_id=1, source_target_pairs={{0,1},{1,0},{2,3},{3,2},{4,5},{5,4},{6,7},{7,6},{8,9},{9,8},{10,11... | collective-permute-start | bytes 2703368 | tf_op jit(solution)/shard_map/ppermute | solution.py:27
  92.3 22.1 %collective-permute-start.22 = (bf16[176,1280]{1,0:T(8,128)(2,1)S(1)}, bf16[176,1280]{1,0:T(8,128)(2,1)S(1)}, u32[]{:S(2)}, u32[]{:S(2)}) collective-permute-start(bf16[176,1280]{1,0:T(8,128)(2,1)S(1)} %collective-permute-done.17.refs_0_), channel_id=1, source_target_pairs={{0,2},{1,3},{2,0},{3,1},{4,6},{5,7},{6,4},{7,5},{8,10},{9,11},{10,... | collective-permute-start | bytes 1351688 | tf_op jit(solution)/shard_map/ppermute | solution.py:27
  93.4 21.4 %collective-permute-start.24 = (bf16[176,1280]{1,0:T(8,128)(2,1)S(1)}, bf16[176,1280]{1,0:T(8,128)(2,1)S(1)}, u32[]{:S(2)}, u32[]{:S(2)}) collective-permute-start(bf16[176,1280]{1,0:T(8,128)(2,1)S(1)} %collective-permute-done.8.refs_0_), channel_id=1, source_target_pairs={{0,2},{1,3},{2,0},{3,1},{4,6},{5,7},{6,4},{7,5},{8,10},{9,11},{10,... | collective-permute-start | bytes 1351688 | tf_op jit(solution)/shard_map/ppermute | solution.py:27
  94.4 13.2 %collective-permute-start.15 = (bf16[160,1280]{1,0:T(8,128)(2,1)S(1)}, bf16[160,1280]{1,0:T(8,128)(2,1)S(1)}, u32[]{:S(2)}, u32[]{:S(2)}) collective-permute-start(bf16[160,1280]{1,0:T(8,128)(2,1)S(1)} %get-tuple-element.49), channel_id=1, source_target_pairs={{0,4},{1,5},{2,6},{3,7},{4,0},{5,1},{6,2},{7,3},{8,12},{9,13},{10,... | collective-permute-start | bytes 1228808 | tf_op jit(solution)/shard_map/ppermute | solution.py:27
  96.0 18.5 %collective-permute-start.21 = (bf16[160,1280]{1,0:T(8,128)(2,1)S(1)}, bf16[160,1280]{1,0:T(8,128)(2,1)S(1)}, u32[]{:S(2)}, u32[]{:S(2)}) collective-permute-start(bf16[160,1280]{1,0:T(8,128)(2,1)S(1)} %get-tuple-element.53), channel_id=1, source_target_pairs={{0,4},{1,5},{2,6},{3,7},{4,0},{5,1},{6,2},{7,3},{8,12},{9,13},{10,... | collective-permute-start | bytes 1228808 | tf_op jit(solution)/shard_map/ppermute | solution.py:27
  114.5 5.2 %collective-permute-start.23 = (bf16[352,1280]{1,0:T(8,128)(2,1)S(1)}, bf16[352,1280]{1,0:T(8,128)(2,1)S(1)}, u32[]{:S(2)}, u32[]{:S(2)}) collective-permute-start(bf16[352,1280]{1,0:T(8,128)(2,1)S(1)} %join.10.refs_1_), channel_id=1, source_target_pairs={{0,1},{1,0},{2,3},{3,2},{4,5},{5,4},{6,7},{7,6},{8,9},{9,8},{10,11... | collective-permute-start | bytes 2703368 | tf_op jit(solution)/shard_map/ppermute | solution.py:27
  114.8 4.9 %collective-permute-start.25 = (bf16[352,1280]{1,0:T(8,128)(2,1)S(1)}, bf16[352,1280]{1,0:T(8,128)(2,1)S(1)}, u32[]{:S(2)}, u32[]{:S(2)}) collective-permute-start(bf16[352,1280]{1,0:T(8,128)(2,1)S(1)} %join.11.refs_3_), channel_id=1, source_target_pairs={{0,1},{1,0},{2,3},{3,2},{4,5},{5,4},{6,7},{7,6},{8,9},{9,8},{10,11... | collective-permute-start | bytes 2703368 | tf_op jit(solution)/shard_map/ppermute | solution.py:27
  115.2 21.1 %collective-permute-start.27 = (bf16[160,1280]{1,0:T(8,128)(2,1)S(1)}, bf16[160,1280]{1,0:T(8,128)(2,1)S(1)}, u32[]{:S(2)}, u32[]{:S(2)}) collective-permute-start(bf16[160,1280]{1,0:T(8,128)(2,1)S(1)} %get-tuple-element.59), channel_id=1, source_target_pairs={{0,4},{1,5},{2,6},{3,7},{4,0},{5,1},{6,2},{7,3},{8,12},{9,13},{10,... | collective-permute-start | bytes 1228808 | tf_op jit(solution)/shard_map/ppermute | solution.py:27
  116.8 19.6 %collective-permute-start.20 = (bf16[160,1280]{1,0:T(8,128)(2,1)S(1)}, bf16[160,1280]{1,0:T(8,128)(2,1)S(1)}, u32[]{:S(2)}, u32[]{:S(2)}) collective-permute-start(bf16[160,1280]{1,0:T(8,128)(2,1)S(1)} %get-tuple-element.56), channel_id=1, source_target_pairs={{0,4},{1,5},{2,6},{3,7},{4,0},{5,1},{6,2},{7,3},{8,12},{9,13},{10,... | collective-permute-start | bytes 1228808 | tf_op jit(solution)/shard_map/ppermute | solution.py:27
  129.7 15.4 %collective-permute-start.28 = (bf16[160,1280]{1,0:T(8,128)(2,1)S(1)}, bf16[160,1280]{1,0:T(8,128)(2,1)S(1)}, u32[]{:S(2)}, u32[]{:S(2)}) collective-permute-start(bf16[160,1280]{1,0:T(8,128)(2,1)S(1)} %get-tuple-element.67), channel_id=1, source_target_pairs={{0,4},{1,5},{2,6},{3,7},{4,0},{5,1},{6,2},{7,3},{8,12},{9,13},{10,... | collective-permute-start | bytes 1228808 | tf_op jit(solution)/shard_map/ppermute | solution.py:27
  131.3 21.8 %collective-permute-start.26 = (bf16[160,1280]{1,0:T(8,128)(2,1)S(1)}, bf16[160,1280]{1,0:T(8,128)(2,1)S(1)}, u32[]{:S(2)}, u32[]{:S(2)}) collective-permute-start(bf16[160,1280]{1,0:T(8,128)(2,1)S(1)} %get-tuple-element.64), channel_id=1, source_target_pairs={{0,4},{1,5},{2,6},{3,7},{4,0},{5,1},{6,2},{7,3},{8,12},{9,13},{10,... | collective-permute-start | bytes 1228808 | tf_op jit(solution)/shard_map/ppermute | solution.py:27
  154.8 3.7 %collective-permute-start.30 = (f32[8,128]{1,0:T(8,128)S(1)}, f32[8,128]{1,0:T(8,128)S(1)}, u32[]{:S(2)}, u32[]{:S(2)}) collective-permute-start(f32[8,128]{1,0:T(8,128)S(1)} %products.11.refs_0_), channel_id=1, source_target_pairs={{0,2},{1,3},{2,0},{3,1},{4,6},{5,7},{6,4},{7,5},{8,10},{9,11},{10,... | collective-permute-start | bytes 12296 | tf_op jit(solution)/shard_map/ppermute | solution.py:27
  159.4 4.5 %collective-permute-start.32 = (f32[8,128]{1,0:T(8,128)S(1)}, f32[8,128]{1,0:T(8,128)S(1)}, u32[]{:S(2)}, u32[]{:S(2)}) collective-permute-start(f32[8,128]{1,0:T(8,128)S(1)} %sum_of.3.refs_0_), channel_id=1, source_target_pairs={{0,8},{1,9},{2,10},{3,11},{4,12},{5,13},{6,14},{7,15},{8,0},{9,1},... | collective-permute-start | bytes 12296 | tf_op jit(solution)/shard_map/ppermute | solution.py:27
  160.7 4.5 %collective-permute-start.33 = (f32[8,128]{1,0:T(8,128)S(1)}, f32[8,128]{1,0:T(8,128)S(1)}, u32[]{:S(2)}, u32[]{:S(2)}) collective-permute-start(f32[8,128]{1,0:T(8,128)S(1)} %sum_of.3.refs_0_), channel_id=1, source_target_pairs={{0,16},{1,17},{2,18},{3,19},{4,20},{5,21},{6,22},{7,23},{8,24},{9,... | collective-permute-start | bytes 12296 | tf_op jit(solution)/shard_map/ppermute | solution.py:27
  162.1 5.4 %collective-permute-start.34 = (f32[8,128]{1,0:T(8,128)S(1)}, f32[8,128]{1,0:T(8,128)S(1)}, u32[]{:S(2)}, u32[]{:S(2)}) collective-permute-start(f32[8,128]{1,0:T(8,128)S(1)} %sum_of.3.refs_0_), channel_id=1, source_target_pairs={{0,24},{1,25},{2,26},{3,27},{4,28},{5,29},{6,30},{7,31},{8,16},{9,... | collective-permute-start | bytes 12296 | tf_op jit(solution)/shard_map/ppermute | solution.py:27
  (11 other events, 77.7 us)

commit v13 on v12

--- a/solution.py
+++ b/solution.py
@@ -510,7 +510,9 @@
         targets,
         tuple(inputs_of.values()),
     )
-    errors_of = {bit: from_mask(error_piece, bit * others, 0) for bit in bits}
+    errors_of = {
+        bit: from_mask(error_piece if bit == bits[0] else error, bit * others, 0) for bit in bits
+    }
 
     def to_half(piece, *before):
         for bit in reversed(range(1, shard_levels)):
@@ -527,20 +529,23 @@
     for n, m in enumerate(masks):
         if n == 0:
             half = error
-        elif m in bits:
+        elif m not in (bits[0], masks[-1]):
+            half = errors_of[m] = ordered(errors_of[m], sent[0], *slots[1][:1])
+            other_inputs = halves[m]
+        elif m == bits[0]:
+            before = [sent[-1], *slots[1]]
             errors_of[m] = ordered(errors_of[m], sent[0])
-            top, of = (bits[0], inputs_of) if n == 1 else (m, errors_of)
-            both = [top | bit for bit in bits[1:]]
-            for to in both:
-                of[to] = from_mask(ordered(of[top], errors_of[m]), (to ^ top) * others, 0)
-            before = [of[to] for to in both] + list(slots[1][: 2 * n - 1]) + sent[1:]
+            for bit in bits[1:]:
+                ready = ordered(errors_of[m], errors_of[bit])
+                errors_of[m | bit] = from_mask(ready, bit * others, 0)
+                before.append(errors_of[m | bit])
+                ready = ordered(halves[m], errors_of[bit])
+                halves[m | bit] = from_mask(ready, bit * others, 0)
             half = to_half(errors_of[m], *before)
             other_inputs = halves[m]
         else:
-            other_inputs, half = (
-                to_half(ordered(of[m], sent[-2]), sent[-1], *slots[2 * n - 3])
-                for of in (inputs_of, errors_of)
-            )
+            half = to_half(ordered(errors_of[m], sent[-2]), sent[-1], *slots[2 * n - 3])
+            other_inputs = ordered(halves[m], sent[-1])
         first, second, *send = gradient(
             place,
             members,

time: 177 us -> 175 us (0.989)
  waiting for transfers between devices: 64.9 us -> 62.9 us
    ppermute x36 -> x34, waiting for transfers between devices: 64.9 us -> 62.9 us  [from_mask(): return lax.ppermute(value, ('dp', 'tensor'), pairs)]
    ppermute x36 -> x34, starting transfers between devices: 35.1 us -> 35.7 us  [from_mask(): return lax.ppermute(value, ('dp', 'tensor'), pairs)]
    pallas_call x23 -> x21, Pallas kernels: 73.2 us -> 73.2 us  [call(): pl.pallas_call(body, grid_spec=pltpu.PrefetchScalarGridSpec(num_scalar_pr...]
  transfers between devices with their start and end apart: 36 -> 34, of which waited for: 21 -> 15; matrix products, arithmetic and copies ran while one was open for 0% -> 0% of each run, Pallas kernels for 31% -> 31%
where the time goes in v13:
time: 175 us
  Pallas kernels  73.2 us (42%)
  waiting for transfers between devices  62.9 us (36%)
  starting transfers between devices  35.7 us (20%)
  local copies, waits for them, and re-layouts  1.87 us (1%)
    pallas_call x21, Pallas kernels, call(): pl.pallas_call(body, grid_spec=pltpu.PrefetchScalarGridSpec(num_scalar_pr...  73.2 us
    ppermute x34, waiting for transfers between devices, from_mask(): return lax.ppermute(value, ('dp', 'tensor'), pairs)  62.9 us
    ppermute x34, starting transfers between devices, from_mask(): return lax.ppermute(value, ('dp', 'tensor'), pairs)  35.7 us
  transfers between devices with their start and end apart: 34, of which 15 were waited for; matrix products, arithmetic and copies ran while one was open for 0% of the time, Pallas kernels for 31%

profile of v13, /device:TPU:0, one launch (start us, length us, event | category | flops | bytes accessed | tf_op | source)
XLA Modules:
  0.0 175.1 jit_solution(8148665016661753274)
XLA Ops:
  1.4 10.7 %forward.1 = (f32[352,1280]{1,0:T(8,128)}, bf16[352,1280]{1,0:T(8,128)(2,1)}, bf16[176,1280]{1,0:T(8,128)(2,1)}) custom-call(s32[8]{0:T(128)} %stack.35.place_ref, bf16[704,1280]{1,0:T(8,128)(2,1)} %refs_2_.3, bf16[1280,1280]{1,0:T(8,128)(2,1)} %refs_5_.5, bf16[1280,1280]{1,0:T(8,128)(2,1)} %refs_6_.3), custom_call_target="tpu_custom_call" | custom-call | flops 1 | bytes 1 | tf_op jit(solution)/shard_map/forward/pallas_call | solution.py:81
  13.7 2.7 %product.1 = f32[352,1280]{1,0:T(8,128)S(1)} custom-call(s32[8]{0:T(128)S(1)} %copy-done.5, bf16[352,1280]{1,0:T(8,128)(2,1)S(1)} %copy-done.4, bf16[1280,1280]{1,0:T(8,128)(2,1)S(1)} %copy-done), custom_call_target="tpu_custom_call" | custom-call | flops 1 | bytes 1 | tf_op jit(solution)/shard_map/product/pallas_call | solution.py:81
  16.7 2.6 %collective-permute-start.3 = (f16[352,1280]{1,0:T(8,128)(2,1)S(1)}, f16[352,1280]{1,0:T(8,128)(2,1)S(1)}, u32[]{:S(2)}, u32[]{:S(2)}) collective-permute-start(f16[352,1280]{1,0:T(8,128)(2,1)S(1)} %get-tuple-element.64), channel_id=1, source_target_pairs={{0,2},{1,3},{2,0},{3,1},{4,6},{5,7},{6,4},{7,5},{8,10},{9,11},{10,... | collective-permute-start | bytes 2703368 | tf_op jit(solution)/shard_map/ppermute | solution.py:27
  19.2 2.6 %collective-permute-start = (bf16[176,1280]{1,0:T(8,128)(2,1)S(1)}, bf16[176,1280]{1,0:T(8,128)(2,1)S(1)}, u32[]{:S(2)}, u32[]{:S(2)}) collective-permute-start(bf16[176,1280]{1,0:T(8,128)(2,1)S(1)} %copy-done.6), channel_id=1, source_target_pairs={{0,16},{1,17},{2,18},{3,19},{4,20},{5,21},{6,22},{7,23},{8,24},{9,... | collective-permute-start | bytes 1351688 | tf_op jit(solution)/shard_map/ppermute | solution.py:27
  21.8 1.6 collective-permute-start.1
  23.4 16.5 %collective-permute-done.3 = f16[352,1280]{1,0:T(8,128)(2,1)S(1)} collective-permute-done((f16[352,1280]{1,0:T(8,128)(2,1)S(1)}, f16[352,1280]{1,0:T(8,128)(2,1)S(1)}, u32[]{:S(2)}, u32[]{:S(2)}) %collective-permute-start.3) | collective-permute-done | bytes 901152 | tf_op jit(solution)/shard_map/ppermute | solution.py:27
  40.1 2.3 %collective-permute-done.refs_0_ = bf16[176,1280]{1,0:T(8,128)(2,1)S(1)} collective-permute-done((bf16[176,1280]{1,0:T(8,128)(2,1)S(1)}, bf16[176,1280]{1,0:T(8,128)(2,1)S(1)}, u32[]{:S(2)}, u32[]{:S(2)}) %collective-permute-start) | collective-permute-done | bytes 450592 | tf_op jit(solution)/shard_map/ppermute | solution.py:27
  46.2 2.3 %collective-permute-start.10 = (bf16[176,1280]{1,0:T(8,128)(2,1)S(1)}, bf16[176,1280]{1,0:T(8,128)(2,1)S(1)}, u32[]{:S(2)}, u32[]{:S(2)}) collective-permute-start(bf16[176,1280]{1,0:T(8,128)(2,1)S(1)} %get-tuple-element.41), channel_id=1, source_target_pairs={{0,16},{1,17},{2,18},{3,19},{4,20},{5,21},{6,22},{7,23},{8,24},{9,... | collective-permute-start | bytes 1351688 | tf_op jit(solution)/shard_map/ppermute | solution.py:27
  49.7 9.7 %gradient.4 = (f32[160,1280]{1,0:T(8,128)S(1)}, f32[160,1280]{1,0:T(8,128)S(1)}, bf16[160,1280]{1,0:T(8,128)(2,1)S(1)}, bf16[160,1280]{1,0:T(8,128)(2,1)S(1)}) custom-call(s32[8]{0:T(128)S(1)} %copy-done.5, bf16[352,1280]{1,0:T(8,128)(2,1)S(1)} %get-tuple-element.36.refs_0_, bf16[352,1280]{1,0:T(8,128)(2,1)S(1)} %collective-permute-done.4.refs_1_, ...), custom_call_target="tpu_custom_call" | custom-call | flops 1 | bytes 1 | tf_op jit(solution)/shard_map/gradient/pallas_call | solution.py:81
  59.3 1.6 collective-permute-start.7
  60.9 13.9 %collective-permute-done.10.refs_0_ = bf16[176,1280]{1,0:T(8,128)(2,1)S(1)} collective-permute-done((bf16[176,1280]{1,0:T(8,128)(2,1)S(1)}, bf16[176,1280]{1,0:T(8,128)(2,1)S(1)}, u32[]{:S(2)}, u32[]{:S(2)}) %collective-permute-start.10) | collective-permute-done | bytes 450592 | tf_op jit(solution)/shard_map/ppermute | solution.py:27
  76.8 2.7 %collective-permute-start.15 = (bf16[176,1280]{1,0:T(8,128)(2,1)S(1)}, bf16[176,1280]{1,0:T(8,128)(2,1)S(1)}, u32[]{:S(2)}, u32[]{:S(2)}) collective-permute-start(bf16[176,1280]{1,0:T(8,128)(2,1)S(1)} %collective-permute-done.10.refs_0_), channel_id=1, source_target_pairs={{0,8},{1,9},{2,10},{3,11},{4,12},{5,13},{6,14},{7,15},{8,0},{9,1},... | collective-permute-start | bytes 1351688 | tf_op jit(solution)/shard_map/ppermute | solution.py:27
  79.6 1.5 collective-permute-start.5
  81.1 9.9 %gradient.5 = (f32[160,1280]{1,0:T(8,128)S(1)}, f32[160,1280]{1,0:T(8,128)S(1)}, bf16[160,1280]{1,0:T(8,128)(2,1)S(1)}, bf16[160,1280]{1,0:T(8,128)(2,1)S(1)}) custom-call(s32[8]{0:T(128)S(1)} %copy-done.5, bf16[352,1280]{1,0:T(8,128)(2,1)S(1)} %collective-permute-done.6.refs_0_, bf16[352,1280]{1,0:T(8,128)(2,1)S(1)} %collective-permute-done.8.refs_1_, ...), custom_call_target="tpu_custom_call" | custom-call | flops 1 | bytes 1 | tf_op jit(solution)/shard_map/gradient/pallas_call | solution.py:81
  93.0 1.5 collective-permute-start.13
  96.5 9.7 %gradient.6 = (f32[160,1280]{1,0:T(8,128)S(1)}, f32[160,1280]{1,0:T(8,128)S(1)}, bf16[160,1280]{1,0:T(8,128)(2,1)S(1)}, bf16[160,1280]{1,0:T(8,128)(2,1)S(1)}) custom-call(s32[8]{0:T(128)S(1)} %copy-done.5, f32[8,128]{1,0:T(8,128)S(1)} %products.6.refs_0_.refs_8_, bf16[352,1280]{1,0:T(8,128)(2,1)S(1)} %join.6.refs_1_, ...), custom_call_target="tpu_custom_call" | custom-call | flops 1 | bytes 1 | tf_op jit(solution)/shard_map/gradient/pallas_call | solution.py:81
  106.3 6.7 %collective-permute-done.19.refs_6_.refs_3_.refs_7_ = bf16[160,1280]{1,0:T(8,128)(2,1)S(1)} collective-permute-done((bf16[160,1280]{1,0:T(8,128)(2,1)S(1)}, bf16[160,1280]{1,0:T(8,128)(2,1)S(1)}, u32[]{:S(2)}, u32[]{:S(2)}) %collective-permute-start.19) | collective-permute-done | bytes 409632 | tf_op jit(solution)/shard_map/ppermute | solution.py:27
  115.7 2.4 %products.7.refs_0_.refs_12_ = f32[8,128]{1,0:T(8,128)S(1)} custom-call(s32[8]{0:T(128)S(1)} %copy-done.5, f32[160,1280]{1,0:T(8,128)S(1)} %get-tuple-element.46.refs_0_.refs_1_, f32[160,1280]{1,0:T(8,128)S(1)} %get-tuple-element.37.refs_1_.refs_0_.refs_2_, bf16[160,1280]{1,0:T(8,128)(2,1)S(1)} %collective-permute-done.7.refs_2_.refs_1_.refs_3_, ...), custom_call_target="tpu_custom_call" | custom-call | flops 1 | bytes 1 | tf_op jit(solution)/shard_map/products/pallas_call | solution.py:81
  118.1 10.0 %gradient.7 = (f32[160,1280]{1,0:T(8,128)S(1)}, f32[160,1280]{1,0:T(8,128)S(1)}, bf16[160,1280]{1,0:T(8,128)(2,1)S(1)}, bf16[160,1280]{1,0:T(8,128)(2,1)S(1)}) custom-call(s32[8]{0:T(128)S(1)} %copy-done.5, f32[8,128]{1,0:T(8,128)S(1)} %products.7.refs_0_.refs_12_, bf16[352,1280]{1,0:T(8,128)(2,1)S(1)} %join.7.refs_1_, ...), custom_call_target="tpu_custom_call" | custom-call | flops 1 | bytes 1 | tf_op jit(solution)/shard_map/gradient/pallas_call | solution.py:81
  128.1 1.5 collective-permute-start.26
  130.2 4.5 %collective-permute-done.18.refs_11_.refs_5_.refs_12_ = bf16[160,1280]{1,0:T(8,128)(2,1)S(1)} collective-permute-done((bf16[160,1280]{1,0:T(8,128)(2,1)S(1)}, bf16[160,1280]{1,0:T(8,128)(2,1)S(1)}, u32[]{:S(2)}, u32[]{:S(2)}) %collective-permute-start.18) | collective-permute-done | bytes 409632 | tf_op jit(solution)/shard_map/ppermute | solution.py:27
  134.7 3.4 %products.8.refs_14_ = f32[8,128]{1,0:T(8,128)S(1)} custom-call(s32[8]{0:T(128)S(1)} %copy-done.5, f32[160,1280]{1,0:T(8,128)S(1)} %get-tuple-element.46.refs_0_.refs_1_, f32[160,1280]{1,0:T(8,128)S(1)} %get-tuple-element.37.refs_1_.refs_0_.refs_2_, bf16[160,1280]{1,0:T(8,128)(2,1)S(1)} %collective-permute-done.7.refs_2_.refs_1_.refs_3_, ...), custom_call_target="tpu_custom_call" | custom-call | flops 1 | bytes 1 | tf_op jit(solution)/shard_map/products/pallas_call | solution.py:81
  138.2 2.8 %products.9.refs_8_ = f32[8,128]{1,0:T(8,128)S(1)} custom-call(s32[8]{0:T(128)S(1)} %copy-done.5, f32[160,1280]{1,0:T(8,128)S(1)} %get-tuple-element.46.refs_0_.refs_1_, f32[160,1280]{1,0:T(8,128)S(1)} %get-tuple-element.37.refs_1_.refs_0_.refs_2_, bf16[160,1280]{1,0:T(8,128)(2,1)S(1)} %collective-permute-done.7.refs_2_.refs_1_.refs_3_, ...), custom_call_target="tpu_custom_call" | custom-call | flops 1 | bytes 1 | tf_op jit(solution)/shard_map/products/pallas_call | solution.py:81
  141.0 2.5 %collective-permute-done.26.refs_7_.refs_15_ = bf16[160,1280]{1,0:T(8,128)(2,1)S(1)} collective-permute-done((bf16[160,1280]{1,0:T(8,128)(2,1)S(1)}, bf16[160,1280]{1,0:T(8,128)(2,1)S(1)}, u32[]{:S(2)}, u32[]{:S(2)}) %collective-permute-start.26) | collective-permute-done | bytes 409632 | tf_op jit(solution)/shard_map/ppermute | solution.py:27
  143.5 1.6 products.10.refs_8_
  145.1 6.7 %collective-permute-done.24.refs_7_.refs_16_ = bf16[160,1280]{1,0:T(8,128)(2,1)S(1)} collective-permute-done((bf16[160,1280]{1,0:T(8,128)(2,1)S(1)}, bf16[160,1280]{1,0:T(8,128)(2,1)S(1)}, u32[]{:S(2)}, u32[]{:S(2)}) %collective-permute-start.24) | collective-permute-done | bytes 409632 | tf_op jit(solution)/shard_map/ppermute | solution.py:27
  151.9 1.6 products.11.refs_0_
  155.5 1.8 %collective-permute-done.28.refs_2_ = f32[8,128]{1,0:T(8,128)S(1)} collective-permute-done((f32[8,128]{1,0:T(8,128)S(1)}, f32[8,128]{1,0:T(8,128)S(1)}, u32[]{:S(2)}, u32[]{:S(2)}) %collective-permute-start.28) | collective-permute-done | bytes 4128 | tf_op jit(solution)/shard_map/ppermute | solution.py:27
  160.7 2.0 %collective-permute-start.32 = (f32[8,128]{1,0:T(8,128)S(1)}, f32[8,128]{1,0:T(8,128)S(1)}, u32[]{:S(2)}, u32[]{:S(2)}) collective-permute-start(f32[8,128]{1,0:T(8,128)S(1)} %sum_of.3.refs_0_), channel_id=1, source_target_pairs={{0,24},{1,25},{2,26},{3,27},{4,28},{5,29},{6,30},{7,31},{8,16},{9,... | collective-permute-start | bytes 12296 | tf_op jit(solution)/shard_map/ppermute | solution.py:27
  163.8 2.4 %collective-permute-done.32.refs_3_ = f32[8,128]{1,0:T(8,128)S(1)} collective-permute-done((f32[8,128]{1,0:T(8,128)S(1)}, f32[8,128]{1,0:T(8,128)S(1)}, u32[]{:S(2)}, u32[]{:S(2)}) %collective-permute-start.32) | collective-permute-done | bytes 4128 | tf_op jit(solution)/shard_map/ppermute | solution.py:27
  167.9 2.5 %collective-permute-done.33.refs_1_ = f32[8,128]{1,0:T(8,128)S(1)} collective-permute-done((f32[8,128]{1,0:T(8,128)S(1)}, f32[8,128]{1,0:T(8,128)S(1)}, u32[]{:S(2)}, u32[]{:S(2)}) %collective-permute-start.33) | collective-permute-done | bytes 4128 | tf_op jit(solution)/shard_map/ppermute | solution.py:27
  170.9 4.1 %merge.1 = (f32[160,1280]{1,0:T(8,128)}, f32[160,1280]{1,0:T(8,128)}) custom-call(s32[8]{0:T(128)S(1)} %copy-done.5, f32[8,128]{1,0:T(8,128)S(1)} %sum_of.5.refs_0_, f32[160,1280]{1,0:T(8,128)S(1)} %get-tuple-element.46.refs_0_.refs_1_, f32[160,1280]{1,0:T(8,128)S(1)} %get-tuple-element.37.refs_1_.refs_0_.refs_2_, ...), custom_call_target="tpu_custom_call" | custom-call | flops 1 | bytes 1 | tf_op jit(solution)/shard_map/merge/pallas_call | solution.py:81
  (75 shorter events, 25.5 us)
Async XLA Ops:
  12.0 4.4 %collective-permute-start.2 = (f32[352,1280]{1,0:T(8,128)}, f32[352,1280]{1,0:T(8,128)S(1)}, u32[]{:S(2)}, u32[]{:S(2)}) collective-permute-start(f32[352,1280]{1,0:T(8,128)} %get-tuple-element.35), channel_id=1, source_target_pairs={{0,1},{1,0},{2,3},{3,2},{4,5},{5,4},{6,7},{7,6},{8,9},{9,8},{10,11... | collective-permute-start | bytes 5406728 | tf_op jit(solution)/shard_map/ppermute | solution.py:27
  16.7 23.2 %collective-permute-start.3 = (f16[352,1280]{1,0:T(8,128)(2,1)S(1)}, f16[352,1280]{1,0:T(8,128)(2,1)S(1)}, u32[]{:S(2)}, u32[]{:S(2)}) collective-permute-start(f16[352,1280]{1,0:T(8,128)(2,1)S(1)} %get-tuple-element.64), channel_id=1, source_target_pairs={{0,2},{1,3},{2,0},{3,1},{4,6},{5,7},{6,4},{7,5},{8,10},{9,11},{10,... | collective-permute-start | bytes 2703368 | tf_op jit(solution)/shard_map/ppermute | solution.py:27
  19.2 23.1 %collective-permute-start = (bf16[176,1280]{1,0:T(8,128)(2,1)S(1)}, bf16[176,1280]{1,0:T(8,128)(2,1)S(1)}, u32[]{:S(2)}, u32[]{:S(2)}) collective-permute-start(bf16[176,1280]{1,0:T(8,128)(2,1)S(1)} %copy-done.6), channel_id=1, source_target_pairs={{0,16},{1,17},{2,18},{3,19},{4,20},{5,21},{6,22},{7,23},{8,24},{9,... | collective-permute-start | bytes 1351688 | tf_op jit(solution)/shard_map/ppermute | solution.py:27
  21.8 20.7 %collective-permute-start.1 = (bf16[176,1280]{1,0:T(8,128)(2,1)S(1)}, bf16[176,1280]{1,0:T(8,128)(2,1)S(1)}, u32[]{:S(2)}, u32[]{:S(2)}) collective-permute-start(bf16[176,1280]{1,0:T(8,128)(2,1)S(1)} %copy-done.6), channel_id=1, source_target_pairs={{0,8},{1,9},{2,10},{3,11},{4,12},{5,13},{6,14},{7,15},{8,0},{9,1},... | collective-permute-start | bytes 1351688 | tf_op jit(solution)/shard_map/ppermute | solution.py:27
  43.7 5.9 %collective-permute-start.4 = (bf16[352,1280]{1,0:T(8,128)(2,1)S(1)}, bf16[352,1280]{1,0:T(8,128)(2,1)S(1)}, u32[]{:S(2)}, u32[]{:S(2)}) collective-permute-start(bf16[352,1280]{1,0:T(8,128)(2,1)S(1)} %get-tuple-element.36.refs_0_), channel_id=1, source_target_pairs={{0,1},{1,0},{2,3},{3,2},{4,5},{5,4},{6,7},{7,6},{8,9},{9,8},{10,11... | collective-permute-start | bytes 2703368 | tf_op jit(solution)/shard_map/ppermute | solution.py:27
  43.8 32.1 %collective-permute-start.6 = (bf16[352,1280]{1,0:T(8,128)(2,1)S(1)}, bf16[352,1280]{1,0:T(8,128)(2,1)S(1)}, u32[]{:S(2)}, u32[]{:S(2)}) collective-permute-start(bf16[352,1280]{1,0:T(8,128)(2,1)S(1)} %get-tuple-element.36.refs_0_), channel_id=1, source_target_pairs={{0,8},{1,9},{2,10},{3,11},{4,12},{5,13},{6,14},{7,15},{8,0},{9,1},... | collective-permute-start | bytes 2703368 | tf_op jit(solution)/shard_map/ppermute | solution.py:27
  45.3 15.6 %collective-permute-start.11 = (bf16[176,1280]{1,0:T(8,128)(2,1)S(1)}, bf16[176,1280]{1,0:T(8,128)(2,1)S(1)}, u32[]{:S(2)}, u32[]{:S(2)}) collective-permute-start(bf16[176,1280]{1,0:T(8,128)(2,1)S(1)} %collective-permute-done.refs_0_), channel_id=1, source_target_pairs={{0,2},{1,3},{2,0},{3,1},{4,6},{5,7},{6,4},{7,5},{8,10},{9,11},{10,... | collective-permute-start | bytes 1351688 | tf_op jit(solution)/shard_map/ppermute | solution.py:27
  46.2 28.6 %collective-permute-start.10 = (bf16[176,1280]{1,0:T(8,128)(2,1)S(1)}, bf16[176,1280]{1,0:T(8,128)(2,1)S(1)}, u32[]{:S(2)}, u32[]{:S(2)}) collective-permute-start(bf16[176,1280]{1,0:T(8,128)(2,1)S(1)} %get-tuple-element.41), channel_id=1, source_target_pairs={{0,16},{1,17},{2,18},{3,19},{4,20},{5,21},{6,22},{7,23},{8,24},{9,... | collective-permute-start | bytes 1351688 | tf_op jit(solution)/shard_map/ppermute | solution.py:27
  48.6 26.3 %collective-permute-start.9 = (bf16[176,1280]{1,0:T(8,128)(2,1)S(1)}, bf16[176,1280]{1,0:T(8,128)(2,1)S(1)}, u32[]{:S(2)}, u32[]{:S(2)}) collective-permute-start(bf16[176,1280]{1,0:T(8,128)(2,1)S(1)} %collective-permute-done.1.refs_1_.refs_0_), channel_id=1, source_target_pairs={{0,2},{1,3},{2,0},{3,1},{4,6},{5,7},{6,4},{7,5},{8,10},{9,11},{10,... | collective-permute-start | bytes 1351688 | tf_op jit(solution)/shard_map/ppermute | solution.py:27
  59.3 16.5 %collective-permute-start.7 = (bf16[160,1280]{1,0:T(8,128)(2,1)S(1)}, bf16[160,1280]{1,0:T(8,128)(2,1)S(1)}, u32[]{:S(2)}, u32[]{:S(2)}) collective-permute-start(bf16[160,1280]{1,0:T(8,128)(2,1)S(1)} %get-tuple-element.39), channel_id=1, source_target_pairs={{0,4},{1,5},{2,6},{3,7},{4,0},{5,1},{6,2},{7,3},{8,12},{9,13},{10,... | collective-permute-start | bytes 1228808 | tf_op jit(solution)/shard_map/ppermute | solution.py:27
  75.0 6.1 %collective-permute-start.12 = (bf16[352,1280]{1,0:T(8,128)(2,1)S(1)}, bf16[352,1280]{1,0:T(8,128)(2,1)S(1)}, u32[]{:S(2)}, u32[]{:S(2)}) collective-permute-start(bf16[352,1280]{1,0:T(8,128)(2,1)S(1)} %join.5.refs_2_), channel_id=1, source_target_pairs={{0,1},{1,0},{2,3},{3,2},{4,5},{5,4},{6,7},{7,6},{8,9},{9,8},{10,11... | collective-permute-start | bytes 2703368 | tf_op jit(solution)/shard_map/ppermute | solution.py:27
  75.9 5.2 %collective-permute-start.8 = (bf16[352,1280]{1,0:T(8,128)(2,1)S(1)}, bf16[352,1280]{1,0:T(8,128)(2,1)S(1)}, u32[]{:S(2)}, u32[]{:S(2)}) collective-permute-start(bf16[352,1280]{1,0:T(8,128)(2,1)S(1)} %collective-permute-done.6.refs_0_), channel_id=1, source_target_pairs={{0,1},{1,0},{2,3},{3,2},{4,5},{5,4},{6,7},{7,6},{8,9},{9,8},{10,11... | collective-permute-start | bytes 2703368 | tf_op jit(solution)/shard_map/ppermute | solution.py:27
  75.9 15.2 %collective-permute-start.14 = (bf16[176,1280]{1,0:T(8,128)(2,1)S(1)}, bf16[176,1280]{1,0:T(8,128)(2,1)S(1)}, u32[]{:S(2)}, u32[]{:S(2)}) collective-permute-start(bf16[176,1280]{1,0:T(8,128)(2,1)S(1)} %collective-permute-done.10.refs_0_), channel_id=1, source_target_pairs={{0,2},{1,3},{2,0},{3,1},{4,6},{5,7},{6,4},{7,5},{8,10},{9,11},{10,... | collective-permute-start | bytes 1351688 | tf_op jit(solution)/shard_map/ppermute | solution.py:27
  76.8 14.2 %collective-permute-start.15 = (bf16[176,1280]{1,0:T(8,128)(2,1)S(1)}, bf16[176,1280]{1,0:T(8,128)(2,1)S(1)}, u32[]{:S(2)}, u32[]{:S(2)}) collective-permute-start(bf16[176,1280]{1,0:T(8,128)(2,1)S(1)} %collective-permute-done.10.refs_0_), channel_id=1, source_target_pairs={{0,8},{1,9},{2,10},{3,11},{4,12},{5,13},{6,14},{7,15},{8,0},{9,1},... | collective-permute-start | bytes 1351688 | tf_op jit(solution)/shard_map/ppermute | solution.py:27
  79.6 11.5 %collective-permute-start.5 = (bf16[160,1280]{1,0:T(8,128)(2,1)S(1)}, bf16[160,1280]{1,0:T(8,128)(2,1)S(1)}, u32[]{:S(2)}, u32[]{:S(2)}) collective-permute-start(bf16[160,1280]{1,0:T(8,128)(2,1)S(1)} %get-tuple-element.38), channel_id=1, source_target_pairs={{0,4},{1,5},{2,6},{3,7},{4,0},{5,1},{6,2},{7,3},{8,12},{9,13},{10,... | collective-permute-start | bytes 1228808 | tf_op jit(solution)/shard_map/ppermute | solution.py:27
  81.1 13.5 %collective-permute-start.17 = (bf16[352,1280]{1,0:T(8,128)(2,1)S(1)}, bf16[352,1280]{1,0:T(8,128)(2,1)S(1)}, u32[]{:S(2)}, u32[]{:S(2)}) collective-permute-start(bf16[352,1280]{1,0:T(8,128)(2,1)S(1)} %join.4.refs_3_), channel_id=1, source_target_pairs={{0,1},{1,0},{2,3},{3,2},{4,5},{5,4},{6,7},{7,6},{8,9},{9,8},{10,11... | collective-permute-start | bytes 2703368 | tf_op jit(solution)/shard_map/ppermute | solution.py:27
  91.1 5.4 %collective-permute-start.16 = (bf16[352,1280]{1,0:T(8,128)(2,1)S(1)}, bf16[352,1280]{1,0:T(8,128)(2,1)S(1)}, u32[]{:S(2)}, u32[]{:S(2)}) collective-permute-start(bf16[352,1280]{1,0:T(8,128)(2,1)S(1)} %join.6.refs_1_), channel_id=1, source_target_pairs={{0,1},{1,0},{2,3},{3,2},{4,5},{5,4},{6,7},{7,6},{8,9},{9,8},{10,11... | collective-permute-start | bytes 2703368 | tf_op jit(solution)/shard_map/ppermute | solution.py:27
  91.7 22.0 %collective-permute-start.22 = (bf16[352,1280]{1,0:T(8,128)(2,1)S(1)}, bf16[352,1280]{1,0:T(8,128)(2,1)S(1)}, u32[]{:S(2)}, u32[]{:S(2)}) collective-permute-start(bf16[352,1280]{1,0:T(8,128)(2,1)S(1)} %join.4.refs_3_), channel_id=1, source_target_pairs={{0,8},{1,9},{2,10},{3,11},{4,12},{5,13},{6,14},{7,15},{8,0},{9,1},... | collective-permute-start | bytes 2703368 | tf_op jit(solution)/shard_map/ppermute | solution.py:27
  92.1 20.9 %collective-permute-start.20 = (bf16[176,1280]{1,0:T(8,128)(2,1)S(1)}, bf16[176,1280]{1,0:T(8,128)(2,1)S(1)}, u32[]{:S(2)}, u32[]{:S(2)}) collective-permute-start(bf16[176,1280]{1,0:T(8,128)(2,1)S(1)} %collective-permute-done.15.refs_0_), channel_id=1, source_target_pairs={{0,2},{1,3},{2,0},{3,1},{4,6},{5,7},{6,4},{7,5},{8,10},{9,11},{10,... | collective-permute-start | bytes 1351688 | tf_op jit(solution)/shard_map/ppermute | solution.py:27
  93.0 13.2 %collective-permute-start.13 = (bf16[160,1280]{1,0:T(8,128)(2,1)S(1)}, bf16[160,1280]{1,0:T(8,128)(2,1)S(1)}, u32[]{:S(2)}, u32[]{:S(2)}) collective-permute-start(bf16[160,1280]{1,0:T(8,128)(2,1)S(1)} %get-tuple-element.45), channel_id=1, source_target_pairs={{0,4},{1,5},{2,6},{3,7},{4,0},{5,1},{6,2},{7,3},{8,12},{9,13},{10,... | collective-permute-start | bytes 1228808 | tf_op jit(solution)/shard_map/ppermute | solution.py:27
  94.5 18.4 %collective-permute-start.19 = (bf16[160,1280]{1,0:T(8,128)(2,1)S(1)}, bf16[160,1280]{1,0:T(8,128)(2,1)S(1)}, u32[]{:S(2)}, u32[]{:S(2)}) collective-permute-start(bf16[160,1280]{1,0:T(8,128)(2,1)S(1)} %get-tuple-element.48), channel_id=1, source_target_pairs={{0,4},{1,5},{2,6},{3,7},{4,0},{5,1},{6,2},{7,3},{8,12},{9,13},{10,... | collective-permute-start | bytes 1228808 | tf_op jit(solution)/shard_map/ppermute | solution.py:27
  113.0 5.1 %collective-permute-start.21 = (bf16[352,1280]{1,0:T(8,128)(2,1)S(1)}, bf16[352,1280]{1,0:T(8,128)(2,1)S(1)}, u32[]{:S(2)}, u32[]{:S(2)}) collective-permute-start(bf16[352,1280]{1,0:T(8,128)(2,1)S(1)} %join.7.refs_1_), channel_id=1, source_target_pairs={{0,1},{1,0},{2,3},{3,2},{4,5},{5,4},{6,7},{7,6},{8,9},{9,8},{10,11... | collective-permute-start | bytes 2703368 | tf_op jit(solution)/shard_map/ppermute | solution.py:27
  113.7 4.5 %collective-permute-start.23 = (bf16[352,1280]{1,0:T(8,128)(2,1)S(1)}, bf16[352,1280]{1,0:T(8,128)(2,1)S(1)}, u32[]{:S(2)}, u32[]{:S(2)}) collective-permute-start(bf16[352,1280]{1,0:T(8,128)(2,1)S(1)} %collective-permute-done.22.refs_3_), channel_id=1, source_target_pairs={{0,1},{1,0},{2,3},{3,2},{4,5},{5,4},{6,7},{7,6},{8,9},{9,8},{10,11... | collective-permute-start | bytes 2703368 | tf_op jit(solution)/shard_map/ppermute | solution.py:27
  113.7 21.0 %collective-permute-start.25 = (bf16[160,1280]{1,0:T(8,128)(2,1)S(1)}, bf16[160,1280]{1,0:T(8,128)(2,1)S(1)}, u32[]{:S(2)}, u32[]{:S(2)}) collective-permute-start(bf16[160,1280]{1,0:T(8,128)(2,1)S(1)} %get-tuple-element.55), channel_id=1, source_target_pairs={{0,4},{1,5},{2,6},{3,7},{4,0},{5,1},{6,2},{7,3},{8,12},{9,13},{10,... | collective-permute-start | bytes 1228808 | tf_op jit(solution)/shard_map/ppermute | solution.py:27
  115.1 19.6 %collective-permute-start.18 = (bf16[160,1280]{1,0:T(8,128)(2,1)S(1)}, bf16[160,1280]{1,0:T(8,128)(2,1)S(1)}, u32[]{:S(2)}, u32[]{:S(2)}) collective-permute-start(bf16[160,1280]{1,0:T(8,128)(2,1)S(1)} %get-tuple-element.52), channel_id=1, source_target_pairs={{0,4},{1,5},{2,6},{3,7},{4,0},{5,1},{6,2},{7,3},{8,12},{9,13},{10,... | collective-permute-start | bytes 1228808 | tf_op jit(solution)/shard_map/ppermute | solution.py:27
  128.1 15.4 %collective-permute-start.26 = (bf16[160,1280]{1,0:T(8,128)(2,1)S(1)}, bf16[160,1280]{1,0:T(8,128)(2,1)S(1)}, u32[]{:S(2)}, u32[]{:S(2)}) collective-permute-start(bf16[160,1280]{1,0:T(8,128)(2,1)S(1)} %get-tuple-element.63), channel_id=1, source_target_pairs={{0,4},{1,5},{2,6},{3,7},{4,0},{5,1},{6,2},{7,3},{8,12},{9,13},{10,... | collective-permute-start | bytes 1228808 | tf_op jit(solution)/shard_map/ppermute | solution.py:27
  129.6 22.3 %collective-permute-start.24 = (bf16[160,1280]{1,0:T(8,128)(2,1)S(1)}, bf16[160,1280]{1,0:T(8,128)(2,1)S(1)}, u32[]{:S(2)}, u32[]{:S(2)}) collective-permute-start(bf16[160,1280]{1,0:T(8,128)(2,1)S(1)} %get-tuple-element.60), channel_id=1, source_target_pairs={{0,4},{1,5},{2,6},{3,7},{4,0},{5,1},{6,2},{7,3},{8,12},{9,13},{10,... | collective-permute-start | bytes 1228808 | tf_op jit(solution)/shard_map/ppermute | solution.py:27
  153.6 3.7 %collective-permute-start.28 = (f32[8,128]{1,0:T(8,128)S(1)}, f32[8,128]{1,0:T(8,128)S(1)}, u32[]{:S(2)}, u32[]{:S(2)}) collective-permute-start(f32[8,128]{1,0:T(8,128)S(1)} %products.11.refs_0_), channel_id=1, source_target_pairs={{0,2},{1,3},{2,0},{3,1},{4,6},{5,7},{6,4},{7,5},{8,10},{9,11},{10,... | collective-permute-start | bytes 12296 | tf_op jit(solution)/shard_map/ppermute | solution.py:27
  158.3 4.5 %collective-permute-start.30 = (f32[8,128]{1,0:T(8,128)S(1)}, f32[8,128]{1,0:T(8,128)S(1)}, u32[]{:S(2)}, u32[]{:S(2)}) collective-permute-start(f32[8,128]{1,0:T(8,128)S(1)} %sum_of.3.refs_0_), channel_id=1, source_target_pairs={{0,8},{1,9},{2,10},{3,11},{4,12},{5,13},{6,14},{7,15},{8,0},{9,1},... | collective-permute-start | bytes 12296 | tf_op jit(solution)/shard_map/ppermute | solution.py:27
  159.3 4.5 %collective-permute-start.31 = (f32[8,128]{1,0:T(8,128)S(1)}, f32[8,128]{1,0:T(8,128)S(1)}, u32[]{:S(2)}, u32[]{:S(2)}) collective-permute-start(f32[8,128]{1,0:T(8,128)S(1)} %sum_of.3.refs_0_), channel_id=1, source_target_pairs={{0,16},{1,17},{2,18},{3,19},{4,20},{5,21},{6,22},{7,23},{8,24},{9,... | collective-permute-start | bytes 12296 | tf_op jit(solution)/shard_map/ppermute | solution.py:27
  160.7 5.4 %collective-permute-start.32 = (f32[8,128]{1,0:T(8,128)S(1)}, f32[8,128]{1,0:T(8,128)S(1)}, u32[]{:S(2)}, u32[]{:S(2)}) collective-permute-start(f32[8,128]{1,0:T(8,128)S(1)} %sum_of.3.refs_0_), channel_id=1, source_target_pairs={{0,24},{1,25},{2,26},{3,27},{4,28},{5,29},{6,30},{7,31},{8,16},{9,... | collective-permute-start | bytes 12296 | tf_op jit(solution)/shard_map/ppermute | solution.py:27
  166.7 3.7 %collective-permute-start.33 = (f32[8,128]{1,0:T(8,128)S(1)}, f32[8,128]{1,0:T(8,128)S(1)}, u32[]{:S(2)}, u32[]{:S(2)}) collective-permute-start(f32[8,128]{1,0:T(8,128)S(1)} %sum_of.4.refs_0_), channel_id=1, source_target_pairs={{0,4},{1,5},{2,6},{3,7},{4,0},{5,1},{6,2},{7,3},{8,12},{9,13},{10,... | collective-permute-start | bytes 12296 | tf_op jit(solution)/shard_map/ppermute | solution.py:27
  (9 other events, 71.4 us)

commit v14 on v12

--- a/solution.py
+++ b/solution.py
@@ -88,7 +88,7 @@
     )(operands[0], *after, *operands[1:])
 
 
-WINDOW, SHIFT, OTHER_SHIFT, MEMBER, NEAR, FAR, PART, PIECE = range(8)
+WINDOW, SHIFT, OTHER_SHIFT, MEMBER, NEAR, FAR, PART, PIECE, OWN_WINDOW, OWN_SHIFT = range(10)
 
 
 def row_start(place_ref, block, where):
@@ -234,7 +234,7 @@
     )
 
 
-def gradient_kernel(wheres, window, own, step_rows, place_ref, *refs):
+def gradient_kernel(wheres, window, own, step_rows, shared, place_ref, *refs):
     error_wheres, input_wheres = wheres
     refs = list(refs)
 
@@ -244,7 +244,8 @@
         return taken
 
     error_refs, input_refs = take(len(error_wheres)), take(len(input_wheres))
-    w_in_ref, w_out_ref, first_ref, second_ref, send_first_ref, send_second_ref = take(6)
+    w_in_ref, w_out_ref, first_ref, second_ref = take(4)
+    send_refs = take(2 if shared else 0)
     errors, inputs, inputs_turned, errors_turned, spread_first, spread_second = refs
     if len(input_refs) == 1:
         inputs = input_refs[0]
@@ -256,12 +257,11 @@
         if len(input_refs) > 1:
             for block, where in zip(input_refs, input_wheres):
                 inputs[pl.ds(row_start(place_ref, block, where), block.shape[0]), :] = block[...]
-        lane = pl.multiple_of(place_ref[WINDOW] * 128, 128)
+        lane = pl.multiple_of(place_ref[WINDOW if shared else OWN_WINDOW] * 128, 128)
         inputs_turned[...] = inputs[:, pl.ds(lane, window * 128)].T
         errors_turned[...] = errors[:, pl.ds(lane, window * 128)].T
 
-    shift = pl.multiple_of(place_ref[SHIFT], step_rows)
-    other_shift = pl.multiple_of(place_ref[OTHER_SHIFT], step_rows)
+    shift = pl.multiple_of(place_ref[SHIFT if shared else OWN_SHIFT], step_rows)
     v = jnp.dot(inputs[...], w_in_ref[...], preferred_element_type=jnp.float32)
     back = lax.dot_general(
         errors[...], w_out_ref[...], (((1,), (1,)), ((), ())), preferred_element_type=jnp.float32
@@ -275,33 +275,35 @@
     dpre = (back * slope).astype(jnp.bfloat16)
     spread_first[...] = jnp.dot(inputs_turned[...], dpre, preferred_element_type=jnp.float32)
     second_ref[...] = spread_second[pl.ds(shift, own), :]
-    send_second_ref[...] = spread_second[pl.ds(other_shift, own), :].astype(jnp.bfloat16)
     first_ref[...] = spread_first[pl.ds(shift, own), :]
-    send_first_ref[...] = spread_first[pl.ds(other_shift, own), :].astype(jnp.bfloat16)
-
-
-def gradient(place, members, swap, errors, inputs, w_in, w_out, after=()):
+    if shared:
+        other = pl.ds(pl.multiple_of(place_ref[OTHER_SHIFT], step_rows), own)
+        send_refs[0][...] = spread_first[other, :].astype(jnp.bfloat16)
+        send_refs[1][...] = spread_second[other, :].astype(jnp.bfloat16)
+
+
+def gradient(place, members, swap, shared, errors, inputs, w_in, w_out, after=()):
     error_arrays, error_wheres = zip(*errors)
     input_arrays, input_wheres = zip(*inputs)
     depth, width = w_in.shape
     rows = sum(a.shape[0] for a in input_arrays)
     own = depth // members
-    reach = max(m * own % 128 for m in range(members) if not m & swap) + (swap + 1) * own
+    starts = [m * own % 128 for m in range(members) if not (shared and m & swap)]
+    reach = max(starts) + (swap + 1 if shared else 1) * own
     window = -(-reach // 128)
     tile = tile_of(width, 640)
     once = pl.Buffered(1)
     return call(
         functools.partial(
-            gradient_kernel, (error_wheres, input_wheres), window, own, math.gcd(own, 128)
+            gradient_kernel, (error_wheres, input_wheres), window, own, math.gcd(own, 128), shared
         ),
         "gradient",
         (place, *error_arrays, *input_arrays, w_in, w_out),
         [
             jax.ShapeDtypeStruct((own, width), jnp.float32),
             jax.ShapeDtypeStruct((own, width), jnp.float32),
-            jax.ShapeDtypeStruct((own, width), jnp.bfloat16),
-            jax.ShapeDtypeStruct((own, width), jnp.bfloat16),
-        ],
+        ]
+        + [jax.ShapeDtypeStruct((own, width), jnp.bfloat16)] * (2 if shared else 0),
         after,
         grid=(width // tile,),
         in_specs=[
@@ -309,7 +311,7 @@
             for a in (*error_arrays, *input_arrays)
         ]
         + [pl.BlockSpec((depth, tile), column), pl.BlockSpec((tile, depth), lambda n, s: (n, 0))],
-        out_specs=[pl.BlockSpec((own, tile), column)] * 4,
+        out_specs=[pl.BlockSpec((own, tile), column)] * (4 if shared else 2),
         scratch_shapes=[
             pltpu.VMEM((rows, depth), jnp.bfloat16),
             pltpu.VMEM((rows, depth), jnp.bfloat16),
@@ -473,21 +475,23 @@
 
     near = shard & 1
     part_rows = row_count // shards
-    own = inputs.shape[1] // members
+    columns = inputs.shape[1] // members
     swap = 1
     bits = [2**b for b in reversed(range(gathered)) if 2**b != swap]
     upper = member // swap % 2
-    first_row = (member - upper * swap) * own
+    first_row = (member - upper * swap) * columns
     place = jnp.stack(
         [
             first_row // 128,
-            first_row % 128 + upper * swap * own,
-            first_row % 128 + (1 - upper) * swap * own,
+            first_row % 128 + upper * swap * columns,
+            first_row % 128 + (1 - upper) * swap * columns,
             member,
             near,
             1 - near,
             part_of(shard),
             part_of(shard) - near * (shards // 2),
+            member * columns // 128,
+            member * columns % 128,
         ]
     ).astype(jnp.int32)
 
@@ -510,7 +514,12 @@
         targets,
         tuple(inputs_of.values()),
     )
-    errors_of = {bit: from_mask(error_piece, bit * others, 0) for bit in bits}
+    high, low = bits
+    errors_of = {
+        high: from_mask(error_piece, high * others, 0),
+        low: from_mask(error, low * others, 0),
+    }
+    inputs_of[high | swap] = from_mask(ordered(inputs_of[high], error), swap * others, 0)
 
     def to_half(piece, *before):
         for bit in reversed(range(1, shard_levels)):
@@ -521,53 +530,58 @@
     def both_halves(half):
         return [(half, NEAR), (from_mask(half, 0, 1), FAR)]
 
-    slots, labels, known, sent, halves = [], [], [], [], {}
+    slots = {}
+
+    def gradient_of(m, half, other_inputs, *after):
+        shared = not m & high or bool(m & low)
+        results = gradient(
+            place, members, swap, shared, both_halves(half), other_inputs, w_in, w_out, after
+        )
+        slots[m] = tuple(results[:2])
+        if shared:
+            slots[m | swap] = tuple(from_mask(a, swap * others, 0) for a in results[2:])
+
+    gradient_of(0, error, [(inputs, None)])
+    own = slots[0][0]
+    halves = {}
+    for bit in bits:
+        halves[bit] = to_half(inputs_of[bit], own, errors_of[high], *halves.values())
+
+    half = errors_of[low] = ordered(
+        errors_of[low], own, slots[swap][0], inputs_of[high | swap]
+    )
+    gradient_of(low, half, both_halves(halves[low]))
+    token = slots[low][0]
+
+    errors_of[high] = ordered(errors_of[high], own)
+    ready = ordered(errors_of[high], half)
+    errors_of[high | low] = from_mask(ready, low * others, 0)
+    errors_of[high | swap] = from_mask(ready, swap * others, 0)
+    halves[high | low] = from_mask(ordered(halves[high], half), low * others, 0)
+    half = to_half(
+        errors_of[high], token, errors_of[high | low], errors_of[high | swap], *slots[swap]
+    )
+    gradient_of(high, half, both_halves(halves[high]))
+    token = slots[high][0]
+
     totals = jnp.zeros((8, 128), jnp.float32)
-    masks = [m for m in range(members) if not m & swap]
-    for n, m in enumerate(masks):
-        if n == 0:
-            half = error
-        elif m in bits:
-            errors_of[m] = ordered(errors_of[m], sent[0])
-            top, of = (bits[0], inputs_of) if n == 1 else (m, errors_of)
-            both = [top | bit for bit in bits[1:]]
-            for to in both:
-                of[to] = from_mask(ordered(of[top], errors_of[m]), (to ^ top) * others, 0)
-            before = [of[to] for to in both] + list(slots[1][: 2 * n - 1]) + sent[1:]
-            half = to_half(errors_of[m], *before)
-            other_inputs = halves[m]
-        else:
-            other_inputs, half = (
-                to_half(ordered(of[m], sent[-2]), sent[-1], *slots[2 * n - 3])
-                for of in (inputs_of, errors_of)
-            )
-        first, second, *send = gradient(
-            place,
-            members,
-            swap,
-            both_halves(half),
-            both_halves(other_inputs) if n else [(inputs, None)],
-            w_in,
-            w_out,
-            known[-2:-1],
-        )
-        if n == 0:
-            for bit in bits:
-                halves[bit] = to_half(inputs_of[bit], send[0], errors_of[bits[0]], *halves.values())
-        sent.append(send[0])
-        slots.append((first, second))
-        labels.append(m)
-        last = n == len(masks) - 1
-        if last:
-            totals = products(place, slots, labels, 1, totals)
-        slots.append(tuple(from_mask(a, swap * others, 0) for a in send))
-        labels.append(m ^ swap)
-        if last:
-            for k in range(2):
-                totals = products(place, [slot[k : k + 1] for slot in slots], labels, 1, totals)
-        else:
-            totals = products(place, slots, labels, 2, totals)
-        known.append(totals)
+    labels = [0, swap, low, high]
+    totals = products(place, [slots[m] for m in labels], labels, 4, totals)
+
+    half = to_half(errors_of[high | low], token)
+    ready = ordered(halves[high | low], token, *slots[low | swap])
+    gradient_of(high | low, half, both_halves(ready), totals)
+    token = slots[high | low][0]
+
+    half = to_half(errors_of[high | swap], token)
+    halves[high | swap] = to_half(inputs_of[high | swap], token)
+    gradient_of(high | swap, half, both_halves(halves[high | swap]))
+    labels += [low | swap, high | low, high | swap]
+    totals = products(place, [slots[m] for m in labels], labels, 3, totals)
+    labels.append(high | low | swap)
+    for k in range(2):
+        totals = products(place, [slots[m][k : k + 1] for m in labels], labels, 1, totals)
+    slots = [slots[m] for m in labels]
 
     rounds = [[(0, mask) for mask in range(1, shards)]]
     rounds.append([(m * others, 0) for m in range(2, members, 2)])

time: 177 us -> 190 us (1.073)
  Pallas kernels: 73.2 us -> 78.7 us
  waiting for transfers between devices: 64.9 us -> 70 us
  starting transfers between devices: 35.1 us -> 37.4 us
    pallas_call x23 -> x22, Pallas kernels: 73.2 us -> 78.7 us  [call(): pl.pallas_call(body, grid_spec=pltpu.PrefetchScalarGridSpec(num_scalar_pr...]
    ppermute x36 -> x38, waiting for transfers between devices: 64.9 us -> 70 us  [from_mask(): return lax.ppermute(value, ('dp', 'tensor'), pairs)]
    ppermute x36 -> x38, starting transfers between devices: 35.1 us -> 37.4 us  [from_mask(): return lax.ppermute(value, ('dp', 'tensor'), pairs)]
  transfers between devices with their start and end apart: 36 -> 38, of which waited for: 21 -> 15; matrix products, arithmetic and copies ran while one was open for 0% -> 0% of each run, Pallas kernels for 31% -> 31%
where the time goes in v14:
time: 190 us; the launch traced here: 189 us
  Pallas kernels  78.7 us (41%)
  waiting for transfers between devices  70 us (37%)
  starting transfers between devices  37.4 us (20%)
    pallas_call x22, Pallas kernels, call(): pl.pallas_call(body, grid_spec=pltpu.PrefetchScalarGridSpec(num_scalar_pr...  78.7 us
    ppermute x38, waiting for transfers between devices, from_mask(): return lax.ppermute(value, ('dp', 'tensor'), pairs)  70 us
    ppermute x38, starting transfers between devices, from_mask(): return lax.ppermute(value, ('dp', 'tensor'), pairs)  37.4 us
  transfers between devices with their start and end apart: 38, of which 15 were waited for; matrix products, arithmetic and copies ran while one was open for 0% of the time, Pallas kernels for 31%

profile of v14, /device:TPU:0, one launch (start us, length us, event | category | flops | bytes accessed | tf_op | source)
XLA Modules:
  0.0 189.3 jit_solution(2074427407676087607)
XLA Ops:
  1.3 10.7 %forward.1 = (f32[352,1280]{1,0:T(8,128)}, bf16[352,1280]{1,0:T(8,128)(2,1)}, bf16[176,1280]{1,0:T(8,128)(2,1)}) custom-call(s32[10]{0:T(128)} %stack.43.place_ref, bf16[704,1280]{1,0:T(8,128)(2,1)} %refs_2_.3, bf16[1280,1280]{1,0:T(8,128)(2,1)} %refs_4_.9, bf16[1280,1280]{1,0:T(8,128)(2,1)} %refs_5_.7), custom_call_target="tpu_custom_call" | custom-call | flops 1 | bytes 1 | tf_op jit(solution)/shard_map/forward/pallas_call | solution.py:81
  13.6 2.7 %product.1 = f32[352,1280]{1,0:T(8,128)S(1)} custom-call(s32[10]{0:T(128)S(1)} %copy-done.5, bf16[352,1280]{1,0:T(8,128)(2,1)S(1)} %copy-done.4, bf16[1280,1280]{1,0:T(8,128)(2,1)S(1)} %copy-done), custom_call_target="tpu_custom_call" | custom-call | flops 1 | bytes 1 | tf_op jit(solution)/shard_map/product/pallas_call | solution.py:81
  16.6 2.6 %collective-permute-start.3 = (f16[352,1280]{1,0:T(8,128)(2,1)S(1)}, f16[352,1280]{1,0:T(8,128)(2,1)S(1)}, u32[]{:S(2)}, u32[]{:S(2)}) collective-permute-start(f16[352,1280]{1,0:T(8,128)(2,1)S(1)} %get-tuple-element.68), channel_id=1, source_target_pairs={{0,2},{1,3},{2,0},{3,1},{4,6},{5,7},{6,4},{7,5},{8,10},{9,11},{10,... | collective-permute-start | bytes 2703368 | tf_op jit(solution)/shard_map/ppermute | solution.py:27
  19.2 2.6 %collective-permute-start = (bf16[176,1280]{1,0:T(8,128)(2,1)S(1)}, bf16[176,1280]{1,0:T(8,128)(2,1)S(1)}, u32[]{:S(2)}, u32[]{:S(2)}) collective-permute-start(bf16[176,1280]{1,0:T(8,128)(2,1)S(1)} %copy-done.6), channel_id=1, source_target_pairs={{0,16},{1,17},{2,18},{3,19},{4,20},{5,21},{6,22},{7,23},{8,24},{9,... | collective-permute-start | bytes 1351688 | tf_op jit(solution)/shard_map/ppermute | solution.py:27
  21.8 1.6 collective-permute-start.1
  23.4 16.5 %collective-permute-done.3 = f16[352,1280]{1,0:T(8,128)(2,1)S(1)} collective-permute-done((f16[352,1280]{1,0:T(8,128)(2,1)S(1)}, f16[352,1280]{1,0:T(8,128)(2,1)S(1)}, u32[]{:S(2)}, u32[]{:S(2)}) %collective-permute-start.3) | collective-permute-done | bytes 901152 | tf_op jit(solution)/shard_map/ppermute | solution.py:27
  40.0 2.3 %collective-permute-done.refs_0_ = bf16[176,1280]{1,0:T(8,128)(2,1)S(1)} collective-permute-done((bf16[176,1280]{1,0:T(8,128)(2,1)S(1)}, bf16[176,1280]{1,0:T(8,128)(2,1)S(1)}, u32[]{:S(2)}, u32[]{:S(2)}) %collective-permute-start) | collective-permute-done | bytes 450592 | tf_op jit(solution)/shard_map/ppermute | solution.py:27
  46.1 2.3 %collective-permute-start.11 = (bf16[176,1280]{1,0:T(8,128)(2,1)S(1)}, bf16[176,1280]{1,0:T(8,128)(2,1)S(1)}, u32[]{:S(2)}, u32[]{:S(2)}) collective-permute-start(bf16[176,1280]{1,0:T(8,128)(2,1)S(1)} %get-tuple-element.45), channel_id=1, source_target_pairs={{0,16},{1,17},{2,18},{3,19},{4,20},{5,21},{6,22},{7,23},{8,24},{9,... | collective-permute-start | bytes 1351688 | tf_op jit(solution)/shard_map/ppermute | solution.py:27
  49.6 1.5 collective-permute-start.8
  51.1 9.6 %gradient.5 = (f32[160,1280]{1,0:T(8,128)S(1)}, f32[160,1280]{1,0:T(8,128)S(1)}, bf16[160,1280]{1,0:T(8,128)(2,1)S(1)}, bf16[160,1280]{1,0:T(8,128)(2,1)S(1)}) custom-call(s32[10]{0:T(128)S(1)} %copy-done.5, bf16[352,1280]{1,0:T(8,128)(2,1)S(1)} %get-tuple-element.38.refs_0_, bf16[352,1280]{1,0:T(8,128)(2,1)S(1)} %collective-permute-done.4.refs_1_, ...), custom_call_target="tpu_custom_call" | custom-call | flops 1 | bytes 1 | tf_op jit(solution)/shard_map/gradient/pallas_call | solution.py:81
  61.3 13.4 %collective-permute-done.11.refs_0_ = bf16[176,1280]{1,0:T(8,128)(2,1)S(1)} collective-permute-done((bf16[176,1280]{1,0:T(8,128)(2,1)S(1)}, bf16[176,1280]{1,0:T(8,128)(2,1)S(1)}, u32[]{:S(2)}, u32[]{:S(2)}) %collective-permute-start.11) | collective-permute-done | bytes 450592 | tf_op jit(solution)/shard_map/ppermute | solution.py:27
  76.7 2.8 %collective-permute-start.15 = (bf16[176,1280]{1,0:T(8,128)(2,1)S(1)}, bf16[176,1280]{1,0:T(8,128)(2,1)S(1)}, u32[]{:S(2)}, u32[]{:S(2)}) collective-permute-start(bf16[176,1280]{1,0:T(8,128)(2,1)S(1)} %collective-permute-done.11.refs_0_), channel_id=1, source_target_pairs={{0,8},{1,9},{2,10},{3,11},{4,12},{5,13},{6,14},{7,15},{8,0},{9,1},... | collective-permute-start | bytes 1351688 | tf_op jit(solution)/shard_map/ppermute | solution.py:27
  81.6 9.9 %gradient.6 = (f32[160,1280]{1,0:T(8,128)S(1)}, f32[160,1280]{1,0:T(8,128)S(1)}, bf16[160,1280]{1,0:T(8,128)(2,1)S(1)}, bf16[160,1280]{1,0:T(8,128)(2,1)S(1)}) custom-call(s32[10]{0:T(128)S(1)} %copy-done.5, bf16[352,1280]{1,0:T(8,128)(2,1)S(1)} %collective-permute-done.6.refs_0_, bf16[352,1280]{1,0:T(8,128)(2,1)S(1)} %collective-permute-done.9.refs_1_, ...), custom_call_target="tpu_custom_call" | custom-call | flops 1 | bytes 1 | tf_op jit(solution)/shard_map/gradient/pallas_call | solution.py:81
  91.5 8.6 %collective-permute-done.5.refs_3_.refs_1_.refs_4_ = bf16[160,1280]{1,0:T(8,128)(2,1)S(1)} collective-permute-done((bf16[160,1280]{1,0:T(8,128)(2,1)S(1)}, bf16[160,1280]{1,0:T(8,128)(2,1)S(1)}, u32[]{:S(2)}, u32[]{:S(2)}) %collective-permute-start.5) | collective-permute-done | bytes 409632 | tf_op jit(solution)/shard_map/ppermute | solution.py:27
  103.7 8.9 %gradient.7 = (f32[160,1280]{1,0:T(8,128)S(1)}, f32[160,1280]{1,0:T(8,128)S(1)}) custom-call(s32[10]{0:T(128)S(1)} %copy-done.5, bf16[352,1280]{1,0:T(8,128)(2,1)S(1)} %join.8.refs_0_, bf16[352,1280]{1,0:T(8,128)(2,1)S(1)} %collective-permute-done.17.refs_1_, bf16[352,1280]{1,0:T(8,128)(2,1)S(1)} %join.6.refs_2_, ...), custom_call_target="tpu_custom_call" | custom-call | flops 1 | bytes 1 | tf_op jit(solution)/shard_map/gradient/pallas_call | solution.py:81
  112.6 10.1 %collective-permute-done.22.refs_3_ = bf16[352,1280]{1,0:T(8,128)(2,1)S(1)} collective-permute-done((bf16[352,1280]{1,0:T(8,128)(2,1)S(1)}, bf16[352,1280]{1,0:T(8,128)(2,1)S(1)}, u32[]{:S(2)}, u32[]{:S(2)}) %collective-permute-start.22) | collective-permute-done | bytes 901152 | tf_op jit(solution)/shard_map/ppermute | solution.py:27
  125.3 2.7 %products.4.refs_0_.refs_14_ = f32[8,128]{1,0:T(8,128)S(1)} custom-call(s32[10]{0:T(128)S(1)} %copy-done.5, f32[160,1280]{1,0:T(8,128)S(1)} %get-tuple-element.41.refs_0_.refs_1_, f32[160,1280]{1,0:T(8,128)S(1)} %get-tuple-element.39.refs_1_.refs_0_.refs_2_, bf16[160,1280]{1,0:T(8,128)(2,1)S(1)} %collective-permute-done.7.refs_2_.refs_1_.refs_3_, ...), custom_call_target="tpu_custom_call" | custom-call | flops 1 | bytes 1 | tf_op jit(solution)/shard_map/products/pallas_call | solution.py:81
  128.1 10.0 %gradient.8 = (f32[160,1280]{1,0:T(8,128)S(1)}, f32[160,1280]{1,0:T(8,128)S(1)}, bf16[160,1280]{1,0:T(8,128)(2,1)S(1)}, bf16[160,1280]{1,0:T(8,128)(2,1)S(1)}) custom-call(s32[10]{0:T(128)S(1)} %copy-done.5, f32[8,128]{1,0:T(8,128)S(1)} %products.4.refs_0_.refs_14_, bf16[352,1280]{1,0:T(8,128)(2,1)S(1)} %join.9.refs_1_, ...), custom_call_target="tpu_custom_call" | custom-call | flops 1 | bytes 1 | tf_op jit(solution)/shard_map/gradient/pallas_call | solution.py:81
  138.3 7.0 %collective-permute-done.25.refs_1_ = bf16[176,1280]{1,0:T(8,128)(2,1)S(1)} collective-permute-done((bf16[176,1280]{1,0:T(8,128)(2,1)S(1)}, bf16[176,1280]{1,0:T(8,128)(2,1)S(1)}, u32[]{:S(2)}, u32[]{:S(2)}) %collective-permute-start.25) | collective-permute-done | bytes 450592 | tf_op jit(solution)/shard_map/ppermute | solution.py:27
  145.4 1.6 collective-permute-start.30
  147.9 8.9 %gradient.9 = (f32[160,1280]{1,0:T(8,128)S(1)}, f32[160,1280]{1,0:T(8,128)S(1)}) custom-call(s32[10]{0:T(128)S(1)} %copy-done.5, bf16[352,1280]{1,0:T(8,128)(2,1)S(1)} %join.10.refs_0_, bf16[352,1280]{1,0:T(8,128)(2,1)S(1)} %collective-permute-done.26.refs_1_, bf16[352,1280]{1,0:T(8,128)(2,1)S(1)} %join.11.refs_2_, ...), custom_call_target="tpu_custom_call" | custom-call | flops 1 | bytes 1 | tf_op jit(solution)/shard_map/gradient/pallas_call | solution.py:81
  156.8 4.7 %products.5.refs_8_ = f32[8,128]{1,0:T(8,128)S(1)} custom-call(s32[10]{0:T(128)S(1)} %copy-done.5, f32[160,1280]{1,0:T(8,128)S(1)} %get-tuple-element.41.refs_0_.refs_1_, f32[160,1280]{1,0:T(8,128)S(1)} %get-tuple-element.39.refs_1_.refs_0_.refs_2_, bf16[160,1280]{1,0:T(8,128)(2,1)S(1)} %collective-permute-done.7.refs_2_.refs_1_.refs_3_, ...), custom_call_target="tpu_custom_call" | custom-call | flops 1 | bytes 1 | tf_op jit(solution)/shard_map/products/pallas_call | solution.py:81
  161.4 1.7 products.6.refs_8_
  163.2 2.9 %collective-permute-done.29.refs_7_.refs_16_ = bf16[160,1280]{1,0:T(8,128)(2,1)S(1)} collective-permute-done((bf16[160,1280]{1,0:T(8,128)(2,1)S(1)}, bf16[160,1280]{1,0:T(8,128)(2,1)S(1)}, u32[]{:S(2)}, u32[]{:S(2)}) %collective-permute-start.29) | collective-permute-done | bytes 409632 | tf_op jit(solution)/shard_map/ppermute | solution.py:27
  166.1 1.7 products.7.refs_0_
  169.8 1.8 collective-permute-done.32.refs_2_
  173.4 1.7 collective-permute-start.35
  175.1 2.0 %collective-permute-start.36 = (f32[8,128]{1,0:T(8,128)S(1)}, f32[8,128]{1,0:T(8,128)S(1)}, u32[]{:S(2)}, u32[]{:S(2)}) collective-permute-start(f32[8,128]{1,0:T(8,128)S(1)} %sum_of.3.refs_0_), channel_id=1, source_target_pairs={{0,24},{1,25},{2,26},{3,27},{4,28},{5,29},{6,30},{7,31},{8,16},{9,... | collective-permute-start | bytes 12296 | tf_op jit(solution)/shard_map/ppermute | solution.py:27
  177.9 2.6 %collective-permute-done.36.refs_3_ = f32[8,128]{1,0:T(8,128)S(1)} collective-permute-done((f32[8,128]{1,0:T(8,128)S(1)}, f32[8,128]{1,0:T(8,128)S(1)}, u32[]{:S(2)}, u32[]{:S(2)}) %collective-permute-start.36) | collective-permute-done | bytes 4128 | tf_op jit(solution)/shard_map/ppermute | solution.py:27
  181.0 1.6 collective-permute-start.37
  182.6 2.1 %collective-permute-done.37.refs_1_ = f32[8,128]{1,0:T(8,128)S(1)} collective-permute-done((f32[8,128]{1,0:T(8,128)S(1)}, f32[8,128]{1,0:T(8,128)S(1)}, u32[]{:S(2)}, u32[]{:S(2)}) %collective-permute-start.37) | collective-permute-done | bytes 4128 | tf_op jit(solution)/shard_map/ppermute | solution.py:27
  185.2 4.1 %merge.1 = (f32[160,1280]{1,0:T(8,128)}, f32[160,1280]{1,0:T(8,128)}) custom-call(s32[10]{0:T(128)S(1)} %copy-done.5, f32[8,128]{1,0:T(8,128)S(1)} %sum_of.5.refs_0_, f32[160,1280]{1,0:T(8,128)S(1)} %get-tuple-element.41.refs_0_.refs_1_, f32[160,1280]{1,0:T(8,128)S(1)} %get-tuple-element.39.refs_1_.refs_0_.refs_2_, ...), custom_call_target="tpu_custom_call" | custom-call | flops 1 | bytes 1 | tf_op jit(solution)/shard_map/merge/pallas_call | solution.py:81
  (84 shorter events, 25.1 us)
Async XLA Ops:
  12.0 4.4 %collective-permute-start.2 = (f32[352,1280]{1,0:T(8,128)}, f32[352,1280]{1,0:T(8,128)S(1)}, u32[]{:S(2)}, u32[]{:S(2)}) collective-permute-start(f32[352,1280]{1,0:T(8,128)} %get-tuple-element.37), channel_id=1, source_target_pairs={{0,1},{1,0},{2,3},{3,2},{4,5},{5,4},{6,7},{7,6},{8,9},{9,8},{10,11... | collective-permute-start | bytes 5406728 | tf_op jit(solution)/shard_map/ppermute | solution.py:27
  16.6 23.2 %collective-permute-start.3 = (f16[352,1280]{1,0:T(8,128)(2,1)S(1)}, f16[352,1280]{1,0:T(8,128)(2,1)S(1)}, u32[]{:S(2)}, u32[]{:S(2)}) collective-permute-start(f16[352,1280]{1,0:T(8,128)(2,1)S(1)} %get-tuple-element.68), channel_id=1, source_target_pairs={{0,2},{1,3},{2,0},{3,1},{4,6},{5,7},{6,4},{7,5},{8,10},{9,11},{10,... | collective-permute-start | bytes 2703368 | tf_op jit(solution)/shard_map/ppermute | solution.py:27
  19.2 23.1 %collective-permute-start = (bf16[176,1280]{1,0:T(8,128)(2,1)S(1)}, bf16[176,1280]{1,0:T(8,128)(2,1)S(1)}, u32[]{:S(2)}, u32[]{:S(2)}) collective-permute-start(bf16[176,1280]{1,0:T(8,128)(2,1)S(1)} %copy-done.6), channel_id=1, source_target_pairs={{0,16},{1,17},{2,18},{3,19},{4,20},{5,21},{6,22},{7,23},{8,24},{9,... | collective-permute-start | bytes 1351688 | tf_op jit(solution)/shard_map/ppermute | solution.py:27
  21.8 20.7 %collective-permute-start.1 = (bf16[176,1280]{1,0:T(8,128)(2,1)S(1)}, bf16[176,1280]{1,0:T(8,128)(2,1)S(1)}, u32[]{:S(2)}, u32[]{:S(2)}) collective-permute-start(bf16[176,1280]{1,0:T(8,128)(2,1)S(1)} %copy-done.6), channel_id=1, source_target_pairs={{0,8},{1,9},{2,10},{3,11},{4,12},{5,13},{6,14},{7,15},{8,0},{9,1},... | collective-permute-start | bytes 1351688 | tf_op jit(solution)/shard_map/ppermute | solution.py:27
  43.6 6.0 %collective-permute-start.4 = (bf16[352,1280]{1,0:T(8,128)(2,1)S(1)}, bf16[352,1280]{1,0:T(8,128)(2,1)S(1)}, u32[]{:S(2)}, u32[]{:S(2)}) collective-permute-start(bf16[352,1280]{1,0:T(8,128)(2,1)S(1)} %get-tuple-element.38.refs_0_), channel_id=1, source_target_pairs={{0,1},{1,0},{2,3},{3,2},{4,5},{5,4},{6,7},{7,6},{8,9},{9,8},{10,11... | collective-permute-start | bytes 2703368 | tf_op jit(solution)/shard_map/ppermute | solution.py:27
  43.7 32.1 %collective-permute-start.6 = (bf16[352,1280]{1,0:T(8,128)(2,1)S(1)}, bf16[352,1280]{1,0:T(8,128)(2,1)S(1)}, u32[]{:S(2)}, u32[]{:S(2)}) collective-permute-start(bf16[352,1280]{1,0:T(8,128)(2,1)S(1)} %get-tuple-element.38.refs_0_), channel_id=1, source_target_pairs={{0,8},{1,9},{2,10},{3,11},{4,12},{5,13},{6,14},{7,15},{8,0},{9,1},... | collective-permute-start | bytes 2703368 | tf_op jit(solution)/shard_map/ppermute | solution.py:27
  45.2 15.5 %collective-permute-start.12 = (bf16[176,1280]{1,0:T(8,128)(2,1)S(1)}, bf16[176,1280]{1,0:T(8,128)(2,1)S(1)}, u32[]{:S(2)}, u32[]{:S(2)}) collective-permute-start(bf16[176,1280]{1,0:T(8,128)(2,1)S(1)} %collective-permute-done.refs_0_), channel_id=1, source_target_pairs={{0,2},{1,3},{2,0},{3,1},{4,6},{5,7},{6,4},{7,5},{8,10},{9,11},{10,... | collective-permute-start | bytes 1351688 | tf_op jit(solution)/shard_map/ppermute | solution.py:27
  46.1 28.6 %collective-permute-start.11 = (bf16[176,1280]{1,0:T(8,128)(2,1)S(1)}, bf16[176,1280]{1,0:T(8,128)(2,1)S(1)}, u32[]{:S(2)}, u32[]{:S(2)}) collective-permute-start(bf16[176,1280]{1,0:T(8,128)(2,1)S(1)} %get-tuple-element.45), channel_id=1, source_target_pairs={{0,16},{1,17},{2,18},{3,19},{4,20},{5,21},{6,22},{7,23},{8,24},{9,... | collective-permute-start | bytes 1351688 | tf_op jit(solution)/shard_map/ppermute | solution.py:27
  48.5 26.3 %collective-permute-start.10 = (bf16[176,1280]{1,0:T(8,128)(2,1)S(1)}, bf16[176,1280]{1,0:T(8,128)(2,1)S(1)}, u32[]{:S(2)}, u32[]{:S(2)}) collective-permute-start(bf16[176,1280]{1,0:T(8,128)(2,1)S(1)} %collective-permute-done.1.refs_1_.refs_0_), channel_id=1, source_target_pairs={{0,2},{1,3},{2,0},{3,1},{4,6},{5,7},{6,4},{7,5},{8,10},{9,11},{10,... | collective-permute-start | bytes 1351688 | tf_op jit(solution)/shard_map/ppermute | solution.py:27
  49.6 25.4 %collective-permute-start.8 = (bf16[176,1280]{1,0:T(8,128)(2,1)S(1)}, bf16[176,1280]{1,0:T(8,128)(2,1)S(1)}, u32[]{:S(2)}, u32[]{:S(2)}) collective-permute-start(bf16[176,1280]{1,0:T(8,128)(2,1)S(1)} %collective-permute-done.refs_0_), channel_id=1, source_target_pairs={{0,4},{1,5},{2,6},{3,7},{4,0},{5,1},{6,2},{7,3},{8,12},{9,13},{10,... | collective-permute-start | bytes 1351688 | tf_op jit(solution)/shard_map/ppermute | solution.py:27
  60.7 15.0 %collective-permute-start.7 = (bf16[160,1280]{1,0:T(8,128)(2,1)S(1)}, bf16[160,1280]{1,0:T(8,128)(2,1)S(1)}, u32[]{:S(2)}, u32[]{:S(2)}) collective-permute-start(bf16[160,1280]{1,0:T(8,128)(2,1)S(1)} %get-tuple-element.42), channel_id=1, source_target_pairs={{0,4},{1,5},{2,6},{3,7},{4,0},{5,1},{6,2},{7,3},{8,12},{9,13},{10,... | collective-permute-start | bytes 1228808 | tf_op jit(solution)/shard_map/ppermute | solution.py:27
  74.9 6.2 %collective-permute-start.13 = (bf16[352,1280]{1,0:T(8,128)(2,1)S(1)}, bf16[352,1280]{1,0:T(8,128)(2,1)S(1)}, u32[]{:S(2)}, u32[]{:S(2)}) collective-permute-start(bf16[352,1280]{1,0:T(8,128)(2,1)S(1)} %join.7.refs_2_), channel_id=1, source_target_pairs={{0,1},{1,0},{2,3},{3,2},{4,5},{5,4},{6,7},{7,6},{8,9},{9,8},{10,11... | collective-permute-start | bytes 2703368 | tf_op jit(solution)/shard_map/ppermute | solution.py:27
  75.8 5.8 %collective-permute-start.9 = (bf16[352,1280]{1,0:T(8,128)(2,1)S(1)}, bf16[352,1280]{1,0:T(8,128)(2,1)S(1)}, u32[]{:S(2)}, u32[]{:S(2)}) collective-permute-start(bf16[352,1280]{1,0:T(8,128)(2,1)S(1)} %collective-permute-done.6.refs_0_), channel_id=1, source_target_pairs={{0,1},{1,0},{2,3},{3,2},{4,5},{5,4},{6,7},{7,6},{8,9},{9,8},{10,11... | collective-permute-start | bytes 2703368 | tf_op jit(solution)/shard_map/ppermute | solution.py:27
  75.8 24.3 %collective-permute-start.14 = (bf16[176,1280]{1,0:T(8,128)(2,1)S(1)}, bf16[176,1280]{1,0:T(8,128)(2,1)S(1)}, u32[]{:S(2)}, u32[]{:S(2)}) collective-permute-start(bf16[176,1280]{1,0:T(8,128)(2,1)S(1)} %collective-permute-done.11.refs_0_), channel_id=1, source_target_pairs={{0,2},{1,3},{2,0},{3,1},{4,6},{5,7},{6,4},{7,5},{8,10},{9,11},{10,... | collective-permute-start | bytes 1351688 | tf_op jit(solution)/shard_map/ppermute | solution.py:27
  76.7 23.4 %collective-permute-start.15 = (bf16[176,1280]{1,0:T(8,128)(2,1)S(1)}, bf16[176,1280]{1,0:T(8,128)(2,1)S(1)}, u32[]{:S(2)}, u32[]{:S(2)}) collective-permute-start(bf16[176,1280]{1,0:T(8,128)(2,1)S(1)} %collective-permute-done.11.refs_0_), channel_id=1, source_target_pairs={{0,8},{1,9},{2,10},{3,11},{4,12},{5,13},{6,14},{7,15},{8,0},{9,1},... | collective-permute-start | bytes 1351688 | tf_op jit(solution)/shard_map/ppermute | solution.py:27
  79.5 20.6 %collective-permute-start.16 = (bf16[176,1280]{1,0:T(8,128)(2,1)S(1)}, bf16[176,1280]{1,0:T(8,128)(2,1)S(1)}, u32[]{:S(2)}, u32[]{:S(2)}) collective-permute-start(bf16[176,1280]{1,0:T(8,128)(2,1)S(1)} %collective-permute-done.11.refs_0_), channel_id=1, source_target_pairs={{0,4},{1,5},{2,6},{3,7},{4,0},{5,1},{6,2},{7,3},{8,12},{9,13},{10,... | collective-permute-start | bytes 1351688 | tf_op jit(solution)/shard_map/ppermute | solution.py:27
  81.1 19.0 %collective-permute-start.5 = (bf16[160,1280]{1,0:T(8,128)(2,1)S(1)}, bf16[160,1280]{1,0:T(8,128)(2,1)S(1)}, u32[]{:S(2)}, u32[]{:S(2)}) collective-permute-start(bf16[160,1280]{1,0:T(8,128)(2,1)S(1)} %get-tuple-element.40), channel_id=1, source_target_pairs={{0,4},{1,5},{2,6},{3,7},{4,0},{5,1},{6,2},{7,3},{8,12},{9,13},{10,... | collective-permute-start | bytes 1228808 | tf_op jit(solution)/shard_map/ppermute | solution.py:27
  81.6 21.6 %collective-permute-start.18 = (bf16[352,1280]{1,0:T(8,128)(2,1)S(1)}, bf16[352,1280]{1,0:T(8,128)(2,1)S(1)}, u32[]{:S(2)}, u32[]{:S(2)}) collective-permute-start(bf16[352,1280]{1,0:T(8,128)(2,1)S(1)} %join.6.refs_2_), channel_id=1, source_target_pairs={{0,1},{1,0},{2,3},{3,2},{4,5},{5,4},{6,7},{7,6},{8,9},{9,8},{10,11... | collective-permute-start | bytes 2703368 | tf_op jit(solution)/shard_map/ppermute | solution.py:27
  100.2 22.4 %collective-permute-start.22 = (bf16[352,1280]{1,0:T(8,128)(2,1)S(1)}, bf16[352,1280]{1,0:T(8,128)(2,1)S(1)}, u32[]{:S(2)}, u32[]{:S(2)}) collective-permute-start(bf16[352,1280]{1,0:T(8,128)(2,1)S(1)} %join.6.refs_2_), channel_id=1, source_target_pairs={{0,8},{1,9},{2,10},{3,11},{4,12},{5,13},{6,14},{7,15},{8,0},{9,1},... | collective-permute-start | bytes 2703368 | tf_op jit(solution)/shard_map/ppermute | solution.py:27
  100.6 22.1 %collective-permute-start.20 = (bf16[176,1280]{1,0:T(8,128)(2,1)S(1)}, bf16[176,1280]{1,0:T(8,128)(2,1)S(1)}, u32[]{:S(2)}, u32[]{:S(2)}) collective-permute-start(bf16[176,1280]{1,0:T(8,128)(2,1)S(1)} %collective-permute-done.15.refs_0_), channel_id=1, source_target_pairs={{0,2},{1,3},{2,0},{3,1},{4,6},{5,7},{6,4},{7,5},{8,10},{9,11},{10,... | collective-permute-start | bytes 1351688 | tf_op jit(solution)/shard_map/ppermute | solution.py:27
  101.7 21.0 %collective-permute-start.19 = (bf16[160,1280]{1,0:T(8,128)(2,1)S(1)}, bf16[160,1280]{1,0:T(8,128)(2,1)S(1)}, u32[]{:S(2)}, u32[]{:S(2)}) collective-permute-start(bf16[160,1280]{1,0:T(8,128)(2,1)S(1)} %get-tuple-element.54), channel_id=1, source_target_pairs={{0,4},{1,5},{2,6},{3,7},{4,0},{5,1},{6,2},{7,3},{8,12},{9,13},{10,... | collective-permute-start | bytes 1228808 | tf_op jit(solution)/shard_map/ppermute | solution.py:27
  103.2 19.5 %collective-permute-start.23 = (bf16[160,1280]{1,0:T(8,128)(2,1)S(1)}, bf16[160,1280]{1,0:T(8,128)(2,1)S(1)}, u32[]{:S(2)}, u32[]{:S(2)}) collective-permute-start(bf16[160,1280]{1,0:T(8,128)(2,1)S(1)} %get-tuple-element.58), channel_id=1, source_target_pairs={{0,4},{1,5},{2,6},{3,7},{4,0},{5,1},{6,2},{7,3},{8,12},{9,13},{10,... | collective-permute-start | bytes 1228808 | tf_op jit(solution)/shard_map/ppermute | solution.py:27
  122.7 5.4 %collective-permute-start.24 = (bf16[352,1280]{1,0:T(8,128)(2,1)S(1)}, bf16[352,1280]{1,0:T(8,128)(2,1)S(1)}, u32[]{:S(2)}, u32[]{:S(2)}) collective-permute-start(bf16[352,1280]{1,0:T(8,128)(2,1)S(1)} %collective-permute-done.22.refs_3_), channel_id=1, source_target_pairs={{0,1},{1,0},{2,3},{3,2},{4,5},{5,4},{6,7},{7,6},{8,9},{9,8},{10,11... | collective-permute-start | bytes 2703368 | tf_op jit(solution)/shard_map/ppermute | solution.py:27
  122.8 5.3 %collective-permute-start.21 = (bf16[352,1280]{1,0:T(8,128)(2,1)S(1)}, bf16[352,1280]{1,0:T(8,128)(2,1)S(1)}, u32[]{:S(2)}, u32[]{:S(2)}) collective-permute-start(bf16[352,1280]{1,0:T(8,128)(2,1)S(1)} %join.9.refs_1_), channel_id=1, source_target_pairs={{0,1},{1,0},{2,3},{3,2},{4,5},{5,4},{6,7},{7,6},{8,9},{9,8},{10,11... | collective-permute-start | bytes 2703368 | tf_op jit(solution)/shard_map/ppermute | solution.py:27
  123.3 14.8 %collective-permute-start.27 = (bf16[176,1280]{1,0:T(8,128)(2,1)S(1)}, bf16[176,1280]{1,0:T(8,128)(2,1)S(1)}, u32[]{:S(2)}, u32[]{:S(2)}) collective-permute-start(bf16[176,1280]{1,0:T(8,128)(2,1)S(1)} %collective-permute-done.8.refs_0_), channel_id=1, source_target_pairs={{0,2},{1,3},{2,0},{3,1},{4,6},{5,7},{6,4},{7,5},{8,10},{9,11},{10,... | collective-permute-start | bytes 1351688 | tf_op jit(solution)/shard_map/ppermute | solution.py:27
  124.4 20.9 %collective-permute-start.25 = (bf16[176,1280]{1,0:T(8,128)(2,1)S(1)}, bf16[176,1280]{1,0:T(8,128)(2,1)S(1)}, u32[]{:S(2)}, u32[]{:S(2)}) collective-permute-start(bf16[176,1280]{1,0:T(8,128)(2,1)S(1)} %collective-permute-done.16.refs_0_), channel_id=1, source_target_pairs={{0,2},{1,3},{2,0},{3,1},{4,6},{5,7},{6,4},{7,5},{8,10},{9,11},{10,... | collective-permute-start | bytes 1351688 | tf_op jit(solution)/shard_map/ppermute | solution.py:27
  138.2 9.4 %collective-permute-start.28 = (bf16[352,1280]{1,0:T(8,128)(2,1)S(1)}, bf16[352,1280]{1,0:T(8,128)(2,1)S(1)}, u32[]{:S(2)}, u32[]{:S(2)}) collective-permute-start(bf16[352,1280]{1,0:T(8,128)(2,1)S(1)} %join.11.refs_2_), channel_id=1, source_target_pairs={{0,1},{1,0},{2,3},{3,2},{4,5},{5,4},{6,7},{7,6},{8,9},{9,8},{10,11... | collective-permute-start | bytes 2703368 | tf_op jit(solution)/shard_map/ppermute | solution.py:27
  145.4 16.0 %collective-permute-start.30 = (bf16[160,1280]{1,0:T(8,128)(2,1)S(1)}, bf16[160,1280]{1,0:T(8,128)(2,1)S(1)}, u32[]{:S(2)}, u32[]{:S(2)}) collective-permute-start(bf16[160,1280]{1,0:T(8,128)(2,1)S(1)} %get-tuple-element.67), channel_id=1, source_target_pairs={{0,4},{1,5},{2,6},{3,7},{4,0},{5,1},{6,2},{7,3},{8,12},{9,13},{10,... | collective-permute-start | bytes 1228808 | tf_op jit(solution)/shard_map/ppermute | solution.py:27
  147.0 19.1 %collective-permute-start.29 = (bf16[160,1280]{1,0:T(8,128)(2,1)S(1)}, bf16[160,1280]{1,0:T(8,128)(2,1)S(1)}, u32[]{:S(2)}, u32[]{:S(2)}) collective-permute-start(bf16[160,1280]{1,0:T(8,128)(2,1)S(1)} %get-tuple-element.65), channel_id=1, source_target_pairs={{0,4},{1,5},{2,6},{3,7},{4,0},{5,1},{6,2},{7,3},{8,12},{9,13},{10,... | collective-permute-start | bytes 1228808 | tf_op jit(solution)/shard_map/ppermute | solution.py:27
  172.6 4.5 %collective-permute-start.34 = (f32[8,128]{1,0:T(8,128)S(1)}, f32[8,128]{1,0:T(8,128)S(1)}, u32[]{:S(2)}, u32[]{:S(2)}) collective-permute-start(f32[8,128]{1,0:T(8,128)S(1)} %sum_of.3.refs_0_), channel_id=1, source_target_pairs={{0,8},{1,9},{2,10},{3,11},{4,12},{5,13},{6,14},{7,15},{8,0},{9,1},... | collective-permute-start | bytes 12296 | tf_op jit(solution)/shard_map/ppermute | solution.py:27
  173.4 4.5 %collective-permute-start.35 = (f32[8,128]{1,0:T(8,128)S(1)}, f32[8,128]{1,0:T(8,128)S(1)}, u32[]{:S(2)}, u32[]{:S(2)}) collective-permute-start(f32[8,128]{1,0:T(8,128)S(1)} %sum_of.3.refs_0_), channel_id=1, source_target_pairs={{0,16},{1,17},{2,18},{3,19},{4,20},{5,21},{6,22},{7,23},{8,24},{9,... | collective-permute-start | bytes 12296 | tf_op jit(solution)/shard_map/ppermute | solution.py:27
  175.1 5.4 %collective-permute-start.36 = (f32[8,128]{1,0:T(8,128)S(1)}, f32[8,128]{1,0:T(8,128)S(1)}, u32[]{:S(2)}, u32[]{:S(2)}) collective-permute-start(f32[8,128]{1,0:T(8,128)S(1)} %sum_of.3.refs_0_), channel_id=1, source_target_pairs={{0,24},{1,25},{2,26},{3,27},{4,28},{5,29},{6,30},{7,31},{8,16},{9,... | collective-permute-start | bytes 12296 | tf_op jit(solution)/shard_map/ppermute | solution.py:27
  (13 other events, 87.7 us)

commit v15 on v14

--- a/solution.py
+++ b/solution.py
@@ -245,7 +245,7 @@
 
     error_refs, input_refs = take(len(error_wheres)), take(len(input_wheres))
     w_in_ref, w_out_ref, first_ref, second_ref = take(4)
-    send_refs = take(2 if shared else 0)
+    send_refs = take(shared)
     errors, inputs, inputs_turned, errors_turned, spread_first, spread_second = refs
     if len(input_refs) == 1:
         inputs = input_refs[0]
@@ -278,8 +278,9 @@
     first_ref[...] = spread_first[pl.ds(shift, own), :]
     if shared:
         other = pl.ds(pl.multiple_of(place_ref[OTHER_SHIFT], step_rows), own)
-        send_refs[0][...] = spread_first[other, :].astype(jnp.bfloat16)
-        send_refs[1][...] = spread_second[other, :].astype(jnp.bfloat16)
+        send_refs[0][:own, :] = spread_first[other, :].astype(jnp.bfloat16)
+        last = send_refs[-1].shape[0]
+        send_refs[-1][last - own :, :] = spread_second[other, :].astype(jnp.bfloat16)
 
 
 def gradient(place, members, swap, shared, errors, inputs, w_in, w_out, after=()):
@@ -303,7 +304,7 @@
             jax.ShapeDtypeStruct((own, width), jnp.float32),
             jax.ShapeDtypeStruct((own, width), jnp.float32),
         ]
-        + [jax.ShapeDtypeStruct((own, width), jnp.bfloat16)] * (2 if shared else 0),
+        + [jax.ShapeDtypeStruct((2 * own // max(shared, 1), width), jnp.bfloat16)] * shared,
         after,
         grid=(width // tile,),
         in_specs=[
@@ -311,7 +312,8 @@
             for a in (*error_arrays, *input_arrays)
         ]
         + [pl.BlockSpec((depth, tile), column), pl.BlockSpec((tile, depth), lambda n, s: (n, 0))],
-        out_specs=[pl.BlockSpec((own, tile), column)] * (4 if shared else 2),
+        out_specs=[pl.BlockSpec((own, tile), column)] * 2
+        + [pl.BlockSpec((2 * own // max(shared, 1), tile), column)] * shared,
         scratch_shapes=[
             pltpu.VMEM((rows, depth), jnp.bfloat16),
             pltpu.VMEM((rows, depth), jnp.bfloat16),
@@ -355,8 +357,9 @@
 
 
 def products(place, slots, labels, fresh, known, after=()):
-    arrays = [a for slot in slots for a in slot]
-    own, width = slots[0][0].shape
+    arrays = [a for slot in slots for a, _ in slot]
+    blocks = [k for slot in slots for _, k in slot]
+    own, width = arrays[0].shape
     tile = tile_of(width, 256)
     pairs = sum(len(slots) - n for n in range(fresh))
     return call(
@@ -366,7 +369,7 @@
         [jax.ShapeDtypeStruct(known.shape, jnp.float32)],
         after,
         grid=(width // tile,),
-        in_specs=[pl.BlockSpec((a.shape[0], tile), lambda n, s: (0, n)) for a in arrays]
+        in_specs=[pl.BlockSpec((own, tile), lambda n, s, k=k: (k, n)) for k in blocks]
         + [pl.BlockSpec(known.shape, whole)],
         out_specs=[pl.BlockSpec(known.shape, whole)],
         scratch_shapes=[pltpu.VMEM((pairs, 8, tile), jnp.float32)],
@@ -436,10 +439,16 @@
 
 
 def merge(place, totals, slots, labels):
-    own, width = slots[0][0].shape
+    arrays = [a for slot in slots for a, _ in slot]
+    own, width = arrays[0].shape
     block = max(b for b in range(16, min(own, 32) + 1, 16) if own % b == 0)
+    steps = own // block
     spec = pl.BlockSpec((block, width), lambda n, s: (n, 0))
-    arrays = [a for slot in slots for a in slot]
+    specs = [
+        pl.BlockSpec((block, width), lambda n, s, k=k: (n + k * steps, 0))
+        for slot in slots
+        for _, k in slot
+    ]
     shape = jax.ShapeDtypeStruct((own, width), jnp.float32)
     return call(
         functools.partial(merge_kernel, tuple(labels)),
@@ -447,8 +456,8 @@
         (place, totals, *arrays),
         [shape, shape],
         vmem=16 * 2**20,
-        grid=(own // block,),
-        in_specs=[pl.BlockSpec(memory_space=pltpu.SMEM)] + [spec] * len(arrays),
+        grid=(steps,),
+        in_specs=[pl.BlockSpec(memory_space=pltpu.SMEM)] + specs,
         out_specs=[spec, spec],
         scratch_shapes=[pltpu.SMEM((len(slots),), jnp.float32)],
     )
@@ -530,50 +539,52 @@
     def both_halves(half):
         return [(half, NEAR), (from_mask(half, 0, 1), FAR)]
 
-    slots = {}
+    slots, got = {}, {}
 
     def gradient_of(m, half, other_inputs, *after):
-        shared = not m & high or bool(m & low)
-        results = gradient(
+        shared = 2 if m == high | low else 0 if m & high else 1
+        first, second, *send = gradient(
             place, members, swap, shared, both_halves(half), other_inputs, w_in, w_out, after
         )
-        slots[m] = tuple(results[:2])
+        if m == 0:
+            send = [ordered(a, inputs_of[high | swap]) for a in send]
+        slots[m] = ((first, 0), (second, 0))
+        got[m] = [from_mask(a, swap * others, 0) for a in send]
         if shared:
-            slots[m | swap] = tuple(from_mask(a, swap * others, 0) for a in results[2:])
+            slots[m | swap] = ((got[m][0], 0), (got[m][-1], 2 - shared))
 
     gradient_of(0, error, [(inputs, None)])
-    own = slots[0][0]
+    own = slots[0][0][0]
     halves = {}
     for bit in bits:
         halves[bit] = to_half(inputs_of[bit], own, errors_of[high], *halves.values())
 
-    half = errors_of[low] = ordered(
-        errors_of[low], own, slots[swap][0], inputs_of[high | swap]
-    )
+    errors_of[low] = ordered(errors_of[low], own)
+    half = ordered(errors_of[low], *got[0])
     gradient_of(low, half, both_halves(halves[low]))
-    token = slots[low][0]
+    token = slots[low][0][0]
 
     errors_of[high] = ordered(errors_of[high], own)
-    ready = ordered(errors_of[high], half)
+    ready = ordered(errors_of[high], errors_of[low])
     errors_of[high | low] = from_mask(ready, low * others, 0)
     errors_of[high | swap] = from_mask(ready, swap * others, 0)
     halves[high | low] = from_mask(ordered(halves[high], half), low * others, 0)
-    half = to_half(
-        errors_of[high], token, errors_of[high | low], errors_of[high | swap], *slots[swap]
-    )
+    before = (errors_of[high | low], errors_of[high | swap])
+    half = to_half(errors_of[high], token, *before)
     gradient_of(high, half, both_halves(halves[high]))
-    token = slots[high][0]
+    token = slots[high][0][0]
 
     totals = jnp.zeros((8, 128), jnp.float32)
     labels = [0, swap, low, high]
     totals = products(place, [slots[m] for m in labels], labels, 4, totals)
 
     half = to_half(errors_of[high | low], token)
-    ready = ordered(halves[high | low], token, *slots[low | swap])
+    partner_half = to_half(errors_of[high | swap], token)
+    ready = ordered(halves[high | low], token, *got[low], partner_half)
     gradient_of(high | low, half, both_halves(ready), totals)
-    token = slots[high | low][0]
-
-    half = to_half(errors_of[high | swap], token)
+    token = slots[high | low][0][0]
+
+    half = ordered(partner_half, token)
     halves[high | swap] = to_half(inputs_of[high | swap], token)
     gradient_of(high | swap, half, both_halves(halves[high | swap]))
     labels += [low | swap, high | low, high | swap]

time: 190 us -> 175 us (0.921)
  waiting for transfers between devices: 70 us -> 59.8 us
  starting transfers between devices: 37.4 us -> 33.6 us
    ppermute x38 -> x36, waiting for transfers between devices: 70 us -> 59.8 us  [from_mask(): return lax.ppermute(value, ('dp', 'tensor'), pairs)]
    ppermute x38 -> x36, starting transfers between devices: 37.4 us -> 33.6 us  [from_mask(): return lax.ppermute(value, ('dp', 'tensor'), pairs)]
  transfers between devices with their start and end apart: 38 -> 36, of which waited for: 15 -> 19; matrix products, arithmetic and copies ran while one was open for 0% -> 0% of each run, Pallas kernels for 31% -> 34%
where the time goes in v15:
time: 175 us
  Pallas kernels  78.7 us (45%)
  waiting for transfers between devices  59.8 us (34%)
  starting transfers between devices  33.6 us (19%)
  local copies, waits for them, and re-layouts  1.78 us (1%)
    pallas_call x22, Pallas kernels, call(): pl.pallas_call(body, grid_spec=pltpu.PrefetchScalarGridSpec(num_scalar_pr...  78.7 us
    ppermute x36, waiting for transfers between devices, from_mask(): return lax.ppermute(value, ('dp', 'tensor'), pairs)  59.8 us
    ppermute x36, starting transfers between devices, from_mask(): return lax.ppermute(value, ('dp', 'tensor'), pairs)  33.6 us
  transfers between devices with their start and end apart: 36, of which 19 were waited for; matrix products, arithmetic and copies ran while one was open for 0% of the time, Pallas kernels for 34%

profile of v15, /device:TPU:0, one launch (start us, length us, event | category | flops | bytes accessed | tf_op | source)
XLA Modules:
  0.0 175.3 jit_solution(5055773828116083338)
XLA Ops:
  1.3 10.7 %forward.1 = (f32[352,1280]{1,0:T(8,128)}, bf16[352,1280]{1,0:T(8,128)(2,1)}, bf16[176,1280]{1,0:T(8,128)(2,1)}) custom-call(s32[10]{0:T(128)} %stack.43.place_ref, bf16[704,1280]{1,0:T(8,128)(2,1)} %refs_2_.3, bf16[1280,1280]{1,0:T(8,128)(2,1)} %refs_4_.9, bf16[1280,1280]{1,0:T(8,128)(2,1)} %refs_5_.7), custom_call_target="tpu_custom_call" | custom-call | flops 1 | bytes 1 | tf_op jit(solution)/shard_map/forward/pallas_call | solution.py:81
  13.6 2.7 %product.1 = f32[352,1280]{1,0:T(8,128)S(1)} custom-call(s32[10]{0:T(128)S(1)} %copy-done.5, bf16[352,1280]{1,0:T(8,128)(2,1)S(1)} %copy-done.4, bf16[1280,1280]{1,0:T(8,128)(2,1)S(1)} %copy-done), custom_call_target="tpu_custom_call" | custom-call | flops 1 | bytes 1 | tf_op jit(solution)/shard_map/product/pallas_call | solution.py:81
  16.6 2.6 %collective-permute-start.3 = (f16[352,1280]{1,0:T(8,128)(2,1)S(1)}, f16[352,1280]{1,0:T(8,128)(2,1)S(1)}, u32[]{:S(2)}, u32[]{:S(2)}) collective-permute-start(f16[352,1280]{1,0:T(8,128)(2,1)S(1)} %get-tuple-element.70), channel_id=1, source_target_pairs={{0,2},{1,3},{2,0},{3,1},{4,6},{5,7},{6,4},{7,5},{8,10},{9,11},{10,... | collective-permute-start | bytes 2703368 | tf_op jit(solution)/shard_map/ppermute | solution.py:27
  19.1 2.6 %collective-permute-start = (bf16[176,1280]{1,0:T(8,128)(2,1)S(1)}, bf16[176,1280]{1,0:T(8,128)(2,1)S(1)}, u32[]{:S(2)}, u32[]{:S(2)}) collective-permute-start(bf16[176,1280]{1,0:T(8,128)(2,1)S(1)} %copy-done.6), channel_id=1, source_target_pairs={{0,16},{1,17},{2,18},{3,19},{4,20},{5,21},{6,22},{7,23},{8,24},{9,... | collective-permute-start | bytes 1351688 | tf_op jit(solution)/shard_map/ppermute | solution.py:27
  21.7 1.6 collective-permute-start.1
  23.3 16.5 %collective-permute-done.3 = f16[352,1280]{1,0:T(8,128)(2,1)S(1)} collective-permute-done((f16[352,1280]{1,0:T(8,128)(2,1)S(1)}, f16[352,1280]{1,0:T(8,128)(2,1)S(1)}, u32[]{:S(2)}, u32[]{:S(2)}) %collective-permute-start.3) | collective-permute-done | bytes 901152 | tf_op jit(solution)/shard_map/ppermute | solution.py:27
  39.9 2.3 %collective-permute-done.refs_0_ = bf16[176,1280]{1,0:T(8,128)(2,1)S(1)} collective-permute-done((bf16[176,1280]{1,0:T(8,128)(2,1)S(1)}, bf16[176,1280]{1,0:T(8,128)(2,1)S(1)}, u32[]{:S(2)}, u32[]{:S(2)}) %collective-permute-start) | collective-permute-done | bytes 450592 | tf_op jit(solution)/shard_map/ppermute | solution.py:27
  43.7 1.6 collective-permute-start.5
  47.7 2.3 %collective-permute-start.10 = (bf16[176,1280]{1,0:T(8,128)(2,1)S(1)}, bf16[176,1280]{1,0:T(8,128)(2,1)S(1)}, u32[]{:S(2)}, u32[]{:S(2)}) collective-permute-start(bf16[176,1280]{1,0:T(8,128)(2,1)S(1)} %get-tuple-element.47), channel_id=1, source_target_pairs={{0,16},{1,17},{2,18},{3,19},{4,20},{5,21},{6,22},{7,23},{8,24},{9,... | collective-permute-start | bytes 1351688 | tf_op jit(solution)/shard_map/ppermute | solution.py:27
  51.1 9.7 %gradient.5 = (f32[160,1280]{1,0:T(8,128)S(1)}, f32[160,1280]{1,0:T(8,128)S(1)}, bf16[320,1280]{1,0:T(8,128)(2,1)S(1)}) custom-call(s32[10]{0:T(128)S(1)} %copy-done.5, bf16[352,1280]{1,0:T(8,128)(2,1)S(1)} %get-tuple-element.39.refs_0_, bf16[352,1280]{1,0:T(8,128)(2,1)S(1)} %collective-permute-done.4.refs_1_, bf16[704,1280]{1,0:T(8,128)(2,1)S(1)} %copy-done.2, ...), custom_call_target="tpu_custom_call" | custom-call | flops 1 | bytes 1 | tf_op jit(solution)/shard_map/gradient/pallas_call | solution.py:81
  61.3 14.6 %collective-permute-done.10.refs_0_ = bf16[176,1280]{1,0:T(8,128)(2,1)S(1)} collective-permute-done((bf16[176,1280]{1,0:T(8,128)(2,1)S(1)}, bf16[176,1280]{1,0:T(8,128)(2,1)S(1)}, u32[]{:S(2)}, u32[]{:S(2)}) %collective-permute-start.10) | collective-permute-done | bytes 450592 | tf_op jit(solution)/shard_map/ppermute | solution.py:27
  77.0 3.0 %collective-permute-done.6.refs_2_.refs_3_.refs_1_.refs_4_ = bf16[320,1280]{1,0:T(8,128)(2,1)S(1)} collective-permute-done((bf16[320,1280]{1,0:T(8,128)(2,1)S(1)}, bf16[320,1280]{1,0:T(8,128)(2,1)S(1)}, u32[]{:S(2)}, u32[]{:S(2)}) %collective-permute-start.6) | collective-permute-done | bytes 819232 | tf_op jit(solution)/shard_map/ppermute | solution.py:27
  82.5 9.9 %gradient.6 = (f32[160,1280]{1,0:T(8,128)S(1)}, f32[160,1280]{1,0:T(8,128)S(1)}, bf16[320,1280]{1,0:T(8,128)(2,1)S(1)}) custom-call(s32[10]{0:T(128)S(1)} %copy-done.5, bf16[352,1280]{1,0:T(8,128)(2,1)S(1)} %collective-permute-done.7.refs_0_, bf16[352,1280]{1,0:T(8,128)(2,1)S(1)} %collective-permute-done.8.refs_1_, bf16[352,1280]{1,0:T(8,128)(2,1)S(1)} %join.7.refs_2_, ...), custom_call_target="tpu_custom_call" | custom-call | flops 1 | bytes 1 | tf_op jit(solution)/shard_map/gradient/pallas_call | solution.py:81
  93.1 1.8 %collective-permute-start.21 = (bf16[352,1280]{1,0:T(8,128)(2,1)S(1)}, bf16[352,1280]{1,0:T(8,128)(2,1)S(1)}, u32[]{:S(2)}, u32[]{:S(2)}) collective-permute-start(bf16[352,1280]{1,0:T(8,128)(2,1)S(1)} %join.6.refs_2_), channel_id=1, source_target_pairs={{0,8},{1,9},{2,10},{3,11},{4,12},{5,13},{6,14},{7,15},{8,0},{9,1},... | collective-permute-start | bytes 2703368 | tf_op jit(solution)/shard_map/ppermute | solution.py:27
  94.9 1.5 collective-permute-start.18
  98.5 8.8 %gradient.7 = (f32[160,1280]{1,0:T(8,128)S(1)}, f32[160,1280]{1,0:T(8,128)S(1)}) custom-call(s32[10]{0:T(128)S(1)} %copy-done.5, bf16[352,1280]{1,0:T(8,128)(2,1)S(1)} %join.8.refs_0_, bf16[352,1280]{1,0:T(8,128)(2,1)S(1)} %collective-permute-done.16.refs_1_, bf16[352,1280]{1,0:T(8,128)(2,1)S(1)} %join.6.refs_2_, ...), custom_call_target="tpu_custom_call" | custom-call | flops 1 | bytes 1 | tf_op jit(solution)/shard_map/gradient/pallas_call | solution.py:81
  107.3 2.3 %collective-permute-done.22.refs_1_ = bf16[176,1280]{1,0:T(8,128)(2,1)S(1)} collective-permute-done((bf16[176,1280]{1,0:T(8,128)(2,1)S(1)}, bf16[176,1280]{1,0:T(8,128)(2,1)S(1)}, u32[]{:S(2)}, u32[]{:S(2)}) %collective-permute-start.22) | collective-permute-done | bytes 450592 | tf_op jit(solution)/shard_map/ppermute | solution.py:27
  109.8 5.8 %collective-permute-done.21.refs_3_ = bf16[352,1280]{1,0:T(8,128)(2,1)S(1)} collective-permute-done((bf16[352,1280]{1,0:T(8,128)(2,1)S(1)}, bf16[352,1280]{1,0:T(8,128)(2,1)S(1)}, u32[]{:S(2)}, u32[]{:S(2)}) %collective-permute-start.21) | collective-permute-done | bytes 901152 | tf_op jit(solution)/shard_map/ppermute | solution.py:27
  115.6 2.7 %collective-permute-done.19.refs_1_ = bf16[176,1280]{1,0:T(8,128)(2,1)S(1)} collective-permute-done((bf16[176,1280]{1,0:T(8,128)(2,1)S(1)}, bf16[176,1280]{1,0:T(8,128)(2,1)S(1)}, u32[]{:S(2)}, u32[]{:S(2)}) %collective-permute-start.19) | collective-permute-done | bytes 450592 | tf_op jit(solution)/shard_map/ppermute | solution.py:27
  119.4 2.7 %products.4.refs_0_.refs_14_ = f32[8,128]{1,0:T(8,128)S(1)} custom-call(s32[10]{0:T(128)S(1)} %copy-done.5, f32[160,1280]{1,0:T(8,128)S(1)} %get-tuple-element.44.refs_0_.refs_1_, f32[160,1280]{1,0:T(8,128)S(1)} %get-tuple-element.40.refs_1_.refs_0_.refs_2_, bf16[320,1280]{1,0:T(8,128)(2,1)S(1)} %collective-permute-done.6.refs_2_.refs_3_.refs_1_.refs_4_, ...), custom_call_target="tpu_custom_call" | custom-call | flops 1 | bytes 1 | tf_op jit(solution)/shard_map/products/pallas_call | solution.py:81
  122.2 9.9 %gradient.8 = (f32[160,1280]{1,0:T(8,128)S(1)}, f32[160,1280]{1,0:T(8,128)S(1)}, bf16[160,1280]{1,0:T(8,128)(2,1)S(1)}, bf16[160,1280]{1,0:T(8,128)(2,1)S(1)}) custom-call(s32[10]{0:T(128)S(1)} %copy-done.5, f32[8,128]{1,0:T(8,128)S(1)} %products.4.refs_0_.refs_14_, bf16[352,1280]{1,0:T(8,128)(2,1)S(1)} %join.9.refs_1_, ...), custom_call_target="tpu_custom_call" | custom-call | flops 1 | bytes 1 | tf_op jit(solution)/shard_map/gradient/pallas_call | solution.py:81
  133.3 1.5 collective-permute-start.27
  136.0 8.9 %gradient.9 = (f32[160,1280]{1,0:T(8,128)S(1)}, f32[160,1280]{1,0:T(8,128)S(1)}) custom-call(s32[10]{0:T(128)S(1)} %copy-done.5, bf16[352,1280]{1,0:T(8,128)(2,1)S(1)} %join.10.refs_0_, bf16[352,1280]{1,0:T(8,128)(2,1)S(1)} %collective-permute-done.24.refs_1_, bf16[352,1280]{1,0:T(8,128)(2,1)S(1)} %join.11.refs_2_, ...), custom_call_target="tpu_custom_call" | custom-call | flops 1 | bytes 1 | tf_op jit(solution)/shard_map/gradient/pallas_call | solution.py:81
  144.9 4.7 %products.5.refs_8_ = f32[8,128]{1,0:T(8,128)S(1)} custom-call(s32[10]{0:T(128)S(1)} %copy-done.5, f32[160,1280]{1,0:T(8,128)S(1)} %get-tuple-element.44.refs_0_.refs_1_, f32[160,1280]{1,0:T(8,128)S(1)} %get-tuple-element.40.refs_1_.refs_0_.refs_2_, bf16[320,1280]{1,0:T(8,128)(2,1)S(1)} %collective-permute-done.6.refs_2_.refs_3_.refs_1_.refs_4_, ...), custom_call_target="tpu_custom_call" | custom-call | flops 1 | bytes 1 | tf_op jit(solution)/shard_map/products/pallas_call | solution.py:81
  149.6 1.7 products.6.refs_8_
  151.3 1.8 %collective-permute-done.27.refs_7_.refs_16_ = bf16[160,1280]{1,0:T(8,128)(2,1)S(1)} collective-permute-done((bf16[160,1280]{1,0:T(8,128)(2,1)S(1)}, bf16[160,1280]{1,0:T(8,128)(2,1)S(1)}, u32[]{:S(2)}, u32[]{:S(2)}) %collective-permute-start.27) | collective-permute-done | bytes 409632 | tf_op jit(solution)/shard_map/ppermute | solution.py:27
  153.1 1.7 products.7.refs_0_
  156.8 1.8 %collective-permute-done.30.refs_2_ = f32[8,128]{1,0:T(8,128)S(1)} collective-permute-done((f32[8,128]{1,0:T(8,128)S(1)}, f32[8,128]{1,0:T(8,128)S(1)}, u32[]{:S(2)}, u32[]{:S(2)}) %collective-permute-start.30) | collective-permute-done | bytes 4128 | tf_op jit(solution)/shard_map/ppermute | solution.py:27
  160.9 3.2 %collective-permute-start.34 = (f32[8,128]{1,0:T(8,128)S(1)}, f32[8,128]{1,0:T(8,128)S(1)}, u32[]{:S(2)}, u32[]{:S(2)}) collective-permute-start(f32[8,128]{1,0:T(8,128)S(1)} %sum_of.3.refs_0_), channel_id=1, source_target_pairs={{0,24},{1,25},{2,26},{3,27},{4,28},{5,29},{6,30},{7,31},{8,16},{9,... | collective-permute-start | bytes 12296 | tf_op jit(solution)/shard_map/ppermute | solution.py:27
  164.5 1.8 %collective-permute-done.34.refs_3_ = f32[8,128]{1,0:T(8,128)S(1)} collective-permute-done((f32[8,128]{1,0:T(8,128)S(1)}, f32[8,128]{1,0:T(8,128)S(1)}, u32[]{:S(2)}, u32[]{:S(2)}) %collective-permute-start.34) | collective-permute-done | bytes 4128 | tf_op jit(solution)/shard_map/ppermute | solution.py:27
  167.8 2.7 %collective-permute-done.35.refs_1_ = f32[8,128]{1,0:T(8,128)S(1)} collective-permute-done((f32[8,128]{1,0:T(8,128)S(1)}, f32[8,128]{1,0:T(8,128)S(1)}, u32[]{:S(2)}, u32[]{:S(2)}) %collective-permute-start.35) | collective-permute-done | bytes 4128 | tf_op jit(solution)/shard_map/ppermute | solution.py:27
  171.1 4.2 %merge.1 = (f32[160,1280]{1,0:T(8,128)}, f32[160,1280]{1,0:T(8,128)}) custom-call(s32[10]{0:T(128)S(1)} %copy-done.5, f32[8,128]{1,0:T(8,128)S(1)} %sum_of.5.refs_0_, f32[160,1280]{1,0:T(8,128)S(1)} %get-tuple-element.44.refs_0_.refs_1_, f32[160,1280]{1,0:T(8,128)S(1)} %get-tuple-element.40.refs_1_.refs_0_.refs_2_, ...), custom_call_target="tpu_custom_call" | custom-call | flops 1 | bytes 1 | tf_op jit(solution)/shard_map/merge/pallas_call | solution.py:81
  (80 shorter events, 24.6 us)
Async XLA Ops:
  11.9 4.4 %collective-permute-start.2 = (f32[352,1280]{1,0:T(8,128)}, f32[352,1280]{1,0:T(8,128)S(1)}, u32[]{:S(2)}, u32[]{:S(2)}) collective-permute-start(f32[352,1280]{1,0:T(8,128)} %get-tuple-element.38), channel_id=1, source_target_pairs={{0,1},{1,0},{2,3},{3,2},{4,5},{5,4},{6,7},{7,6},{8,9},{9,8},{10,11... | collective-permute-start | bytes 5406728 | tf_op jit(solution)/shard_map/ppermute | solution.py:27
  16.6 23.2 %collective-permute-start.3 = (f16[352,1280]{1,0:T(8,128)(2,1)S(1)}, f16[352,1280]{1,0:T(8,128)(2,1)S(1)}, u32[]{:S(2)}, u32[]{:S(2)}) collective-permute-start(f16[352,1280]{1,0:T(8,128)(2,1)S(1)} %get-tuple-element.70), channel_id=1, source_target_pairs={{0,2},{1,3},{2,0},{3,1},{4,6},{5,7},{6,4},{7,5},{8,10},{9,11},{10,... | collective-permute-start | bytes 2703368 | tf_op jit(solution)/shard_map/ppermute | solution.py:27
  19.1 23.1 %collective-permute-start = (bf16[176,1280]{1,0:T(8,128)(2,1)S(1)}, bf16[176,1280]{1,0:T(8,128)(2,1)S(1)}, u32[]{:S(2)}, u32[]{:S(2)}) collective-permute-start(bf16[176,1280]{1,0:T(8,128)(2,1)S(1)} %copy-done.6), channel_id=1, source_target_pairs={{0,16},{1,17},{2,18},{3,19},{4,20},{5,21},{6,22},{7,23},{8,24},{9,... | collective-permute-start | bytes 1351688 | tf_op jit(solution)/shard_map/ppermute | solution.py:27
  21.7 20.7 %collective-permute-start.1 = (bf16[176,1280]{1,0:T(8,128)(2,1)S(1)}, bf16[176,1280]{1,0:T(8,128)(2,1)S(1)}, u32[]{:S(2)}, u32[]{:S(2)}) collective-permute-start(bf16[176,1280]{1,0:T(8,128)(2,1)S(1)} %copy-done.6), channel_id=1, source_target_pairs={{0,8},{1,9},{2,10},{3,11},{4,12},{5,13},{6,14},{7,15},{8,0},{9,1},... | collective-permute-start | bytes 1351688 | tf_op jit(solution)/shard_map/ppermute | solution.py:27
  43.6 6.4 %collective-permute-start.4 = (bf16[352,1280]{1,0:T(8,128)(2,1)S(1)}, bf16[352,1280]{1,0:T(8,128)(2,1)S(1)}, u32[]{:S(2)}, u32[]{:S(2)}) collective-permute-start(bf16[352,1280]{1,0:T(8,128)(2,1)S(1)} %get-tuple-element.39.refs_0_), channel_id=1, source_target_pairs={{0,1},{1,0},{2,3},{3,2},{4,5},{5,4},{6,7},{7,6},{8,9},{9,8},{10,11... | collective-permute-start | bytes 2703368 | tf_op jit(solution)/shard_map/ppermute | solution.py:27
  43.7 17.1 %collective-permute-start.5 = (bf16[176,1280]{1,0:T(8,128)(2,1)S(1)}, bf16[176,1280]{1,0:T(8,128)(2,1)S(1)}, u32[]{:S(2)}, u32[]{:S(2)}) collective-permute-start(bf16[176,1280]{1,0:T(8,128)(2,1)S(1)} %collective-permute-done.refs_0_), channel_id=1, source_target_pairs={{0,4},{1,5},{2,6},{3,7},{4,0},{5,1},{6,2},{7,3},{8,12},{9,13},{10,... | collective-permute-start | bytes 1351688 | tf_op jit(solution)/shard_map/ppermute | solution.py:27
  45.3 31.7 %collective-permute-start.7 = (bf16[352,1280]{1,0:T(8,128)(2,1)S(1)}, bf16[352,1280]{1,0:T(8,128)(2,1)S(1)}, u32[]{:S(2)}, u32[]{:S(2)}) collective-permute-start(bf16[352,1280]{1,0:T(8,128)(2,1)S(1)} %get-tuple-element.39.refs_0_), channel_id=1, source_target_pairs={{0,8},{1,9},{2,10},{3,11},{4,12},{5,13},{6,14},{7,15},{8,0},{9,1},... | collective-permute-start | bytes 2703368 | tf_op jit(solution)/shard_map/ppermute | solution.py:27
  46.7 14.6 %collective-permute-start.11 = (bf16[176,1280]{1,0:T(8,128)(2,1)S(1)}, bf16[176,1280]{1,0:T(8,128)(2,1)S(1)}, u32[]{:S(2)}, u32[]{:S(2)}) collective-permute-start(bf16[176,1280]{1,0:T(8,128)(2,1)S(1)} %collective-permute-done.refs_0_), channel_id=1, source_target_pairs={{0,2},{1,3},{2,0},{3,1},{4,6},{5,7},{6,4},{7,5},{8,10},{9,11},{10,... | collective-permute-start | bytes 1351688 | tf_op jit(solution)/shard_map/ppermute | solution.py:27
  47.7 28.3 %collective-permute-start.10 = (bf16[176,1280]{1,0:T(8,128)(2,1)S(1)}, bf16[176,1280]{1,0:T(8,128)(2,1)S(1)}, u32[]{:S(2)}, u32[]{:S(2)}) collective-permute-start(bf16[176,1280]{1,0:T(8,128)(2,1)S(1)} %get-tuple-element.47), channel_id=1, source_target_pairs={{0,16},{1,17},{2,18},{3,19},{4,20},{5,21},{6,22},{7,23},{8,24},{9,... | collective-permute-start | bytes 1351688 | tf_op jit(solution)/shard_map/ppermute | solution.py:27
  50.0 26.0 %collective-permute-start.9 = (bf16[176,1280]{1,0:T(8,128)(2,1)S(1)}, bf16[176,1280]{1,0:T(8,128)(2,1)S(1)}, u32[]{:S(2)}, u32[]{:S(2)}) collective-permute-start(bf16[176,1280]{1,0:T(8,128)(2,1)S(1)} %collective-permute-done.1.refs_1_.refs_0_), channel_id=1, source_target_pairs={{0,2},{1,3},{2,0},{3,1},{4,6},{5,7},{6,4},{7,5},{8,10},{9,11},{10,... | collective-permute-start | bytes 1351688 | tf_op jit(solution)/shard_map/ppermute | solution.py:27
  60.7 19.3 %collective-permute-start.6 = (bf16[320,1280]{1,0:T(8,128)(2,1)S(1)}, bf16[320,1280]{1,0:T(8,128)(2,1)S(1)}, u32[]{:S(2)}, u32[]{:S(2)}) collective-permute-start(bf16[320,1280]{1,0:T(8,128)(2,1)S(1)} %get-tuple-element.43), channel_id=1, source_target_pairs={{0,4},{1,5},{2,6},{3,7},{4,0},{5,1},{6,2},{7,3},{8,12},{9,13},{10,... | collective-permute-start | bytes 2457608 | tf_op jit(solution)/shard_map/ppermute | solution.py:27
  76.1 5.6 %collective-permute-start.12 = (bf16[352,1280]{1,0:T(8,128)(2,1)S(1)}, bf16[352,1280]{1,0:T(8,128)(2,1)S(1)}, u32[]{:S(2)}, u32[]{:S(2)}) collective-permute-start(bf16[352,1280]{1,0:T(8,128)(2,1)S(1)} %join.7.refs_2_), channel_id=1, source_target_pairs={{0,1},{1,0},{2,3},{3,2},{4,5},{5,4},{6,7},{7,6},{8,9},{9,8},{10,11... | collective-permute-start | bytes 2703368 | tf_op jit(solution)/shard_map/ppermute | solution.py:27
  80.0 12.8 %collective-permute-start.14 = (bf16[176,1280]{1,0:T(8,128)(2,1)S(1)}, bf16[176,1280]{1,0:T(8,128)(2,1)S(1)}, u32[]{:S(2)}, u32[]{:S(2)}) collective-permute-start(bf16[176,1280]{1,0:T(8,128)(2,1)S(1)} %collective-permute-done.10.refs_0_), channel_id=1, source_target_pairs={{0,8},{1,9},{2,10},{3,11},{4,12},{5,13},{6,14},{7,15},{8,0},{9,1},... | collective-permute-start | bytes 1351688 | tf_op jit(solution)/shard_map/ppermute | solution.py:27
  80.3 12.5 %collective-permute-start.15 = (bf16[176,1280]{1,0:T(8,128)(2,1)S(1)}, bf16[176,1280]{1,0:T(8,128)(2,1)S(1)}, u32[]{:S(2)}, u32[]{:S(2)}) collective-permute-start(bf16[176,1280]{1,0:T(8,128)(2,1)S(1)} %collective-permute-done.10.refs_0_), channel_id=1, source_target_pairs={{0,4},{1,5},{2,6},{3,7},{4,0},{5,1},{6,2},{7,3},{8,12},{9,13},{10,... | collective-permute-start | bytes 1351688 | tf_op jit(solution)/shard_map/ppermute | solution.py:27
  80.8 12.2 %collective-permute-start.13 = (bf16[176,1280]{1,0:T(8,128)(2,1)S(1)}, bf16[176,1280]{1,0:T(8,128)(2,1)S(1)}, u32[]{:S(2)}, u32[]{:S(2)}) collective-permute-start(bf16[176,1280]{1,0:T(8,128)(2,1)S(1)} %collective-permute-done.10.refs_0_), channel_id=1, source_target_pairs={{0,2},{1,3},{2,0},{3,1},{4,6},{5,7},{6,4},{7,5},{8,10},{9,11},{10,... | collective-permute-start | bytes 1351688 | tf_op jit(solution)/shard_map/ppermute | solution.py:27
  81.7 15.7 %collective-permute-start.17 = (bf16[352,1280]{1,0:T(8,128)(2,1)S(1)}, bf16[352,1280]{1,0:T(8,128)(2,1)S(1)}, u32[]{:S(2)}, u32[]{:S(2)}) collective-permute-start(bf16[352,1280]{1,0:T(8,128)(2,1)S(1)} %join.6.refs_2_), channel_id=1, source_target_pairs={{0,1},{1,0},{2,3},{3,2},{4,5},{5,4},{6,7},{7,6},{8,9},{9,8},{10,11... | collective-permute-start | bytes 2703368 | tf_op jit(solution)/shard_map/ppermute | solution.py:27
  93.1 5.4 %collective-permute-start.16 = (bf16[352,1280]{1,0:T(8,128)(2,1)S(1)}, bf16[352,1280]{1,0:T(8,128)(2,1)S(1)}, u32[]{:S(2)}, u32[]{:S(2)}) collective-permute-start(bf16[352,1280]{1,0:T(8,128)(2,1)S(1)} %join.8.refs_0_), channel_id=1, source_target_pairs={{0,1},{1,0},{2,3},{3,2},{4,5},{5,4},{6,7},{7,6},{8,9},{9,8},{10,11... | collective-permute-start | bytes 2703368 | tf_op jit(solution)/shard_map/ppermute | solution.py:27
  93.1 22.4 %collective-permute-start.21 = (bf16[352,1280]{1,0:T(8,128)(2,1)S(1)}, bf16[352,1280]{1,0:T(8,128)(2,1)S(1)}, u32[]{:S(2)}, u32[]{:S(2)}) collective-permute-start(bf16[352,1280]{1,0:T(8,128)(2,1)S(1)} %join.6.refs_2_), channel_id=1, source_target_pairs={{0,8},{1,9},{2,10},{3,11},{4,12},{5,13},{6,14},{7,15},{8,0},{9,1},... | collective-permute-start | bytes 2703368 | tf_op jit(solution)/shard_map/ppermute | solution.py:27
  94.9 20.6 %collective-permute-start.18 = (bf16[320,1280]{1,0:T(8,128)(2,1)S(1)}, bf16[320,1280]{1,0:T(8,128)(2,1)S(1)}, u32[]{:S(2)}, u32[]{:S(2)}) collective-permute-start(bf16[320,1280]{1,0:T(8,128)(2,1)S(1)} %get-tuple-element.56), channel_id=1, source_target_pairs={{0,4},{1,5},{2,6},{3,7},{4,0},{5,1},{6,2},{7,3},{8,12},{9,13},{10,... | collective-permute-start | bytes 2457608 | tf_op jit(solution)/shard_map/ppermute | solution.py:27
  96.5 13.2 %collective-permute-start.22 = (bf16[176,1280]{1,0:T(8,128)(2,1)S(1)}, bf16[176,1280]{1,0:T(8,128)(2,1)S(1)}, u32[]{:S(2)}, u32[]{:S(2)}) collective-permute-start(bf16[176,1280]{1,0:T(8,128)(2,1)S(1)} %collective-permute-done.15.refs_0_), channel_id=1, source_target_pairs={{0,2},{1,3},{2,0},{3,1},{4,6},{5,7},{6,4},{7,5},{8,10},{9,11},{10,... | collective-permute-start | bytes 1351688 | tf_op jit(solution)/shard_map/ppermute | solution.py:27
  97.4 20.8 %collective-permute-start.19 = (bf16[176,1280]{1,0:T(8,128)(2,1)S(1)}, bf16[176,1280]{1,0:T(8,128)(2,1)S(1)}, u32[]{:S(2)}, u32[]{:S(2)}) collective-permute-start(bf16[176,1280]{1,0:T(8,128)(2,1)S(1)} %collective-permute-done.14.refs_0_), channel_id=1, source_target_pairs={{0,2},{1,3},{2,0},{3,1},{4,6},{5,7},{6,4},{7,5},{8,10},{9,11},{10,... | collective-permute-start | bytes 1351688 | tf_op jit(solution)/shard_map/ppermute | solution.py:27
  115.6 6.6 %collective-permute-start.23 = (bf16[352,1280]{1,0:T(8,128)(2,1)S(1)}, bf16[352,1280]{1,0:T(8,128)(2,1)S(1)}, u32[]{:S(2)}, u32[]{:S(2)}) collective-permute-start(bf16[352,1280]{1,0:T(8,128)(2,1)S(1)} %collective-permute-done.21.refs_3_), channel_id=1, source_target_pairs={{0,1},{1,0},{2,3},{3,2},{4,5},{5,4},{6,7},{7,6},{8,9},{9,8},{10,11... | collective-permute-start | bytes 2703368 | tf_op jit(solution)/shard_map/ppermute | solution.py:27
  118.3 3.9 %collective-permute-start.20 = (bf16[352,1280]{1,0:T(8,128)(2,1)S(1)}, bf16[352,1280]{1,0:T(8,128)(2,1)S(1)}, u32[]{:S(2)}, u32[]{:S(2)}) collective-permute-start(bf16[352,1280]{1,0:T(8,128)(2,1)S(1)} %join.9.refs_1_), channel_id=1, source_target_pairs={{0,1},{1,0},{2,3},{3,2},{4,5},{5,4},{6,7},{7,6},{8,9},{9,8},{10,11... | collective-permute-start | bytes 2703368 | tf_op jit(solution)/shard_map/ppermute | solution.py:27
  118.4 13.7 %collective-permute-start.25 = (bf16[176,1280]{1,0:T(8,128)(2,1)S(1)}, bf16[176,1280]{1,0:T(8,128)(2,1)S(1)}, u32[]{:S(2)}, u32[]{:S(2)}) collective-permute-start(bf16[176,1280]{1,0:T(8,128)(2,1)S(1)} %collective-permute-done.5.refs_0_), channel_id=1, source_target_pairs={{0,2},{1,3},{2,0},{3,1},{4,6},{5,7},{6,4},{7,5},{8,10},{9,11},{10,... | collective-permute-start | bytes 1351688 | tf_op jit(solution)/shard_map/ppermute | solution.py:27
  132.4 3.6 %collective-permute-start.24 = (bf16[352,1280]{1,0:T(8,128)(2,1)S(1)}, bf16[352,1280]{1,0:T(8,128)(2,1)S(1)}, u32[]{:S(2)}, u32[]{:S(2)}) collective-permute-start(bf16[352,1280]{1,0:T(8,128)(2,1)S(1)} %join.10.refs_0_), channel_id=1, source_target_pairs={{0,1},{1,0},{2,3},{3,2},{4,5},{5,4},{6,7},{7,6},{8,9},{9,8},{10,11... | collective-permute-start | bytes 2703368 | tf_op jit(solution)/shard_map/ppermute | solution.py:27
  132.8 16.8 %collective-permute-start.28 = (bf16[160,1280]{1,0:T(8,128)(2,1)S(1)}, bf16[160,1280]{1,0:T(8,128)(2,1)S(1)}, u32[]{:S(2)}, u32[]{:S(2)}) collective-permute-start(bf16[160,1280]{1,0:T(8,128)(2,1)S(1)} %get-tuple-element.69), channel_id=1, source_target_pairs={{0,4},{1,5},{2,6},{3,7},{4,0},{5,1},{6,2},{7,3},{8,12},{9,13},{10,... | collective-permute-start | bytes 1228808 | tf_op jit(solution)/shard_map/ppermute | solution.py:27
  133.3 19.8 %collective-permute-start.27 = (bf16[160,1280]{1,0:T(8,128)(2,1)S(1)}, bf16[160,1280]{1,0:T(8,128)(2,1)S(1)}, u32[]{:S(2)}, u32[]{:S(2)}) collective-permute-start(bf16[160,1280]{1,0:T(8,128)(2,1)S(1)} %get-tuple-element.67), channel_id=1, source_target_pairs={{0,4},{1,5},{2,6},{3,7},{4,0},{5,1},{6,2},{7,3},{8,12},{9,13},{10,... | collective-permute-start | bytes 1228808 | tf_op jit(solution)/shard_map/ppermute | solution.py:27
  154.9 3.7 %collective-permute-start.30 = (f32[8,128]{1,0:T(8,128)S(1)}, f32[8,128]{1,0:T(8,128)S(1)}, u32[]{:S(2)}, u32[]{:S(2)}) collective-permute-start(f32[8,128]{1,0:T(8,128)S(1)} %products.7.refs_0_), channel_id=1, source_target_pairs={{0,2},{1,3},{2,0},{3,1},{4,6},{5,7},{6,4},{7,5},{8,10},{9,11},{10,... | collective-permute-start | bytes 12296 | tf_op jit(solution)/shard_map/ppermute | solution.py:27
  159.6 4.5 %collective-permute-start.32 = (f32[8,128]{1,0:T(8,128)S(1)}, f32[8,128]{1,0:T(8,128)S(1)}, u32[]{:S(2)}, u32[]{:S(2)}) collective-permute-start(f32[8,128]{1,0:T(8,128)S(1)} %sum_of.3.refs_0_), channel_id=1, source_target_pairs={{0,8},{1,9},{2,10},{3,11},{4,12},{5,13},{6,14},{7,15},{8,0},{9,1},... | collective-permute-start | bytes 12296 | tf_op jit(solution)/shard_map/ppermute | solution.py:27
  160.0 4.5 %collective-permute-start.33 = (f32[8,128]{1,0:T(8,128)S(1)}, f32[8,128]{1,0:T(8,128)S(1)}, u32[]{:S(2)}, u32[]{:S(2)}) collective-permute-start(f32[8,128]{1,0:T(8,128)S(1)} %sum_of.3.refs_0_), channel_id=1, source_target_pairs={{0,16},{1,17},{2,18},{3,19},{4,20},{5,21},{6,22},{7,23},{8,24},{9,... | collective-permute-start | bytes 12296 | tf_op jit(solution)/shard_map/ppermute | solution.py:27
  160.9 5.4 %collective-permute-start.34 = (f32[8,128]{1,0:T(8,128)S(1)}, f32[8,128]{1,0:T(8,128)S(1)}, u32[]{:S(2)}, u32[]{:S(2)}) collective-permute-start(f32[8,128]{1,0:T(8,128)S(1)} %sum_of.3.refs_0_), channel_id=1, source_target_pairs={{0,24},{1,25},{2,26},{3,27},{4,28},{5,29},{6,30},{7,31},{8,16},{9,... | collective-permute-start | bytes 12296 | tf_op jit(solution)/shard_map/ppermute | solution.py:27
  166.8 3.7 %collective-permute-start.35 = (f32[8,128]{1,0:T(8,128)S(1)}, f32[8,128]{1,0:T(8,128)S(1)}, u32[]{:S(2)}, u32[]{:S(2)}) collective-permute-start(f32[8,128]{1,0:T(8,128)S(1)} %sum_of.4.refs_0_), channel_id=1, source_target_pairs={{0,4},{1,5},{2,6},{3,7},{4,0},{5,1},{6,2},{7,3},{8,12},{9,13},{10,... | collective-permute-start | bytes 12296 | tf_op jit(solution)/shard_map/ppermute | solution.py:27
  (11 other events, 79.5 us)

commit v16 on v15

--- a/solution.py
+++ b/solution.py
@@ -564,31 +564,32 @@
     gradient_of(low, half, both_halves(halves[low]))
     token = slots[low][0][0]
 
-    errors_of[high] = ordered(errors_of[high], own)
-    ready = ordered(errors_of[high], errors_of[low])
+    ready = errors_of[high] = ordered(errors_of[high], errors_of[low])
     errors_of[high | low] = from_mask(ready, low * others, 0)
     errors_of[high | swap] = from_mask(ready, swap * others, 0)
-    halves[high | low] = from_mask(ordered(halves[high], half), low * others, 0)
-    before = (errors_of[high | low], errors_of[high | swap])
-    half = to_half(errors_of[high], token, *before)
+    halves[high | low] = from_mask(ordered(halves[high], errors_of[low]), low * others, 0)
+    partner_half = to_half(ready)
+    halves[high | swap] = to_half(ordered(inputs_of[high | swap], errors_of[low]))
+    half = ordered(
+        errors_of[high | low], token, errors_of[high | swap], partner_half, halves[high | swap]
+    )
+    half = to_half(half, *got[low])
+    totals = jnp.zeros((8, 128), jnp.float32)
+    labels = [0, swap, low]
+    totals = products(place, [slots[m] for m in labels], labels, 3, totals)
+    gradient_of(
+        high | low, half, both_halves(ordered(halves[high | low], token)), totals
+    )
+    token = slots[high | low][0][0]
+
+    half = ordered(partner_half, token)
     gradient_of(high, half, both_halves(halves[high]))
     token = slots[high][0][0]
 
-    totals = jnp.zeros((8, 128), jnp.float32)
-    labels = [0, swap, low, high]
+    half = to_half(errors_of[high | swap], slots[high | low][0][0])
+    gradient_of(high | swap, half, both_halves(halves[high | swap]), token)
+    labels += [low | swap, high | low, high, high | swap]
     totals = products(place, [slots[m] for m in labels], labels, 4, totals)
-
-    half = to_half(errors_of[high | low], token)
-    partner_half = to_half(errors_of[high | swap], token)
-    ready = ordered(halves[high | low], token, *got[low], partner_half)
-    gradient_of(high | low, half, both_halves(ready), totals)
-    token = slots[high | low][0][0]
-
-    half = ordered(partner_half, token)
-    halves[high | swap] = to_half(inputs_of[high | swap], token)
-    gradient_of(high | swap, half, both_halves(halves[high | swap]))
-    labels += [low | swap, high | low, high | swap]
-    totals = products(place, [slots[m] for m in labels], labels, 3, totals)
     labels.append(high | low | swap)
     for k in range(2):
         totals = products(place, [slots[m][k : k + 1] for m in labels], labels, 1, totals)

time: 175 us -> 181 us (1.034)
  waiting for transfers between devices: 59.8 us -> 64.1 us
    ppermute x36, waiting for transfers between devices: 59.8 us -> 64.1 us  [from_mask(): return lax.ppermute(value, ('dp', 'tensor'), pairs)]
  transfers between devices with their start and end apart: 36 -> 36, of which waited for: 19 -> 15; matrix products, arithmetic and copies ran while one was open for 0% -> 0% of each run, Pallas kernels for 34% -> 33%
where the time goes in v16:
time: 181 us
  Pallas kernels  78.5 us (43%)
  waiting for transfers between devices  64.1 us (35%)
  starting transfers between devices  35.3 us (20%)
    pallas_call x22, Pallas kernels, call(): pl.pallas_call(body, grid_spec=pltpu.PrefetchScalarGridSpec(num_scalar_pr...  78.5 us
    ppermute x36, waiting for transfers between devices, from_mask(): return lax.ppermute(value, ('dp', 'tensor'), pairs)  64.1 us
    ppermute x36, starting transfers between devices, from_mask(): return lax.ppermute(value, ('dp', 'tensor'), pairs)  35.3 us
  transfers between devices with their start and end apart: 36, of which 15 were waited for; matrix products, arithmetic and copies ran while one was open for 0% of the time, Pallas kernels for 33%

profile of v16, /device:TPU:0, one launch (start us, length us, event | category | flops | bytes accessed | tf_op | source)
XLA Modules:
  0.0 181.2 jit_solution(5398696684722436753)
XLA Ops:
  1.3 10.7 %forward.1 = (f32[352,1280]{1,0:T(8,128)}, bf16[352,1280]{1,0:T(8,128)(2,1)}, bf16[176,1280]{1,0:T(8,128)(2,1)}) custom-call(s32[10]{0:T(128)} %stack.43.place_ref, bf16[704,1280]{1,0:T(8,128)(2,1)} %refs_2_.3, bf16[1280,1280]{1,0:T(8,128)(2,1)} %refs_5_.7, bf16[1280,1280]{1,0:T(8,128)(2,1)} %refs_6_.3), custom_call_target="tpu_custom_call" | custom-call | flops 1 | bytes 1 | tf_op jit(solution)/shard_map/forward/pallas_call | solution.py:81
  13.6 2.7 %product.1 = f32[352,1280]{1,0:T(8,128)S(1)} custom-call(s32[10]{0:T(128)S(1)} %copy-done.5, bf16[352,1280]{1,0:T(8,128)(2,1)S(1)} %copy-done.4, bf16[1280,1280]{1,0:T(8,128)(2,1)S(1)} %copy-done), custom_call_target="tpu_custom_call" | custom-call | flops 1 | bytes 1 | tf_op jit(solution)/shard_map/product/pallas_call | solution.py:81
  16.6 2.6 %collective-permute-start.3 = (f16[352,1280]{1,0:T(8,128)(2,1)S(1)}, f16[352,1280]{1,0:T(8,128)(2,1)S(1)}, u32[]{:S(2)}, u32[]{:S(2)}) collective-permute-start(f16[352,1280]{1,0:T(8,128)(2,1)S(1)} %get-tuple-element.68), channel_id=1, source_target_pairs={{0,2},{1,3},{2,0},{3,1},{4,6},{5,7},{6,4},{7,5},{8,10},{9,11},{10,... | collective-permute-start | bytes 2703368 | tf_op jit(solution)/shard_map/ppermute | solution.py:27
  19.1 2.6 %collective-permute-start = (bf16[176,1280]{1,0:T(8,128)(2,1)S(1)}, bf16[176,1280]{1,0:T(8,128)(2,1)S(1)}, u32[]{:S(2)}, u32[]{:S(2)}) collective-permute-start(bf16[176,1280]{1,0:T(8,128)(2,1)S(1)} %copy-done.6), channel_id=1, source_target_pairs={{0,16},{1,17},{2,18},{3,19},{4,20},{5,21},{6,22},{7,23},{8,24},{9,... | collective-permute-start | bytes 1351688 | tf_op jit(solution)/shard_map/ppermute | solution.py:27
  21.7 1.6 collective-permute-start.1
  23.3 16.5 %collective-permute-done.3 = f16[352,1280]{1,0:T(8,128)(2,1)S(1)} collective-permute-done((f16[352,1280]{1,0:T(8,128)(2,1)S(1)}, f16[352,1280]{1,0:T(8,128)(2,1)S(1)}, u32[]{:S(2)}, u32[]{:S(2)}) %collective-permute-start.3) | collective-permute-done | bytes 901152 | tf_op jit(solution)/shard_map/ppermute | solution.py:27
  39.9 2.3 %collective-permute-done.refs_0_ = bf16[176,1280]{1,0:T(8,128)(2,1)S(1)} collective-permute-done((bf16[176,1280]{1,0:T(8,128)(2,1)S(1)}, bf16[176,1280]{1,0:T(8,128)(2,1)S(1)}, u32[]{:S(2)}, u32[]{:S(2)}) %collective-permute-start) | collective-permute-done | bytes 450592 | tf_op jit(solution)/shard_map/ppermute | solution.py:27
  43.7 1.6 collective-permute-start.5
  45.3 1.4 collective-permute-start.7
  46.7 9.6 %gradient.5 = (f32[160,1280]{1,0:T(8,128)S(1)}, f32[160,1280]{1,0:T(8,128)S(1)}, bf16[320,1280]{1,0:T(8,128)(2,1)S(1)}) custom-call(s32[10]{0:T(128)S(1)} %copy-done.5, bf16[352,1280]{1,0:T(8,128)(2,1)S(1)} %get-tuple-element.38.refs_0_, bf16[352,1280]{1,0:T(8,128)(2,1)S(1)} %collective-permute-done.4.refs_1_, bf16[704,1280]{1,0:T(8,128)(2,1)S(1)} %copy-done.2, ...), custom_call_target="tpu_custom_call" | custom-call | flops 1 | bytes 1 | tf_op jit(solution)/shard_map/gradient/pallas_call | solution.py:81
  56.4 1.5 collective-permute-start.6
  58.9 1.3 collective-permute-start.10
  61.3 9.9 %collective-permute-done.11.refs_1_ = bf16[176,1280]{1,0:T(8,128)(2,1)S(1)} collective-permute-done((bf16[176,1280]{1,0:T(8,128)(2,1)S(1)}, bf16[176,1280]{1,0:T(8,128)(2,1)S(1)}, u32[]{:S(2)}, u32[]{:S(2)}) %collective-permute-start.11) | collective-permute-done | bytes 450592 | tf_op jit(solution)/shard_map/ppermute | solution.py:27
  71.2 9.6 %collective-permute-done.10.refs_0_ = bf16[176,1280]{1,0:T(8,128)(2,1)S(1)} collective-permute-done((bf16[176,1280]{1,0:T(8,128)(2,1)S(1)}, bf16[176,1280]{1,0:T(8,128)(2,1)S(1)}, u32[]{:S(2)}, u32[]{:S(2)}) %collective-permute-start.10) | collective-permute-done | bytes 450592 | tf_op jit(solution)/shard_map/ppermute | solution.py:27
  84.0 1.6 collective-permute-start.20
  86.4 9.9 %gradient.6 = (f32[160,1280]{1,0:T(8,128)S(1)}, f32[160,1280]{1,0:T(8,128)S(1)}, bf16[320,1280]{1,0:T(8,128)(2,1)S(1)}) custom-call(s32[10]{0:T(128)S(1)} %copy-done.5, bf16[352,1280]{1,0:T(8,128)(2,1)S(1)} %collective-permute-done.7.refs_0_, bf16[352,1280]{1,0:T(8,128)(2,1)S(1)} %collective-permute-done.8.refs_1_, bf16[352,1280]{1,0:T(8,128)(2,1)S(1)} %join.7.refs_2_, ...), custom_call_target="tpu_custom_call" | custom-call | flops 1 | bytes 1 | tf_op jit(solution)/shard_map/gradient/pallas_call | solution.py:81
  96.3 1.4 collective-permute-start.13
  97.7 5.9 %collective-permute-done.17.refs_1_ = bf16[176,1280]{1,0:T(8,128)(2,1)S(1)} collective-permute-done((bf16[176,1280]{1,0:T(8,128)(2,1)S(1)}, bf16[176,1280]{1,0:T(8,128)(2,1)S(1)}, u32[]{:S(2)}, u32[]{:S(2)}) %collective-permute-start.17) | collective-permute-done | bytes 450592 | tf_op jit(solution)/shard_map/ppermute | solution.py:27
  104.9 9.2 %collective-permute-done.20.refs_3_ = bf16[352,1280]{1,0:T(8,128)(2,1)S(1)} collective-permute-done((bf16[352,1280]{1,0:T(8,128)(2,1)S(1)}, bf16[352,1280]{1,0:T(8,128)(2,1)S(1)}, u32[]{:S(2)}, u32[]{:S(2)}) %collective-permute-start.20) | collective-permute-done | bytes 901152 | tf_op jit(solution)/shard_map/ppermute | solution.py:27
  117.3 2.0 %products.4.refs_0_.refs_14_ = f32[8,128]{1,0:T(8,128)S(1)} custom-call(s32[10]{0:T(128)S(1)} %copy-done.5, f32[160,1280]{1,0:T(8,128)S(1)} %get-tuple-element.43.refs_0_.refs_1_, f32[160,1280]{1,0:T(8,128)S(1)} %get-tuple-element.39.refs_1_.refs_0_.refs_2_, bf16[320,1280]{1,0:T(8,128)(2,1)S(1)} %collective-permute-done.6.refs_2_.refs_3_.refs_1_.refs_4_, ...), custom_call_target="tpu_custom_call" | custom-call | flops 1 | bytes 1 | tf_op jit(solution)/shard_map/products/pallas_call | solution.py:81
  119.4 9.7 %gradient.7 = (f32[160,1280]{1,0:T(8,128)S(1)}, f32[160,1280]{1,0:T(8,128)S(1)}, bf16[160,1280]{1,0:T(8,128)(2,1)S(1)}, bf16[160,1280]{1,0:T(8,128)(2,1)S(1)}) custom-call(s32[10]{0:T(128)S(1)} %copy-done.5, f32[8,128]{1,0:T(8,128)S(1)} %products.4.refs_0_.refs_14_, bf16[352,1280]{1,0:T(8,128)(2,1)S(1)} %join.10.refs_1_, ...), custom_call_target="tpu_custom_call" | custom-call | flops 1 | bytes 1 | tf_op jit(solution)/shard_map/gradient/pallas_call | solution.py:81
  131.8 9.1 %gradient.8 = (f32[160,1280]{1,0:T(8,128)S(1)}, f32[160,1280]{1,0:T(8,128)S(1)}) custom-call(s32[10]{0:T(128)S(1)} %copy-done.5, bf16[352,1280]{1,0:T(8,128)(2,1)S(1)} %join.8.refs_0_, bf16[352,1280]{1,0:T(8,128)(2,1)S(1)} %collective-permute-done.22.refs_1_, bf16[352,1280]{1,0:T(8,128)(2,1)S(1)} %join.6.refs_2_, ...), custom_call_target="tpu_custom_call" | custom-call | flops 1 | bytes 1 | tf_op jit(solution)/shard_map/gradient/pallas_call | solution.py:81
  140.9 8.9 %gradient.9 = (f32[160,1280]{1,0:T(8,128)S(1)}, f32[160,1280]{1,0:T(8,128)S(1)}) custom-call(s32[10]{0:T(128)S(1)} %copy-done.5, f32[160,1280]{1,0:T(8,128)S(1)} %get-tuple-element.62.refs_0_.refs_10_.refs_5_.refs_11_, bf16[352,1280]{1,0:T(8,128)(2,1)S(1)} %join.11.refs_1_, bf16[352,1280]{1,0:T(8,128)(2,1)S(1)} %collective-permute-done.25.refs_2_, ...), custom_call_target="tpu_custom_call" | custom-call | flops 1 | bytes 1 | tf_op jit(solution)/shard_map/gradient/pallas_call | solution.py:81
  149.8 5.3 %products.5.refs_8_ = f32[8,128]{1,0:T(8,128)S(1)} custom-call(s32[10]{0:T(128)S(1)} %copy-done.5, f32[160,1280]{1,0:T(8,128)S(1)} %get-tuple-element.43.refs_0_.refs_1_, f32[160,1280]{1,0:T(8,128)S(1)} %get-tuple-element.39.refs_1_.refs_0_.refs_2_, bf16[320,1280]{1,0:T(8,128)(2,1)S(1)} %collective-permute-done.6.refs_2_.refs_3_.refs_1_.refs_4_, ...), custom_call_target="tpu_custom_call" | custom-call | flops 1 | bytes 1 | tf_op jit(solution)/shard_map/products/pallas_call | solution.py:81
  155.1 1.7 products.6.refs_8_
  156.8 1.7 products.7.refs_0_
  160.5 1.8 collective-permute-done.30.refs_2_
  163.8 3.1 %collective-permute-start.33 = (f32[8,128]{1,0:T(8,128)S(1)}, f32[8,128]{1,0:T(8,128)S(1)}, u32[]{:S(2)}, u32[]{:S(2)}) collective-permute-start(f32[8,128]{1,0:T(8,128)S(1)} %sum_of.3.refs_0_), channel_id=1, source_target_pairs={{0,16},{1,17},{2,18},{3,19},{4,20},{5,21},{6,22},{7,23},{8,24},{9,... | collective-permute-start | bytes 12296 | tf_op jit(solution)/shard_map/ppermute | solution.py:27
  168.5 3.8 %collective-permute-done.34.refs_3_ = f32[8,128]{1,0:T(8,128)S(1)} collective-permute-done((f32[8,128]{1,0:T(8,128)S(1)}, f32[8,128]{1,0:T(8,128)S(1)}, u32[]{:S(2)}, u32[]{:S(2)}) %collective-permute-start.34) | collective-permute-done | bytes 4128 | tf_op jit(solution)/shard_map/ppermute | solution.py:27
  172.9 1.6 collective-permute-start.35
  174.4 2.1 %collective-permute-done.35.refs_1_ = f32[8,128]{1,0:T(8,128)S(1)} collective-permute-done((f32[8,128]{1,0:T(8,128)S(1)}, f32[8,128]{1,0:T(8,128)S(1)}, u32[]{:S(2)}, u32[]{:S(2)}) %collective-permute-start.35) | collective-permute-done | bytes 4128 | tf_op jit(solution)/shard_map/ppermute | solution.py:27
  177.1 4.1 %merge.1 = (f32[160,1280]{1,0:T(8,128)}, f32[160,1280]{1,0:T(8,128)}) custom-call(s32[10]{0:T(128)S(1)} %copy-done.5, f32[8,128]{1,0:T(8,128)S(1)} %sum_of.5.refs_0_, f32[160,1280]{1,0:T(8,128)S(1)} %get-tuple-element.43.refs_0_.refs_1_, f32[160,1280]{1,0:T(8,128)S(1)} %get-tuple-element.39.refs_1_.refs_0_.refs_2_, ...), custom_call_target="tpu_custom_call" | custom-call | flops 1 | bytes 1 | tf_op jit(solution)/shard_map/merge/pallas_call | solution.py:81
  (80 shorter events, 23.3 us)
Async XLA Ops:
  11.9 4.4 %collective-permute-start.2 = (f32[352,1280]{1,0:T(8,128)}, f32[352,1280]{1,0:T(8,128)S(1)}, u32[]{:S(2)}, u32[]{:S(2)}) collective-permute-start(f32[352,1280]{1,0:T(8,128)} %get-tuple-element.37), channel_id=1, source_target_pairs={{0,1},{1,0},{2,3},{3,2},{4,5},{5,4},{6,7},{7,6},{8,9},{9,8},{10,11... | collective-permute-start | bytes 5406728 | tf_op jit(solution)/shard_map/ppermute | solution.py:27
  16.6 23.2 %collective-permute-start.3 = (f16[352,1280]{1,0:T(8,128)(2,1)S(1)}, f16[352,1280]{1,0:T(8,128)(2,1)S(1)}, u32[]{:S(2)}, u32[]{:S(2)}) collective-permute-start(f16[352,1280]{1,0:T(8,128)(2,1)S(1)} %get-tuple-element.68), channel_id=1, source_target_pairs={{0,2},{1,3},{2,0},{3,1},{4,6},{5,7},{6,4},{7,5},{8,10},{9,11},{10,... | collective-permute-start | bytes 2703368 | tf_op jit(solution)/shard_map/ppermute | solution.py:27
  19.1 23.1 %collective-permute-start = (bf16[176,1280]{1,0:T(8,128)(2,1)S(1)}, bf16[176,1280]{1,0:T(8,128)(2,1)S(1)}, u32[]{:S(2)}, u32[]{:S(2)}) collective-permute-start(bf16[176,1280]{1,0:T(8,128)(2,1)S(1)} %copy-done.6), channel_id=1, source_target_pairs={{0,16},{1,17},{2,18},{3,19},{4,20},{5,21},{6,22},{7,23},{8,24},{9,... | collective-permute-start | bytes 1351688 | tf_op jit(solution)/shard_map/ppermute | solution.py:27
  21.7 20.7 %collective-permute-start.1 = (bf16[176,1280]{1,0:T(8,128)(2,1)S(1)}, bf16[176,1280]{1,0:T(8,128)(2,1)S(1)}, u32[]{:S(2)}, u32[]{:S(2)}) collective-permute-start(bf16[176,1280]{1,0:T(8,128)(2,1)S(1)} %copy-done.6), channel_id=1, source_target_pairs={{0,8},{1,9},{2,10},{3,11},{4,12},{5,13},{6,14},{7,15},{8,0},{9,1},... | collective-permute-start | bytes 1351688 | tf_op jit(solution)/shard_map/ppermute | solution.py:27
  43.6 3.1 %collective-permute-start.4 = (bf16[352,1280]{1,0:T(8,128)(2,1)S(1)}, bf16[352,1280]{1,0:T(8,128)(2,1)S(1)}, u32[]{:S(2)}, u32[]{:S(2)}) collective-permute-start(bf16[352,1280]{1,0:T(8,128)(2,1)S(1)} %get-tuple-element.38.refs_0_), channel_id=1, source_target_pairs={{0,1},{1,0},{2,3},{3,2},{4,5},{5,4},{6,7},{7,6},{8,9},{9,8},{10,11... | collective-permute-start | bytes 2703368 | tf_op jit(solution)/shard_map/ppermute | solution.py:27
  43.7 12.8 %collective-permute-start.5 = (bf16[176,1280]{1,0:T(8,128)(2,1)S(1)}, bf16[176,1280]{1,0:T(8,128)(2,1)S(1)}, u32[]{:S(2)}, u32[]{:S(2)}) collective-permute-start(bf16[176,1280]{1,0:T(8,128)(2,1)S(1)} %collective-permute-done.refs_0_), channel_id=1, source_target_pairs={{0,4},{1,5},{2,6},{3,7},{4,0},{5,1},{6,2},{7,3},{8,12},{9,13},{10,... | collective-permute-start | bytes 1351688 | tf_op jit(solution)/shard_map/ppermute | solution.py:27
  45.3 35.8 %collective-permute-start.7 = (bf16[352,1280]{1,0:T(8,128)(2,1)S(1)}, bf16[352,1280]{1,0:T(8,128)(2,1)S(1)}, u32[]{:S(2)}, u32[]{:S(2)}) collective-permute-start(bf16[352,1280]{1,0:T(8,128)(2,1)S(1)} %get-tuple-element.38.refs_0_), channel_id=1, source_target_pairs={{0,8},{1,9},{2,10},{3,11},{4,12},{5,13},{6,14},{7,15},{8,0},{9,1},... | collective-permute-start | bytes 2703368 | tf_op jit(solution)/shard_map/ppermute | solution.py:27
  56.4 24.7 %collective-permute-start.6 = (bf16[320,1280]{1,0:T(8,128)(2,1)S(1)}, bf16[320,1280]{1,0:T(8,128)(2,1)S(1)}, u32[]{:S(2)}, u32[]{:S(2)}) collective-permute-start(bf16[320,1280]{1,0:T(8,128)(2,1)S(1)} %get-tuple-element.42), channel_id=1, source_target_pairs={{0,4},{1,5},{2,6},{3,7},{4,0},{5,1},{6,2},{7,3},{8,12},{9,13},{10,... | collective-permute-start | bytes 2457608 | tf_op jit(solution)/shard_map/ppermute | solution.py:27
  58.0 13.3 %collective-permute-start.11 = (bf16[176,1280]{1,0:T(8,128)(2,1)S(1)}, bf16[176,1280]{1,0:T(8,128)(2,1)S(1)}, u32[]{:S(2)}, u32[]{:S(2)}) collective-permute-start(bf16[176,1280]{1,0:T(8,128)(2,1)S(1)} %collective-permute-done.refs_0_), channel_id=1, source_target_pairs={{0,2},{1,3},{2,0},{3,1},{4,6},{5,7},{6,4},{7,5},{8,10},{9,11},{10,... | collective-permute-start | bytes 1351688 | tf_op jit(solution)/shard_map/ppermute | solution.py:27
  58.9 21.9 %collective-permute-start.10 = (bf16[176,1280]{1,0:T(8,128)(2,1)S(1)}, bf16[176,1280]{1,0:T(8,128)(2,1)S(1)}, u32[]{:S(2)}, u32[]{:S(2)}) collective-permute-start(bf16[176,1280]{1,0:T(8,128)(2,1)S(1)} %get-tuple-element.46), channel_id=1, source_target_pairs={{0,16},{1,17},{2,18},{3,19},{4,20},{5,21},{6,22},{7,23},{8,24},{9,... | collective-permute-start | bytes 1351688 | tf_op jit(solution)/shard_map/ppermute | solution.py:27
  60.2 20.7 %collective-permute-start.9 = (bf16[176,1280]{1,0:T(8,128)(2,1)S(1)}, bf16[176,1280]{1,0:T(8,128)(2,1)S(1)}, u32[]{:S(2)}, u32[]{:S(2)}) collective-permute-start(bf16[176,1280]{1,0:T(8,128)(2,1)S(1)} %collective-permute-done.1.refs_1_.refs_0_), channel_id=1, source_target_pairs={{0,2},{1,3},{2,0},{3,1},{4,6},{5,7},{6,4},{7,5},{8,10},{9,11},{10,... | collective-permute-start | bytes 1351688 | tf_op jit(solution)/shard_map/ppermute | solution.py:27
  81.1 4.6 %collective-permute-start.8 = (bf16[352,1280]{1,0:T(8,128)(2,1)S(1)}, bf16[352,1280]{1,0:T(8,128)(2,1)S(1)}, u32[]{:S(2)}, u32[]{:S(2)}) collective-permute-start(bf16[352,1280]{1,0:T(8,128)(2,1)S(1)} %collective-permute-done.7.refs_0_), channel_id=1, source_target_pairs={{0,1},{1,0},{2,3},{3,2},{4,5},{5,4},{6,7},{7,6},{8,9},{9,8},{10,11... | collective-permute-start | bytes 2703368 | tf_op jit(solution)/shard_map/ppermute | solution.py:27
  81.6 14.7 %collective-permute-start.16 = (bf16[176,1280]{1,0:T(8,128)(2,1)S(1)}, bf16[176,1280]{1,0:T(8,128)(2,1)S(1)}, u32[]{:S(2)}, u32[]{:S(2)}) collective-permute-start(bf16[176,1280]{1,0:T(8,128)(2,1)S(1)} %collective-permute-done.10.refs_0_), channel_id=1, source_target_pairs={{0,2},{1,3},{2,0},{3,1},{4,6},{5,7},{6,4},{7,5},{8,10},{9,11},{10,... | collective-permute-start | bytes 1351688 | tf_op jit(solution)/shard_map/ppermute | solution.py:27
  82.7 21.1 %collective-permute-start.14 = (bf16[176,1280]{1,0:T(8,128)(2,1)S(1)}, bf16[176,1280]{1,0:T(8,128)(2,1)S(1)}, u32[]{:S(2)}, u32[]{:S(2)}) collective-permute-start(bf16[176,1280]{1,0:T(8,128)(2,1)S(1)} %collective-permute-done.10.refs_0_), channel_id=1, source_target_pairs={{0,8},{1,9},{2,10},{3,11},{4,12},{5,13},{6,14},{7,15},{8,0},{9,1},... | collective-permute-start | bytes 1351688 | tf_op jit(solution)/shard_map/ppermute | solution.py:27
  83.1 20.5 %collective-permute-start.17 = (bf16[176,1280]{1,0:T(8,128)(2,1)S(1)}, bf16[176,1280]{1,0:T(8,128)(2,1)S(1)}, u32[]{:S(2)}, u32[]{:S(2)}) collective-permute-start(bf16[176,1280]{1,0:T(8,128)(2,1)S(1)} %collective-permute-done.5.refs_0_), channel_id=1, source_target_pairs={{0,2},{1,3},{2,0},{3,1},{4,6},{5,7},{6,4},{7,5},{8,10},{9,11},{10,... | collective-permute-start | bytes 1351688 | tf_op jit(solution)/shard_map/ppermute | solution.py:27
  84.0 30.0 %collective-permute-start.20 = (bf16[352,1280]{1,0:T(8,128)(2,1)S(1)}, bf16[352,1280]{1,0:T(8,128)(2,1)S(1)}, u32[]{:S(2)}, u32[]{:S(2)}) collective-permute-start(bf16[352,1280]{1,0:T(8,128)(2,1)S(1)} %join.6.refs_2_), channel_id=1, source_target_pairs={{0,8},{1,9},{2,10},{3,11},{4,12},{5,13},{6,14},{7,15},{8,0},{9,1},... | collective-permute-start | bytes 2703368 | tf_op jit(solution)/shard_map/ppermute | solution.py:27
  85.7 18.1 %collective-permute-start.15 = (bf16[176,1280]{1,0:T(8,128)(2,1)S(1)}, bf16[176,1280]{1,0:T(8,128)(2,1)S(1)}, u32[]{:S(2)}, u32[]{:S(2)}) collective-permute-start(bf16[176,1280]{1,0:T(8,128)(2,1)S(1)} %collective-permute-done.10.refs_0_), channel_id=1, source_target_pairs={{0,4},{1,5},{2,6},{3,7},{4,0},{5,1},{6,2},{7,3},{8,12},{9,13},{10,... | collective-permute-start | bytes 1351688 | tf_op jit(solution)/shard_map/ppermute | solution.py:27
  96.3 19.2 %collective-permute-start.13 = (bf16[320,1280]{1,0:T(8,128)(2,1)S(1)}, bf16[320,1280]{1,0:T(8,128)(2,1)S(1)}, u32[]{:S(2)}, u32[]{:S(2)}) collective-permute-start(bf16[320,1280]{1,0:T(8,128)(2,1)S(1)} %get-tuple-element.50), channel_id=1, source_target_pairs={{0,4},{1,5},{2,6},{3,7},{4,0},{5,1},{6,2},{7,3},{8,12},{9,13},{10,... | collective-permute-start | bytes 2457608 | tf_op jit(solution)/shard_map/ppermute | solution.py:27
  103.8 11.6 %collective-permute-start.18 = (bf16[176,1280]{1,0:T(8,128)(2,1)S(1)}, bf16[176,1280]{1,0:T(8,128)(2,1)S(1)}, u32[]{:S(2)}, u32[]{:S(2)}) collective-permute-start(bf16[176,1280]{1,0:T(8,128)(2,1)S(1)} %collective-permute-done.14.refs_0_), channel_id=1, source_target_pairs={{0,2},{1,3},{2,0},{3,1},{4,6},{5,7},{6,4},{7,5},{8,10},{9,11},{10,... | collective-permute-start | bytes 1351688 | tf_op jit(solution)/shard_map/ppermute | solution.py:27
  114.0 5.3 %collective-permute-start.21 = (bf16[352,1280]{1,0:T(8,128)(2,1)S(1)}, bf16[352,1280]{1,0:T(8,128)(2,1)S(1)}, u32[]{:S(2)}, u32[]{:S(2)}) collective-permute-start(bf16[352,1280]{1,0:T(8,128)(2,1)S(1)} %collective-permute-done.20.refs_3_), channel_id=1, source_target_pairs={{0,1},{1,0},{2,3},{3,2},{4,5},{5,4},{6,7},{7,6},{8,9},{9,8},{10,11... | collective-permute-start | bytes 2703368 | tf_op jit(solution)/shard_map/ppermute | solution.py:27
  115.6 3.8 %collective-permute-start.19 = (bf16[352,1280]{1,0:T(8,128)(2,1)S(1)}, bf16[352,1280]{1,0:T(8,128)(2,1)S(1)}, u32[]{:S(2)}, u32[]{:S(2)}) collective-permute-start(bf16[352,1280]{1,0:T(8,128)(2,1)S(1)} %join.10.refs_1_), channel_id=1, source_target_pairs={{0,1},{1,0},{2,3},{3,2},{4,5},{5,4},{6,7},{7,6},{8,9},{9,8},{10,11... | collective-permute-start | bytes 2703368 | tf_op jit(solution)/shard_map/ppermute | solution.py:27
  115.7 13.6 %collective-permute-start.24 = (bf16[176,1280]{1,0:T(8,128)(2,1)S(1)}, bf16[176,1280]{1,0:T(8,128)(2,1)S(1)}, u32[]{:S(2)}, u32[]{:S(2)}) collective-permute-start(bf16[176,1280]{1,0:T(8,128)(2,1)S(1)} %collective-permute-done.15.refs_0_), channel_id=1, source_target_pairs={{0,2},{1,3},{2,0},{3,1},{4,6},{5,7},{6,4},{7,5},{8,10},{9,11},{10,... | collective-permute-start | bytes 1351688 | tf_op jit(solution)/shard_map/ppermute | solution.py:27
  116.8 14.3 %collective-permute-start.23 = (bf16[352,1280]{1,0:T(8,128)(2,1)S(1)}, bf16[352,1280]{1,0:T(8,128)(2,1)S(1)}, u32[]{:S(2)}, u32[]{:S(2)}) collective-permute-start(bf16[352,1280]{1,0:T(8,128)(2,1)S(1)} %join.6.refs_2_), channel_id=1, source_target_pairs={{0,1},{1,0},{2,3},{3,2},{4,5},{5,4},{6,7},{7,6},{8,9},{9,8},{10,11... | collective-permute-start | bytes 2703368 | tf_op jit(solution)/shard_map/ppermute | solution.py:27
  117.0 23.9 %collective-permute-start.26 = (bf16[352,1280]{1,0:T(8,128)(2,1)S(1)}, bf16[352,1280]{1,0:T(8,128)(2,1)S(1)}, u32[]{:S(2)}, u32[]{:S(2)}) collective-permute-start(bf16[352,1280]{1,0:T(8,128)(2,1)S(1)} %join.9.refs_3_), channel_id=1, source_target_pairs={{0,1},{1,0},{2,3},{3,2},{4,5},{5,4},{6,7},{7,6},{8,9},{9,8},{10,11... | collective-permute-start | bytes 2703368 | tf_op jit(solution)/shard_map/ppermute | solution.py:27
  129.4 11.5 %collective-permute-start.25 = (bf16[352,1280]{1,0:T(8,128)(2,1)S(1)}, bf16[352,1280]{1,0:T(8,128)(2,1)S(1)}, u32[]{:S(2)}, u32[]{:S(2)}) collective-permute-start(bf16[352,1280]{1,0:T(8,128)(2,1)S(1)} %join.11.refs_1_), channel_id=1, source_target_pairs={{0,1},{1,0},{2,3},{3,2},{4,5},{5,4},{6,7},{7,6},{8,9},{9,8},{10,11... | collective-permute-start | bytes 2703368 | tf_op jit(solution)/shard_map/ppermute | solution.py:27
  129.8 25.3 %collective-permute-start.28 = (bf16[160,1280]{1,0:T(8,128)(2,1)S(1)}, bf16[160,1280]{1,0:T(8,128)(2,1)S(1)}, u32[]{:S(2)}, u32[]{:S(2)}) collective-permute-start(bf16[160,1280]{1,0:T(8,128)(2,1)S(1)} %get-tuple-element.67), channel_id=1, source_target_pairs={{0,4},{1,5},{2,6},{3,7},{4,0},{5,1},{6,2},{7,3},{8,12},{9,13},{10,... | collective-permute-start | bytes 1228808 | tf_op jit(solution)/shard_map/ppermute | solution.py:27
  131.1 25.7 %collective-permute-start.27 = (bf16[160,1280]{1,0:T(8,128)(2,1)S(1)}, bf16[160,1280]{1,0:T(8,128)(2,1)S(1)}, u32[]{:S(2)}, u32[]{:S(2)}) collective-permute-start(bf16[160,1280]{1,0:T(8,128)(2,1)S(1)} %get-tuple-element.65), channel_id=1, source_target_pairs={{0,4},{1,5},{2,6},{3,7},{4,0},{5,1},{6,2},{7,3},{8,12},{9,13},{10,... | collective-permute-start | bytes 1228808 | tf_op jit(solution)/shard_map/ppermute | solution.py:27
  158.7 3.7 %collective-permute-start.30 = (f32[8,128]{1,0:T(8,128)S(1)}, f32[8,128]{1,0:T(8,128)S(1)}, u32[]{:S(2)}, u32[]{:S(2)}) collective-permute-start(f32[8,128]{1,0:T(8,128)S(1)} %products.7.refs_0_), channel_id=1, source_target_pairs={{0,2},{1,3},{2,0},{3,1},{4,6},{5,7},{6,4},{7,5},{8,10},{9,11},{10,... | collective-permute-start | bytes 12296 | tf_op jit(solution)/shard_map/ppermute | solution.py:27
  163.3 4.5 %collective-permute-start.32 = (f32[8,128]{1,0:T(8,128)S(1)}, f32[8,128]{1,0:T(8,128)S(1)}, u32[]{:S(2)}, u32[]{:S(2)}) collective-permute-start(f32[8,128]{1,0:T(8,128)S(1)} %sum_of.3.refs_0_), channel_id=1, source_target_pairs={{0,8},{1,9},{2,10},{3,11},{4,12},{5,13},{6,14},{7,15},{8,0},{9,1},... | collective-permute-start | bytes 12296 | tf_op jit(solution)/shard_map/ppermute | solution.py:27
  163.8 4.7 %collective-permute-start.33 = (f32[8,128]{1,0:T(8,128)S(1)}, f32[8,128]{1,0:T(8,128)S(1)}, u32[]{:S(2)}, u32[]{:S(2)}) collective-permute-start(f32[8,128]{1,0:T(8,128)S(1)} %sum_of.3.refs_0_), channel_id=1, source_target_pairs={{0,16},{1,17},{2,18},{3,19},{4,20},{5,21},{6,22},{7,23},{8,24},{9,... | collective-permute-start | bytes 12296 | tf_op jit(solution)/shard_map/ppermute | solution.py:27
  166.9 5.4 %collective-permute-start.34 = (f32[8,128]{1,0:T(8,128)S(1)}, f32[8,128]{1,0:T(8,128)S(1)}, u32[]{:S(2)}, u32[]{:S(2)}) collective-permute-start(f32[8,128]{1,0:T(8,128)S(1)} %sum_of.3.refs_0_), channel_id=1, source_target_pairs={{0,24},{1,25},{2,26},{3,27},{4,28},{5,29},{6,30},{7,31},{8,16},{9,... | collective-permute-start | bytes 12296 | tf_op jit(solution)/shard_map/ppermute | solution.py:27
  172.9 3.7 %collective-permute-start.35 = (f32[8,128]{1,0:T(8,128)S(1)}, f32[8,128]{1,0:T(8,128)S(1)}, u32[]{:S(2)}, u32[]{:S(2)}) collective-permute-start(f32[8,128]{1,0:T(8,128)S(1)} %sum_of.4.refs_0_), channel_id=1, source_target_pairs={{0,4},{1,5},{2,6},{3,7},{4,0},{5,1},{6,2},{7,3},{8,12},{9,13},{10,... | collective-permute-start | bytes 12296 | tf_op jit(solution)/shard_map/ppermute | solution.py:27
  (11 other events, 71.4 us)

commit v17 on v13

--- a/solution.py
+++ b/solution.py
@@ -88,7 +88,7 @@
     )(operands[0], *after, *operands[1:])
 
 
-WINDOW, SHIFT, OTHER_SHIFT, MEMBER, NEAR, FAR, PART, PIECE = range(8)
+WINDOW, SHIFT, OTHER_SHIFT, MEMBER, NEAR, FAR, PART, PIECE, OWN_WINDOW, OWN_SHIFT = range(10)
 
 
 def row_start(place_ref, block, where):
@@ -234,7 +234,7 @@
     )
 
 
-def gradient_kernel(wheres, window, own, step_rows, place_ref, *refs):
+def gradient_kernel(wheres, window, own, step_rows, shared, place_ref, *refs):
     error_wheres, input_wheres = wheres
     refs = list(refs)
 
@@ -244,7 +244,8 @@
         return taken
 
     error_refs, input_refs = take(len(error_wheres)), take(len(input_wheres))
-    w_in_ref, w_out_ref, first_ref, second_ref, send_first_ref, send_second_ref = take(6)
+    w_in_ref, w_out_ref, first_ref, second_ref = take(4)
+    send_refs = take(shared)
     errors, inputs, inputs_turned, errors_turned, spread_first, spread_second = refs
     if len(input_refs) == 1:
         inputs = input_refs[0]
@@ -256,12 +257,11 @@
         if len(input_refs) > 1:
             for block, where in zip(input_refs, input_wheres):
                 inputs[pl.ds(row_start(place_ref, block, where), block.shape[0]), :] = block[...]
-        lane = pl.multiple_of(place_ref[WINDOW] * 128, 128)
+        lane = pl.multiple_of(place_ref[WINDOW if shared else OWN_WINDOW] * 128, 128)
         inputs_turned[...] = inputs[:, pl.ds(lane, window * 128)].T
         errors_turned[...] = errors[:, pl.ds(lane, window * 128)].T
 
-    shift = pl.multiple_of(place_ref[SHIFT], step_rows)
-    other_shift = pl.multiple_of(place_ref[OTHER_SHIFT], step_rows)
+    shift = pl.multiple_of(place_ref[SHIFT if shared else OWN_SHIFT], step_rows)
     v = jnp.dot(inputs[...], w_in_ref[...], preferred_element_type=jnp.float32)
     back = lax.dot_general(
         errors[...], w_out_ref[...], (((1,), (1,)), ((), ())), preferred_element_type=jnp.float32
@@ -275,33 +275,36 @@
     dpre = (back * slope).astype(jnp.bfloat16)
     spread_first[...] = jnp.dot(inputs_turned[...], dpre, preferred_element_type=jnp.float32)
     second_ref[...] = spread_second[pl.ds(shift, own), :]
-    send_second_ref[...] = spread_second[pl.ds(other_shift, own), :].astype(jnp.bfloat16)
     first_ref[...] = spread_first[pl.ds(shift, own), :]
-    send_first_ref[...] = spread_first[pl.ds(other_shift, own), :].astype(jnp.bfloat16)
-
-
-def gradient(place, members, swap, errors, inputs, w_in, w_out, after=()):
+    if shared:
+        other = pl.ds(pl.multiple_of(place_ref[OTHER_SHIFT], step_rows), own)
+        send_refs[0][:own, :] = spread_first[other, :].astype(jnp.bfloat16)
+        last = send_refs[-1].shape[0]
+        send_refs[-1][last - own :, :] = spread_second[other, :].astype(jnp.bfloat16)
+
+
+def gradient(place, members, swap, shared, errors, inputs, w_in, w_out, after=()):
     error_arrays, error_wheres = zip(*errors)
     input_arrays, input_wheres = zip(*inputs)
     depth, width = w_in.shape
     rows = sum(a.shape[0] for a in input_arrays)
     own = depth // members
-    reach = max(m * own % 128 for m in range(members) if not m & swap) + (swap + 1) * own
+    starts = [m * own % 128 for m in range(members) if not (shared and m & swap)]
+    reach = max(starts) + (swap + 1 if shared else 1) * own
     window = -(-reach // 128)
     tile = tile_of(width, 640)
     once = pl.Buffered(1)
     return call(
         functools.partial(
-            gradient_kernel, (error_wheres, input_wheres), window, own, math.gcd(own, 128)
+            gradient_kernel, (error_wheres, input_wheres), window, own, math.gcd(own, 128), shared
         ),
         "gradient",
         (place, *error_arrays, *input_arrays, w_in, w_out),
         [
             jax.ShapeDtypeStruct((own, width), jnp.float32),
             jax.ShapeDtypeStruct((own, width), jnp.float32),
-            jax.ShapeDtypeStruct((own, width), jnp.bfloat16),
-            jax.ShapeDtypeStruct((own, width), jnp.bfloat16),
-        ],
+        ]
+        + [jax.ShapeDtypeStruct((2 * own // max(shared, 1), width), jnp.bfloat16)] * shared,
         after,
         grid=(width // tile,),
         in_specs=[
@@ -309,7 +312,8 @@
             for a in (*error_arrays, *input_arrays)
         ]
         + [pl.BlockSpec((depth, tile), column), pl.BlockSpec((tile, depth), lambda n, s: (n, 0))],
-        out_specs=[pl.BlockSpec((own, tile), column)] * 4,
+        out_specs=[pl.BlockSpec((own, tile), column)] * 2
+        + [pl.BlockSpec((2 * own // max(shared, 1), tile), column)] * shared,
         scratch_shapes=[
             pltpu.VMEM((rows, depth), jnp.bfloat16),
             pltpu.VMEM((rows, depth), jnp.bfloat16),
@@ -353,8 +357,9 @@
 
 
 def products(place, slots, labels, fresh, known, after=()):
-    arrays = [a for slot in slots for a in slot]
-    own, width = slots[0][0].shape
+    arrays = [a for slot in slots for a, _ in slot]
+    blocks = [k for slot in slots for _, k in slot]
+    own, width = arrays[0].shape
     tile = tile_of(width, 256)
     pairs = sum(len(slots) - n for n in range(fresh))
     return call(
@@ -364,7 +369,7 @@
         [jax.ShapeDtypeStruct(known.shape, jnp.float32)],
         after,
         grid=(width // tile,),
-        in_specs=[pl.BlockSpec((a.shape[0], tile), lambda n, s: (0, n)) for a in arrays]
+        in_specs=[pl.BlockSpec((own, tile), lambda n, s, k=k: (k, n)) for k in blocks]
         + [pl.BlockSpec(known.shape, whole)],
         out_specs=[pl.BlockSpec(known.shape, whole)],
         scratch_shapes=[pltpu.VMEM((pairs, 8, tile), jnp.float32)],
@@ -434,10 +439,16 @@
 
 
 def merge(place, totals, slots, labels):
-    own, width = slots[0][0].shape
+    arrays = [a for slot in slots for a, _ in slot]
+    own, width = arrays[0].shape
     block = max(b for b in range(16, min(own, 32) + 1, 16) if own % b == 0)
+    steps = own // block
     spec = pl.BlockSpec((block, width), lambda n, s: (n, 0))
-    arrays = [a for slot in slots for a in slot]
+    specs = [
+        pl.BlockSpec((block, width), lambda n, s, k=k: (n + k * steps, 0))
+        for slot in slots
+        for _, k in slot
+    ]
     shape = jax.ShapeDtypeStruct((own, width), jnp.float32)
     return call(
         functools.partial(merge_kernel, tuple(labels)),
@@ -445,8 +456,8 @@
         (place, totals, *arrays),
         [shape, shape],
         vmem=16 * 2**20,
-        grid=(own // block,),
-        in_specs=[pl.BlockSpec(memory_space=pltpu.SMEM)] + [spec] * len(arrays),
+        grid=(steps,),
+        in_specs=[pl.BlockSpec(memory_space=pltpu.SMEM)] + specs,
         out_specs=[spec, spec],
         scratch_shapes=[pltpu.SMEM((len(slots),), jnp.float32)],
     )
@@ -488,6 +499,8 @@
             1 - near,
             part_of(shard),
             part_of(shard) - near * (shards // 2),
+            member * own // 128,
+            member * own % 128,
         ]
     ).astype(jnp.int32)
 
@@ -523,17 +536,17 @@
     def both_halves(half):
         return [(half, NEAR), (from_mask(half, 0, 1), FAR)]
 
-    slots, labels, known, sent, halves = [], [], [], [], {}
+    slots, labels, known, sent, got, halves = [], [], [], [], [], {}
     totals = jnp.zeros((8, 128), jnp.float32)
     masks = [m for m in range(members) if not m & swap]
     for n, m in enumerate(masks):
         if n == 0:
             half = error
         elif m not in (bits[0], masks[-1]):
-            half = errors_of[m] = ordered(errors_of[m], sent[0], *slots[1][:1])
+            half = errors_of[m] = ordered(errors_of[m], sent[0], *got[0][:1])
             other_inputs = halves[m]
         elif m == bits[0]:
-            before = [sent[-1], *slots[1]]
+            before = [sent[-1], *got[0]]
             errors_of[m] = ordered(errors_of[m], sent[0])
             for bit in bits[1:]:
                 ready = ordered(errors_of[m], errors_of[bit])
@@ -544,12 +557,15 @@
             half = to_half(errors_of[m], *before)
             other_inputs = halves[m]
         else:
-            half = to_half(ordered(errors_of[m], sent[-2]), sent[-1], *slots[2 * n - 3])
+            half = to_half(ordered(errors_of[m], sent[-2]), sent[-1], *got[n - 2])
             other_inputs = ordered(halves[m], sent[-1])
+        last = n == len(masks) - 1
+        shared = 2 if n == 0 or last else 1
         first, second, *send = gradient(
             place,
             members,
             swap,
+            shared,
             both_halves(half),
             both_halves(other_inputs) if n else [(inputs, None)],
             w_in,
@@ -559,13 +575,13 @@
         if n == 0:
             for bit in bits:
                 halves[bit] = to_half(inputs_of[bit], send[0], errors_of[bits[0]], *halves.values())
-        sent.append(send[0])
-        slots.append((first, second))
+        sent.append(first)
+        slots.append(((first, 0), (second, 0)))
         labels.append(m)
-        last = n == len(masks) - 1
         if last:
             totals = products(place, slots, labels, 1, totals)
-        slots.append(tuple(from_mask(a, swap * others, 0) for a in send))
+        got.append([from_mask(a, swap * others, 0) for a in send])
+        slots.append(((got[n][0], 0), (got[n][-1], 2 - shared)))
         labels.append(m ^ swap)
         if last:
             for k in range(2):

time: 175 us -> 175 us (level)
    ppermute x34 -> x32, waiting for transfers between devices: 62.9 us -> 64.5 us  [from_mask(): return lax.ppermute(value, ('dp', 'tensor'), pairs)]
    ppermute x34 -> x32, starting transfers between devices: 35.7 us -> 34.1 us  [from_mask(): return lax.ppermute(value, ('dp', 'tensor'), pairs)]
  transfers between devices with their start and end apart: 34 -> 32, of which waited for: 15 -> 15; matrix products, arithmetic and copies ran while one was open for 0% -> 0% of each run, Pallas kernels for 31% -> 31%
where the time goes in v17:
time: 175 us
  Pallas kernels  73.2 us (42%)
  waiting for transfers between devices  64.5 us (37%)
  starting transfers between devices  34.1 us (19%)
  local copies, waits for them, and re-layouts  1.81 us (1%)
    pallas_call x21, Pallas kernels, call(): pl.pallas_call(body, grid_spec=pltpu.PrefetchScalarGridSpec(num_scalar_pr...  73.2 us
    ppermute x32, waiting for transfers between devices, from_mask(): return lax.ppermute(value, ('dp', 'tensor'), pairs)  64.5 us
    ppermute x32, starting transfers between devices, from_mask(): return lax.ppermute(value, ('dp', 'tensor'), pairs)  34.1 us
  transfers between devices with their start and end apart: 32, of which 15 were waited for; matrix products, arithmetic and copies ran while one was open for 0% of the time, Pallas kernels for 31%

profile of v17, /device:TPU:0, one launch (start us, length us, event | category | flops | bytes accessed | tf_op | source)
XLA Modules:
  0.0 175.0 jit_solution(5321253948652761679)
XLA Ops:
  1.3 10.7 %forward.1 = (f32[352,1280]{1,0:T(8,128)}, bf16[352,1280]{1,0:T(8,128)(2,1)}, bf16[176,1280]{1,0:T(8,128)(2,1)}) custom-call(s32[10]{0:T(128)} %stack.43.place_ref, bf16[704,1280]{1,0:T(8,128)(2,1)} %refs_2_.3, bf16[1280,1280]{1,0:T(8,128)(2,1)} %refs_5_.5, bf16[1280,1280]{1,0:T(8,128)(2,1)} %refs_6_.3), custom_call_target="tpu_custom_call" | custom-call | flops 1 | bytes 1 | tf_op jit(solution)/shard_map/forward/pallas_call | solution.py:81
  13.6 2.7 %product.1 = f32[352,1280]{1,0:T(8,128)S(1)} custom-call(s32[10]{0:T(128)S(1)} %copy-done.5, bf16[352,1280]{1,0:T(8,128)(2,1)S(1)} %copy-done.4, bf16[1280,1280]{1,0:T(8,128)(2,1)S(1)} %copy-done), custom_call_target="tpu_custom_call" | custom-call | flops 1 | bytes 1 | tf_op jit(solution)/shard_map/product/pallas_call | solution.py:81
  16.6 2.6 %collective-permute-start.3 = (f16[352,1280]{1,0:T(8,128)(2,1)S(1)}, f16[352,1280]{1,0:T(8,128)(2,1)S(1)}, u32[]{:S(2)}, u32[]{:S(2)}) collective-permute-start(f16[352,1280]{1,0:T(8,128)(2,1)S(1)} %get-tuple-element.60), channel_id=1, source_target_pairs={{0,2},{1,3},{2,0},{3,1},{4,6},{5,7},{6,4},{7,5},{8,10},{9,11},{10,... | collective-permute-start | bytes 2703368 | tf_op jit(solution)/shard_map/ppermute | solution.py:27
  19.2 2.6 %collective-permute-start = (bf16[176,1280]{1,0:T(8,128)(2,1)S(1)}, bf16[176,1280]{1,0:T(8,128)(2,1)S(1)}, u32[]{:S(2)}, u32[]{:S(2)}) collective-permute-start(bf16[176,1280]{1,0:T(8,128)(2,1)S(1)} %copy-done.6), channel_id=1, source_target_pairs={{0,16},{1,17},{2,18},{3,19},{4,20},{5,21},{6,22},{7,23},{8,24},{9,... | collective-permute-start | bytes 1351688 | tf_op jit(solution)/shard_map/ppermute | solution.py:27
  21.8 1.6 collective-permute-start.1
  23.4 16.5 %collective-permute-done.3 = f16[352,1280]{1,0:T(8,128)(2,1)S(1)} collective-permute-done((f16[352,1280]{1,0:T(8,128)(2,1)S(1)}, f16[352,1280]{1,0:T(8,128)(2,1)S(1)}, u32[]{:S(2)}, u32[]{:S(2)}) %collective-permute-start.3) | collective-permute-done | bytes 901152 | tf_op jit(solution)/shard_map/ppermute | solution.py:27
  40.0 2.3 %collective-permute-done.refs_0_ = bf16[176,1280]{1,0:T(8,128)(2,1)S(1)} collective-permute-done((bf16[176,1280]{1,0:T(8,128)(2,1)S(1)}, bf16[176,1280]{1,0:T(8,128)(2,1)S(1)}, u32[]{:S(2)}, u32[]{:S(2)}) %collective-permute-start) | collective-permute-done | bytes 450592 | tf_op jit(solution)/shard_map/ppermute | solution.py:27
  46.1 2.3 %collective-permute-start.10 = (bf16[176,1280]{1,0:T(8,128)(2,1)S(1)}, bf16[176,1280]{1,0:T(8,128)(2,1)S(1)}, u32[]{:S(2)}, u32[]{:S(2)}) collective-permute-start(bf16[176,1280]{1,0:T(8,128)(2,1)S(1)} %get-tuple-element.40), channel_id=1, source_target_pairs={{0,16},{1,17},{2,18},{3,19},{4,20},{5,21},{6,22},{7,23},{8,24},{9,... | collective-permute-start | bytes 1351688 | tf_op jit(solution)/shard_map/ppermute | solution.py:27
  49.6 9.7 %gradient.4 = (f32[160,1280]{1,0:T(8,128)S(1)}, f32[160,1280]{1,0:T(8,128)S(1)}, bf16[160,1280]{1,0:T(8,128)(2,1)S(1)}, bf16[160,1280]{1,0:T(8,128)(2,1)S(1)}) custom-call(s32[10]{0:T(128)S(1)} %copy-done.5, bf16[352,1280]{1,0:T(8,128)(2,1)S(1)} %get-tuple-element.34.refs_0_, bf16[352,1280]{1,0:T(8,128)(2,1)S(1)} %collective-permute-done.4.refs_1_, ...), custom_call_target="tpu_custom_call" | custom-call | flops 1 | bytes 1 | tf_op jit(solution)/shard_map/gradient/pallas_call | solution.py:81
  59.2 1.6 collective-permute-start.7
  60.8 13.9 %collective-permute-done.10.refs_0_ = bf16[176,1280]{1,0:T(8,128)(2,1)S(1)} collective-permute-done((bf16[176,1280]{1,0:T(8,128)(2,1)S(1)}, bf16[176,1280]{1,0:T(8,128)(2,1)S(1)}, u32[]{:S(2)}, u32[]{:S(2)}) %collective-permute-start.10) | collective-permute-done | bytes 450592 | tf_op jit(solution)/shard_map/ppermute | solution.py:27
  76.7 2.8 %collective-permute-start.15 = (bf16[176,1280]{1,0:T(8,128)(2,1)S(1)}, bf16[176,1280]{1,0:T(8,128)(2,1)S(1)}, u32[]{:S(2)}, u32[]{:S(2)}) collective-permute-start(bf16[176,1280]{1,0:T(8,128)(2,1)S(1)} %collective-permute-done.10.refs_0_), channel_id=1, source_target_pairs={{0,8},{1,9},{2,10},{3,11},{4,12},{5,13},{6,14},{7,15},{8,0},{9,1},... | collective-permute-start | bytes 1351688 | tf_op jit(solution)/shard_map/ppermute | solution.py:27
  79.5 1.5 collective-permute-start.5
  81.0 9.9 %gradient.5 = (f32[160,1280]{1,0:T(8,128)S(1)}, f32[160,1280]{1,0:T(8,128)S(1)}, bf16[320,1280]{1,0:T(8,128)(2,1)S(1)}) custom-call(s32[10]{0:T(128)S(1)} %copy-done.5, bf16[352,1280]{1,0:T(8,128)(2,1)S(1)} %collective-permute-done.6.refs_0_, bf16[352,1280]{1,0:T(8,128)(2,1)S(1)} %collective-permute-done.8.refs_1_, bf16[352,1280]{1,0:T(8,128)(2,1)S(1)} %join.5.refs_2_, ...), custom_call_target="tpu_custom_call" | custom-call | flops 1 | bytes 1 | tf_op jit(solution)/shard_map/gradient/pallas_call | solution.py:81
  92.0 1.5 collective-permute-start.13
  95.9 9.7 %gradient.6 = (f32[160,1280]{1,0:T(8,128)S(1)}, f32[160,1280]{1,0:T(8,128)S(1)}, bf16[320,1280]{1,0:T(8,128)(2,1)S(1)}) custom-call(s32[10]{0:T(128)S(1)} %copy-done.5, f32[8,128]{1,0:T(8,128)S(1)} %products.6.refs_0_.refs_8_, bf16[352,1280]{1,0:T(8,128)(2,1)S(1)} %join.6.refs_1_, bf16[352,1280]{1,0:T(8,128)(2,1)S(1)} %collective-permute-done.16.refs_2_, ...), custom_call_target="tpu_custom_call" | custom-call | flops 1 | bytes 1 | tf_op jit(solution)/shard_map/gradient/pallas_call | solution.py:81
  105.7 6.5 %collective-permute-done.13.refs_6_.refs_7_.refs_3_.refs_8_ = bf16[320,1280]{1,0:T(8,128)(2,1)S(1)} collective-permute-done((bf16[320,1280]{1,0:T(8,128)(2,1)S(1)}, bf16[320,1280]{1,0:T(8,128)(2,1)S(1)}, u32[]{:S(2)}, u32[]{:S(2)}) %collective-permute-start.13) | collective-permute-done | bytes 819232 | tf_op jit(solution)/shard_map/ppermute | solution.py:27
  114.5 2.4 %products.7.refs_0_.refs_12_ = f32[8,128]{1,0:T(8,128)S(1)} custom-call(s32[10]{0:T(128)S(1)} %copy-done.5, f32[160,1280]{1,0:T(8,128)S(1)} %get-tuple-element.37.refs_0_.refs_1_, f32[160,1280]{1,0:T(8,128)S(1)} %get-tuple-element.35.refs_1_.refs_0_.refs_2_, bf16[160,1280]{1,0:T(8,128)(2,1)S(1)} %collective-permute-done.7.refs_2_.refs_1_.refs_3_, ...), custom_call_target="tpu_custom_call" | custom-call | flops 1 | bytes 1 | tf_op jit(solution)/shard_map/products/pallas_call | solution.py:81
  116.9 10.0 %gradient.7 = (f32[160,1280]{1,0:T(8,128)S(1)}, f32[160,1280]{1,0:T(8,128)S(1)}, bf16[160,1280]{1,0:T(8,128)(2,1)S(1)}, bf16[160,1280]{1,0:T(8,128)(2,1)S(1)}) custom-call(s32[10]{0:T(128)S(1)} %copy-done.5, f32[8,128]{1,0:T(8,128)S(1)} %products.7.refs_0_.refs_12_, bf16[352,1280]{1,0:T(8,128)(2,1)S(1)} %join.7.refs_1_, ...), custom_call_target="tpu_custom_call" | custom-call | flops 1 | bytes 1 | tf_op jit(solution)/shard_map/gradient/pallas_call | solution.py:81
  128.9 5.7 %collective-permute-done.18.refs_10_.refs_11_.refs_5_.refs_12_ = bf16[320,1280]{1,0:T(8,128)(2,1)S(1)} collective-permute-done((bf16[320,1280]{1,0:T(8,128)(2,1)S(1)}, bf16[320,1280]{1,0:T(8,128)(2,1)S(1)}, u32[]{:S(2)}, u32[]{:S(2)}) %collective-permute-start.18) | collective-permute-done | bytes 819232 | tf_op jit(solution)/shard_map/ppermute | solution.py:27
  134.6 3.4 %products.8.refs_14_ = f32[8,128]{1,0:T(8,128)S(1)} custom-call(s32[10]{0:T(128)S(1)} %copy-done.5, f32[160,1280]{1,0:T(8,128)S(1)} %get-tuple-element.37.refs_0_.refs_1_, f32[160,1280]{1,0:T(8,128)S(1)} %get-tuple-element.35.refs_1_.refs_0_.refs_2_, bf16[160,1280]{1,0:T(8,128)(2,1)S(1)} %collective-permute-done.7.refs_2_.refs_1_.refs_3_, ...), custom_call_target="tpu_custom_call" | custom-call | flops 1 | bytes 1 | tf_op jit(solution)/shard_map/products/pallas_call | solution.py:81
  138.1 2.8 %products.9.refs_8_ = f32[8,128]{1,0:T(8,128)S(1)} custom-call(s32[10]{0:T(128)S(1)} %copy-done.5, f32[160,1280]{1,0:T(8,128)S(1)} %get-tuple-element.37.refs_0_.refs_1_, f32[160,1280]{1,0:T(8,128)S(1)} %get-tuple-element.35.refs_1_.refs_0_.refs_2_, bf16[160,1280]{1,0:T(8,128)(2,1)S(1)} %collective-permute-done.7.refs_2_.refs_1_.refs_3_, ...), custom_call_target="tpu_custom_call" | custom-call | flops 1 | bytes 1 | tf_op jit(solution)/shard_map/products/pallas_call | solution.py:81
  140.9 2.5 %collective-permute-done.24.refs_7_.refs_15_ = bf16[160,1280]{1,0:T(8,128)(2,1)S(1)} collective-permute-done((bf16[160,1280]{1,0:T(8,128)(2,1)S(1)}, bf16[160,1280]{1,0:T(8,128)(2,1)S(1)}, u32[]{:S(2)}, u32[]{:S(2)}) %collective-permute-start.24) | collective-permute-done | bytes 409632 | tf_op jit(solution)/shard_map/ppermute | solution.py:27
  143.4 1.6 products.10.refs_8_
  145.0 6.7 %collective-permute-done.23.refs_7_.refs_16_ = bf16[160,1280]{1,0:T(8,128)(2,1)S(1)} collective-permute-done((bf16[160,1280]{1,0:T(8,128)(2,1)S(1)}, bf16[160,1280]{1,0:T(8,128)(2,1)S(1)}, u32[]{:S(2)}, u32[]{:S(2)}) %collective-permute-start.23) | collective-permute-done | bytes 409632 | tf_op jit(solution)/shard_map/ppermute | solution.py:27
  151.8 1.6 products.11.refs_0_
  155.4 1.8 %collective-permute-done.26.refs_2_ = f32[8,128]{1,0:T(8,128)S(1)} collective-permute-done((f32[8,128]{1,0:T(8,128)S(1)}, f32[8,128]{1,0:T(8,128)S(1)}, u32[]{:S(2)}, u32[]{:S(2)}) %collective-permute-start.26) | collective-permute-done | bytes 4128 | tf_op jit(solution)/shard_map/ppermute | solution.py:27
  158.9 1.8 %collective-permute-start.29 = (f32[8,128]{1,0:T(8,128)S(1)}, f32[8,128]{1,0:T(8,128)S(1)}, u32[]{:S(2)}, u32[]{:S(2)}) collective-permute-start(f32[8,128]{1,0:T(8,128)S(1)} %sum_of.3.refs_0_), channel_id=1, source_target_pairs={{0,16},{1,17},{2,18},{3,19},{4,20},{5,21},{6,22},{7,23},{8,24},{9,... | collective-permute-start | bytes 12296 | tf_op jit(solution)/shard_map/ppermute | solution.py:27
  160.7 2.0 %collective-permute-start.30 = (f32[8,128]{1,0:T(8,128)S(1)}, f32[8,128]{1,0:T(8,128)S(1)}, u32[]{:S(2)}, u32[]{:S(2)}) collective-permute-start(f32[8,128]{1,0:T(8,128)S(1)} %sum_of.3.refs_0_), channel_id=1, source_target_pairs={{0,24},{1,25},{2,26},{3,27},{4,28},{5,29},{6,30},{7,31},{8,16},{9,... | collective-permute-start | bytes 12296 | tf_op jit(solution)/shard_map/ppermute | solution.py:27
  163.4 2.7 %collective-permute-done.30.refs_3_ = f32[8,128]{1,0:T(8,128)S(1)} collective-permute-done((f32[8,128]{1,0:T(8,128)S(1)}, f32[8,128]{1,0:T(8,128)S(1)}, u32[]{:S(2)}, u32[]{:S(2)}) %collective-permute-start.30) | collective-permute-done | bytes 4128 | tf_op jit(solution)/shard_map/ppermute | solution.py:27
  167.8 2.5 %collective-permute-done.31.refs_1_ = f32[8,128]{1,0:T(8,128)S(1)} collective-permute-done((f32[8,128]{1,0:T(8,128)S(1)}, f32[8,128]{1,0:T(8,128)S(1)}, u32[]{:S(2)}, u32[]{:S(2)}) %collective-permute-start.31) | collective-permute-done | bytes 4128 | tf_op jit(solution)/shard_map/ppermute | solution.py:27
  170.8 4.1 %merge.1 = (f32[160,1280]{1,0:T(8,128)}, f32[160,1280]{1,0:T(8,128)}) custom-call(s32[10]{0:T(128)S(1)} %copy-done.5, f32[8,128]{1,0:T(8,128)S(1)} %sum_of.5.refs_0_, f32[160,1280]{1,0:T(8,128)S(1)} %get-tuple-element.37.refs_0_.refs_1_, f32[160,1280]{1,0:T(8,128)S(1)} %get-tuple-element.35.refs_1_.refs_0_.refs_2_, ...), custom_call_target="tpu_custom_call" | custom-call | flops 1 | bytes 1 | tf_op jit(solution)/shard_map/merge/pallas_call | solution.py:81
  (71 shorter events, 23.8 us)
Async XLA Ops:
  12.0 4.4 %collective-permute-start.2 = (f32[352,1280]{1,0:T(8,128)}, f32[352,1280]{1,0:T(8,128)S(1)}, u32[]{:S(2)}, u32[]{:S(2)}) collective-permute-start(f32[352,1280]{1,0:T(8,128)} %get-tuple-element.33), channel_id=1, source_target_pairs={{0,1},{1,0},{2,3},{3,2},{4,5},{5,4},{6,7},{7,6},{8,9},{9,8},{10,11... | collective-permute-start | bytes 5406728 | tf_op jit(solution)/shard_map/ppermute | solution.py:27
  16.6 23.2 %collective-permute-start.3 = (f16[352,1280]{1,0:T(8,128)(2,1)S(1)}, f16[352,1280]{1,0:T(8,128)(2,1)S(1)}, u32[]{:S(2)}, u32[]{:S(2)}) collective-permute-start(f16[352,1280]{1,0:T(8,128)(2,1)S(1)} %get-tuple-element.60), channel_id=1, source_target_pairs={{0,2},{1,3},{2,0},{3,1},{4,6},{5,7},{6,4},{7,5},{8,10},{9,11},{10,... | collective-permute-start | bytes 2703368 | tf_op jit(solution)/shard_map/ppermute | solution.py:27
  19.2 23.1 %collective-permute-start = (bf16[176,1280]{1,0:T(8,128)(2,1)S(1)}, bf16[176,1280]{1,0:T(8,128)(2,1)S(1)}, u32[]{:S(2)}, u32[]{:S(2)}) collective-permute-start(bf16[176,1280]{1,0:T(8,128)(2,1)S(1)} %copy-done.6), channel_id=1, source_target_pairs={{0,16},{1,17},{2,18},{3,19},{4,20},{5,21},{6,22},{7,23},{8,24},{9,... | collective-permute-start | bytes 1351688 | tf_op jit(solution)/shard_map/ppermute | solution.py:27
  21.8 20.7 %collective-permute-start.1 = (bf16[176,1280]{1,0:T(8,128)(2,1)S(1)}, bf16[176,1280]{1,0:T(8,128)(2,1)S(1)}, u32[]{:S(2)}, u32[]{:S(2)}) collective-permute-start(bf16[176,1280]{1,0:T(8,128)(2,1)S(1)} %copy-done.6), channel_id=1, source_target_pairs={{0,8},{1,9},{2,10},{3,11},{4,12},{5,13},{6,14},{7,15},{8,0},{9,1},... | collective-permute-start | bytes 1351688 | tf_op jit(solution)/shard_map/ppermute | solution.py:27
  43.6 6.0 %collective-permute-start.4 = (bf16[352,1280]{1,0:T(8,128)(2,1)S(1)}, bf16[352,1280]{1,0:T(8,128)(2,1)S(1)}, u32[]{:S(2)}, u32[]{:S(2)}) collective-permute-start(bf16[352,1280]{1,0:T(8,128)(2,1)S(1)} %get-tuple-element.34.refs_0_), channel_id=1, source_target_pairs={{0,1},{1,0},{2,3},{3,2},{4,5},{5,4},{6,7},{7,6},{8,9},{9,8},{10,11... | collective-permute-start | bytes 2703368 | tf_op jit(solution)/shard_map/ppermute | solution.py:27
  43.7 32.1 %collective-permute-start.6 = (bf16[352,1280]{1,0:T(8,128)(2,1)S(1)}, bf16[352,1280]{1,0:T(8,128)(2,1)S(1)}, u32[]{:S(2)}, u32[]{:S(2)}) collective-permute-start(bf16[352,1280]{1,0:T(8,128)(2,1)S(1)} %get-tuple-element.34.refs_0_), channel_id=1, source_target_pairs={{0,8},{1,9},{2,10},{3,11},{4,12},{5,13},{6,14},{7,15},{8,0},{9,1},... | collective-permute-start | bytes 2703368 | tf_op jit(solution)/shard_map/ppermute | solution.py:27
  45.2 15.6 %collective-permute-start.11 = (bf16[176,1280]{1,0:T(8,128)(2,1)S(1)}, bf16[176,1280]{1,0:T(8,128)(2,1)S(1)}, u32[]{:S(2)}, u32[]{:S(2)}) collective-permute-start(bf16[176,1280]{1,0:T(8,128)(2,1)S(1)} %collective-permute-done.refs_0_), channel_id=1, source_target_pairs={{0,2},{1,3},{2,0},{3,1},{4,6},{5,7},{6,4},{7,5},{8,10},{9,11},{10,... | collective-permute-start | bytes 1351688 | tf_op jit(solution)/shard_map/ppermute | solution.py:27
  46.1 28.6 %collective-permute-start.10 = (bf16[176,1280]{1,0:T(8,128)(2,1)S(1)}, bf16[176,1280]{1,0:T(8,128)(2,1)S(1)}, u32[]{:S(2)}, u32[]{:S(2)}) collective-permute-start(bf16[176,1280]{1,0:T(8,128)(2,1)S(1)} %get-tuple-element.40), channel_id=1, source_target_pairs={{0,16},{1,17},{2,18},{3,19},{4,20},{5,21},{6,22},{7,23},{8,24},{9,... | collective-permute-start | bytes 1351688 | tf_op jit(solution)/shard_map/ppermute | solution.py:27
  48.5 26.3 %collective-permute-start.9 = (bf16[176,1280]{1,0:T(8,128)(2,1)S(1)}, bf16[176,1280]{1,0:T(8,128)(2,1)S(1)}, u32[]{:S(2)}, u32[]{:S(2)}) collective-permute-start(bf16[176,1280]{1,0:T(8,128)(2,1)S(1)} %collective-permute-done.1.refs_1_.refs_0_), channel_id=1, source_target_pairs={{0,2},{1,3},{2,0},{3,1},{4,6},{5,7},{6,4},{7,5},{8,10},{9,11},{10,... | collective-permute-start | bytes 1351688 | tf_op jit(solution)/shard_map/ppermute | solution.py:27
  59.2 16.5 %collective-permute-start.7 = (bf16[160,1280]{1,0:T(8,128)(2,1)S(1)}, bf16[160,1280]{1,0:T(8,128)(2,1)S(1)}, u32[]{:S(2)}, u32[]{:S(2)}) collective-permute-start(bf16[160,1280]{1,0:T(8,128)(2,1)S(1)} %get-tuple-element.38), channel_id=1, source_target_pairs={{0,4},{1,5},{2,6},{3,7},{4,0},{5,1},{6,2},{7,3},{8,12},{9,13},{10,... | collective-permute-start | bytes 1228808 | tf_op jit(solution)/shard_map/ppermute | solution.py:27
  74.9 6.1 %collective-permute-start.12 = (bf16[352,1280]{1,0:T(8,128)(2,1)S(1)}, bf16[352,1280]{1,0:T(8,128)(2,1)S(1)}, u32[]{:S(2)}, u32[]{:S(2)}) collective-permute-start(bf16[352,1280]{1,0:T(8,128)(2,1)S(1)} %join.5.refs_2_), channel_id=1, source_target_pairs={{0,1},{1,0},{2,3},{3,2},{4,5},{5,4},{6,7},{7,6},{8,9},{9,8},{10,11... | collective-permute-start | bytes 2703368 | tf_op jit(solution)/shard_map/ppermute | solution.py:27
  75.8 5.2 %collective-permute-start.8 = (bf16[352,1280]{1,0:T(8,128)(2,1)S(1)}, bf16[352,1280]{1,0:T(8,128)(2,1)S(1)}, u32[]{:S(2)}, u32[]{:S(2)}) collective-permute-start(bf16[352,1280]{1,0:T(8,128)(2,1)S(1)} %collective-permute-done.6.refs_0_), channel_id=1, source_target_pairs={{0,1},{1,0},{2,3},{3,2},{4,5},{5,4},{6,7},{7,6},{8,9},{9,8},{10,11... | collective-permute-start | bytes 2703368 | tf_op jit(solution)/shard_map/ppermute | solution.py:27
  75.8 15.2 %collective-permute-start.14 = (bf16[176,1280]{1,0:T(8,128)(2,1)S(1)}, bf16[176,1280]{1,0:T(8,128)(2,1)S(1)}, u32[]{:S(2)}, u32[]{:S(2)}) collective-permute-start(bf16[176,1280]{1,0:T(8,128)(2,1)S(1)} %collective-permute-done.10.refs_0_), channel_id=1, source_target_pairs={{0,2},{1,3},{2,0},{3,1},{4,6},{5,7},{6,4},{7,5},{8,10},{9,11},{10,... | collective-permute-start | bytes 1351688 | tf_op jit(solution)/shard_map/ppermute | solution.py:27
  76.7 14.2 %collective-permute-start.15 = (bf16[176,1280]{1,0:T(8,128)(2,1)S(1)}, bf16[176,1280]{1,0:T(8,128)(2,1)S(1)}, u32[]{:S(2)}, u32[]{:S(2)}) collective-permute-start(bf16[176,1280]{1,0:T(8,128)(2,1)S(1)} %collective-permute-done.10.refs_0_), channel_id=1, source_target_pairs={{0,8},{1,9},{2,10},{3,11},{4,12},{5,13},{6,14},{7,15},{8,0},{9,1},... | collective-permute-start | bytes 1351688 | tf_op jit(solution)/shard_map/ppermute | solution.py:27
  79.5 11.5 %collective-permute-start.5 = (bf16[160,1280]{1,0:T(8,128)(2,1)S(1)}, bf16[160,1280]{1,0:T(8,128)(2,1)S(1)}, u32[]{:S(2)}, u32[]{:S(2)}) collective-permute-start(bf16[160,1280]{1,0:T(8,128)(2,1)S(1)} %get-tuple-element.36), channel_id=1, source_target_pairs={{0,4},{1,5},{2,6},{3,7},{4,0},{5,1},{6,2},{7,3},{8,12},{9,13},{10,... | collective-permute-start | bytes 1228808 | tf_op jit(solution)/shard_map/ppermute | solution.py:27
  81.0 14.9 %collective-permute-start.17 = (bf16[352,1280]{1,0:T(8,128)(2,1)S(1)}, bf16[352,1280]{1,0:T(8,128)(2,1)S(1)}, u32[]{:S(2)}, u32[]{:S(2)}) collective-permute-start(bf16[352,1280]{1,0:T(8,128)(2,1)S(1)} %join.4.refs_3_), channel_id=1, source_target_pairs={{0,1},{1,0},{2,3},{3,2},{4,5},{5,4},{6,7},{7,6},{8,9},{9,8},{10,11... | collective-permute-start | bytes 2703368 | tf_op jit(solution)/shard_map/ppermute | solution.py:27
  91.0 4.9 %collective-permute-start.16 = (bf16[352,1280]{1,0:T(8,128)(2,1)S(1)}, bf16[352,1280]{1,0:T(8,128)(2,1)S(1)}, u32[]{:S(2)}, u32[]{:S(2)}) collective-permute-start(bf16[352,1280]{1,0:T(8,128)(2,1)S(1)} %join.6.refs_1_), channel_id=1, source_target_pairs={{0,1},{1,0},{2,3},{3,2},{4,5},{5,4},{6,7},{7,6},{8,9},{9,8},{10,11... | collective-permute-start | bytes 2703368 | tf_op jit(solution)/shard_map/ppermute | solution.py:27
  91.6 22.0 %collective-permute-start.21 = (bf16[352,1280]{1,0:T(8,128)(2,1)S(1)}, bf16[352,1280]{1,0:T(8,128)(2,1)S(1)}, u32[]{:S(2)}, u32[]{:S(2)}) collective-permute-start(bf16[352,1280]{1,0:T(8,128)(2,1)S(1)} %join.4.refs_3_), channel_id=1, source_target_pairs={{0,8},{1,9},{2,10},{3,11},{4,12},{5,13},{6,14},{7,15},{8,0},{9,1},... | collective-permute-start | bytes 2703368 | tf_op jit(solution)/shard_map/ppermute | solution.py:27
  92.0 20.2 %collective-permute-start.13 = (bf16[320,1280]{1,0:T(8,128)(2,1)S(1)}, bf16[320,1280]{1,0:T(8,128)(2,1)S(1)}, u32[]{:S(2)}, u32[]{:S(2)}) collective-permute-start(bf16[320,1280]{1,0:T(8,128)(2,1)S(1)} %get-tuple-element.44), channel_id=1, source_target_pairs={{0,4},{1,5},{2,6},{3,7},{4,0},{5,1},{6,2},{7,3},{8,12},{9,13},{10,... | collective-permute-start | bytes 2457608 | tf_op jit(solution)/shard_map/ppermute | solution.py:27
  93.5 12.2 %collective-permute-start.19 = (bf16[176,1280]{1,0:T(8,128)(2,1)S(1)}, bf16[176,1280]{1,0:T(8,128)(2,1)S(1)}, u32[]{:S(2)}, u32[]{:S(2)}) collective-permute-start(bf16[176,1280]{1,0:T(8,128)(2,1)S(1)} %collective-permute-done.15.refs_0_), channel_id=1, source_target_pairs={{0,2},{1,3},{2,0},{3,1},{4,6},{5,7},{6,4},{7,5},{8,10},{9,11},{10,... | collective-permute-start | bytes 1351688 | tf_op jit(solution)/shard_map/ppermute | solution.py:27
  112.3 4.6 %collective-permute-start.20 = (bf16[352,1280]{1,0:T(8,128)(2,1)S(1)}, bf16[352,1280]{1,0:T(8,128)(2,1)S(1)}, u32[]{:S(2)}, u32[]{:S(2)}) collective-permute-start(bf16[352,1280]{1,0:T(8,128)(2,1)S(1)} %join.7.refs_1_), channel_id=1, source_target_pairs={{0,1},{1,0},{2,3},{3,2},{4,5},{5,4},{6,7},{7,6},{8,9},{9,8},{10,11... | collective-permute-start | bytes 2703368 | tf_op jit(solution)/shard_map/ppermute | solution.py:27
  113.6 3.3 %collective-permute-start.22 = (bf16[352,1280]{1,0:T(8,128)(2,1)S(1)}, bf16[352,1280]{1,0:T(8,128)(2,1)S(1)}, u32[]{:S(2)}, u32[]{:S(2)}) collective-permute-start(bf16[352,1280]{1,0:T(8,128)(2,1)S(1)} %collective-permute-done.21.refs_3_), channel_id=1, source_target_pairs={{0,1},{1,0},{2,3},{3,2},{4,5},{5,4},{6,7},{7,6},{8,9},{9,8},{10,11... | collective-permute-start | bytes 2703368 | tf_op jit(solution)/shard_map/ppermute | solution.py:27
  113.6 21.0 %collective-permute-start.18 = (bf16[320,1280]{1,0:T(8,128)(2,1)S(1)}, bf16[320,1280]{1,0:T(8,128)(2,1)S(1)}, u32[]{:S(2)}, u32[]{:S(2)}) collective-permute-start(bf16[320,1280]{1,0:T(8,128)(2,1)S(1)} %get-tuple-element.50), channel_id=1, source_target_pairs={{0,4},{1,5},{2,6},{3,7},{4,0},{5,1},{6,2},{7,3},{8,12},{9,13},{10,... | collective-permute-start | bytes 2457608 | tf_op jit(solution)/shard_map/ppermute | solution.py:27
  126.9 16.5 %collective-permute-start.24 = (bf16[160,1280]{1,0:T(8,128)(2,1)S(1)}, bf16[160,1280]{1,0:T(8,128)(2,1)S(1)}, u32[]{:S(2)}, u32[]{:S(2)}) collective-permute-start(bf16[160,1280]{1,0:T(8,128)(2,1)S(1)} %get-tuple-element.59), channel_id=1, source_target_pairs={{0,4},{1,5},{2,6},{3,7},{4,0},{5,1},{6,2},{7,3},{8,12},{9,13},{10,... | collective-permute-start | bytes 1228808 | tf_op jit(solution)/shard_map/ppermute | solution.py:27
  128.1 23.7 %collective-permute-start.23 = (bf16[160,1280]{1,0:T(8,128)(2,1)S(1)}, bf16[160,1280]{1,0:T(8,128)(2,1)S(1)}, u32[]{:S(2)}, u32[]{:S(2)}) collective-permute-start(bf16[160,1280]{1,0:T(8,128)(2,1)S(1)} %get-tuple-element.57), channel_id=1, source_target_pairs={{0,4},{1,5},{2,6},{3,7},{4,0},{5,1},{6,2},{7,3},{8,12},{9,13},{10,... | collective-permute-start | bytes 1228808 | tf_op jit(solution)/shard_map/ppermute | solution.py:27
  153.4 1.9 %collective-permute-start.25 = (f32[8,128]{1,0:T(8,128)S(1)}, f32[8,128]{1,0:T(8,128)S(1)}, u32[]{:S(2)}, u32[]{:S(2)}) collective-permute-start(f32[8,128]{1,0:T(8,128)S(1)} %products.11.refs_0_), channel_id=1, source_target_pairs={{0,1},{1,0},{2,3},{3,2},{4,5},{5,4},{6,7},{7,6},{8,9},{9,8},{10,11... | collective-permute-start | bytes 12296 | tf_op jit(solution)/shard_map/ppermute | solution.py:27
  153.5 3.7 %collective-permute-start.26 = (f32[8,128]{1,0:T(8,128)S(1)}, f32[8,128]{1,0:T(8,128)S(1)}, u32[]{:S(2)}, u32[]{:S(2)}) collective-permute-start(f32[8,128]{1,0:T(8,128)S(1)} %products.11.refs_0_), channel_id=1, source_target_pairs={{0,2},{1,3},{2,0},{3,1},{4,6},{5,7},{6,4},{7,5},{8,10},{9,11},{10,... | collective-permute-start | bytes 12296 | tf_op jit(solution)/shard_map/ppermute | solution.py:27
  154.7 3.0 %collective-permute-start.27 = (f32[8,128]{1,0:T(8,128)S(1)}, f32[8,128]{1,0:T(8,128)S(1)}, u32[]{:S(2)}, u32[]{:S(2)}) collective-permute-start(f32[8,128]{1,0:T(8,128)S(1)} %products.11.refs_0_), channel_id=1, source_target_pairs={{0,3},{1,2},{2,1},{3,0},{4,7},{5,6},{6,5},{7,4},{8,11},{9,10},{10,... | collective-permute-start | bytes 12296 | tf_op jit(solution)/shard_map/ppermute | solution.py:27
  158.2 4.5 %collective-permute-start.28 = (f32[8,128]{1,0:T(8,128)S(1)}, f32[8,128]{1,0:T(8,128)S(1)}, u32[]{:S(2)}, u32[]{:S(2)}) collective-permute-start(f32[8,128]{1,0:T(8,128)S(1)} %sum_of.3.refs_0_), channel_id=1, source_target_pairs={{0,8},{1,9},{2,10},{3,11},{4,12},{5,13},{6,14},{7,15},{8,0},{9,1},... | collective-permute-start | bytes 12296 | tf_op jit(solution)/shard_map/ppermute | solution.py:27
  158.9 4.5 %collective-permute-start.29 = (f32[8,128]{1,0:T(8,128)S(1)}, f32[8,128]{1,0:T(8,128)S(1)}, u32[]{:S(2)}, u32[]{:S(2)}) collective-permute-start(f32[8,128]{1,0:T(8,128)S(1)} %sum_of.3.refs_0_), channel_id=1, source_target_pairs={{0,16},{1,17},{2,18},{3,19},{4,20},{5,21},{6,22},{7,23},{8,24},{9,... | collective-permute-start | bytes 12296 | tf_op jit(solution)/shard_map/ppermute | solution.py:27
  160.7 5.4 %collective-permute-start.30 = (f32[8,128]{1,0:T(8,128)S(1)}, f32[8,128]{1,0:T(8,128)S(1)}, u32[]{:S(2)}, u32[]{:S(2)}) collective-permute-start(f32[8,128]{1,0:T(8,128)S(1)} %sum_of.3.refs_0_), channel_id=1, source_target_pairs={{0,24},{1,25},{2,26},{3,27},{4,28},{5,29},{6,30},{7,31},{8,16},{9,... | collective-permute-start | bytes 12296 | tf_op jit(solution)/shard_map/ppermute | solution.py:27
  166.6 3.7 %collective-permute-start.31 = (f32[8,128]{1,0:T(8,128)S(1)}, f32[8,128]{1,0:T(8,128)S(1)}, u32[]{:S(2)}, u32[]{:S(2)}) collective-permute-start(f32[8,128]{1,0:T(8,128)S(1)} %sum_of.4.refs_0_), channel_id=1, source_target_pairs={{0,4},{1,5},{2,6},{3,7},{4,0},{5,1},{6,2},{7,3},{8,12},{9,13},{10,... | collective-permute-start | bytes 12296 | tf_op jit(solution)/shard_map/ppermute | solution.py:27
  (7 other events, 66.3 us)

commit v18 on v13

--- a/solution.py
+++ b/solution.py
@@ -107,12 +107,8 @@
 CUBE = 0.044715
 
 
-def forward_kernel(
-    steps, place_ref, rows_ref, w_in_ref, w_out_ref, out_ref, near_ref, part_ref, hidden
-):
+def forward_kernel(steps, place_ref, rows_ref, w_in_ref, w_out_ref, out_ref, part_ref, hidden):
     step = pl.program_id(0)
-    half = out_ref.shape[0]
-    far = pl.ds(row_start(place_ref, out_ref, FAR), half)
     tile = w_in_ref.shape[1]
 
     for n in range(steps):
@@ -125,19 +121,15 @@
 
     @pl.when(step == 0)
     def _():
-        part_ref[...] = rows_ref[pl.ds(row_start(place_ref, part_ref, PART), part_ref.shape[0]), :]
-
-    @pl.when(step == steps)
-    def _():
-        near_ref[...] = hidden[pl.ds(row_start(place_ref, out_ref, NEAR), half), :]
+        part_ref[...] = rows_ref[pl.ds(row_start(place_ref, part_ref, PIECE), part_ref.shape[0]), :]
 
     @pl.when(step >= steps)
     def _():
-        out_ref[...] = jnp.dot(hidden[far, :], w_out_ref[...], preferred_element_type=jnp.float32)
-
-
-def forward(place, part_rows, inputs, w_in, w_out):
-    rows = inputs.shape[0]
+        out_ref[...] = jnp.dot(hidden[...], w_out_ref[...], preferred_element_type=jnp.float32)
+
+
+def forward(place, which, part_rows, inputs, w_in, w_out):
+    rows = inputs.shape[0] // 2
     depth, width = w_in.shape
     tile, out_tile = tile_of(width, 640), tile_of(depth, 640)
     steps = width // tile
@@ -147,43 +139,22 @@
         "forward",
         (place, inputs, w_in, w_out),
         [
-            jax.ShapeDtypeStruct((rows // 2, depth), jnp.float32),
-            jax.ShapeDtypeStruct((rows // 2, width), jnp.bfloat16),
+            jax.ShapeDtypeStruct((rows, depth), jnp.float32),
             jax.ShapeDtypeStruct((part_rows, depth), jnp.bfloat16),
         ],
         vmem=vmem_most,
         grid=(steps + depth // out_tile,),
         in_specs=[
-            pl.BlockSpec((rows, depth), whole),
+            pl.BlockSpec((rows, depth), lambda n, s: (s[which], 0)),
             pl.BlockSpec((depth, tile), lambda n, s: (0, jnp.minimum(n, steps - 1))),
             pl.BlockSpec((width, out_tile), lambda n, s: (0, last(n))),
         ],
         out_specs=[
-            pl.BlockSpec((rows // 2, out_tile), lambda n, s: (0, last(n))),
-            pl.BlockSpec((rows // 2, width), whole),
+            pl.BlockSpec((rows, out_tile), lambda n, s: (0, last(n))),
             pl.BlockSpec((part_rows, depth), whole),
         ],
         scratch_shapes=[pltpu.VMEM((rows, width), jnp.bfloat16)],
     )
-
-
-def product_kernel(place_ref, left_ref, right_ref, out_ref):
-    out_ref[...] = jnp.dot(left_ref[...], right_ref[...], preferred_element_type=jnp.float32)
-
-
-def product(place, left, right):
-    rows, depth = left.shape
-    width = right.shape[1]
-    tile = tile_of(width, 640)
-    return call(
-        product_kernel,
-        "product",
-        (place, left, right),
-        [jax.ShapeDtypeStruct((rows, width), jnp.float32)],
-        grid=(width // tile,),
-        in_specs=[pl.BlockSpec((rows, depth), whole), pl.BlockSpec((depth, tile), column)],
-        out_specs=[pl.BlockSpec((rows, tile), column)],
-    )[0]
 
 
 def join_kernel(place_ref, own_ref, got_ref, out_ref):
@@ -412,14 +383,14 @@
     )[0]
 
 
-def merge_kernel(labels, place_ref, totals_ref, *refs):
+def merge_kernel(labels, place_ref, totals_ref, got_ref, *refs):
     refs, (first_ref, second_ref, weights_ref) = refs[:-3], refs[-3:]
 
     @pl.when(pl.program_id(0) == 0)
     def _():
         def entry(i, j):
             i, j = (jnp.bitwise_xor(place_ref[MEMBER], k) for k in (i, j))
-            return totals_ref[i, j]
+            return totals_ref[i, j] + got_ref[i, j]
 
         for n, weight in enumerate(tree_weights(len(labels), entry)):
             weights_ref[n] = weight
@@ -433,7 +404,7 @@
     second_ref[...] = second
 
 
-def merge(place, totals, slots, labels):
+def merge(place, totals, got, slots, labels):
     own, width = slots[0][0].shape
     block = max(b for b in range(16, min(own, 32) + 1, 16) if own % b == 0)
     spec = pl.BlockSpec((block, width), lambda n, s: (n, 0))
@@ -442,11 +413,11 @@
     return call(
         functools.partial(merge_kernel, tuple(labels)),
         "merge",
-        (place, totals, *arrays),
+        (place, totals, got, *arrays),
         [shape, shape],
         vmem=16 * 2**20,
         grid=(own // block,),
-        in_specs=[pl.BlockSpec(memory_space=pltpu.SMEM)] + [spec] * len(arrays),
+        in_specs=[pl.BlockSpec(memory_space=pltpu.SMEM)] * 2 + [spec] * len(arrays),
         out_specs=[spec, spec],
         scratch_shapes=[pltpu.SMEM((len(slots),), jnp.float32)],
     )
@@ -491,11 +462,12 @@
         ]
     ).astype(jnp.int32)
 
-    send, hidden_near, own_part = forward(place, part_rows, inputs, w_in, w_out)
+    send, _ = forward(place, FAR, part_rows, inputs, w_in, w_out)
     got = from_mask(send, 0, 1)
+    summed, own_part = forward(place, NEAR, part_rows, inputs, w_in, w_out)
     inputs_of = {bit: from_mask(own_part, bit * others, 0) for bit in bits}
 
-    summed = product(place, hidden_near, w_out) + got
+    summed = summed + got
     most = 24.0 * 0.15625 * 0.078125 * inputs.shape[1] * w_in.shape[1] * shards
     scale = 2.0 ** math.ceil(math.log2(most / 65504.0))
     sums = [summed]
@@ -576,10 +548,9 @@
 
     rounds = [[(0, mask) for mask in range(1, shards)]]
     rounds.append([(m * others, 0) for m in range(2, members, 2)])
-    rounds.append([(others, 0)])
     for partners in rounds:
         totals = sum_of(place, [totals] + [from_mask(totals, *mask) for mask in partners])
-    pieces = merge(place, totals, slots, labels)
+    pieces = merge(place, totals, from_mask(totals, others, 0), slots, labels)
 
     for section in range(gathered, levels):
         upper_flag = position >> levels - 1 - section & 1

time: 175 us -> 178 us (1.017)
  Pallas kernels: 73.2 us -> 75.8 us
    pallas_call x21 -> x20, Pallas kernels: 73.2 us -> 75.8 us  [call(): pl.pallas_call(body, grid_spec=pltpu.PrefetchScalarGridSpec(num_scalar_pr...]
  transfers between devices with their start and end apart: 34 -> 34, of which waited for: 15 -> 15; matrix products, arithmetic and copies ran while one was open for 0% -> 0% of each run, Pallas kernels for 31% -> 33%
where the time goes in v18:
time: 178 us
  Pallas kernels  75.8 us (43%)
  waiting for transfers between devices  62.7 us (35%)
  starting transfers between devices  35.9 us (20%)
  other arithmetic  2.03 us (1%)
    pallas_call x20, Pallas kernels, call(): pl.pallas_call(body, grid_spec=pltpu.PrefetchScalarGridSpec(num_scalar_pr...  75.8 us
    ppermute x34, waiting for transfers between devices, from_mask(): return lax.ppermute(value, ('dp', 'tensor'), pairs)  62.7 us
    ppermute x34, starting transfers between devices, from_mask(): return lax.ppermute(value, ('dp', 'tensor'), pairs)  35.9 us
  transfers between devices with their start and end apart: 34, of which 15 were waited for; matrix products, arithmetic and copies ran while one was open for 0% of the time, Pallas kernels for 33%

profile of v18, /device:TPU:0, one launch (start us, length us, event | category | flops | bytes accessed | tf_op | source)
XLA Modules:
  0.0 178.1 jit_solution(16192248376268936047)
XLA Ops:
  1.4 8.2 %forward.3 = (f32[352,1280]{1,0:T(8,128)}, bf16[176,1280]{1,0:T(8,128)(2,1)}) custom-call(s32[8]{0:T(128)} %stack.35.place_ref, bf16[704,1280]{1,0:T(8,128)(2,1)} %refs_2_.5, bf16[1280,1280]{1,0:T(8,128)(2,1)} %refs_5_.5, bf16[1280,1280]{1,0:T(8,128)(2,1)} %refs_6_.3), custom_call_target="tpu_custom_call" | custom-call | flops 1 | bytes 1 | tf_op jit(solution)/shard_map/forward/pallas_call | solution.py:81
  10.0 8.2 %forward.2 = (f32[352,1280]{1,0:T(8,128)}, bf16[176,1280]{1,0:T(8,128)(2,1)}) custom-call(s32[8]{0:T(128)} %stack.35.place_ref, bf16[704,1280]{1,0:T(8,128)(2,1)} %refs_2_.5, bf16[1280,1280]{1,0:T(8,128)(2,1)} %refs_5_.5, bf16[1280,1280]{1,0:T(8,128)(2,1)} %refs_6_.3), custom_call_target="tpu_custom_call" | custom-call | flops 1 | bytes 1 | tf_op jit(solution)/shard_map/forward/pallas_call | solution.py:81
  18.3 1.9 %multiply_convert_fusion = (f16[352,1280]{1,0:T(8,128)(2,1)S(1)}, f32[352,1280]{1,0:T(8,128)S(1)}) fusion(f32[352,1280]{1,0:T(8,128)} %get-tuple-element.34, f32[352,1280]{1,0:T(8,128)S(1)} %collective-permute-done.2), kind=kLoop, calls=%fused_computation.1 | loop fusion | flops 1351680 | bytes 6307840 | tf_op jit(solution)/shard_map/convert_element_type | solution.py:475
  20.2 2.6 %collective-permute-start.3 = (f16[352,1280]{1,0:T(8,128)(2,1)S(1)}, f16[352,1280]{1,0:T(8,128)(2,1)S(1)}, u32[]{:S(2)}, u32[]{:S(2)}) collective-permute-start(f16[352,1280]{1,0:T(8,128)(2,1)S(1)} %get-tuple-element.64), channel_id=1, source_target_pairs={{0,2},{1,3},{2,0},{3,1},{4,6},{5,7},{6,4},{7,5},{8,10},{9,11},{10,... | collective-permute-start | bytes 2703368 | tf_op jit(solution)/shard_map/ppermute | solution.py:27
  22.7 2.6 %collective-permute-start = (bf16[176,1280]{1,0:T(8,128)(2,1)S(1)}, bf16[176,1280]{1,0:T(8,128)(2,1)S(1)}, u32[]{:S(2)}, u32[]{:S(2)}) collective-permute-start(bf16[176,1280]{1,0:T(8,128)(2,1)S(1)} %copy-done.5), channel_id=1, source_target_pairs={{0,16},{1,17},{2,18},{3,19},{4,20},{5,21},{6,22},{7,23},{8,24},{9,... | collective-permute-start | bytes 1351688 | tf_op jit(solution)/shard_map/ppermute | solution.py:27
  25.3 1.6 collective-permute-start.1
  26.9 16.5 %collective-permute-done.3 = f16[352,1280]{1,0:T(8,128)(2,1)S(1)} collective-permute-done((f16[352,1280]{1,0:T(8,128)(2,1)S(1)}, f16[352,1280]{1,0:T(8,128)(2,1)S(1)}, u32[]{:S(2)}, u32[]{:S(2)}) %collective-permute-start.3) | collective-permute-done | bytes 901152 | tf_op jit(solution)/shard_map/ppermute | solution.py:27
  43.6 2.3 %collective-permute-done.refs_0_ = bf16[176,1280]{1,0:T(8,128)(2,1)S(1)} collective-permute-done((bf16[176,1280]{1,0:T(8,128)(2,1)S(1)}, bf16[176,1280]{1,0:T(8,128)(2,1)S(1)}, u32[]{:S(2)}, u32[]{:S(2)}) %collective-permute-start) | collective-permute-done | bytes 450592 | tf_op jit(solution)/shard_map/ppermute | solution.py:27
  49.3 2.3 %collective-permute-start.10 = (bf16[176,1280]{1,0:T(8,128)(2,1)S(1)}, bf16[176,1280]{1,0:T(8,128)(2,1)S(1)}, u32[]{:S(2)}, u32[]{:S(2)}) collective-permute-start(bf16[176,1280]{1,0:T(8,128)(2,1)S(1)} %get-tuple-element.41), channel_id=1, source_target_pairs={{0,16},{1,17},{2,18},{3,19},{4,20},{5,21},{6,22},{7,23},{8,24},{9,... | collective-permute-start | bytes 1351688 | tf_op jit(solution)/shard_map/ppermute | solution.py:27
  53.1 9.7 %gradient.4 = (f32[160,1280]{1,0:T(8,128)S(1)}, f32[160,1280]{1,0:T(8,128)S(1)}, bf16[160,1280]{1,0:T(8,128)(2,1)S(1)}, bf16[160,1280]{1,0:T(8,128)(2,1)S(1)}) custom-call(s32[8]{0:T(128)S(1)} %copy-done.4, bf16[352,1280]{1,0:T(8,128)(2,1)S(1)} %get-tuple-element.36.refs_0_, bf16[352,1280]{1,0:T(8,128)(2,1)S(1)} %collective-permute-done.4.refs_1_, ...), custom_call_target="tpu_custom_call" | custom-call | flops 1 | bytes 1 | tf_op jit(solution)/shard_map/gradient/pallas_call | solution.py:81
  62.8 1.6 collective-permute-start.7
  64.4 13.9 %collective-permute-done.10.refs_0_ = bf16[176,1280]{1,0:T(8,128)(2,1)S(1)} collective-permute-done((bf16[176,1280]{1,0:T(8,128)(2,1)S(1)}, bf16[176,1280]{1,0:T(8,128)(2,1)S(1)}, u32[]{:S(2)}, u32[]{:S(2)}) %collective-permute-start.10) | collective-permute-done | bytes 450592 | tf_op jit(solution)/shard_map/ppermute | solution.py:27
  79.8 2.8 %collective-permute-start.15 = (bf16[176,1280]{1,0:T(8,128)(2,1)S(1)}, bf16[176,1280]{1,0:T(8,128)(2,1)S(1)}, u32[]{:S(2)}, u32[]{:S(2)}) collective-permute-start(bf16[176,1280]{1,0:T(8,128)(2,1)S(1)} %collective-permute-done.10.refs_0_), channel_id=1, source_target_pairs={{0,8},{1,9},{2,10},{3,11},{4,12},{5,13},{6,14},{7,15},{8,0},{9,1},... | collective-permute-start | bytes 1351688 | tf_op jit(solution)/shard_map/ppermute | solution.py:27
  84.1 9.9 %gradient.5 = (f32[160,1280]{1,0:T(8,128)S(1)}, f32[160,1280]{1,0:T(8,128)S(1)}, bf16[160,1280]{1,0:T(8,128)(2,1)S(1)}, bf16[160,1280]{1,0:T(8,128)(2,1)S(1)}) custom-call(s32[8]{0:T(128)S(1)} %copy-done.4, bf16[352,1280]{1,0:T(8,128)(2,1)S(1)} %collective-permute-done.6.refs_0_, bf16[352,1280]{1,0:T(8,128)(2,1)S(1)} %collective-permute-done.8.refs_1_, ...), custom_call_target="tpu_custom_call" | custom-call | flops 1 | bytes 1 | tf_op jit(solution)/shard_map/gradient/pallas_call | solution.py:81
  99.9 9.7 %gradient.6 = (f32[160,1280]{1,0:T(8,128)S(1)}, f32[160,1280]{1,0:T(8,128)S(1)}, bf16[160,1280]{1,0:T(8,128)(2,1)S(1)}, bf16[160,1280]{1,0:T(8,128)(2,1)S(1)}) custom-call(s32[8]{0:T(128)S(1)} %copy-done.4, f32[8,128]{1,0:T(8,128)S(1)} %products.6.refs_0_.refs_8_, bf16[352,1280]{1,0:T(8,128)(2,1)S(1)} %join.6.refs_1_, ...), custom_call_target="tpu_custom_call" | custom-call | flops 1 | bytes 1 | tf_op jit(solution)/shard_map/gradient/pallas_call | solution.py:81
  109.6 6.8 %collective-permute-done.19.refs_6_.refs_3_.refs_8_ = bf16[160,1280]{1,0:T(8,128)(2,1)S(1)} collective-permute-done((bf16[160,1280]{1,0:T(8,128)(2,1)S(1)}, bf16[160,1280]{1,0:T(8,128)(2,1)S(1)}, u32[]{:S(2)}, u32[]{:S(2)}) %collective-permute-start.19) | collective-permute-done | bytes 409632 | tf_op jit(solution)/shard_map/ppermute | solution.py:27
  119.1 2.4 %products.7.refs_0_.refs_12_ = f32[8,128]{1,0:T(8,128)S(1)} custom-call(s32[8]{0:T(128)S(1)} %copy-done.4, f32[160,1280]{1,0:T(8,128)S(1)} %get-tuple-element.46.refs_0_.refs_2_, f32[160,1280]{1,0:T(8,128)S(1)} %get-tuple-element.37.refs_1_.refs_0_.refs_3_, bf16[160,1280]{1,0:T(8,128)(2,1)S(1)} %collective-permute-done.7.refs_2_.refs_1_.refs_4_, ...), custom_call_target="tpu_custom_call" | custom-call | flops 1 | bytes 1 | tf_op jit(solution)/shard_map/products/pallas_call | solution.py:81
  121.5 10.0 %gradient.7 = (f32[160,1280]{1,0:T(8,128)S(1)}, f32[160,1280]{1,0:T(8,128)S(1)}, bf16[160,1280]{1,0:T(8,128)(2,1)S(1)}, bf16[160,1280]{1,0:T(8,128)(2,1)S(1)}) custom-call(s32[8]{0:T(128)S(1)} %copy-done.4, f32[8,128]{1,0:T(8,128)S(1)} %products.7.refs_0_.refs_12_, bf16[352,1280]{1,0:T(8,128)(2,1)S(1)} %join.7.refs_1_, ...), custom_call_target="tpu_custom_call" | custom-call | flops 1 | bytes 1 | tf_op jit(solution)/shard_map/gradient/pallas_call | solution.py:81
  131.5 1.6 collective-permute-start.26
  133.6 4.6 %collective-permute-done.18.refs_11_.refs_5_.refs_13_ = bf16[160,1280]{1,0:T(8,128)(2,1)S(1)} collective-permute-done((bf16[160,1280]{1,0:T(8,128)(2,1)S(1)}, bf16[160,1280]{1,0:T(8,128)(2,1)S(1)}, u32[]{:S(2)}, u32[]{:S(2)}) %collective-permute-start.18) | collective-permute-done | bytes 409632 | tf_op jit(solution)/shard_map/ppermute | solution.py:27
  138.1 3.4 %products.8.refs_14_ = f32[8,128]{1,0:T(8,128)S(1)} custom-call(s32[8]{0:T(128)S(1)} %copy-done.4, f32[160,1280]{1,0:T(8,128)S(1)} %get-tuple-element.46.refs_0_.refs_2_, f32[160,1280]{1,0:T(8,128)S(1)} %get-tuple-element.37.refs_1_.refs_0_.refs_3_, bf16[160,1280]{1,0:T(8,128)(2,1)S(1)} %collective-permute-done.7.refs_2_.refs_1_.refs_4_, ...), custom_call_target="tpu_custom_call" | custom-call | flops 1 | bytes 1 | tf_op jit(solution)/shard_map/products/pallas_call | solution.py:81
  141.6 2.8 %products.9.refs_8_ = f32[8,128]{1,0:T(8,128)S(1)} custom-call(s32[8]{0:T(128)S(1)} %copy-done.4, f32[160,1280]{1,0:T(8,128)S(1)} %get-tuple-element.46.refs_0_.refs_2_, f32[160,1280]{1,0:T(8,128)S(1)} %get-tuple-element.37.refs_1_.refs_0_.refs_3_, bf16[160,1280]{1,0:T(8,128)(2,1)S(1)} %collective-permute-done.7.refs_2_.refs_1_.refs_4_, ...), custom_call_target="tpu_custom_call" | custom-call | flops 1 | bytes 1 | tf_op jit(solution)/shard_map/products/pallas_call | solution.py:81
  144.4 2.5 %collective-permute-done.26.refs_7_.refs_16_ = bf16[160,1280]{1,0:T(8,128)(2,1)S(1)} collective-permute-done((bf16[160,1280]{1,0:T(8,128)(2,1)S(1)}, bf16[160,1280]{1,0:T(8,128)(2,1)S(1)}, u32[]{:S(2)}, u32[]{:S(2)}) %collective-permute-start.26) | collective-permute-done | bytes 409632 | tf_op jit(solution)/shard_map/ppermute | solution.py:27
  146.9 1.6 products.10.refs_8_
  148.6 6.4 %collective-permute-done.24.refs_7_.refs_17_ = bf16[160,1280]{1,0:T(8,128)(2,1)S(1)} collective-permute-done((bf16[160,1280]{1,0:T(8,128)(2,1)S(1)}, bf16[160,1280]{1,0:T(8,128)(2,1)S(1)}, u32[]{:S(2)}, u32[]{:S(2)}) %collective-permute-start.24) | collective-permute-done | bytes 409632 | tf_op jit(solution)/shard_map/ppermute | solution.py:27
  154.9 1.6 products.11.refs_0_
  158.5 1.8 %collective-permute-done.28.refs_2_ = f32[8,128]{1,0:T(8,128)S(1)} collective-permute-done((f32[8,128]{1,0:T(8,128)S(1)}, f32[8,128]{1,0:T(8,128)S(1)}, u32[]{:S(2)}, u32[]{:S(2)}) %collective-permute-start.28) | collective-permute-done | bytes 4128 | tf_op jit(solution)/shard_map/ppermute | solution.py:27
  162.4 1.8 %collective-permute-start.31 = (f32[8,128]{1,0:T(8,128)S(1)}, f32[8,128]{1,0:T(8,128)S(1)}, u32[]{:S(2)}, u32[]{:S(2)}) collective-permute-start(f32[8,128]{1,0:T(8,128)S(1)} %sum_of.2.refs_0_), channel_id=1, source_target_pairs={{0,16},{1,17},{2,18},{3,19},{4,20},{5,21},{6,22},{7,23},{8,24},{9,... | collective-permute-start | bytes 12296 | tf_op jit(solution)/shard_map/ppermute | solution.py:27
  164.2 2.0 %collective-permute-start.32 = (f32[8,128]{1,0:T(8,128)S(1)}, f32[8,128]{1,0:T(8,128)S(1)}, u32[]{:S(2)}, u32[]{:S(2)}) collective-permute-start(f32[8,128]{1,0:T(8,128)S(1)} %sum_of.2.refs_0_), channel_id=1, source_target_pairs={{0,24},{1,25},{2,26},{3,27},{4,28},{5,29},{6,30},{7,31},{8,16},{9,... | collective-permute-start | bytes 12296 | tf_op jit(solution)/shard_map/ppermute | solution.py:27
  166.9 2.7 %collective-permute-done.32.refs_3_ = f32[8,128]{1,0:T(8,128)S(1)} collective-permute-done((f32[8,128]{1,0:T(8,128)S(1)}, f32[8,128]{1,0:T(8,128)S(1)}, u32[]{:S(2)}, u32[]{:S(2)}) %collective-permute-start.32) | collective-permute-done | bytes 4128 | tf_op jit(solution)/shard_map/ppermute | solution.py:27
  171.4 2.5 %collective-permute-done.33.refs_1_ = f32[8,128]{1,0:T(8,128)S(1)} collective-permute-done((f32[8,128]{1,0:T(8,128)S(1)}, f32[8,128]{1,0:T(8,128)S(1)}, u32[]{:S(2)}, u32[]{:S(2)}) %collective-permute-start.33) | collective-permute-done | bytes 4128 | tf_op jit(solution)/shard_map/ppermute | solution.py:27
  173.9 4.2 %merge.1 = (f32[160,1280]{1,0:T(8,128)}, f32[160,1280]{1,0:T(8,128)}) custom-call(s32[8]{0:T(128)S(1)} %copy-done.4, f32[8,128]{1,0:T(8,128)S(1)} %sum_of.3.refs_0_, f32[8,128]{1,0:T(8,128)S(1)} %collective-permute-done.33.refs_1_, f32[160,1280]{1,0:T(8,128)S(1)} %get-tuple-element.46.refs_0_.refs_2_, ...), custom_call_target="tpu_custom_call" | custom-call | flops 1 | bytes 1 | tf_op jit(solution)/shard_map/merge/pallas_call | solution.py:81
  (72 shorter events, 24.5 us)
Async XLA Ops:
  9.6 8.7 %collective-permute-start.2 = (f32[352,1280]{1,0:T(8,128)}, f32[352,1280]{1,0:T(8,128)S(1)}, u32[]{:S(2)}, u32[]{:S(2)}) collective-permute-start(f32[352,1280]{1,0:T(8,128)} %get-tuple-element.35), channel_id=1, source_target_pairs={{0,1},{1,0},{2,3},{3,2},{4,5},{5,4},{6,7},{7,6},{8,9},{9,8},{10,11... | collective-permute-start | bytes 5406728 | tf_op jit(solution)/shard_map/ppermute | solution.py:27
  20.2 23.2 %collective-permute-start.3 = (f16[352,1280]{1,0:T(8,128)(2,1)S(1)}, f16[352,1280]{1,0:T(8,128)(2,1)S(1)}, u32[]{:S(2)}, u32[]{:S(2)}) collective-permute-start(f16[352,1280]{1,0:T(8,128)(2,1)S(1)} %get-tuple-element.64), channel_id=1, source_target_pairs={{0,2},{1,3},{2,0},{3,1},{4,6},{5,7},{6,4},{7,5},{8,10},{9,11},{10,... | collective-permute-start | bytes 2703368 | tf_op jit(solution)/shard_map/ppermute | solution.py:27
  22.7 23.1 %collective-permute-start = (bf16[176,1280]{1,0:T(8,128)(2,1)S(1)}, bf16[176,1280]{1,0:T(8,128)(2,1)S(1)}, u32[]{:S(2)}, u32[]{:S(2)}) collective-permute-start(bf16[176,1280]{1,0:T(8,128)(2,1)S(1)} %copy-done.5), channel_id=1, source_target_pairs={{0,16},{1,17},{2,18},{3,19},{4,20},{5,21},{6,22},{7,23},{8,24},{9,... | collective-permute-start | bytes 1351688 | tf_op jit(solution)/shard_map/ppermute | solution.py:27
  25.3 20.7 %collective-permute-start.1 = (bf16[176,1280]{1,0:T(8,128)(2,1)S(1)}, bf16[176,1280]{1,0:T(8,128)(2,1)S(1)}, u32[]{:S(2)}, u32[]{:S(2)}) collective-permute-start(bf16[176,1280]{1,0:T(8,128)(2,1)S(1)} %copy-done.5), channel_id=1, source_target_pairs={{0,8},{1,9},{2,10},{3,11},{4,12},{5,13},{6,14},{7,15},{8,0},{9,1},... | collective-permute-start | bytes 1351688 | tf_op jit(solution)/shard_map/ppermute | solution.py:27
  47.2 6.0 %collective-permute-start.4 = (bf16[352,1280]{1,0:T(8,128)(2,1)S(1)}, bf16[352,1280]{1,0:T(8,128)(2,1)S(1)}, u32[]{:S(2)}, u32[]{:S(2)}) collective-permute-start(bf16[352,1280]{1,0:T(8,128)(2,1)S(1)} %get-tuple-element.36.refs_0_), channel_id=1, source_target_pairs={{0,1},{1,0},{2,3},{3,2},{4,5},{5,4},{6,7},{7,6},{8,9},{9,8},{10,11... | collective-permute-start | bytes 2703368 | tf_op jit(solution)/shard_map/ppermute | solution.py:27
  47.2 32.1 %collective-permute-start.6 = (bf16[352,1280]{1,0:T(8,128)(2,1)S(1)}, bf16[352,1280]{1,0:T(8,128)(2,1)S(1)}, u32[]{:S(2)}, u32[]{:S(2)}) collective-permute-start(bf16[352,1280]{1,0:T(8,128)(2,1)S(1)} %get-tuple-element.36.refs_0_), channel_id=1, source_target_pairs={{0,8},{1,9},{2,10},{3,11},{4,12},{5,13},{6,14},{7,15},{8,0},{9,1},... | collective-permute-start | bytes 2703368 | tf_op jit(solution)/shard_map/ppermute | solution.py:27
  48.7 15.7 %collective-permute-start.11 = (bf16[176,1280]{1,0:T(8,128)(2,1)S(1)}, bf16[176,1280]{1,0:T(8,128)(2,1)S(1)}, u32[]{:S(2)}, u32[]{:S(2)}) collective-permute-start(bf16[176,1280]{1,0:T(8,128)(2,1)S(1)} %collective-permute-done.refs_0_), channel_id=1, source_target_pairs={{0,2},{1,3},{2,0},{3,1},{4,6},{5,7},{6,4},{7,5},{8,10},{9,11},{10,... | collective-permute-start | bytes 1351688 | tf_op jit(solution)/shard_map/ppermute | solution.py:27
  49.3 29.0 %collective-permute-start.10 = (bf16[176,1280]{1,0:T(8,128)(2,1)S(1)}, bf16[176,1280]{1,0:T(8,128)(2,1)S(1)}, u32[]{:S(2)}, u32[]{:S(2)}) collective-permute-start(bf16[176,1280]{1,0:T(8,128)(2,1)S(1)} %get-tuple-element.41), channel_id=1, source_target_pairs={{0,16},{1,17},{2,18},{3,19},{4,20},{5,21},{6,22},{7,23},{8,24},{9,... | collective-permute-start | bytes 1351688 | tf_op jit(solution)/shard_map/ppermute | solution.py:27
  51.6 26.7 %collective-permute-start.9 = (bf16[176,1280]{1,0:T(8,128)(2,1)S(1)}, bf16[176,1280]{1,0:T(8,128)(2,1)S(1)}, u32[]{:S(2)}, u32[]{:S(2)}) collective-permute-start(bf16[176,1280]{1,0:T(8,128)(2,1)S(1)} %collective-permute-done.1.refs_1_.refs_0_), channel_id=1, source_target_pairs={{0,2},{1,3},{2,0},{3,1},{4,6},{5,7},{6,4},{7,5},{8,10},{9,11},{10,... | collective-permute-start | bytes 1351688 | tf_op jit(solution)/shard_map/ppermute | solution.py:27
  62.8 16.5 %collective-permute-start.7 = (bf16[160,1280]{1,0:T(8,128)(2,1)S(1)}, bf16[160,1280]{1,0:T(8,128)(2,1)S(1)}, u32[]{:S(2)}, u32[]{:S(2)}) collective-permute-start(bf16[160,1280]{1,0:T(8,128)(2,1)S(1)} %get-tuple-element.39), channel_id=1, source_target_pairs={{0,4},{1,5},{2,6},{3,7},{4,0},{5,1},{6,2},{7,3},{8,12},{9,13},{10,... | collective-permute-start | bytes 1228808 | tf_op jit(solution)/shard_map/ppermute | solution.py:27
  78.4 5.7 %collective-permute-start.12 = (bf16[352,1280]{1,0:T(8,128)(2,1)S(1)}, bf16[352,1280]{1,0:T(8,128)(2,1)S(1)}, u32[]{:S(2)}, u32[]{:S(2)}) collective-permute-start(bf16[352,1280]{1,0:T(8,128)(2,1)S(1)} %join.5.refs_2_), channel_id=1, source_target_pairs={{0,1},{1,0},{2,3},{3,2},{4,5},{5,4},{6,7},{7,6},{8,9},{9,8},{10,11... | collective-permute-start | bytes 2703368 | tf_op jit(solution)/shard_map/ppermute | solution.py:27
  79.3 4.8 %collective-permute-start.8 = (bf16[352,1280]{1,0:T(8,128)(2,1)S(1)}, bf16[352,1280]{1,0:T(8,128)(2,1)S(1)}, u32[]{:S(2)}, u32[]{:S(2)}) collective-permute-start(bf16[352,1280]{1,0:T(8,128)(2,1)S(1)} %collective-permute-done.6.refs_0_), channel_id=1, source_target_pairs={{0,1},{1,0},{2,3},{3,2},{4,5},{5,4},{6,7},{7,6},{8,9},{9,8},{10,11... | collective-permute-start | bytes 2703368 | tf_op jit(solution)/shard_map/ppermute | solution.py:27
  79.3 14.8 %collective-permute-start.14 = (bf16[176,1280]{1,0:T(8,128)(2,1)S(1)}, bf16[176,1280]{1,0:T(8,128)(2,1)S(1)}, u32[]{:S(2)}, u32[]{:S(2)}) collective-permute-start(bf16[176,1280]{1,0:T(8,128)(2,1)S(1)} %collective-permute-done.10.refs_0_), channel_id=1, source_target_pairs={{0,2},{1,3},{2,0},{3,1},{4,6},{5,7},{6,4},{7,5},{8,10},{9,11},{10,... | collective-permute-start | bytes 1351688 | tf_op jit(solution)/shard_map/ppermute | solution.py:27
  79.8 14.3 %collective-permute-start.15 = (bf16[176,1280]{1,0:T(8,128)(2,1)S(1)}, bf16[176,1280]{1,0:T(8,128)(2,1)S(1)}, u32[]{:S(2)}, u32[]{:S(2)}) collective-permute-start(bf16[176,1280]{1,0:T(8,128)(2,1)S(1)} %collective-permute-done.10.refs_0_), channel_id=1, source_target_pairs={{0,8},{1,9},{2,10},{3,11},{4,12},{5,13},{6,14},{7,15},{8,0},{9,1},... | collective-permute-start | bytes 1351688 | tf_op jit(solution)/shard_map/ppermute | solution.py:27
  82.6 11.5 %collective-permute-start.5 = (bf16[160,1280]{1,0:T(8,128)(2,1)S(1)}, bf16[160,1280]{1,0:T(8,128)(2,1)S(1)}, u32[]{:S(2)}, u32[]{:S(2)}) collective-permute-start(bf16[160,1280]{1,0:T(8,128)(2,1)S(1)} %get-tuple-element.38), channel_id=1, source_target_pairs={{0,4},{1,5},{2,6},{3,7},{4,0},{5,1},{6,2},{7,3},{8,12},{9,13},{10,... | collective-permute-start | bytes 1228808 | tf_op jit(solution)/shard_map/ppermute | solution.py:27
  84.1 13.8 %collective-permute-start.17 = (bf16[352,1280]{1,0:T(8,128)(2,1)S(1)}, bf16[352,1280]{1,0:T(8,128)(2,1)S(1)}, u32[]{:S(2)}, u32[]{:S(2)}) collective-permute-start(bf16[352,1280]{1,0:T(8,128)(2,1)S(1)} %join.4.refs_3_), channel_id=1, source_target_pairs={{0,1},{1,0},{2,3},{3,2},{4,5},{5,4},{6,7},{7,6},{8,9},{9,8},{10,11... | collective-permute-start | bytes 2703368 | tf_op jit(solution)/shard_map/ppermute | solution.py:27
  94.2 5.7 %collective-permute-start.16 = (bf16[352,1280]{1,0:T(8,128)(2,1)S(1)}, bf16[352,1280]{1,0:T(8,128)(2,1)S(1)}, u32[]{:S(2)}, u32[]{:S(2)}) collective-permute-start(bf16[352,1280]{1,0:T(8,128)(2,1)S(1)} %join.6.refs_1_), channel_id=1, source_target_pairs={{0,1},{1,0},{2,3},{3,2},{4,5},{5,4},{6,7},{7,6},{8,9},{9,8},{10,11... | collective-permute-start | bytes 2703368 | tf_op jit(solution)/shard_map/ppermute | solution.py:27
  94.7 22.0 %collective-permute-start.22 = (bf16[352,1280]{1,0:T(8,128)(2,1)S(1)}, bf16[352,1280]{1,0:T(8,128)(2,1)S(1)}, u32[]{:S(2)}, u32[]{:S(2)}) collective-permute-start(bf16[352,1280]{1,0:T(8,128)(2,1)S(1)} %join.4.refs_3_), channel_id=1, source_target_pairs={{0,8},{1,9},{2,10},{3,11},{4,12},{5,13},{6,14},{7,15},{8,0},{9,1},... | collective-permute-start | bytes 2703368 | tf_op jit(solution)/shard_map/ppermute | solution.py:27
  95.5 20.9 %collective-permute-start.20 = (bf16[176,1280]{1,0:T(8,128)(2,1)S(1)}, bf16[176,1280]{1,0:T(8,128)(2,1)S(1)}, u32[]{:S(2)}, u32[]{:S(2)}) collective-permute-start(bf16[176,1280]{1,0:T(8,128)(2,1)S(1)} %collective-permute-done.15.refs_0_), channel_id=1, source_target_pairs={{0,2},{1,3},{2,0},{3,1},{4,6},{5,7},{6,4},{7,5},{8,10},{9,11},{10,... | collective-permute-start | bytes 1351688 | tf_op jit(solution)/shard_map/ppermute | solution.py:27
  96.4 13.2 %collective-permute-start.13 = (bf16[160,1280]{1,0:T(8,128)(2,1)S(1)}, bf16[160,1280]{1,0:T(8,128)(2,1)S(1)}, u32[]{:S(2)}, u32[]{:S(2)}) collective-permute-start(bf16[160,1280]{1,0:T(8,128)(2,1)S(1)} %get-tuple-element.45), channel_id=1, source_target_pairs={{0,4},{1,5},{2,6},{3,7},{4,0},{5,1},{6,2},{7,3},{8,12},{9,13},{10,... | collective-permute-start | bytes 1228808 | tf_op jit(solution)/shard_map/ppermute | solution.py:27
  97.9 18.5 %collective-permute-start.19 = (bf16[160,1280]{1,0:T(8,128)(2,1)S(1)}, bf16[160,1280]{1,0:T(8,128)(2,1)S(1)}, u32[]{:S(2)}, u32[]{:S(2)}) collective-permute-start(bf16[160,1280]{1,0:T(8,128)(2,1)S(1)} %get-tuple-element.48), channel_id=1, source_target_pairs={{0,4},{1,5},{2,6},{3,7},{4,0},{5,1},{6,2},{7,3},{8,12},{9,13},{10,... | collective-permute-start | bytes 1228808 | tf_op jit(solution)/shard_map/ppermute | solution.py:27
  116.5 5.0 %collective-permute-start.21 = (bf16[352,1280]{1,0:T(8,128)(2,1)S(1)}, bf16[352,1280]{1,0:T(8,128)(2,1)S(1)}, u32[]{:S(2)}, u32[]{:S(2)}) collective-permute-start(bf16[352,1280]{1,0:T(8,128)(2,1)S(1)} %join.7.refs_1_), channel_id=1, source_target_pairs={{0,1},{1,0},{2,3},{3,2},{4,5},{5,4},{6,7},{7,6},{8,9},{9,8},{10,11... | collective-permute-start | bytes 2703368 | tf_op jit(solution)/shard_map/ppermute | solution.py:27
  116.7 4.8 %collective-permute-start.23 = (bf16[352,1280]{1,0:T(8,128)(2,1)S(1)}, bf16[352,1280]{1,0:T(8,128)(2,1)S(1)}, u32[]{:S(2)}, u32[]{:S(2)}) collective-permute-start(bf16[352,1280]{1,0:T(8,128)(2,1)S(1)} %collective-permute-done.22.refs_3_), channel_id=1, source_target_pairs={{0,1},{1,0},{2,3},{3,2},{4,5},{5,4},{6,7},{7,6},{8,9},{9,8},{10,11... | collective-permute-start | bytes 2703368 | tf_op jit(solution)/shard_map/ppermute | solution.py:27
  117.1 21.1 %collective-permute-start.25 = (bf16[160,1280]{1,0:T(8,128)(2,1)S(1)}, bf16[160,1280]{1,0:T(8,128)(2,1)S(1)}, u32[]{:S(2)}, u32[]{:S(2)}) collective-permute-start(bf16[160,1280]{1,0:T(8,128)(2,1)S(1)} %get-tuple-element.55), channel_id=1, source_target_pairs={{0,4},{1,5},{2,6},{3,7},{4,0},{5,1},{6,2},{7,3},{8,12},{9,13},{10,... | collective-permute-start | bytes 1228808 | tf_op jit(solution)/shard_map/ppermute | solution.py:27
  118.6 19.6 %collective-permute-start.18 = (bf16[160,1280]{1,0:T(8,128)(2,1)S(1)}, bf16[160,1280]{1,0:T(8,128)(2,1)S(1)}, u32[]{:S(2)}, u32[]{:S(2)}) collective-permute-start(bf16[160,1280]{1,0:T(8,128)(2,1)S(1)} %get-tuple-element.52), channel_id=1, source_target_pairs={{0,4},{1,5},{2,6},{3,7},{4,0},{5,1},{6,2},{7,3},{8,12},{9,13},{10,... | collective-permute-start | bytes 1228808 | tf_op jit(solution)/shard_map/ppermute | solution.py:27
  131.5 15.4 %collective-permute-start.26 = (bf16[160,1280]{1,0:T(8,128)(2,1)S(1)}, bf16[160,1280]{1,0:T(8,128)(2,1)S(1)}, u32[]{:S(2)}, u32[]{:S(2)}) collective-permute-start(bf16[160,1280]{1,0:T(8,128)(2,1)S(1)} %get-tuple-element.63), channel_id=1, source_target_pairs={{0,4},{1,5},{2,6},{3,7},{4,0},{5,1},{6,2},{7,3},{8,12},{9,13},{10,... | collective-permute-start | bytes 1228808 | tf_op jit(solution)/shard_map/ppermute | solution.py:27
  133.1 21.9 %collective-permute-start.24 = (bf16[160,1280]{1,0:T(8,128)(2,1)S(1)}, bf16[160,1280]{1,0:T(8,128)(2,1)S(1)}, u32[]{:S(2)}, u32[]{:S(2)}) collective-permute-start(bf16[160,1280]{1,0:T(8,128)(2,1)S(1)} %get-tuple-element.60), channel_id=1, source_target_pairs={{0,4},{1,5},{2,6},{3,7},{4,0},{5,1},{6,2},{7,3},{8,12},{9,13},{10,... | collective-permute-start | bytes 1228808 | tf_op jit(solution)/shard_map/ppermute | solution.py:27
  156.7 3.7 %collective-permute-start.28 = (f32[8,128]{1,0:T(8,128)S(1)}, f32[8,128]{1,0:T(8,128)S(1)}, u32[]{:S(2)}, u32[]{:S(2)}) collective-permute-start(f32[8,128]{1,0:T(8,128)S(1)} %products.11.refs_0_), channel_id=1, source_target_pairs={{0,2},{1,3},{2,0},{3,1},{4,6},{5,7},{6,4},{7,5},{8,10},{9,11},{10,... | collective-permute-start | bytes 12296 | tf_op jit(solution)/shard_map/ppermute | solution.py:27
  161.8 4.5 %collective-permute-start.30 = (f32[8,128]{1,0:T(8,128)S(1)}, f32[8,128]{1,0:T(8,128)S(1)}, u32[]{:S(2)}, u32[]{:S(2)}) collective-permute-start(f32[8,128]{1,0:T(8,128)S(1)} %sum_of.2.refs_0_), channel_id=1, source_target_pairs={{0,8},{1,9},{2,10},{3,11},{4,12},{5,13},{6,14},{7,15},{8,0},{9,1},... | collective-permute-start | bytes 12296 | tf_op jit(solution)/shard_map/ppermute | solution.py:27
  162.4 4.5 %collective-permute-start.31 = (f32[8,128]{1,0:T(8,128)S(1)}, f32[8,128]{1,0:T(8,128)S(1)}, u32[]{:S(2)}, u32[]{:S(2)}) collective-permute-start(f32[8,128]{1,0:T(8,128)S(1)} %sum_of.2.refs_0_), channel_id=1, source_target_pairs={{0,16},{1,17},{2,18},{3,19},{4,20},{5,21},{6,22},{7,23},{8,24},{9,... | collective-permute-start | bytes 12296 | tf_op jit(solution)/shard_map/ppermute | solution.py:27
  164.2 5.4 %collective-permute-start.32 = (f32[8,128]{1,0:T(8,128)S(1)}, f32[8,128]{1,0:T(8,128)S(1)}, u32[]{:S(2)}, u32[]{:S(2)}) collective-permute-start(f32[8,128]{1,0:T(8,128)S(1)} %sum_of.2.refs_0_), channel_id=1, source_target_pairs={{0,24},{1,25},{2,26},{3,27},{4,28},{5,29},{6,30},{7,31},{8,16},{9,... | collective-permute-start | bytes 12296 | tf_op jit(solution)/shard_map/ppermute | solution.py:27
  170.2 3.7 %collective-permute-start.33 = (f32[8,128]{1,0:T(8,128)S(1)}, f32[8,128]{1,0:T(8,128)S(1)}, u32[]{:S(2)}, u32[]{:S(2)}) collective-permute-start(f32[8,128]{1,0:T(8,128)S(1)} %sum_of.3.refs_0_), channel_id=1, source_target_pairs={{0,4},{1,5},{2,6},{3,7},{4,0},{5,1},{6,2},{7,3},{8,12},{9,13},{10,... | collective-permute-start | bytes 12296 | tf_op jit(solution)/shard_map/ppermute | solution.py:27
  (8 other events, 87.0 us)

commit v19 on v13

--- a/solution.py
+++ b/solution.py
@@ -107,19 +107,24 @@
 CUBE = 0.044715
 
 
-def forward_kernel(
-    steps, place_ref, rows_ref, w_in_ref, w_out_ref, out_ref, near_ref, part_ref, hidden
-):
+def dot_of_halves(left, upper_ref, lower_ref):
+    middle = upper_ref.shape[0]
+    upper = jnp.dot(left[:, :middle], upper_ref[...], preferred_element_type=jnp.float32)
+    return upper + jnp.dot(left[:, middle:], lower_ref[...], preferred_element_type=jnp.float32)
+
+
+def forward_kernel(steps, place_ref, rows_ref, *refs):
+    w_in_refs, w_out_refs, (out_ref, near_ref, part_ref, hidden) = refs[:2], refs[2:4], refs[4:]
     step = pl.program_id(0)
     half = out_ref.shape[0]
     far = pl.ds(row_start(place_ref, out_ref, FAR), half)
-    tile = w_in_ref.shape[1]
+    tile = w_in_refs[0].shape[1]
 
     for n in range(steps):
 
         @pl.when(step == n)
         def _():
-            v = jnp.dot(rows_ref[...], w_in_ref[...], preferred_element_type=jnp.float32)
+            v = dot_of_halves(rows_ref[...], *w_in_refs)
             t = jnp.tanh(v * (SCALE + (SCALE * CUBE) * (v * v)))
             hidden[:, n * tile : (n + 1) * tile] = (v * (0.5 + 0.5 * t)).astype(jnp.bfloat16)
 
@@ -133,7 +138,7 @@
 
     @pl.when(step >= steps)
     def _():
-        out_ref[...] = jnp.dot(hidden[far, :], w_out_ref[...], preferred_element_type=jnp.float32)
+        out_ref[...] = dot_of_halves(hidden[far, :], *w_out_refs)
 
 
 def forward(place, part_rows, inputs, w_in, w_out):
@@ -145,7 +150,7 @@
     return call(
         functools.partial(forward_kernel, steps),
         "forward",
-        (place, inputs, w_in, w_out),
+        (place, inputs, w_in, w_in, w_out, w_out),
         [
             jax.ShapeDtypeStruct((rows // 2, depth), jnp.float32),
             jax.ShapeDtypeStruct((rows // 2, width), jnp.bfloat16),
@@ -153,10 +158,13 @@
         ],
         vmem=vmem_most,
         grid=(steps + depth // out_tile,),
-        in_specs=[
-            pl.BlockSpec((rows, depth), whole),
-            pl.BlockSpec((depth, tile), lambda n, s: (0, jnp.minimum(n, steps - 1))),
-            pl.BlockSpec((width, out_tile), lambda n, s: (0, last(n))),
+        in_specs=[pl.BlockSpec((rows, depth), whole)]
+        + [
+            pl.BlockSpec((depth // 2, tile), lambda n, s, k=k: (k, jnp.minimum(n, steps - 1)))
+            for k in range(2)
+        ]
+        + [
+            pl.BlockSpec((width // 2, out_tile), lambda n, s, k=k: (k, last(n))) for k in range(2)
         ],
         out_specs=[
             pl.BlockSpec((rows // 2, out_tile), lambda n, s: (0, last(n))),
@@ -412,14 +420,14 @@
     )[0]
 
 
-def merge_kernel(labels, place_ref, totals_ref, *refs):
+def merge_kernel(labels, place_ref, totals_ref, got_ref, *refs):
     refs, (first_ref, second_ref, weights_ref) = refs[:-3], refs[-3:]
 
     @pl.when(pl.program_id(0) == 0)
     def _():
         def entry(i, j):
             i, j = (jnp.bitwise_xor(place_ref[MEMBER], k) for k in (i, j))
-            return totals_ref[i, j]
+            return totals_ref[i, j] + got_ref[i, j]
 
         for n, weight in enumerate(tree_weights(len(labels), entry)):
             weights_ref[n] = weight
@@ -433,7 +441,7 @@
     second_ref[...] = second
 
 
-def merge(place, totals, slots, labels):
+def merge(place, totals, got, slots, labels):
     own, width = slots[0][0].shape
     block = max(b for b in range(16, min(own, 32) + 1, 16) if own % b == 0)
     spec = pl.BlockSpec((block, width), lambda n, s: (n, 0))
@@ -442,11 +450,11 @@
     return call(
         functools.partial(merge_kernel, tuple(labels)),
         "merge",
-        (place, totals, *arrays),
+        (place, totals, got, *arrays),
         [shape, shape],
         vmem=16 * 2**20,
         grid=(own // block,),
-        in_specs=[pl.BlockSpec(memory_space=pltpu.SMEM)] + [spec] * len(arrays),
+        in_specs=[pl.BlockSpec(memory_space=pltpu.SMEM)] * 2 + [spec] * len(arrays),
         out_specs=[spec, spec],
         scratch_shapes=[pltpu.SMEM((len(slots),), jnp.float32)],
     )
@@ -576,10 +584,9 @@
 
     rounds = [[(0, mask) for mask in range(1, shards)]]
     rounds.append([(m * others, 0) for m in range(2, members, 2)])
-    rounds.append([(others, 0)])
     for partners in rounds:
         totals = sum_of(place, [totals] + [from_mask(totals, *mask) for mask in partners])
-    pieces = merge(place, totals, slots, labels)
+    pieces = merge(place, totals, from_mask(totals, others, 0), slots, labels)
 
     for section in range(gathered, levels):
         upper_flag = position >> levels - 1 - section & 1

time: 175 us -> 176 us (level)
    pallas_call x21 -> x20, Pallas kernels: 73.2 us -> 73.5 us  [call(): pl.pallas_call(body, grid_spec=pltpu.PrefetchScalarGridSpec(num_scalar_pr...]
where the time goes in v19:
time: 176 us; the launch traced here: 175 us
  Pallas kernels  73.5 us (42%)
  waiting for transfers between devices  62.9 us (36%)
  starting transfers between devices  35.8 us (20%)
  local copies, waits for them, and re-layouts  1.87 us (1%)
    pallas_call x20, Pallas kernels, call(): pl.pallas_call(body, grid_spec=pltpu.PrefetchScalarGridSpec(num_scalar_pr...  73.5 us
    ppermute x34, waiting for transfers between devices, from_mask(): return lax.ppermute(value, ('dp', 'tensor'), pairs)  62.9 us
    ppermute x34, starting transfers between devices, from_mask(): return lax.ppermute(value, ('dp', 'tensor'), pairs)  35.8 us
  transfers between devices with their start and end apart: 34, of which 15 were waited for; matrix products, arithmetic and copies ran while one was open for 0% of the time, Pallas kernels for 31%

profile of v19, /device:TPU:0, one launch (start us, length us, event | category | flops | bytes accessed | tf_op | source)
XLA Modules:
  0.0 175.4 jit_solution(1142640671422210303)
XLA Ops:
  1.4 11.5 %forward.1 = (f32[352,1280]{1,0:T(8,128)}, bf16[352,1280]{1,0:T(8,128)(2,1)}, bf16[176,1280]{1,0:T(8,128)(2,1)}) custom-call(s32[8]{0:T(128)} %stack.35.place_ref, bf16[704,1280]{1,0:T(8,128)(2,1)} %refs_2_.3, bf16[1280,1280]{1,0:T(8,128)(2,1)} %refs_5_.5, bf16[1280,1280]{1,0:T(8,128)(2,1)} %refs_5_.5, bf16[1280,1280]{1,0:T(8,128)(2,1)} %refs_6_.3, ...), custom_call_target="tpu_custom_call" | custom-call | flops 1 | bytes 1 | tf_op jit(solution)/shard_map/forward/pallas_call | solution.py:81
  14.5 2.7 %product.1 = f32[352,1280]{1,0:T(8,128)S(1)} custom-call(s32[8]{0:T(128)S(1)} %copy-done.5, bf16[352,1280]{1,0:T(8,128)(2,1)S(1)} %copy-done.4, bf16[1280,1280]{1,0:T(8,128)(2,1)S(1)} %copy-done), custom_call_target="tpu_custom_call" | custom-call | flops 1 | bytes 1 | tf_op jit(solution)/shard_map/product/pallas_call | solution.py:81
  17.5 2.6 %collective-permute-start.3 = (f16[352,1280]{1,0:T(8,128)(2,1)S(1)}, f16[352,1280]{1,0:T(8,128)(2,1)S(1)}, u32[]{:S(2)}, u32[]{:S(2)}) collective-permute-start(f16[352,1280]{1,0:T(8,128)(2,1)S(1)} %get-tuple-element.64), channel_id=1, source_target_pairs={{0,2},{1,3},{2,0},{3,1},{4,6},{5,7},{6,4},{7,5},{8,10},{9,11},{10,... | collective-permute-start | bytes 2703368 | tf_op jit(solution)/shard_map/ppermute | solution.py:27
  20.1 2.6 %collective-permute-start = (bf16[176,1280]{1,0:T(8,128)(2,1)S(1)}, bf16[176,1280]{1,0:T(8,128)(2,1)S(1)}, u32[]{:S(2)}, u32[]{:S(2)}) collective-permute-start(bf16[176,1280]{1,0:T(8,128)(2,1)S(1)} %copy-done.6), channel_id=1, source_target_pairs={{0,16},{1,17},{2,18},{3,19},{4,20},{5,21},{6,22},{7,23},{8,24},{9,... | collective-permute-start | bytes 1351688 | tf_op jit(solution)/shard_map/ppermute | solution.py:27
  22.7 1.6 collective-permute-start.1
  24.3 16.5 %collective-permute-done.3 = f16[352,1280]{1,0:T(8,128)(2,1)S(1)} collective-permute-done((f16[352,1280]{1,0:T(8,128)(2,1)S(1)}, f16[352,1280]{1,0:T(8,128)(2,1)S(1)}, u32[]{:S(2)}, u32[]{:S(2)}) %collective-permute-start.3) | collective-permute-done | bytes 901152 | tf_op jit(solution)/shard_map/ppermute | solution.py:27
  40.9 2.3 %collective-permute-done.refs_0_ = bf16[176,1280]{1,0:T(8,128)(2,1)S(1)} collective-permute-done((bf16[176,1280]{1,0:T(8,128)(2,1)S(1)}, bf16[176,1280]{1,0:T(8,128)(2,1)S(1)}, u32[]{:S(2)}, u32[]{:S(2)}) %collective-permute-start) | collective-permute-done | bytes 450592 | tf_op jit(solution)/shard_map/ppermute | solution.py:27
  47.1 2.3 %collective-permute-start.10 = (bf16[176,1280]{1,0:T(8,128)(2,1)S(1)}, bf16[176,1280]{1,0:T(8,128)(2,1)S(1)}, u32[]{:S(2)}, u32[]{:S(2)}) collective-permute-start(bf16[176,1280]{1,0:T(8,128)(2,1)S(1)} %get-tuple-element.41), channel_id=1, source_target_pairs={{0,16},{1,17},{2,18},{3,19},{4,20},{5,21},{6,22},{7,23},{8,24},{9,... | collective-permute-start | bytes 1351688 | tf_op jit(solution)/shard_map/ppermute | solution.py:27
  50.5 9.7 %gradient.4 = (f32[160,1280]{1,0:T(8,128)S(1)}, f32[160,1280]{1,0:T(8,128)S(1)}, bf16[160,1280]{1,0:T(8,128)(2,1)S(1)}, bf16[160,1280]{1,0:T(8,128)(2,1)S(1)}) custom-call(s32[8]{0:T(128)S(1)} %copy-done.5, bf16[352,1280]{1,0:T(8,128)(2,1)S(1)} %get-tuple-element.36.refs_0_, bf16[352,1280]{1,0:T(8,128)(2,1)S(1)} %collective-permute-done.4.refs_1_, ...), custom_call_target="tpu_custom_call" | custom-call | flops 1 | bytes 1 | tf_op jit(solution)/shard_map/gradient/pallas_call | solution.py:81
  60.2 1.6 collective-permute-start.7
  61.8 13.9 %collective-permute-done.10.refs_0_ = bf16[176,1280]{1,0:T(8,128)(2,1)S(1)} collective-permute-done((bf16[176,1280]{1,0:T(8,128)(2,1)S(1)}, bf16[176,1280]{1,0:T(8,128)(2,1)S(1)}, u32[]{:S(2)}, u32[]{:S(2)}) %collective-permute-start.10) | collective-permute-done | bytes 450592 | tf_op jit(solution)/shard_map/ppermute | solution.py:27
  77.7 2.7 %collective-permute-start.15 = (bf16[176,1280]{1,0:T(8,128)(2,1)S(1)}, bf16[176,1280]{1,0:T(8,128)(2,1)S(1)}, u32[]{:S(2)}, u32[]{:S(2)}) collective-permute-start(bf16[176,1280]{1,0:T(8,128)(2,1)S(1)} %collective-permute-done.10.refs_0_), channel_id=1, source_target_pairs={{0,8},{1,9},{2,10},{3,11},{4,12},{5,13},{6,14},{7,15},{8,0},{9,1},... | collective-permute-start | bytes 1351688 | tf_op jit(solution)/shard_map/ppermute | solution.py:27
  80.4 1.5 collective-permute-start.5
  81.9 9.9 %gradient.5 = (f32[160,1280]{1,0:T(8,128)S(1)}, f32[160,1280]{1,0:T(8,128)S(1)}, bf16[160,1280]{1,0:T(8,128)(2,1)S(1)}, bf16[160,1280]{1,0:T(8,128)(2,1)S(1)}) custom-call(s32[8]{0:T(128)S(1)} %copy-done.5, bf16[352,1280]{1,0:T(8,128)(2,1)S(1)} %collective-permute-done.6.refs_0_, bf16[352,1280]{1,0:T(8,128)(2,1)S(1)} %collective-permute-done.8.refs_1_, ...), custom_call_target="tpu_custom_call" | custom-call | flops 1 | bytes 1 | tf_op jit(solution)/shard_map/gradient/pallas_call | solution.py:81
  93.8 1.5 collective-permute-start.13
  97.3 9.7 %gradient.6 = (f32[160,1280]{1,0:T(8,128)S(1)}, f32[160,1280]{1,0:T(8,128)S(1)}, bf16[160,1280]{1,0:T(8,128)(2,1)S(1)}, bf16[160,1280]{1,0:T(8,128)(2,1)S(1)}) custom-call(s32[8]{0:T(128)S(1)} %copy-done.5, f32[8,128]{1,0:T(8,128)S(1)} %products.6.refs_0_.refs_8_, bf16[352,1280]{1,0:T(8,128)(2,1)S(1)} %join.6.refs_1_, ...), custom_call_target="tpu_custom_call" | custom-call | flops 1 | bytes 1 | tf_op jit(solution)/shard_map/gradient/pallas_call | solution.py:81
  107.1 6.7 %collective-permute-done.19.refs_6_.refs_3_.refs_8_ = bf16[160,1280]{1,0:T(8,128)(2,1)S(1)} collective-permute-done((bf16[160,1280]{1,0:T(8,128)(2,1)S(1)}, bf16[160,1280]{1,0:T(8,128)(2,1)S(1)}, u32[]{:S(2)}, u32[]{:S(2)}) %collective-permute-start.19) | collective-permute-done | bytes 409632 | tf_op jit(solution)/shard_map/ppermute | solution.py:27
  116.5 2.4 %products.7.refs_0_.refs_12_ = f32[8,128]{1,0:T(8,128)S(1)} custom-call(s32[8]{0:T(128)S(1)} %copy-done.5, f32[160,1280]{1,0:T(8,128)S(1)} %get-tuple-element.46.refs_0_.refs_2_, f32[160,1280]{1,0:T(8,128)S(1)} %get-tuple-element.37.refs_1_.refs_0_.refs_3_, bf16[160,1280]{1,0:T(8,128)(2,1)S(1)} %collective-permute-done.7.refs_2_.refs_1_.refs_4_, ...), custom_call_target="tpu_custom_call" | custom-call | flops 1 | bytes 1 | tf_op jit(solution)/shard_map/products/pallas_call | solution.py:81
  119.0 9.9 %gradient.7 = (f32[160,1280]{1,0:T(8,128)S(1)}, f32[160,1280]{1,0:T(8,128)S(1)}, bf16[160,1280]{1,0:T(8,128)(2,1)S(1)}, bf16[160,1280]{1,0:T(8,128)(2,1)S(1)}) custom-call(s32[8]{0:T(128)S(1)} %copy-done.5, f32[8,128]{1,0:T(8,128)S(1)} %products.7.refs_0_.refs_12_, bf16[352,1280]{1,0:T(8,128)(2,1)S(1)} %join.7.refs_1_, ...), custom_call_target="tpu_custom_call" | custom-call | flops 1 | bytes 1 | tf_op jit(solution)/shard_map/gradient/pallas_call | solution.py:81
  128.9 1.5 collective-permute-start.26
  131.0 4.5 %collective-permute-done.18.refs_11_.refs_5_.refs_13_ = bf16[160,1280]{1,0:T(8,128)(2,1)S(1)} collective-permute-done((bf16[160,1280]{1,0:T(8,128)(2,1)S(1)}, bf16[160,1280]{1,0:T(8,128)(2,1)S(1)}, u32[]{:S(2)}, u32[]{:S(2)}) %collective-permute-start.18) | collective-permute-done | bytes 409632 | tf_op jit(solution)/shard_map/ppermute | solution.py:27
  135.5 3.4 %products.8.refs_14_ = f32[8,128]{1,0:T(8,128)S(1)} custom-call(s32[8]{0:T(128)S(1)} %copy-done.5, f32[160,1280]{1,0:T(8,128)S(1)} %get-tuple-element.46.refs_0_.refs_2_, f32[160,1280]{1,0:T(8,128)S(1)} %get-tuple-element.37.refs_1_.refs_0_.refs_3_, bf16[160,1280]{1,0:T(8,128)(2,1)S(1)} %collective-permute-done.7.refs_2_.refs_1_.refs_4_, ...), custom_call_target="tpu_custom_call" | custom-call | flops 1 | bytes 1 | tf_op jit(solution)/shard_map/products/pallas_call | solution.py:81
  139.0 2.8 %products.9.refs_8_ = f32[8,128]{1,0:T(8,128)S(1)} custom-call(s32[8]{0:T(128)S(1)} %copy-done.5, f32[160,1280]{1,0:T(8,128)S(1)} %get-tuple-element.46.refs_0_.refs_2_, f32[160,1280]{1,0:T(8,128)S(1)} %get-tuple-element.37.refs_1_.refs_0_.refs_3_, bf16[160,1280]{1,0:T(8,128)(2,1)S(1)} %collective-permute-done.7.refs_2_.refs_1_.refs_4_, ...), custom_call_target="tpu_custom_call" | custom-call | flops 1 | bytes 1 | tf_op jit(solution)/shard_map/products/pallas_call | solution.py:81
  141.8 2.5 %collective-permute-done.26.refs_7_.refs_16_ = bf16[160,1280]{1,0:T(8,128)(2,1)S(1)} collective-permute-done((bf16[160,1280]{1,0:T(8,128)(2,1)S(1)}, bf16[160,1280]{1,0:T(8,128)(2,1)S(1)}, u32[]{:S(2)}, u32[]{:S(2)}) %collective-permute-start.26) | collective-permute-done | bytes 409632 | tf_op jit(solution)/shard_map/ppermute | solution.py:27
  144.3 1.6 products.10.refs_8_
  146.0 6.7 %collective-permute-done.24.refs_7_.refs_17_ = bf16[160,1280]{1,0:T(8,128)(2,1)S(1)} collective-permute-done((bf16[160,1280]{1,0:T(8,128)(2,1)S(1)}, bf16[160,1280]{1,0:T(8,128)(2,1)S(1)}, u32[]{:S(2)}, u32[]{:S(2)}) %collective-permute-start.24) | collective-permute-done | bytes 409632 | tf_op jit(solution)/shard_map/ppermute | solution.py:27
  152.7 1.6 products.11.refs_0_
  156.3 1.8 %collective-permute-done.28.refs_2_ = f32[8,128]{1,0:T(8,128)S(1)} collective-permute-done((f32[8,128]{1,0:T(8,128)S(1)}, f32[8,128]{1,0:T(8,128)S(1)}, u32[]{:S(2)}, u32[]{:S(2)}) %collective-permute-start.28) | collective-permute-done | bytes 4128 | tf_op jit(solution)/shard_map/ppermute | solution.py:27
  161.6 2.0 %collective-permute-start.32 = (f32[8,128]{1,0:T(8,128)S(1)}, f32[8,128]{1,0:T(8,128)S(1)}, u32[]{:S(2)}, u32[]{:S(2)}) collective-permute-start(f32[8,128]{1,0:T(8,128)S(1)} %sum_of.2.refs_0_), channel_id=1, source_target_pairs={{0,24},{1,25},{2,26},{3,27},{4,28},{5,29},{6,30},{7,31},{8,16},{9,... | collective-permute-start | bytes 12296 | tf_op jit(solution)/shard_map/ppermute | solution.py:27
  164.6 2.4 %collective-permute-done.32.refs_3_ = f32[8,128]{1,0:T(8,128)S(1)} collective-permute-done((f32[8,128]{1,0:T(8,128)S(1)}, f32[8,128]{1,0:T(8,128)S(1)}, u32[]{:S(2)}, u32[]{:S(2)}) %collective-permute-start.32) | collective-permute-done | bytes 4128 | tf_op jit(solution)/shard_map/ppermute | solution.py:27
  168.7 2.5 %collective-permute-done.33.refs_1_ = f32[8,128]{1,0:T(8,128)S(1)} collective-permute-done((f32[8,128]{1,0:T(8,128)S(1)}, f32[8,128]{1,0:T(8,128)S(1)}, u32[]{:S(2)}, u32[]{:S(2)}) %collective-permute-start.33) | collective-permute-done | bytes 4128 | tf_op jit(solution)/shard_map/ppermute | solution.py:27
  171.2 4.2 %merge.1 = (f32[160,1280]{1,0:T(8,128)}, f32[160,1280]{1,0:T(8,128)}) custom-call(s32[8]{0:T(128)S(1)} %copy-done.5, f32[8,128]{1,0:T(8,128)S(1)} %sum_of.3.refs_0_, f32[8,128]{1,0:T(8,128)S(1)} %collective-permute-done.33.refs_1_, f32[160,1280]{1,0:T(8,128)S(1)} %get-tuple-element.46.refs_0_.refs_2_, ...), custom_call_target="tpu_custom_call" | custom-call | flops 1 | bytes 1 | tf_op jit(solution)/shard_map/merge/pallas_call | solution.py:81
  (74 shorter events, 25.0 us)
Async XLA Ops:
  12.9 4.4 %collective-permute-start.2 = (f32[352,1280]{1,0:T(8,128)}, f32[352,1280]{1,0:T(8,128)S(1)}, u32[]{:S(2)}, u32[]{:S(2)}) collective-permute-start(f32[352,1280]{1,0:T(8,128)} %get-tuple-element.35), channel_id=1, source_target_pairs={{0,1},{1,0},{2,3},{3,2},{4,5},{5,4},{6,7},{7,6},{8,9},{9,8},{10,11... | collective-permute-start | bytes 5406728 | tf_op jit(solution)/shard_map/ppermute | solution.py:27
  17.5 23.2 %collective-permute-start.3 = (f16[352,1280]{1,0:T(8,128)(2,1)S(1)}, f16[352,1280]{1,0:T(8,128)(2,1)S(1)}, u32[]{:S(2)}, u32[]{:S(2)}) collective-permute-start(f16[352,1280]{1,0:T(8,128)(2,1)S(1)} %get-tuple-element.64), channel_id=1, source_target_pairs={{0,2},{1,3},{2,0},{3,1},{4,6},{5,7},{6,4},{7,5},{8,10},{9,11},{10,... | collective-permute-start | bytes 2703368 | tf_op jit(solution)/shard_map/ppermute | solution.py:27
  20.1 23.1 %collective-permute-start = (bf16[176,1280]{1,0:T(8,128)(2,1)S(1)}, bf16[176,1280]{1,0:T(8,128)(2,1)S(1)}, u32[]{:S(2)}, u32[]{:S(2)}) collective-permute-start(bf16[176,1280]{1,0:T(8,128)(2,1)S(1)} %copy-done.6), channel_id=1, source_target_pairs={{0,16},{1,17},{2,18},{3,19},{4,20},{5,21},{6,22},{7,23},{8,24},{9,... | collective-permute-start | bytes 1351688 | tf_op jit(solution)/shard_map/ppermute | solution.py:27
  22.7 20.7 %collective-permute-start.1 = (bf16[176,1280]{1,0:T(8,128)(2,1)S(1)}, bf16[176,1280]{1,0:T(8,128)(2,1)S(1)}, u32[]{:S(2)}, u32[]{:S(2)}) collective-permute-start(bf16[176,1280]{1,0:T(8,128)(2,1)S(1)} %copy-done.6), channel_id=1, source_target_pairs={{0,8},{1,9},{2,10},{3,11},{4,12},{5,13},{6,14},{7,15},{8,0},{9,1},... | collective-permute-start | bytes 1351688 | tf_op jit(solution)/shard_map/ppermute | solution.py:27
  44.5 6.0 %collective-permute-start.4 = (bf16[352,1280]{1,0:T(8,128)(2,1)S(1)}, bf16[352,1280]{1,0:T(8,128)(2,1)S(1)}, u32[]{:S(2)}, u32[]{:S(2)}) collective-permute-start(bf16[352,1280]{1,0:T(8,128)(2,1)S(1)} %get-tuple-element.36.refs_0_), channel_id=1, source_target_pairs={{0,1},{1,0},{2,3},{3,2},{4,5},{5,4},{6,7},{7,6},{8,9},{9,8},{10,11... | collective-permute-start | bytes 2703368 | tf_op jit(solution)/shard_map/ppermute | solution.py:27
  44.6 32.1 %collective-permute-start.6 = (bf16[352,1280]{1,0:T(8,128)(2,1)S(1)}, bf16[352,1280]{1,0:T(8,128)(2,1)S(1)}, u32[]{:S(2)}, u32[]{:S(2)}) collective-permute-start(bf16[352,1280]{1,0:T(8,128)(2,1)S(1)} %get-tuple-element.36.refs_0_), channel_id=1, source_target_pairs={{0,8},{1,9},{2,10},{3,11},{4,12},{5,13},{6,14},{7,15},{8,0},{9,1},... | collective-permute-start | bytes 2703368 | tf_op jit(solution)/shard_map/ppermute | solution.py:27
  46.1 15.6 %collective-permute-start.11 = (bf16[176,1280]{1,0:T(8,128)(2,1)S(1)}, bf16[176,1280]{1,0:T(8,128)(2,1)S(1)}, u32[]{:S(2)}, u32[]{:S(2)}) collective-permute-start(bf16[176,1280]{1,0:T(8,128)(2,1)S(1)} %collective-permute-done.refs_0_), channel_id=1, source_target_pairs={{0,2},{1,3},{2,0},{3,1},{4,6},{5,7},{6,4},{7,5},{8,10},{9,11},{10,... | collective-permute-start | bytes 1351688 | tf_op jit(solution)/shard_map/ppermute | solution.py:27
  47.1 28.6 %collective-permute-start.10 = (bf16[176,1280]{1,0:T(8,128)(2,1)S(1)}, bf16[176,1280]{1,0:T(8,128)(2,1)S(1)}, u32[]{:S(2)}, u32[]{:S(2)}) collective-permute-start(bf16[176,1280]{1,0:T(8,128)(2,1)S(1)} %get-tuple-element.41), channel_id=1, source_target_pairs={{0,16},{1,17},{2,18},{3,19},{4,20},{5,21},{6,22},{7,23},{8,24},{9,... | collective-permute-start | bytes 1351688 | tf_op jit(solution)/shard_map/ppermute | solution.py:27
  49.4 26.3 %collective-permute-start.9 = (bf16[176,1280]{1,0:T(8,128)(2,1)S(1)}, bf16[176,1280]{1,0:T(8,128)(2,1)S(1)}, u32[]{:S(2)}, u32[]{:S(2)}) collective-permute-start(bf16[176,1280]{1,0:T(8,128)(2,1)S(1)} %collective-permute-done.1.refs_1_.refs_0_), channel_id=1, source_target_pairs={{0,2},{1,3},{2,0},{3,1},{4,6},{5,7},{6,4},{7,5},{8,10},{9,11},{10,... | collective-permute-start | bytes 1351688 | tf_op jit(solution)/shard_map/ppermute | solution.py:27
  60.2 16.5 %collective-permute-start.7 = (bf16[160,1280]{1,0:T(8,128)(2,1)S(1)}, bf16[160,1280]{1,0:T(8,128)(2,1)S(1)}, u32[]{:S(2)}, u32[]{:S(2)}) collective-permute-start(bf16[160,1280]{1,0:T(8,128)(2,1)S(1)} %get-tuple-element.39), channel_id=1, source_target_pairs={{0,4},{1,5},{2,6},{3,7},{4,0},{5,1},{6,2},{7,3},{8,12},{9,13},{10,... | collective-permute-start | bytes 1228808 | tf_op jit(solution)/shard_map/ppermute | solution.py:27
  75.8 6.1 %collective-permute-start.12 = (bf16[352,1280]{1,0:T(8,128)(2,1)S(1)}, bf16[352,1280]{1,0:T(8,128)(2,1)S(1)}, u32[]{:S(2)}, u32[]{:S(2)}) collective-permute-start(bf16[352,1280]{1,0:T(8,128)(2,1)S(1)} %join.5.refs_2_), channel_id=1, source_target_pairs={{0,1},{1,0},{2,3},{3,2},{4,5},{5,4},{6,7},{7,6},{8,9},{9,8},{10,11... | collective-permute-start | bytes 2703368 | tf_op jit(solution)/shard_map/ppermute | solution.py:27
  76.7 5.2 %collective-permute-start.8 = (bf16[352,1280]{1,0:T(8,128)(2,1)S(1)}, bf16[352,1280]{1,0:T(8,128)(2,1)S(1)}, u32[]{:S(2)}, u32[]{:S(2)}) collective-permute-start(bf16[352,1280]{1,0:T(8,128)(2,1)S(1)} %collective-permute-done.6.refs_0_), channel_id=1, source_target_pairs={{0,1},{1,0},{2,3},{3,2},{4,5},{5,4},{6,7},{7,6},{8,9},{9,8},{10,11... | collective-permute-start | bytes 2703368 | tf_op jit(solution)/shard_map/ppermute | solution.py:27
  76.7 15.2 %collective-permute-start.14 = (bf16[176,1280]{1,0:T(8,128)(2,1)S(1)}, bf16[176,1280]{1,0:T(8,128)(2,1)S(1)}, u32[]{:S(2)}, u32[]{:S(2)}) collective-permute-start(bf16[176,1280]{1,0:T(8,128)(2,1)S(1)} %collective-permute-done.10.refs_0_), channel_id=1, source_target_pairs={{0,2},{1,3},{2,0},{3,1},{4,6},{5,7},{6,4},{7,5},{8,10},{9,11},{10,... | collective-permute-start | bytes 1351688 | tf_op jit(solution)/shard_map/ppermute | solution.py:27
  77.7 14.2 %collective-permute-start.15 = (bf16[176,1280]{1,0:T(8,128)(2,1)S(1)}, bf16[176,1280]{1,0:T(8,128)(2,1)S(1)}, u32[]{:S(2)}, u32[]{:S(2)}) collective-permute-start(bf16[176,1280]{1,0:T(8,128)(2,1)S(1)} %collective-permute-done.10.refs_0_), channel_id=1, source_target_pairs={{0,8},{1,9},{2,10},{3,11},{4,12},{5,13},{6,14},{7,15},{8,0},{9,1},... | collective-permute-start | bytes 1351688 | tf_op jit(solution)/shard_map/ppermute | solution.py:27
  80.4 11.5 %collective-permute-start.5 = (bf16[160,1280]{1,0:T(8,128)(2,1)S(1)}, bf16[160,1280]{1,0:T(8,128)(2,1)S(1)}, u32[]{:S(2)}, u32[]{:S(2)}) collective-permute-start(bf16[160,1280]{1,0:T(8,128)(2,1)S(1)} %get-tuple-element.38), channel_id=1, source_target_pairs={{0,4},{1,5},{2,6},{3,7},{4,0},{5,1},{6,2},{7,3},{8,12},{9,13},{10,... | collective-permute-start | bytes 1228808 | tf_op jit(solution)/shard_map/ppermute | solution.py:27
  81.9 13.4 %collective-permute-start.17 = (bf16[352,1280]{1,0:T(8,128)(2,1)S(1)}, bf16[352,1280]{1,0:T(8,128)(2,1)S(1)}, u32[]{:S(2)}, u32[]{:S(2)}) collective-permute-start(bf16[352,1280]{1,0:T(8,128)(2,1)S(1)} %join.4.refs_3_), channel_id=1, source_target_pairs={{0,1},{1,0},{2,3},{3,2},{4,5},{5,4},{6,7},{7,6},{8,9},{9,8},{10,11... | collective-permute-start | bytes 2703368 | tf_op jit(solution)/shard_map/ppermute | solution.py:27
  92.0 5.4 %collective-permute-start.16 = (bf16[352,1280]{1,0:T(8,128)(2,1)S(1)}, bf16[352,1280]{1,0:T(8,128)(2,1)S(1)}, u32[]{:S(2)}, u32[]{:S(2)}) collective-permute-start(bf16[352,1280]{1,0:T(8,128)(2,1)S(1)} %join.6.refs_1_), channel_id=1, source_target_pairs={{0,1},{1,0},{2,3},{3,2},{4,5},{5,4},{6,7},{7,6},{8,9},{9,8},{10,11... | collective-permute-start | bytes 2703368 | tf_op jit(solution)/shard_map/ppermute | solution.py:27
  92.5 22.0 %collective-permute-start.22 = (bf16[352,1280]{1,0:T(8,128)(2,1)S(1)}, bf16[352,1280]{1,0:T(8,128)(2,1)S(1)}, u32[]{:S(2)}, u32[]{:S(2)}) collective-permute-start(bf16[352,1280]{1,0:T(8,128)(2,1)S(1)} %join.4.refs_3_), channel_id=1, source_target_pairs={{0,8},{1,9},{2,10},{3,11},{4,12},{5,13},{6,14},{7,15},{8,0},{9,1},... | collective-permute-start | bytes 2703368 | tf_op jit(solution)/shard_map/ppermute | solution.py:27
  92.9 20.9 %collective-permute-start.20 = (bf16[176,1280]{1,0:T(8,128)(2,1)S(1)}, bf16[176,1280]{1,0:T(8,128)(2,1)S(1)}, u32[]{:S(2)}, u32[]{:S(2)}) collective-permute-start(bf16[176,1280]{1,0:T(8,128)(2,1)S(1)} %collective-permute-done.15.refs_0_), channel_id=1, source_target_pairs={{0,2},{1,3},{2,0},{3,1},{4,6},{5,7},{6,4},{7,5},{8,10},{9,11},{10,... | collective-permute-start | bytes 1351688 | tf_op jit(solution)/shard_map/ppermute | solution.py:27
  93.8 13.2 %collective-permute-start.13 = (bf16[160,1280]{1,0:T(8,128)(2,1)S(1)}, bf16[160,1280]{1,0:T(8,128)(2,1)S(1)}, u32[]{:S(2)}, u32[]{:S(2)}) collective-permute-start(bf16[160,1280]{1,0:T(8,128)(2,1)S(1)} %get-tuple-element.45), channel_id=1, source_target_pairs={{0,4},{1,5},{2,6},{3,7},{4,0},{5,1},{6,2},{7,3},{8,12},{9,13},{10,... | collective-permute-start | bytes 1228808 | tf_op jit(solution)/shard_map/ppermute | solution.py:27
  95.4 18.4 %collective-permute-start.19 = (bf16[160,1280]{1,0:T(8,128)(2,1)S(1)}, bf16[160,1280]{1,0:T(8,128)(2,1)S(1)}, u32[]{:S(2)}, u32[]{:S(2)}) collective-permute-start(bf16[160,1280]{1,0:T(8,128)(2,1)S(1)} %get-tuple-element.48), channel_id=1, source_target_pairs={{0,4},{1,5},{2,6},{3,7},{4,0},{5,1},{6,2},{7,3},{8,12},{9,13},{10,... | collective-permute-start | bytes 1228808 | tf_op jit(solution)/shard_map/ppermute | solution.py:27
  113.9 5.1 %collective-permute-start.21 = (bf16[352,1280]{1,0:T(8,128)(2,1)S(1)}, bf16[352,1280]{1,0:T(8,128)(2,1)S(1)}, u32[]{:S(2)}, u32[]{:S(2)}) collective-permute-start(bf16[352,1280]{1,0:T(8,128)(2,1)S(1)} %join.7.refs_1_), channel_id=1, source_target_pairs={{0,1},{1,0},{2,3},{3,2},{4,5},{5,4},{6,7},{7,6},{8,9},{9,8},{10,11... | collective-permute-start | bytes 2703368 | tf_op jit(solution)/shard_map/ppermute | solution.py:27
  114.5 4.5 %collective-permute-start.23 = (bf16[352,1280]{1,0:T(8,128)(2,1)S(1)}, bf16[352,1280]{1,0:T(8,128)(2,1)S(1)}, u32[]{:S(2)}, u32[]{:S(2)}) collective-permute-start(bf16[352,1280]{1,0:T(8,128)(2,1)S(1)} %collective-permute-done.22.refs_3_), channel_id=1, source_target_pairs={{0,1},{1,0},{2,3},{3,2},{4,5},{5,4},{6,7},{7,6},{8,9},{9,8},{10,11... | collective-permute-start | bytes 2703368 | tf_op jit(solution)/shard_map/ppermute | solution.py:27
  114.5 21.0 %collective-permute-start.25 = (bf16[160,1280]{1,0:T(8,128)(2,1)S(1)}, bf16[160,1280]{1,0:T(8,128)(2,1)S(1)}, u32[]{:S(2)}, u32[]{:S(2)}) collective-permute-start(bf16[160,1280]{1,0:T(8,128)(2,1)S(1)} %get-tuple-element.55), channel_id=1, source_target_pairs={{0,4},{1,5},{2,6},{3,7},{4,0},{5,1},{6,2},{7,3},{8,12},{9,13},{10,... | collective-permute-start | bytes 1228808 | tf_op jit(solution)/shard_map/ppermute | solution.py:27
  116.0 19.6 %collective-permute-start.18 = (bf16[160,1280]{1,0:T(8,128)(2,1)S(1)}, bf16[160,1280]{1,0:T(8,128)(2,1)S(1)}, u32[]{:S(2)}, u32[]{:S(2)}) collective-permute-start(bf16[160,1280]{1,0:T(8,128)(2,1)S(1)} %get-tuple-element.52), channel_id=1, source_target_pairs={{0,4},{1,5},{2,6},{3,7},{4,0},{5,1},{6,2},{7,3},{8,12},{9,13},{10,... | collective-permute-start | bytes 1228808 | tf_op jit(solution)/shard_map/ppermute | solution.py:27
  128.9 15.4 %collective-permute-start.26 = (bf16[160,1280]{1,0:T(8,128)(2,1)S(1)}, bf16[160,1280]{1,0:T(8,128)(2,1)S(1)}, u32[]{:S(2)}, u32[]{:S(2)}) collective-permute-start(bf16[160,1280]{1,0:T(8,128)(2,1)S(1)} %get-tuple-element.63), channel_id=1, source_target_pairs={{0,4},{1,5},{2,6},{3,7},{4,0},{5,1},{6,2},{7,3},{8,12},{9,13},{10,... | collective-permute-start | bytes 1228808 | tf_op jit(solution)/shard_map/ppermute | solution.py:27
  130.4 22.3 %collective-permute-start.24 = (bf16[160,1280]{1,0:T(8,128)(2,1)S(1)}, bf16[160,1280]{1,0:T(8,128)(2,1)S(1)}, u32[]{:S(2)}, u32[]{:S(2)}) collective-permute-start(bf16[160,1280]{1,0:T(8,128)(2,1)S(1)} %get-tuple-element.60), channel_id=1, source_target_pairs={{0,4},{1,5},{2,6},{3,7},{4,0},{5,1},{6,2},{7,3},{8,12},{9,13},{10,... | collective-permute-start | bytes 1228808 | tf_op jit(solution)/shard_map/ppermute | solution.py:27
  154.4 3.7 %collective-permute-start.28 = (f32[8,128]{1,0:T(8,128)S(1)}, f32[8,128]{1,0:T(8,128)S(1)}, u32[]{:S(2)}, u32[]{:S(2)}) collective-permute-start(f32[8,128]{1,0:T(8,128)S(1)} %products.11.refs_0_), channel_id=1, source_target_pairs={{0,2},{1,3},{2,0},{3,1},{4,6},{5,7},{6,4},{7,5},{8,10},{9,11},{10,... | collective-permute-start | bytes 12296 | tf_op jit(solution)/shard_map/ppermute | solution.py:27
  159.2 4.5 %collective-permute-start.30 = (f32[8,128]{1,0:T(8,128)S(1)}, f32[8,128]{1,0:T(8,128)S(1)}, u32[]{:S(2)}, u32[]{:S(2)}) collective-permute-start(f32[8,128]{1,0:T(8,128)S(1)} %sum_of.2.refs_0_), channel_id=1, source_target_pairs={{0,8},{1,9},{2,10},{3,11},{4,12},{5,13},{6,14},{7,15},{8,0},{9,1},... | collective-permute-start | bytes 12296 | tf_op jit(solution)/shard_map/ppermute | solution.py:27
  160.1 4.5 %collective-permute-start.31 = (f32[8,128]{1,0:T(8,128)S(1)}, f32[8,128]{1,0:T(8,128)S(1)}, u32[]{:S(2)}, u32[]{:S(2)}) collective-permute-start(f32[8,128]{1,0:T(8,128)S(1)} %sum_of.2.refs_0_), channel_id=1, source_target_pairs={{0,16},{1,17},{2,18},{3,19},{4,20},{5,21},{6,22},{7,23},{8,24},{9,... | collective-permute-start | bytes 12296 | tf_op jit(solution)/shard_map/ppermute | solution.py:27
  161.6 5.4 %collective-permute-start.32 = (f32[8,128]{1,0:T(8,128)S(1)}, f32[8,128]{1,0:T(8,128)S(1)}, u32[]{:S(2)}, u32[]{:S(2)}) collective-permute-start(f32[8,128]{1,0:T(8,128)S(1)} %sum_of.2.refs_0_), channel_id=1, source_target_pairs={{0,24},{1,25},{2,26},{3,27},{4,28},{5,29},{6,30},{7,31},{8,16},{9,... | collective-permute-start | bytes 12296 | tf_op jit(solution)/shard_map/ppermute | solution.py:27
  167.5 3.7 %collective-permute-start.33 = (f32[8,128]{1,0:T(8,128)S(1)}, f32[8,128]{1,0:T(8,128)S(1)}, u32[]{:S(2)}, u32[]{:S(2)}) collective-permute-start(f32[8,128]{1,0:T(8,128)S(1)} %sum_of.3.refs_0_), channel_id=1, source_target_pairs={{0,4},{1,5},{2,6},{3,7},{4,0},{5,1},{6,2},{7,3},{8,12},{9,13},{10,... | collective-permute-start | bytes 12296 | tf_op jit(solution)/shard_map/ppermute | solution.py:27
  (9 other events, 73.1 us)

commit v20 on v13

--- a/solution.py
+++ b/solution.py
@@ -139,7 +139,7 @@
 def forward(place, part_rows, inputs, w_in, w_out):
     rows = inputs.shape[0]
     depth, width = w_in.shape
-    tile, out_tile = tile_of(width, 640), tile_of(depth, 640)
+    tile, out_tile = tile_of(width, 256), tile_of(depth, 640)
     steps = width // tile
     last = lambda n: jnp.maximum(n - steps, 0)
     return call(
@@ -412,14 +412,14 @@
     )[0]
 
 
-def merge_kernel(labels, place_ref, totals_ref, *refs):
+def merge_kernel(labels, place_ref, totals_ref, got_ref, *refs):
     refs, (first_ref, second_ref, weights_ref) = refs[:-3], refs[-3:]
 
     @pl.when(pl.program_id(0) == 0)
     def _():
         def entry(i, j):
             i, j = (jnp.bitwise_xor(place_ref[MEMBER], k) for k in (i, j))
-            return totals_ref[i, j]
+            return totals_ref[i, j] + got_ref[i, j]
 
         for n, weight in enumerate(tree_weights(len(labels), entry)):
             weights_ref[n] = weight
@@ -433,7 +433,7 @@
     second_ref[...] = second
 
 
-def merge(place, totals, slots, labels):
+def merge(place, totals, got, slots, labels):
     own, width = slots[0][0].shape
     block = max(b for b in range(16, min(own, 32) + 1, 16) if own % b == 0)
     spec = pl.BlockSpec((block, width), lambda n, s: (n, 0))
@@ -442,11 +442,11 @@
     return call(
         functools.partial(merge_kernel, tuple(labels)),
         "merge",
-        (place, totals, *arrays),
+        (place, totals, got, *arrays),
         [shape, shape],
         vmem=16 * 2**20,
         grid=(own // block,),
-        in_specs=[pl.BlockSpec(memory_space=pltpu.SMEM)] + [spec] * len(arrays),
+        in_specs=[pl.BlockSpec(memory_space=pltpu.SMEM)] * 2 + [spec] * len(arrays),
         out_specs=[spec, spec],
         scratch_shapes=[pltpu.SMEM((len(slots),), jnp.float32)],
     )
@@ -576,10 +576,9 @@
 
     rounds = [[(0, mask) for mask in range(1, shards)]]
     rounds.append([(m * others, 0) for m in range(2, members, 2)])
-    rounds.append([(others, 0)])
     for partners in rounds:
         totals = sum_of(place, [totals] + [from_mask(totals, *mask) for mask in partners])
-    pieces = merge(place, totals, slots, labels)
+    pieces = merge(place, totals, from_mask(totals, others, 0), slots, labels)
 
     for section in range(gathered, levels):
         upper_flag = position >> levels - 1 - section & 1

time: 175 us -> 175 us (level)
    pallas_call x21 -> x20, Pallas kernels: 73.2 us -> 73.3 us  [call(): pl.pallas_call(body, grid_spec=pltpu.PrefetchScalarGridSpec(num_scalar_pr...]
where the time goes in v20:
time: 175 us
  Pallas kernels  73.3 us (42%)
  waiting for transfers between devices  62.9 us (36%)
  starting transfers between devices  35.7 us (20%)
  local copies, waits for them, and re-layouts  1.87 us (1%)
    pallas_call x20, Pallas kernels, call(): pl.pallas_call(body, grid_spec=pltpu.PrefetchScalarGridSpec(num_scalar_pr...  73.3 us
    ppermute x34, waiting for transfers between devices, from_mask(): return lax.ppermute(value, ('dp', 'tensor'), pairs)  62.9 us
    ppermute x34, starting transfers between devices, from_mask(): return lax.ppermute(value, ('dp', 'tensor'), pairs)  35.7 us
  transfers between devices with their start and end apart: 34, of which 15 were waited for; matrix products, arithmetic and copies ran while one was open for 0% of the time, Pallas kernels for 31%

profile of v20, /device:TPU:0, one launch (start us, length us, event | category | flops | bytes accessed | tf_op | source)
XLA Modules:
  0.0 175.1 jit_solution(9294836501072171204)
XLA Ops:
  1.4 11.3 %forward.1 = (f32[352,1280]{1,0:T(8,128)}, bf16[352,1280]{1,0:T(8,128)(2,1)}, bf16[176,1280]{1,0:T(8,128)(2,1)}) custom-call(s32[8]{0:T(128)} %stack.35.place_ref, bf16[704,1280]{1,0:T(8,128)(2,1)} %refs_2_.3, bf16[1280,1280]{1,0:T(8,128)(2,1)} %refs_5_.5, bf16[1280,1280]{1,0:T(8,128)(2,1)} %refs_6_.3), custom_call_target="tpu_custom_call" | custom-call | flops 1 | bytes 1 | tf_op jit(solution)/shard_map/forward/pallas_call | solution.py:81
  14.3 2.7 %product.1 = f32[352,1280]{1,0:T(8,128)S(1)} custom-call(s32[8]{0:T(128)S(1)} %copy-done.5, bf16[352,1280]{1,0:T(8,128)(2,1)S(1)} %copy-done.4, bf16[1280,1280]{1,0:T(8,128)(2,1)S(1)} %copy-done), custom_call_target="tpu_custom_call" | custom-call | flops 1 | bytes 1 | tf_op jit(solution)/shard_map/product/pallas_call | solution.py:81
  17.2 2.6 %collective-permute-start.3 = (f16[352,1280]{1,0:T(8,128)(2,1)S(1)}, f16[352,1280]{1,0:T(8,128)(2,1)S(1)}, u32[]{:S(2)}, u32[]{:S(2)}) collective-permute-start(f16[352,1280]{1,0:T(8,128)(2,1)S(1)} %get-tuple-element.64), channel_id=1, source_target_pairs={{0,2},{1,3},{2,0},{3,1},{4,6},{5,7},{6,4},{7,5},{8,10},{9,11},{10,... | collective-permute-start | bytes 2703368 | tf_op jit(solution)/shard_map/ppermute | solution.py:27
  19.8 2.6 %collective-permute-start = (bf16[176,1280]{1,0:T(8,128)(2,1)S(1)}, bf16[176,1280]{1,0:T(8,128)(2,1)S(1)}, u32[]{:S(2)}, u32[]{:S(2)}) collective-permute-start(bf16[176,1280]{1,0:T(8,128)(2,1)S(1)} %copy-done.6), channel_id=1, source_target_pairs={{0,16},{1,17},{2,18},{3,19},{4,20},{5,21},{6,22},{7,23},{8,24},{9,... | collective-permute-start | bytes 1351688 | tf_op jit(solution)/shard_map/ppermute | solution.py:27
  22.4 1.6 collective-permute-start.1
  24.0 16.5 %collective-permute-done.3 = f16[352,1280]{1,0:T(8,128)(2,1)S(1)} collective-permute-done((f16[352,1280]{1,0:T(8,128)(2,1)S(1)}, f16[352,1280]{1,0:T(8,128)(2,1)S(1)}, u32[]{:S(2)}, u32[]{:S(2)}) %collective-permute-start.3) | collective-permute-done | bytes 901152 | tf_op jit(solution)/shard_map/ppermute | solution.py:27
  40.6 2.3 %collective-permute-done.refs_0_ = bf16[176,1280]{1,0:T(8,128)(2,1)S(1)} collective-permute-done((bf16[176,1280]{1,0:T(8,128)(2,1)S(1)}, bf16[176,1280]{1,0:T(8,128)(2,1)S(1)}, u32[]{:S(2)}, u32[]{:S(2)}) %collective-permute-start) | collective-permute-done | bytes 450592 | tf_op jit(solution)/shard_map/ppermute | solution.py:27
  46.8 2.3 %collective-permute-start.10 = (bf16[176,1280]{1,0:T(8,128)(2,1)S(1)}, bf16[176,1280]{1,0:T(8,128)(2,1)S(1)}, u32[]{:S(2)}, u32[]{:S(2)}) collective-permute-start(bf16[176,1280]{1,0:T(8,128)(2,1)S(1)} %get-tuple-element.41), channel_id=1, source_target_pairs={{0,16},{1,17},{2,18},{3,19},{4,20},{5,21},{6,22},{7,23},{8,24},{9,... | collective-permute-start | bytes 1351688 | tf_op jit(solution)/shard_map/ppermute | solution.py:27
  50.2 9.7 %gradient.4 = (f32[160,1280]{1,0:T(8,128)S(1)}, f32[160,1280]{1,0:T(8,128)S(1)}, bf16[160,1280]{1,0:T(8,128)(2,1)S(1)}, bf16[160,1280]{1,0:T(8,128)(2,1)S(1)}) custom-call(s32[8]{0:T(128)S(1)} %copy-done.5, bf16[352,1280]{1,0:T(8,128)(2,1)S(1)} %get-tuple-element.36.refs_0_, bf16[352,1280]{1,0:T(8,128)(2,1)S(1)} %collective-permute-done.4.refs_1_, ...), custom_call_target="tpu_custom_call" | custom-call | flops 1 | bytes 1 | tf_op jit(solution)/shard_map/gradient/pallas_call | solution.py:81
  59.9 1.6 collective-permute-start.7
  61.5 13.9 %collective-permute-done.10.refs_0_ = bf16[176,1280]{1,0:T(8,128)(2,1)S(1)} collective-permute-done((bf16[176,1280]{1,0:T(8,128)(2,1)S(1)}, bf16[176,1280]{1,0:T(8,128)(2,1)S(1)}, u32[]{:S(2)}, u32[]{:S(2)}) %collective-permute-start.10) | collective-permute-done | bytes 450592 | tf_op jit(solution)/shard_map/ppermute | solution.py:27
  77.4 2.7 %collective-permute-start.15 = (bf16[176,1280]{1,0:T(8,128)(2,1)S(1)}, bf16[176,1280]{1,0:T(8,128)(2,1)S(1)}, u32[]{:S(2)}, u32[]{:S(2)}) collective-permute-start(bf16[176,1280]{1,0:T(8,128)(2,1)S(1)} %collective-permute-done.10.refs_0_), channel_id=1, source_target_pairs={{0,8},{1,9},{2,10},{3,11},{4,12},{5,13},{6,14},{7,15},{8,0},{9,1},... | collective-permute-start | bytes 1351688 | tf_op jit(solution)/shard_map/ppermute | solution.py:27
  80.1 1.5 collective-permute-start.5
  81.7 9.9 %gradient.5 = (f32[160,1280]{1,0:T(8,128)S(1)}, f32[160,1280]{1,0:T(8,128)S(1)}, bf16[160,1280]{1,0:T(8,128)(2,1)S(1)}, bf16[160,1280]{1,0:T(8,128)(2,1)S(1)}) custom-call(s32[8]{0:T(128)S(1)} %copy-done.5, bf16[352,1280]{1,0:T(8,128)(2,1)S(1)} %collective-permute-done.6.refs_0_, bf16[352,1280]{1,0:T(8,128)(2,1)S(1)} %collective-permute-done.8.refs_1_, ...), custom_call_target="tpu_custom_call" | custom-call | flops 1 | bytes 1 | tf_op jit(solution)/shard_map/gradient/pallas_call | solution.py:81
  93.6 1.5 collective-permute-start.13
  97.0 9.7 %gradient.6 = (f32[160,1280]{1,0:T(8,128)S(1)}, f32[160,1280]{1,0:T(8,128)S(1)}, bf16[160,1280]{1,0:T(8,128)(2,1)S(1)}, bf16[160,1280]{1,0:T(8,128)(2,1)S(1)}) custom-call(s32[8]{0:T(128)S(1)} %copy-done.5, f32[8,128]{1,0:T(8,128)S(1)} %products.6.refs_0_.refs_8_, bf16[352,1280]{1,0:T(8,128)(2,1)S(1)} %join.6.refs_1_, ...), custom_call_target="tpu_custom_call" | custom-call | flops 1 | bytes 1 | tf_op jit(solution)/shard_map/gradient/pallas_call | solution.py:81
  106.8 6.7 %collective-permute-done.19.refs_6_.refs_3_.refs_8_ = bf16[160,1280]{1,0:T(8,128)(2,1)S(1)} collective-permute-done((bf16[160,1280]{1,0:T(8,128)(2,1)S(1)}, bf16[160,1280]{1,0:T(8,128)(2,1)S(1)}, u32[]{:S(2)}, u32[]{:S(2)}) %collective-permute-start.19) | collective-permute-done | bytes 409632 | tf_op jit(solution)/shard_map/ppermute | solution.py:27
  116.3 2.4 %products.7.refs_0_.refs_12_ = f32[8,128]{1,0:T(8,128)S(1)} custom-call(s32[8]{0:T(128)S(1)} %copy-done.5, f32[160,1280]{1,0:T(8,128)S(1)} %get-tuple-element.46.refs_0_.refs_2_, f32[160,1280]{1,0:T(8,128)S(1)} %get-tuple-element.37.refs_1_.refs_0_.refs_3_, bf16[160,1280]{1,0:T(8,128)(2,1)S(1)} %collective-permute-done.7.refs_2_.refs_1_.refs_4_, ...), custom_call_target="tpu_custom_call" | custom-call | flops 1 | bytes 1 | tf_op jit(solution)/shard_map/products/pallas_call | solution.py:81
  118.7 9.9 %gradient.7 = (f32[160,1280]{1,0:T(8,128)S(1)}, f32[160,1280]{1,0:T(8,128)S(1)}, bf16[160,1280]{1,0:T(8,128)(2,1)S(1)}, bf16[160,1280]{1,0:T(8,128)(2,1)S(1)}) custom-call(s32[8]{0:T(128)S(1)} %copy-done.5, f32[8,128]{1,0:T(8,128)S(1)} %products.7.refs_0_.refs_12_, bf16[352,1280]{1,0:T(8,128)(2,1)S(1)} %join.7.refs_1_, ...), custom_call_target="tpu_custom_call" | custom-call | flops 1 | bytes 1 | tf_op jit(solution)/shard_map/gradient/pallas_call | solution.py:81
  128.7 1.5 collective-permute-start.26
  130.7 4.5 %collective-permute-done.18.refs_11_.refs_5_.refs_13_ = bf16[160,1280]{1,0:T(8,128)(2,1)S(1)} collective-permute-done((bf16[160,1280]{1,0:T(8,128)(2,1)S(1)}, bf16[160,1280]{1,0:T(8,128)(2,1)S(1)}, u32[]{:S(2)}, u32[]{:S(2)}) %collective-permute-start.18) | collective-permute-done | bytes 409632 | tf_op jit(solution)/shard_map/ppermute | solution.py:27
  135.3 3.4 %products.8.refs_14_ = f32[8,128]{1,0:T(8,128)S(1)} custom-call(s32[8]{0:T(128)S(1)} %copy-done.5, f32[160,1280]{1,0:T(8,128)S(1)} %get-tuple-element.46.refs_0_.refs_2_, f32[160,1280]{1,0:T(8,128)S(1)} %get-tuple-element.37.refs_1_.refs_0_.refs_3_, bf16[160,1280]{1,0:T(8,128)(2,1)S(1)} %collective-permute-done.7.refs_2_.refs_1_.refs_4_, ...), custom_call_target="tpu_custom_call" | custom-call | flops 1 | bytes 1 | tf_op jit(solution)/shard_map/products/pallas_call | solution.py:81
  138.7 2.8 %products.9.refs_8_ = f32[8,128]{1,0:T(8,128)S(1)} custom-call(s32[8]{0:T(128)S(1)} %copy-done.5, f32[160,1280]{1,0:T(8,128)S(1)} %get-tuple-element.46.refs_0_.refs_2_, f32[160,1280]{1,0:T(8,128)S(1)} %get-tuple-element.37.refs_1_.refs_0_.refs_3_, bf16[160,1280]{1,0:T(8,128)(2,1)S(1)} %collective-permute-done.7.refs_2_.refs_1_.refs_4_, ...), custom_call_target="tpu_custom_call" | custom-call | flops 1 | bytes 1 | tf_op jit(solution)/shard_map/products/pallas_call | solution.py:81
  141.6 2.5 %collective-permute-done.26.refs_7_.refs_16_ = bf16[160,1280]{1,0:T(8,128)(2,1)S(1)} collective-permute-done((bf16[160,1280]{1,0:T(8,128)(2,1)S(1)}, bf16[160,1280]{1,0:T(8,128)(2,1)S(1)}, u32[]{:S(2)}, u32[]{:S(2)}) %collective-permute-start.26) | collective-permute-done | bytes 409632 | tf_op jit(solution)/shard_map/ppermute | solution.py:27
  144.1 1.6 products.10.refs_8_
  145.7 6.7 %collective-permute-done.24.refs_7_.refs_17_ = bf16[160,1280]{1,0:T(8,128)(2,1)S(1)} collective-permute-done((bf16[160,1280]{1,0:T(8,128)(2,1)S(1)}, bf16[160,1280]{1,0:T(8,128)(2,1)S(1)}, u32[]{:S(2)}, u32[]{:S(2)}) %collective-permute-start.24) | collective-permute-done | bytes 409632 | tf_op jit(solution)/shard_map/ppermute | solution.py:27
  152.4 1.6 products.11.refs_0_
  156.0 1.8 %collective-permute-done.28.refs_2_ = f32[8,128]{1,0:T(8,128)S(1)} collective-permute-done((f32[8,128]{1,0:T(8,128)S(1)}, f32[8,128]{1,0:T(8,128)S(1)}, u32[]{:S(2)}, u32[]{:S(2)}) %collective-permute-start.28) | collective-permute-done | bytes 4128 | tf_op jit(solution)/shard_map/ppermute | solution.py:27
  161.3 2.0 %collective-permute-start.32 = (f32[8,128]{1,0:T(8,128)S(1)}, f32[8,128]{1,0:T(8,128)S(1)}, u32[]{:S(2)}, u32[]{:S(2)}) collective-permute-start(f32[8,128]{1,0:T(8,128)S(1)} %sum_of.2.refs_0_), channel_id=1, source_target_pairs={{0,24},{1,25},{2,26},{3,27},{4,28},{5,29},{6,30},{7,31},{8,16},{9,... | collective-permute-start | bytes 12296 | tf_op jit(solution)/shard_map/ppermute | solution.py:27
  164.4 2.4 %collective-permute-done.32.refs_3_ = f32[8,128]{1,0:T(8,128)S(1)} collective-permute-done((f32[8,128]{1,0:T(8,128)S(1)}, f32[8,128]{1,0:T(8,128)S(1)}, u32[]{:S(2)}, u32[]{:S(2)}) %collective-permute-start.32) | collective-permute-done | bytes 4128 | tf_op jit(solution)/shard_map/ppermute | solution.py:27
  168.5 2.5 %collective-permute-done.33.refs_1_ = f32[8,128]{1,0:T(8,128)S(1)} collective-permute-done((f32[8,128]{1,0:T(8,128)S(1)}, f32[8,128]{1,0:T(8,128)S(1)}, u32[]{:S(2)}, u32[]{:S(2)}) %collective-permute-start.33) | collective-permute-done | bytes 4128 | tf_op jit(solution)/shard_map/ppermute | solution.py:27
  170.9 4.2 %merge.1 = (f32[160,1280]{1,0:T(8,128)}, f32[160,1280]{1,0:T(8,128)}) custom-call(s32[8]{0:T(128)S(1)} %copy-done.5, f32[8,128]{1,0:T(8,128)S(1)} %sum_of.3.refs_0_, f32[8,128]{1,0:T(8,128)S(1)} %collective-permute-done.33.refs_1_, f32[160,1280]{1,0:T(8,128)S(1)} %get-tuple-element.46.refs_0_.refs_2_, ...), custom_call_target="tpu_custom_call" | custom-call | flops 1 | bytes 1 | tf_op jit(solution)/shard_map/merge/pallas_call | solution.py:81
  (74 shorter events, 25.0 us)
Async XLA Ops:
  12.6 4.4 %collective-permute-start.2 = (f32[352,1280]{1,0:T(8,128)}, f32[352,1280]{1,0:T(8,128)S(1)}, u32[]{:S(2)}, u32[]{:S(2)}) collective-permute-start(f32[352,1280]{1,0:T(8,128)} %get-tuple-element.35), channel_id=1, source_target_pairs={{0,1},{1,0},{2,3},{3,2},{4,5},{5,4},{6,7},{7,6},{8,9},{9,8},{10,11... | collective-permute-start | bytes 5406728 | tf_op jit(solution)/shard_map/ppermute | solution.py:27
  17.2 23.2 %collective-permute-start.3 = (f16[352,1280]{1,0:T(8,128)(2,1)S(1)}, f16[352,1280]{1,0:T(8,128)(2,1)S(1)}, u32[]{:S(2)}, u32[]{:S(2)}) collective-permute-start(f16[352,1280]{1,0:T(8,128)(2,1)S(1)} %get-tuple-element.64), channel_id=1, source_target_pairs={{0,2},{1,3},{2,0},{3,1},{4,6},{5,7},{6,4},{7,5},{8,10},{9,11},{10,... | collective-permute-start | bytes 2703368 | tf_op jit(solution)/shard_map/ppermute | solution.py:27
  19.8 23.1 %collective-permute-start = (bf16[176,1280]{1,0:T(8,128)(2,1)S(1)}, bf16[176,1280]{1,0:T(8,128)(2,1)S(1)}, u32[]{:S(2)}, u32[]{:S(2)}) collective-permute-start(bf16[176,1280]{1,0:T(8,128)(2,1)S(1)} %copy-done.6), channel_id=1, source_target_pairs={{0,16},{1,17},{2,18},{3,19},{4,20},{5,21},{6,22},{7,23},{8,24},{9,... | collective-permute-start | bytes 1351688 | tf_op jit(solution)/shard_map/ppermute | solution.py:27
  22.4 20.7 %collective-permute-start.1 = (bf16[176,1280]{1,0:T(8,128)(2,1)S(1)}, bf16[176,1280]{1,0:T(8,128)(2,1)S(1)}, u32[]{:S(2)}, u32[]{:S(2)}) collective-permute-start(bf16[176,1280]{1,0:T(8,128)(2,1)S(1)} %copy-done.6), channel_id=1, source_target_pairs={{0,8},{1,9},{2,10},{3,11},{4,12},{5,13},{6,14},{7,15},{8,0},{9,1},... | collective-permute-start | bytes 1351688 | tf_op jit(solution)/shard_map/ppermute | solution.py:27
  44.3 5.9 %collective-permute-start.4 = (bf16[352,1280]{1,0:T(8,128)(2,1)S(1)}, bf16[352,1280]{1,0:T(8,128)(2,1)S(1)}, u32[]{:S(2)}, u32[]{:S(2)}) collective-permute-start(bf16[352,1280]{1,0:T(8,128)(2,1)S(1)} %get-tuple-element.36.refs_0_), channel_id=1, source_target_pairs={{0,1},{1,0},{2,3},{3,2},{4,5},{5,4},{6,7},{7,6},{8,9},{9,8},{10,11... | collective-permute-start | bytes 2703368 | tf_op jit(solution)/shard_map/ppermute | solution.py:27
  44.4 32.1 %collective-permute-start.6 = (bf16[352,1280]{1,0:T(8,128)(2,1)S(1)}, bf16[352,1280]{1,0:T(8,128)(2,1)S(1)}, u32[]{:S(2)}, u32[]{:S(2)}) collective-permute-start(bf16[352,1280]{1,0:T(8,128)(2,1)S(1)} %get-tuple-element.36.refs_0_), channel_id=1, source_target_pairs={{0,8},{1,9},{2,10},{3,11},{4,12},{5,13},{6,14},{7,15},{8,0},{9,1},... | collective-permute-start | bytes 2703368 | tf_op jit(solution)/shard_map/ppermute | solution.py:27
  45.9 15.6 %collective-permute-start.11 = (bf16[176,1280]{1,0:T(8,128)(2,1)S(1)}, bf16[176,1280]{1,0:T(8,128)(2,1)S(1)}, u32[]{:S(2)}, u32[]{:S(2)}) collective-permute-start(bf16[176,1280]{1,0:T(8,128)(2,1)S(1)} %collective-permute-done.refs_0_), channel_id=1, source_target_pairs={{0,2},{1,3},{2,0},{3,1},{4,6},{5,7},{6,4},{7,5},{8,10},{9,11},{10,... | collective-permute-start | bytes 1351688 | tf_op jit(solution)/shard_map/ppermute | solution.py:27
  46.8 28.6 %collective-permute-start.10 = (bf16[176,1280]{1,0:T(8,128)(2,1)S(1)}, bf16[176,1280]{1,0:T(8,128)(2,1)S(1)}, u32[]{:S(2)}, u32[]{:S(2)}) collective-permute-start(bf16[176,1280]{1,0:T(8,128)(2,1)S(1)} %get-tuple-element.41), channel_id=1, source_target_pairs={{0,16},{1,17},{2,18},{3,19},{4,20},{5,21},{6,22},{7,23},{8,24},{9,... | collective-permute-start | bytes 1351688 | tf_op jit(solution)/shard_map/ppermute | solution.py:27
  49.1 26.3 %collective-permute-start.9 = (bf16[176,1280]{1,0:T(8,128)(2,1)S(1)}, bf16[176,1280]{1,0:T(8,128)(2,1)S(1)}, u32[]{:S(2)}, u32[]{:S(2)}) collective-permute-start(bf16[176,1280]{1,0:T(8,128)(2,1)S(1)} %collective-permute-done.1.refs_1_.refs_0_), channel_id=1, source_target_pairs={{0,2},{1,3},{2,0},{3,1},{4,6},{5,7},{6,4},{7,5},{8,10},{9,11},{10,... | collective-permute-start | bytes 1351688 | tf_op jit(solution)/shard_map/ppermute | solution.py:27
  59.9 16.5 %collective-permute-start.7 = (bf16[160,1280]{1,0:T(8,128)(2,1)S(1)}, bf16[160,1280]{1,0:T(8,128)(2,1)S(1)}, u32[]{:S(2)}, u32[]{:S(2)}) collective-permute-start(bf16[160,1280]{1,0:T(8,128)(2,1)S(1)} %get-tuple-element.39), channel_id=1, source_target_pairs={{0,4},{1,5},{2,6},{3,7},{4,0},{5,1},{6,2},{7,3},{8,12},{9,13},{10,... | collective-permute-start | bytes 1228808 | tf_op jit(solution)/shard_map/ppermute | solution.py:27
  75.5 6.1 %collective-permute-start.12 = (bf16[352,1280]{1,0:T(8,128)(2,1)S(1)}, bf16[352,1280]{1,0:T(8,128)(2,1)S(1)}, u32[]{:S(2)}, u32[]{:S(2)}) collective-permute-start(bf16[352,1280]{1,0:T(8,128)(2,1)S(1)} %join.5.refs_2_), channel_id=1, source_target_pairs={{0,1},{1,0},{2,3},{3,2},{4,5},{5,4},{6,7},{7,6},{8,9},{9,8},{10,11... | collective-permute-start | bytes 2703368 | tf_op jit(solution)/shard_map/ppermute | solution.py:27
  76.4 5.2 %collective-permute-start.8 = (bf16[352,1280]{1,0:T(8,128)(2,1)S(1)}, bf16[352,1280]{1,0:T(8,128)(2,1)S(1)}, u32[]{:S(2)}, u32[]{:S(2)}) collective-permute-start(bf16[352,1280]{1,0:T(8,128)(2,1)S(1)} %collective-permute-done.6.refs_0_), channel_id=1, source_target_pairs={{0,1},{1,0},{2,3},{3,2},{4,5},{5,4},{6,7},{7,6},{8,9},{9,8},{10,11... | collective-permute-start | bytes 2703368 | tf_op jit(solution)/shard_map/ppermute | solution.py:27
  76.4 15.2 %collective-permute-start.14 = (bf16[176,1280]{1,0:T(8,128)(2,1)S(1)}, bf16[176,1280]{1,0:T(8,128)(2,1)S(1)}, u32[]{:S(2)}, u32[]{:S(2)}) collective-permute-start(bf16[176,1280]{1,0:T(8,128)(2,1)S(1)} %collective-permute-done.10.refs_0_), channel_id=1, source_target_pairs={{0,2},{1,3},{2,0},{3,1},{4,6},{5,7},{6,4},{7,5},{8,10},{9,11},{10,... | collective-permute-start | bytes 1351688 | tf_op jit(solution)/shard_map/ppermute | solution.py:27
  77.4 14.2 %collective-permute-start.15 = (bf16[176,1280]{1,0:T(8,128)(2,1)S(1)}, bf16[176,1280]{1,0:T(8,128)(2,1)S(1)}, u32[]{:S(2)}, u32[]{:S(2)}) collective-permute-start(bf16[176,1280]{1,0:T(8,128)(2,1)S(1)} %collective-permute-done.10.refs_0_), channel_id=1, source_target_pairs={{0,8},{1,9},{2,10},{3,11},{4,12},{5,13},{6,14},{7,15},{8,0},{9,1},... | collective-permute-start | bytes 1351688 | tf_op jit(solution)/shard_map/ppermute | solution.py:27
  80.1 11.5 %collective-permute-start.5 = (bf16[160,1280]{1,0:T(8,128)(2,1)S(1)}, bf16[160,1280]{1,0:T(8,128)(2,1)S(1)}, u32[]{:S(2)}, u32[]{:S(2)}) collective-permute-start(bf16[160,1280]{1,0:T(8,128)(2,1)S(1)} %get-tuple-element.38), channel_id=1, source_target_pairs={{0,4},{1,5},{2,6},{3,7},{4,0},{5,1},{6,2},{7,3},{8,12},{9,13},{10,... | collective-permute-start | bytes 1228808 | tf_op jit(solution)/shard_map/ppermute | solution.py:27
  81.7 13.4 %collective-permute-start.17 = (bf16[352,1280]{1,0:T(8,128)(2,1)S(1)}, bf16[352,1280]{1,0:T(8,128)(2,1)S(1)}, u32[]{:S(2)}, u32[]{:S(2)}) collective-permute-start(bf16[352,1280]{1,0:T(8,128)(2,1)S(1)} %join.4.refs_3_), channel_id=1, source_target_pairs={{0,1},{1,0},{2,3},{3,2},{4,5},{5,4},{6,7},{7,6},{8,9},{9,8},{10,11... | collective-permute-start | bytes 2703368 | tf_op jit(solution)/shard_map/ppermute | solution.py:27
  91.7 5.4 %collective-permute-start.16 = (bf16[352,1280]{1,0:T(8,128)(2,1)S(1)}, bf16[352,1280]{1,0:T(8,128)(2,1)S(1)}, u32[]{:S(2)}, u32[]{:S(2)}) collective-permute-start(bf16[352,1280]{1,0:T(8,128)(2,1)S(1)} %join.6.refs_1_), channel_id=1, source_target_pairs={{0,1},{1,0},{2,3},{3,2},{4,5},{5,4},{6,7},{7,6},{8,9},{9,8},{10,11... | collective-permute-start | bytes 2703368 | tf_op jit(solution)/shard_map/ppermute | solution.py:27
  92.2 22.0 %collective-permute-start.22 = (bf16[352,1280]{1,0:T(8,128)(2,1)S(1)}, bf16[352,1280]{1,0:T(8,128)(2,1)S(1)}, u32[]{:S(2)}, u32[]{:S(2)}) collective-permute-start(bf16[352,1280]{1,0:T(8,128)(2,1)S(1)} %join.4.refs_3_), channel_id=1, source_target_pairs={{0,8},{1,9},{2,10},{3,11},{4,12},{5,13},{6,14},{7,15},{8,0},{9,1},... | collective-permute-start | bytes 2703368 | tf_op jit(solution)/shard_map/ppermute | solution.py:27
  92.6 20.9 %collective-permute-start.20 = (bf16[176,1280]{1,0:T(8,128)(2,1)S(1)}, bf16[176,1280]{1,0:T(8,128)(2,1)S(1)}, u32[]{:S(2)}, u32[]{:S(2)}) collective-permute-start(bf16[176,1280]{1,0:T(8,128)(2,1)S(1)} %collective-permute-done.15.refs_0_), channel_id=1, source_target_pairs={{0,2},{1,3},{2,0},{3,1},{4,6},{5,7},{6,4},{7,5},{8,10},{9,11},{10,... | collective-permute-start | bytes 1351688 | tf_op jit(solution)/shard_map/ppermute | solution.py:27
  93.6 13.2 %collective-permute-start.13 = (bf16[160,1280]{1,0:T(8,128)(2,1)S(1)}, bf16[160,1280]{1,0:T(8,128)(2,1)S(1)}, u32[]{:S(2)}, u32[]{:S(2)}) collective-permute-start(bf16[160,1280]{1,0:T(8,128)(2,1)S(1)} %get-tuple-element.45), channel_id=1, source_target_pairs={{0,4},{1,5},{2,6},{3,7},{4,0},{5,1},{6,2},{7,3},{8,12},{9,13},{10,... | collective-permute-start | bytes 1228808 | tf_op jit(solution)/shard_map/ppermute | solution.py:27
  95.1 18.4 %collective-permute-start.19 = (bf16[160,1280]{1,0:T(8,128)(2,1)S(1)}, bf16[160,1280]{1,0:T(8,128)(2,1)S(1)}, u32[]{:S(2)}, u32[]{:S(2)}) collective-permute-start(bf16[160,1280]{1,0:T(8,128)(2,1)S(1)} %get-tuple-element.48), channel_id=1, source_target_pairs={{0,4},{1,5},{2,6},{3,7},{4,0},{5,1},{6,2},{7,3},{8,12},{9,13},{10,... | collective-permute-start | bytes 1228808 | tf_op jit(solution)/shard_map/ppermute | solution.py:27
  113.6 5.1 %collective-permute-start.21 = (bf16[352,1280]{1,0:T(8,128)(2,1)S(1)}, bf16[352,1280]{1,0:T(8,128)(2,1)S(1)}, u32[]{:S(2)}, u32[]{:S(2)}) collective-permute-start(bf16[352,1280]{1,0:T(8,128)(2,1)S(1)} %join.7.refs_1_), channel_id=1, source_target_pairs={{0,1},{1,0},{2,3},{3,2},{4,5},{5,4},{6,7},{7,6},{8,9},{9,8},{10,11... | collective-permute-start | bytes 2703368 | tf_op jit(solution)/shard_map/ppermute | solution.py:27
  114.2 4.5 %collective-permute-start.23 = (bf16[352,1280]{1,0:T(8,128)(2,1)S(1)}, bf16[352,1280]{1,0:T(8,128)(2,1)S(1)}, u32[]{:S(2)}, u32[]{:S(2)}) collective-permute-start(bf16[352,1280]{1,0:T(8,128)(2,1)S(1)} %collective-permute-done.22.refs_3_), channel_id=1, source_target_pairs={{0,1},{1,0},{2,3},{3,2},{4,5},{5,4},{6,7},{7,6},{8,9},{9,8},{10,11... | collective-permute-start | bytes 2703368 | tf_op jit(solution)/shard_map/ppermute | solution.py:27
  114.2 21.0 %collective-permute-start.25 = (bf16[160,1280]{1,0:T(8,128)(2,1)S(1)}, bf16[160,1280]{1,0:T(8,128)(2,1)S(1)}, u32[]{:S(2)}, u32[]{:S(2)}) collective-permute-start(bf16[160,1280]{1,0:T(8,128)(2,1)S(1)} %get-tuple-element.55), channel_id=1, source_target_pairs={{0,4},{1,5},{2,6},{3,7},{4,0},{5,1},{6,2},{7,3},{8,12},{9,13},{10,... | collective-permute-start | bytes 1228808 | tf_op jit(solution)/shard_map/ppermute | solution.py:27
  115.7 19.6 %collective-permute-start.18 = (bf16[160,1280]{1,0:T(8,128)(2,1)S(1)}, bf16[160,1280]{1,0:T(8,128)(2,1)S(1)}, u32[]{:S(2)}, u32[]{:S(2)}) collective-permute-start(bf16[160,1280]{1,0:T(8,128)(2,1)S(1)} %get-tuple-element.52), channel_id=1, source_target_pairs={{0,4},{1,5},{2,6},{3,7},{4,0},{5,1},{6,2},{7,3},{8,12},{9,13},{10,... | collective-permute-start | bytes 1228808 | tf_op jit(solution)/shard_map/ppermute | solution.py:27
  128.7 15.4 %collective-permute-start.26 = (bf16[160,1280]{1,0:T(8,128)(2,1)S(1)}, bf16[160,1280]{1,0:T(8,128)(2,1)S(1)}, u32[]{:S(2)}, u32[]{:S(2)}) collective-permute-start(bf16[160,1280]{1,0:T(8,128)(2,1)S(1)} %get-tuple-element.63), channel_id=1, source_target_pairs={{0,4},{1,5},{2,6},{3,7},{4,0},{5,1},{6,2},{7,3},{8,12},{9,13},{10,... | collective-permute-start | bytes 1228808 | tf_op jit(solution)/shard_map/ppermute | solution.py:27
  130.2 22.3 %collective-permute-start.24 = (bf16[160,1280]{1,0:T(8,128)(2,1)S(1)}, bf16[160,1280]{1,0:T(8,128)(2,1)S(1)}, u32[]{:S(2)}, u32[]{:S(2)}) collective-permute-start(bf16[160,1280]{1,0:T(8,128)(2,1)S(1)} %get-tuple-element.60), channel_id=1, source_target_pairs={{0,4},{1,5},{2,6},{3,7},{4,0},{5,1},{6,2},{7,3},{8,12},{9,13},{10,... | collective-permute-start | bytes 1228808 | tf_op jit(solution)/shard_map/ppermute | solution.py:27
  154.2 3.7 %collective-permute-start.28 = (f32[8,128]{1,0:T(8,128)S(1)}, f32[8,128]{1,0:T(8,128)S(1)}, u32[]{:S(2)}, u32[]{:S(2)}) collective-permute-start(f32[8,128]{1,0:T(8,128)S(1)} %products.11.refs_0_), channel_id=1, source_target_pairs={{0,2},{1,3},{2,0},{3,1},{4,6},{5,7},{6,4},{7,5},{8,10},{9,11},{10,... | collective-permute-start | bytes 12296 | tf_op jit(solution)/shard_map/ppermute | solution.py:27
  158.9 4.5 %collective-permute-start.30 = (f32[8,128]{1,0:T(8,128)S(1)}, f32[8,128]{1,0:T(8,128)S(1)}, u32[]{:S(2)}, u32[]{:S(2)}) collective-permute-start(f32[8,128]{1,0:T(8,128)S(1)} %sum_of.2.refs_0_), channel_id=1, source_target_pairs={{0,8},{1,9},{2,10},{3,11},{4,12},{5,13},{6,14},{7,15},{8,0},{9,1},... | collective-permute-start | bytes 12296 | tf_op jit(solution)/shard_map/ppermute | solution.py:27
  159.9 4.5 %collective-permute-start.31 = (f32[8,128]{1,0:T(8,128)S(1)}, f32[8,128]{1,0:T(8,128)S(1)}, u32[]{:S(2)}, u32[]{:S(2)}) collective-permute-start(f32[8,128]{1,0:T(8,128)S(1)} %sum_of.2.refs_0_), channel_id=1, source_target_pairs={{0,16},{1,17},{2,18},{3,19},{4,20},{5,21},{6,22},{7,23},{8,24},{9,... | collective-permute-start | bytes 12296 | tf_op jit(solution)/shard_map/ppermute | solution.py:27
  161.3 5.4 %collective-permute-start.32 = (f32[8,128]{1,0:T(8,128)S(1)}, f32[8,128]{1,0:T(8,128)S(1)}, u32[]{:S(2)}, u32[]{:S(2)}) collective-permute-start(f32[8,128]{1,0:T(8,128)S(1)} %sum_of.2.refs_0_), channel_id=1, source_target_pairs={{0,24},{1,25},{2,26},{3,27},{4,28},{5,29},{6,30},{7,31},{8,16},{9,... | collective-permute-start | bytes 12296 | tf_op jit(solution)/shard_map/ppermute | solution.py:27
  167.3 3.7 %collective-permute-start.33 = (f32[8,128]{1,0:T(8,128)S(1)}, f32[8,128]{1,0:T(8,128)S(1)}, u32[]{:S(2)}, u32[]{:S(2)}) collective-permute-start(f32[8,128]{1,0:T(8,128)S(1)} %sum_of.3.refs_0_), channel_id=1, source_target_pairs={{0,4},{1,5},{2,6},{3,7},{4,0},{5,1},{6,2},{7,3},{8,12},{9,13},{10,... | collective-permute-start | bytes 12296 | tf_op jit(solution)/shard_map/ppermute | solution.py:27
  (9 other events, 72.6 us)

commit v21 on v20

--- a/solution.py
+++ b/solution.py
@@ -139,7 +139,7 @@
 def forward(place, part_rows, inputs, w_in, w_out):
     rows = inputs.shape[0]
     depth, width = w_in.shape
-    tile, out_tile = tile_of(width, 256), tile_of(depth, 640)
+    tile, out_tile = tile_of(width, 640), tile_of(depth, 640)
     steps = width // tile
     last = lambda n: jnp.maximum(n - steps, 0)
     return call(
@@ -180,6 +180,7 @@
         "product",
         (place, left, right),
         [jax.ShapeDtypeStruct((rows, width), jnp.float32)],
+        vmem=vmem_most,
         grid=(width // tile,),
         in_specs=[pl.BlockSpec((rows, depth), whole), pl.BlockSpec((depth, tile), column)],
         out_specs=[pl.BlockSpec((rows, tile), column)],

time: 175 us -> 177 us (1.011)
  transfers between devices with their start and end apart: 34 -> 34, of which waited for: 15 -> 15; matrix products, arithmetic and copies ran while one was open for 0% -> 0% of each run, Pallas kernels for 31% -> 32%
where the time goes in v21:
time: 177 us
  Pallas kernels  74.8 us (42%)
  waiting for transfers between devices  62.7 us (35%)
  starting transfers between devices  35.9 us (20%)
  other arithmetic  2.03 us (1%)
    pallas_call x20, Pallas kernels, call(): pl.pallas_call(body, grid_spec=pltpu.PrefetchScalarGridSpec(num_scalar_pr...  74.8 us
    ppermute x34, waiting for transfers between devices, from_mask(): return lax.ppermute(value, ('dp', 'tensor'), pairs)  62.7 us
    ppermute x34, starting transfers between devices, from_mask(): return lax.ppermute(value, ('dp', 'tensor'), pairs)  35.9 us
  transfers between devices with their start and end apart: 34, of which 15 were waited for; matrix products, arithmetic and copies ran while one was open for 0% of the time, Pallas kernels for 32%

profile of v21, /device:TPU:0, one launch (start us, length us, event | category | flops | bytes accessed | tf_op | source)
XLA Modules:
  0.0 176.9 jit_solution(15772016756779330904)
XLA Ops:
  1.3 10.4 %forward.1 = (f32[352,1280]{1,0:T(8,128)}, bf16[352,1280]{1,0:T(8,128)(2,1)}, bf16[176,1280]{1,0:T(8,128)(2,1)}) custom-call(s32[8]{0:T(128)} %stack.35.place_ref, bf16[704,1280]{1,0:T(8,128)(2,1)} %refs_2_.3, bf16[1280,1280]{1,0:T(8,128)(2,1)} %refs_5_.5, bf16[1280,1280]{1,0:T(8,128)(2,1)} %refs_6_.3), custom_call_target="tpu_custom_call" | custom-call | flops 1 | bytes 1 | tf_op jit(solution)/shard_map/forward/pallas_call | solution.py:81
  12.1 5.0 %product.1 = f32[352,1280]{1,0:T(8,128)} custom-call(s32[8]{0:T(128)} %stack.35.place_ref, bf16[352,1280]{1,0:T(8,128)(2,1)} %get-tuple-element.34.refs_0_, bf16[1280,1280]{1,0:T(8,128)(2,1)} %refs_6_.3), custom_call_target="tpu_custom_call" | custom-call | flops 1 | bytes 1 | tf_op jit(solution)/shard_map/product/pallas_call | solution.py:81
  17.1 1.9 %multiply_convert_fusion = (f16[352,1280]{1,0:T(8,128)(2,1)S(1)}, f32[352,1280]{1,0:T(8,128)S(1)}) fusion(f32[352,1280]{1,0:T(8,128)} %product.1, f32[352,1280]{1,0:T(8,128)S(1)} %collective-permute-done.2), kind=kLoop, calls=%fused_computation.1 | loop fusion | flops 1351680 | bytes 6307840 | tf_op jit(solution)/shard_map/convert_element_type | solution.py:504
  19.0 2.6 %collective-permute-start.3 = (f16[352,1280]{1,0:T(8,128)(2,1)S(1)}, f16[352,1280]{1,0:T(8,128)(2,1)S(1)}, u32[]{:S(2)}, u32[]{:S(2)}) collective-permute-start(f16[352,1280]{1,0:T(8,128)(2,1)S(1)} %get-tuple-element.64), channel_id=1, source_target_pairs={{0,2},{1,3},{2,0},{3,1},{4,6},{5,7},{6,4},{7,5},{8,10},{9,11},{10,... | collective-permute-start | bytes 2703368 | tf_op jit(solution)/shard_map/ppermute | solution.py:27
  21.6 2.6 %collective-permute-start = (bf16[176,1280]{1,0:T(8,128)(2,1)S(1)}, bf16[176,1280]{1,0:T(8,128)(2,1)S(1)}, u32[]{:S(2)}, u32[]{:S(2)}) collective-permute-start(bf16[176,1280]{1,0:T(8,128)(2,1)S(1)} %copy-done.5), channel_id=1, source_target_pairs={{0,16},{1,17},{2,18},{3,19},{4,20},{5,21},{6,22},{7,23},{8,24},{9,... | collective-permute-start | bytes 1351688 | tf_op jit(solution)/shard_map/ppermute | solution.py:27
  24.2 1.6 collective-permute-start.1
  25.8 16.5 %collective-permute-done.3 = f16[352,1280]{1,0:T(8,128)(2,1)S(1)} collective-permute-done((f16[352,1280]{1,0:T(8,128)(2,1)S(1)}, f16[352,1280]{1,0:T(8,128)(2,1)S(1)}, u32[]{:S(2)}, u32[]{:S(2)}) %collective-permute-start.3) | collective-permute-done | bytes 901152 | tf_op jit(solution)/shard_map/ppermute | solution.py:27
  42.4 2.3 %collective-permute-done.refs_0_ = bf16[176,1280]{1,0:T(8,128)(2,1)S(1)} collective-permute-done((bf16[176,1280]{1,0:T(8,128)(2,1)S(1)}, bf16[176,1280]{1,0:T(8,128)(2,1)S(1)}, u32[]{:S(2)}, u32[]{:S(2)}) %collective-permute-start) | collective-permute-done | bytes 450592 | tf_op jit(solution)/shard_map/ppermute | solution.py:27
  48.1 2.3 %collective-permute-start.10 = (bf16[176,1280]{1,0:T(8,128)(2,1)S(1)}, bf16[176,1280]{1,0:T(8,128)(2,1)S(1)}, u32[]{:S(2)}, u32[]{:S(2)}) collective-permute-start(bf16[176,1280]{1,0:T(8,128)(2,1)S(1)} %get-tuple-element.41), channel_id=1, source_target_pairs={{0,16},{1,17},{2,18},{3,19},{4,20},{5,21},{6,22},{7,23},{8,24},{9,... | collective-permute-start | bytes 1351688 | tf_op jit(solution)/shard_map/ppermute | solution.py:27
  52.0 9.7 %gradient.4 = (f32[160,1280]{1,0:T(8,128)S(1)}, f32[160,1280]{1,0:T(8,128)S(1)}, bf16[160,1280]{1,0:T(8,128)(2,1)S(1)}, bf16[160,1280]{1,0:T(8,128)(2,1)S(1)}) custom-call(s32[8]{0:T(128)S(1)} %copy-done.4, bf16[352,1280]{1,0:T(8,128)(2,1)S(1)} %get-tuple-element.36.refs_0_, bf16[352,1280]{1,0:T(8,128)(2,1)S(1)} %collective-permute-done.4.refs_1_, ...), custom_call_target="tpu_custom_call" | custom-call | flops 1 | bytes 1 | tf_op jit(solution)/shard_map/gradient/pallas_call | solution.py:81
  61.7 1.6 collective-permute-start.7
  63.2 13.9 %collective-permute-done.10.refs_0_ = bf16[176,1280]{1,0:T(8,128)(2,1)S(1)} collective-permute-done((bf16[176,1280]{1,0:T(8,128)(2,1)S(1)}, bf16[176,1280]{1,0:T(8,128)(2,1)S(1)}, u32[]{:S(2)}, u32[]{:S(2)}) %collective-permute-start.10) | collective-permute-done | bytes 450592 | tf_op jit(solution)/shard_map/ppermute | solution.py:27
  78.7 2.8 %collective-permute-start.15 = (bf16[176,1280]{1,0:T(8,128)(2,1)S(1)}, bf16[176,1280]{1,0:T(8,128)(2,1)S(1)}, u32[]{:S(2)}, u32[]{:S(2)}) collective-permute-start(bf16[176,1280]{1,0:T(8,128)(2,1)S(1)} %collective-permute-done.10.refs_0_), channel_id=1, source_target_pairs={{0,8},{1,9},{2,10},{3,11},{4,12},{5,13},{6,14},{7,15},{8,0},{9,1},... | collective-permute-start | bytes 1351688 | tf_op jit(solution)/shard_map/ppermute | solution.py:27
  83.0 9.9 %gradient.5 = (f32[160,1280]{1,0:T(8,128)S(1)}, f32[160,1280]{1,0:T(8,128)S(1)}, bf16[160,1280]{1,0:T(8,128)(2,1)S(1)}, bf16[160,1280]{1,0:T(8,128)(2,1)S(1)}) custom-call(s32[8]{0:T(128)S(1)} %copy-done.4, bf16[352,1280]{1,0:T(8,128)(2,1)S(1)} %collective-permute-done.6.refs_0_, bf16[352,1280]{1,0:T(8,128)(2,1)S(1)} %collective-permute-done.8.refs_1_, ...), custom_call_target="tpu_custom_call" | custom-call | flops 1 | bytes 1 | tf_op jit(solution)/shard_map/gradient/pallas_call | solution.py:81
  98.7 9.7 %gradient.6 = (f32[160,1280]{1,0:T(8,128)S(1)}, f32[160,1280]{1,0:T(8,128)S(1)}, bf16[160,1280]{1,0:T(8,128)(2,1)S(1)}, bf16[160,1280]{1,0:T(8,128)(2,1)S(1)}) custom-call(s32[8]{0:T(128)S(1)} %copy-done.4, f32[8,128]{1,0:T(8,128)S(1)} %products.6.refs_0_.refs_8_, bf16[352,1280]{1,0:T(8,128)(2,1)S(1)} %join.6.refs_1_, ...), custom_call_target="tpu_custom_call" | custom-call | flops 1 | bytes 1 | tf_op jit(solution)/shard_map/gradient/pallas_call | solution.py:81
  108.5 6.8 %collective-permute-done.19.refs_6_.refs_3_.refs_8_ = bf16[160,1280]{1,0:T(8,128)(2,1)S(1)} collective-permute-done((bf16[160,1280]{1,0:T(8,128)(2,1)S(1)}, bf16[160,1280]{1,0:T(8,128)(2,1)S(1)}, u32[]{:S(2)}, u32[]{:S(2)}) %collective-permute-start.19) | collective-permute-done | bytes 409632 | tf_op jit(solution)/shard_map/ppermute | solution.py:27
  117.9 2.4 %products.7.refs_0_.refs_12_ = f32[8,128]{1,0:T(8,128)S(1)} custom-call(s32[8]{0:T(128)S(1)} %copy-done.4, f32[160,1280]{1,0:T(8,128)S(1)} %get-tuple-element.46.refs_0_.refs_2_, f32[160,1280]{1,0:T(8,128)S(1)} %get-tuple-element.37.refs_1_.refs_0_.refs_3_, bf16[160,1280]{1,0:T(8,128)(2,1)S(1)} %collective-permute-done.7.refs_2_.refs_1_.refs_4_, ...), custom_call_target="tpu_custom_call" | custom-call | flops 1 | bytes 1 | tf_op jit(solution)/shard_map/products/pallas_call | solution.py:81
  120.4 10.0 %gradient.7 = (f32[160,1280]{1,0:T(8,128)S(1)}, f32[160,1280]{1,0:T(8,128)S(1)}, bf16[160,1280]{1,0:T(8,128)(2,1)S(1)}, bf16[160,1280]{1,0:T(8,128)(2,1)S(1)}) custom-call(s32[8]{0:T(128)S(1)} %copy-done.4, f32[8,128]{1,0:T(8,128)S(1)} %products.7.refs_0_.refs_12_, bf16[352,1280]{1,0:T(8,128)(2,1)S(1)} %join.7.refs_1_, ...), custom_call_target="tpu_custom_call" | custom-call | flops 1 | bytes 1 | tf_op jit(solution)/shard_map/gradient/pallas_call | solution.py:81
  130.3 1.6 collective-permute-start.26
  132.4 4.6 %collective-permute-done.18.refs_11_.refs_5_.refs_13_ = bf16[160,1280]{1,0:T(8,128)(2,1)S(1)} collective-permute-done((bf16[160,1280]{1,0:T(8,128)(2,1)S(1)}, bf16[160,1280]{1,0:T(8,128)(2,1)S(1)}, u32[]{:S(2)}, u32[]{:S(2)}) %collective-permute-start.18) | collective-permute-done | bytes 409632 | tf_op jit(solution)/shard_map/ppermute | solution.py:27
  137.0 3.4 %products.8.refs_14_ = f32[8,128]{1,0:T(8,128)S(1)} custom-call(s32[8]{0:T(128)S(1)} %copy-done.4, f32[160,1280]{1,0:T(8,128)S(1)} %get-tuple-element.46.refs_0_.refs_2_, f32[160,1280]{1,0:T(8,128)S(1)} %get-tuple-element.37.refs_1_.refs_0_.refs_3_, bf16[160,1280]{1,0:T(8,128)(2,1)S(1)} %collective-permute-done.7.refs_2_.refs_1_.refs_4_, ...), custom_call_target="tpu_custom_call" | custom-call | flops 1 | bytes 1 | tf_op jit(solution)/shard_map/products/pallas_call | solution.py:81
  140.4 2.8 %products.9.refs_8_ = f32[8,128]{1,0:T(8,128)S(1)} custom-call(s32[8]{0:T(128)S(1)} %copy-done.4, f32[160,1280]{1,0:T(8,128)S(1)} %get-tuple-element.46.refs_0_.refs_2_, f32[160,1280]{1,0:T(8,128)S(1)} %get-tuple-element.37.refs_1_.refs_0_.refs_3_, bf16[160,1280]{1,0:T(8,128)(2,1)S(1)} %collective-permute-done.7.refs_2_.refs_1_.refs_4_, ...), custom_call_target="tpu_custom_call" | custom-call | flops 1 | bytes 1 | tf_op jit(solution)/shard_map/products/pallas_call | solution.py:81
  143.3 2.5 %collective-permute-done.26.refs_7_.refs_16_ = bf16[160,1280]{1,0:T(8,128)(2,1)S(1)} collective-permute-done((bf16[160,1280]{1,0:T(8,128)(2,1)S(1)}, bf16[160,1280]{1,0:T(8,128)(2,1)S(1)}, u32[]{:S(2)}, u32[]{:S(2)}) %collective-permute-start.26) | collective-permute-done | bytes 409632 | tf_op jit(solution)/shard_map/ppermute | solution.py:27
  145.8 1.6 products.10.refs_8_
  147.4 6.4 %collective-permute-done.24.refs_7_.refs_17_ = bf16[160,1280]{1,0:T(8,128)(2,1)S(1)} collective-permute-done((bf16[160,1280]{1,0:T(8,128)(2,1)S(1)}, bf16[160,1280]{1,0:T(8,128)(2,1)S(1)}, u32[]{:S(2)}, u32[]{:S(2)}) %collective-permute-start.24) | collective-permute-done | bytes 409632 | tf_op jit(solution)/shard_map/ppermute | solution.py:27
  153.8 1.6 products.11.refs_0_
  157.4 1.8 %collective-permute-done.28.refs_2_ = f32[8,128]{1,0:T(8,128)S(1)} collective-permute-done((f32[8,128]{1,0:T(8,128)S(1)}, f32[8,128]{1,0:T(8,128)S(1)}, u32[]{:S(2)}, u32[]{:S(2)}) %collective-permute-start.28) | collective-permute-done | bytes 4128 | tf_op jit(solution)/shard_map/ppermute | solution.py:27
  161.3 1.8 %collective-permute-start.31 = (f32[8,128]{1,0:T(8,128)S(1)}, f32[8,128]{1,0:T(8,128)S(1)}, u32[]{:S(2)}, u32[]{:S(2)}) collective-permute-start(f32[8,128]{1,0:T(8,128)S(1)} %sum_of.2.refs_0_), channel_id=1, source_target_pairs={{0,16},{1,17},{2,18},{3,19},{4,20},{5,21},{6,22},{7,23},{8,24},{9,... | collective-permute-start | bytes 12296 | tf_op jit(solution)/shard_map/ppermute | solution.py:27
  163.1 2.0 %collective-permute-start.32 = (f32[8,128]{1,0:T(8,128)S(1)}, f32[8,128]{1,0:T(8,128)S(1)}, u32[]{:S(2)}, u32[]{:S(2)}) collective-permute-start(f32[8,128]{1,0:T(8,128)S(1)} %sum_of.2.refs_0_), channel_id=1, source_target_pairs={{0,24},{1,25},{2,26},{3,27},{4,28},{5,29},{6,30},{7,31},{8,16},{9,... | collective-permute-start | bytes 12296 | tf_op jit(solution)/shard_map/ppermute | solution.py:27
  165.8 2.7 %collective-permute-done.32.refs_3_ = f32[8,128]{1,0:T(8,128)S(1)} collective-permute-done((f32[8,128]{1,0:T(8,128)S(1)}, f32[8,128]{1,0:T(8,128)S(1)}, u32[]{:S(2)}, u32[]{:S(2)}) %collective-permute-start.32) | collective-permute-done | bytes 4128 | tf_op jit(solution)/shard_map/ppermute | solution.py:27
  170.2 2.5 %collective-permute-done.33.refs_1_ = f32[8,128]{1,0:T(8,128)S(1)} collective-permute-done((f32[8,128]{1,0:T(8,128)S(1)}, f32[8,128]{1,0:T(8,128)S(1)}, u32[]{:S(2)}, u32[]{:S(2)}) %collective-permute-start.33) | collective-permute-done | bytes 4128 | tf_op jit(solution)/shard_map/ppermute | solution.py:27
  172.7 4.2 %merge.1 = (f32[160,1280]{1,0:T(8,128)}, f32[160,1280]{1,0:T(8,128)}) custom-call(s32[8]{0:T(128)S(1)} %copy-done.4, f32[8,128]{1,0:T(8,128)S(1)} %sum_of.3.refs_0_, f32[8,128]{1,0:T(8,128)S(1)} %collective-permute-done.33.refs_1_, f32[160,1280]{1,0:T(8,128)S(1)} %get-tuple-element.46.refs_0_.refs_2_, ...), custom_call_target="tpu_custom_call" | custom-call | flops 1 | bytes 1 | tf_op jit(solution)/shard_map/merge/pallas_call | solution.py:81
  (72 shorter events, 24.5 us)
Async XLA Ops:
  11.6 5.5 %collective-permute-start.2 = (f32[352,1280]{1,0:T(8,128)}, f32[352,1280]{1,0:T(8,128)S(1)}, u32[]{:S(2)}, u32[]{:S(2)}) collective-permute-start(f32[352,1280]{1,0:T(8,128)} %get-tuple-element.35), channel_id=1, source_target_pairs={{0,1},{1,0},{2,3},{3,2},{4,5},{5,4},{6,7},{7,6},{8,9},{9,8},{10,11... | collective-permute-start | bytes 5406728 | tf_op jit(solution)/shard_map/ppermute | solution.py:27
  19.0 23.2 %collective-permute-start.3 = (f16[352,1280]{1,0:T(8,128)(2,1)S(1)}, f16[352,1280]{1,0:T(8,128)(2,1)S(1)}, u32[]{:S(2)}, u32[]{:S(2)}) collective-permute-start(f16[352,1280]{1,0:T(8,128)(2,1)S(1)} %get-tuple-element.64), channel_id=1, source_target_pairs={{0,2},{1,3},{2,0},{3,1},{4,6},{5,7},{6,4},{7,5},{8,10},{9,11},{10,... | collective-permute-start | bytes 2703368 | tf_op jit(solution)/shard_map/ppermute | solution.py:27
  21.6 23.1 %collective-permute-start = (bf16[176,1280]{1,0:T(8,128)(2,1)S(1)}, bf16[176,1280]{1,0:T(8,128)(2,1)S(1)}, u32[]{:S(2)}, u32[]{:S(2)}) collective-permute-start(bf16[176,1280]{1,0:T(8,128)(2,1)S(1)} %copy-done.5), channel_id=1, source_target_pairs={{0,16},{1,17},{2,18},{3,19},{4,20},{5,21},{6,22},{7,23},{8,24},{9,... | collective-permute-start | bytes 1351688 | tf_op jit(solution)/shard_map/ppermute | solution.py:27
  24.2 20.7 %collective-permute-start.1 = (bf16[176,1280]{1,0:T(8,128)(2,1)S(1)}, bf16[176,1280]{1,0:T(8,128)(2,1)S(1)}, u32[]{:S(2)}, u32[]{:S(2)}) collective-permute-start(bf16[176,1280]{1,0:T(8,128)(2,1)S(1)} %copy-done.5), channel_id=1, source_target_pairs={{0,8},{1,9},{2,10},{3,11},{4,12},{5,13},{6,14},{7,15},{8,0},{9,1},... | collective-permute-start | bytes 1351688 | tf_op jit(solution)/shard_map/ppermute | solution.py:27
  46.0 6.0 %collective-permute-start.4 = (bf16[352,1280]{1,0:T(8,128)(2,1)S(1)}, bf16[352,1280]{1,0:T(8,128)(2,1)S(1)}, u32[]{:S(2)}, u32[]{:S(2)}) collective-permute-start(bf16[352,1280]{1,0:T(8,128)(2,1)S(1)} %get-tuple-element.36.refs_0_), channel_id=1, source_target_pairs={{0,1},{1,0},{2,3},{3,2},{4,5},{5,4},{6,7},{7,6},{8,9},{9,8},{10,11... | collective-permute-start | bytes 2703368 | tf_op jit(solution)/shard_map/ppermute | solution.py:27
  46.1 32.1 %collective-permute-start.6 = (bf16[352,1280]{1,0:T(8,128)(2,1)S(1)}, bf16[352,1280]{1,0:T(8,128)(2,1)S(1)}, u32[]{:S(2)}, u32[]{:S(2)}) collective-permute-start(bf16[352,1280]{1,0:T(8,128)(2,1)S(1)} %get-tuple-element.36.refs_0_), channel_id=1, source_target_pairs={{0,8},{1,9},{2,10},{3,11},{4,12},{5,13},{6,14},{7,15},{8,0},{9,1},... | collective-permute-start | bytes 2703368 | tf_op jit(solution)/shard_map/ppermute | solution.py:27
  47.6 15.7 %collective-permute-start.11 = (bf16[176,1280]{1,0:T(8,128)(2,1)S(1)}, bf16[176,1280]{1,0:T(8,128)(2,1)S(1)}, u32[]{:S(2)}, u32[]{:S(2)}) collective-permute-start(bf16[176,1280]{1,0:T(8,128)(2,1)S(1)} %collective-permute-done.refs_0_), channel_id=1, source_target_pairs={{0,2},{1,3},{2,0},{3,1},{4,6},{5,7},{6,4},{7,5},{8,10},{9,11},{10,... | collective-permute-start | bytes 1351688 | tf_op jit(solution)/shard_map/ppermute | solution.py:27
  48.1 29.0 %collective-permute-start.10 = (bf16[176,1280]{1,0:T(8,128)(2,1)S(1)}, bf16[176,1280]{1,0:T(8,128)(2,1)S(1)}, u32[]{:S(2)}, u32[]{:S(2)}) collective-permute-start(bf16[176,1280]{1,0:T(8,128)(2,1)S(1)} %get-tuple-element.41), channel_id=1, source_target_pairs={{0,16},{1,17},{2,18},{3,19},{4,20},{5,21},{6,22},{7,23},{8,24},{9,... | collective-permute-start | bytes 1351688 | tf_op jit(solution)/shard_map/ppermute | solution.py:27
  50.5 26.7 %collective-permute-start.9 = (bf16[176,1280]{1,0:T(8,128)(2,1)S(1)}, bf16[176,1280]{1,0:T(8,128)(2,1)S(1)}, u32[]{:S(2)}, u32[]{:S(2)}) collective-permute-start(bf16[176,1280]{1,0:T(8,128)(2,1)S(1)} %collective-permute-done.1.refs_1_.refs_0_), channel_id=1, source_target_pairs={{0,2},{1,3},{2,0},{3,1},{4,6},{5,7},{6,4},{7,5},{8,10},{9,11},{10,... | collective-permute-start | bytes 1351688 | tf_op jit(solution)/shard_map/ppermute | solution.py:27
  61.7 16.5 %collective-permute-start.7 = (bf16[160,1280]{1,0:T(8,128)(2,1)S(1)}, bf16[160,1280]{1,0:T(8,128)(2,1)S(1)}, u32[]{:S(2)}, u32[]{:S(2)}) collective-permute-start(bf16[160,1280]{1,0:T(8,128)(2,1)S(1)} %get-tuple-element.39), channel_id=1, source_target_pairs={{0,4},{1,5},{2,6},{3,7},{4,0},{5,1},{6,2},{7,3},{8,12},{9,13},{10,... | collective-permute-start | bytes 1228808 | tf_op jit(solution)/shard_map/ppermute | solution.py:27
  77.3 5.7 %collective-permute-start.12 = (bf16[352,1280]{1,0:T(8,128)(2,1)S(1)}, bf16[352,1280]{1,0:T(8,128)(2,1)S(1)}, u32[]{:S(2)}, u32[]{:S(2)}) collective-permute-start(bf16[352,1280]{1,0:T(8,128)(2,1)S(1)} %join.5.refs_2_), channel_id=1, source_target_pairs={{0,1},{1,0},{2,3},{3,2},{4,5},{5,4},{6,7},{7,6},{8,9},{9,8},{10,11... | collective-permute-start | bytes 2703368 | tf_op jit(solution)/shard_map/ppermute | solution.py:27
  78.2 4.8 %collective-permute-start.8 = (bf16[352,1280]{1,0:T(8,128)(2,1)S(1)}, bf16[352,1280]{1,0:T(8,128)(2,1)S(1)}, u32[]{:S(2)}, u32[]{:S(2)}) collective-permute-start(bf16[352,1280]{1,0:T(8,128)(2,1)S(1)} %collective-permute-done.6.refs_0_), channel_id=1, source_target_pairs={{0,1},{1,0},{2,3},{3,2},{4,5},{5,4},{6,7},{7,6},{8,9},{9,8},{10,11... | collective-permute-start | bytes 2703368 | tf_op jit(solution)/shard_map/ppermute | solution.py:27
  78.2 14.7 %collective-permute-start.14 = (bf16[176,1280]{1,0:T(8,128)(2,1)S(1)}, bf16[176,1280]{1,0:T(8,128)(2,1)S(1)}, u32[]{:S(2)}, u32[]{:S(2)}) collective-permute-start(bf16[176,1280]{1,0:T(8,128)(2,1)S(1)} %collective-permute-done.10.refs_0_), channel_id=1, source_target_pairs={{0,2},{1,3},{2,0},{3,1},{4,6},{5,7},{6,4},{7,5},{8,10},{9,11},{10,... | collective-permute-start | bytes 1351688 | tf_op jit(solution)/shard_map/ppermute | solution.py:27
  78.7 14.3 %collective-permute-start.15 = (bf16[176,1280]{1,0:T(8,128)(2,1)S(1)}, bf16[176,1280]{1,0:T(8,128)(2,1)S(1)}, u32[]{:S(2)}, u32[]{:S(2)}) collective-permute-start(bf16[176,1280]{1,0:T(8,128)(2,1)S(1)} %collective-permute-done.10.refs_0_), channel_id=1, source_target_pairs={{0,8},{1,9},{2,10},{3,11},{4,12},{5,13},{6,14},{7,15},{8,0},{9,1},... | collective-permute-start | bytes 1351688 | tf_op jit(solution)/shard_map/ppermute | solution.py:27
  81.5 11.5 %collective-permute-start.5 = (bf16[160,1280]{1,0:T(8,128)(2,1)S(1)}, bf16[160,1280]{1,0:T(8,128)(2,1)S(1)}, u32[]{:S(2)}, u32[]{:S(2)}) collective-permute-start(bf16[160,1280]{1,0:T(8,128)(2,1)S(1)} %get-tuple-element.38), channel_id=1, source_target_pairs={{0,4},{1,5},{2,6},{3,7},{4,0},{5,1},{6,2},{7,3},{8,12},{9,13},{10,... | collective-permute-start | bytes 1228808 | tf_op jit(solution)/shard_map/ppermute | solution.py:27
  83.0 13.8 %collective-permute-start.17 = (bf16[352,1280]{1,0:T(8,128)(2,1)S(1)}, bf16[352,1280]{1,0:T(8,128)(2,1)S(1)}, u32[]{:S(2)}, u32[]{:S(2)}) collective-permute-start(bf16[352,1280]{1,0:T(8,128)(2,1)S(1)} %join.4.refs_3_), channel_id=1, source_target_pairs={{0,1},{1,0},{2,3},{3,2},{4,5},{5,4},{6,7},{7,6},{8,9},{9,8},{10,11... | collective-permute-start | bytes 2703368 | tf_op jit(solution)/shard_map/ppermute | solution.py:27
  93.0 5.7 %collective-permute-start.16 = (bf16[352,1280]{1,0:T(8,128)(2,1)S(1)}, bf16[352,1280]{1,0:T(8,128)(2,1)S(1)}, u32[]{:S(2)}, u32[]{:S(2)}) collective-permute-start(bf16[352,1280]{1,0:T(8,128)(2,1)S(1)} %join.6.refs_1_), channel_id=1, source_target_pairs={{0,1},{1,0},{2,3},{3,2},{4,5},{5,4},{6,7},{7,6},{8,9},{9,8},{10,11... | collective-permute-start | bytes 2703368 | tf_op jit(solution)/shard_map/ppermute | solution.py:27
  93.6 22.0 %collective-permute-start.22 = (bf16[352,1280]{1,0:T(8,128)(2,1)S(1)}, bf16[352,1280]{1,0:T(8,128)(2,1)S(1)}, u32[]{:S(2)}, u32[]{:S(2)}) collective-permute-start(bf16[352,1280]{1,0:T(8,128)(2,1)S(1)} %join.4.refs_3_), channel_id=1, source_target_pairs={{0,8},{1,9},{2,10},{3,11},{4,12},{5,13},{6,14},{7,15},{8,0},{9,1},... | collective-permute-start | bytes 2703368 | tf_op jit(solution)/shard_map/ppermute | solution.py:27
  94.4 20.9 %collective-permute-start.20 = (bf16[176,1280]{1,0:T(8,128)(2,1)S(1)}, bf16[176,1280]{1,0:T(8,128)(2,1)S(1)}, u32[]{:S(2)}, u32[]{:S(2)}) collective-permute-start(bf16[176,1280]{1,0:T(8,128)(2,1)S(1)} %collective-permute-done.15.refs_0_), channel_id=1, source_target_pairs={{0,2},{1,3},{2,0},{3,1},{4,6},{5,7},{6,4},{7,5},{8,10},{9,11},{10,... | collective-permute-start | bytes 1351688 | tf_op jit(solution)/shard_map/ppermute | solution.py:27
  95.2 13.2 %collective-permute-start.13 = (bf16[160,1280]{1,0:T(8,128)(2,1)S(1)}, bf16[160,1280]{1,0:T(8,128)(2,1)S(1)}, u32[]{:S(2)}, u32[]{:S(2)}) collective-permute-start(bf16[160,1280]{1,0:T(8,128)(2,1)S(1)} %get-tuple-element.45), channel_id=1, source_target_pairs={{0,4},{1,5},{2,6},{3,7},{4,0},{5,1},{6,2},{7,3},{8,12},{9,13},{10,... | collective-permute-start | bytes 1228808 | tf_op jit(solution)/shard_map/ppermute | solution.py:27
  96.7 18.5 %collective-permute-start.19 = (bf16[160,1280]{1,0:T(8,128)(2,1)S(1)}, bf16[160,1280]{1,0:T(8,128)(2,1)S(1)}, u32[]{:S(2)}, u32[]{:S(2)}) collective-permute-start(bf16[160,1280]{1,0:T(8,128)(2,1)S(1)} %get-tuple-element.48), channel_id=1, source_target_pairs={{0,4},{1,5},{2,6},{3,7},{4,0},{5,1},{6,2},{7,3},{8,12},{9,13},{10,... | collective-permute-start | bytes 1228808 | tf_op jit(solution)/shard_map/ppermute | solution.py:27
  115.3 5.0 %collective-permute-start.21 = (bf16[352,1280]{1,0:T(8,128)(2,1)S(1)}, bf16[352,1280]{1,0:T(8,128)(2,1)S(1)}, u32[]{:S(2)}, u32[]{:S(2)}) collective-permute-start(bf16[352,1280]{1,0:T(8,128)(2,1)S(1)} %join.7.refs_1_), channel_id=1, source_target_pairs={{0,1},{1,0},{2,3},{3,2},{4,5},{5,4},{6,7},{7,6},{8,9},{9,8},{10,11... | collective-permute-start | bytes 2703368 | tf_op jit(solution)/shard_map/ppermute | solution.py:27
  115.6 4.8 %collective-permute-start.23 = (bf16[352,1280]{1,0:T(8,128)(2,1)S(1)}, bf16[352,1280]{1,0:T(8,128)(2,1)S(1)}, u32[]{:S(2)}, u32[]{:S(2)}) collective-permute-start(bf16[352,1280]{1,0:T(8,128)(2,1)S(1)} %collective-permute-done.22.refs_3_), channel_id=1, source_target_pairs={{0,1},{1,0},{2,3},{3,2},{4,5},{5,4},{6,7},{7,6},{8,9},{9,8},{10,11... | collective-permute-start | bytes 2703368 | tf_op jit(solution)/shard_map/ppermute | solution.py:27
  115.9 21.1 %collective-permute-start.25 = (bf16[160,1280]{1,0:T(8,128)(2,1)S(1)}, bf16[160,1280]{1,0:T(8,128)(2,1)S(1)}, u32[]{:S(2)}, u32[]{:S(2)}) collective-permute-start(bf16[160,1280]{1,0:T(8,128)(2,1)S(1)} %get-tuple-element.55), channel_id=1, source_target_pairs={{0,4},{1,5},{2,6},{3,7},{4,0},{5,1},{6,2},{7,3},{8,12},{9,13},{10,... | collective-permute-start | bytes 1228808 | tf_op jit(solution)/shard_map/ppermute | solution.py:27
  117.4 19.6 %collective-permute-start.18 = (bf16[160,1280]{1,0:T(8,128)(2,1)S(1)}, bf16[160,1280]{1,0:T(8,128)(2,1)S(1)}, u32[]{:S(2)}, u32[]{:S(2)}) collective-permute-start(bf16[160,1280]{1,0:T(8,128)(2,1)S(1)} %get-tuple-element.52), channel_id=1, source_target_pairs={{0,4},{1,5},{2,6},{3,7},{4,0},{5,1},{6,2},{7,3},{8,12},{9,13},{10,... | collective-permute-start | bytes 1228808 | tf_op jit(solution)/shard_map/ppermute | solution.py:27
  130.3 15.4 %collective-permute-start.26 = (bf16[160,1280]{1,0:T(8,128)(2,1)S(1)}, bf16[160,1280]{1,0:T(8,128)(2,1)S(1)}, u32[]{:S(2)}, u32[]{:S(2)}) collective-permute-start(bf16[160,1280]{1,0:T(8,128)(2,1)S(1)} %get-tuple-element.63), channel_id=1, source_target_pairs={{0,4},{1,5},{2,6},{3,7},{4,0},{5,1},{6,2},{7,3},{8,12},{9,13},{10,... | collective-permute-start | bytes 1228808 | tf_op jit(solution)/shard_map/ppermute | solution.py:27
  131.9 21.9 %collective-permute-start.24 = (bf16[160,1280]{1,0:T(8,128)(2,1)S(1)}, bf16[160,1280]{1,0:T(8,128)(2,1)S(1)}, u32[]{:S(2)}, u32[]{:S(2)}) collective-permute-start(bf16[160,1280]{1,0:T(8,128)(2,1)S(1)} %get-tuple-element.60), channel_id=1, source_target_pairs={{0,4},{1,5},{2,6},{3,7},{4,0},{5,1},{6,2},{7,3},{8,12},{9,13},{10,... | collective-permute-start | bytes 1228808 | tf_op jit(solution)/shard_map/ppermute | solution.py:27
  155.5 3.7 %collective-permute-start.28 = (f32[8,128]{1,0:T(8,128)S(1)}, f32[8,128]{1,0:T(8,128)S(1)}, u32[]{:S(2)}, u32[]{:S(2)}) collective-permute-start(f32[8,128]{1,0:T(8,128)S(1)} %products.11.refs_0_), channel_id=1, source_target_pairs={{0,2},{1,3},{2,0},{3,1},{4,6},{5,7},{6,4},{7,5},{8,10},{9,11},{10,... | collective-permute-start | bytes 12296 | tf_op jit(solution)/shard_map/ppermute | solution.py:27
  160.6 4.5 %collective-permute-start.30 = (f32[8,128]{1,0:T(8,128)S(1)}, f32[8,128]{1,0:T(8,128)S(1)}, u32[]{:S(2)}, u32[]{:S(2)}) collective-permute-start(f32[8,128]{1,0:T(8,128)S(1)} %sum_of.2.refs_0_), channel_id=1, source_target_pairs={{0,8},{1,9},{2,10},{3,11},{4,12},{5,13},{6,14},{7,15},{8,0},{9,1},... | collective-permute-start | bytes 12296 | tf_op jit(solution)/shard_map/ppermute | solution.py:27
  161.3 4.5 %collective-permute-start.31 = (f32[8,128]{1,0:T(8,128)S(1)}, f32[8,128]{1,0:T(8,128)S(1)}, u32[]{:S(2)}, u32[]{:S(2)}) collective-permute-start(f32[8,128]{1,0:T(8,128)S(1)} %sum_of.2.refs_0_), channel_id=1, source_target_pairs={{0,16},{1,17},{2,18},{3,19},{4,20},{5,21},{6,22},{7,23},{8,24},{9,... | collective-permute-start | bytes 12296 | tf_op jit(solution)/shard_map/ppermute | solution.py:27
  163.1 5.4 %collective-permute-start.32 = (f32[8,128]{1,0:T(8,128)S(1)}, f32[8,128]{1,0:T(8,128)S(1)}, u32[]{:S(2)}, u32[]{:S(2)}) collective-permute-start(f32[8,128]{1,0:T(8,128)S(1)} %sum_of.2.refs_0_), channel_id=1, source_target_pairs={{0,24},{1,25},{2,26},{3,27},{4,28},{5,29},{6,30},{7,31},{8,16},{9,... | collective-permute-start | bytes 12296 | tf_op jit(solution)/shard_map/ppermute | solution.py:27
  169.0 3.7 %collective-permute-start.33 = (f32[8,128]{1,0:T(8,128)S(1)}, f32[8,128]{1,0:T(8,128)S(1)}, u32[]{:S(2)}, u32[]{:S(2)}) collective-permute-start(f32[8,128]{1,0:T(8,128)S(1)} %sum_of.3.refs_0_), channel_id=1, source_target_pairs={{0,4},{1,5},{2,6},{3,7},{4,0},{5,1},{6,2},{7,3},{8,12},{9,13},{10,... | collective-permute-start | bytes 12296 | tf_op jit(solution)/shard_map/ppermute | solution.py:27
  (8 other events, 86.9 us)
